TPU v7x, 32 devices: a whole 2x2x4 slice. The times are simulated.
32 devices in a mesh: rep: 2 (over x), blk: 16 (over z, y, core).
Axes of the slice: x: 2, y: 2, z: 4, core: 2. Of those that a mesh axis runs over, the one named last changes fastest.
Arguments:
- hidden: bfloat16 [128, 12288], P(('rep', 'blk')), parts along dimension 0, may hold values from -6 to 6
- ln_gain: float32 [12288], replicated, may hold values from 0.1 to 1.9
- ln_shift: float32 [12288], replicated, may hold values from -2 to 2
- lists: int32 [8, 6], P('rep'), parts along dimension 0, may hold values from 0 to 15, as said below
- counts: int32 [8], P('rep'), parts along dimension 0, may hold values from 1 to 6
- block_slot: int32 [16], replicated, may hold values from 0 to 15, each once
- w_in: bfloat16 [12288, 2048], P(None, 'blk'), may hold values from -0.0546875 to 0.0546875
- b_in: float32 [2048], P('blk'), may hold values from -3 to 3
- w_out: bfloat16 [2048, 12288], P('blk'), may hold values from -0.3125 to 0.3125
- low_in: bfloat16 [12288, 512], P('blk'), may hold values from -0.0546875 to 0.0546875
- low_bias: float32 [512], replicated, may hold values from -3 to 3
- low_out: bfloat16 [512, 12288], P(None, 'blk'), may hold values from -0.25 to 0.25
Outputs:
- mixed: bfloat16 [128, 12288], P(('rep', 'blk')), parts along dimension 0
There are 2 independent parts, one for each index of `rep`. A program takes and returns all parts, laid end to end along the dimension named above; an argument that names none is the same for every part. Nothing has to cross between parts.
Inputs may be any that keep to these rules, and one draw needn't show every extreme that they name: `lists`: entries of one group's list are distinct block ids. Among the live entries of all groups, no block is listed by more than 2 groups, and some block is listed by exactly that many.
All inputs are finite; a program needn't handle non-finite values.
Results may differ from a plain program's by a relative error of at most 0.0063.
Values may be sent and summed in bfloat16 or wider, within the bound.
No kernel may reach another device: no remote copies, remote signals or barrier semaphores. Data moves between devices by JAX's collectives and lax.ppermute only.
A program may use at most 64 MiB of HBM per device.

v0:
```python
import jax
import jax.numpy as jnp
from jax import lax
from jax.sharding import PartitionSpec as P

GROUP = 16


def layer_norm(hidden, ln_gain, ln_shift):
    wide = hidden.astype(jnp.float32)
    mean = jnp.mean(wide, axis=-1, keepdims=True)
    centred = wide - mean
    variance = jnp.mean(centred * centred, axis=-1, keepdims=True)
    return (centred * lax.rsqrt(variance + 1e-05) * ln_gain + ln_shift).astype(jnp.bfloat16)


def activity(lists, counts, block_slot):
    groups, top = lists.shape
    nblocks = block_slot.shape[0]
    names = jnp.arange(nblocks, dtype=jnp.int32)
    live = (jnp.arange(top, dtype=jnp.int32)[None, :] < counts[:, None]).astype(jnp.int32)
    hits = (lists[:, :, None] == names[None, None, :]).astype(jnp.int32) * live[:, :, None]
    by_block = jnp.sum(hits, axis=1)
    placed = (block_slot[:, None] == names[None, :]).astype(jnp.int32)
    return jnp.sum(by_block[:, :, None] * placed[None, :, :], axis=1)


def shards(
    hidden,
    ln_gain,
    ln_shift,
    lists,
    counts,
    block_slot,
    w_in,
    b_in,
    w_out,
    low_in,
    low_bias,
    low_out,
):
    devices = lax.axis_size("blk")
    position = lax.axis_index("blk")
    row_dev, width = hidden.shape
    normed = layer_norm(hidden, ln_gain, ln_shift)
    table = activity(lists, counts, block_slot)
    share = low_in.shape[0]
    every = lax.all_gather(normed, "blk", axis=0, tiled=True)
    columns = lax.dynamic_slice_in_dim(every, position * share, share, 1)
    row_table = jnp.repeat(table, GROUP, axis=0)
    owner_flags = lax.dynamic_slice_in_dim(row_table, position, 1, 1)[:, 0]
    pre = jnp.dot(every, w_in, preferred_element_type=jnp.float32) + b_in
    act = jnp.maximum(pre, 0.0).astype(jnp.bfloat16)
    dense_part = jnp.dot(act, w_out, preferred_element_type=jnp.float32).astype(jnp.bfloat16)
    result = jnp.where(owner_flags[:, None] > 0, dense_part, jnp.zeros_like(dense_part))
    lowz = lax.psum_scatter(
        jnp.dot(columns, low_in, preferred_element_type=jnp.float32),
        "blk",
        scatter_dimension=0,
        tiled=True,
    )
    low_h = jnp.maximum(lowz + low_bias, 0.0).astype(jnp.bfloat16)
    low_cols = jnp.dot(
        lax.all_gather(low_h, "blk", axis=0, tiled=True),
        low_out,
        preferred_element_type=jnp.float32,
    ).astype(jnp.bfloat16)
    low_y = lax.all_to_all(low_cols, "blk", split_axis=0, concat_axis=1, tiled=True)
    returned = lax.all_to_all(result, "blk", split_axis=0, concat_axis=0, tiled=True)
    sparse = jnp.sum(returned.reshape(devices, row_dev, width), axis=0, dtype=jnp.float32)
    return (low_y.astype(jnp.float32) + sparse).astype(jnp.bfloat16)


def solution(mesh):
    return jax.shard_map(
        shards,
        mesh=mesh,
        in_specs=(
            P(("rep", "blk"), None),
            P(),
            P(),
            P("rep", None),
            P("rep"),
            P(),
            P(None, "blk"),
            P("blk"),
            P("blk", None),
            P("blk", None),
            P(),
            P(None, "blk"),
        ),
        out_specs=P(("rep", "blk"), None),
        check_vma=False,
    )
```

profile of v0, /device:TPU:0, one launch (start us, length us, event | category | flops | bytes accessed | tf_op | source)
XLA Modules:
  0.0 229.9 jit_solution(2917876594392851235)
XLA Ops:
  6.5 1.3 convert_reduce_fusion.1
  7.8 1.2 fusion.5
  9.0 1.7 fusion.9
  10.7 0.0 all-gather.4.cloned.1.call-update
  10.7 0.0 all-reduce.3.cloned.1.call-start
  10.8 0.8 copy.16
  11.6 0.7 fusion.18
  12.2 0.1 select_reduce_fusion
  12.3 0.7 fusion.16
  13.0 0.1 multiply_reduce_fusion
  13.1 0.1 copy.17
  13.2 0.1 broadcast_in_dim.11
  13.3 0.1 reshape.71
  13.4 1.3 dynamic-slice
  15.4 0.0 copy-start.1
  15.4 37.8 %all-gather.4.cloned.1.call-done = bf16[16,4,12288]{2,1,0:T(4,128)(2,1)} async-done(((bf16[1,4,12288]{2,1,0:T(4,128)(2,1)}), bf16[16,4,12288]{2,1,0:T(4,128)(2,1)}) %all-gather.4.cloned.1.call-update) | async-done | bytes 1572880 | tf_op jit(solution)/shard_map/all_gather | solution.py:48
  53.3 3.7 %reshape.74 = bf16[64,12288]{1,0:T(8,128)(2,1)} reshape(bf16[16,4,12288]{2,1,0:T(4,128)(2,1)} %all-gather.4.cloned.1.call-done) | data formatting | bytes 3145728
  56.9 2.1 fusion.10
  59.0 0.0 all-reduce.3.cloned.1.call-update
  59.1 86.0 %all-reduce.3.cloned.1.call-done = f32[64,512]{1,0:T(8,128)} async-done(((f32[64,512]{1,0:T(8,128)}), f32[64,512]{1,0:T(8,128)}) %all-reduce.3.cloned.1.call-update) | async-done | bytes 131088
  145.1 0.7 fusion.17
  145.8 22.2 %all-gather.1 = bf16[16,4,512]{2,1,0:T(4,128)(2,1)S(1)} all-gather(bf16[1,4,512]{2,1,0:T(4,128)(2,1)S(1)} %fusion.17), channel_id=1, replica_groups=mesh['rep'=2,'blk'=16] {'blk'}, dimensions={0}, use_global_device_ids=true | all-gather | bytes 69632 | tf_op jit(solution)/shard_map/all_gather | solution.py:64
  168.0 1.4 convolution_convert_fusion.1
  169.4 0.7 all_to_all.16
  170.1 3.5 %all-to-all-start = ((bf16[16,4,768]{2,1,0:T(4,128)(2,1)}), bf16[16,4,768]{2,1,0:T(4,128)(2,1)S(1)}, u32[]{:S(2)}, u32[]{:S(2)}) async-start(bf16[16,4,768]{2,1,0:T(4,128)(2,1)} %all_to_all.16), calls=%async_computation | async-start | bytes 196608 | tf_op jit(solution)/shard_map/all_to_all | solution.py:68
  173.6 4.8 %fusion = bf16[64,12288]{1,0:T(8,128)(2,1)} fusion(bf16[128,12288]{1,0:T(8,128)(2,1)S(1)} %copy-done, pred[64]{0:T(512)(128)(4,1)S(1)} %compare_bitcast_fusion, bf16[64,12288]{1,0:T(8,128)(2,1)} %reshape.74, bf16[12288,128]{1,0:T(8,128)(2,1)} %param.18, f32[128]{0:T(128)S(1)} %copy-done.2), kind=kOutput, calls=%fused_computation.1 | convolution fusion | flops 404250624 | bytes 9437760 | tf_op jit(solution)/shard_map/dot_general | solution.py:54
  178.4 3.8 %all_to_all.18 = bf16[16,4,12288]{2,1,0:T(4,128)(2,1)} reshape(bf16[64,12288]{1,0:T(8,128)(2,1)} %fusion) | data formatting | bytes 3145728 | tf_op jit(solution)/shard_map/all_to_all | solution.py:69
  182.2 0.0 all-to-all-done
  182.2 6.0 %all-to-all-start.1 = ((bf16[16,4,12288]{2,1,0:T(4,128)(2,1)}), bf16[16,4,12288]{2,1,0:T(4,128)(2,1)}, u32[]{:S(2)}, u32[]{:S(2)}) async-start(bf16[16,4,12288]{2,1,0:T(4,128)(2,1)} %all_to_all.18), calls=%async_computation.1 | async-start | bytes 3145728 | tf_op jit(solution)/shard_map/all_to_all | solution.py:69
  188.2 32.0 %all-to-all-done.1 = bf16[16,4,12288]{2,1,0:T(4,128)(2,1)} async-done(((bf16[16,4,12288]{2,1,0:T(4,128)(2,1)}), bf16[16,4,12288]{2,1,0:T(4,128)(2,1)}, u32[]{:S(2)}, u32[]{:S(2)}) %all-to-all-start.1) | async-done | bytes 1572896 | tf_op jit(solution)/shard_map/all_to_all | solution.py:69
  220.2 2.1 convert_reduce_fusion
  222.3 0.7 add_convert_fusion
  (11 shorter events, 0.1 us)
Async XLA Ops:
  6.5 167.1 %copy-start = (bf16[128,12288]{1,0:T(8,128)(2,1)S(1)}, bf16[128,12288]{1,0:T(8,128)(2,1)}, u32[]{:S(2)}) copy-start(bf16[128,12288]{1,0:T(8,128)(2,1)} %param.20) | copy-start | bytes 9437188
  6.5 46.7 %all-gather.4.cloned.1.call-start = ((), (), s32[]{:S(2)}) async-start(), calls=%async_computation.2 | async-start | bytes 1671168 | tf_op jit(solution)/shard_map/all_gather | solution.py:48
  10.7 134.3 %all-reduce.3.cloned.1.call-start = ((), (), s32[]{:S(2)}) async-start(), calls=%async_computation.3 | async-start | bytes 262144
  15.4 129.7 %copy-start.1 = (f32[512]{0:T(512)S(1)}, f32[512]{0:T(512)}, u32[]{:S(2)}) copy-start(f32[512]{0:T(512)} %param.22) | copy-start | bytes 6148
  56.9 116.7 %copy-start.2 = (f32[128]{0:T(128)S(1)}, f32[128]{0:T(128)}, u32[]{:S(2)}) copy-start(f32[128]{0:T(128)} %param.19) | copy-start | bytes 1540
  170.1 12.1 %all-to-all-start = ((bf16[16,4,768]{2,1,0:T(4,128)(2,1)}), bf16[16,4,768]{2,1,0:T(4,128)(2,1)S(1)}, u32[]{:S(2)}, u32[]{:S(2)}) async-start(bf16[16,4,768]{2,1,0:T(4,128)(2,1)} %all_to_all.16), calls=%async_computation | async-start | bytes 196608 | tf_op jit(solution)/shard_map/all_to_all | solution.py:68
  182.2 38.1 %all-to-all-start.1 = ((bf16[16,4,12288]{2,1,0:T(4,128)(2,1)}), bf16[16,4,12288]{2,1,0:T(4,128)(2,1)}, u32[]{:S(2)}, u32[]{:S(2)}) async-start(bf16[16,4,12288]{2,1,0:T(4,128)(2,1)} %all_to_all.18), calls=%async_computation.1 | async-start | bytes 3145728 | tf_op jit(solution)/shard_map/all_to_all | solution.py:69
Sparse Core Ops, SparseCore 0:
  10.8 42.3 all-gather.3
  59.2 85.8 all-reduce.2
where the time goes:
time: 234 us; the launch traced here: 230 us
  waiting for transfers between devices  156 us (67%)
  blocking collectives  22.2 us (9%)
  between operations  14.2 us (6%)
  local copies, waits for them, and re-layouts  10.5 us (4%)
  starting transfers between devices  9.56 us (4%)
  other arithmetic  9.27 us (4%)
  matrix products  8.25 us (4%)
    unnamed x3, waiting for transfers between devices  86 us
    all_gather x1, waiting for transfers between devices, shards(): every = lax.all_gather(normed, 'blk', axis=0, tiled=True)  37.8 us
    all_to_all x1, waiting for transfers between devices, shards(): lax.all_to_all(result, 'blk', split_axis=0, concat_axis=0, tiled=True)  32 us
    all_gather x1, blocking collectives, shards(): lax.all_gather(low_h, 'blk', axis=0, tiled=True)  22.2 us
    all_to_all x1, starting transfers between devices, shards(): lax.all_to_all(result, 'blk', split_axis=0, concat_axis=0, tiled=True)  6.01 us
    unnamed x10, local copies, waits for them, and re-layouts  5.79 us
    dot_general x1, matrix products, shards(): jnp.dot(act, w_out, preferred_element_type=jnp.float32).astype(jnp.bfloat16)  4.76 us
  transfers between devices with their start and end apart: 4, of which 3 were waited for; matrix products, arithmetic and copies ran while one was open for 4% of the time, Pallas kernels for 0%

commit v1 on v0

--- a/solution.py
+++ b/solution.py
@@ -39,36 +39,81 @@
     low_bias,
     low_out,
 ):
+    f32, bf16 = jnp.float32, jnp.bfloat16
     devices = lax.axis_size("blk")
     position = lax.axis_index("blk")
     row_dev, width = hidden.shape
+    groups = lists.shape[0]
+    mates = devices // groups
+    slots = groups // 2
+    share = low_in.shape[0]
+    plane = position // mates
+    mate = position % mates
+
+    def across(x, k):
+        return x if k == 0 else lax.ppermute(x, "blk", [(i, i ^ (mates * k)) for i in range(devices)])
+
+    def within(x, j):
+        return x if j == 0 else lax.ppermute(x, "blk", [(i, i ^ j) for i in range(devices)])
+
     normed = layer_norm(hidden, ln_gain, ln_shift)
     table = activity(lists, counts, block_slot)
-    share = low_in.shape[0]
-    every = lax.all_gather(normed, "blk", axis=0, tiled=True)
-    columns = lax.dynamic_slice_in_dim(every, position * share, share, 1)
-    row_table = jnp.repeat(table, GROUP, axis=0)
-    owner_flags = lax.dynamic_slice_in_dim(row_table, position, 1, 1)[:, 0]
-    pre = jnp.dot(every, w_in, preferred_element_type=jnp.float32) + b_in
-    act = jnp.maximum(pre, 0.0).astype(jnp.bfloat16)
-    dense_part = jnp.dot(act, w_out, preferred_element_type=jnp.float32).astype(jnp.bfloat16)
-    result = jnp.where(owner_flags[:, None] > 0, dense_part, jnp.zeros_like(dense_part))
-    lowz = lax.psum_scatter(
-        jnp.dot(columns, low_in, preferred_element_type=jnp.float32),
-        "blk",
-        scatter_dimension=0,
-        tiled=True,
-    )
-    low_h = jnp.maximum(lowz + low_bias, 0.0).astype(jnp.bfloat16)
+    mine = lax.dynamic_slice_in_dim(table, plane * mates, mates, 1)
+    order = jnp.arange(mates, dtype=jnp.int32) ^ mate
+    mine = mine[:, order]
+    rank = jnp.cumsum(mine, axis=0) - mine
+    hot = (mine[:, :, None] > 0) & (rank[:, :, None] == jnp.arange(slots)[None, None, :])
+    pick = jnp.sum(jnp.where(hot, jnp.arange(groups, dtype=jnp.int32)[:, None, None], 0), axis=0)
+    seat = pick ^ plane
+
+    held = jnp.stack([across(normed, k) for k in range(groups)])
+    rows, lows = [], []
+    for j in range(mates):
+        wanted = jnp.stack([lax.dynamic_index_in_dim(held, seat[j, s], 0, False) for s in range(slots)])
+        rows.append(within(wanted, j))
+        cols = lax.dynamic_slice_in_dim(held, (position ^ j) * share, share, 2)
+        lows.append(within(cols, j))
+    x = jnp.stack(rows)
+    x = x[order].transpose(1, 0, 2, 3).reshape(slots * GROUP, width)
+    xl = jnp.stack(lows).reshape(mates * groups * row_dev, share)
+    partial = jnp.dot(xl, low_in, preferred_element_type=f32).reshape(mates, groups, row_dev, -1)
+    summed = sum(within(partial[j], j) for j in range(mates))
+    lowz = 0.0
+    for k in range(groups):
+        got = across(summed, k)
+        lowz = lowz + jnp.stack([got[q ^ k] for q in range(groups)])
+    low_h = jnp.maximum(lowz + low_bias, 0.0).astype(bf16)
+    all_h = jnp.stack([within(low_h, j) for j in range(mates)])
     low_cols = jnp.dot(
-        lax.all_gather(low_h, "blk", axis=0, tiled=True),
-        low_out,
-        preferred_element_type=jnp.float32,
-    ).astype(jnp.bfloat16)
-    low_y = lax.all_to_all(low_cols, "blk", split_axis=0, concat_axis=1, tiled=True)
-    returned = lax.all_to_all(result, "blk", split_axis=0, concat_axis=0, tiled=True)
-    sparse = jnp.sum(returned.reshape(devices, row_dev, width), axis=0, dtype=jnp.float32)
-    return (low_y.astype(jnp.float32) + sparse).astype(jnp.bfloat16)
+        all_h.reshape(mates * groups * row_dev, -1), low_out, preferred_element_type=f32
+    ).astype(bf16).reshape(mates, groups, row_dev, share)
+
+    pre = jnp.dot(x, w_in, preferred_element_type=f32) + b_in
+    act = jnp.maximum(pre, 0.0).astype(bf16)
+    part = jnp.dot(act, w_out, preferred_element_type=f32).astype(bf16)
+    part = part.reshape(slots, mates, row_dev, width)
+
+    back = [within(lax.dynamic_index_in_dim(part, mate ^ j, 1, False), j) for j in range(mates)]
+    low_back = jnp.stack([within(low_cols[j], j) for j in range(mates)])[order]
+    low_back = low_back.transpose(1, 2, 0, 3).reshape(groups, row_dev, mates * share)
+    live = hot.astype(f32)
+    total = None
+    for k in range(groups):
+        group = plane ^ k
+        flags = lax.dynamic_index_in_dim(live, group, 0, False)
+        partsum = jnp.zeros((row_dev, width), f32)
+        for j in range(mates):
+            for s in range(slots):
+                partsum = partsum + jnp.where(flags[j, s] > 0, back[j][s].astype(f32), 0.0)
+        here = lax.dynamic_slice_in_dim(partsum, plane * mates * share, mates * share, 1)
+        partsum = lax.dynamic_update_slice_in_dim(
+            partsum, here + low_back[k].astype(f32), plane * mates * share, 1
+        )
+        if k == 0:
+            total = partsum
+        else:
+            total = total + across(partsum.astype(bf16), k).astype(f32)
+    return total.astype(bf16)
 
 
 def solution(mesh):

time: 234 us -> 147 us (0.63); the launches traced: 230 us -> 146 us
  waiting for transfers between devices: 156 us -> 22.2 us
  blocking collectives: 22.2 us -> 0 us
  between operations: 14.2 us -> 35.3 us
  local copies, waits for them, and re-layouts: 10.5 us -> 29.1 us
  starting transfers between devices: 9.56 us -> 26.2 us
  other arithmetic: 9.27 us -> 25.8 us
    unnamed x3 -> x0, waiting for transfers between devices: 86 us -> none
    all_gather x1 -> x0, waiting for transfers between devices: 37.8 us -> none  [shards(): every = lax.all_gather(normed, 'blk', axis=0, tiled=True)]
    all_to_all x2 -> x0, waiting for transfers between devices: 32 us -> none  [the longest x1 32 us: shards(): lax.all_to_all(result, 'blk', split_axis=0, concat_axis=0, tiled=True)]
    ppermute x0 -> x27, starting transfers between devices: none -> 26.2 us  [the longest x9 14.5 us: across(): lax.ppermute(x, 'blk', [(i, i ^ mates * k) for i in range(devices)])]
    all_gather x1 -> x0, blocking collectives: 22.2 us -> none  [shards(): lax.all_gather(low_h, 'blk', axis=0, tiled=True)]
    ppermute x0 -> x27, waiting for transfers between devices: none -> 22.2 us  [the longest x18 14.2 us: within(): lax.ppermute(x, 'blk', [(i, i ^ j) for i in range(devices)])]
    another operation x0 -> x11, other arithmetic: none -> 13.9 us  [the longest x3 5.29 us: shards(): jnp.stack([lax.dynamic_index_in_dim(held, seat[j, s], 0, False) for s in...]
    all_to_all x2 -> x0, starting transfers between devices: 9.52 us -> none  [the longest x1 6.01 us: shards(): lax.all_to_all(result, 'blk', split_axis=0, concat_axis=0, tiled=True)]
  transfers between devices with their start and end apart: 4 -> 27, of which waited for: 3 -> 10; matrix products, arithmetic and copies ran while one was open for 4% -> 17% of each run, Pallas kernels for 0% -> 0%
where the time goes in v1:
time: 147 us; the launch traced here: 146 us
  between operations  35.3 us (24%)
  local copies, waits for them, and re-layouts  29.1 us (20%)
  starting transfers between devices  26.2 us (18%)
  other arithmetic  25.8 us (18%)
  waiting for transfers between devices  22.2 us (15%)
  matrix products  6.98 us (5%)
    ppermute x9, starting transfers between devices, across(): lax.ppermute(x, 'blk', [(i, i ^ mates * k) for i in range(devices)])  14.5 us
    ppermute x18, waiting for transfers between devices, within(): lax.ppermute(x, 'blk', [(i, i ^ j) for i in range(devices)])  14.2 us
    ppermute x18, starting transfers between devices, within(): lax.ppermute(x, 'blk', [(i, i ^ j) for i in range(devices)])  11.7 us
    ppermute x9, waiting for transfers between devices, across(): lax.ppermute(x, 'blk', [(i, i ^ mates * k) for i in range(devices)])  7.98 us
    another operation x3, other arithmetic, shards(): jnp.stack([lax.dynamic_index_in_dim(held, seat[j, s], 0, False) for s in...  5.29 us
    squeeze x4, local copies, waits for them, and re-layouts, shards(): summed = sum((within(partial[j], j) for j in range(mates)))  4.93 us
    dot_general x1, matrix products, shards(): part = jnp.dot(act, w_out, preferred_element_type=f32).astype(bf16)  4.15 us
    gather x1, local copies, waits for them, and re-layouts, shards(): x = x[order].transpose(1, 0, 2, 3).reshape(slots * GROUP, width)  3.33 us
  transfers between devices with their start and end apart: 27, of which 10 were waited for; matrix products, arithmetic and copies ran while one was open for 17% of the time, Pallas kernels for 0%

profile of v1, /device:TPU:0, one launch (start us, length us, event | category | flops | bytes accessed | tf_op | source)
XLA Modules:
  0.0 145.6 jit_solution(11335266653143330313)
XLA Ops:
  3.5 4.1 %collective-permute-start.1 = (bf16[4,12288]{1,0:T(4,128)(2,1)S(1)}, bf16[4,12288]{1,0:T(4,128)(2,1)S(1)}, u32[]{:S(2)}, u32[]{:S(2)}) collective-permute-start(bf16[4,12288]{1,0:T(4,128)(2,1)S(1)} %fusion.7), channel_id=1, source_target_pairs={{0,8},{1,9},{2,10},{3,11},{4,12},{5,13},{6,14},{7,15},{8,0},{9,1},... | collective-permute-start | bytes 294920 | tf_op jit(solution)/shard_map/ppermute | solution.py:54
  7.6 1.6 %collective-permute-start = (bf16[4,12288]{1,0:T(4,128)(2,1)S(1)}, bf16[4,12288]{1,0:T(4,128)(2,1)S(1)}, u32[]{:S(2)}, u32[]{:S(2)}) collective-permute-start(bf16[4,12288]{1,0:T(4,128)(2,1)S(1)} %fusion.7), channel_id=1, source_target_pairs={{0,4},{1,5},{2,6},{3,7},{4,0},{5,1},{6,2},{7,3},{8,12},{9,13},{10,... | collective-permute-start | bytes 294920 | tf_op jit(solution)/shard_map/ppermute | solution.py:54
  15.3 1.7 %fusion.103 = bf16[1,4,12288]{2,1,0:T(4,128)(2,1)} fusion(f32[12288]{0:T(1024)} %param.14, f32[12288]{0:T(1024)} %param.13, f32[4]{0:T(128)} %copy-done.10, f32[4]{0:T(128)} %copy-done.8, bf16[4,12288]{1,0:T(4,128)(2,1)} %param.12), kind=kLoop, calls=%fused_computation.186 | loop fusion | flops 294912 | bytes 294944 | tf_op jit(solution)/shard_map/stack | solution.py:69
  19.2 1.4 pad_maximum_fusion.1
  58.7 1.5 %pad_maximum_fusion.5 = bf16[4,4,4,768]{3,2,1,0:T(4,128)(2,1)} fusion(bf16[1,4,4,768]{3,2,1,0:T(4,128)(2,1)} %bitcast.41, bf16[1,4,4,768]{3,2,1,0:T(4,128)(2,1)} %bitcast.40, bf16[1,4,4,768]{3,2,1,0:T(4,128)(2,1)} %bitcast.39, bf16[1,4,4,768]{3,2,1,0:T(4,128)(2,1)} %get-tuple-element.8), kind=kLoop, calls=%fused_computation.114 | loop fusion | flops 147456 | bytes 196608 | tf_op jit(solution)/shard_map/stack | solution.py:78
  60.2 1.6 %reshape.349 = bf16[64,768]{1,0:T(8,128)(2,1)} reshape(bf16[4,4,4,768]{3,2,1,0:T(4,128)(2,1)} %pad_maximum_fusion.5) | data formatting | bytes 196608 | tf_op jit(solution)/shard_map/reshape | solution.py:78
  61.8 1.4 fusion.95
  63.9 1.4 squeeze.76
  68.0 1.7 %collective-permute-start.13 = (f32[4,4,512]{2,1,0:T(4,128)}, f32[4,4,512]{2,1,0:T(4,128)}, u32[]{:S(2)}, u32[]{:S(2)}) collective-permute-start(f32[4,4,512]{2,1,0:T(4,128)} %squeeze.77), channel_id=1, source_target_pairs={{0,2},{1,3},{2,0},{3,1},{4,6},{5,7},{6,4},{7,5},{8,10},{9,11},{10,... | collective-permute-start | bytes 98312 | tf_op jit(solution)/shard_map/ppermute | solution.py:57
  74.4 1.8 %collective-permute-start.16 = (f32[4,4,512]{2,1,0:T(4,128)S(1)}, f32[4,4,512]{2,1,0:T(4,128)S(1)}, u32[]{:S(2)}, u32[]{:S(2)}) collective-permute-start(f32[4,4,512]{2,1,0:T(4,128)S(1)} %bitcast.258), channel_id=1, source_target_pairs={{0,8},{1,9},{2,10},{3,11},{4,12},{5,13},{6,14},{7,15},{8,0},{9,1},... | collective-permute-start | bytes 98312 | tf_op jit(solution)/shard_map/ppermute | solution.py:54
  76.2 1.8 %pad_maximum_fusion.2 = bf16[2,4,12288]{2,1,0:T(4,128)(2,1)} fusion(bf16[1,4,12288]{2,1,0:T(4,128)(2,1)} %get-tuple-element.17, bf16[1,4,12288]{2,1,0:T(4,128)(2,1)} %get-tuple-element.18), kind=kLoop, calls=%fused_computation.107 | loop fusion | flops 98304 | bytes 393216 | tf_op jit(solution)/shard_map/stack | solution.py:72
  77.9 1.9 %collective-permute-start.17 = (f32[4,4,512]{2,1,0:T(4,128)S(1)}, f32[4,4,512]{2,1,0:T(4,128)S(1)}, u32[]{:S(2)}, u32[]{:S(2)}) collective-permute-start(f32[4,4,512]{2,1,0:T(4,128)S(1)} %bitcast.259), channel_id=1, source_target_pairs={{0,12},{1,13},{2,14},{3,15},{4,8},{5,9},{6,10},{7,11},{8,4},{9,5},... | collective-permute-start | bytes 98312 | tf_op jit(solution)/shard_map/ppermute | solution.py:54
  80.4 3.3 %collective-permute-done.17 = f32[4,4,512]{2,1,0:T(4,128)S(1)} collective-permute-done((f32[4,4,512]{2,1,0:T(4,128)S(1)}, f32[4,4,512]{2,1,0:T(4,128)S(1)}, u32[]{:S(2)}, u32[]{:S(2)}) %collective-permute-start.17) | collective-permute-done | bytes 32800 | tf_op jit(solution)/shard_map/ppermute | solution.py:54
  84.2 1.4 collective-permute-start.19
  86.1 1.7 %pad_maximum_fusion.3 = bf16[2,4,12288]{2,1,0:T(4,128)(2,1)} fusion(bf16[1,4,12288]{2,1,0:T(4,128)(2,1)} %get-tuple-element.15, bf16[1,4,12288]{2,1,0:T(4,128)(2,1)} %get-tuple-element.16), kind=kLoop, calls=%fused_computation.108 | loop fusion | flops 98304 | bytes 393216 | tf_op jit(solution)/shard_map/stack | solution.py:72
  88.5 1.4 convolution_convert_fusion.1
  90.6 1.8 %pad_maximum_fusion.4 = bf16[2,4,12288]{2,1,0:T(4,128)(2,1)} fusion(bf16[1,4,12288]{2,1,0:T(4,128)(2,1)} %get-tuple-element.13, bf16[1,4,12288]{2,1,0:T(4,128)(2,1)} %get-tuple-element.14), kind=kLoop, calls=%fused_computation.109 | loop fusion | flops 98304 | bytes 393216 | tf_op jit(solution)/shard_map/stack | solution.py:72
  92.4 1.5 %collective-permute-start.5 = (bf16[2,4,12288]{2,1,0:T(4,128)(2,1)}, bf16[2,4,12288]{2,1,0:T(4,128)(2,1)}, u32[]{:S(2)}, u32[]{:S(2)}) collective-permute-start(bf16[2,4,12288]{2,1,0:T(4,128)(2,1)} %pad_maximum_fusion.4), channel_id=1, source_target_pairs={{0,3},{1,2},{2,1},{3,0},{4,7},{5,6},{6,5},{7,4},{8,11},{9,10},{10,... | collective-permute-start | bytes 589832 | tf_op jit(solution)/shard_map/ppermute | solution.py:57
  97.4 3.3 %collective-permute-done.22 = bf16[4,4,768]{2,1,0:T(4,128)(2,1)} collective-permute-done((bf16[4,4,768]{2,1,0:T(4,128)(2,1)}, bf16[4,4,768]{2,1,0:T(4,128)(2,1)}, u32[]{:S(2)}, u32[]{:S(2)}) %collective-permute-start.22) | collective-permute-done | bytes 24608 | tf_op jit(solution)/shard_map/ppermute | solution.py:57
  102.4 2.7 %pad_maximum_fusion = bf16[4,2,4,12288]{3,2,1,0:T(4,128)(2,1)} fusion(bf16[1,2,4,12288]{3,2,1,0:T(4,128)(2,1)} %bitcast.19, bf16[1,2,4,12288]{3,2,1,0:T(4,128)(2,1)} %bitcast.16, bf16[1,2,4,12288]{3,2,1,0:T(4,128)(2,1)} %bitcast.13, bf16[1,2,4,12288]{3,2,1,0:T(4,128)(2,1)S(1)} %maximum_bitcast_fusion), kind=kLoop, calls=%fused_computation.8 | loop fusion | flops 1179648 | bytes 1572864 | tf_op jit(solution)/shard_map/stack | solution.py:76
  105.1 3.3 %gather_fusion.1 = bf16[4,2,4,12288]{3,2,1,0:T(4,128)(2,1)} fusion(bf16[4,2,4,12288]{3,2,1,0:T(4,128)(2,1)} %pad_maximum_fusion, s32[1024]{0:T(1024)} %pad_clamp_fusion), kind=kCustom, calls=%fused_computation.1 | custom fusion | bytes 1572880 | tf_op jit(solution)/shard_map/gather | solution.py:77
  108.4 2.3 %copy.28 = bf16[2,4,4,12288]{3,2,1,0:T(4,128)(2,1)} copy(bf16[2,4,4,12288]{3,2,0,1:T(4,128)(2,1)} %bitcast.255) | data formatting | bytes 1572864 | tf_op jit(solution)/shard_map/transpose | solution.py:77
  110.7 2.3 %reshape.347 = bf16[32,12288]{1,0:T(8,128)(2,1)} reshape(bf16[2,4,4,12288]{3,2,1,0:T(4,128)(2,1)} %copy.28) | data formatting | bytes 1572864 | tf_op jit(solution)/shard_map/reshape | solution.py:77
  113.0 4.2 %convolution_convert_fusion = bf16[32,12288]{1,0:T(8,128)(2,1)} fusion(bf16[128,12288]{1,0:T(8,128)(2,1)S(1)} %copy-done, bf16[32,12288]{1,0:T(8,128)(2,1)} %reshape.347, bf16[12288,128]{1,0:T(8,128)(2,1)} %param.18, f32[128]{0:T(128)S(1)} %copy-done.11), kind=kOutput, calls=%fused_computation.3 | convolution fusion | flops 201732096 | bytes 7864832 | tf_op jit(solution)/shard_map/dot_general | solution.py:93
  117.2 2.4 %reshape.348 = bf16[2,4,4,12288]{3,2,1,0:T(4,128)(2,1)} reshape(bf16[32,12288]{1,0:T(8,128)(2,1)} %convolution_convert_fusion) | data formatting | bytes 1572864 | tf_op jit(solution)/shard_map/reshape | solution.py:94
  119.6 1.4 dynamic-slice_bitcast_fusion.2
  121.2 1.5 %collective-permute-start.8 = (bf16[2,4,12288]{2,1,0:T(4,128)(2,1)S(1)}, bf16[2,4,12288]{2,1,0:T(4,128)(2,1)S(1)}, u32[]{:S(2)}, u32[]{:S(2)}) collective-permute-start(bf16[2,4,12288]{2,1,0:T(4,128)(2,1)S(1)} %get-tuple-element.6), channel_id=1, source_target_pairs={{0,3},{1,2},{2,1},{3,0},{4,7},{5,6},{6,5},{7,4},{8,11},{9,10},{10,... | collective-permute-start | bytes 589832 | tf_op jit(solution)/shard_map/ppermute | solution.py:57
  123.3 4.6 %collective-permute-done.8 = bf16[2,4,12288]{2,1,0:T(4,128)(2,1)S(1)} collective-permute-done((bf16[2,4,12288]{2,1,0:T(4,128)(2,1)S(1)}, bf16[2,4,12288]{2,1,0:T(4,128)(2,1)S(1)}, u32[]{:S(2)}, u32[]{:S(2)}) %collective-permute-start.8) | collective-permute-done | bytes 196640 | tf_op jit(solution)/shard_map/ppermute | solution.py:57
  127.9 4.7 %collective-permute-done.7 = bf16[2,4,12288]{2,1,0:T(4,128)(2,1)S(1)} collective-permute-done((bf16[2,4,12288]{2,1,0:T(4,128)(2,1)S(1)}, bf16[2,4,12288]{2,1,0:T(4,128)(2,1)S(1)}, u32[]{:S(2)}, u32[]{:S(2)}) %collective-permute-start.7) | collective-permute-done | bytes 196640 | tf_op jit(solution)/shard_map/ppermute | solution.py:57
  133.9 1.8 %collective-permute-start.25 = (bf16[4,12288]{1,0:T(4,128)(2,1)S(1)}, bf16[4,12288]{1,0:T(4,128)(2,1)S(1)}, u32[]{:S(2)}, u32[]{:S(2)}) collective-permute-start(bf16[4,12288]{1,0:T(4,128)(2,1)S(1)} %convert_element_type.167), channel_id=1, source_target_pairs={{0,8},{1,9},{2,10},{3,11},{4,12},{5,13},{6,14},{7,15},{8,0},{9,1},... | collective-permute-start | bytes 294920 | tf_op jit(solution)/shard_map/ppermute | solution.py:54
  138.3 1.9 %collective-permute-start.26 = (bf16[4,12288]{1,0:T(4,128)(2,1)S(1)}, bf16[4,12288]{1,0:T(4,128)(2,1)S(1)}, u32[]{:S(2)}, u32[]{:S(2)}) collective-permute-start(bf16[4,12288]{1,0:T(4,128)(2,1)S(1)} %convert_element_type.171), channel_id=1, source_target_pairs={{0,12},{1,13},{2,14},{3,15},{4,8},{5,9},{6,10},{7,11},{8,4},{9,5},... | collective-permute-start | bytes 294920 | tf_op jit(solution)/shard_map/ppermute | solution.py:54
  141.7 1.9 %collective-permute-done.24 = bf16[4,12288]{1,0:T(4,128)(2,1)S(1)} collective-permute-done((bf16[4,12288]{1,0:T(4,128)(2,1)S(1)}, bf16[4,12288]{1,0:T(4,128)(2,1)S(1)}, u32[]{:S(2)}, u32[]{:S(2)}) %collective-permute-start.24) | collective-permute-done | bytes 98336 | tf_op jit(solution)/shard_map/ppermute | solution.py:54
  (124 shorter events, 39.1 us)
Async XLA Ops:
  0.0 113.0 %copy-start = (bf16[128,12288]{1,0:T(8,128)(2,1)S(1)}, bf16[128,12288]{1,0:T(8,128)(2,1)}, u32[]{:S(2)}) copy-start(bf16[128,12288]{1,0:T(8,128)(2,1)} %param.20) | copy-start | bytes 9437188
  3.5 14.9 %collective-permute-start.1 = (bf16[4,12288]{1,0:T(4,128)(2,1)S(1)}, bf16[4,12288]{1,0:T(4,128)(2,1)S(1)}, u32[]{:S(2)}, u32[]{:S(2)}) collective-permute-start(bf16[4,12288]{1,0:T(4,128)(2,1)S(1)} %fusion.7), channel_id=1, source_target_pairs={{0,8},{1,9},{2,10},{3,11},{4,12},{5,13},{6,14},{7,15},{8,0},{9,1},... | collective-permute-start | bytes 294920 | tf_op jit(solution)/shard_map/ppermute | solution.py:54
  7.6 10.9 %collective-permute-start = (bf16[4,12288]{1,0:T(4,128)(2,1)S(1)}, bf16[4,12288]{1,0:T(4,128)(2,1)S(1)}, u32[]{:S(2)}, u32[]{:S(2)}) collective-permute-start(bf16[4,12288]{1,0:T(4,128)(2,1)S(1)} %fusion.7), channel_id=1, source_target_pairs={{0,4},{1,5},{2,6},{3,7},{4,0},{5,1},{6,2},{7,3},{8,12},{9,13},{10,... | collective-permute-start | bytes 294920 | tf_op jit(solution)/shard_map/ppermute | solution.py:54
  9.2 9.3 %collective-permute-start.2 = (bf16[4,12288]{1,0:T(4,128)(2,1)S(1)}, bf16[4,12288]{1,0:T(4,128)(2,1)S(1)}, u32[]{:S(2)}, u32[]{:S(2)}) collective-permute-start(bf16[4,12288]{1,0:T(4,128)(2,1)S(1)} %fusion.7), channel_id=1, source_target_pairs={{0,12},{1,13},{2,14},{3,15},{4,8},{5,9},{6,10},{7,11},{8,4},{9,5},... | collective-permute-start | bytes 294920 | tf_op jit(solution)/shard_map/ppermute | solution.py:54
  12.1 72.0 %copy-start.9 = (f32[512]{0:T(512)S(1)}, f32[512]{0:T(512)}, u32[]{:S(2)}) copy-start(f32[512]{0:T(512)} %param.22) | copy-start | bytes 6148
  21.2 37.5 %collective-permute-start.11 = (bf16[4,4,768]{2,1,0:T(4,128)(2,1)}, bf16[4,4,768]{2,1,0:T(4,128)(2,1)}, u32[]{:S(2)}, u32[]{:S(2)}) collective-permute-start(bf16[4,4,768]{2,1,0:T(4,128)(2,1)} %get-tuple-element.9), channel_id=1, source_target_pairs={{0,3},{1,2},{2,1},{3,0},{4,7},{5,6},{6,5},{7,4},{8,11},{9,10},{10,... | collective-permute-start | bytes 73736 | tf_op jit(solution)/shard_map/ppermute | solution.py:57
  21.6 37.1 %collective-permute-start.10 = (bf16[4,4,768]{2,1,0:T(4,128)(2,1)}, bf16[4,4,768]{2,1,0:T(4,128)(2,1)}, u32[]{:S(2)}, u32[]{:S(2)}) collective-permute-start(bf16[4,4,768]{2,1,0:T(4,128)(2,1)} %get-tuple-element.10), channel_id=1, source_target_pairs={{0,2},{1,3},{2,0},{3,1},{4,6},{5,7},{6,4},{7,5},{8,10},{9,11},{10,... | collective-permute-start | bytes 73736 | tf_op jit(solution)/shard_map/ppermute | solution.py:57
  23.0 35.8 %collective-permute-start.9 = (bf16[4,4,768]{2,1,0:T(4,128)(2,1)}, bf16[4,4,768]{2,1,0:T(4,128)(2,1)}, u32[]{:S(2)}, u32[]{:S(2)}) collective-permute-start(bf16[4,4,768]{2,1,0:T(4,128)(2,1)} %get-tuple-element.11), channel_id=1, source_target_pairs={{0,1},{1,0},{2,3},{3,2},{4,5},{5,4},{6,7},{7,6},{8,9},{9,8},{10,11... | collective-permute-start | bytes 73736 | tf_op jit(solution)/shard_map/ppermute | solution.py:57
  68.0 4.2 %collective-permute-start.13 = (f32[4,4,512]{2,1,0:T(4,128)}, f32[4,4,512]{2,1,0:T(4,128)}, u32[]{:S(2)}, u32[]{:S(2)}) collective-permute-start(f32[4,4,512]{2,1,0:T(4,128)} %squeeze.77), channel_id=1, source_target_pairs={{0,2},{1,3},{2,0},{3,1},{4,6},{5,7},{6,4},{7,5},{8,10},{9,11},{10,... | collective-permute-start | bytes 98312 | tf_op jit(solution)/shard_map/ppermute | solution.py:57
  69.7 3.9 %collective-permute-start.14 = (f32[4,4,512]{2,1,0:T(4,128)}, f32[4,4,512]{2,1,0:T(4,128)}, u32[]{:S(2)}, u32[]{:S(2)}) collective-permute-start(f32[4,4,512]{2,1,0:T(4,128)} %squeeze.78), channel_id=1, source_target_pairs={{0,3},{1,2},{2,1},{3,0},{4,7},{5,6},{6,5},{7,4},{8,11},{9,10},{10,... | collective-permute-start | bytes 98312 | tf_op jit(solution)/shard_map/ppermute | solution.py:57
  69.7 3.9 %collective-permute-start.12 = (f32[4,4,512]{2,1,0:T(4,128)}, f32[4,4,512]{2,1,0:T(4,128)}, u32[]{:S(2)}, u32[]{:S(2)}) collective-permute-start(f32[4,4,512]{2,1,0:T(4,128)} %squeeze.76), channel_id=1, source_target_pairs={{0,1},{1,0},{2,3},{3,2},{4,5},{5,4},{6,7},{7,6},{8,9},{9,8},{10,11... | collective-permute-start | bytes 98312 | tf_op jit(solution)/shard_map/ppermute | solution.py:57
  71.2 25.3 %copy-start.2 = (bf16[1,4,12288]{2,1,0:T(4,128)(2,1)S(1)}, bf16[1,4,12288]{2,1,0:T(4,128)(2,1)}, u32[]{:S(2)}) copy-start(bf16[1,4,12288]{2,1,0:T(4,128)(2,1)} %get-tuple-element.12) | copy-start | bytes 294916
  71.2 25.3 %copy-start.3 = (bf16[1,4,12288]{2,1,0:T(4,128)(2,1)S(1)}, bf16[1,4,12288]{2,1,0:T(4,128)(2,1)}, u32[]{:S(2)}) copy-start(bf16[1,4,12288]{2,1,0:T(4,128)(2,1)} %get-tuple-element.19) | copy-start | bytes 294916
  74.4 6.0 %collective-permute-start.16 = (f32[4,4,512]{2,1,0:T(4,128)S(1)}, f32[4,4,512]{2,1,0:T(4,128)S(1)}, u32[]{:S(2)}, u32[]{:S(2)}) collective-permute-start(f32[4,4,512]{2,1,0:T(4,128)S(1)} %bitcast.258), channel_id=1, source_target_pairs={{0,8},{1,9},{2,10},{3,11},{4,12},{5,13},{6,14},{7,15},{8,0},{9,1},... | collective-permute-start | bytes 98312 | tf_op jit(solution)/shard_map/ppermute | solution.py:54
  77.9 24.4 %collective-permute-start.3 = (bf16[2,4,12288]{2,1,0:T(4,128)(2,1)}, bf16[2,4,12288]{2,1,0:T(4,128)(2,1)}, u32[]{:S(2)}, u32[]{:S(2)}) collective-permute-start(bf16[2,4,12288]{2,1,0:T(4,128)(2,1)} %pad_maximum_fusion.2), channel_id=1, source_target_pairs={{0,1},{1,0},{2,3},{3,2},{4,5},{5,4},{6,7},{7,6},{8,9},{9,8},{10,11... | collective-permute-start | bytes 589832 | tf_op jit(solution)/shard_map/ppermute | solution.py:57
  77.9 5.8 %collective-permute-start.17 = (f32[4,4,512]{2,1,0:T(4,128)S(1)}, f32[4,4,512]{2,1,0:T(4,128)S(1)}, u32[]{:S(2)}, u32[]{:S(2)}) collective-permute-start(f32[4,4,512]{2,1,0:T(4,128)S(1)} %bitcast.259), channel_id=1, source_target_pairs={{0,12},{1,13},{2,14},{3,15},{4,8},{5,9},{6,10},{7,11},{8,4},{9,5},... | collective-permute-start | bytes 98312 | tf_op jit(solution)/shard_map/ppermute | solution.py:54
  79.9 4.2 %collective-permute-start.15 = (f32[4,4,512]{2,1,0:T(4,128)S(1)}, f32[4,4,512]{2,1,0:T(4,128)S(1)}, u32[]{:S(2)}, u32[]{:S(2)}) collective-permute-start(f32[4,4,512]{2,1,0:T(4,128)S(1)} %bitcast.260), channel_id=1, source_target_pairs={{0,4},{1,5},{2,6},{3,7},{4,0},{5,1},{6,2},{7,3},{8,12},{9,13},{10,... | collective-permute-start | bytes 98312 | tf_op jit(solution)/shard_map/ppermute | solution.py:54
  84.1 4.3 %collective-permute-start.20 = (bf16[4,4,512]{2,1,0:T(4,128)(2,1)S(1)}, bf16[4,4,512]{2,1,0:T(4,128)(2,1)S(1)}, u32[]{:S(2)}, u32[]{:S(2)}) collective-permute-start(bf16[4,4,512]{2,1,0:T(4,128)(2,1)S(1)} %fusion.72), channel_id=1, source_target_pairs={{0,3},{1,2},{2,1},{3,0},{4,7},{5,6},{6,5},{7,4},{8,11},{9,10},{10,... | collective-permute-start | bytes 49160 | tf_op jit(solution)/shard_map/ppermute | solution.py:57
  84.2 4.2 %collective-permute-start.19 = (bf16[4,4,512]{2,1,0:T(4,128)(2,1)S(1)}, bf16[4,4,512]{2,1,0:T(4,128)(2,1)S(1)}, u32[]{:S(2)}, u32[]{:S(2)}) collective-permute-start(bf16[4,4,512]{2,1,0:T(4,128)(2,1)S(1)} %fusion.72), channel_id=1, source_target_pairs={{0,2},{1,3},{2,0},{3,1},{4,6},{5,7},{6,4},{7,5},{8,10},{9,11},{10,... | collective-permute-start | bytes 49160 | tf_op jit(solution)/shard_map/ppermute | solution.py:57
  85.7 2.8 %collective-permute-start.18 = (bf16[4,4,512]{2,1,0:T(4,128)(2,1)S(1)}, bf16[4,4,512]{2,1,0:T(4,128)(2,1)S(1)}, u32[]{:S(2)}, u32[]{:S(2)}) collective-permute-start(bf16[4,4,512]{2,1,0:T(4,128)(2,1)S(1)} %fusion.72), channel_id=1, source_target_pairs={{0,1},{1,0},{2,3},{3,2},{4,5},{5,4},{6,7},{7,6},{8,9},{9,8},{10,11... | collective-permute-start | bytes 49160 | tf_op jit(solution)/shard_map/ppermute | solution.py:57
  87.8 14.5 %collective-permute-start.4 = (bf16[2,4,12288]{2,1,0:T(4,128)(2,1)}, bf16[2,4,12288]{2,1,0:T(4,128)(2,1)}, u32[]{:S(2)}, u32[]{:S(2)}) collective-permute-start(bf16[2,4,12288]{2,1,0:T(4,128)(2,1)} %pad_maximum_fusion.3), channel_id=1, source_target_pairs={{0,2},{1,3},{2,0},{3,1},{4,6},{5,7},{6,4},{7,5},{8,10},{9,11},{10,... | collective-permute-start | bytes 589832 | tf_op jit(solution)/shard_map/ppermute | solution.py:57
  90.5 5.2 %collective-permute-start.21 = (bf16[4,4,768]{2,1,0:T(4,128)(2,1)S(1)}, bf16[4,4,768]{2,1,0:T(4,128)(2,1)S(1)}, u32[]{:S(2)}, u32[]{:S(2)}) collective-permute-start(bf16[4,4,768]{2,1,0:T(4,128)(2,1)S(1)} %squeeze.79), channel_id=1, source_target_pairs={{0,1},{1,0},{2,3},{3,2},{4,5},{5,4},{6,7},{7,6},{8,9},{9,8},{10,11... | collective-permute-start | bytes 73736 | tf_op jit(solution)/shard_map/ppermute | solution.py:57
  92.4 10.0 %collective-permute-start.5 = (bf16[2,4,12288]{2,1,0:T(4,128)(2,1)}, bf16[2,4,12288]{2,1,0:T(4,128)(2,1)}, u32[]{:S(2)}, u32[]{:S(2)}) collective-permute-start(bf16[2,4,12288]{2,1,0:T(4,128)(2,1)} %pad_maximum_fusion.4), channel_id=1, source_target_pairs={{0,3},{1,2},{2,1},{3,0},{4,7},{5,6},{6,5},{7,4},{8,11},{9,10},{10,... | collective-permute-start | bytes 589832 | tf_op jit(solution)/shard_map/ppermute | solution.py:57
  95.1 5.6 %collective-permute-start.22 = (bf16[4,4,768]{2,1,0:T(4,128)(2,1)}, bf16[4,4,768]{2,1,0:T(4,128)(2,1)}, u32[]{:S(2)}, u32[]{:S(2)}) collective-permute-start(bf16[4,4,768]{2,1,0:T(4,128)(2,1)} %squeeze.80), channel_id=1, source_target_pairs={{0,2},{1,3},{2,0},{3,1},{4,6},{5,7},{6,4},{7,5},{8,10},{9,11},{10,... | collective-permute-start | bytes 73736 | tf_op jit(solution)/shard_map/ppermute | solution.py:57
  95.7 5.0 %collective-permute-start.23 = (bf16[4,4,768]{2,1,0:T(4,128)(2,1)}, bf16[4,4,768]{2,1,0:T(4,128)(2,1)}, u32[]{:S(2)}, u32[]{:S(2)}) collective-permute-start(bf16[4,4,768]{2,1,0:T(4,128)(2,1)} %squeeze.81), channel_id=1, source_target_pairs={{0,3},{1,2},{2,1},{3,0},{4,7},{5,6},{6,5},{7,4},{8,11},{9,10},{10,... | collective-permute-start | bytes 73736 | tf_op jit(solution)/shard_map/ppermute | solution.py:57
  119.6 18.3 %copy-start.1 = (bf16[2,4,4,12288]{3,2,1,0:T(4,128)(2,1)S(1)}, bf16[2,4,4,12288]{3,2,1,0:T(4,128)(2,1)}, u32[]{:S(2)}) copy-start(bf16[2,4,4,12288]{3,2,1,0:T(4,128)(2,1)} %reshape.348) | copy-start | bytes 2359300
  121.0 2.3 %collective-permute-start.6 = (bf16[2,4,12288]{2,1,0:T(4,128)(2,1)S(1)}, bf16[2,4,12288]{2,1,0:T(4,128)(2,1)S(1)}, u32[]{:S(2)}, u32[]{:S(2)}) collective-permute-start(bf16[2,4,12288]{2,1,0:T(4,128)(2,1)S(1)} %get-tuple-element.5), channel_id=1, source_target_pairs={{0,1},{1,0},{2,3},{3,2},{4,5},{5,4},{6,7},{7,6},{8,9},{9,8},{10,11... | collective-permute-start | bytes 589832 | tf_op jit(solution)/shard_map/ppermute | solution.py:57
  121.2 6.7 %collective-permute-start.8 = (bf16[2,4,12288]{2,1,0:T(4,128)(2,1)S(1)}, bf16[2,4,12288]{2,1,0:T(4,128)(2,1)S(1)}, u32[]{:S(2)}, u32[]{:S(2)}) collective-permute-start(bf16[2,4,12288]{2,1,0:T(4,128)(2,1)S(1)} %get-tuple-element.6), channel_id=1, source_target_pairs={{0,3},{1,2},{2,1},{3,0},{4,7},{5,6},{6,5},{7,4},{8,11},{9,10},{10,... | collective-permute-start | bytes 589832 | tf_op jit(solution)/shard_map/ppermute | solution.py:57
  122.6 10.0 %collective-permute-start.7 = (bf16[2,4,12288]{2,1,0:T(4,128)(2,1)S(1)}, bf16[2,4,12288]{2,1,0:T(4,128)(2,1)S(1)}, u32[]{:S(2)}, u32[]{:S(2)}) collective-permute-start(bf16[2,4,12288]{2,1,0:T(4,128)(2,1)S(1)} %get-tuple-element.7), channel_id=1, source_target_pairs={{0,2},{1,3},{2,0},{3,1},{4,6},{5,7},{6,4},{7,5},{8,10},{9,11},{10,... | collective-permute-start | bytes 589832 | tf_op jit(solution)/shard_map/ppermute | solution.py:57
  133.9 7.8 %collective-permute-start.25 = (bf16[4,12288]{1,0:T(4,128)(2,1)S(1)}, bf16[4,12288]{1,0:T(4,128)(2,1)S(1)}, u32[]{:S(2)}, u32[]{:S(2)}) collective-permute-start(bf16[4,12288]{1,0:T(4,128)(2,1)S(1)} %convert_element_type.167), channel_id=1, source_target_pairs={{0,8},{1,9},{2,10},{3,11},{4,12},{5,13},{6,14},{7,15},{8,0},{9,1},... | collective-permute-start | bytes 294920 | tf_op jit(solution)/shard_map/ppermute | solution.py:54
  137.0 6.6 %collective-permute-start.24 = (bf16[4,12288]{1,0:T(4,128)(2,1)S(1)}, bf16[4,12288]{1,0:T(4,128)(2,1)S(1)}, u32[]{:S(2)}, u32[]{:S(2)}) collective-permute-start(bf16[4,12288]{1,0:T(4,128)(2,1)S(1)} %convert_element_type.163), channel_id=1, source_target_pairs={{0,4},{1,5},{2,6},{3,7},{4,0},{5,1},{6,2},{7,3},{8,12},{9,13},{10,... | collective-permute-start | bytes 294920 | tf_op jit(solution)/shard_map/ppermute | solution.py:54
  138.3 6.5 %collective-permute-start.26 = (bf16[4,12288]{1,0:T(4,128)(2,1)S(1)}, bf16[4,12288]{1,0:T(4,128)(2,1)S(1)}, u32[]{:S(2)}, u32[]{:S(2)}) collective-permute-start(bf16[4,12288]{1,0:T(4,128)(2,1)S(1)} %convert_element_type.171), channel_id=1, source_target_pairs={{0,12},{1,13},{2,14},{3,15},{4,8},{5,9},{6,10},{7,11},{8,4},{9,5},... | collective-permute-start | bytes 294920 | tf_op jit(solution)/shard_map/ppermute | solution.py:54
  (7 other events, 28.1 us)

commit v2 on v0

v2 whole, which is shorter than its diff:
```python
import functools

import jax
import jax.numpy as jnp
from jax import lax
from jax.experimental import pallas as pl
from jax.experimental.pallas import tpu as pltpu
from jax.sharding import PartitionSpec as P

GROUP = 16
MIB = 1 << 20
VMEM = pl.BlockSpec(memory_space=pltpu.VMEM)
SMEM = pl.BlockSpec(memory_space=pltpu.SMEM)
f32, bf16 = jnp.float32, jnp.bfloat16


def piece(width, most):
    size = 128
    while size * 2 <= most and width % (size * 2) == 0:
        size *= 2
    return size


def call(body, outs, ins, limit, scratch=(), flops=0, moved=0):
    return pl.pallas_call(
        body,
        out_shape=outs,
        in_specs=ins,
        out_specs=[VMEM] * len(outs),
        scratch_shapes=list(scratch),
        compiler_params=pltpu.CompilerParams(vmem_limit_bytes=limit * MIB),
        cost_estimate=pl.CostEstimate(flops=flops, bytes_accessed=moved, transcendentals=0),
    )


def norm_body(hidden, gain, shift, out):
    wide = hidden[...].astype(f32)
    mean = jnp.mean(wide, axis=-1, keepdims=True)
    centred = wide - mean
    variance = jnp.mean(centred * centred, axis=-1, keepdims=True)
    out[...] = (centred * lax.rsqrt(variance + 1e-05) * gain[...] + shift[...]).astype(bf16)


def window(index, size):
    return pl.ds(pl.multiple_of(index * size, 128), size)


def strip(whole, index, mates, share):
    wide = whole[:, window(index // mates, mates * share)].astype(f32)
    own = [jnp.where(index % mates == a, wide[:, a * share : (a + 1) * share], 0.0) for a in range(mates)]
    return sum(own).astype(bf16)


def pack_body(groups, mates, share, place, pick, *refs):
    held, rows, lows, whole = refs[:groups], refs[groups : groups + mates], refs[groups + mates : -1], refs[-1]
    width = held[0].shape[1]
    each = rows[0].shape[0]
    step = piece(width, 2048)

    @pl.loop(0, width // step)
    def _(i):
        cols = pl.ds(pl.multiple_of(i * step, step), step)
        block = jnp.concatenate([h[:, cols] for h in held], axis=0)
        whole[:, cols] = block
        chosen = jnp.dot(pick[...], block, preferred_element_type=f32).astype(bf16)
        for j in range(mates):
            rows[j][:, cols] = chosen[j * each : (j + 1) * each]

    for j in range(mates):
        lows[j][...] = whole[:, window(place[0] ^ j, share)] if share % 128 == 0 else strip(whole, place[0] ^ j, mates, share)


def block_body(mates, *refs):
    x, w_in, b_in, w_out, outs = refs[:mates], refs[mates], refs[mates + 1], refs[mates + 2], refs[mates + 3 :]
    width = w_in.shape[0]
    each = x[0].shape[0]
    step = piece(width, 2048)

    def add(i, total):
        cols = pl.ds(pl.multiple_of(i * step, step), step)
        rows = jnp.concatenate([r[:, cols] for r in x], axis=0)
        return total + jnp.dot(rows, w_in[cols, :], preferred_element_type=f32)

    pre = lax.fori_loop(0, width // step, add, jnp.zeros((mates * each, w_in.shape[1]), f32))
    act = jnp.maximum(pre + b_in[...], 0.0).astype(bf16)

    @pl.loop(0, width // step)
    def _(i):
        cols = pl.ds(pl.multiple_of(i * step, step), step)
        part = jnp.dot(act, w_out[:, cols], preferred_element_type=f32).astype(bf16)
        for j in range(mates):
            outs[j][:, cols] = part[j * each : (j + 1) * each]


def sum_body(groups, mates, share, place, pick, *refs):
    back, lows, outs, whole = refs[:mates], refs[mates : 2 * mates], refs[2 * mates : -1], refs[-1]
    width = back[0].shape[1]
    row_dev = outs[0].shape[0]
    step = piece(width, 2048)

    @pl.loop(0, width // step)
    def _(i):
        cols = pl.ds(pl.multiple_of(i * step, step), step)
        block = jnp.concatenate([b[:, cols] for b in back], axis=0)
        whole[:, cols] = jnp.dot(pick[...], block, preferred_element_type=f32)

    if share % 128 == 0:
        for j in range(mates):
            whole[:, window(place[0] ^ j, share)] += lows[j][...].astype(f32)
    else:
        mate = place[0] % mates
        ordered = [sum(jnp.where(mate ^ j == a, lows[j][...].astype(f32), 0.0) for j in range(mates)) for a in range(mates)]
        whole[:, window(place[0] // mates, mates * share)] += jnp.concatenate(ordered, axis=1)

    @pl.loop(0, width // step)
    def _(i):
        cols = pl.ds(pl.multiple_of(i * step, step), step)
        for k in range(groups):
            outs[k][:, cols] = whole[k * row_dev : (k + 1) * row_dev, cols].astype(outs[k].dtype)


def activity(lists, counts, block_slot):
    groups, top = lists.shape
    nblocks = block_slot.shape[0]
    names = jnp.arange(nblocks, dtype=jnp.int32)
    live = (jnp.arange(top, dtype=jnp.int32)[None, :] < counts[:, None]).astype(jnp.int32)
    hits = (lists[:, :, None] == names[None, None, :]).astype(jnp.int32) * live[:, :, None]
    by_block = jnp.sum(hits, axis=1)
    placed = (block_slot[:, None] == names[None, :]).astype(jnp.int32)
    return jnp.sum(by_block[:, :, None] * placed[None, :, :], axis=1)


def shards(
    hidden,
    ln_gain,
    ln_shift,
    lists,
    counts,
    block_slot,
    w_in,
    b_in,
    w_out,
    low_in,
    low_bias,
    low_out,
):
    devices = lax.axis_size("blk")
    position = lax.axis_index("blk")
    row_dev, width = hidden.shape
    groups = lists.shape[0]
    mates = devices // groups
    slots = groups // 2
    share = low_in.shape[0]
    rank = low_in.shape[1]
    plane = position // mates
    mate = position % mates
    place = jnp.reshape(position, (1,)).astype(jnp.int32)

    def across(x, k):
        return x if k == 0 else lax.ppermute(x, "blk", [(i, i ^ (mates * k)) for i in range(devices)])

    def within(x, j):
        return x if j == 0 else lax.ppermute(x, "blk", [(i, i ^ j) for i in range(devices)])

    def shape(*dims, dtype=bf16):
        return jax.ShapeDtypeStruct(dims, dtype)

    normed = call(norm_body, [shape(row_dev, width)], [VMEM] * 3, 16)(
        hidden, ln_gain.reshape(1, width), ln_shift.reshape(1, width)
    )[0]

    table = activity(lists, counts, block_slot)
    upto = jnp.sum(
        jnp.where(jnp.arange(groups)[:, None] > jnp.arange(groups)[None, :], 1, 0)[:, :, None] * table[None], axis=1
    )
    at = plane * mates + (mate ^ jnp.arange(mates))
    by = plane ^ jnp.arange(groups)
    choose = (at[:, None] == jnp.arange(devices)[None, :])[:, None, None, :]
    relate = (by[:, None] == jnp.arange(groups)[None, :])[None, :, :, None]
    code = jnp.where(table > 0, upto, -1)
    code = jnp.sum(jnp.where(choose & relate, code[None, None], 0), axis=(2, 3))
    hot = (code[:, None, :] == jnp.arange(slots)[None, :, None]).astype(f32)
    eye = jnp.eye(row_dev, dtype=f32)
    pick = (hot[:, :, None, :, None] * eye[None, None, :, None, :]).reshape(
        mates * slots * row_dev, groups * row_dev
    ).astype(bf16)

    held = [across(normed, k) for k in range(groups)]
    each = slots * row_dev
    packed = call(
        functools.partial(pack_body, groups, mates, share),
        [shape(each, width)] * mates + [shape(groups * row_dev, share)] * mates,
        [SMEM, VMEM] + [VMEM] * groups,
        24,
        [pltpu.VMEM((groups * row_dev, width), bf16)],
    )(place, pick, *held)
    lows = [within(packed[mates + j], j) for j in range(mates)]
    rows = [within(packed[j], j) for j in range(mates)]

    partial = jnp.dot(jnp.concatenate(lows, axis=0), low_in, preferred_element_type=f32)
    partial = partial.reshape(mates, groups * row_dev, rank)
    summed = sum(within(partial[j], j) for j in range(mates))
    lowz = 0.0
    for k in range(groups):
        got = across(summed, k).reshape(groups, row_dev, rank)
        lowz = lowz + jnp.stack([got[q ^ k] for q in range(groups)])
    low_h = jnp.maximum(lowz + low_bias, 0.0).astype(bf16).reshape(groups * row_dev, rank)
    all_h = jnp.concatenate([within(low_h, j) for j in range(mates)], axis=0)
    low_cols = jnp.dot(all_h, low_out, preferred_element_type=f32).astype(bf16)
    low_cols = low_cols.reshape(mates, groups * row_dev, share)
    low_back = [within(low_cols[j], j) for j in range(mates)]

    parts = call(
        functools.partial(block_body, mates),
        [shape(each, width)] * mates,
        [VMEM] * (mates + 3),
        32,
    )(*rows, w_in, b_in.reshape(1, -1), w_out)
    back = [within(parts[j], j) for j in range(mates)]
    sums = call(
        functools.partial(sum_body, groups, mates, share),
        [shape(row_dev, width, dtype=f32)] + [shape(row_dev, width)] * (groups - 1),
        [SMEM, VMEM] + [VMEM] * (2 * mates),
        32,
        [pltpu.VMEM((groups * row_dev, width), f32)],
    )(place, pick.T, *back, *low_back)
    total = sums[0]
    for k in range(1, groups):
        total = total + across(sums[k], k).astype(f32)
    return total.astype(bf16)


def solution(mesh):
    return jax.shard_map(
        shards,
        mesh=mesh,
        in_specs=(
            P(("rep", "blk"), None),
            P(),
            P(),
            P("rep", None),
            P("rep"),
            P(),
            P(None, "blk"),
            P("blk"),
            P("blk", None),
            P("blk", None),
            P(),
            P(None, "blk"),
        ),
        out_specs=P(("rep", "blk"), None),
        check_vma=False,
    )
```

time: 234 us -> 83.1 us (0.36); the launches traced: 230 us -> 82.7 us
  waiting for transfers between devices: 156 us -> 37.3 us
  blocking collectives: 22.2 us -> 0 us
  starting transfers between devices: 9.56 us -> 27.3 us
  between operations: 14.2 us -> 0.17 us
  matrix products: 8.25 us -> 1.63 us
  other arithmetic: 9.27 us -> 3.92 us
  Pallas kernels: 0 us -> 4.99 us
  local copies, waits for them, and re-layouts: 10.5 us -> 7.46 us
    unnamed x3 -> x0, waiting for transfers between devices: 86 us -> none
    all_gather x1 -> x0, waiting for transfers between devices: 37.8 us -> none  [shards(): every = lax.all_gather(normed, 'blk', axis=0, tiled=True)]
    ppermute x0 -> x27, waiting for transfers between devices: none -> 37.3 us  [the longest x18 23 us: within(): lax.ppermute(x, 'blk', [(i, i ^ j) for i in range(devices)])]
    all_to_all x2 -> x0, waiting for transfers between devices: 32 us -> none  [the longest x1 32 us: shards(): lax.all_to_all(result, 'blk', split_axis=0, concat_axis=0, tiled=True)]
    ppermute x0 -> x27, starting transfers between devices: none -> 27.3 us  [the longest x9 14.7 us: across(): lax.ppermute(x, 'blk', [(i, i ^ mates * k) for i in range(devices)])]
    all_gather x1 -> x0, blocking collectives: 22.2 us -> none  [shards(): lax.all_gather(low_h, 'blk', axis=0, tiled=True)]
    all_to_all x2 -> x0, starting transfers between devices: 9.52 us -> none  [the longest x1 6.01 us: shards(): lax.all_to_all(result, 'blk', split_axis=0, concat_axis=0, tiled=True)]
    dot_general x3 -> x2, matrix products: 8.25 us -> 1.63 us  [the longest x1 1.37 us: shards(): jnp.dot(jnp.concatenate(lows, axis=0), low_in, preferred_element_type=f32)]
  transfers between devices with their start and end apart: 4 -> 27, of which waited for: 3 -> 16; matrix products, arithmetic and copies ran while one was open for 4% -> 5% of each run, Pallas kernels for 0% -> 0%
where the time goes in v2:
time: 83.1 us; the launch traced here: 82.7 us
  waiting for transfers between devices  37.3 us (45%)
  starting transfers between devices  27.3 us (33%)
  local copies, waits for them, and re-layouts  7.46 us (9%)
  Pallas kernels  4.99 us (6%)
  other arithmetic  3.92 us (5%)
  matrix products  1.63 us (2%)
    ppermute x18, waiting for transfers between devices, within(): lax.ppermute(x, 'blk', [(i, i ^ j) for i in range(devices)])  23 us
    ppermute x9, starting transfers between devices, across(): lax.ppermute(x, 'blk', [(i, i ^ mates * k) for i in range(devices)])  14.7 us
    ppermute x9, waiting for transfers between devices, across(): lax.ppermute(x, 'blk', [(i, i ^ mates * k) for i in range(devices)])  14.3 us
    ppermute x18, starting transfers between devices, within(): lax.ppermute(x, 'blk', [(i, i ^ j) for i in range(devices)])  12.6 us
    unnamed x15, local copies, waits for them, and re-layouts  7.12 us
    pallas_call x1, Pallas kernels, shards(): call(functools.partial(block_body, mates), [shape(each, width)] * mates,...  2.5 us
  transfers between devices with their start and end apart: 27, of which 16 were waited for; matrix products, arithmetic and copies ran while one was open for 5% of the time, Pallas kernels for 0%

profile of v2, /device:TPU:0, one launch (start us, length us, event | category | flops | bytes accessed | tf_op | source)
XLA Modules:
  0.0 82.7 jit_solution(13315922914514729817)
XLA Ops:
  0.0 1.0 %copy-done.3 = bf16[4,12288]{1,0:T(4,128)(2,1)S(1)} copy-done((bf16[4,12288]{1,0:T(4,128)(2,1)S(1)}, bf16[4,12288]{1,0:T(4,128)(2,1)}, u32[]{:S(2)}) %copy-start.3) | copy-done | bytes 98328
  3.0 5.1 %collective-permute-start.2 = (bf16[4,12288]{1,0:T(4,128)(2,1)S(1)}, bf16[4,12288]{1,0:T(4,128)(2,1)S(1)}, u32[]{:S(2)}, u32[]{:S(2)}) collective-permute-start(bf16[4,12288]{1,0:T(4,128)(2,1)S(1)} %shard_map.118.refs_0_), channel_id=1, source_target_pairs={{0,12},{1,13},{2,14},{3,15},{4,8},{5,9},{6,10},{7,11},{8,4},{9,5},... | collective-permute-start | bytes 294920 | tf_op jit(solution)/shard_map/ppermute | solution.py:160
  12.3 4.1 %collective-permute-done.1.refs_2_ = bf16[4,12288]{1,0:T(4,128)(2,1)S(1)} collective-permute-done((bf16[4,12288]{1,0:T(4,128)(2,1)S(1)}, bf16[4,12288]{1,0:T(4,128)(2,1)S(1)}, u32[]{:S(2)}, u32[]{:S(2)}) %collective-permute-start.1) | collective-permute-done | bytes 98336 | tf_op jit(solution)/shard_map/ppermute | solution.py:160
  16.4 1.0 %shard_map.119 = (bf16[8,12288]{1,0:T(8,128)(2,1)S(1)}, bf16[8,12288]{1,0:T(8,128)(2,1)S(1)}, bf16[8,12288]{1,0:T(8,128)(2,1)S(1)}, bf16[8,12288]{1,0:T(8,128)(2...) custom-call(s32[1]{0:T(128)} %bitcast.place, ...), custom_call_target="tpu_custom_call" | custom-call | tf_op jit(solution)/shard_map/pallas_call | solution.py:190
  17.5 1.6 %collective-permute-start.10 = (bf16[16,768]{1,0:T(8,128)(2,1)S(1)}, bf16[16,768]{1,0:T(8,128)(2,1)S(1)}, u32[]{:S(2)}, u32[]{:S(2)}) collective-permute-start(bf16[16,768]{1,0:T(8,128)(2,1)S(1)} %get-tuple-element.31), channel_id=1, source_target_pairs={{0,2},{1,3},{2,0},{3,1},{4,6},{5,7},{6,4},{7,5},{8,10},{9,11},{10,... | collective-permute-start | bytes 73736 | tf_op jit(solution)/shard_map/ppermute | solution.py:163
  19.4 2.0 %collective-permute-done.10 = bf16[16,768]{1,0:T(8,128)(2,1)S(1)} collective-permute-done((bf16[16,768]{1,0:T(8,128)(2,1)S(1)}, bf16[16,768]{1,0:T(8,128)(2,1)S(1)}, u32[]{:S(2)}, u32[]{:S(2)}) %collective-permute-start.10) | collective-permute-done | bytes 24608 | tf_op jit(solution)/shard_map/ppermute | solution.py:163
  21.4 0.9 %collective-permute-done.11 = bf16[16,768]{1,0:T(8,128)(2,1)S(1)} collective-permute-done((bf16[16,768]{1,0:T(8,128)(2,1)S(1)}, bf16[16,768]{1,0:T(8,128)(2,1)S(1)}, u32[]{:S(2)}, u32[]{:S(2)}) %collective-permute-start.11) | collective-permute-done | bytes 24608 | tf_op jit(solution)/shard_map/ppermute | solution.py:163
  22.3 1.4 %fusion = f32[64,512]{1,0:T(8,128)S(1)} fusion(bf16[768,512]{1,0:T(8,128)(2,1)} %param.21, bf16[16,768]{1,0:T(8,128)(2,1)S(1)} %collective-permute-done.11, bf16[16,768]{1,0:T(8,128)(2,1)S(1)} %collective-permute-done.10, bf16[16,768]{1,0:T(8,128)(2,1)S(1)} %collective-permute-done.9, bf16[16,768]{1,0:T(8,128)(2,1)S(1)} %get-tuple-element.29), kind=kOutput, calls=%fused_computation.2 | convolution fusion | flops 50724864 | bytes 1015808 | tf_op jit(solution)/shard_map/dot_general | solution.py:200
  24.7 1.2 %collective-permute-start.13 = (f32[16,512]{1,0:T(8,128)S(1)}, f32[16,512]{1,0:T(8,128)S(1)}, u32[]{:S(2)}, u32[]{:S(2)}) collective-permute-start(f32[16,512]{1,0:T(8,128)S(1)} %get-tuple-element.39), channel_id=1, source_target_pairs={{0,2},{1,3},{2,0},{3,1},{4,6},{5,7},{6,4},{7,5},{8,10},{9,11},{10,... | collective-permute-start | bytes 98312 | tf_op jit(solution)/shard_map/ppermute | solution.py:163
  26.0 1.4 %collective-permute-done.14 = f32[16,512]{1,0:T(8,128)S(1)} collective-permute-done((f32[16,512]{1,0:T(8,128)S(1)}, f32[16,512]{1,0:T(8,128)S(1)}, u32[]{:S(2)}, u32[]{:S(2)}) %collective-permute-start.14) | collective-permute-done | bytes 32800 | tf_op jit(solution)/shard_map/ppermute | solution.py:163
  27.3 1.3 %collective-permute-done.13 = f32[16,512]{1,0:T(8,128)S(1)} collective-permute-done((f32[16,512]{1,0:T(8,128)S(1)}, f32[16,512]{1,0:T(8,128)S(1)}, u32[]{:S(2)}, u32[]{:S(2)}) %collective-permute-start.13) | collective-permute-done | bytes 32800 | tf_op jit(solution)/shard_map/ppermute | solution.py:163
  28.7 2.6 %collective-permute-start.17 = (f32[16,512]{1,0:T(8,128)S(1)}, f32[16,512]{1,0:T(8,128)S(1)}, u32[]{:S(2)}, u32[]{:S(2)}) collective-permute-start(f32[16,512]{1,0:T(8,128)S(1)} %fusion.16), channel_id=1, source_target_pairs={{0,12},{1,13},{2,14},{3,15},{4,8},{5,9},{6,10},{7,11},{8,4},{9,5},... | collective-permute-start | bytes 98312 | tf_op jit(solution)/shard_map/ppermute | solution.py:160
  31.2 1.9 %collective-permute-start.15 = (f32[16,512]{1,0:T(8,128)S(1)}, f32[16,512]{1,0:T(8,128)S(1)}, u32[]{:S(2)}, u32[]{:S(2)}) collective-permute-start(f32[16,512]{1,0:T(8,128)S(1)} %fusion.16), channel_id=1, source_target_pairs={{0,4},{1,5},{2,6},{3,7},{4,0},{5,1},{6,2},{7,3},{8,12},{9,13},{10,... | collective-permute-start | bytes 98312 | tf_op jit(solution)/shard_map/ppermute | solution.py:160
  33.1 1.3 %collective-permute-done.17 = f32[16,512]{1,0:T(8,128)S(1)} collective-permute-done((f32[16,512]{1,0:T(8,128)S(1)}, f32[16,512]{1,0:T(8,128)S(1)}, u32[]{:S(2)}, u32[]{:S(2)}) %collective-permute-start.17) | collective-permute-done | bytes 32800 | tf_op jit(solution)/shard_map/ppermute | solution.py:160
  34.4 1.6 %collective-permute-done.16 = f32[16,512]{1,0:T(8,128)S(1)} collective-permute-done((f32[16,512]{1,0:T(8,128)S(1)}, f32[16,512]{1,0:T(8,128)S(1)}, u32[]{:S(2)}, u32[]{:S(2)}) %collective-permute-start.16) | collective-permute-done | bytes 32800 | tf_op jit(solution)/shard_map/ppermute | solution.py:160
  36.8 1.3 %collective-permute-start.19 = (bf16[16,512]{1,0:T(8,128)(2,1)S(1)}, bf16[16,512]{1,0:T(8,128)(2,1)S(1)}, u32[]{:S(2)}, u32[]{:S(2)}) collective-permute-start(bf16[16,512]{1,0:T(8,128)(2,1)S(1)} %maximum_convert_fusion), channel_id=1, source_target_pairs={{0,2},{1,3},{2,0},{3,1},{4,6},{5,7},{6,4},{7,5},{8,10},{9,11},{10,... | collective-permute-start | bytes 49160 | tf_op jit(solution)/shard_map/ppermute | solution.py:163
  38.7 1.2 %collective-permute-start.4 = (bf16[8,12288]{1,0:T(8,128)(2,1)S(1)}, bf16[8,12288]{1,0:T(8,128)(2,1)S(1)}, u32[]{:S(2)}, u32[]{:S(2)}) collective-permute-start(bf16[8,12288]{1,0:T(8,128)(2,1)S(1)} %get-tuple-element.23), channel_id=1, source_target_pairs={{0,2},{1,3},{2,0},{3,1},{4,6},{5,7},{6,4},{7,5},{8,10},{9,11},{10,... | collective-permute-start | bytes 589832 | tf_op jit(solution)/shard_map/ppermute | solution.py:163
  40.9 5.5 %collective-permute-done.4.refs_2_ = bf16[8,12288]{1,0:T(8,128)(2,1)S(1)} collective-permute-done((bf16[8,12288]{1,0:T(8,128)(2,1)S(1)}, bf16[8,12288]{1,0:T(8,128)(2,1)S(1)}, u32[]{:S(2)}, u32[]{:S(2)}) %collective-permute-start.4) | collective-permute-done | bytes 196640 | tf_op jit(solution)/shard_map/ppermute | solution.py:163
  46.4 3.4 %collective-permute-done.5.refs_3_ = bf16[8,12288]{1,0:T(8,128)(2,1)S(1)} collective-permute-done((bf16[8,12288]{1,0:T(8,128)(2,1)S(1)}, bf16[8,12288]{1,0:T(8,128)(2,1)S(1)}, u32[]{:S(2)}, u32[]{:S(2)}) %collective-permute-start.5) | collective-permute-done | bytes 196640 | tf_op jit(solution)/shard_map/ppermute | solution.py:163
  49.8 1.9 %copy-done.1 = bf16[12288,128]{1,0:T(8,128)(2,1)S(1)} copy-done((bf16[12288,128]{1,0:T(8,128)(2,1)S(1)}, bf16[12288,128]{1,0:T(8,128)(2,1)}, u32[]{:S(2)}) %copy-start.1) | copy-done | bytes 3145752
  51.7 1.9 %copy-done.2 = bf16[128,12288]{1,0:T(8,128)(2,1)S(1)} copy-done((bf16[128,12288]{1,0:T(8,128)(2,1)S(1)}, bf16[128,12288]{1,0:T(8,128)(2,1)}, u32[]{:S(2)}) %copy-start.2) | copy-done | bytes 3145752
  53.6 2.5 %shard_map.120 = (bf16[8,12288]{1,0:T(8,128)(2,1)S(1)}, bf16[8,12288]{1,0:T(8,128)(2,1)S(1)}, bf16[8,12288]{1,0:T(8,128)(2,1)S(1)}, bf16[8,12288]{1,0:T(8,128)(2,1)S(1)}) custom-call(bf16[8,12288]{1,0:T(8,128)(2,1)S(1)} %get-tuple-element.21.refs_0_, bf16[8,12288]{1,0:T(8,128)(2,1)S(1)} %collective-permute-done.3.refs_1_, ...), custom_call_target="tpu_custom_call" | custom-call | tf_op jit(solution)/shard_map/pallas_call | solution.py:213
  56.4 1.2 %collective-permute-start.7 = (bf16[8,12288]{1,0:T(8,128)(2,1)S(1)}, bf16[8,12288]{1,0:T(8,128)(2,1)S(1)}, u32[]{:S(2)}, u32[]{:S(2)}) collective-permute-start(bf16[8,12288]{1,0:T(8,128)(2,1)S(1)} %get-tuple-element.27), channel_id=1, source_target_pairs={{0,2},{1,3},{2,0},{3,1},{4,6},{5,7},{6,4},{7,5},{8,10},{9,11},{10,... | collective-permute-start | bytes 589832 | tf_op jit(solution)/shard_map/ppermute | solution.py:163
  58.1 1.4 %collective-permute-start.23 = (bf16[16,768]{1,0:T(8,128)(2,1)S(1)}, bf16[16,768]{1,0:T(8,128)(2,1)S(1)}, u32[]{:S(2)}, u32[]{:S(2)}) collective-permute-start(bf16[16,768]{1,0:T(8,128)(2,1)S(1)} %get-tuple-element.40), channel_id=1, source_target_pairs={{0,3},{1,2},{2,1},{3,0},{4,7},{5,6},{6,5},{7,4},{8,11},{9,10},{10,... | collective-permute-start | bytes 73736 | tf_op jit(solution)/shard_map/ppermute | solution.py:163
  59.4 0.8 collective-permute-start.22
  60.3 7.4 %collective-permute-done.23.refs_7_ = bf16[16,768]{1,0:T(8,128)(2,1)S(1)} collective-permute-done((bf16[16,768]{1,0:T(8,128)(2,1)S(1)}, bf16[16,768]{1,0:T(8,128)(2,1)S(1)}, u32[]{:S(2)}, u32[]{:S(2)}) %collective-permute-start.23) | collective-permute-done | bytes 24608 | tf_op jit(solution)/shard_map/ppermute | solution.py:163
  69.2 1.0 %shard_map.121 = (f32[4,12288]{1,0:T(4,128)S(1)}, bf16[4,12288]{1,0:T(4,128)(2,1)S(1)}, bf16[4,12288]{1,0:T(4,128)(2,1)S(1)}, bf16[4,12288]{1,0:T(4,128)(2,1)S(1)}) custom-call(s32[1]{0:T(128)} %bitcast.place, bf16[16,32]{1,0:T(8,128)(2,1)S(1)} %bitcast.43, bf16[8,12288]{1,0:T(8,128)(2,1)S(1)} %get-tuple-element.25.refs_0_, ...), custom_call_target="tpu_custom_call" | custom-call | tf_op jit(solution)/shard_map/pallas_call | solution.py:220
  70.2 1.0 %collective-permute-start.24 = (bf16[4,12288]{1,0:T(4,128)(2,1)S(1)}, bf16[4,12288]{1,0:T(4,128)(2,1)S(1)}, u32[]{:S(2)}, u32[]{:S(2)}) collective-permute-start(bf16[4,12288]{1,0:T(4,128)(2,1)S(1)} %get-tuple-element.34), channel_id=1, source_target_pairs={{0,4},{1,5},{2,6},{3,7},{4,0},{5,1},{6,2},{7,3},{8,12},{9,13},{10,... | collective-permute-start | bytes 294920 | tf_op jit(solution)/shard_map/ppermute | solution.py:160
  71.2 1.4 %collective-permute-start.25 = (bf16[4,12288]{1,0:T(4,128)(2,1)S(1)}, bf16[4,12288]{1,0:T(4,128)(2,1)S(1)}, u32[]{:S(2)}, u32[]{:S(2)}) collective-permute-start(bf16[4,12288]{1,0:T(4,128)(2,1)S(1)} %get-tuple-element.35), channel_id=1, source_target_pairs={{0,8},{1,9},{2,10},{3,11},{4,12},{5,13},{6,14},{7,15},{8,0},{9,1},... | collective-permute-start | bytes 294920 | tf_op jit(solution)/shard_map/ppermute | solution.py:160
  72.7 2.0 %collective-permute-start.26 = (bf16[4,12288]{1,0:T(4,128)(2,1)S(1)}, bf16[4,12288]{1,0:T(4,128)(2,1)S(1)}, u32[]{:S(2)}, u32[]{:S(2)}) collective-permute-start(bf16[4,12288]{1,0:T(4,128)(2,1)S(1)} %get-tuple-element.36), channel_id=1, source_target_pairs={{0,12},{1,13},{2,14},{3,15},{4,8},{5,9},{6,10},{7,11},{8,4},{9,5},... | collective-permute-start | bytes 294920 | tf_op jit(solution)/shard_map/ppermute | solution.py:160
  74.7 2.1 %collective-permute-done.24 = bf16[4,12288]{1,0:T(4,128)(2,1)S(1)} collective-permute-done((bf16[4,12288]{1,0:T(4,128)(2,1)S(1)}, bf16[4,12288]{1,0:T(4,128)(2,1)S(1)}, u32[]{:S(2)}, u32[]{:S(2)}) %collective-permute-start.24) | collective-permute-done | bytes 98336 | tf_op jit(solution)/shard_map/ppermute | solution.py:160
  76.8 5.2 %collective-permute-done.25 = bf16[4,12288]{1,0:T(4,128)(2,1)S(1)} collective-permute-done((bf16[4,12288]{1,0:T(4,128)(2,1)S(1)}, bf16[4,12288]{1,0:T(4,128)(2,1)S(1)}, u32[]{:S(2)}, u32[]{:S(2)}) %collective-permute-start.25) | collective-permute-done | bytes 98336 | tf_op jit(solution)/shard_map/ppermute | solution.py:160
  (72 shorter events, 12.9 us)
Async XLA Ops:
  0.0 40.6 %copy-start = (bf16[512,768]{1,0:T(8,128)(2,1)S(1)}, bf16[512,768]{1,0:T(8,128)(2,1)}, u32[]{:S(2)}) copy-start(bf16[512,768]{1,0:T(8,128)(2,1)} %param.23) | copy-start | bytes 2359300
  0.0 49.8 %copy-start.6 = (f32[128]{0:T(128)S(1)}, f32[128]{0:T(128)}, u32[]{:S(2)}) copy-start(f32[128]{0:T(128)} %param.19) | copy-start | bytes 1540
  0.0 1.0 %copy-start.3 = (bf16[4,12288]{1,0:T(4,128)(2,1)S(1)}, bf16[4,12288]{1,0:T(4,128)(2,1)}, u32[]{:S(2)}) copy-start(bf16[4,12288]{1,0:T(4,128)(2,1)} %hidden.1) | copy-start | bytes 294916
  3.0 9.3 %collective-permute-start.2 = (bf16[4,12288]{1,0:T(4,128)(2,1)S(1)}, bf16[4,12288]{1,0:T(4,128)(2,1)S(1)}, u32[]{:S(2)}, u32[]{:S(2)}) collective-permute-start(bf16[4,12288]{1,0:T(4,128)(2,1)S(1)} %shard_map.118.refs_0_), channel_id=1, source_target_pairs={{0,12},{1,13},{2,14},{3,15},{4,8},{5,9},{6,10},{7,11},{8,4},{9,5},... | collective-permute-start | bytes 294920 | tf_op jit(solution)/shard_map/ppermute | solution.py:160
  8.1 8.3 %collective-permute-start.1 = (bf16[4,12288]{1,0:T(4,128)(2,1)S(1)}, bf16[4,12288]{1,0:T(4,128)(2,1)S(1)}, u32[]{:S(2)}, u32[]{:S(2)}) collective-permute-start(bf16[4,12288]{1,0:T(4,128)(2,1)S(1)} %shard_map.118.refs_0_), channel_id=1, source_target_pairs={{0,8},{1,9},{2,10},{3,11},{4,12},{5,13},{6,14},{7,15},{8,0},{9,1},... | collective-permute-start | bytes 294920 | tf_op jit(solution)/shard_map/ppermute | solution.py:160
  8.1 8.3 %collective-permute-start = (bf16[4,12288]{1,0:T(4,128)(2,1)S(1)}, bf16[4,12288]{1,0:T(4,128)(2,1)S(1)}, u32[]{:S(2)}, u32[]{:S(2)}) collective-permute-start(bf16[4,12288]{1,0:T(4,128)(2,1)S(1)} %shard_map.118.refs_0_), channel_id=1, source_target_pairs={{0,4},{1,5},{2,6},{3,7},{4,0},{5,1},{6,2},{7,3},{8,12},{9,13},{10,... | collective-permute-start | bytes 294920 | tf_op jit(solution)/shard_map/ppermute | solution.py:160
  17.4 1.9 %collective-permute-start.9 = (bf16[16,768]{1,0:T(8,128)(2,1)S(1)}, bf16[16,768]{1,0:T(8,128)(2,1)S(1)}, u32[]{:S(2)}, u32[]{:S(2)}) collective-permute-start(bf16[16,768]{1,0:T(8,128)(2,1)S(1)} %get-tuple-element.30), channel_id=1, source_target_pairs={{0,1},{1,0},{2,3},{3,2},{4,5},{5,4},{6,7},{7,6},{8,9},{9,8},{10,11... | collective-permute-start | bytes 73736 | tf_op jit(solution)/shard_map/ppermute | solution.py:163
  17.5 3.9 %collective-permute-start.10 = (bf16[16,768]{1,0:T(8,128)(2,1)S(1)}, bf16[16,768]{1,0:T(8,128)(2,1)S(1)}, u32[]{:S(2)}, u32[]{:S(2)}) collective-permute-start(bf16[16,768]{1,0:T(8,128)(2,1)S(1)} %get-tuple-element.31), channel_id=1, source_target_pairs={{0,2},{1,3},{2,0},{3,1},{4,6},{5,7},{6,4},{7,5},{8,10},{9,11},{10,... | collective-permute-start | bytes 73736 | tf_op jit(solution)/shard_map/ppermute | solution.py:163
  19.1 3.3 %collective-permute-start.11 = (bf16[16,768]{1,0:T(8,128)(2,1)S(1)}, bf16[16,768]{1,0:T(8,128)(2,1)S(1)}, u32[]{:S(2)}, u32[]{:S(2)}) collective-permute-start(bf16[16,768]{1,0:T(8,128)(2,1)S(1)} %get-tuple-element.32), channel_id=1, source_target_pairs={{0,3},{1,2},{2,1},{3,0},{4,7},{5,6},{6,5},{7,4},{8,11},{9,10},{10,... | collective-permute-start | bytes 73736 | tf_op jit(solution)/shard_map/ppermute | solution.py:163
  23.7 2.2 %collective-permute-start.12 = (f32[16,512]{1,0:T(8,128)S(1)}, f32[16,512]{1,0:T(8,128)S(1)}, u32[]{:S(2)}, u32[]{:S(2)}) collective-permute-start(f32[16,512]{1,0:T(8,128)S(1)} %get-tuple-element.37), channel_id=1, source_target_pairs={{0,1},{1,0},{2,3},{3,2},{4,5},{5,4},{6,7},{7,6},{8,9},{9,8},{10,11... | collective-permute-start | bytes 98312 | tf_op jit(solution)/shard_map/ppermute | solution.py:163
  24.0 3.3 %collective-permute-start.14 = (f32[16,512]{1,0:T(8,128)S(1)}, f32[16,512]{1,0:T(8,128)S(1)}, u32[]{:S(2)}, u32[]{:S(2)}) collective-permute-start(f32[16,512]{1,0:T(8,128)S(1)} %get-tuple-element.38), channel_id=1, source_target_pairs={{0,3},{1,2},{2,1},{3,0},{4,7},{5,6},{6,5},{7,4},{8,11},{9,10},{10,... | collective-permute-start | bytes 98312 | tf_op jit(solution)/shard_map/ppermute | solution.py:163
  24.7 3.9 %collective-permute-start.13 = (f32[16,512]{1,0:T(8,128)S(1)}, f32[16,512]{1,0:T(8,128)S(1)}, u32[]{:S(2)}, u32[]{:S(2)}) collective-permute-start(f32[16,512]{1,0:T(8,128)S(1)} %get-tuple-element.39), channel_id=1, source_target_pairs={{0,2},{1,3},{2,0},{3,1},{4,6},{5,7},{6,4},{7,5},{8,10},{9,11},{10,... | collective-permute-start | bytes 98312 | tf_op jit(solution)/shard_map/ppermute | solution.py:163
  28.7 5.8 %collective-permute-start.17 = (f32[16,512]{1,0:T(8,128)S(1)}, f32[16,512]{1,0:T(8,128)S(1)}, u32[]{:S(2)}, u32[]{:S(2)}) collective-permute-start(f32[16,512]{1,0:T(8,128)S(1)} %fusion.16), channel_id=1, source_target_pairs={{0,12},{1,13},{2,14},{3,15},{4,8},{5,9},{6,10},{7,11},{8,4},{9,5},... | collective-permute-start | bytes 98312 | tf_op jit(solution)/shard_map/ppermute | solution.py:160
  31.2 4.8 %collective-permute-start.16 = (f32[16,512]{1,0:T(8,128)S(1)}, f32[16,512]{1,0:T(8,128)S(1)}, u32[]{:S(2)}, u32[]{:S(2)}) collective-permute-start(f32[16,512]{1,0:T(8,128)S(1)} %fusion.16), channel_id=1, source_target_pairs={{0,8},{1,9},{2,10},{3,11},{4,12},{5,13},{6,14},{7,15},{8,0},{9,1},... | collective-permute-start | bytes 98312 | tf_op jit(solution)/shard_map/ppermute | solution.py:160
  31.2 4.8 %collective-permute-start.15 = (f32[16,512]{1,0:T(8,128)S(1)}, f32[16,512]{1,0:T(8,128)S(1)}, u32[]{:S(2)}, u32[]{:S(2)}) collective-permute-start(f32[16,512]{1,0:T(8,128)S(1)} %fusion.16), channel_id=1, source_target_pairs={{0,4},{1,5},{2,6},{3,7},{4,0},{5,1},{6,2},{7,3},{8,12},{9,13},{10,... | collective-permute-start | bytes 98312 | tf_op jit(solution)/shard_map/ppermute | solution.py:160
  36.8 3.2 %collective-permute-start.20 = (bf16[16,512]{1,0:T(8,128)(2,1)S(1)}, bf16[16,512]{1,0:T(8,128)(2,1)S(1)}, u32[]{:S(2)}, u32[]{:S(2)}) collective-permute-start(bf16[16,512]{1,0:T(8,128)(2,1)S(1)} %maximum_convert_fusion), channel_id=1, source_target_pairs={{0,3},{1,2},{2,1},{3,0},{4,7},{5,6},{6,5},{7,4},{8,11},{9,10},{10,... | collective-permute-start | bytes 49160 | tf_op jit(solution)/shard_map/ppermute | solution.py:163
  36.8 3.8 %collective-permute-start.19 = (bf16[16,512]{1,0:T(8,128)(2,1)S(1)}, bf16[16,512]{1,0:T(8,128)(2,1)S(1)}, u32[]{:S(2)}, u32[]{:S(2)}) collective-permute-start(bf16[16,512]{1,0:T(8,128)(2,1)S(1)} %maximum_convert_fusion), channel_id=1, source_target_pairs={{0,2},{1,3},{2,0},{3,1},{4,6},{5,7},{6,4},{7,5},{8,10},{9,11},{10,... | collective-permute-start | bytes 49160 | tf_op jit(solution)/shard_map/ppermute | solution.py:163
  38.1 2.5 %collective-permute-start.18 = (bf16[16,512]{1,0:T(8,128)(2,1)S(1)}, bf16[16,512]{1,0:T(8,128)(2,1)S(1)}, u32[]{:S(2)}, u32[]{:S(2)}) collective-permute-start(bf16[16,512]{1,0:T(8,128)(2,1)S(1)} %maximum_convert_fusion), channel_id=1, source_target_pairs={{0,1},{1,0},{2,3},{3,2},{4,5},{5,4},{6,7},{7,6},{8,9},{9,8},{10,11... | collective-permute-start | bytes 49160 | tf_op jit(solution)/shard_map/ppermute | solution.py:163
  38.7 2.2 %collective-permute-start.3 = (bf16[8,12288]{1,0:T(8,128)(2,1)S(1)}, bf16[8,12288]{1,0:T(8,128)(2,1)S(1)}, u32[]{:S(2)}, u32[]{:S(2)}) collective-permute-start(bf16[8,12288]{1,0:T(8,128)(2,1)S(1)} %get-tuple-element.22), channel_id=1, source_target_pairs={{0,1},{1,0},{2,3},{3,2},{4,5},{5,4},{6,7},{7,6},{8,9},{9,8},{10,11... | collective-permute-start | bytes 589832 | tf_op jit(solution)/shard_map/ppermute | solution.py:163
  38.7 7.7 %collective-permute-start.4 = (bf16[8,12288]{1,0:T(8,128)(2,1)S(1)}, bf16[8,12288]{1,0:T(8,128)(2,1)S(1)}, u32[]{:S(2)}, u32[]{:S(2)}) collective-permute-start(bf16[8,12288]{1,0:T(8,128)(2,1)S(1)} %get-tuple-element.23), channel_id=1, source_target_pairs={{0,2},{1,3},{2,0},{3,1},{4,6},{5,7},{6,4},{7,5},{8,10},{9,11},{10,... | collective-permute-start | bytes 589832 | tf_op jit(solution)/shard_map/ppermute | solution.py:163
  40.0 9.8 %collective-permute-start.5 = (bf16[8,12288]{1,0:T(8,128)(2,1)S(1)}, bf16[8,12288]{1,0:T(8,128)(2,1)S(1)}, u32[]{:S(2)}, u32[]{:S(2)}) collective-permute-start(bf16[8,12288]{1,0:T(8,128)(2,1)S(1)} %get-tuple-element.24), channel_id=1, source_target_pairs={{0,3},{1,2},{2,1},{3,0},{4,7},{5,6},{6,5},{7,4},{8,11},{9,10},{10,... | collective-permute-start | bytes 589832 | tf_op jit(solution)/shard_map/ppermute | solution.py:163
  49.8 1.9 %copy-start.1 = (bf16[12288,128]{1,0:T(8,128)(2,1)S(1)}, bf16[12288,128]{1,0:T(8,128)(2,1)}, u32[]{:S(2)}) copy-start(bf16[12288,128]{1,0:T(8,128)(2,1)} %refs_4_.1) | copy-start | bytes 9437188
  51.7 1.9 %copy-start.2 = (bf16[128,12288]{1,0:T(8,128)(2,1)S(1)}, bf16[128,12288]{1,0:T(8,128)(2,1)}, u32[]{:S(2)}) copy-start(bf16[128,12288]{1,0:T(8,128)(2,1)} %refs_6_.1) | copy-start | bytes 9437188
  56.1 13.1 %collective-permute-start.6 = (bf16[8,12288]{1,0:T(8,128)(2,1)S(1)}, bf16[8,12288]{1,0:T(8,128)(2,1)S(1)}, u32[]{:S(2)}, u32[]{:S(2)}) collective-permute-start(bf16[8,12288]{1,0:T(8,128)(2,1)S(1)} %get-tuple-element.26), channel_id=1, source_target_pairs={{0,1},{1,0},{2,3},{3,2},{4,5},{5,4},{6,7},{7,6},{8,9},{9,8},{10,11... | collective-permute-start | bytes 589832 | tf_op jit(solution)/shard_map/ppermute | solution.py:163
  56.4 12.8 %collective-permute-start.7 = (bf16[8,12288]{1,0:T(8,128)(2,1)S(1)}, bf16[8,12288]{1,0:T(8,128)(2,1)S(1)}, u32[]{:S(2)}, u32[]{:S(2)}) collective-permute-start(bf16[8,12288]{1,0:T(8,128)(2,1)S(1)} %get-tuple-element.27), channel_id=1, source_target_pairs={{0,2},{1,3},{2,0},{3,1},{4,6},{5,7},{6,4},{7,5},{8,10},{9,11},{10,... | collective-permute-start | bytes 589832 | tf_op jit(solution)/shard_map/ppermute | solution.py:163
  57.6 11.6 %collective-permute-start.8 = (bf16[8,12288]{1,0:T(8,128)(2,1)S(1)}, bf16[8,12288]{1,0:T(8,128)(2,1)S(1)}, u32[]{:S(2)}, u32[]{:S(2)}) collective-permute-start(bf16[8,12288]{1,0:T(8,128)(2,1)S(1)} %get-tuple-element.28), channel_id=1, source_target_pairs={{0,3},{1,2},{2,1},{3,0},{4,7},{5,6},{6,5},{7,4},{8,11},{9,10},{10,... | collective-permute-start | bytes 589832 | tf_op jit(solution)/shard_map/ppermute | solution.py:163
  58.1 9.6 %collective-permute-start.23 = (bf16[16,768]{1,0:T(8,128)(2,1)S(1)}, bf16[16,768]{1,0:T(8,128)(2,1)S(1)}, u32[]{:S(2)}, u32[]{:S(2)}) collective-permute-start(bf16[16,768]{1,0:T(8,128)(2,1)S(1)} %get-tuple-element.40), channel_id=1, source_target_pairs={{0,3},{1,2},{2,1},{3,0},{4,7},{5,6},{6,5},{7,4},{8,11},{9,10},{10,... | collective-permute-start | bytes 73736 | tf_op jit(solution)/shard_map/ppermute | solution.py:163
  59.4 9.3 %collective-permute-start.22 = (bf16[16,768]{1,0:T(8,128)(2,1)S(1)}, bf16[16,768]{1,0:T(8,128)(2,1)S(1)}, u32[]{:S(2)}, u32[]{:S(2)}) collective-permute-start(bf16[16,768]{1,0:T(8,128)(2,1)S(1)} %get-tuple-element.41), channel_id=1, source_target_pairs={{0,2},{1,3},{2,0},{3,1},{4,6},{5,7},{6,4},{7,5},{8,10},{9,11},{10,... | collective-permute-start | bytes 73736 | tf_op jit(solution)/shard_map/ppermute | solution.py:163
  67.6 1.6 %collective-permute-start.21 = (bf16[16,768]{1,0:T(8,128)(2,1)S(1)}, bf16[16,768]{1,0:T(8,128)(2,1)S(1)}, u32[]{:S(2)}, u32[]{:S(2)}) collective-permute-start(bf16[16,768]{1,0:T(8,128)(2,1)S(1)} %get-tuple-element.42), channel_id=1, source_target_pairs={{0,1},{1,0},{2,3},{3,2},{4,5},{5,4},{6,7},{7,6},{8,9},{9,8},{10,11... | collective-permute-start | bytes 73736 | tf_op jit(solution)/shard_map/ppermute | solution.py:163
  70.2 6.6 %collective-permute-start.24 = (bf16[4,12288]{1,0:T(4,128)(2,1)S(1)}, bf16[4,12288]{1,0:T(4,128)(2,1)S(1)}, u32[]{:S(2)}, u32[]{:S(2)}) collective-permute-start(bf16[4,12288]{1,0:T(4,128)(2,1)S(1)} %get-tuple-element.34), channel_id=1, source_target_pairs={{0,4},{1,5},{2,6},{3,7},{4,0},{5,1},{6,2},{7,3},{8,12},{9,13},{10,... | collective-permute-start | bytes 294920 | tf_op jit(solution)/shard_map/ppermute | solution.py:160
  71.2 10.7 %collective-permute-start.25 = (bf16[4,12288]{1,0:T(4,128)(2,1)S(1)}, bf16[4,12288]{1,0:T(4,128)(2,1)S(1)}, u32[]{:S(2)}, u32[]{:S(2)}) collective-permute-start(bf16[4,12288]{1,0:T(4,128)(2,1)S(1)} %get-tuple-element.35), channel_id=1, source_target_pairs={{0,8},{1,9},{2,10},{3,11},{4,12},{5,13},{6,14},{7,15},{8,0},{9,1},... | collective-permute-start | bytes 294920 | tf_op jit(solution)/shard_map/ppermute | solution.py:160
  72.7 9.3 %collective-permute-start.26 = (bf16[4,12288]{1,0:T(4,128)(2,1)S(1)}, bf16[4,12288]{1,0:T(4,128)(2,1)S(1)}, u32[]{:S(2)}, u32[]{:S(2)}) collective-permute-start(bf16[4,12288]{1,0:T(4,128)(2,1)S(1)} %get-tuple-element.36), channel_id=1, source_target_pairs={{0,12},{1,13},{2,14},{3,15},{4,8},{5,9},{6,10},{7,11},{8,4},{9,5},... | collective-permute-start | bytes 294920 | tf_op jit(solution)/shard_map/ppermute | solution.py:160
  (2 other events, 1.6 us)

commit v3 on v0

v3 whole, which is shorter than its diff:
```python
import functools

import jax
import jax.numpy as jnp
from jax import lax
from jax.experimental import pallas as pl
from jax.experimental.pallas import tpu as pltpu
from jax.sharding import PartitionSpec as P

MIB = 1 << 20
VMEM = pl.BlockSpec(memory_space=pltpu.VMEM)
SMEM = pl.BlockSpec(memory_space=pltpu.SMEM)
HBM = pl.BlockSpec(memory_space=pl.ANY)
f32, bf16 = jnp.float32, jnp.bfloat16


def piece(width, most):
    size = 128
    while size * 2 <= most and width % (size * 2) == 0:
        size *= 2
    return size


def window(index, size):
    return pl.ds(pl.multiple_of(index * size, 128), size)


def call(body, outs, ins, limit, scratch=(), flops=0, moved=0):
    return pl.pallas_call(
        body,
        out_shape=outs,
        in_specs=ins,
        out_specs=[VMEM] * len(outs),
        scratch_shapes=list(scratch),
        compiler_params=pltpu.CompilerParams(vmem_limit_bytes=limit * MIB),
        cost_estimate=pl.CostEstimate(flops=flops, bytes_accessed=moved, transcendentals=0),
    )


def norm_body(groups, place, hidden, gain, shift, out, *rest):
    strips, (held, gains, shifts, sems) = rest[:groups], rest[groups:]
    copies = [
        pltpu.make_async_copy(src, dst, sems.at[i])
        for i, (src, dst) in enumerate(((hidden, held), (gain, gains), (shift, shifts)))
    ]
    for copy in copies:
        copy.start()
    copies[0].wait()
    wide = held[...].astype(f32)
    mean = jnp.mean(wide, axis=-1, keepdims=True)
    centred = wide - mean
    variance = jnp.mean(centred * centred, axis=-1, keepdims=True)
    copies[1].wait()
    copies[2].wait()
    out[...] = (centred * lax.rsqrt(variance + 1e-05) * gains[...] + shifts[...]).astype(bf16)
    span = strips[0].shape[1]
    for k in range(groups):
        strips[k][...] = out[:, window((place[0] // 4) ^ k, span)]


def sort_body(groups, place, *refs):
    strips, (keep, send) = refs[:groups], refs[groups:]
    span = keep.shape[1]
    upper = (place[0] // 2) % 2
    rows = jnp.concatenate([s[...].astype(f32) for s in strips], axis=0)
    low, high = rows[:, :span], rows[:, span:]
    keep[...] = jnp.where(upper == 0, low, high).astype(bf16)
    send[...] = jnp.where(upper == 0, high, low).astype(bf16)


def down_body(place, keep, got, own, mate, near, far):
    share = own.shape[0]
    core = place[0] % 2
    rows = jnp.concatenate([keep[...].astype(f32), got[...].astype(f32)], axis=0)
    low, high = rows[:, :share], rows[:, share:]
    mine = jnp.where(core == 0, low, high).astype(bf16)
    other = jnp.where(core == 0, high, low).astype(bf16)
    total = jnp.dot(mine, own[...], preferred_element_type=f32) + jnp.dot(
        other, mate[...], preferred_element_type=f32
    )
    half = near.shape[0]
    near[...] = total[:half]
    far[...] = total[half:]


def relu_body(groups, bias, *refs):
    sums, out = refs[:groups], refs[groups]
    rows = out.shape[0] // groups
    for q in range(groups):
        total = bias[...]
        for k in range(groups):
            p = q ^ k
            total = total + sums[k][p * rows : (p + 1) * rows, :]
        out[q * rows : (q + 1) * rows, :] = jnp.maximum(total, 0.0).astype(bf16)


def fetch(srcs, dsts, sems, step, axis):
    copies = []
    for i in range(srcs[0].shape[axis] // step):
        at = (pl.ds(i * step, step), slice(None)) if axis == 0 else (slice(None), pl.ds(i * step, step))
        pair = [pltpu.make_async_copy(s.at[at], d.at[at], sems.at[n, i]) for n, (s, d) in enumerate(zip(srcs, dsts))]
        for copy in pair:
            copy.start()
        copies.append(pair)
    return copies


def act_body(count, step, *refs):
    x, (w_own, w_mate, b_own, b_mate, mask, out, own, mate, sems) = refs[:count], refs[count:]
    copies = fetch((w_own, w_mate), (own, mate), sems, step, 0)
    total = jnp.zeros(out.shape, f32)
    for i, pair in enumerate(copies):
        rows = jnp.concatenate([r[:, i * step : (i + 1) * step] for r in x], axis=0)
        for copy in pair:
            copy.wait()
        both = jnp.concatenate([own[i * step : (i + 1) * step, :], mate[i * step : (i + 1) * step, :]], axis=1)
        total = total + jnp.dot(rows, both, preferred_element_type=f32)
    bias = jnp.concatenate([b_own[...], b_mate[...]], axis=1)
    out[...] = (jnp.maximum(total + bias, 0.0) * mask[...]).astype(bf16)


def part_body(groups, step, place, *refs):
    act, w_own, w_mate, near_h, far_h, low_own, low_mate = refs[:7]
    outs, (own, mate, whole, sems) = refs[7 : 7 + 2 * groups], refs[7 + 2 * groups :]
    share = low_own.shape[1]
    copies = fetch((w_own, w_mate), (own, mate), sems, step, 1)
    for i, pair in enumerate(copies):
        for copy in pair:
            copy.wait()
        both = jnp.concatenate([own[:, i * step : (i + 1) * step], mate[:, i * step : (i + 1) * step]], axis=0)
        whole[:, i * step : (i + 1) * step] = jnp.dot(act[...], both, preferred_element_type=f32)
    core = place[0] % 2
    hidden = jnp.concatenate([near_h[...], far_h[...]], axis=0)
    mine = jnp.dot(hidden, low_own[...], preferred_element_type=f32)
    other = jnp.dot(hidden, low_mate[...], preferred_element_type=f32)
    low, high = jnp.where(core == 0, mine, other), jnp.where(core == 0, other, mine)
    whole[:, window(place[0] // 2, 2 * share)] += jnp.concatenate([low, high], axis=1)
    rows = outs[0].shape[0]
    for q in range(2 * groups):
        outs[q][...] = whole[q * rows : (q + 1) * rows, :].astype(outs[q].dtype)


def activity(lists, counts, block_slot):
    groups, top = lists.shape
    nblocks = block_slot.shape[0]
    names = jnp.arange(nblocks, dtype=jnp.int32)
    live = (jnp.arange(top, dtype=jnp.int32)[None, :] < counts[:, None]).astype(jnp.int32)
    hits = (lists[:, :, None] == names[None, None, :]).astype(jnp.int32) * live[:, :, None]
    by_block = jnp.sum(hits, axis=1)
    placed = (block_slot[:, None] == names[None, :]).astype(jnp.int32)
    return jnp.sum(by_block[:, :, None] * placed[None, :, :], axis=1)


def shards(
    hidden,
    ln_gain,
    ln_shift,
    lists,
    counts,
    block_slot,
    w_in,
    b_in,
    w_out,
    low_in,
    low_bias,
    low_out,
):
    devices = lax.axis_size("blk")
    position = lax.axis_index("blk")
    row_dev, width = hidden.shape
    groups = lists.shape[0]
    share, rank = low_in.shape
    block = w_in.shape[1]
    assert devices == 4 * groups
    plane = position // 4
    place = jnp.reshape(position, (1,)).astype(jnp.int32)
    some, rows = groups * row_dev, 2 * groups * row_dev

    def across(x, k):
        return lax.ppermute(x, "blk", [(i, i ^ (4 * k)) for i in range(devices)])

    def beside(x):
        return lax.ppermute(x, "blk", [(i, i ^ 2) for i in range(devices)])

    def core(x):
        return lax.ppermute(x, "blk", [(i, i ^ 1) for i in range(devices)])

    def shape(*dims, dtype=bf16):
        return jax.ShapeDtypeStruct(dims, dtype)

    normed, *strips = call(
        functools.partial(norm_body, groups),
        [shape(row_dev, width)] + [shape(row_dev, 4 * share)] * groups,
        [SMEM] + [HBM] * 3,
        16,
        [
            pltpu.VMEM((row_dev, width), bf16),
            pltpu.VMEM((1, width), f32),
            pltpu.VMEM((1, width), f32),
            pltpu.SemaphoreType.DMA((3,)),
        ],
    )(place, hidden, ln_gain.reshape(1, width), ln_shift.reshape(1, width))

    bias = b_in.reshape(1, block)
    low_in_mate, low_out_mate, w_in_mate, w_out_mate, bias_mate = (
        core(low_in),
        core(low_out),
        core(w_in),
        core(w_out),
        core(bias),
    )

    strips = [strips[0]] + [across(strips[k], k) for k in range(1, groups)]
    held = [normed] + [across(normed, k) for k in range(1, groups)]
    keep, send = call(
        functools.partial(sort_body, groups), [shape(some, 2 * share)] * 2, [SMEM] + [VMEM] * groups, 16
    )(place, *strips)
    near, far = call(down_body, [shape(some, rank, dtype=f32)] * 2, [SMEM] + [VMEM] * 4, 16)(
        place, keep, beside(send), low_in, low_in_mate
    )
    summed = near + beside(far)
    low_h = call(functools.partial(relu_body, groups), [shape(some, rank)], [VMEM] * (groups + 1), 16)(
        low_bias.reshape(1, rank), summed, *[across(summed, k) for k in range(1, groups)]
    )[0]
    far_h = beside(low_h)

    table = activity(lists, counts, block_slot)
    by = plane ^ jnp.arange(groups)
    at = position ^ jnp.arange(2)
    relate = (by[:, None] == jnp.arange(groups)[None, :])[:, None, :, None]
    choose = (at[:, None] == jnp.arange(devices)[None, :])[None, :, None, :]
    live = jnp.sum(jnp.where(relate & choose, table[None, None], 0), axis=(2, 3)).astype(f32)
    mask = jnp.broadcast_to(live[None, :, None, :, None], (2, groups, row_dev, 2, block)).reshape(rows, 2 * block)

    held = held + [beside(h) for h in held]
    step = piece(width, 2048)
    act = call(
        functools.partial(act_body, 2 * groups, step),
        [shape(rows, 2 * block)],
        [VMEM] * (2 * groups) + [HBM] * 2 + [VMEM] * 3,
        32,
        [pltpu.VMEM((width, block), bf16)] * 2 + [pltpu.SemaphoreType.DMA((2, width // step))],
    )(*held, w_in, w_in_mate, bias, bias_mate, mask)[0]
    parts = call(
        functools.partial(part_body, groups, step),
        [shape(row_dev, width, dtype=f32)] * groups + [shape(row_dev, width)] * groups,
        [SMEM, VMEM] + [HBM] * 2 + [VMEM] * 4,
        32,
        [pltpu.VMEM((block, width), bf16)] * 2
        + [pltpu.VMEM((rows, width), f32), pltpu.SemaphoreType.DMA((2, width // step))],
    )(place, act, w_out, w_out_mate, low_h, far_h, low_out, low_out_mate)
    total = None
    for k in range(groups - 1, -1, -1):
        here = parts[k] + beside(parts[groups + k]).astype(f32)
        if k:
            here = across(here.astype(bf16), k).astype(f32)
        total = here if total is None else total + here
    return total.astype(bf16)


def solution(mesh):
    return jax.shard_map(
        shards,
        mesh=mesh,
        in_specs=(
            P(("rep", "blk"), None),
            P(),
            P(),
            P("rep", None),
            P("rep"),
            P(),
            P(None, "blk"),
            P("blk"),
            P("blk", None),
            P("blk", None),
            P(),
            P(None, "blk"),
        ),
        out_specs=P(("rep", "blk"), None),
        check_vma=False,
    )
```

time: 234 us -> 81.5 us (0.35); the launches traced: 230 us -> 81 us
  waiting for transfers between devices: 156 us -> 25.7 us
  starting transfers between devices: 9.56 us -> 32.5 us
  blocking collectives: 22.2 us -> 0 us
  between operations: 14.2 us -> 0.15 us
  Pallas kernels: 0 us -> 10.5 us
  matrix products: 8.25 us -> 0 us
  other arithmetic: 9.27 us -> 2.93 us
    unnamed x3 -> x0, waiting for transfers between devices: 86 us -> none
    all_gather x1 -> x0, waiting for transfers between devices: 37.8 us -> none  [shards(): every = lax.all_gather(normed, 'blk', axis=0, tiled=True)]
    ppermute x0 -> x28, starting transfers between devices: none -> 32.5 us  [the longest x12 17.9 us: across(): return lax.ppermute(x, 'blk', [(i, i ^ 4 * k) for i in range(devices)])]
    all_to_all x2 -> x0, waiting for transfers between devices: 32 us -> none  [the longest x1 32 us: shards(): lax.all_to_all(result, 'blk', split_axis=0, concat_axis=0, tiled=True)]
    ppermute x0 -> x28, waiting for transfers between devices: none -> 25.7 us  [the longest x12 18.7 us: across(): return lax.ppermute(x, 'blk', [(i, i ^ 4 * k) for i in range(devices)])]
    all_gather x1 -> x0, blocking collectives: 22.2 us -> none  [shards(): lax.all_gather(low_h, 'blk', axis=0, tiled=True)]
    pallas_call x0 -> x6, Pallas kernels: none -> 10.5 us  [the longest x1 4.44 us: shards(): call(functools.partial(act_body, 2 * groups, step), [shape(rows, 2 * bloc...]
    all_to_all x2 -> x0, starting transfers between devices: 9.52 us -> none  [the longest x1 6.01 us: shards(): lax.all_to_all(result, 'blk', split_axis=0, concat_axis=0, tiled=True)]
  transfers between devices with their start and end apart: 4 -> 28, of which waited for: 3 -> 14; matrix products, arithmetic and copies ran while one was open for 4% -> 4% of each run, Pallas kernels for 0% -> 8%
where the time goes in v3:
time: 81.5 us; the launch traced here: 81 us
  starting transfers between devices  32.5 us (40%)
  waiting for transfers between devices  25.7 us (32%)
  Pallas kernels  10.5 us (13%)
  local copies, waits for them, and re-layouts  9.23 us (11%)
  other arithmetic  2.93 us (4%)
    ppermute x12, waiting for transfers between devices, across(): return lax.ppermute(x, 'blk', [(i, i ^ 4 * k) for i in range(devices)])  18.7 us
    ppermute x12, starting transfers between devices, across(): return lax.ppermute(x, 'blk', [(i, i ^ 4 * k) for i in range(devices)])  17.9 us
    ppermute x11, starting transfers between devices, beside(): return lax.ppermute(x, 'blk', [(i, i ^ 2) for i in range(devices)])  13.6 us
    unnamed x24, local copies, waits for them, and re-layouts  9.16 us
    ppermute x11, waiting for transfers between devices, beside(): return lax.ppermute(x, 'blk', [(i, i ^ 2) for i in range(devices)])  6.9 us
    pallas_call x1, Pallas kernels, shards(): call(functools.partial(act_body, 2 * groups, step), [shape(rows, 2 * bloc...  4.44 us
    pallas_call x1, Pallas kernels, shards(): call(functools.partial(part_body, groups, step), [shape(row_dev, width, d...  3.84 us
  transfers between devices with their start and end apart: 28, of which 14 were waited for; matrix products, arithmetic and copies ran while one was open for 4% of the time, Pallas kernels for 8%

profile of v3, /device:TPU:0, one launch (start us, length us, event | category | flops | bytes accessed | tf_op | source)
XLA Modules:
  0.0 81.0 jit_solution(9526037443360289051)
XLA Ops:
  1.0 0.9 %copy-done.4 = bf16[4,12288]{1,0:T(4,128)(2,1)S(1)} copy-done((bf16[4,12288]{1,0:T(4,128)(2,1)S(1)}, bf16[4,12288]{1,0:T(4,128)(2,1)}, u32[]{:S(2)}) %copy-start.4) | copy-done | bytes 98328
  4.2 2.6 %collective-permute-start.10 = (bf16[4,3072]{1,0:T(4,128)(2,1)S(1)}, bf16[4,3072]{1,0:T(4,128)(2,1)S(1)}, u32[]{:S(2)}, u32[]{:S(2)}) collective-permute-start(bf16[4,3072]{1,0:T(4,128)(2,1)S(1)} %get-tuple-element.24), channel_id=1, source_target_pairs={{0,4},{1,5},{2,6},{3,7},{4,0},{5,1},{6,2},{7,3},{8,12},{9,13},{10,... | collective-permute-start | bytes 73736 | tf_op jit(solution)/shard_map/ppermute | solution.py:180
  6.8 2.6 %collective-permute-start.11 = (bf16[4,3072]{1,0:T(4,128)(2,1)S(1)}, bf16[4,3072]{1,0:T(4,128)(2,1)S(1)}, u32[]{:S(2)}, u32[]{:S(2)}) collective-permute-start(bf16[4,3072]{1,0:T(4,128)(2,1)S(1)} %get-tuple-element.25), channel_id=1, source_target_pairs={{0,8},{1,9},{2,10},{3,11},{4,12},{5,13},{6,14},{7,15},{8,0},{9,1},... | collective-permute-start | bytes 73736 | tf_op jit(solution)/shard_map/ppermute | solution.py:180
  10.1 2.5 %collective-permute-start.12 = (bf16[4,3072]{1,0:T(4,128)(2,1)S(1)}, bf16[4,3072]{1,0:T(4,128)(2,1)S(1)}, u32[]{:S(2)}, u32[]{:S(2)}) collective-permute-start(bf16[4,3072]{1,0:T(4,128)(2,1)S(1)} %get-tuple-element.26), channel_id=1, source_target_pairs={{0,12},{1,13},{2,14},{3,15},{4,8},{5,9},{6,10},{7,11},{8,4},{9,5},... | collective-permute-start | bytes 73736 | tf_op jit(solution)/shard_map/ppermute | solution.py:180
  13.3 2.4 %collective-permute-done.12.refs_3_ = bf16[4,3072]{1,0:T(4,128)(2,1)S(1)} collective-permute-done((bf16[4,3072]{1,0:T(4,128)(2,1)S(1)}, bf16[4,3072]{1,0:T(4,128)(2,1)S(1)}, u32[]{:S(2)}, u32[]{:S(2)}) %collective-permute-start.12) | collective-permute-done | bytes 24608 | tf_op jit(solution)/shard_map/ppermute | solution.py:180
  15.8 1.6 %collective-permute-start.13 = (bf16[16,1536]{1,0:T(8,128)(2,1)S(1)}, bf16[16,1536]{1,0:T(8,128)(2,1)S(1)}, u32[]{:S(2)}, u32[]{:S(2)}) collective-permute-start(bf16[16,1536]{1,0:T(8,128)(2,1)S(1)} %get-tuple-element.28), channel_id=1, source_target_pairs={{0,2},{1,3},{2,0},{3,1},{4,6},{5,7},{6,4},{7,5},{8,10},{9,11},{10,... | collective-permute-start | bytes 147464 | tf_op jit(solution)/shard_map/ppermute | solution.py:183
  17.4 2.6 %collective-permute-done.13.got = bf16[16,1536]{1,0:T(8,128)(2,1)S(1)} collective-permute-done((bf16[16,1536]{1,0:T(8,128)(2,1)S(1)}, bf16[16,1536]{1,0:T(8,128)(2,1)S(1)}, u32[]{:S(2)}, u32[]{:S(2)}) %collective-permute-start.13) | collective-permute-done | bytes 49184 | tf_op jit(solution)/shard_map/ppermute | solution.py:183
  20.0 1.5 %collective-permute-start.3 = (bf16[4,12288]{1,0:T(4,128)(2,1)S(1)}, bf16[4,12288]{1,0:T(4,128)(2,1)S(1)}, u32[]{:S(2)}, u32[]{:S(2)}) collective-permute-start(bf16[4,12288]{1,0:T(4,128)(2,1)S(1)} %get-tuple-element.22.refs_0_), channel_id=1, source_target_pairs={{0,2},{1,3},{2,0},{3,1},{4,6},{5,7},{6,4},{7,5},{8,10},{9,11},{10,... | collective-permute-start | bytes 294920 | tf_op jit(solution)/shard_map/ppermute | solution.py:183
  21.5 1.1 %copy-done.2 = bf16[768,512]{1,0:T(8,128)(2,1)S(1)} copy-done((bf16[768,512]{1,0:T(8,128)(2,1)S(1)}, bf16[768,512]{1,0:T(8,128)(2,1)}, u32[]{:S(2)}) %copy-start.2) | copy-done | bytes 786456
  22.6 1.5 %shard_map.121 = (f32[16,512]{1,0:T(8,128)S(1)}, f32[16,512]{1,0:T(8,128)S(1)}) custom-call(s32[1]{0:T(128)} %bitcast.place, bf16[16,1536]{1,0:T(8,128)(2,1)S(1)} %get-tuple-element.27.keep, bf16[16,1536]{1,0:T(8,128)(2,1)S(1)} %collective-permute-done.13.got, bf16[768,512]{1,0:T(8,128)(2,1)S(1)} %copy-done.2, bf16[768,512]{1,0:T(8,128)(2,1)} %collective-permute-done.14.mate), custom_call_target="tpu_custom_call" | custom-call | tf_op jit(solution)/shard_map/pallas_call | solution.py:218
  24.7 2.8 %collective-permute-start.2 = (bf16[4,12288]{1,0:T(4,128)(2,1)S(1)}, bf16[4,12288]{1,0:T(4,128)(2,1)S(1)}, u32[]{:S(2)}, u32[]{:S(2)}) collective-permute-start(bf16[4,12288]{1,0:T(4,128)(2,1)S(1)} %get-tuple-element.22.refs_0_), channel_id=1, source_target_pairs={{0,12},{1,13},{2,14},{3,15},{4,8},{5,9},{6,10},{7,11},{8,4},{9,5},... | collective-permute-start | bytes 294920 | tf_op jit(solution)/shard_map/ppermute | solution.py:180
  28.1 3.8 %collective-permute-done.2.refs_3_ = bf16[4,12288]{1,0:T(4,128)(2,1)S(1)} collective-permute-done((bf16[4,12288]{1,0:T(4,128)(2,1)S(1)}, bf16[4,12288]{1,0:T(4,128)(2,1)S(1)}, u32[]{:S(2)}, u32[]{:S(2)}) %collective-permute-start.2) | collective-permute-done | bytes 98336 | tf_op jit(solution)/shard_map/ppermute | solution.py:180
  31.9 3.9 %collective-permute-done.1.refs_2_ = bf16[4,12288]{1,0:T(4,128)(2,1)S(1)} collective-permute-done((bf16[4,12288]{1,0:T(4,128)(2,1)S(1)}, bf16[4,12288]{1,0:T(4,128)(2,1)S(1)}, u32[]{:S(2)}, u32[]{:S(2)}) %collective-permute-start.1) | collective-permute-done | bytes 98336 | tf_op jit(solution)/shard_map/ppermute | solution.py:180
  36.4 2.8 %collective-permute-start.18 = (f32[16,512]{1,0:T(8,128)S(1)}, f32[16,512]{1,0:T(8,128)S(1)}, u32[]{:S(2)}, u32[]{:S(2)}) collective-permute-start(f32[16,512]{1,0:T(8,128)S(1)} %add.25.refs_0_), channel_id=1, source_target_pairs={{0,12},{1,13},{2,14},{3,15},{4,8},{5,9},{6,10},{7,11},{8,4},{9,5},... | collective-permute-start | bytes 98312 | tf_op jit(solution)/shard_map/ppermute | solution.py:180
  40.1 2.2 %collective-permute-done.18.refs_3_ = f32[16,512]{1,0:T(8,128)S(1)} collective-permute-done((f32[16,512]{1,0:T(8,128)S(1)}, f32[16,512]{1,0:T(8,128)S(1)}, u32[]{:S(2)}, u32[]{:S(2)}) %collective-permute-start.18) | collective-permute-done | bytes 32800 | tf_op jit(solution)/shard_map/ppermute | solution.py:180
  42.4 2.5 %collective-permute-done.17.refs_2_ = f32[16,512]{1,0:T(8,128)S(1)} collective-permute-done((f32[16,512]{1,0:T(8,128)S(1)}, f32[16,512]{1,0:T(8,128)S(1)}, u32[]{:S(2)}, u32[]{:S(2)}) %collective-permute-start.17) | collective-permute-done | bytes 32800 | tf_op jit(solution)/shard_map/ppermute | solution.py:180
  44.9 1.5 %collective-permute-start.6 = (bf16[4,12288]{1,0:T(4,128)(2,1)S(1)}, bf16[4,12288]{1,0:T(4,128)(2,1)S(1)}, u32[]{:S(2)}, u32[]{:S(2)}) collective-permute-start(bf16[4,12288]{1,0:T(4,128)(2,1)S(1)} %collective-permute-done.2.refs_3_), channel_id=1, source_target_pairs={{0,2},{1,3},{2,0},{3,1},{4,6},{5,7},{6,4},{7,5},{8,10},{9,11},{10,... | collective-permute-start | bytes 294920 | tf_op jit(solution)/shard_map/ppermute | solution.py:183
  46.4 1.3 %collective-permute-start.5 = (bf16[4,12288]{1,0:T(4,128)(2,1)}, bf16[4,12288]{1,0:T(4,128)(2,1)S(1)}, u32[]{:S(2)}, u32[]{:S(2)}) collective-permute-start(bf16[4,12288]{1,0:T(4,128)(2,1)} %copy-done.5), channel_id=1, source_target_pairs={{0,2},{1,3},{2,0},{3,1},{4,6},{5,7},{6,4},{7,5},{8,10},{9,11},{10,... | collective-permute-start | bytes 294920 | tf_op jit(solution)/shard_map/ppermute | solution.py:183
  48.6 1.0 %collective-permute-done.6.refs_7_ = bf16[4,12288]{1,0:T(4,128)(2,1)S(1)} collective-permute-done((bf16[4,12288]{1,0:T(4,128)(2,1)S(1)}, bf16[4,12288]{1,0:T(4,128)(2,1)S(1)}, u32[]{:S(2)}, u32[]{:S(2)}) %collective-permute-start.6) | collective-permute-done | bytes 98336 | tf_op jit(solution)/shard_map/ppermute | solution.py:183
  49.6 1.5 %collective-permute-start.4 = (bf16[4,12288]{1,0:T(4,128)(2,1)}, bf16[4,12288]{1,0:T(4,128)(2,1)S(1)}, u32[]{:S(2)}, u32[]{:S(2)}) collective-permute-start(bf16[4,12288]{1,0:T(4,128)(2,1)} %collective-permute-done.refs_1_), channel_id=1, source_target_pairs={{0,2},{1,3},{2,0},{3,1},{4,6},{5,7},{6,4},{7,5},{8,10},{9,11},{10,... | collective-permute-start | bytes 294920 | tf_op jit(solution)/shard_map/ppermute | solution.py:183
  51.1 0.9 %collective-permute-done.5.refs_6_ = bf16[4,12288]{1,0:T(4,128)(2,1)S(1)} collective-permute-done((bf16[4,12288]{1,0:T(4,128)(2,1)}, bf16[4,12288]{1,0:T(4,128)(2,1)S(1)}, u32[]{:S(2)}, u32[]{:S(2)}) %collective-permute-start.5) | collective-permute-done | bytes 98336 | tf_op jit(solution)/shard_map/ppermute | solution.py:183
  52.0 1.5 %collective-permute-start.19 = (bf16[16,512]{1,0:T(8,128)(2,1)S(1)}, bf16[16,512]{1,0:T(8,128)(2,1)S(1)}, u32[]{:S(2)}, u32[]{:S(2)}) collective-permute-start(bf16[16,512]{1,0:T(8,128)(2,1)S(1)} %shard_map.122.refs_3_), channel_id=1, source_target_pairs={{0,2},{1,3},{2,0},{3,1},{4,6},{5,7},{6,4},{7,5},{8,10},{9,11},{10,... | collective-permute-start | bytes 49160 | tf_op jit(solution)/shard_map/ppermute | solution.py:183
  54.4 1.9 %copy-done = bf16[12288,128]{1,0:T(8,128)(2,1)S(1)} copy-done((bf16[12288,128]{1,0:T(8,128)(2,1)S(1)}, bf16[12288,128]{1,0:T(8,128)(2,1)}, u32[]{:S(2)}) %copy-start) | copy-done | bytes 3145752
  57.9 4.4 %shard_map.119.refs_0_ = bf16[32,256]{1,0:T(8,128)(2,1)S(1)} custom-call(bf16[4,12288]{1,0:T(4,128)(2,1)S(1)} %get-tuple-element.22.refs_0_, bf16[4,12288]{1,0:T(4,128)(2,1)} %collective-permute-done.refs_1_, bf16[4,12288]{1,0:T(4,128)(2,1)S(1)} %copy-done.6, bf16[4,12288]{1,0:T(4,128)(2,1)S(1)} %collective-permute-done.2.refs_3_, ...), custom_call_target="tpu_custom_call" | custom-call | tf_op jit(solution)/shard_map/pallas_call | solution.py:237
  62.4 3.8 %shard_map.123 = (f32[4,12288]{1,0:T(4,128)S(1)}, f32[4,12288]{1,0:T(4,128)S(1)}, f32[4,12288]{1,0:T(4,128)S(1)}, f32[4,12288]{1,0:T(4,128)S(1)}, bf16[4,12288]{...) custom-call(s32[1]{0:T(128)} %bitcast.place, ...), custom_call_target="tpu_custom_call" | custom-call | tf_op jit(solution)/shard_map/pallas_call | solution.py:244
  66.2 1.5 %collective-permute-start.21 = (bf16[4,12288]{1,0:T(4,128)(2,1)S(1)}, bf16[4,12288]{1,0:T(4,128)(2,1)S(1)}, u32[]{:S(2)}, u32[]{:S(2)}) collective-permute-start(bf16[4,12288]{1,0:T(4,128)(2,1)S(1)} %get-tuple-element.32), channel_id=1, source_target_pairs={{0,2},{1,3},{2,0},{3,1},{4,6},{5,7},{6,4},{7,5},{8,10},{9,11},{10,... | collective-permute-start | bytes 294920 | tf_op jit(solution)/shard_map/ppermute | solution.py:183
  68.3 1.5 %collective-permute-start.25 = (bf16[4,12288]{1,0:T(4,128)(2,1)S(1)}, bf16[4,12288]{1,0:T(4,128)(2,1)S(1)}, u32[]{:S(2)}, u32[]{:S(2)}) collective-permute-start(bf16[4,12288]{1,0:T(4,128)(2,1)S(1)} %get-tuple-element.36), channel_id=1, source_target_pairs={{0,2},{1,3},{2,0},{3,1},{4,6},{5,7},{6,4},{7,5},{8,10},{9,11},{10,... | collective-permute-start | bytes 294920 | tf_op jit(solution)/shard_map/ppermute | solution.py:183
  70.4 1.2 %collective-permute-done.21 = bf16[4,12288]{1,0:T(4,128)(2,1)S(1)} collective-permute-done((bf16[4,12288]{1,0:T(4,128)(2,1)S(1)}, bf16[4,12288]{1,0:T(4,128)(2,1)S(1)}, u32[]{:S(2)}, u32[]{:S(2)}) %collective-permute-start.21) | collective-permute-done | bytes 98336 | tf_op jit(solution)/shard_map/ppermute | solution.py:183
  71.6 1.4 %collective-permute-start.22 = (bf16[4,12288]{1,0:T(4,128)(2,1)S(1)}, bf16[4,12288]{1,0:T(4,128)(2,1)S(1)}, u32[]{:S(2)}, u32[]{:S(2)}) collective-permute-start(bf16[4,12288]{1,0:T(4,128)(2,1)S(1)} %add_convert_fusion.3), channel_id=1, source_target_pairs={{0,12},{1,13},{2,14},{3,15},{4,8},{5,9},{6,10},{7,11},{8,4},{9,5},... | collective-permute-start | bytes 294920 | tf_op jit(solution)/shard_map/ppermute | solution.py:180
  73.7 2.6 %collective-permute-start.26 = (bf16[4,12288]{1,0:T(4,128)(2,1)S(1)}, bf16[4,12288]{1,0:T(4,128)(2,1)S(1)}, u32[]{:S(2)}, u32[]{:S(2)}) collective-permute-start(bf16[4,12288]{1,0:T(4,128)(2,1)S(1)} %add_convert_fusion.1), channel_id=1, source_target_pairs={{0,4},{1,5},{2,6},{3,7},{4,0},{5,1},{6,2},{7,3},{8,12},{9,13},{10,... | collective-permute-start | bytes 294920 | tf_op jit(solution)/shard_map/ppermute | solution.py:180
  76.3 1.9 %collective-permute-done.22 = bf16[4,12288]{1,0:T(4,128)(2,1)S(1)} collective-permute-done((bf16[4,12288]{1,0:T(4,128)(2,1)S(1)}, bf16[4,12288]{1,0:T(4,128)(2,1)S(1)}, u32[]{:S(2)}, u32[]{:S(2)}) %collective-permute-start.22) | collective-permute-done | bytes 98336 | tf_op jit(solution)/shard_map/ppermute | solution.py:180
  78.2 2.0 %collective-permute-done.24 = bf16[4,12288]{1,0:T(4,128)(2,1)S(1)} collective-permute-done((bf16[4,12288]{1,0:T(4,128)(2,1)S(1)}, bf16[4,12288]{1,0:T(4,128)(2,1)S(1)}, u32[]{:S(2)}, u32[]{:S(2)}) %collective-permute-start.24) | collective-permute-done | bytes 98336 | tf_op jit(solution)/shard_map/ppermute | solution.py:180
  (70 shorter events, 13.3 us)
Async XLA Ops:
  0.0 54.4 %collective-permute-start.7 = (bf16[12288,128]{1,0:T(8,128)(2,1)}, bf16[12288,128]{1,0:T(8,128)(2,1)}, u32[]{:S(2)}, u32[]{:S(2)}) collective-permute-start(bf16[12288,128]{1,0:T(8,128)(2,1)} %refs_8_.1), channel_id=1, source_target_pairs={{0,1},{1,0},{2,3},{3,2},{4,5},{5,4},{6,7},{7,6},{8,9},{9,8},{10,11... | collective-permute-start | bytes 9437192 | tf_op jit(solution)/shard_map/ppermute | solution.py:186
  0.5 61.9 %collective-permute-start.9 = (bf16[128,12288]{1,0:T(8,128)(2,1)}, bf16[128,12288]{1,0:T(8,128)(2,1)S(1)}, u32[]{:S(2)}, u32[]{:S(2)}) collective-permute-start(bf16[128,12288]{1,0:T(8,128)(2,1)} %refs_1_.1), channel_id=1, source_target_pairs={{0,1},{1,0},{2,3},{3,2},{4,5},{5,4},{6,7},{7,6},{8,9},{9,8},{10,11... | collective-permute-start | bytes 9437192 | tf_op jit(solution)/shard_map/ppermute | solution.py:186
  0.5 21.0 %collective-permute-start.14 = (bf16[768,512]{1,0:T(8,128)(2,1)}, bf16[768,512]{1,0:T(8,128)(2,1)}, u32[]{:S(2)}, u32[]{:S(2)}) collective-permute-start(bf16[768,512]{1,0:T(8,128)(2,1)} %own.1), channel_id=1, source_target_pairs={{0,1},{1,0},{2,3},{3,2},{4,5},{5,4},{6,7},{7,6},{8,9},{9,8},{10,11... | collective-permute-start | bytes 2359304 | tf_op jit(solution)/shard_map/ppermute | solution.py:186
  4.2 6.0 %collective-permute-start.10 = (bf16[4,3072]{1,0:T(4,128)(2,1)S(1)}, bf16[4,3072]{1,0:T(4,128)(2,1)S(1)}, u32[]{:S(2)}, u32[]{:S(2)}) collective-permute-start(bf16[4,3072]{1,0:T(4,128)(2,1)S(1)} %get-tuple-element.24), channel_id=1, source_target_pairs={{0,4},{1,5},{2,6},{3,7},{4,0},{5,1},{6,2},{7,3},{8,12},{9,13},{10,... | collective-permute-start | bytes 73736 | tf_op jit(solution)/shard_map/ppermute | solution.py:180
  6.8 6.5 %collective-permute-start.11 = (bf16[4,3072]{1,0:T(4,128)(2,1)S(1)}, bf16[4,3072]{1,0:T(4,128)(2,1)S(1)}, u32[]{:S(2)}, u32[]{:S(2)}) collective-permute-start(bf16[4,3072]{1,0:T(4,128)(2,1)S(1)} %get-tuple-element.25), channel_id=1, source_target_pairs={{0,8},{1,9},{2,10},{3,11},{4,12},{5,13},{6,14},{7,15},{8,0},{9,1},... | collective-permute-start | bytes 73736 | tf_op jit(solution)/shard_map/ppermute | solution.py:180
  10.1 5.6 %collective-permute-start.12 = (bf16[4,3072]{1,0:T(4,128)(2,1)S(1)}, bf16[4,3072]{1,0:T(4,128)(2,1)S(1)}, u32[]{:S(2)}, u32[]{:S(2)}) collective-permute-start(bf16[4,3072]{1,0:T(4,128)(2,1)S(1)} %get-tuple-element.26), channel_id=1, source_target_pairs={{0,12},{1,13},{2,14},{3,15},{4,8},{5,9},{6,10},{7,11},{8,4},{9,5},... | collective-permute-start | bytes 73736 | tf_op jit(solution)/shard_map/ppermute | solution.py:180
  13.3 10.8 %collective-permute-start.8 = (f32[1,128]{1,0:T(1,128)}, f32[1,128]{1,0:T(1,128)S(1)}, u32[]{:S(2)}, u32[]{:S(2)}) collective-permute-start(f32[1,128]{1,0:T(1,128)} %bitcast.14), channel_id=1, source_target_pairs={{0,1},{1,0},{2,3},{3,2},{4,5},{5,4},{6,7},{7,6},{8,9},{9,8},{10,11... | collective-permute-start | bytes 1544 | tf_op jit(solution)/shard_map/ppermute | solution.py:186
  15.8 4.2 %collective-permute-start.13 = (bf16[16,1536]{1,0:T(8,128)(2,1)S(1)}, bf16[16,1536]{1,0:T(8,128)(2,1)S(1)}, u32[]{:S(2)}, u32[]{:S(2)}) collective-permute-start(bf16[16,1536]{1,0:T(8,128)(2,1)S(1)} %get-tuple-element.28), channel_id=1, source_target_pairs={{0,2},{1,3},{2,0},{3,1},{4,6},{5,7},{6,4},{7,5},{8,10},{9,11},{10,... | collective-permute-start | bytes 147464 | tf_op jit(solution)/shard_map/ppermute | solution.py:183
  20.0 4.8 %collective-permute-start.3 = (bf16[4,12288]{1,0:T(4,128)(2,1)S(1)}, bf16[4,12288]{1,0:T(4,128)(2,1)S(1)}, u32[]{:S(2)}, u32[]{:S(2)}) collective-permute-start(bf16[4,12288]{1,0:T(4,128)(2,1)S(1)} %get-tuple-element.22.refs_0_), channel_id=1, source_target_pairs={{0,2},{1,3},{2,0},{3,1},{4,6},{5,7},{6,4},{7,5},{8,10},{9,11},{10,... | collective-permute-start | bytes 294920 | tf_op jit(solution)/shard_map/ppermute | solution.py:183
  21.5 40.9 %collective-permute-start.20 = (bf16[512,768]{1,0:T(8,128)(2,1)}, bf16[512,768]{1,0:T(8,128)(2,1)}, u32[]{:S(2)}, u32[]{:S(2)}) collective-permute-start(bf16[512,768]{1,0:T(8,128)(2,1)} %refs_5_.1), channel_id=1, source_target_pairs={{0,1},{1,0},{2,3},{3,2},{4,5},{5,4},{6,7},{7,6},{8,9},{9,8},{10,11... | collective-permute-start | bytes 2359304 | tf_op jit(solution)/shard_map/ppermute | solution.py:186
  21.5 1.1 %copy-start.2 = (bf16[768,512]{1,0:T(8,128)(2,1)S(1)}, bf16[768,512]{1,0:T(8,128)(2,1)}, u32[]{:S(2)}) copy-start(bf16[768,512]{1,0:T(8,128)(2,1)} %own.1) | copy-start | bytes 2359300
  24.1 4.0 %collective-permute-start.15 = (f32[16,512]{1,0:T(8,128)S(1)}, f32[16,512]{1,0:T(8,128)S(1)}, u32[]{:S(2)}, u32[]{:S(2)}) collective-permute-start(f32[16,512]{1,0:T(8,128)S(1)} %get-tuple-element.30), channel_id=1, source_target_pairs={{0,2},{1,3},{2,0},{3,1},{4,6},{5,7},{6,4},{7,5},{8,10},{9,11},{10,... | collective-permute-start | bytes 98312 | tf_op jit(solution)/shard_map/ppermute | solution.py:183
  24.7 7.2 %collective-permute-start.2 = (bf16[4,12288]{1,0:T(4,128)(2,1)S(1)}, bf16[4,12288]{1,0:T(4,128)(2,1)S(1)}, u32[]{:S(2)}, u32[]{:S(2)}) collective-permute-start(bf16[4,12288]{1,0:T(4,128)(2,1)S(1)} %get-tuple-element.22.refs_0_), channel_id=1, source_target_pairs={{0,12},{1,13},{2,14},{3,15},{4,8},{5,9},{6,10},{7,11},{8,4},{9,5},... | collective-permute-start | bytes 294920 | tf_op jit(solution)/shard_map/ppermute | solution.py:180
  28.1 7.7 %collective-permute-start.1 = (bf16[4,12288]{1,0:T(4,128)(2,1)S(1)}, bf16[4,12288]{1,0:T(4,128)(2,1)S(1)}, u32[]{:S(2)}, u32[]{:S(2)}) collective-permute-start(bf16[4,12288]{1,0:T(4,128)(2,1)S(1)} %get-tuple-element.22.refs_0_), channel_id=1, source_target_pairs={{0,8},{1,9},{2,10},{3,11},{4,12},{5,13},{6,14},{7,15},{8,0},{9,1},... | collective-permute-start | bytes 294920 | tf_op jit(solution)/shard_map/ppermute | solution.py:180
  31.9 8.2 %collective-permute-start = (bf16[4,12288]{1,0:T(4,128)(2,1)S(1)}, bf16[4,12288]{1,0:T(4,128)(2,1)}, u32[]{:S(2)}, u32[]{:S(2)}) collective-permute-start(bf16[4,12288]{1,0:T(4,128)(2,1)S(1)} %get-tuple-element.22.refs_0_), channel_id=1, source_target_pairs={{0,4},{1,5},{2,6},{3,7},{4,0},{5,1},{6,2},{7,3},{8,12},{9,13},{10,... | collective-permute-start | bytes 294920 | tf_op jit(solution)/shard_map/ppermute | solution.py:180
  36.4 5.9 %collective-permute-start.18 = (f32[16,512]{1,0:T(8,128)S(1)}, f32[16,512]{1,0:T(8,128)S(1)}, u32[]{:S(2)}, u32[]{:S(2)}) collective-permute-start(f32[16,512]{1,0:T(8,128)S(1)} %add.25.refs_0_), channel_id=1, source_target_pairs={{0,12},{1,13},{2,14},{3,15},{4,8},{5,9},{6,10},{7,11},{8,4},{9,5},... | collective-permute-start | bytes 98312 | tf_op jit(solution)/shard_map/ppermute | solution.py:180
  40.1 4.8 %collective-permute-start.17 = (f32[16,512]{1,0:T(8,128)S(1)}, f32[16,512]{1,0:T(8,128)S(1)}, u32[]{:S(2)}, u32[]{:S(2)}) collective-permute-start(f32[16,512]{1,0:T(8,128)S(1)} %add.25.refs_0_), channel_id=1, source_target_pairs={{0,8},{1,9},{2,10},{3,11},{4,12},{5,13},{6,14},{7,15},{8,0},{9,1},... | collective-permute-start | bytes 98312 | tf_op jit(solution)/shard_map/ppermute | solution.py:180
  42.3 4.1 %collective-permute-start.16 = (f32[16,512]{1,0:T(8,128)S(1)}, f32[16,512]{1,0:T(8,128)S(1)}, u32[]{:S(2)}, u32[]{:S(2)}) collective-permute-start(f32[16,512]{1,0:T(8,128)S(1)} %add.25.refs_0_), channel_id=1, source_target_pairs={{0,4},{1,5},{2,6},{3,7},{4,0},{5,1},{6,2},{7,3},{8,12},{9,13},{10,... | collective-permute-start | bytes 98312 | tf_op jit(solution)/shard_map/ppermute | solution.py:180
  44.9 4.7 %collective-permute-start.6 = (bf16[4,12288]{1,0:T(4,128)(2,1)S(1)}, bf16[4,12288]{1,0:T(4,128)(2,1)S(1)}, u32[]{:S(2)}, u32[]{:S(2)}) collective-permute-start(bf16[4,12288]{1,0:T(4,128)(2,1)S(1)} %collective-permute-done.2.refs_3_), channel_id=1, source_target_pairs={{0,2},{1,3},{2,0},{3,1},{4,6},{5,7},{6,4},{7,5},{8,10},{9,11},{10,... | collective-permute-start | bytes 294920 | tf_op jit(solution)/shard_map/ppermute | solution.py:183
  46.4 5.6 %collective-permute-start.5 = (bf16[4,12288]{1,0:T(4,128)(2,1)}, bf16[4,12288]{1,0:T(4,128)(2,1)S(1)}, u32[]{:S(2)}, u32[]{:S(2)}) collective-permute-start(bf16[4,12288]{1,0:T(4,128)(2,1)} %copy-done.5), channel_id=1, source_target_pairs={{0,2},{1,3},{2,0},{3,1},{4,6},{5,7},{6,4},{7,5},{8,10},{9,11},{10,... | collective-permute-start | bytes 294920 | tf_op jit(solution)/shard_map/ppermute | solution.py:183
  49.6 4.8 %collective-permute-start.4 = (bf16[4,12288]{1,0:T(4,128)(2,1)}, bf16[4,12288]{1,0:T(4,128)(2,1)S(1)}, u32[]{:S(2)}, u32[]{:S(2)}) collective-permute-start(bf16[4,12288]{1,0:T(4,128)(2,1)} %collective-permute-done.refs_1_), channel_id=1, source_target_pairs={{0,2},{1,3},{2,0},{3,1},{4,6},{5,7},{6,4},{7,5},{8,10},{9,11},{10,... | collective-permute-start | bytes 294920 | tf_op jit(solution)/shard_map/ppermute | solution.py:183
  52.0 10.3 %collective-permute-start.19 = (bf16[16,512]{1,0:T(8,128)(2,1)S(1)}, bf16[16,512]{1,0:T(8,128)(2,1)S(1)}, u32[]{:S(2)}, u32[]{:S(2)}) collective-permute-start(bf16[16,512]{1,0:T(8,128)(2,1)S(1)} %shard_map.122.refs_3_), channel_id=1, source_target_pairs={{0,2},{1,3},{2,0},{3,1},{4,6},{5,7},{6,4},{7,5},{8,10},{9,11},{10,... | collective-permute-start | bytes 49160 | tf_op jit(solution)/shard_map/ppermute | solution.py:183
  54.4 1.9 %copy-start = (bf16[12288,128]{1,0:T(8,128)(2,1)S(1)}, bf16[12288,128]{1,0:T(8,128)(2,1)}, u32[]{:S(2)}) copy-start(bf16[12288,128]{1,0:T(8,128)(2,1)} %refs_8_.1) | copy-start | bytes 9437188
  57.9 4.5 %copy-start.1 = (bf16[128,12288]{1,0:T(8,128)(2,1)S(1)}, bf16[128,12288]{1,0:T(8,128)(2,1)}, u32[]{:S(2)}) copy-start(bf16[128,12288]{1,0:T(8,128)(2,1)} %refs_1_.1) | copy-start | bytes 9437188
  57.9 4.5 %copy-start.3 = (bf16[512,768]{1,0:T(8,128)(2,1)S(1)}, bf16[512,768]{1,0:T(8,128)(2,1)}, u32[]{:S(2)}) copy-start(bf16[512,768]{1,0:T(8,128)(2,1)} %refs_5_.1) | copy-start | bytes 2359300
  66.2 5.3 %collective-permute-start.21 = (bf16[4,12288]{1,0:T(4,128)(2,1)S(1)}, bf16[4,12288]{1,0:T(4,128)(2,1)S(1)}, u32[]{:S(2)}, u32[]{:S(2)}) collective-permute-start(bf16[4,12288]{1,0:T(4,128)(2,1)S(1)} %get-tuple-element.32), channel_id=1, source_target_pairs={{0,2},{1,3},{2,0},{3,1},{4,6},{5,7},{6,4},{7,5},{8,10},{9,11},{10,... | collective-permute-start | bytes 294920 | tf_op jit(solution)/shard_map/ppermute | solution.py:183
  67.8 5.3 %collective-permute-start.23 = (bf16[4,12288]{1,0:T(4,128)(2,1)S(1)}, bf16[4,12288]{1,0:T(4,128)(2,1)S(1)}, u32[]{:S(2)}, u32[]{:S(2)}) collective-permute-start(bf16[4,12288]{1,0:T(4,128)(2,1)S(1)} %get-tuple-element.34), channel_id=1, source_target_pairs={{0,2},{1,3},{2,0},{3,1},{4,6},{5,7},{6,4},{7,5},{8,10},{9,11},{10,... | collective-permute-start | bytes 294920 | tf_op jit(solution)/shard_map/ppermute | solution.py:183
  68.3 5.3 %collective-permute-start.25 = (bf16[4,12288]{1,0:T(4,128)(2,1)S(1)}, bf16[4,12288]{1,0:T(4,128)(2,1)S(1)}, u32[]{:S(2)}, u32[]{:S(2)}) collective-permute-start(bf16[4,12288]{1,0:T(4,128)(2,1)S(1)} %get-tuple-element.36), channel_id=1, source_target_pairs={{0,2},{1,3},{2,0},{3,1},{4,6},{5,7},{6,4},{7,5},{8,10},{9,11},{10,... | collective-permute-start | bytes 294920 | tf_op jit(solution)/shard_map/ppermute | solution.py:183
  69.8 6.5 %collective-permute-start.27 = (bf16[4,12288]{1,0:T(4,128)(2,1)S(1)}, bf16[4,12288]{1,0:T(4,128)(2,1)S(1)}, u32[]{:S(2)}, u32[]{:S(2)}) collective-permute-start(bf16[4,12288]{1,0:T(4,128)(2,1)S(1)} %get-tuple-element.38), channel_id=1, source_target_pairs={{0,2},{1,3},{2,0},{3,1},{4,6},{5,7},{6,4},{7,5},{8,10},{9,11},{10,... | collective-permute-start | bytes 294920 | tf_op jit(solution)/shard_map/ppermute | solution.py:183
  71.6 6.6 %collective-permute-start.22 = (bf16[4,12288]{1,0:T(4,128)(2,1)S(1)}, bf16[4,12288]{1,0:T(4,128)(2,1)S(1)}, u32[]{:S(2)}, u32[]{:S(2)}) collective-permute-start(bf16[4,12288]{1,0:T(4,128)(2,1)S(1)} %add_convert_fusion.3), channel_id=1, source_target_pairs={{0,12},{1,13},{2,14},{3,15},{4,8},{5,9},{6,10},{7,11},{8,4},{9,5},... | collective-permute-start | bytes 294920 | tf_op jit(solution)/shard_map/ppermute | solution.py:180
  73.1 7.1 %collective-permute-start.24 = (bf16[4,12288]{1,0:T(4,128)(2,1)S(1)}, bf16[4,12288]{1,0:T(4,128)(2,1)S(1)}, u32[]{:S(2)}, u32[]{:S(2)}) collective-permute-start(bf16[4,12288]{1,0:T(4,128)(2,1)S(1)} %add_convert_fusion.2), channel_id=1, source_target_pairs={{0,8},{1,9},{2,10},{3,11},{4,12},{5,13},{6,14},{7,15},{8,0},{9,1},... | collective-permute-start | bytes 294920 | tf_op jit(solution)/shard_map/ppermute | solution.py:180
  73.7 6.5 %collective-permute-start.26 = (bf16[4,12288]{1,0:T(4,128)(2,1)S(1)}, bf16[4,12288]{1,0:T(4,128)(2,1)S(1)}, u32[]{:S(2)}, u32[]{:S(2)}) collective-permute-start(bf16[4,12288]{1,0:T(4,128)(2,1)S(1)} %add_convert_fusion.1), channel_id=1, source_target_pairs={{0,4},{1,5},{2,6},{3,7},{4,0},{5,1},{6,2},{7,3},{8,12},{9,13},{10,... | collective-permute-start | bytes 294920 | tf_op jit(solution)/shard_map/ppermute | solution.py:180
  (7 other events, 5.4 us)

commit v4 on v3

v4 whole, which is shorter than its diff:
```python
import functools

import jax
import jax.numpy as jnp
from jax import lax
from jax.experimental import pallas as pl
from jax.experimental.pallas import tpu as pltpu
from jax.sharding import PartitionSpec as P

MIB = 1 << 20
VMEM = pl.BlockSpec(memory_space=pltpu.VMEM)
SMEM = pl.BlockSpec(memory_space=pltpu.SMEM)
HBM = pl.BlockSpec(memory_space=pl.ANY)
f32, bf16 = jnp.float32, jnp.bfloat16


def piece(width, most):
    size = 128
    while size * 2 <= most and width % (size * 2) == 0:
        size *= 2
    return size


def window(index, size):
    return pl.ds(pl.multiple_of(index * size, 128), size)


def call(body, outs, ins, limit, scratch=(), flops=0, moved=0):
    return pl.pallas_call(
        body,
        out_shape=outs,
        in_specs=ins,
        out_specs=[VMEM] * len(outs),
        scratch_shapes=list(scratch),
        compiler_params=pltpu.CompilerParams(vmem_limit_bytes=limit * MIB),
        cost_estimate=pl.CostEstimate(flops=flops, bytes_accessed=moved, transcendentals=0),
    )


def normal(hidden, gain, shift):
    wide = hidden.astype(f32)
    mean = jnp.mean(wide, axis=-1, keepdims=True)
    centred = wide - mean
    variance = jnp.mean(centred * centred, axis=-1, keepdims=True)
    return (centred * lax.rsqrt(variance + 1e-05) * gain + shift).astype(bf16)


def norm_body(groups, place, *refs):
    held, (gain, shift, out, keep, send) = refs[:groups], refs[groups:]
    rows = held[0].shape[0]
    for k in range(groups):
        out[k * rows : (k + 1) * rows, :] = normal(held[k][...], gain[...], shift[...])
    span = keep.shape[1]
    chip = place[0] // 2
    keep[...] = out[:, window(chip, span)]
    send[...] = out[:, window(chip ^ 1, span)]


def turn(x, groups, bit):
    rows = x.shape[0] // (2 * groups)
    at = [h * groups + (k ^ bit) for h in range(2) for k in range(groups)]
    return jnp.concatenate([x[i * rows : (i + 1) * rows] for i in at], axis=0)


def down_body(place, keep, got, own, mate, total, message):
    share = own.shape[0]
    core = place[0] % 2
    rows = jnp.concatenate([keep[...].astype(f32), got[...].astype(f32)], axis=0)
    low, high = rows[:, :share], rows[:, share:]
    mine = jnp.where(core == 0, low, high).astype(bf16)
    other = jnp.where(core == 0, high, low).astype(bf16)
    sums = jnp.dot(mine, own[...], preferred_element_type=f32) + jnp.dot(
        other, mate[...], preferred_element_type=f32
    )
    half = keep.shape[0]
    total[...] = sums
    message[:half, :] = sums[half:].astype(bf16)
    message[half:, :] = sums[:half].astype(bf16)


def merge_body(groups, bit, total, got, out, message):
    sums = total[...] + got[...].astype(f32)
    out[...] = sums
    message[...] = turn(sums, groups, bit).astype(bf16)


def up_body(place, total, got, bias, own, mate, near, far):
    hidden = jnp.maximum(total[...] + got[...].astype(f32) + bias[...], 0.0).astype(bf16)
    core = place[0] % 2
    mine = jnp.dot(hidden, own[...], preferred_element_type=f32)
    other = jnp.dot(hidden, mate[...], preferred_element_type=f32)
    low, high = jnp.where(core == 0, mine, other), jnp.where(core == 0, other, mine)
    both = jnp.concatenate([low, high], axis=1)
    half = near.shape[0]
    near[...] = both[:half].astype(bf16)
    far[...] = both[half:].astype(bf16)


def strip_body(groups, place, near, got, *outs):
    upper = (place[0] // 2) % 2
    mine, other = near[...].astype(f32), got[...].astype(f32)
    both = jnp.concatenate([jnp.where(upper == 0, mine, other), jnp.where(upper == 0, other, mine)], axis=1)
    rows = outs[0].shape[0]
    for k in range(groups):
        outs[k][...] = both[k * rows : (k + 1) * rows].astype(bf16)


def last_body(groups, place, *refs):
    sums, strips, (out, total) = refs[:groups], refs[groups : 2 * groups], refs[2 * groups :]
    whole = sums[0][...]
    for k in range(1, groups):
        whole = whole + sums[k][...].astype(f32)
    total[...] = whole
    for k in range(groups):
        total[:, window((place[0] // 4) ^ k, strips[k].shape[1])] += strips[k][...].astype(f32)
    out[...] = total[...].astype(bf16)


def fetch(srcs, dsts, sems, step, axis):
    copies = []
    for i in range(srcs[0].shape[axis] // step):
        at = (pl.ds(i * step, step), slice(None)) if axis == 0 else (slice(None), pl.ds(i * step, step))
        pair = [pltpu.make_async_copy(s.at[at], d.at[at], sems.at[n, i]) for n, (s, d) in enumerate(zip(srcs, dsts))]
        for copy in pair:
            copy.start()
        copies.append(pair)
    return copies


def act_body(groups, step, normed, *refs):
    held, (gain, shift, w_own, w_mate, b_own, b_mate, mask, out, own, mate, whole, sems) = refs[:groups], refs[groups:]
    copies = fetch((w_own, w_mate), (own, mate), sems, step, 0)
    some, rows = normed.shape[0], held[0].shape[0]
    whole[:some, :] = normed[...]
    for k in range(groups):
        whole[some + k * rows : some + (k + 1) * rows, :] = normal(held[k][...], gain[...], shift[...])
    total = jnp.zeros(out.shape, f32)
    for i, pair in enumerate(copies):
        for copy in pair:
            copy.wait()
        both = jnp.concatenate([own[i * step : (i + 1) * step, :], mate[i * step : (i + 1) * step, :]], axis=1)
        total = total + jnp.dot(whole[:, i * step : (i + 1) * step], both, preferred_element_type=f32)
    bias = jnp.concatenate([b_own[...], b_mate[...]], axis=1)
    out[...] = (jnp.maximum(total + bias, 0.0) * mask[...]).astype(bf16)


def part_body(groups, step, act, w_own, w_mate, *refs):
    outs, (own, mate, sems) = refs[: 2 * groups], refs[2 * groups :]
    rows = outs[0].shape[0]
    copies = fetch((w_own, w_mate), (own, mate), sems, step, 1)
    for i, pair in enumerate(copies):
        for copy in pair:
            copy.wait()
        cols = slice(i * step, (i + 1) * step)
        both = jnp.concatenate([own[:, cols], mate[:, cols]], axis=0)
        part = jnp.dot(act[...], both, preferred_element_type=f32)
        for q in range(2 * groups):
            outs[q][:, cols] = part[q * rows : (q + 1) * rows].astype(outs[q].dtype)


def activity(lists, counts, block_slot):
    groups, top = lists.shape
    nblocks = block_slot.shape[0]
    names = jnp.arange(nblocks, dtype=jnp.int32)
    live = (jnp.arange(top, dtype=jnp.int32)[None, :] < counts[:, None]).astype(jnp.int32)
    hits = (lists[:, :, None] == names[None, None, :]).astype(jnp.int32) * live[:, :, None]
    by_block = jnp.sum(hits, axis=1)
    placed = (block_slot[:, None] == names[None, :]).astype(jnp.int32)
    return jnp.sum(by_block[:, :, None] * placed[None, :, :], axis=1)


def shards(
    hidden,
    ln_gain,
    ln_shift,
    lists,
    counts,
    block_slot,
    w_in,
    b_in,
    w_out,
    low_in,
    low_bias,
    low_out,
):
    devices = lax.axis_size("blk")
    position = lax.axis_index("blk")
    row_dev, width = hidden.shape
    groups = lists.shape[0]
    share, rank = low_in.shape
    block = w_in.shape[1]
    assert devices == 4 * groups
    plane = position // 4
    place = jnp.reshape(position, (1,)).astype(jnp.int32)
    some, rows = groups * row_dev, 2 * groups * row_dev

    def across(x, k):
        return lax.ppermute(x, "blk", [(i, i ^ (4 * k)) for i in range(devices)])

    def beside(x):
        return lax.ppermute(x, "blk", [(i, i ^ 2) for i in range(devices)])

    def core(x):
        return lax.ppermute(x, "blk", [(i, i ^ 1) for i in range(devices)])

    def shape(*dims, dtype=bf16):
        return jax.ShapeDtypeStruct(dims, dtype)

    gain, shift, bias = ln_gain.reshape(1, width), ln_shift.reshape(1, width), b_in.reshape(1, block)
    span = 2 * share

    held = [hidden] + [across(hidden, k) for k in range(1, groups)]
    beyond = [beside(h) for h in held]

    mates, previous = [], None
    for w in (bias, low_in, w_in, w_out, low_out):
        if previous is not None:
            w, previous = lax.optimization_barrier((w, previous))
            mates.append(previous)
        previous = core(w)
    bias_mate, low_in_mate, w_in_mate, w_out_mate = mates
    low_out_mate = previous

    normed, keep, send = call(
        functools.partial(norm_body, groups),
        [shape(some, width)] + [shape(some, span)] * 2,
        [SMEM] + [VMEM] * (groups + 2),
        16,
    )(place, *held, gain, shift)
    total, message = call(
        down_body, [shape(rows, rank, dtype=f32), shape(rows, rank)], [SMEM] + [VMEM] * 4, 16
    )(place, keep, beside(send), low_in, low_in_mate)
    got = beside(message)
    bit = 1
    while bit < groups:
        total, message = call(
            functools.partial(merge_body, groups, bit),
            [shape(rows, rank, dtype=f32), shape(rows, rank)],
            [VMEM] * 2,
            16,
        )(total, got)
        got = across(message, bit)
        bit *= 2
    near, far = call(up_body, [shape(some, span)] * 2, [SMEM] + [VMEM] * 5, 16)(
        place, total, got, low_bias.reshape(1, rank), low_out, low_out_mate
    )
    strips = call(
        functools.partial(strip_body, groups), [shape(row_dev, 2 * span)] * groups, [SMEM] + [VMEM] * 2, 16
    )(place, near, beside(far))
    strips = [strips[0]] + [across(strips[k], k) for k in range(1, groups)]

    table = activity(lists, counts, block_slot)
    by = plane ^ jnp.arange(groups)
    at = position ^ jnp.arange(2)
    relate = (by[:, None] == jnp.arange(groups)[None, :])[:, None, :, None]
    choose = (at[:, None] == jnp.arange(devices)[None, :])[None, :, None, :]
    live = jnp.sum(jnp.where(relate & choose, table[None, None], 0), axis=(2, 3)).astype(f32)
    mask = jnp.broadcast_to(live[None, :, None, :, None], (2, groups, row_dev, 2, block)).reshape(rows, 2 * block)

    step = piece(width, 2048)
    act = call(
        functools.partial(act_body, groups, step),
        [shape(rows, 2 * block)],
        [VMEM] * (groups + 3) + [HBM] * 2 + [VMEM] * 3,
        56,
        [pltpu.VMEM((width, block), bf16)] * 2
        + [pltpu.VMEM((rows, width), bf16), pltpu.SemaphoreType.DMA((2, width // step))],
    )(normed, *beyond, gain, shift, w_in, w_in_mate, bias, bias_mate, mask)[0]
    parts = call(
        functools.partial(part_body, groups, step),
        [shape(row_dev, width, dtype=f32)] * groups + [shape(row_dev, width)] * groups,
        [VMEM] + [HBM] * 2,
        56,
        [pltpu.VMEM((block, width), bf16)] * 2 + [pltpu.SemaphoreType.DMA((2, width // step))],
    )(act, w_out, w_out_mate)
    sums = []
    for k in range(groups - 1, -1, -1):
        here = parts[k] + beside(parts[groups + k]).astype(f32)
        sums.append(across(here.astype(bf16), k) if k else here)
    return call(
        functools.partial(last_body, groups),
        [shape(row_dev, width)],
        [SMEM] + [VMEM] * (2 * groups),
        16,
        [pltpu.VMEM((row_dev, width), f32)],
    )(place, *sums[::-1], *strips)[0]


def solution(mesh):
    return jax.shard_map(
        shards,
        mesh=mesh,
        in_specs=(
            P(("rep", "blk"), None),
            P(),
            P(),
            P("rep", None),
            P("rep"),
            P(),
            P(None, "blk"),
            P("blk"),
            P("blk", None),
            P("blk", None),
            P(),
            P(None, "blk"),
        ),
        out_specs=P(("rep", "blk"), None),
        check_vma=False,
    )
```

time: 81.5 us -> 83.6 us (1.026)
  waiting for transfers between devices: 25.7 us -> 29.8 us
  local copies, waits for them, and re-layouts: 9.23 us -> 5.38 us
  Pallas kernels: 10.5 us -> 12.7 us
  starting transfers between devices: 32.5 us -> 31.1 us
  other arithmetic: 2.93 us -> 4.11 us
    ppermute x5, waiting for transfers between devices: 0.01 us -> 8.72 us  [core(): return lax.ppermute(x, 'blk', [(i, i ^ 1) for i in range(devices)])]
    ppermute x12 -> x11, waiting for transfers between devices: 18.7 us -> 10.6 us  [across(): return lax.ppermute(x, 'blk', [(i, i ^ 4 * k) for i in range(devices)])]
    unnamed x24 -> x32, local copies, waits for them, and re-layouts: 9.16 us -> 5.3 us
    ppermute x11, waiting for transfers between devices: 6.9 us -> 10.4 us  [beside(): return lax.ppermute(x, 'blk', [(i, i ^ 2) for i in range(devices)])]
    ppermute x11, starting transfers between devices: 13.6 us -> 11.4 us  [beside(): return lax.ppermute(x, 'blk', [(i, i ^ 2) for i in range(devices)])]
    pallas_call x1, Pallas kernels: 3.84 us -> 5 us  [shards(): call(functools.partial(part_body, groups, step), [shape(row_dev, width, d...]
    convert_element_type x4 -> x3, other arithmetic: 0.92 us -> 2.04 us  [shards(): sums.append(across(here.astype(bf16), k) if k else here)]
    pallas_call x5 -> x8, Pallas kernels: 6.68 us -> 7.68 us  [the longest x1 5.29 us: shards(): call(functools.partial(act_body, groups, step), [shape(rows, 2 * block)],...]
  transfers between devices with their start and end apart: 28 -> 27, of which waited for: 14 -> 14; matrix products, arithmetic and copies ran while one was open for 4% -> 7% of each run, Pallas kernels for 8% -> 14%
where the time goes in v4:
time: 83.6 us; the launch traced here: 83.2 us
  starting transfers between devices  31.1 us (37%)
  waiting for transfers between devices  29.8 us (36%)
  Pallas kernels  12.7 us (15%)
  local copies, waits for them, and re-layouts  5.38 us (6%)
  other arithmetic  4.11 us (5%)
    ppermute x11, starting transfers between devices, across(): return lax.ppermute(x, 'blk', [(i, i ^ 4 * k) for i in range(devices)])  18.3 us
    ppermute x11, starting transfers between devices, beside(): return lax.ppermute(x, 'blk', [(i, i ^ 2) for i in range(devices)])  11.4 us
    ppermute x11, waiting for transfers between devices, across(): return lax.ppermute(x, 'blk', [(i, i ^ 4 * k) for i in range(devices)])  10.6 us
    ppermute x11, waiting for transfers between devices, beside(): return lax.ppermute(x, 'blk', [(i, i ^ 2) for i in range(devices)])  10.4 us
    ppermute x5, waiting for transfers between devices, core(): return lax.ppermute(x, 'blk', [(i, i ^ 1) for i in range(devices)])  8.72 us
    unnamed x32, local copies, waits for them, and re-layouts  5.3 us
    pallas_call x1, Pallas kernels, shards(): call(functools.partial(act_body, groups, step), [shape(rows, 2 * block)],...  5.29 us
    pallas_call x1, Pallas kernels, shards(): call(functools.partial(part_body, groups, step), [shape(row_dev, width, d...  5 us
  transfers between devices with their start and end apart: 27, of which 14 were waited for; matrix products, arithmetic and copies ran while one was open for 7% of the time, Pallas kernels for 14%

profile of v4, /device:TPU:0, one launch (start us, length us, event | category | flops | bytes accessed | tf_op | source)
XLA Modules:
  0.0 83.2 jit_solution(17620886273727741824)
XLA Ops:
  0.5 1.0 %collective-permute-done.7.refs_9_ = f32[1,128]{1,0:T(1,128)S(1)} collective-permute-done((f32[1,128]{1,0:T(1,128)}, f32[1,128]{1,0:T(1,128)S(1)}, u32[]{:S(2)}, u32[]{:S(2)}) %collective-permute-start.7) | collective-permute-done | bytes 544 | tf_op jit(solution)/shard_map/ppermute | solution.py:204
  1.7 2.2 %collective-permute-done.8.mate = bf16[768,512]{1,0:T(8,128)(2,1)S(1)} collective-permute-done((bf16[768,512]{1,0:T(8,128)(2,1)}, bf16[768,512]{1,0:T(8,128)(2,1)S(1)}, u32[]{:S(2)}, u32[]{:S(2)}) %collective-permute-start.8) | collective-permute-done | bytes 786464 | tf_op jit(solution)/shard_map/ppermute | solution.py:204
  4.2 5.6 %collective-permute-done.9.refs_7_ = bf16[12288,128]{1,0:T(8,128)(2,1)S(1)} collective-permute-done((bf16[12288,128]{1,0:T(8,128)(2,1)}, bf16[12288,128]{1,0:T(8,128)(2,1)S(1)}, u32[]{:S(2)}, u32[]{:S(2)}) %collective-permute-start.9) | collective-permute-done | bytes 3145760 | tf_op jit(solution)/shard_map/ppermute | solution.py:204
  10.1 4.8 %collective-permute-start.2 = (bf16[4,12288]{1,0:T(4,128)(2,1)}, bf16[4,12288]{1,0:T(4,128)(2,1)S(1)}, u32[]{:S(2)}, u32[]{:S(2)}) collective-permute-start(bf16[4,12288]{1,0:T(4,128)(2,1)} %refs_0_.1), channel_id=1, source_target_pairs={{0,12},{1,13},{2,14},{3,15},{4,8},{5,9},{6,10},{7,11},{8,4},{9,5},... | collective-permute-start | bytes 294920 | tf_op jit(solution)/shard_map/ppermute | solution.py:198
  15.4 1.6 %collective-permute-start = (bf16[4,12288]{1,0:T(4,128)(2,1)}, bf16[4,12288]{1,0:T(4,128)(2,1)S(1)}, u32[]{:S(2)}, u32[]{:S(2)}) collective-permute-start(bf16[4,12288]{1,0:T(4,128)(2,1)} %refs_0_.1), channel_id=1, source_target_pairs={{0,4},{1,5},{2,6},{3,7},{4,0},{5,1},{6,2},{7,3},{8,12},{9,13},{10,... | collective-permute-start | bytes 294920 | tf_op jit(solution)/shard_map/ppermute | solution.py:198
  16.9 1.5 %collective-permute-start.3 = (bf16[4,12288]{1,0:T(4,128)(2,1)}, bf16[4,12288]{1,0:T(4,128)(2,1)S(1)}, u32[]{:S(2)}, u32[]{:S(2)}) collective-permute-start(bf16[4,12288]{1,0:T(4,128)(2,1)} %refs_0_.1), channel_id=1, source_target_pairs={{0,2},{1,3},{2,0},{3,1},{4,6},{5,7},{6,4},{7,5},{8,10},{9,11},{10,... | collective-permute-start | bytes 294920 | tf_op jit(solution)/shard_map/ppermute | solution.py:201
  21.0 2.9 %collective-permute-done.1.refs_2_ = bf16[4,12288]{1,0:T(4,128)(2,1)S(1)} collective-permute-done((bf16[4,12288]{1,0:T(4,128)(2,1)}, bf16[4,12288]{1,0:T(4,128)(2,1)S(1)}, u32[]{:S(2)}, u32[]{:S(2)}) %collective-permute-start.1) | collective-permute-done | bytes 98336 | tf_op jit(solution)/shard_map/ppermute | solution.py:198
  25.4 0.9 %copy-done.5 = bf16[4,12288]{1,0:T(4,128)(2,1)S(1)} copy-done((bf16[4,12288]{1,0:T(4,128)(2,1)S(1)}, bf16[4,12288]{1,0:T(4,128)(2,1)}, u32[]{:S(2)}) %copy-start.5) | copy-done | bytes 98328
  26.3 0.9 %shard_map.118 = (bf16[16,12288]{1,0:T(8,128)(2,1)S(1)}, bf16[16,1536]{1,0:T(8,128)(2,1)S(1)}, bf16[16,1536]{1,0:T(8,128)(2,1)S(1)}) custom-call(s32[1]{0:T(128)} %bitcast.place, bf16[4,12288]{1,0:T(4,128)(2,1)S(1)} %copy-done.5, bf16[4,12288]{1,0:T(4,128)(2,1)S(1)} %collective-permute-done.refs_1_, bf16[4,12288]{1,0:T(4,128)(2,1)S(1)} %collective-permute-done.1.refs_2_, ...), custom_call_target="tpu_custom_call" | custom-call | tf_op jit(solution)/shard_map/pallas_call | solution.py:224
  28.0 1.5 %collective-permute-start.18 = (bf16[16,1536]{1,0:T(8,128)(2,1)S(1)}, bf16[16,1536]{1,0:T(8,128)(2,1)S(1)}, u32[]{:S(2)}, u32[]{:S(2)}) collective-permute-start(bf16[16,1536]{1,0:T(8,128)(2,1)S(1)} %get-tuple-element.52), channel_id=1, source_target_pairs={{0,2},{1,3},{2,0},{3,1},{4,6},{5,7},{6,4},{7,5},{8,10},{9,11},{10,... | collective-permute-start | bytes 147464 | tf_op jit(solution)/shard_map/ppermute | solution.py:201
  30.0 1.5 %collective-permute-start.5 = (bf16[4,12288]{1,0:T(4,128)(2,1)S(1)}, bf16[4,12288]{1,0:T(4,128)(2,1)S(1)}, u32[]{:S(2)}, u32[]{:S(2)}) collective-permute-start(bf16[4,12288]{1,0:T(4,128)(2,1)S(1)} %collective-permute-done.1.refs_2_), channel_id=1, source_target_pairs={{0,2},{1,3},{2,0},{3,1},{4,6},{5,7},{6,4},{7,5},{8,10},{9,11},{10,... | collective-permute-start | bytes 294920 | tf_op jit(solution)/shard_map/ppermute | solution.py:201
  33.0 2.2 %collective-permute-done.6.refs_3_ = bf16[4,12288]{1,0:T(4,128)(2,1)S(1)} collective-permute-done((bf16[4,12288]{1,0:T(4,128)(2,1)S(1)}, bf16[4,12288]{1,0:T(4,128)(2,1)S(1)}, u32[]{:S(2)}, u32[]{:S(2)}) %collective-permute-start.6) | collective-permute-done | bytes 98336 | tf_op jit(solution)/shard_map/ppermute | solution.py:201
  35.2 1.9 %collective-permute-done.5.refs_2_ = bf16[4,12288]{1,0:T(4,128)(2,1)S(1)} collective-permute-done((bf16[4,12288]{1,0:T(4,128)(2,1)S(1)}, bf16[4,12288]{1,0:T(4,128)(2,1)S(1)}, u32[]{:S(2)}, u32[]{:S(2)}) %collective-permute-start.5) | collective-permute-done | bytes 98336 | tf_op jit(solution)/shard_map/ppermute | solution.py:201
  37.1 1.1 %collective-permute-done.4.refs_1_ = bf16[4,12288]{1,0:T(4,128)(2,1)S(1)} collective-permute-done((bf16[4,12288]{1,0:T(4,128)(2,1)S(1)}, bf16[4,12288]{1,0:T(4,128)(2,1)S(1)}, u32[]{:S(2)}, u32[]{:S(2)}) %collective-permute-start.4) | collective-permute-done | bytes 98336 | tf_op jit(solution)/shard_map/ppermute | solution.py:201
  38.8 5.3 %shard_map.119.act = bf16[32,256]{1,0:T(8,128)(2,1)} custom-call(bf16[16,12288]{1,0:T(8,128)(2,1)} %copy-done.2, bf16[4,12288]{1,0:T(4,128)(2,1)} %copy-done.10, bf16[4,12288]{1,0:T(4,128)(2,1)} %copy-done.13, bf16[4,12288]{1,0:T(4,128)(2,1)} %copy-done.12, bf16[4,12288]{1,0:T(4,128)(2,1)} %copy-done.11, f32[1,12288]{1,0:T(1,128)} %bitcast.10, ...), custom_call_target="tpu_custom_call" | custom-call | tf_op jit(solution)/shard_map/pallas_call | solution.py:261
  44.1 5.0 %shard_map.120 = (f32[4,12288]{1,0:T(4,128)}, f32[4,12288]{1,0:T(4,128)}, f32[4,12288]{1,0:T(4,128)}, f32[4,12288]{1,0:T(4,128)}, bf16[4,12288]{1,0:T(4,128)(2,1...) custom-call(bf16[32,256]{1,0:T(8,128)(2,1)} %shard_map.119.act, ...), custom_call_target="tpu_custom_call" | custom-call | tf_op jit(solution)/shard_map/pallas_call | solution.py:269
  50.4 1.2 %collective-permute-start.19 = (bf16[32,512]{1,0:T(8,128)(2,1)S(1)}, bf16[32,512]{1,0:T(8,128)(2,1)S(1)}, u32[]{:S(2)}, u32[]{:S(2)}) collective-permute-start(bf16[32,512]{1,0:T(8,128)(2,1)S(1)} %get-tuple-element.55), channel_id=1, source_target_pairs={{0,2},{1,3},{2,0},{3,1},{4,6},{5,7},{6,4},{7,5},{8,10},{9,11},{10,... | collective-permute-start | bytes 98312 | tf_op jit(solution)/shard_map/ppermute | solution.py:201
  51.6 2.8 %collective-permute-done.19.got = bf16[32,512]{1,0:T(8,128)(2,1)S(1)} collective-permute-done((bf16[32,512]{1,0:T(8,128)(2,1)S(1)}, bf16[32,512]{1,0:T(8,128)(2,1)S(1)}, u32[]{:S(2)}, u32[]{:S(2)}) %collective-permute-start.19) | collective-permute-done | bytes 32800 | tf_op jit(solution)/shard_map/ppermute | solution.py:201
  55.0 3.4 %collective-permute-done.20.got = bf16[32,512]{1,0:T(8,128)(2,1)S(1)} collective-permute-done((bf16[32,512]{1,0:T(8,128)(2,1)S(1)}, bf16[32,512]{1,0:T(8,128)(2,1)S(1)}, u32[]{:S(2)}, u32[]{:S(2)}) %collective-permute-start.20) | collective-permute-done | bytes 32800 | tf_op jit(solution)/shard_map/ppermute | solution.py:198
  58.4 1.9 %collective-permute-start.21 = (bf16[32,512]{1,0:T(8,128)(2,1)S(1)}, bf16[32,512]{1,0:T(8,128)(2,1)S(1)}, u32[]{:S(2)}, u32[]{:S(2)}) collective-permute-start(bf16[32,512]{1,0:T(8,128)(2,1)S(1)} %get-tuple-element.59), channel_id=1, source_target_pairs={{0,8},{1,9},{2,10},{3,11},{4,12},{5,13},{6,14},{7,15},{8,0},{9,1},... | collective-permute-start | bytes 98312 | tf_op jit(solution)/shard_map/ppermute | solution.py:198
  61.0 1.4 %collective-permute-start.14 = (bf16[4,12288]{1,0:T(4,128)(2,1)}, bf16[4,12288]{1,0:T(4,128)(2,1)S(1)}, u32[]{:S(2)}, u32[]{:S(2)}) collective-permute-start(bf16[4,12288]{1,0:T(4,128)(2,1)} %get-tuple-element.48), channel_id=1, source_target_pairs={{0,2},{1,3},{2,0},{3,1},{4,6},{5,7},{6,4},{7,5},{8,10},{9,11},{10,... | collective-permute-start | bytes 294920 | tf_op jit(solution)/shard_map/ppermute | solution.py:201
  63.0 1.0 %add_convert_fusion.2 = bf16[4,12288]{1,0:T(4,128)(2,1)S(1)} fusion(f32[4,12288]{1,0:T(4,128)} %get-tuple-element.45, bf16[4,12288]{1,0:T(4,128)(2,1)S(1)} %collective-permute-done.12), kind=kLoop, calls=%fused_computation.2 | loop fusion | flops 147456 | bytes 393216 | tf_op jit(solution)/shard_map/convert_element_type | solution.py:279
  64.0 2.2 %collective-permute-done.14 = bf16[4,12288]{1,0:T(4,128)(2,1)S(1)} collective-permute-done((bf16[4,12288]{1,0:T(4,128)(2,1)}, bf16[4,12288]{1,0:T(4,128)(2,1)S(1)}, u32[]{:S(2)}, u32[]{:S(2)}) %collective-permute-start.14) | collective-permute-done | bytes 98336 | tf_op jit(solution)/shard_map/ppermute | solution.py:201
  66.2 1.7 %collective-permute-start.13 = (bf16[4,12288]{1,0:T(4,128)(2,1)S(1)}, bf16[4,12288]{1,0:T(4,128)(2,1)S(1)}, u32[]{:S(2)}, u32[]{:S(2)}) collective-permute-start(bf16[4,12288]{1,0:T(4,128)(2,1)S(1)} %add_convert_fusion.2), channel_id=1, source_target_pairs={{0,4},{1,5},{2,6},{3,7},{4,0},{5,1},{6,2},{7,3},{8,12},{9,13},{10,... | collective-permute-start | bytes 294920 | tf_op jit(solution)/shard_map/ppermute | solution.py:198
  67.9 1.0 %add_convert_fusion.1 = bf16[4,12288]{1,0:T(4,128)(2,1)S(1)} fusion(f32[4,12288]{1,0:T(4,128)} %get-tuple-element.47, bf16[4,12288]{1,0:T(4,128)(2,1)S(1)} %collective-permute-done.14), kind=kLoop, calls=%fused_computation.1 | loop fusion | flops 147456 | bytes 393216 | tf_op jit(solution)/shard_map/convert_element_type | solution.py:279
  69.4 1.0 %collective-permute-start.23 = (bf16[16,1536]{1,0:T(8,128)(2,1)S(1)}, bf16[16,1536]{1,0:T(8,128)(2,1)S(1)}, u32[]{:S(2)}, u32[]{:S(2)}) collective-permute-start(bf16[16,1536]{1,0:T(8,128)(2,1)S(1)} %get-tuple-element.62), channel_id=1, source_target_pairs={{0,2},{1,3},{2,0},{3,1},{4,6},{5,7},{6,4},{7,5},{8,10},{9,11},{10,... | collective-permute-start | bytes 147464 | tf_op jit(solution)/shard_map/ppermute | solution.py:201
  70.6 2.7 %collective-permute-start.17 = (bf16[4,12288]{1,0:T(4,128)(2,1)S(1)}, bf16[4,12288]{1,0:T(4,128)(2,1)S(1)}, u32[]{:S(2)}, u32[]{:S(2)}) collective-permute-start(bf16[4,12288]{1,0:T(4,128)(2,1)S(1)} %add_convert_fusion), channel_id=1, source_target_pairs={{0,12},{1,13},{2,14},{3,15},{4,8},{5,9},{6,10},{7,11},{8,4},{9,5},... | collective-permute-start | bytes 294920 | tf_op jit(solution)/shard_map/ppermute | solution.py:198
  73.6 1.8 %collective-permute-start.24 = (bf16[4,3072]{1,0:T(4,128)(2,1)S(1)}, bf16[4,3072]{1,0:T(4,128)(2,1)S(1)}, u32[]{:S(2)}, u32[]{:S(2)}) collective-permute-start(bf16[4,3072]{1,0:T(4,128)(2,1)S(1)} %get-tuple-element.64), channel_id=1, source_target_pairs={{0,4},{1,5},{2,6},{3,7},{4,0},{5,1},{6,2},{7,3},{8,12},{9,13},{10,... | collective-permute-start | bytes 73736 | tf_op jit(solution)/shard_map/ppermute | solution.py:198
  75.5 1.4 %collective-permute-start.25 = (bf16[4,3072]{1,0:T(4,128)(2,1)S(1)}, bf16[4,3072]{1,0:T(4,128)(2,1)S(1)}, u32[]{:S(2)}, u32[]{:S(2)}) collective-permute-start(bf16[4,3072]{1,0:T(4,128)(2,1)S(1)} %get-tuple-element.65), channel_id=1, source_target_pairs={{0,8},{1,9},{2,10},{3,11},{4,12},{5,13},{6,14},{7,15},{8,0},{9,1},... | collective-permute-start | bytes 73736 | tf_op jit(solution)/shard_map/ppermute | solution.py:198
  76.9 1.2 %collective-permute-start.26 = (bf16[4,3072]{1,0:T(4,128)(2,1)S(1)}, bf16[4,3072]{1,0:T(4,128)(2,1)S(1)}, u32[]{:S(2)}, u32[]{:S(2)}) collective-permute-start(bf16[4,3072]{1,0:T(4,128)(2,1)S(1)} %get-tuple-element.66), channel_id=1, source_target_pairs={{0,12},{1,13},{2,14},{3,15},{4,8},{5,9},{6,10},{7,11},{8,4},{9,5},... | collective-permute-start | bytes 73736 | tf_op jit(solution)/shard_map/ppermute | solution.py:198
  79.0 1.6 %collective-permute-done.25.refs_6_ = bf16[4,3072]{1,0:T(4,128)(2,1)S(1)} collective-permute-done((bf16[4,3072]{1,0:T(4,128)(2,1)S(1)}, bf16[4,3072]{1,0:T(4,128)(2,1)S(1)}, u32[]{:S(2)}, u32[]{:S(2)}) %collective-permute-start.25) | collective-permute-done | bytes 24608 | tf_op jit(solution)/shard_map/ppermute | solution.py:198
  80.6 1.9 %collective-permute-done.26.refs_7_ = bf16[4,3072]{1,0:T(4,128)(2,1)S(1)} collective-permute-done((bf16[4,3072]{1,0:T(4,128)(2,1)S(1)}, bf16[4,3072]{1,0:T(4,128)(2,1)S(1)}, u32[]{:S(2)}, u32[]{:S(2)}) %collective-permute-start.26) | collective-permute-done | bytes 24608 | tf_op jit(solution)/shard_map/ppermute | solution.py:198
  (78 shorter events, 15.1 us)
Async XLA Ops:
  0.0 1.4 %collective-permute-start.7 = (f32[1,128]{1,0:T(1,128)}, f32[1,128]{1,0:T(1,128)S(1)}, u32[]{:S(2)}, u32[]{:S(2)}) collective-permute-start(f32[1,128]{1,0:T(1,128)} %bitcast.17), channel_id=1, source_target_pairs={{0,1},{1,0},{2,3},{3,2},{4,5},{5,4},{6,7},{7,6},{8,9},{9,8},{10,11... | collective-permute-start | bytes 1544 | tf_op jit(solution)/shard_map/ppermute | solution.py:204
  1.4 36.7 %copy-start.14 = (f32[1,128]{1,0:T(1,128)}, f32[1,128]{1,0:T(1,128)S(1)}, u32[]{:S(2)}) copy-start(f32[1,128]{1,0:T(1,128)S(1)} %collective-permute-done.7.refs_9_) | copy-start | bytes 1540
  1.4 2.5 %collective-permute-start.8 = (bf16[768,512]{1,0:T(8,128)(2,1)}, bf16[768,512]{1,0:T(8,128)(2,1)S(1)}, u32[]{:S(2)}, u32[]{:S(2)}) collective-permute-start(bf16[768,512]{1,0:T(8,128)(2,1)} %own.2), channel_id=1, source_target_pairs={{0,1},{1,0},{2,3},{3,2},{4,5},{5,4},{6,7},{7,6},{8,9},{9,8},{10,11... | collective-permute-start | bytes 2359304 | tf_op jit(solution)/shard_map/ppermute | solution.py:204
  3.9 5.9 %collective-permute-start.9 = (bf16[12288,128]{1,0:T(8,128)(2,1)}, bf16[12288,128]{1,0:T(8,128)(2,1)S(1)}, u32[]{:S(2)}, u32[]{:S(2)}) collective-permute-start(bf16[12288,128]{1,0:T(8,128)(2,1)} %refs_6_.1), channel_id=1, source_target_pairs={{0,1},{1,0},{2,3},{3,2},{4,5},{5,4},{6,7},{7,6},{8,9},{9,8},{10,11... | collective-permute-start | bytes 9437192 | tf_op jit(solution)/shard_map/ppermute | solution.py:204
  9.8 34.3 %collective-permute-start.10 = (bf16[128,12288]{1,0:T(8,128)(2,1)}, bf16[128,12288]{1,0:T(8,128)(2,1)}, u32[]{:S(2)}, u32[]{:S(2)}) collective-permute-start(bf16[128,12288]{1,0:T(8,128)(2,1)} %w_own.1), channel_id=1, source_target_pairs={{0,1},{1,0},{2,3},{3,2},{4,5},{5,4},{6,7},{7,6},{8,9},{9,8},{10,11... | collective-permute-start | bytes 9437192 | tf_op jit(solution)/shard_map/ppermute | solution.py:204
  10.1 10.9 %collective-permute-start.2 = (bf16[4,12288]{1,0:T(4,128)(2,1)}, bf16[4,12288]{1,0:T(4,128)(2,1)S(1)}, u32[]{:S(2)}, u32[]{:S(2)}) collective-permute-start(bf16[4,12288]{1,0:T(4,128)(2,1)} %refs_0_.1), channel_id=1, source_target_pairs={{0,12},{1,13},{2,14},{3,15},{4,8},{5,9},{6,10},{7,11},{8,4},{9,5},... | collective-permute-start | bytes 294920 | tf_op jit(solution)/shard_map/ppermute | solution.py:198
  14.9 8.9 %collective-permute-start.1 = (bf16[4,12288]{1,0:T(4,128)(2,1)}, bf16[4,12288]{1,0:T(4,128)(2,1)S(1)}, u32[]{:S(2)}, u32[]{:S(2)}) collective-permute-start(bf16[4,12288]{1,0:T(4,128)(2,1)} %refs_0_.1), channel_id=1, source_target_pairs={{0,8},{1,9},{2,10},{3,11},{4,12},{5,13},{6,14},{7,15},{8,0},{9,1},... | collective-permute-start | bytes 294920 | tf_op jit(solution)/shard_map/ppermute | solution.py:198
  15.4 8.5 %collective-permute-start = (bf16[4,12288]{1,0:T(4,128)(2,1)}, bf16[4,12288]{1,0:T(4,128)(2,1)S(1)}, u32[]{:S(2)}, u32[]{:S(2)}) collective-permute-start(bf16[4,12288]{1,0:T(4,128)(2,1)} %refs_0_.1), channel_id=1, source_target_pairs={{0,4},{1,5},{2,6},{3,7},{4,0},{5,1},{6,2},{7,3},{8,12},{9,13},{10,... | collective-permute-start | bytes 294920 | tf_op jit(solution)/shard_map/ppermute | solution.py:198
  16.9 14.6 %collective-permute-start.3 = (bf16[4,12288]{1,0:T(4,128)(2,1)}, bf16[4,12288]{1,0:T(4,128)(2,1)S(1)}, u32[]{:S(2)}, u32[]{:S(2)}) collective-permute-start(bf16[4,12288]{1,0:T(4,128)(2,1)} %refs_0_.1), channel_id=1, source_target_pairs={{0,2},{1,3},{2,0},{3,1},{4,6},{5,7},{6,4},{7,5},{8,10},{9,11},{10,... | collective-permute-start | bytes 294920 | tf_op jit(solution)/shard_map/ppermute | solution.py:201
  28.0 22.1 %collective-permute-start.18 = (bf16[16,1536]{1,0:T(8,128)(2,1)S(1)}, bf16[16,1536]{1,0:T(8,128)(2,1)S(1)}, u32[]{:S(2)}, u32[]{:S(2)}) collective-permute-start(bf16[16,1536]{1,0:T(8,128)(2,1)S(1)} %get-tuple-element.52), channel_id=1, source_target_pairs={{0,2},{1,3},{2,0},{3,1},{4,6},{5,7},{6,4},{7,5},{8,10},{9,11},{10,... | collective-permute-start | bytes 147464 | tf_op jit(solution)/shard_map/ppermute | solution.py:201
  29.5 5.7 %collective-permute-start.6 = (bf16[4,12288]{1,0:T(4,128)(2,1)S(1)}, bf16[4,12288]{1,0:T(4,128)(2,1)S(1)}, u32[]{:S(2)}, u32[]{:S(2)}) collective-permute-start(bf16[4,12288]{1,0:T(4,128)(2,1)S(1)} %collective-permute-done.2.refs_3_), channel_id=1, source_target_pairs={{0,2},{1,3},{2,0},{3,1},{4,6},{5,7},{6,4},{7,5},{8,10},{9,11},{10,... | collective-permute-start | bytes 294920 | tf_op jit(solution)/shard_map/ppermute | solution.py:201
  30.0 7.1 %collective-permute-start.5 = (bf16[4,12288]{1,0:T(4,128)(2,1)S(1)}, bf16[4,12288]{1,0:T(4,128)(2,1)S(1)}, u32[]{:S(2)}, u32[]{:S(2)}) collective-permute-start(bf16[4,12288]{1,0:T(4,128)(2,1)S(1)} %collective-permute-done.1.refs_2_), channel_id=1, source_target_pairs={{0,2},{1,3},{2,0},{3,1},{4,6},{5,7},{6,4},{7,5},{8,10},{9,11},{10,... | collective-permute-start | bytes 294920 | tf_op jit(solution)/shard_map/ppermute | solution.py:201
  31.5 6.6 %collective-permute-start.4 = (bf16[4,12288]{1,0:T(4,128)(2,1)S(1)}, bf16[4,12288]{1,0:T(4,128)(2,1)S(1)}, u32[]{:S(2)}, u32[]{:S(2)}) collective-permute-start(bf16[4,12288]{1,0:T(4,128)(2,1)S(1)} %collective-permute-done.refs_1_), channel_id=1, source_target_pairs={{0,2},{1,3},{2,0},{3,1},{4,6},{5,7},{6,4},{7,5},{8,10},{9,11},{10,... | collective-permute-start | bytes 294920 | tf_op jit(solution)/shard_map/ppermute | solution.py:201
  44.1 18.9 %copy-start.1 = (bf16[512,768]{1,0:T(8,128)(2,1)S(1)}, bf16[512,768]{1,0:T(8,128)(2,1)}, u32[]{:S(2)}) copy-start(bf16[512,768]{1,0:T(8,128)(2,1)} %own.3) | copy-start | bytes 2359300
  44.1 24.9 %copy-start.6 = (f32[512]{0:T(512)S(1)}, f32[512]{0:T(512)}, u32[]{:S(2)}) copy-start(f32[512]{0:T(512)} %param.22) | copy-start | bytes 6148
  49.1 21.4 %copy-start.8 = (f32[4,12288]{1,0:T(4,128)S(1)}, f32[4,12288]{1,0:T(4,128)}, u32[]{:S(2)}) copy-start(f32[4,12288]{1,0:T(4,128)} %get-tuple-element.49) | copy-start | bytes 589828
  49.1 29.0 %copy-start.9 = (f32[4,12288]{1,0:T(4,128)S(1)}, f32[4,12288]{1,0:T(4,128)}, u32[]{:S(2)}) copy-start(f32[4,12288]{1,0:T(4,128)} %get-tuple-element.43) | copy-start | bytes 589828
  49.2 13.9 %collective-permute-start.12 = (bf16[4,12288]{1,0:T(4,128)(2,1)}, bf16[4,12288]{1,0:T(4,128)(2,1)S(1)}, u32[]{:S(2)}, u32[]{:S(2)}) collective-permute-start(bf16[4,12288]{1,0:T(4,128)(2,1)} %get-tuple-element.46), channel_id=1, source_target_pairs={{0,2},{1,3},{2,0},{3,1},{4,6},{5,7},{6,4},{7,5},{8,10},{9,11},{10,... | collective-permute-start | bytes 294920 | tf_op jit(solution)/shard_map/ppermute | solution.py:201
  50.4 4.0 %collective-permute-start.19 = (bf16[32,512]{1,0:T(8,128)(2,1)S(1)}, bf16[32,512]{1,0:T(8,128)(2,1)S(1)}, u32[]{:S(2)}, u32[]{:S(2)}) collective-permute-start(bf16[32,512]{1,0:T(8,128)(2,1)S(1)} %get-tuple-element.55), channel_id=1, source_target_pairs={{0,2},{1,3},{2,0},{3,1},{4,6},{5,7},{6,4},{7,5},{8,10},{9,11},{10,... | collective-permute-start | bytes 98312 | tf_op jit(solution)/shard_map/ppermute | solution.py:201
  54.4 4.0 %collective-permute-start.20 = (bf16[32,512]{1,0:T(8,128)(2,1)S(1)}, bf16[32,512]{1,0:T(8,128)(2,1)S(1)}, u32[]{:S(2)}, u32[]{:S(2)}) collective-permute-start(bf16[32,512]{1,0:T(8,128)(2,1)S(1)} %get-tuple-element.57), channel_id=1, source_target_pairs={{0,4},{1,5},{2,6},{3,7},{4,0},{5,1},{6,2},{7,3},{8,12},{9,13},{10,... | collective-permute-start | bytes 98312 | tf_op jit(solution)/shard_map/ppermute | solution.py:198
  58.4 10.5 %collective-permute-start.21 = (bf16[32,512]{1,0:T(8,128)(2,1)S(1)}, bf16[32,512]{1,0:T(8,128)(2,1)S(1)}, u32[]{:S(2)}, u32[]{:S(2)}) collective-permute-start(bf16[32,512]{1,0:T(8,128)(2,1)S(1)} %get-tuple-element.59), channel_id=1, source_target_pairs={{0,8},{1,9},{2,10},{3,11},{4,12},{5,13},{6,14},{7,15},{8,0},{9,1},... | collective-permute-start | bytes 98312 | tf_op jit(solution)/shard_map/ppermute | solution.py:198
  60.3 15.1 %collective-permute-start.11 = (bf16[4,12288]{1,0:T(4,128)(2,1)}, bf16[4,12288]{1,0:T(4,128)(2,1)S(1)}, u32[]{:S(2)}, u32[]{:S(2)}) collective-permute-start(bf16[4,12288]{1,0:T(4,128)(2,1)} %get-tuple-element.44), channel_id=1, source_target_pairs={{0,2},{1,3},{2,0},{3,1},{4,6},{5,7},{6,4},{7,5},{8,10},{9,11},{10,... | collective-permute-start | bytes 294920 | tf_op jit(solution)/shard_map/ppermute | solution.py:201
  61.0 5.2 %collective-permute-start.14 = (bf16[4,12288]{1,0:T(4,128)(2,1)}, bf16[4,12288]{1,0:T(4,128)(2,1)S(1)}, u32[]{:S(2)}, u32[]{:S(2)}) collective-permute-start(bf16[4,12288]{1,0:T(4,128)(2,1)} %get-tuple-element.48), channel_id=1, source_target_pairs={{0,2},{1,3},{2,0},{3,1},{4,6},{5,7},{6,4},{7,5},{8,10},{9,11},{10,... | collective-permute-start | bytes 294920 | tf_op jit(solution)/shard_map/ppermute | solution.py:201
  62.4 8.1 %collective-permute-start.16 = (bf16[4,12288]{1,0:T(4,128)(2,1)}, bf16[4,12288]{1,0:T(4,128)(2,1)S(1)}, u32[]{:S(2)}, u32[]{:S(2)}) collective-permute-start(bf16[4,12288]{1,0:T(4,128)(2,1)} %get-tuple-element.50), channel_id=1, source_target_pairs={{0,2},{1,3},{2,0},{3,1},{4,6},{5,7},{6,4},{7,5},{8,10},{9,11},{10,... | collective-permute-start | bytes 294920 | tf_op jit(solution)/shard_map/ppermute | solution.py:201
  63.0 6.0 %collective-permute-start.22 = (bf16[512,768]{1,0:T(8,128)(2,1)S(1)}, bf16[512,768]{1,0:T(8,128)(2,1)S(1)}, u32[]{:S(2)}, u32[]{:S(2)}) collective-permute-start(bf16[512,768]{1,0:T(8,128)(2,1)S(1)} %copy-done.1), channel_id=1, source_target_pairs={{0,1},{1,0},{2,3},{3,2},{4,5},{5,4},{6,7},{7,6},{8,9},{9,8},{10,11... | collective-permute-start | bytes 2359304 | tf_op jit(solution)/shard_map/ppermute | solution.py:204
  66.2 10.7 %collective-permute-start.13 = (bf16[4,12288]{1,0:T(4,128)(2,1)S(1)}, bf16[4,12288]{1,0:T(4,128)(2,1)S(1)}, u32[]{:S(2)}, u32[]{:S(2)}) collective-permute-start(bf16[4,12288]{1,0:T(4,128)(2,1)S(1)} %add_convert_fusion.2), channel_id=1, source_target_pairs={{0,4},{1,5},{2,6},{3,7},{4,0},{5,1},{6,2},{7,3},{8,12},{9,13},{10,... | collective-permute-start | bytes 294920 | tf_op jit(solution)/shard_map/ppermute | solution.py:198
  68.9 10.1 %collective-permute-start.15 = (bf16[4,12288]{1,0:T(4,128)(2,1)S(1)}, bf16[4,12288]{1,0:T(4,128)(2,1)S(1)}, u32[]{:S(2)}, u32[]{:S(2)}) collective-permute-start(bf16[4,12288]{1,0:T(4,128)(2,1)S(1)} %add_convert_fusion.1), channel_id=1, source_target_pairs={{0,8},{1,9},{2,10},{3,11},{4,12},{5,13},{6,14},{7,15},{8,0},{9,1},... | collective-permute-start | bytes 294920 | tf_op jit(solution)/shard_map/ppermute | solution.py:198
  69.4 4.2 %collective-permute-start.23 = (bf16[16,1536]{1,0:T(8,128)(2,1)S(1)}, bf16[16,1536]{1,0:T(8,128)(2,1)S(1)}, u32[]{:S(2)}, u32[]{:S(2)}) collective-permute-start(bf16[16,1536]{1,0:T(8,128)(2,1)S(1)} %get-tuple-element.62), channel_id=1, source_target_pairs={{0,2},{1,3},{2,0},{3,1},{4,6},{5,7},{6,4},{7,5},{8,10},{9,11},{10,... | collective-permute-start | bytes 147464 | tf_op jit(solution)/shard_map/ppermute | solution.py:201
  70.6 8.4 %collective-permute-start.17 = (bf16[4,12288]{1,0:T(4,128)(2,1)S(1)}, bf16[4,12288]{1,0:T(4,128)(2,1)S(1)}, u32[]{:S(2)}, u32[]{:S(2)}) collective-permute-start(bf16[4,12288]{1,0:T(4,128)(2,1)S(1)} %add_convert_fusion), channel_id=1, source_target_pairs={{0,12},{1,13},{2,14},{3,15},{4,8},{5,9},{6,10},{7,11},{8,4},{9,5},... | collective-permute-start | bytes 294920 | tf_op jit(solution)/shard_map/ppermute | solution.py:198
  73.6 5.4 %collective-permute-start.24 = (bf16[4,3072]{1,0:T(4,128)(2,1)S(1)}, bf16[4,3072]{1,0:T(4,128)(2,1)S(1)}, u32[]{:S(2)}, u32[]{:S(2)}) collective-permute-start(bf16[4,3072]{1,0:T(4,128)(2,1)S(1)} %get-tuple-element.64), channel_id=1, source_target_pairs={{0,4},{1,5},{2,6},{3,7},{4,0},{5,1},{6,2},{7,3},{8,12},{9,13},{10,... | collective-permute-start | bytes 73736 | tf_op jit(solution)/shard_map/ppermute | solution.py:198
  75.5 5.1 %collective-permute-start.25 = (bf16[4,3072]{1,0:T(4,128)(2,1)S(1)}, bf16[4,3072]{1,0:T(4,128)(2,1)S(1)}, u32[]{:S(2)}, u32[]{:S(2)}) collective-permute-start(bf16[4,3072]{1,0:T(4,128)(2,1)S(1)} %get-tuple-element.65), channel_id=1, source_target_pairs={{0,8},{1,9},{2,10},{3,11},{4,12},{5,13},{6,14},{7,15},{8,0},{9,1},... | collective-permute-start | bytes 73736 | tf_op jit(solution)/shard_map/ppermute | solution.py:198
  76.9 5.6 %collective-permute-start.26 = (bf16[4,3072]{1,0:T(4,128)(2,1)S(1)}, bf16[4,3072]{1,0:T(4,128)(2,1)S(1)}, u32[]{:S(2)}, u32[]{:S(2)}) collective-permute-start(bf16[4,3072]{1,0:T(4,128)(2,1)S(1)} %get-tuple-element.66), channel_id=1, source_target_pairs={{0,12},{1,13},{2,14},{3,15},{4,8},{5,9},{6,10},{7,11},{8,4},{9,5},... | collective-permute-start | bytes 73736 | tf_op jit(solution)/shard_map/ppermute | solution.py:198
  (10 other events, 25.6 us)

commit v5 on v4

--- a/solution.py
+++ b/solution.py
@@ -25,7 +25,7 @@
     return pl.ds(pl.multiple_of(index * size, 128), size)
 
 
-def call(body, outs, ins, limit, scratch=(), flops=0, moved=0):
+def call(body, outs, ins, limit, scratch=(), moved=2 * MIB):
     return pl.pallas_call(
         body,
         out_shape=outs,
@@ -33,7 +33,7 @@
         out_specs=[VMEM] * len(outs),
         scratch_shapes=list(scratch),
         compiler_params=pltpu.CompilerParams(vmem_limit_bytes=limit * MIB),
-        cost_estimate=pl.CostEstimate(flops=flops, bytes_accessed=moved, transcendentals=0),
+        cost_estimate=pl.CostEstimate(flops=0, bytes_accessed=moved, transcendentals=0),
     )
 
 
@@ -45,15 +45,15 @@
     return (centred * lax.rsqrt(variance + 1e-05) * gain + shift).astype(bf16)
 
 
-def norm_body(groups, place, *refs):
-    held, (gain, shift, out, keep, send) = refs[:groups], refs[groups:]
+def norm_body(count, place, *refs):
+    held, (gain, shift, out, keep, send) = refs[:count], refs[count:]
     rows = held[0].shape[0]
-    for k in range(groups):
+    for k in range(count):
         out[k * rows : (k + 1) * rows, :] = normal(held[k][...], gain[...], shift[...])
-    span = keep.shape[1]
+    some, span = keep.shape
     chip = place[0] // 2
-    keep[...] = out[:, window(chip, span)]
-    send[...] = out[:, window(chip ^ 1, span)]
+    keep[...] = out[:some, window(chip, span)]
+    send[...] = out[:some, window(chip ^ 1, span)]
 
 
 def turn(x, groups, bit):
@@ -127,12 +127,12 @@
     return copies
 
 
-def act_body(groups, step, normed, *refs):
-    held, (gain, shift, w_own, w_mate, b_own, b_mate, mask, out, own, mate, whole, sems) = refs[:groups], refs[groups:]
+def act_body(count, step, normed, *refs):
+    held, (gain, shift, w_own, w_mate, b_own, b_mate, mask, out, own, mate, whole, sems) = refs[:count], refs[count:]
     copies = fetch((w_own, w_mate), (own, mate), sems, step, 0)
     some, rows = normed.shape[0], held[0].shape[0]
     whole[:some, :] = normed[...]
-    for k in range(groups):
+    for k in range(count):
         whole[some + k * rows : some + (k + 1) * rows, :] = normal(held[k][...], gain[...], shift[...])
     total = jnp.zeros(out.shape, f32)
     for i, pair in enumerate(copies):
@@ -210,28 +210,53 @@
     span = 2 * share
 
     held = [hidden] + [across(hidden, k) for k in range(1, groups)]
+    w_in_mate = core(w_in)
+    held[-1], low_in_sent, bias_sent = lax.optimization_barrier((held[-1], low_in, bias))
+    low_in_mate, bias_mate = core(low_in_sent), core(bias_sent)
     beyond = [beside(h) for h in held]
 
-    mates, previous = [], None
-    for w in (bias, low_in, w_in, w_out, low_out):
-        if previous is not None:
-            w, previous = lax.optimization_barrier((w, previous))
-            mates.append(previous)
-        previous = core(w)
-    bias_mate, low_in_mate, w_in_mate, w_out_mate = mates
-    low_out_mate = previous
-
+    soon = groups // 2
     normed, keep, send = call(
-        functools.partial(norm_body, groups),
-        [shape(some, width)] + [shape(some, span)] * 2,
-        [SMEM] + [VMEM] * (groups + 2),
+        functools.partial(norm_body, groups + soon),
+        [shape(some + soon * row_dev, width)] + [shape(some, span)] * 2,
+        [SMEM] + [VMEM] * (groups + soon + 2),
         16,
-    )(place, *held, gain, shift)
+    )(place, *held, *beyond[:soon], gain, shift)
+    send, w_in_mate, w_out_sent = lax.optimization_barrier((send, w_in_mate, w_out))
+    w_out_mate = core(w_out_sent)
     total, message = call(
         down_body, [shape(rows, rank, dtype=f32), shape(rows, rank)], [SMEM] + [VMEM] * 4, 16
     )(place, keep, beside(send), low_in, low_in_mate)
+    message, normed, low_out_sent = lax.optimization_barrier((message, normed, low_out))
+    low_out_mate = core(low_out_sent)
     got = beside(message)
-    bit = 1
+    table = activity(lists, counts, block_slot)
+    by = plane ^ jnp.arange(groups)
+    at = position ^ jnp.arange(2)
+    relate = (by[:, None] == jnp.arange(groups)[None, :])[:, None, :, None]
+    choose = (at[:, None] == jnp.arange(devices)[None, :])[None, :, None, :]
+    live = jnp.sum(jnp.where(relate & choose, table[None, None], 0), axis=(2, 3)).astype(f32)
+    mask = jnp.broadcast_to(live[None, :, None, :, None], (2, groups, row_dev, 2, block)).reshape(rows, 2 * block)
+
+    step = piece(width, 2048)
+    act = call(
+        functools.partial(act_body, groups - soon, step),
+        [shape(rows, 2 * block)],
+        [VMEM] * (groups - soon + 3) + [HBM] * 2 + [VMEM] * 3,
+        56,
+        [pltpu.VMEM((width, block), bf16)] * 2
+        + [pltpu.VMEM((rows, width), bf16), pltpu.SemaphoreType.DMA((2, width // step))],
+        16 * MIB,
+    )(normed, *beyond[soon:], gain, shift, w_in, w_in_mate, bias, bias_mate, mask)[0]
+    total, message = call(
+        functools.partial(merge_body, groups, 1),
+        [shape(rows, rank, dtype=f32), shape(rows, rank)],
+        [VMEM] * 2,
+        16,
+    )(total, got)
+    message, act = lax.optimization_barrier((message, act))
+    got = across(message, 1)
+    bit = 2
     while bit < groups:
         total, message = call(
             functools.partial(merge_body, groups, bit),
@@ -241,42 +266,31 @@
         )(total, got)
         got = across(message, bit)
         bit *= 2
-    near, far = call(up_body, [shape(some, span)] * 2, [SMEM] + [VMEM] * 5, 16)(
-        place, total, got, low_bias.reshape(1, rank), low_out, low_out_mate
-    )
-    strips = call(
-        functools.partial(strip_body, groups), [shape(row_dev, 2 * span)] * groups, [SMEM] + [VMEM] * 2, 16
-    )(place, near, beside(far))
-    strips = [strips[0]] + [across(strips[k], k) for k in range(1, groups)]
-
-    table = activity(lists, counts, block_slot)
-    by = plane ^ jnp.arange(groups)
-    at = position ^ jnp.arange(2)
-    relate = (by[:, None] == jnp.arange(groups)[None, :])[:, None, :, None]
-    choose = (at[:, None] == jnp.arange(devices)[None, :])[None, :, None, :]
-    live = jnp.sum(jnp.where(relate & choose, table[None, None], 0), axis=(2, 3)).astype(f32)
-    mask = jnp.broadcast_to(live[None, :, None, :, None], (2, groups, row_dev, 2, block)).reshape(rows, 2 * block)
-
-    step = piece(width, 2048)
-    act = call(
-        functools.partial(act_body, groups, step),
-        [shape(rows, 2 * block)],
-        [VMEM] * (groups + 3) + [HBM] * 2 + [VMEM] * 3,
-        56,
-        [pltpu.VMEM((width, block), bf16)] * 2
-        + [pltpu.VMEM((rows, width), bf16), pltpu.SemaphoreType.DMA((2, width // step))],
-    )(normed, *beyond, gain, shift, w_in, w_in_mate, bias, bias_mate, mask)[0]
     parts = call(
         functools.partial(part_body, groups, step),
         [shape(row_dev, width, dtype=f32)] * groups + [shape(row_dev, width)] * groups,
         [VMEM] + [HBM] * 2,
         56,
         [pltpu.VMEM((block, width), bf16)] * 2 + [pltpu.SemaphoreType.DMA((2, width // step))],
+        16 * MIB,
     )(act, w_out, w_out_mate)
+    come = [beside(parts[groups + k]) for k in range(1, groups)]
+
+    got, come[-1] = lax.optimization_barrier((got, come[-1]))
+    near, far = call(up_body, [shape(some, span)] * 2, [SMEM] + [VMEM] * 5, 16)(
+        place, total, got, low_bias.reshape(1, rank), low_out, low_out_mate
+    )
+    far, come[-2] = lax.optimization_barrier((beside(far), come[-2]))
+    strips = call(
+        functools.partial(strip_body, groups), [shape(row_dev, 2 * span)] * groups, [SMEM] + [VMEM] * 2, 16
+    )(place, near, far)
+    strips = [strips[0]] + [across(strips[k], k) for k in range(1, groups)]
+
+    far_part, come[-1] = lax.optimization_barrier((parts[groups], come[-1]))
     sums = []
-    for k in range(groups - 1, -1, -1):
-        here = parts[k] + beside(parts[groups + k]).astype(f32)
-        sums.append(across(here.astype(bf16), k) if k else here)
+    for k in range(groups - 1, 0, -1):
+        sums.append(across((parts[k] + come[k - 1].astype(f32)).astype(bf16), k))
+    sums.append(parts[0] + beside(far_part).astype(f32))
     return call(
         functools.partial(last_body, groups),
         [shape(row_dev, width)],

time: 83.6 us -> 76.7 us (0.917)
  waiting for transfers between devices: 29.8 us -> 19.2 us
  local copies, waits for them, and re-layouts: 5.38 us -> 8.19 us
  other arithmetic: 4.11 us -> 5.01 us
    ppermute x11, waiting for transfers between devices: 10.4 us -> 0.69 us  [beside(): return lax.ppermute(x, 'blk', [(i, i ^ 2) for i in range(devices)])]
    ppermute x5, waiting for transfers between devices: 8.72 us -> 1.85 us  [core(): return lax.ppermute(x, 'blk', [(i, i ^ 1) for i in range(devices)])]
    ppermute x11, waiting for transfers between devices: 10.6 us -> 16.7 us  [across(): return lax.ppermute(x, 'blk', [(i, i ^ 4 * k) for i in range(devices)])]
    unnamed x32 -> x26, local copies, waits for them, and re-layouts: 5.3 us -> 8.11 us
    ppermute x11, starting transfers between devices: 18.3 us -> 16.6 us  [across(): return lax.ppermute(x, 'blk', [(i, i ^ 4 * k) for i in range(devices)])]
    ppermute x11, starting transfers between devices: 11.4 us -> 13.1 us  [beside(): return lax.ppermute(x, 'blk', [(i, i ^ 2) for i in range(devices)])]
    convert_element_type x3, other arithmetic: 2.04 us -> 2.95 us  [shards(): sums.append(across((parts[k] + come[k - 1].astype(f32)).astype(bf16), k))]
    pallas_call x2 -> x3, Pallas kernels: 6.17 us -> 6.53 us  [the longest x1 5.28 us: shards(): call(functools.partial(act_body, groups - soon, step), [shape(rows, 2 * b...]
  transfers between devices with their start and end apart: 27 -> 27, of which waited for: 14 -> 9; matrix products, arithmetic and copies ran while one was open for 7% -> 8% of each run, Pallas kernels for 14% -> 10%
where the time goes in v5:
time: 76.7 us; the launch traced here: 76.2 us
  starting transfers between devices  30.6 us (40%)
  waiting for transfers between devices  19.2 us (25%)
  Pallas kernels  12.9 us (17%)
  local copies, waits for them, and re-layouts  8.19 us (11%)
  other arithmetic  5.01 us (7%)
    ppermute x11, waiting for transfers between devices, across(): return lax.ppermute(x, 'blk', [(i, i ^ 4 * k) for i in range(devices)])  16.7 us
    ppermute x11, starting transfers between devices, across(): return lax.ppermute(x, 'blk', [(i, i ^ 4 * k) for i in range(devices)])  16.6 us
    ppermute x11, starting transfers between devices, beside(): return lax.ppermute(x, 'blk', [(i, i ^ 2) for i in range(devices)])  13.1 us
    unnamed x26, local copies, waits for them, and re-layouts  8.11 us
    pallas_call x1, Pallas kernels, shards(): call(functools.partial(act_body, groups - soon, step), [shape(rows, 2 * b...  5.28 us
    pallas_call x1, Pallas kernels, shards(): call(functools.partial(part_body, groups, step), [shape(row_dev, width, d...  4.88 us
    convert_element_type x3, other arithmetic, shards(): sums.append(across((parts[k] + come[k - 1].astype(f32)).astype(bf16), k))  2.95 us
    ppermute x5, waiting for transfers between devices, core(): return lax.ppermute(x, 'blk', [(i, i ^ 1) for i in range(devices)])  1.85 us
  transfers between devices with their start and end apart: 27, of which 9 were waited for; matrix products, arithmetic and copies ran while one was open for 8% of the time, Pallas kernels for 10%

profile of v5, /device:TPU:0, one launch (start us, length us, event | category | flops | bytes accessed | tf_op | source)
XLA Modules:
  0.0 76.2 jit_solution(18403980533499045783)
XLA Ops:
  0.5 2.6 %collective-permute-start = (bf16[4,12288]{1,0:T(4,128)(2,1)}, bf16[4,12288]{1,0:T(4,128)(2,1)S(1)}, u32[]{:S(2)}, u32[]{:S(2)}) collective-permute-start(bf16[4,12288]{1,0:T(4,128)(2,1)} %refs_0_.1), channel_id=1, source_target_pairs={{0,4},{1,5},{2,6},{3,7},{4,0},{5,1},{6,2},{7,3},{8,12},{9,13},{10,... | collective-permute-start | bytes 294920 | tf_op jit(solution)/shard_map/ppermute | solution.py:198
  3.0 2.5 %collective-permute-start.2 = (bf16[4,12288]{1,0:T(4,128)(2,1)}, bf16[4,12288]{1,0:T(4,128)(2,1)S(1)}, u32[]{:S(2)}, u32[]{:S(2)}) collective-permute-start(bf16[4,12288]{1,0:T(4,128)(2,1)} %refs_0_.1), channel_id=1, source_target_pairs={{0,12},{1,13},{2,14},{3,15},{4,8},{5,9},{6,10},{7,11},{8,4},{9,5},... | collective-permute-start | bytes 294920 | tf_op jit(solution)/shard_map/ppermute | solution.py:198
  5.6 1.5 %collective-permute-start.3 = (bf16[4,12288]{1,0:T(4,128)(2,1)}, bf16[4,12288]{1,0:T(4,128)(2,1)S(1)}, u32[]{:S(2)}, u32[]{:S(2)}) collective-permute-start(bf16[4,12288]{1,0:T(4,128)(2,1)} %refs_0_.1), channel_id=1, source_target_pairs={{0,2},{1,3},{2,0},{3,1},{4,6},{5,7},{6,4},{7,5},{8,10},{9,11},{10,... | collective-permute-start | bytes 294920 | tf_op jit(solution)/shard_map/ppermute | solution.py:201
  7.1 1.2 %collective-permute-start.4 = (bf16[4,12288]{1,0:T(4,128)(2,1)S(1)}, bf16[4,12288]{1,0:T(4,128)(2,1)S(1)}, u32[]{:S(2)}, u32[]{:S(2)}) collective-permute-start(bf16[4,12288]{1,0:T(4,128)(2,1)S(1)} %collective-permute-done.refs_1_), channel_id=1, source_target_pairs={{0,2},{1,3},{2,0},{3,1},{4,6},{5,7},{6,4},{7,5},{8,10},{9,11},{10,... | collective-permute-start | bytes 294920 | tf_op jit(solution)/shard_map/ppermute | solution.py:201
  8.4 3.1 %collective-permute-done.2.refs_3_ = bf16[4,12288]{1,0:T(4,128)(2,1)S(1)} collective-permute-done((bf16[4,12288]{1,0:T(4,128)(2,1)}, bf16[4,12288]{1,0:T(4,128)(2,1)S(1)}, u32[]{:S(2)}, u32[]{:S(2)}) %collective-permute-start.2) | collective-permute-done | bytes 98336 | tf_op jit(solution)/shard_map/ppermute | solution.py:198
  11.5 3.9 %collective-permute-done.1.refs_2_ = bf16[4,12288]{1,0:T(4,128)(2,1)S(1)} collective-permute-done((bf16[4,12288]{1,0:T(4,128)(2,1)}, bf16[4,12288]{1,0:T(4,128)(2,1)S(1)}, u32[]{:S(2)}, u32[]{:S(2)}) %collective-permute-start.1) | collective-permute-done | bytes 98336 | tf_op jit(solution)/shard_map/ppermute | solution.py:198
  17.0 0.9 %copy-done.5 = bf16[4,12288]{1,0:T(4,128)(2,1)S(1)} copy-done((bf16[4,12288]{1,0:T(4,128)(2,1)S(1)}, bf16[4,12288]{1,0:T(4,128)(2,1)}, u32[]{:S(2)}) %copy-start.5) | copy-done | bytes 98328
  17.9 1.2 %shard_map.118 = (bf16[24,12288]{1,0:T(8,128)(2,1)S(1)}, bf16[16,1536]{1,0:T(8,128)(2,1)S(1)}, bf16[16,1536]{1,0:T(8,128)(2,1)S(1)}) custom-call(s32[1]{0:T(128)} %bitcast.place, bf16[4,12288]{1,0:T(4,128)(2,1)S(1)} %copy-done.5, bf16[4,12288]{1,0:T(4,128)(2,1)S(1)} %collective-permute-done.refs_1_, bf16[4,12288]{1,0:T(4,128)(2,1)S(1)} %collective-permute-done.1.refs_2_, ...), custom_call_target="tpu_custom_call" | custom-call | bytes 2097152 | tf_op jit(solution)/shard_map/pallas_call | solution.py:219
  19.1 0.8 %copy-done.2 = bf16[24,12288]{1,0:T(8,128)(2,1)} copy-done((bf16[24,12288]{1,0:T(8,128)(2,1)}, bf16[24,12288]{1,0:T(8,128)(2,1)S(1)}, u32[]{:S(2)}) %copy-start.2) | copy-done | bytes 589848
  22.9 1.6 %collective-permute-start.6 = (bf16[16,1536]{1,0:T(8,128)(2,1)S(1)}, bf16[16,1536]{1,0:T(8,128)(2,1)S(1)}, u32[]{:S(2)}, u32[]{:S(2)}) collective-permute-start(bf16[16,1536]{1,0:T(8,128)(2,1)S(1)} %get-tuple-element.48), channel_id=1, source_target_pairs={{0,2},{1,3},{2,0},{3,1},{4,6},{5,7},{6,4},{7,5},{8,10},{9,11},{10,... | collective-permute-start | bytes 147464 | tf_op jit(solution)/shard_map/ppermute | solution.py:201
  25.1 1.8 %collective-permute-done.7.mate = bf16[768,512]{1,0:T(8,128)(2,1)S(1)} collective-permute-done((bf16[768,512]{1,0:T(8,128)(2,1)}, bf16[768,512]{1,0:T(8,128)(2,1)S(1)}, u32[]{:S(2)}, u32[]{:S(2)}) %collective-permute-start.7) | collective-permute-done | bytes 786464 | tf_op jit(solution)/shard_map/ppermute | solution.py:204
  26.9 1.5 %collective-permute-start.9 = (bf16[4,12288]{1,0:T(4,128)(2,1)S(1)}, bf16[4,12288]{1,0:T(4,128)(2,1)S(1)}, u32[]{:S(2)}, u32[]{:S(2)}) collective-permute-start(bf16[4,12288]{1,0:T(4,128)(2,1)S(1)} %collective-permute-done.1.refs_2_), channel_id=1, source_target_pairs={{0,2},{1,3},{2,0},{3,1},{4,6},{5,7},{6,4},{7,5},{8,10},{9,11},{10,... | collective-permute-start | bytes 294920 | tf_op jit(solution)/shard_map/ppermute | solution.py:201
  28.4 1.1 %copy-done = bf16[768,512]{1,0:T(8,128)(2,1)S(1)} copy-done((bf16[768,512]{1,0:T(8,128)(2,1)S(1)}, bf16[768,512]{1,0:T(8,128)(2,1)}, u32[]{:S(2)}) %copy-start) | copy-done | bytes 786456
  32.4 5.3 %shard_map.121.act = bf16[32,256]{1,0:T(8,128)(2,1)} custom-call(bf16[24,12288]{1,0:T(8,128)(2,1)} %copy-done.2, bf16[4,12288]{1,0:T(4,128)(2,1)} %copy-done.10, bf16[4,12288]{1,0:T(4,128)(2,1)} %copy-done.9, f32[1,12288]{1,0:T(1,128)} %bitcast.10, f32[1,12288]{1,0:T(1,128)} %bitcast.12, bf16[12288,128]{1,0:T(8,128)(2,1)} %refs_4_.1, ...), custom_call_target="tpu_custom_call" | custom-call | bytes 16777216 | tf_op jit(solution)/shard_map/pallas_call | solution.py:242
  37.8 1.6 %copy-done.7 = bf16[128,12288]{1,0:T(8,128)(2,1)} copy-done((bf16[128,12288]{1,0:T(8,128)(2,1)}, bf16[128,12288]{1,0:T(8,128)(2,1)S(1)}, u32[]{:S(2)}) %copy-start.7) | copy-done | bytes 3145752
  39.4 4.9 %shard_map.122 = (f32[4,12288]{1,0:T(4,128)}, f32[4,12288]{1,0:T(4,128)}, f32[4,12288]{1,0:T(4,128)}, f32[4,12288]{1,0:T(4,128)}, bf16[4,12288]{1,0:T(4,128)(2,1...) custom-call(bf16[32,256]{1,0:T(8,128)(2,1)} %shard_map.121.act, ...), custom_call_target="tpu_custom_call" | custom-call | bytes 16777216 | tf_op jit(solution)/shard_map/pallas_call | solution.py:269
  44.3 1.9 %collective-permute-start.15 = (bf16[4,12288]{1,0:T(4,128)(2,1)}, bf16[4,12288]{1,0:T(4,128)(2,1)S(1)}, u32[]{:S(2)}, u32[]{:S(2)}) collective-permute-start(bf16[4,12288]{1,0:T(4,128)(2,1)} %get-tuple-element.65), channel_id=1, source_target_pairs={{0,2},{1,3},{2,0},{3,1},{4,6},{5,7},{6,4},{7,5},{8,10},{9,11},{10,... | collective-permute-start | bytes 294920 | tf_op jit(solution)/shard_map/ppermute | solution.py:201
  46.4 3.9 %collective-permute-done.13.got = bf16[32,512]{1,0:T(8,128)(2,1)S(1)} collective-permute-done((bf16[32,512]{1,0:T(8,128)(2,1)S(1)}, bf16[32,512]{1,0:T(8,128)(2,1)S(1)}, u32[]{:S(2)}, u32[]{:S(2)}) %collective-permute-start.13) | collective-permute-done | bytes 32800 | tf_op jit(solution)/shard_map/ppermute | solution.py:198
  50.3 1.2 %collective-permute-start.14 = (bf16[32,512]{1,0:T(8,128)(2,1)S(1)}, bf16[32,512]{1,0:T(8,128)(2,1)S(1)}, u32[]{:S(2)}, u32[]{:S(2)}) collective-permute-start(bf16[32,512]{1,0:T(8,128)(2,1)S(1)} %get-tuple-element.64), channel_id=1, source_target_pairs={{0,8},{1,9},{2,10},{3,11},{4,12},{5,13},{6,14},{7,15},{8,0},{9,1},... | collective-permute-start | bytes 98312 | tf_op jit(solution)/shard_map/ppermute | solution.py:198
  51.6 1.9 %collective-permute-start.21 = (bf16[4,12288]{1,0:T(4,128)(2,1)}, bf16[4,12288]{1,0:T(4,128)(2,1)S(1)}, u32[]{:S(2)}, u32[]{:S(2)}) collective-permute-start(bf16[4,12288]{1,0:T(4,128)(2,1)} %get-tuple-element.75), channel_id=1, source_target_pairs={{0,2},{1,3},{2,0},{3,1},{4,6},{5,7},{6,4},{7,5},{8,10},{9,11},{10,... | collective-permute-start | bytes 294920 | tf_op jit(solution)/shard_map/ppermute | solution.py:201
  53.4 1.8 %collective-permute-done.14.got = bf16[32,512]{1,0:T(8,128)(2,1)S(1)} collective-permute-done((bf16[32,512]{1,0:T(8,128)(2,1)S(1)}, bf16[32,512]{1,0:T(8,128)(2,1)S(1)}, u32[]{:S(2)}, u32[]{:S(2)}) %collective-permute-start.14) | collective-permute-done | bytes 32800 | tf_op jit(solution)/shard_map/ppermute | solution.py:198
  55.3 1.9 %collective-permute-start.16 = (bf16[4,12288]{1,0:T(4,128)(2,1)}, bf16[4,12288]{1,0:T(4,128)(2,1)S(1)}, u32[]{:S(2)}, u32[]{:S(2)}) collective-permute-start(bf16[4,12288]{1,0:T(4,128)(2,1)} %get-tuple-element.67), channel_id=1, source_target_pairs={{0,2},{1,3},{2,0},{3,1},{4,6},{5,7},{6,4},{7,5},{8,10},{9,11},{10,... | collective-permute-start | bytes 294920 | tf_op jit(solution)/shard_map/ppermute | solution.py:201
  57.1 1.0 %add_convert_fusion.2 = bf16[4,12288]{1,0:T(4,128)(2,1)S(1)} fusion(f32[4,12288]{1,0:T(4,128)} %get-tuple-element.68, bf16[4,12288]{1,0:T(4,128)(2,1)S(1)} %collective-permute-done.17), kind=kLoop, calls=%fused_computation.2 | loop fusion | flops 147456 | bytes 393216 | tf_op jit(solution)/shard_map/convert_element_type | solution.py:292
  59.0 1.0 %add_convert_fusion = bf16[4,12288]{1,0:T(4,128)(2,1)S(1)} fusion(f32[4,12288]{1,0:T(4,128)} %get-tuple-element.77, bf16[4,12288]{1,0:T(4,128)(2,1)S(1)} %collective-permute-done.15), kind=kLoop, calls=%fused_computation | loop fusion | flops 147456 | bytes 393216 | tf_op jit(solution)/shard_map/convert_element_type | solution.py:292
  60.0 2.5 %collective-permute-start.23 = (bf16[4,12288]{1,0:T(4,128)(2,1)S(1)}, bf16[4,12288]{1,0:T(4,128)(2,1)S(1)}, u32[]{:S(2)}, u32[]{:S(2)}) collective-permute-start(bf16[4,12288]{1,0:T(4,128)(2,1)S(1)} %add_convert_fusion), channel_id=1, source_target_pairs={{0,12},{1,13},{2,14},{3,15},{4,8},{5,9},{6,10},{7,11},{8,4},{9,5},... | collective-permute-start | bytes 294920 | tf_op jit(solution)/shard_map/ppermute | solution.py:198
  63.0 1.9 %collective-permute-start.24 = (bf16[4,3072]{1,0:T(4,128)(2,1)S(1)}, bf16[4,3072]{1,0:T(4,128)(2,1)S(1)}, u32[]{:S(2)}, u32[]{:S(2)}) collective-permute-start(bf16[4,3072]{1,0:T(4,128)(2,1)S(1)} %get-tuple-element.82), channel_id=1, source_target_pairs={{0,4},{1,5},{2,6},{3,7},{4,0},{5,1},{6,2},{7,3},{8,12},{9,13},{10,... | collective-permute-start | bytes 73736 | tf_op jit(solution)/shard_map/ppermute | solution.py:198
  64.8 1.0 %add_convert_fusion.1 = bf16[4,12288]{1,0:T(4,128)(2,1)S(1)} fusion(f32[4,12288]{1,0:T(4,128)} %get-tuple-element.70, bf16[4,12288]{1,0:T(4,128)(2,1)S(1)} %collective-permute-done.21), kind=kLoop, calls=%fused_computation.1 | loop fusion | flops 147456 | bytes 393216 | tf_op jit(solution)/shard_map/convert_element_type | solution.py:292
  65.8 1.2 %collective-permute-start.22 = (bf16[4,12288]{1,0:T(4,128)(2,1)S(1)}, bf16[4,12288]{1,0:T(4,128)(2,1)S(1)}, u32[]{:S(2)}, u32[]{:S(2)}) collective-permute-start(bf16[4,12288]{1,0:T(4,128)(2,1)S(1)} %add_convert_fusion.1), channel_id=1, source_target_pairs={{0,8},{1,9},{2,10},{3,11},{4,12},{5,13},{6,14},{7,15},{8,0},{9,1},... | collective-permute-start | bytes 294920 | tf_op jit(solution)/shard_map/ppermute | solution.py:198
  67.0 2.7 %collective-permute-start.25 = (bf16[4,3072]{1,0:T(4,128)(2,1)S(1)}, bf16[4,3072]{1,0:T(4,128)(2,1)S(1)}, u32[]{:S(2)}, u32[]{:S(2)}) collective-permute-start(bf16[4,3072]{1,0:T(4,128)(2,1)S(1)} %get-tuple-element.83), channel_id=1, source_target_pairs={{0,8},{1,9},{2,10},{3,11},{4,12},{5,13},{6,14},{7,15},{8,0},{9,1},... | collective-permute-start | bytes 73736 | tf_op jit(solution)/shard_map/ppermute | solution.py:198
  69.8 1.6 %collective-permute-start.26 = (bf16[4,3072]{1,0:T(4,128)(2,1)S(1)}, bf16[4,3072]{1,0:T(4,128)(2,1)S(1)}, u32[]{:S(2)}, u32[]{:S(2)}) collective-permute-start(bf16[4,3072]{1,0:T(4,128)(2,1)S(1)} %get-tuple-element.84), channel_id=1, source_target_pairs={{0,12},{1,13},{2,14},{3,15},{4,8},{5,9},{6,10},{7,11},{8,4},{9,5},... | collective-permute-start | bytes 73736 | tf_op jit(solution)/shard_map/ppermute | solution.py:198
  71.5 1.1 %collective-permute-done.25.refs_6_ = bf16[4,3072]{1,0:T(4,128)(2,1)S(1)} collective-permute-done((bf16[4,3072]{1,0:T(4,128)(2,1)S(1)}, bf16[4,3072]{1,0:T(4,128)(2,1)S(1)}, u32[]{:S(2)}, u32[]{:S(2)}) %collective-permute-start.25) | collective-permute-done | bytes 24608 | tf_op jit(solution)/shard_map/ppermute | solution.py:198
  72.6 2.9 %collective-permute-done.26.refs_7_ = bf16[4,3072]{1,0:T(4,128)(2,1)S(1)} collective-permute-done((bf16[4,3072]{1,0:T(4,128)(2,1)S(1)}, bf16[4,3072]{1,0:T(4,128)(2,1)S(1)}, u32[]{:S(2)}, u32[]{:S(2)}) %collective-permute-start.26) | collective-permute-done | bytes 24608 | tf_op jit(solution)/shard_map/ppermute | solution.py:198
  (72 shorter events, 11.0 us)
Async XLA Ops:
  0.0 19.9 %collective-permute-start.5 = (bf16[12288,128]{1,0:T(8,128)(2,1)}, bf16[12288,128]{1,0:T(8,128)(2,1)}, u32[]{:S(2)}, u32[]{:S(2)}) collective-permute-start(bf16[12288,128]{1,0:T(8,128)(2,1)} %refs_4_.1), channel_id=1, source_target_pairs={{0,1},{1,0},{2,3},{3,2},{4,5},{5,4},{6,7},{7,6},{8,9},{9,8},{10,11... | collective-permute-start | bytes 9437192 | tf_op jit(solution)/shard_map/ppermute | solution.py:204
  0.5 6.7 %collective-permute-start = (bf16[4,12288]{1,0:T(4,128)(2,1)}, bf16[4,12288]{1,0:T(4,128)(2,1)S(1)}, u32[]{:S(2)}, u32[]{:S(2)}) collective-permute-start(bf16[4,12288]{1,0:T(4,128)(2,1)} %refs_0_.1), channel_id=1, source_target_pairs={{0,4},{1,5},{2,6},{3,7},{4,0},{5,1},{6,2},{7,3},{8,12},{9,13},{10,... | collective-permute-start | bytes 294920 | tf_op jit(solution)/shard_map/ppermute | solution.py:198
  3.0 8.5 %collective-permute-start.2 = (bf16[4,12288]{1,0:T(4,128)(2,1)}, bf16[4,12288]{1,0:T(4,128)(2,1)S(1)}, u32[]{:S(2)}, u32[]{:S(2)}) collective-permute-start(bf16[4,12288]{1,0:T(4,128)(2,1)} %refs_0_.1), channel_id=1, source_target_pairs={{0,12},{1,13},{2,14},{3,15},{4,8},{5,9},{6,10},{7,11},{8,4},{9,5},... | collective-permute-start | bytes 294920 | tf_op jit(solution)/shard_map/ppermute | solution.py:198
  5.5 9.9 %collective-permute-start.1 = (bf16[4,12288]{1,0:T(4,128)(2,1)}, bf16[4,12288]{1,0:T(4,128)(2,1)S(1)}, u32[]{:S(2)}, u32[]{:S(2)}) collective-permute-start(bf16[4,12288]{1,0:T(4,128)(2,1)} %refs_0_.1), channel_id=1, source_target_pairs={{0,8},{1,9},{2,10},{3,11},{4,12},{5,13},{6,14},{7,15},{8,0},{9,1},... | collective-permute-start | bytes 294920 | tf_op jit(solution)/shard_map/ppermute | solution.py:198
  5.6 9.7 %collective-permute-start.3 = (bf16[4,12288]{1,0:T(4,128)(2,1)}, bf16[4,12288]{1,0:T(4,128)(2,1)S(1)}, u32[]{:S(2)}, u32[]{:S(2)}) collective-permute-start(bf16[4,12288]{1,0:T(4,128)(2,1)} %refs_0_.1), channel_id=1, source_target_pairs={{0,2},{1,3},{2,0},{3,1},{4,6},{5,7},{6,4},{7,5},{8,10},{9,11},{10,... | collective-permute-start | bytes 294920 | tf_op jit(solution)/shard_map/ppermute | solution.py:201
  7.1 8.2 %collective-permute-start.4 = (bf16[4,12288]{1,0:T(4,128)(2,1)S(1)}, bf16[4,12288]{1,0:T(4,128)(2,1)S(1)}, u32[]{:S(2)}, u32[]{:S(2)}) collective-permute-start(bf16[4,12288]{1,0:T(4,128)(2,1)S(1)} %collective-permute-done.refs_1_), channel_id=1, source_target_pairs={{0,2},{1,3},{2,0},{3,1},{4,6},{5,7},{6,4},{7,5},{8,10},{9,11},{10,... | collective-permute-start | bytes 294920 | tf_op jit(solution)/shard_map/ppermute | solution.py:201
  19.9 17.8 %collective-permute-start.12 = (bf16[128,12288]{1,0:T(8,128)(2,1)}, bf16[128,12288]{1,0:T(8,128)(2,1)S(1)}, u32[]{:S(2)}, u32[]{:S(2)}) collective-permute-start(bf16[128,12288]{1,0:T(8,128)(2,1)} %w_own.1), channel_id=1, source_target_pairs={{0,1},{1,0},{2,3},{3,2},{4,5},{5,4},{6,7},{7,6},{8,9},{9,8},{10,11... | collective-permute-start | bytes 9437192 | tf_op jit(solution)/shard_map/ppermute | solution.py:204
  21.5 5.5 %collective-permute-start.7 = (bf16[768,512]{1,0:T(8,128)(2,1)}, bf16[768,512]{1,0:T(8,128)(2,1)S(1)}, u32[]{:S(2)}, u32[]{:S(2)}) collective-permute-start(bf16[768,512]{1,0:T(8,128)(2,1)} %own.2), channel_id=1, source_target_pairs={{0,1},{1,0},{2,3},{3,2},{4,5},{5,4},{6,7},{7,6},{8,9},{9,8},{10,11... | collective-permute-start | bytes 2359304 | tf_op jit(solution)/shard_map/ppermute | solution.py:204
  22.9 5.5 %collective-permute-start.6 = (bf16[16,1536]{1,0:T(8,128)(2,1)S(1)}, bf16[16,1536]{1,0:T(8,128)(2,1)S(1)}, u32[]{:S(2)}, u32[]{:S(2)}) collective-permute-start(bf16[16,1536]{1,0:T(8,128)(2,1)S(1)} %get-tuple-element.48), channel_id=1, source_target_pairs={{0,2},{1,3},{2,0},{3,1},{4,6},{5,7},{6,4},{7,5},{8,10},{9,11},{10,... | collective-permute-start | bytes 147464 | tf_op jit(solution)/shard_map/ppermute | solution.py:201
  24.5 7.2 %collective-permute-start.10 = (bf16[4,12288]{1,0:T(4,128)(2,1)S(1)}, bf16[4,12288]{1,0:T(4,128)(2,1)S(1)}, u32[]{:S(2)}, u32[]{:S(2)}) collective-permute-start(bf16[4,12288]{1,0:T(4,128)(2,1)S(1)} %collective-permute-done.2.refs_3_), channel_id=1, source_target_pairs={{0,2},{1,3},{2,0},{3,1},{4,6},{5,7},{6,4},{7,5},{8,10},{9,11},{10,... | collective-permute-start | bytes 294920 | tf_op jit(solution)/shard_map/ppermute | solution.py:201
  25.1 6.5 %collective-permute-start.11 = (f32[1,128]{1,0:T(1,128)}, f32[1,128]{1,0:T(1,128)S(1)}, u32[]{:S(2)}, u32[]{:S(2)}) collective-permute-start(f32[1,128]{1,0:T(1,128)} %bitcast.17), channel_id=1, source_target_pairs={{0,1},{1,0},{2,3},{3,2},{4,5},{5,4},{6,7},{7,6},{8,9},{9,8},{10,11... | collective-permute-start | bytes 1544 | tf_op jit(solution)/shard_map/ppermute | solution.py:204
  26.9 4.8 %collective-permute-start.9 = (bf16[4,12288]{1,0:T(4,128)(2,1)S(1)}, bf16[4,12288]{1,0:T(4,128)(2,1)S(1)}, u32[]{:S(2)}, u32[]{:S(2)}) collective-permute-start(bf16[4,12288]{1,0:T(4,128)(2,1)S(1)} %collective-permute-done.1.refs_2_), channel_id=1, source_target_pairs={{0,2},{1,3},{2,0},{3,1},{4,6},{5,7},{6,4},{7,5},{8,10},{9,11},{10,... | collective-permute-start | bytes 294920 | tf_op jit(solution)/shard_map/ppermute | solution.py:201
  28.4 1.1 %copy-start = (bf16[768,512]{1,0:T(8,128)(2,1)S(1)}, bf16[768,512]{1,0:T(8,128)(2,1)}, u32[]{:S(2)}) copy-start(bf16[768,512]{1,0:T(8,128)(2,1)} %own.2) | copy-start | bytes 2359300
  29.9 7.8 %collective-permute-start.8 = (bf16[32,512]{1,0:T(8,128)(2,1)S(1)}, bf16[32,512]{1,0:T(8,128)(2,1)S(1)}, u32[]{:S(2)}, u32[]{:S(2)}) collective-permute-start(bf16[32,512]{1,0:T(8,128)(2,1)S(1)} %get-tuple-element.53), channel_id=1, source_target_pairs={{0,2},{1,3},{2,0},{3,1},{4,6},{5,7},{6,4},{7,5},{8,10},{9,11},{10,... | collective-permute-start | bytes 98312 | tf_op jit(solution)/shard_map/ppermute | solution.py:201
  37.7 13.8 %copy-start.1 = (bf16[512,768]{1,0:T(8,128)(2,1)S(1)}, bf16[512,768]{1,0:T(8,128)(2,1)}, u32[]{:S(2)}) copy-start(bf16[512,768]{1,0:T(8,128)(2,1)} %own.3) | copy-start | bytes 2359300
  37.8 20.6 %copy-start.6 = (f32[512]{0:T(512)S(1)}, f32[512]{0:T(512)}, u32[]{:S(2)}) copy-start(f32[512]{0:T(512)} %param.22) | copy-start | bytes 6148
  37.8 1.6 %copy-start.7 = (bf16[128,12288]{1,0:T(8,128)(2,1)}, bf16[128,12288]{1,0:T(8,128)(2,1)S(1)}, u32[]{:S(2)}) copy-start(bf16[128,12288]{1,0:T(8,128)(2,1)S(1)} %collective-permute-done.12.w_mate) | copy-start | bytes 9437188
  44.3 27.1 %copy-start.8 = (f32[4,12288]{1,0:T(4,128)S(1)}, f32[4,12288]{1,0:T(4,128)}, u32[]{:S(2)}) copy-start(f32[4,12288]{1,0:T(4,128)} %get-tuple-element.60) | copy-start | bytes 589828
  44.3 10.9 %collective-permute-start.15 = (bf16[4,12288]{1,0:T(4,128)(2,1)}, bf16[4,12288]{1,0:T(4,128)(2,1)S(1)}, u32[]{:S(2)}, u32[]{:S(2)}) collective-permute-start(bf16[4,12288]{1,0:T(4,128)(2,1)} %get-tuple-element.65), channel_id=1, source_target_pairs={{0,2},{1,3},{2,0},{3,1},{4,6},{5,7},{6,4},{7,5},{8,10},{9,11},{10,... | collective-permute-start | bytes 294920 | tf_op jit(solution)/shard_map/ppermute | solution.py:201
  46.2 10.9 %collective-permute-start.17 = (bf16[4,12288]{1,0:T(4,128)(2,1)}, bf16[4,12288]{1,0:T(4,128)(2,1)S(1)}, u32[]{:S(2)}, u32[]{:S(2)}) collective-permute-start(bf16[4,12288]{1,0:T(4,128)(2,1)} %get-tuple-element.69), channel_id=1, source_target_pairs={{0,2},{1,3},{2,0},{3,1},{4,6},{5,7},{6,4},{7,5},{8,10},{9,11},{10,... | collective-permute-start | bytes 294920 | tf_op jit(solution)/shard_map/ppermute | solution.py:201
  46.4 3.9 %collective-permute-start.13 = (bf16[32,512]{1,0:T(8,128)(2,1)S(1)}, bf16[32,512]{1,0:T(8,128)(2,1)S(1)}, u32[]{:S(2)}, u32[]{:S(2)}) collective-permute-start(bf16[32,512]{1,0:T(8,128)(2,1)S(1)} %get-tuple-element.63), channel_id=1, source_target_pairs={{0,4},{1,5},{2,6},{3,7},{4,0},{5,1},{6,2},{7,3},{8,12},{9,13},{10,... | collective-permute-start | bytes 98312 | tf_op jit(solution)/shard_map/ppermute | solution.py:198
  50.3 4.9 %collective-permute-start.14 = (bf16[32,512]{1,0:T(8,128)(2,1)S(1)}, bf16[32,512]{1,0:T(8,128)(2,1)S(1)}, u32[]{:S(2)}, u32[]{:S(2)}) collective-permute-start(bf16[32,512]{1,0:T(8,128)(2,1)S(1)} %get-tuple-element.64), channel_id=1, source_target_pairs={{0,8},{1,9},{2,10},{3,11},{4,12},{5,13},{6,14},{7,15},{8,0},{9,1},... | collective-permute-start | bytes 98312 | tf_op jit(solution)/shard_map/ppermute | solution.py:198
  51.6 6.8 %collective-permute-start.19 = (bf16[512,768]{1,0:T(8,128)(2,1)S(1)}, bf16[512,768]{1,0:T(8,128)(2,1)S(1)}, u32[]{:S(2)}, u32[]{:S(2)}) collective-permute-start(bf16[512,768]{1,0:T(8,128)(2,1)S(1)} %copy-done.1), channel_id=1, source_target_pairs={{0,1},{1,0},{2,3},{3,2},{4,5},{5,4},{6,7},{7,6},{8,9},{9,8},{10,11... | collective-permute-start | bytes 2359304 | tf_op jit(solution)/shard_map/ppermute | solution.py:204
  51.6 10.9 %collective-permute-start.21 = (bf16[4,12288]{1,0:T(4,128)(2,1)}, bf16[4,12288]{1,0:T(4,128)(2,1)S(1)}, u32[]{:S(2)}, u32[]{:S(2)}) collective-permute-start(bf16[4,12288]{1,0:T(4,128)(2,1)} %get-tuple-element.75), channel_id=1, source_target_pairs={{0,2},{1,3},{2,0},{3,1},{4,6},{5,7},{6,4},{7,5},{8,10},{9,11},{10,... | collective-permute-start | bytes 294920 | tf_op jit(solution)/shard_map/ppermute | solution.py:201
  55.3 14.5 %collective-permute-start.16 = (bf16[4,12288]{1,0:T(4,128)(2,1)}, bf16[4,12288]{1,0:T(4,128)(2,1)S(1)}, u32[]{:S(2)}, u32[]{:S(2)}) collective-permute-start(bf16[4,12288]{1,0:T(4,128)(2,1)} %get-tuple-element.67), channel_id=1, source_target_pairs={{0,2},{1,3},{2,0},{3,1},{4,6},{5,7},{6,4},{7,5},{8,10},{9,11},{10,... | collective-permute-start | bytes 294920 | tf_op jit(solution)/shard_map/ppermute | solution.py:201
  58.1 17.3 %collective-permute-start.18 = (bf16[4,12288]{1,0:T(4,128)(2,1)S(1)}, bf16[4,12288]{1,0:T(4,128)(2,1)S(1)}, u32[]{:S(2)}, u32[]{:S(2)}) collective-permute-start(bf16[4,12288]{1,0:T(4,128)(2,1)S(1)} %add_convert_fusion.2), channel_id=1, source_target_pairs={{0,4},{1,5},{2,6},{3,7},{4,0},{5,1},{6,2},{7,3},{8,12},{9,13},{10,... | collective-permute-start | bytes 294920 | tf_op jit(solution)/shard_map/ppermute | solution.py:198
  58.8 4.2 %collective-permute-start.20 = (bf16[16,1536]{1,0:T(8,128)(2,1)S(1)}, bf16[16,1536]{1,0:T(8,128)(2,1)S(1)}, u32[]{:S(2)}, u32[]{:S(2)}) collective-permute-start(bf16[16,1536]{1,0:T(8,128)(2,1)S(1)} %get-tuple-element.74), channel_id=1, source_target_pairs={{0,2},{1,3},{2,0},{3,1},{4,6},{5,7},{6,4},{7,5},{8,10},{9,11},{10,... | collective-permute-start | bytes 147464 | tf_op jit(solution)/shard_map/ppermute | solution.py:201
  60.0 15.4 %collective-permute-start.23 = (bf16[4,12288]{1,0:T(4,128)(2,1)S(1)}, bf16[4,12288]{1,0:T(4,128)(2,1)S(1)}, u32[]{:S(2)}, u32[]{:S(2)}) collective-permute-start(bf16[4,12288]{1,0:T(4,128)(2,1)S(1)} %add_convert_fusion), channel_id=1, source_target_pairs={{0,12},{1,13},{2,14},{3,15},{4,8},{5,9},{6,10},{7,11},{8,4},{9,5},... | collective-permute-start | bytes 294920 | tf_op jit(solution)/shard_map/ppermute | solution.py:198
  63.0 4.1 %collective-permute-start.24 = (bf16[4,3072]{1,0:T(4,128)(2,1)S(1)}, bf16[4,3072]{1,0:T(4,128)(2,1)S(1)}, u32[]{:S(2)}, u32[]{:S(2)}) collective-permute-start(bf16[4,3072]{1,0:T(4,128)(2,1)S(1)} %get-tuple-element.82), channel_id=1, source_target_pairs={{0,4},{1,5},{2,6},{3,7},{4,0},{5,1},{6,2},{7,3},{8,12},{9,13},{10,... | collective-permute-start | bytes 73736 | tf_op jit(solution)/shard_map/ppermute | solution.py:198
  65.8 9.6 %collective-permute-start.22 = (bf16[4,12288]{1,0:T(4,128)(2,1)S(1)}, bf16[4,12288]{1,0:T(4,128)(2,1)S(1)}, u32[]{:S(2)}, u32[]{:S(2)}) collective-permute-start(bf16[4,12288]{1,0:T(4,128)(2,1)S(1)} %add_convert_fusion.1), channel_id=1, source_target_pairs={{0,8},{1,9},{2,10},{3,11},{4,12},{5,13},{6,14},{7,15},{8,0},{9,1},... | collective-permute-start | bytes 294920 | tf_op jit(solution)/shard_map/ppermute | solution.py:198
  67.0 5.5 %collective-permute-start.25 = (bf16[4,3072]{1,0:T(4,128)(2,1)S(1)}, bf16[4,3072]{1,0:T(4,128)(2,1)S(1)}, u32[]{:S(2)}, u32[]{:S(2)}) collective-permute-start(bf16[4,3072]{1,0:T(4,128)(2,1)S(1)} %get-tuple-element.83), channel_id=1, source_target_pairs={{0,8},{1,9},{2,10},{3,11},{4,12},{5,13},{6,14},{7,15},{8,0},{9,1},... | collective-permute-start | bytes 73736 | tf_op jit(solution)/shard_map/ppermute | solution.py:198
  69.8 5.6 %collective-permute-start.26 = (bf16[4,3072]{1,0:T(4,128)(2,1)S(1)}, bf16[4,3072]{1,0:T(4,128)(2,1)S(1)}, u32[]{:S(2)}, u32[]{:S(2)}) collective-permute-start(bf16[4,3072]{1,0:T(4,128)(2,1)S(1)} %get-tuple-element.84), channel_id=1, source_target_pairs={{0,12},{1,13},{2,14},{3,15},{4,8},{5,9},{6,10},{7,11},{8,4},{9,5},... | collective-permute-start | bytes 73736 | tf_op jit(solution)/shard_map/ppermute | solution.py:198
  (7 other events, 5.1 us)

commit v6 on v0

v6 whole, which is shorter than its diff:
```python
import functools

import jax
import jax.numpy as jnp
from jax import lax
from jax.experimental import pallas as pl
from jax.experimental.pallas import tpu as pltpu
from jax.sharding import PartitionSpec as P

MIB = 1 << 20
VMEM = pl.BlockSpec(memory_space=pltpu.VMEM)
HBM = pl.BlockSpec(memory_space=pl.ANY)
SMEM = pl.BlockSpec(memory_space=pltpu.SMEM)
f32, bf16 = jnp.float32, jnp.bfloat16


def piece(width, most):
    size = 128
    while size * 2 <= most and width % (size * 2) == 0:
        size *= 2
    return size


def window(index, size):
    return pl.ds(pl.multiple_of(index * size, 128), size)


def call(body, outs, ins, limit, scratch=(), moved=2 * MIB):
    return pl.pallas_call(
        body,
        out_shape=outs,
        in_specs=ins,
        out_specs=[VMEM] * len(outs),
        scratch_shapes=list(scratch),
        compiler_params=pltpu.CompilerParams(vmem_limit_bytes=limit * MIB),
        cost_estimate=pl.CostEstimate(flops=0, bytes_accessed=moved, transcendentals=0),
    )


def normal(hidden, gain, shift):
    wide = hidden.astype(f32)
    mean = jnp.mean(wide, axis=-1, keepdims=True)
    centred = wide - mean
    variance = jnp.mean(centred * centred, axis=-1, keepdims=True)
    return (centred * lax.rsqrt(variance + 1e-05) * gain + shift).astype(bf16)


def load_body(count, *refs):
    srcs, dsts, sems = refs[:count], refs[count : 2 * count], refs[2 * count]
    copies = [pltpu.make_async_copy(srcs[i], dsts[i], sems.at[i]) for i in range(count)]
    for copy in copies:
        copy.start()
    for copy in copies:
        copy.wait()


def norm_body(groups, place, *refs):
    held, (gain, shift, own, mate, out, total, message) = refs[: 2 * groups], refs[2 * groups :]
    rows = held[0].shape[0]
    for i in range(0, 2 * groups, 2):
        pair = jnp.concatenate([held[i][...], held[i + 1][...]], axis=0)
        out[i * rows : (i + 2) * rows, :] = normal(pair, gain[...], shift[...])
    share = own.shape[0]
    core = place[0] % 2
    columns = out[:, window(place[0] // 2, 2 * share)].astype(f32)
    low, high = columns[:, :share], columns[:, share:]
    mine = jnp.where(core == 0, low, high).astype(bf16)
    other = jnp.where(core == 0, high, low).astype(bf16)
    sums = jnp.dot(mine, own[...], preferred_element_type=f32) + jnp.dot(
        other, mate[...], preferred_element_type=f32
    )
    half = groups * rows
    total[...] = sums
    message[:half, :] = sums[half:].astype(bf16)
    message[half:, :] = sums[:half].astype(bf16)


def turn(x, groups, bit):
    rows = x.shape[0] // (2 * groups)
    at = [h * groups + (k ^ bit) for h in range(2) for k in range(groups)]
    return jnp.concatenate([x[i * rows : (i + 1) * rows] for i in at], axis=0)


def merge_body(groups, bit, total, got, out, message):
    sums = total[...] + got[...].astype(f32)
    out[...] = sums
    message[...] = turn(sums, groups, bit).astype(bf16)


def up_body(groups, place, total, got, bias, own, mate, part, *outs):
    hidden = jnp.maximum(total[...] + got[...].astype(f32) + bias[...], 0.0).astype(bf16)
    core = place[0] % 2
    mine = jnp.dot(hidden, own[...], preferred_element_type=f32)
    other = jnp.dot(hidden, mate[...], preferred_element_type=f32)
    both = jnp.concatenate([jnp.where(core == 0, mine, other), jnp.where(core == 0, other, mine)], axis=1)
    at = window(place[0] // 2, both.shape[1])
    rows = outs[0].shape[0]
    for q in range(2 * groups):
        some = slice(q * rows, (q + 1) * rows)
        outs[q][...] = part[some, :].astype(outs[q].dtype)
        outs[q][:, at] = (part[some, at] + both[some]).astype(outs[q].dtype)


def last_body(groups, *refs):
    sums, out = refs[:groups], refs[groups]
    total = sums[0][...]
    for k in range(1, groups):
        total = total + sums[k][...].astype(f32)
    out[...] = total.astype(bf16)


def act_body(step, normed, w_own, w_mate, b_own, b_mate, mask, out):
    total = jnp.zeros(out.shape, f32)
    for i in range(normed.shape[1] // step):
        at = slice(i * step, (i + 1) * step)
        both = jnp.concatenate([w_own[at, :], w_mate[at, :]], axis=1)
        total = total + jnp.dot(normed[:, at], both, preferred_element_type=f32)
    bias = jnp.concatenate([b_own[...], b_mate[...]], axis=1)
    out[...] = (jnp.maximum(total + bias, 0.0) * mask[...]).astype(bf16)


def part_body(step, act, w_own, w_mate, out):
    for i in range(out.shape[1] // step):
        at = slice(i * step, (i + 1) * step)
        both = jnp.concatenate([w_own[:, at], w_mate[:, at]], axis=0)
        out[:, at] = jnp.dot(act[...], both, preferred_element_type=f32)


def activity(lists, counts, block_slot):
    groups, top = lists.shape
    nblocks = block_slot.shape[0]
    names = jnp.arange(nblocks, dtype=jnp.int32)
    live = (jnp.arange(top, dtype=jnp.int32)[None, :] < counts[:, None]).astype(jnp.int32)
    hits = (lists[:, :, None] == names[None, None, :]).astype(jnp.int32) * live[:, :, None]
    by_block = jnp.sum(hits, axis=1)
    placed = (block_slot[:, None] == names[None, :]).astype(jnp.int32)
    return jnp.sum(by_block[:, :, None] * placed[None, :, :], axis=1)


def shards(
    hidden,
    ln_gain,
    ln_shift,
    lists,
    counts,
    block_slot,
    w_in,
    b_in,
    w_out,
    low_in,
    low_bias,
    low_out,
):
    devices = lax.axis_size("blk")
    position = lax.axis_index("blk")
    row_dev, width = hidden.shape
    groups = lists.shape[0]
    share, rank = low_in.shape
    block = w_in.shape[1]
    assert devices == 4 * groups
    plane = position // 4
    place = jnp.reshape(position, (1,)).astype(jnp.int32)
    some, rows = groups * row_dev, 2 * groups * row_dev

    def across(x, k):
        return lax.ppermute(x, "blk", [(i, i ^ (4 * k)) for i in range(devices)])

    def beside(x):
        return lax.ppermute(x, "blk", [(i, i ^ 2) for i in range(devices)])

    def core(x):
        return lax.ppermute(x, "blk", [(i, i ^ 1) for i in range(devices)])

    def shape(*dims, dtype=bf16):
        return jax.ShapeDtypeStruct(dims, dtype)

    gain, shift, bias = ln_gain.reshape(1, width), ln_shift.reshape(1, width), b_in.reshape(1, block)
    span = 2 * share

    table = activity(lists, counts, block_slot)
    by = plane ^ jnp.arange(groups)
    at = position ^ jnp.arange(2)
    relate = (by[:, None] == jnp.arange(groups)[None, :])[:, None, :, None]
    choose = (at[:, None] == jnp.arange(devices)[None, :])[None, :, None, :]
    live = jnp.sum(jnp.where(relate & choose, table[None, None], 0), axis=(2, 3)).astype(f32)
    mask = jnp.broadcast_to(live[None, :, None, :, None], (2, groups, row_dev, 2, block)).reshape(rows, 2 * block)

    held = [hidden] + [across(hidden, k) for k in range(1, groups)]
    w_in_mate, low_in_mate = core(w_in), core(low_in)
    held[1], low_in_mate, mask = lax.optimization_barrier((held[1], low_in_mate, mask))
    near = (hidden, gain, shift, low_in, w_in, w_out, low_out)
    *near, mask = lax.optimization_barrier((*near, mask))
    near = call(
        functools.partial(load_body, len(near)),
        [shape(*x.shape, dtype=x.dtype) for x in near],
        [HBM] * len(near),
        16,
        [pltpu.SemaphoreType.DMA((len(near),))],
        8 * MIB,
    )(*near)
    held[2], *near = lax.optimization_barrier((held[2], *near))
    hidden_near, gain, shift, low_in, w_in, w_out_near, low_out_near = near
    *_, w_in_mate, w_out_sent, low_out_sent, bias_sent = lax.optimization_barrier(
        (*held, w_in_mate, w_out, low_out, bias)
    )
    bias_mate, w_out_mate, low_out_mate = core(bias_sent), core(w_out_sent), core(low_out_sent)
    beyond = [beside(h) for h in held]
    held = [hidden_near] + held[1:] + beyond

    normed, total, message = call(
        functools.partial(norm_body, groups),
        [shape(rows, width), shape(rows, rank, dtype=f32), shape(rows, rank)],
        [SMEM] + [VMEM] * (2 * groups + 4),
        16,
        (),
        6 * MIB,
    )(place, *held, gain, shift, low_in, low_in_mate)
    got = beside(message)
    step = piece(width, 2048)
    act = call(
        functools.partial(act_body, step),
        [shape(rows, 2 * block)],
        [VMEM] * 6,
        16,
        (),
        6 * MIB,
    )(normed, w_in, w_in_mate, bias, bias_mate, mask)[0]
    bit = 1
    while bit < groups:
        total, message = call(
            functools.partial(merge_body, groups, bit),
            [shape(rows, rank, dtype=f32), shape(rows, rank)],
            [VMEM] * 2,
            16,
        )(total, got)
        if bit == 1:
            message, act = lax.optimization_barrier((message, act))
        got = across(message, bit)
        bit *= 2
    part = call(
        functools.partial(part_body, step),
        [shape(rows, width, dtype=f32)],
        [VMEM] * 3,
        16,
        (),
        6 * MIB,
    )(act, w_out_near, w_out_mate)[0]
    got, part = lax.optimization_barrier((got, part))
    parts = call(
        functools.partial(up_body, groups),
        [shape(row_dev, width, dtype=f32)] * groups + [shape(row_dev, width)] * groups,
        [SMEM] + [VMEM] * 6,
        16,
        (),
        6 * MIB,
    )(place, total, got, low_bias.reshape(1, rank), low_out_near, low_out_mate, part)

    sums = []
    for k in range(groups - 1, -1, -1):
        here = parts[k] + beside(parts[groups + k]).astype(f32)
        sums.append(across(here.astype(bf16), k) if k else here)
    return call(functools.partial(last_body, groups), [shape(row_dev, width)], [VMEM] * groups, 16)(*sums[::-1])[0]


def solution(mesh):
    return jax.shard_map(
        shards,
        mesh=mesh,
        in_specs=(
            P(("rep", "blk"), None),
            P(),
            P(),
            P("rep", None),
            P("rep"),
            P(),
            P(None, "blk"),
            P("blk"),
            P("blk", None),
            P("blk", None),
            P(),
            P(None, "blk"),
        ),
        out_specs=P(("rep", "blk"), None),
        check_vma=False,
    )
```

time: 234 us -> 64.8 us (0.28); the launches traced: 230 us -> 64.3 us
  waiting for transfers between devices: 156 us -> 18.9 us
  blocking collectives: 22.2 us -> 0 us
  starting transfers between devices: 9.56 us -> 27.2 us
  between operations: 14.2 us -> 0.16 us
  Pallas kernels: 0 us -> 8.38 us
  matrix products: 8.25 us -> 0 us
  other arithmetic: 9.27 us -> 2.24 us
  local copies, waits for them, and re-layouts: 10.5 us -> 7.51 us
    unnamed x3 -> x0, waiting for transfers between devices: 86 us -> none
    all_gather x1 -> x0, waiting for transfers between devices: 37.8 us -> none  [shards(): every = lax.all_gather(normed, 'blk', axis=0, tiled=True)]
    all_to_all x2 -> x0, waiting for transfers between devices: 32 us -> none  [the longest x1 32 us: shards(): lax.all_to_all(result, 'blk', split_axis=0, concat_axis=0, tiled=True)]
    ppermute x0 -> x22, starting transfers between devices: none -> 27.2 us  [the longest x8 15.5 us: across(): return lax.ppermute(x, 'blk', [(i, i ^ 4 * k) for i in range(devices)])]
    all_gather x1 -> x0, blocking collectives: 22.2 us -> none  [shards(): lax.all_gather(low_h, 'blk', axis=0, tiled=True)]
    ppermute x0 -> x22, waiting for transfers between devices: none -> 18.9 us  [the longest x9 9.67 us: beside(): return lax.ppermute(x, 'blk', [(i, i ^ 2) for i in range(devices)])]
    all_to_all x2 -> x0, starting transfers between devices: 9.52 us -> none  [the longest x1 6.01 us: shards(): lax.all_to_all(result, 'blk', split_axis=0, concat_axis=0, tiled=True)]
    pallas_call x0 -> x8, Pallas kernels: none -> 8.38 us  [the longest x1 2.45 us: shards(): call(functools.partial(load_body, len(near)), [shape(*x.shape, dtype=x.dt...]
  transfers between devices with their start and end apart: 4 -> 22, of which waited for: 3 -> 12; matrix products, arithmetic and copies ran while one was open for 4% -> 5% of each run, Pallas kernels for 0% -> 11%
where the time goes in v6:
time: 64.8 us; the launch traced here: 64.3 us
  starting transfers between devices  27.2 us (42%)
  waiting for transfers between devices  18.9 us (29%)
  Pallas kernels  8.38 us (13%)
  local copies, waits for them, and re-layouts  7.51 us (12%)
  other arithmetic  2.24 us (3%)
    ppermute x8, starting transfers between devices, across(): return lax.ppermute(x, 'blk', [(i, i ^ 4 * k) for i in range(devices)])  15.5 us
    ppermute x9, starting transfers between devices, beside(): return lax.ppermute(x, 'blk', [(i, i ^ 2) for i in range(devices)])  10.6 us
    ppermute x9, waiting for transfers between devices, beside(): return lax.ppermute(x, 'blk', [(i, i ^ 2) for i in range(devices)])  9.67 us
    ppermute x8, waiting for transfers between devices, across(): return lax.ppermute(x, 'blk', [(i, i ^ 4 * k) for i in range(devices)])  9.2 us
    unnamed x20, local copies, waits for them, and re-layouts  7.43 us
    pallas_call x1, Pallas kernels, shards(): call(functools.partial(load_body, len(near)), [shape(*x.shape, dtype=x.dt...  2.45 us
    pallas_call x1, Pallas kernels, shards(): call(functools.partial(norm_body, groups), [shape(rows, width), shape(row...  2.38 us
  transfers between devices with their start and end apart: 22, of which 12 were waited for; matrix products, arithmetic and copies ran while one was open for 5% of the time, Pallas kernels for 11%

profile of v6, /device:TPU:0, one launch (start us, length us, event | category | flops | bytes accessed | tf_op | source)
XLA Modules:
  0.0 64.3 jit_solution(3045338420943654212)
XLA Ops:
  0.5 3.6 %collective-permute-start = (bf16[4,12288]{1,0:T(4,128)(2,1)}, bf16[4,12288]{1,0:T(4,128)(2,1)S(1)}, u32[]{:S(2)}, u32[]{:S(2)}) collective-permute-start(bf16[4,12288]{1,0:T(4,128)(2,1)} %refs_0_), channel_id=1, source_target_pairs={{0,8},{1,9},{2,10},{3,11},{4,12},{5,13},{6,14},{7,15},{8,0},{9,1},... | collective-permute-start | bytes 294920 | tf_op jit(solution)/shard_map/ppermute | solution.py:166
  4.0 1.6 %collective-permute-start.1 = (bf16[4,12288]{1,0:T(4,128)(2,1)}, bf16[4,12288]{1,0:T(4,128)(2,1)S(1)}, u32[]{:S(2)}, u32[]{:S(2)}) collective-permute-start(bf16[4,12288]{1,0:T(4,128)(2,1)} %refs_0_), channel_id=1, source_target_pairs={{0,4},{1,5},{2,6},{3,7},{4,0},{5,1},{6,2},{7,3},{8,12},{9,13},{10,... | collective-permute-start | bytes 294920 | tf_op jit(solution)/shard_map/ppermute | solution.py:166
  5.6 0.8 %copy.13 = s32[4,6]{0,1:T(8,128)S(1)} copy(s32[4,6]{1,0:T(4,128)} %param.15) | data formatting | bytes 192 | tf_op args[3]
  8.5 1.6 %collective-permute-done.1.refs_1_ = bf16[4,12288]{1,0:T(4,128)(2,1)S(1)} collective-permute-done((bf16[4,12288]{1,0:T(4,128)(2,1)}, bf16[4,12288]{1,0:T(4,128)(2,1)S(1)}, u32[]{:S(2)}, u32[]{:S(2)}) %collective-permute-start.1) | collective-permute-done | bytes 98336 | tf_op jit(solution)/shard_map/ppermute | solution.py:166
  10.1 1.9 %copy-done = bf16[12288,128]{1,0:T(8,128)(2,1)S(1)} copy-done((bf16[12288,128]{1,0:T(8,128)(2,1)S(1)}, bf16[12288,128]{1,0:T(8,128)(2,1)}, u32[]{:S(2)}) %copy-start) | copy-done | bytes 3145752
  12.0 1.1 %copy-done.1 = bf16[768,512]{1,0:T(8,128)(2,1)S(1)} copy-done((bf16[768,512]{1,0:T(8,128)(2,1)S(1)}, bf16[768,512]{1,0:T(8,128)(2,1)}, u32[]{:S(2)}) %copy-start.1) | copy-done | bytes 786456
  13.1 1.1 %copy-done.2 = bf16[512,768]{1,0:T(8,128)(2,1)S(1)} copy-done((bf16[512,768]{1,0:T(8,128)(2,1)S(1)}, bf16[512,768]{1,0:T(8,128)(2,1)}, u32[]{:S(2)}) %copy-start.2) | copy-done | bytes 786456
  14.3 0.9 %copy-done.4 = bf16[4,12288]{1,0:T(4,128)(2,1)S(1)} copy-done((bf16[4,12288]{1,0:T(4,128)(2,1)S(1)}, bf16[4,12288]{1,0:T(4,128)(2,1)}, u32[]{:S(2)}) %copy-start.4) | copy-done | bytes 98328
  15.2 0.8 %copy-done.5 = f32[12288]{0:T(1024)S(1)} copy-done((f32[12288]{0:T(1024)S(1)}, f32[12288]{0:T(1024)}, u32[]{:S(2)}) %copy-start.5) | copy-done | bytes 49176
  16.0 0.8 %copy-done.6 = f32[12288]{0:T(1024)S(1)} copy-done((f32[12288]{0:T(1024)S(1)}, f32[12288]{0:T(1024)}, u32[]{:S(2)}) %copy-start.6) | copy-done | bytes 49176
  16.8 2.4 %shard_map.118 = (bf16[4,12288]{1,0:T(4,128)(2,1)S(1)}, f32[1,12288]{1,0:T(1,128)S(1)}, f32[1,12288]{1,0:T(1,128)S(1)}, bf16[768,512]{1,0:T(8,128)(2,1)S(1)}, bf...) custom-call(bf16[4,12288]{1,0:T(4,128)(2,1)S(1)} %copy-done.4, ...), custom_call_target="tpu_custom_call" | custom-call | bytes 8388608 | tf_op jit(solution)/shard_map/pallas_call | solution.py:193
  19.8 1.5 %collective-permute-start.4 = (bf16[4,12288]{1,0:T(4,128)(2,1)S(1)}, bf16[4,12288]{1,0:T(4,128)(2,1)S(1)}, u32[]{:S(2)}, u32[]{:S(2)}) collective-permute-start(bf16[4,12288]{1,0:T(4,128)(2,1)S(1)} %copy-done.4), channel_id=1, source_target_pairs={{0,2},{1,3},{2,0},{3,1},{4,6},{5,7},{6,4},{7,5},{8,10},{9,11},{10,... | collective-permute-start | bytes 294920 | tf_op jit(solution)/shard_map/ppermute | solution.py:169
  21.9 1.5 %collective-permute-start.5 = (bf16[4,12288]{1,0:T(4,128)(2,1)S(1)}, bf16[4,12288]{1,0:T(4,128)(2,1)S(1)}, u32[]{:S(2)}, u32[]{:S(2)}) collective-permute-start(bf16[4,12288]{1,0:T(4,128)(2,1)S(1)} %collective-permute-done.1.refs_1_), channel_id=1, source_target_pairs={{0,2},{1,3},{2,0},{3,1},{4,6},{5,7},{6,4},{7,5},{8,10},{9,11},{10,... | collective-permute-start | bytes 294920 | tf_op jit(solution)/shard_map/ppermute | solution.py:169
  23.4 2.1 %collective-permute-done.4.refs_4_ = bf16[4,12288]{1,0:T(4,128)(2,1)S(1)} collective-permute-done((bf16[4,12288]{1,0:T(4,128)(2,1)S(1)}, bf16[4,12288]{1,0:T(4,128)(2,1)S(1)}, u32[]{:S(2)}, u32[]{:S(2)}) %collective-permute-start.4) | collective-permute-done | bytes 98336 | tf_op jit(solution)/shard_map/ppermute | solution.py:169
  25.5 1.5 %collective-permute-start.6 = (bf16[4,12288]{1,0:T(4,128)(2,1)S(1)}, bf16[4,12288]{1,0:T(4,128)(2,1)S(1)}, u32[]{:S(2)}, u32[]{:S(2)}) collective-permute-start(bf16[4,12288]{1,0:T(4,128)(2,1)S(1)} %collective-permute-done.refs_2_), channel_id=1, source_target_pairs={{0,2},{1,3},{2,0},{3,1},{4,6},{5,7},{6,4},{7,5},{8,10},{9,11},{10,... | collective-permute-start | bytes 294920 | tf_op jit(solution)/shard_map/ppermute | solution.py:169
  27.6 2.1 %collective-permute-done.5.refs_5_ = bf16[4,12288]{1,0:T(4,128)(2,1)S(1)} collective-permute-done((bf16[4,12288]{1,0:T(4,128)(2,1)S(1)}, bf16[4,12288]{1,0:T(4,128)(2,1)S(1)}, u32[]{:S(2)}, u32[]{:S(2)}) %collective-permute-start.5) | collective-permute-done | bytes 98336 | tf_op jit(solution)/shard_map/ppermute | solution.py:169
  29.7 1.2 %collective-permute-done.6.refs_6_ = bf16[4,12288]{1,0:T(4,128)(2,1)S(1)} collective-permute-done((bf16[4,12288]{1,0:T(4,128)(2,1)S(1)}, bf16[4,12288]{1,0:T(4,128)(2,1)S(1)}, u32[]{:S(2)}, u32[]{:S(2)}) %collective-permute-start.6) | collective-permute-done | bytes 98336 | tf_op jit(solution)/shard_map/ppermute | solution.py:169
  30.9 2.4 %shard_map.119 = (bf16[32,12288]{1,0:T(8,128)(2,1)S(1)}, f32[32,512]{1,0:T(8,128)S(1)}, bf16[32,512]{1,0:T(8,128)(2,1)S(1)}) custom-call(s32[1]{0:T(128)} %bitcast.place, bf16[4,12288]{1,0:T(4,128)(2,1)S(1)} %get-tuple-element.69.refs_0_, bf16[4,12288]{1,0:T(4,128)(2,1)S(1)} %collective-permute-done.1.refs_1_, ...), custom_call_target="tpu_custom_call" | custom-call | bytes 6291456 | tf_op jit(solution)/shard_map/pallas_call | solution.py:210
  33.3 1.5 %collective-permute-start.8 = (bf16[32,512]{1,0:T(8,128)(2,1)S(1)}, bf16[32,512]{1,0:T(8,128)(2,1)S(1)}, u32[]{:S(2)}, u32[]{:S(2)}) collective-permute-start(bf16[32,512]{1,0:T(8,128)(2,1)S(1)} %get-tuple-element.77), channel_id=1, source_target_pairs={{0,2},{1,3},{2,0},{3,1},{4,6},{5,7},{6,4},{7,5},{8,10},{9,11},{10,... | collective-permute-start | bytes 98312 | tf_op jit(solution)/shard_map/ppermute | solution.py:169
  34.9 2.4 %collective-permute-done.8.got = bf16[32,512]{1,0:T(8,128)(2,1)S(1)} collective-permute-done((bf16[32,512]{1,0:T(8,128)(2,1)S(1)}, bf16[32,512]{1,0:T(8,128)(2,1)S(1)}, u32[]{:S(2)}, u32[]{:S(2)}) %collective-permute-start.8) | collective-permute-done | bytes 32800 | tf_op jit(solution)/shard_map/ppermute | solution.py:169
  37.3 1.2 %shard_map.121.act = bf16[32,256]{1,0:T(8,128)(2,1)S(1)} custom-call(bf16[32,12288]{1,0:T(8,128)(2,1)S(1)} %get-tuple-element.80.normed, bf16[12288,128]{1,0:T(8,128)(2,1)S(1)} %get-tuple-element.81.w_own, bf16[12288,128]{1,0:T(8,128)(2,1)S(1)} %collective-permute-done.9.w_mate, f32[1,128]{1,0:T(1,128)S(1)} %bitcast.15, ...), custom_call_target="tpu_custom_call" | custom-call | bytes 6291456 | tf_op jit(solution)/shard_map/pallas_call | solution.py:220
  38.5 1.9 %collective-permute-start.11 = (bf16[32,512]{1,0:T(8,128)(2,1)S(1)}, bf16[32,512]{1,0:T(8,128)(2,1)S(1)}, u32[]{:S(2)}, u32[]{:S(2)}) collective-permute-start(bf16[32,512]{1,0:T(8,128)(2,1)S(1)} %get-tuple-element.85), channel_id=1, source_target_pairs={{0,4},{1,5},{2,6},{3,7},{4,0},{5,1},{6,2},{7,3},{8,12},{9,13},{10,... | collective-permute-start | bytes 98312 | tf_op jit(solution)/shard_map/ppermute | solution.py:166
  40.4 2.1 %collective-permute-done.11.got = bf16[32,512]{1,0:T(8,128)(2,1)S(1)} collective-permute-done((bf16[32,512]{1,0:T(8,128)(2,1)S(1)}, bf16[32,512]{1,0:T(8,128)(2,1)S(1)}, u32[]{:S(2)}, u32[]{:S(2)}) %collective-permute-start.11) | collective-permute-done | bytes 32800 | tf_op jit(solution)/shard_map/ppermute | solution.py:166
  42.5 1.8 %collective-permute-start.12 = (bf16[32,512]{1,0:T(8,128)(2,1)S(1)}, bf16[32,512]{1,0:T(8,128)(2,1)S(1)}, u32[]{:S(2)}, u32[]{:S(2)}) collective-permute-start(bf16[32,512]{1,0:T(8,128)(2,1)S(1)} %get-tuple-element.87), channel_id=1, source_target_pairs={{0,8},{1,9},{2,10},{3,11},{4,12},{5,13},{6,14},{7,15},{8,0},{9,1},... | collective-permute-start | bytes 98312 | tf_op jit(solution)/shard_map/ppermute | solution.py:166
  44.4 1.2 %shard_map.123.part = f32[32,12288]{1,0:T(8,128)S(1)} custom-call(bf16[32,256]{1,0:T(8,128)(2,1)S(1)} %shard_map.121.act, bf16[128,12288]{1,0:T(8,128)(2,1)S(1)} %get-tuple-element.89.w_own, bf16[128,12288]{1,0:T(8,128)(2,1)S(1)} %collective-permute-done.13.w_mate), custom_call_target="tpu_custom_call" | custom-call | bytes 6291456 | tf_op jit(solution)/shard_map/pallas_call | solution.py:240
  45.5 1.9 %collective-permute-done.12.got = bf16[32,512]{1,0:T(8,128)(2,1)S(1)} collective-permute-done((bf16[32,512]{1,0:T(8,128)(2,1)S(1)}, bf16[32,512]{1,0:T(8,128)(2,1)S(1)}, u32[]{:S(2)}, u32[]{:S(2)}) %collective-permute-start.12) | collective-permute-done | bytes 32800 | tf_op jit(solution)/shard_map/ppermute | solution.py:166
  47.9 1.5 %collective-permute-start.16 = (bf16[4,12288]{1,0:T(4,128)(2,1)S(1)}, bf16[4,12288]{1,0:T(4,128)(2,1)S(1)}, u32[]{:S(2)}, u32[]{:S(2)}) collective-permute-start(bf16[4,12288]{1,0:T(4,128)(2,1)S(1)} %get-tuple-element.98), channel_id=1, source_target_pairs={{0,2},{1,3},{2,0},{3,1},{4,6},{5,7},{6,4},{7,5},{8,10},{9,11},{10,... | collective-permute-start | bytes 294920 | tf_op jit(solution)/shard_map/ppermute | solution.py:169
  49.9 1.5 %collective-permute-start.18 = (bf16[4,12288]{1,0:T(4,128)(2,1)S(1)}, bf16[4,12288]{1,0:T(4,128)(2,1)S(1)}, u32[]{:S(2)}, u32[]{:S(2)}) collective-permute-start(bf16[4,12288]{1,0:T(4,128)(2,1)S(1)} %get-tuple-element.100), channel_id=1, source_target_pairs={{0,2},{1,3},{2,0},{3,1},{4,6},{5,7},{6,4},{7,5},{8,10},{9,11},{10,... | collective-permute-start | bytes 294920 | tf_op jit(solution)/shard_map/ppermute | solution.py:169
  52.6 1.9 %collective-permute-start.17 = (bf16[4,12288]{1,0:T(4,128)(2,1)S(1)}, bf16[4,12288]{1,0:T(4,128)(2,1)S(1)}, u32[]{:S(2)}, u32[]{:S(2)}) collective-permute-start(bf16[4,12288]{1,0:T(4,128)(2,1)S(1)} %add_convert_fusion.2), channel_id=1, source_target_pairs={{0,4},{1,5},{2,6},{3,7},{4,0},{5,1},{6,2},{7,3},{8,12},{9,13},{10,... | collective-permute-start | bytes 294920 | tf_op jit(solution)/shard_map/ppermute | solution.py:166
  55.1 1.9 %collective-permute-start.19 = (bf16[4,12288]{1,0:T(4,128)(2,1)S(1)}, bf16[4,12288]{1,0:T(4,128)(2,1)S(1)}, u32[]{:S(2)}, u32[]{:S(2)}) collective-permute-start(bf16[4,12288]{1,0:T(4,128)(2,1)S(1)} %add_convert_fusion.1), channel_id=1, source_target_pairs={{0,8},{1,9},{2,10},{3,11},{4,12},{5,13},{6,14},{7,15},{8,0},{9,1},... | collective-permute-start | bytes 294920 | tf_op jit(solution)/shard_map/ppermute | solution.py:166
  57.1 2.8 %collective-permute-start.21 = (bf16[4,12288]{1,0:T(4,128)(2,1)S(1)}, bf16[4,12288]{1,0:T(4,128)(2,1)S(1)}, u32[]{:S(2)}, u32[]{:S(2)}) collective-permute-start(bf16[4,12288]{1,0:T(4,128)(2,1)S(1)} %add_convert_fusion), channel_id=1, source_target_pairs={{0,12},{1,13},{2,14},{3,15},{4,8},{5,9},{6,10},{7,11},{8,4},{9,5},... | collective-permute-start | bytes 294920 | tf_op jit(solution)/shard_map/ppermute | solution.py:166
  60.7 2.9 %collective-permute-done.21.refs_3_ = bf16[4,12288]{1,0:T(4,128)(2,1)S(1)} collective-permute-done((bf16[4,12288]{1,0:T(4,128)(2,1)S(1)}, bf16[4,12288]{1,0:T(4,128)(2,1)S(1)}, u32[]{:S(2)}, u32[]{:S(2)}) %collective-permute-start.21) | collective-permute-done | bytes 98336 | tf_op jit(solution)/shard_map/ppermute | solution.py:166
  (55 shorter events, 8.7 us)
Async XLA Ops:
  0.0 19.3 %collective-permute-start.9 = (bf16[12288,128]{1,0:T(8,128)(2,1)}, bf16[12288,128]{1,0:T(8,128)(2,1)S(1)}, u32[]{:S(2)}, u32[]{:S(2)}) collective-permute-start(bf16[12288,128]{1,0:T(8,128)(2,1)} %refs_4_), channel_id=1, source_target_pairs={{0,1},{1,0},{2,3},{3,2},{4,5},{5,4},{6,7},{7,6},{8,9},{9,8},{10,11... | collective-permute-start | bytes 9437192 | tf_op jit(solution)/shard_map/ppermute | solution.py:172
  0.5 18.8 %collective-permute-start = (bf16[4,12288]{1,0:T(4,128)(2,1)}, bf16[4,12288]{1,0:T(4,128)(2,1)S(1)}, u32[]{:S(2)}, u32[]{:S(2)}) collective-permute-start(bf16[4,12288]{1,0:T(4,128)(2,1)} %refs_0_), channel_id=1, source_target_pairs={{0,8},{1,9},{2,10},{3,11},{4,12},{5,13},{6,14},{7,15},{8,0},{9,1},... | collective-permute-start | bytes 294920 | tf_op jit(solution)/shard_map/ppermute | solution.py:166
  4.0 6.1 %collective-permute-start.1 = (bf16[4,12288]{1,0:T(4,128)(2,1)}, bf16[4,12288]{1,0:T(4,128)(2,1)S(1)}, u32[]{:S(2)}, u32[]{:S(2)}) collective-permute-start(bf16[4,12288]{1,0:T(4,128)(2,1)} %refs_0_), channel_id=1, source_target_pairs={{0,4},{1,5},{2,6},{3,7},{4,0},{5,1},{6,2},{7,3},{8,12},{9,13},{10,... | collective-permute-start | bytes 294920 | tf_op jit(solution)/shard_map/ppermute | solution.py:166
  5.6 13.6 %collective-permute-start.3 = (bf16[4,12288]{1,0:T(4,128)(2,1)}, bf16[4,12288]{1,0:T(4,128)(2,1)S(1)}, u32[]{:S(2)}, u32[]{:S(2)}) collective-permute-start(bf16[4,12288]{1,0:T(4,128)(2,1)} %refs_0_), channel_id=1, source_target_pairs={{0,12},{1,13},{2,14},{3,15},{4,8},{5,9},{6,10},{7,11},{8,4},{9,5},... | collective-permute-start | bytes 294920 | tf_op jit(solution)/shard_map/ppermute | solution.py:166
  5.6 4.5 %collective-permute-start.2 = (bf16[768,512]{1,0:T(8,128)(2,1)}, bf16[768,512]{1,0:T(8,128)(2,1)}, u32[]{:S(2)}, u32[]{:S(2)}) collective-permute-start(bf16[768,512]{1,0:T(8,128)(2,1)} %refs_3_), channel_id=1, source_target_pairs={{0,1},{1,0},{2,3},{3,2},{4,5},{5,4},{6,7},{7,6},{8,9},{9,8},{10,11... | collective-permute-start | bytes 2359304 | tf_op jit(solution)/shard_map/ppermute | solution.py:172
  10.1 1.9 %copy-start = (bf16[12288,128]{1,0:T(8,128)(2,1)S(1)}, bf16[12288,128]{1,0:T(8,128)(2,1)}, u32[]{:S(2)}) copy-start(bf16[12288,128]{1,0:T(8,128)(2,1)} %refs_4_) | copy-start | bytes 9437188
  12.0 1.1 %copy-start.1 = (bf16[768,512]{1,0:T(8,128)(2,1)S(1)}, bf16[768,512]{1,0:T(8,128)(2,1)}, u32[]{:S(2)}) copy-start(bf16[768,512]{1,0:T(8,128)(2,1)} %refs_3_) | copy-start | bytes 2359300
  13.1 1.1 %copy-start.2 = (bf16[512,768]{1,0:T(8,128)(2,1)S(1)}, bf16[512,768]{1,0:T(8,128)(2,1)}, u32[]{:S(2)}) copy-start(bf16[512,768]{1,0:T(8,128)(2,1)} %refs_6_) | copy-start | bytes 2359300
  14.3 0.9 %copy-start.4 = (bf16[4,12288]{1,0:T(4,128)(2,1)S(1)}, bf16[4,12288]{1,0:T(4,128)(2,1)}, u32[]{:S(2)}) copy-start(bf16[4,12288]{1,0:T(4,128)(2,1)} %refs_0_) | copy-start | bytes 294916
  15.2 0.8 %copy-start.5 = (f32[12288]{0:T(1024)S(1)}, f32[12288]{0:T(1024)}, u32[]{:S(2)}) copy-start(f32[12288]{0:T(1024)} %param.13) | copy-start | bytes 147460
  16.0 0.8 %copy-start.6 = (f32[12288]{0:T(1024)S(1)}, f32[12288]{0:T(1024)}, u32[]{:S(2)}) copy-start(f32[12288]{0:T(1024)} %param.14) | copy-start | bytes 147460
  16.8 2.6 %copy-start.3 = (bf16[512,768]{1,0:T(8,128)(2,1)S(1)}, bf16[512,768]{1,0:T(8,128)(2,1)}, u32[]{:S(2)}) copy-start(bf16[512,768]{1,0:T(8,128)(2,1)} %refs_6_) | copy-start | bytes 2359300
  16.8 18.1 %copy-start.8 = (f32[128]{0:T(128)S(1)}, f32[128]{0:T(128)}, u32[]{:S(2)}) copy-start(f32[128]{0:T(128)} %param.19) | copy-start | bytes 1540
  19.3 25.1 %collective-permute-start.13 = (bf16[128,12288]{1,0:T(8,128)(2,1)}, bf16[128,12288]{1,0:T(8,128)(2,1)S(1)}, u32[]{:S(2)}, u32[]{:S(2)}) collective-permute-start(bf16[128,12288]{1,0:T(8,128)(2,1)} %refs_5_), channel_id=1, source_target_pairs={{0,1},{1,0},{2,3},{3,2},{4,5},{5,4},{6,7},{7,6},{8,9},{9,8},{10,11... | collective-permute-start | bytes 9437192 | tf_op jit(solution)/shard_map/ppermute | solution.py:172
  19.4 28.0 %collective-permute-start.14 = (bf16[512,768]{1,0:T(8,128)(2,1)S(1)}, bf16[512,768]{1,0:T(8,128)(2,1)S(1)}, u32[]{:S(2)}, u32[]{:S(2)}) collective-permute-start(bf16[512,768]{1,0:T(8,128)(2,1)S(1)} %copy-done.3), channel_id=1, source_target_pairs={{0,1},{1,0},{2,3},{3,2},{4,5},{5,4},{6,7},{7,6},{8,9},{9,8},{10,11... | collective-permute-start | bytes 2359304 | tf_op jit(solution)/shard_map/ppermute | solution.py:172
  19.8 5.6 %collective-permute-start.4 = (bf16[4,12288]{1,0:T(4,128)(2,1)S(1)}, bf16[4,12288]{1,0:T(4,128)(2,1)S(1)}, u32[]{:S(2)}, u32[]{:S(2)}) collective-permute-start(bf16[4,12288]{1,0:T(4,128)(2,1)S(1)} %copy-done.4), channel_id=1, source_target_pairs={{0,2},{1,3},{2,0},{3,1},{4,6},{5,7},{6,4},{7,5},{8,10},{9,11},{10,... | collective-permute-start | bytes 294920 | tf_op jit(solution)/shard_map/ppermute | solution.py:169
  21.3 6.3 %collective-permute-start.7 = (bf16[4,12288]{1,0:T(4,128)(2,1)S(1)}, bf16[4,12288]{1,0:T(4,128)(2,1)S(1)}, u32[]{:S(2)}, u32[]{:S(2)}) collective-permute-start(bf16[4,12288]{1,0:T(4,128)(2,1)S(1)} %collective-permute-done.3.refs_3_), channel_id=1, source_target_pairs={{0,2},{1,3},{2,0},{3,1},{4,6},{5,7},{6,4},{7,5},{8,10},{9,11},{10,... | collective-permute-start | bytes 294920 | tf_op jit(solution)/shard_map/ppermute | solution.py:169
  21.9 7.8 %collective-permute-start.5 = (bf16[4,12288]{1,0:T(4,128)(2,1)S(1)}, bf16[4,12288]{1,0:T(4,128)(2,1)S(1)}, u32[]{:S(2)}, u32[]{:S(2)}) collective-permute-start(bf16[4,12288]{1,0:T(4,128)(2,1)S(1)} %collective-permute-done.1.refs_1_), channel_id=1, source_target_pairs={{0,2},{1,3},{2,0},{3,1},{4,6},{5,7},{6,4},{7,5},{8,10},{9,11},{10,... | collective-permute-start | bytes 294920 | tf_op jit(solution)/shard_map/ppermute | solution.py:169
  25.5 5.5 %collective-permute-start.6 = (bf16[4,12288]{1,0:T(4,128)(2,1)S(1)}, bf16[4,12288]{1,0:T(4,128)(2,1)S(1)}, u32[]{:S(2)}, u32[]{:S(2)}) collective-permute-start(bf16[4,12288]{1,0:T(4,128)(2,1)S(1)} %collective-permute-done.refs_2_), channel_id=1, source_target_pairs={{0,2},{1,3},{2,0},{3,1},{4,6},{5,7},{6,4},{7,5},{8,10},{9,11},{10,... | collective-permute-start | bytes 294920 | tf_op jit(solution)/shard_map/ppermute | solution.py:169
  33.3 4.0 %collective-permute-start.8 = (bf16[32,512]{1,0:T(8,128)(2,1)S(1)}, bf16[32,512]{1,0:T(8,128)(2,1)S(1)}, u32[]{:S(2)}, u32[]{:S(2)}) collective-permute-start(bf16[32,512]{1,0:T(8,128)(2,1)S(1)} %get-tuple-element.77), channel_id=1, source_target_pairs={{0,2},{1,3},{2,0},{3,1},{4,6},{5,7},{6,4},{7,5},{8,10},{9,11},{10,... | collective-permute-start | bytes 98312 | tf_op jit(solution)/shard_map/ppermute | solution.py:169
  34.9 2.4 %collective-permute-start.10 = (f32[1,128]{1,0:T(1,128)S(1)}, f32[1,128]{1,0:T(1,128)S(1)}, u32[]{:S(2)}, u32[]{:S(2)}) collective-permute-start(f32[1,128]{1,0:T(1,128)S(1)} %bitcast.14), channel_id=1, source_target_pairs={{0,1},{1,0},{2,3},{3,2},{4,5},{5,4},{6,7},{7,6},{8,9},{9,8},{10,11... | collective-permute-start | bytes 1544 | tf_op jit(solution)/shard_map/ppermute | solution.py:172
  38.5 4.0 %collective-permute-start.11 = (bf16[32,512]{1,0:T(8,128)(2,1)S(1)}, bf16[32,512]{1,0:T(8,128)(2,1)S(1)}, u32[]{:S(2)}, u32[]{:S(2)}) collective-permute-start(bf16[32,512]{1,0:T(8,128)(2,1)S(1)} %get-tuple-element.85), channel_id=1, source_target_pairs={{0,4},{1,5},{2,6},{3,7},{4,0},{5,1},{6,2},{7,3},{8,12},{9,13},{10,... | collective-permute-start | bytes 98312 | tf_op jit(solution)/shard_map/ppermute | solution.py:166
  42.5 4.9 %copy-start.7 = (f32[512]{0:T(512)S(1)}, f32[512]{0:T(512)}, u32[]{:S(2)}) copy-start(f32[512]{0:T(512)} %param.22) | copy-start | bytes 6148
  42.5 4.9 %collective-permute-start.12 = (bf16[32,512]{1,0:T(8,128)(2,1)S(1)}, bf16[32,512]{1,0:T(8,128)(2,1)S(1)}, u32[]{:S(2)}, u32[]{:S(2)}) collective-permute-start(bf16[32,512]{1,0:T(8,128)(2,1)S(1)} %get-tuple-element.87), channel_id=1, source_target_pairs={{0,8},{1,9},{2,10},{3,11},{4,12},{5,13},{6,14},{7,15},{8,0},{9,1},... | collective-permute-start | bytes 98312 | tf_op jit(solution)/shard_map/ppermute | solution.py:166
  47.9 4.7 %collective-permute-start.16 = (bf16[4,12288]{1,0:T(4,128)(2,1)S(1)}, bf16[4,12288]{1,0:T(4,128)(2,1)S(1)}, u32[]{:S(2)}, u32[]{:S(2)}) collective-permute-start(bf16[4,12288]{1,0:T(4,128)(2,1)S(1)} %get-tuple-element.98), channel_id=1, source_target_pairs={{0,2},{1,3},{2,0},{3,1},{4,6},{5,7},{6,4},{7,5},{8,10},{9,11},{10,... | collective-permute-start | bytes 294920 | tf_op jit(solution)/shard_map/ppermute | solution.py:169
  49.4 10.5 %collective-permute-start.15 = (bf16[4,12288]{1,0:T(4,128)(2,1)S(1)}, bf16[4,12288]{1,0:T(4,128)(2,1)S(1)}, u32[]{:S(2)}, u32[]{:S(2)}) collective-permute-start(bf16[4,12288]{1,0:T(4,128)(2,1)S(1)} %get-tuple-element.96), channel_id=1, source_target_pairs={{0,2},{1,3},{2,0},{3,1},{4,6},{5,7},{6,4},{7,5},{8,10},{9,11},{10,... | collective-permute-start | bytes 294920 | tf_op jit(solution)/shard_map/ppermute | solution.py:169
  49.9 5.1 %collective-permute-start.18 = (bf16[4,12288]{1,0:T(4,128)(2,1)S(1)}, bf16[4,12288]{1,0:T(4,128)(2,1)S(1)}, u32[]{:S(2)}, u32[]{:S(2)}) collective-permute-start(bf16[4,12288]{1,0:T(4,128)(2,1)S(1)} %get-tuple-element.100), channel_id=1, source_target_pairs={{0,2},{1,3},{2,0},{3,1},{4,6},{5,7},{6,4},{7,5},{8,10},{9,11},{10,... | collective-permute-start | bytes 294920 | tf_op jit(solution)/shard_map/ppermute | solution.py:169
  51.4 5.6 %collective-permute-start.20 = (bf16[4,12288]{1,0:T(4,128)(2,1)S(1)}, bf16[4,12288]{1,0:T(4,128)(2,1)S(1)}, u32[]{:S(2)}, u32[]{:S(2)}) collective-permute-start(bf16[4,12288]{1,0:T(4,128)(2,1)S(1)} %get-tuple-element.102), channel_id=1, source_target_pairs={{0,2},{1,3},{2,0},{3,1},{4,6},{5,7},{6,4},{7,5},{8,10},{9,11},{10,... | collective-permute-start | bytes 294920 | tf_op jit(solution)/shard_map/ppermute | solution.py:169
  52.6 7.4 %collective-permute-start.17 = (bf16[4,12288]{1,0:T(4,128)(2,1)S(1)}, bf16[4,12288]{1,0:T(4,128)(2,1)S(1)}, u32[]{:S(2)}, u32[]{:S(2)}) collective-permute-start(bf16[4,12288]{1,0:T(4,128)(2,1)S(1)} %add_convert_fusion.2), channel_id=1, source_target_pairs={{0,4},{1,5},{2,6},{3,7},{4,0},{5,1},{6,2},{7,3},{8,12},{9,13},{10,... | collective-permute-start | bytes 294920 | tf_op jit(solution)/shard_map/ppermute | solution.py:166
  55.1 5.6 %collective-permute-start.19 = (bf16[4,12288]{1,0:T(4,128)(2,1)S(1)}, bf16[4,12288]{1,0:T(4,128)(2,1)S(1)}, u32[]{:S(2)}, u32[]{:S(2)}) collective-permute-start(bf16[4,12288]{1,0:T(4,128)(2,1)S(1)} %add_convert_fusion.1), channel_id=1, source_target_pairs={{0,8},{1,9},{2,10},{3,11},{4,12},{5,13},{6,14},{7,15},{8,0},{9,1},... | collective-permute-start | bytes 294920 | tf_op jit(solution)/shard_map/ppermute | solution.py:166
  57.1 6.5 %collective-permute-start.21 = (bf16[4,12288]{1,0:T(4,128)(2,1)S(1)}, bf16[4,12288]{1,0:T(4,128)(2,1)S(1)}, u32[]{:S(2)}, u32[]{:S(2)}) collective-permute-start(bf16[4,12288]{1,0:T(4,128)(2,1)S(1)} %add_convert_fusion), channel_id=1, source_target_pairs={{0,12},{1,13},{2,14},{3,15},{4,8},{5,9},{6,10},{7,11},{8,4},{9,5},... | collective-permute-start | bytes 294920 | tf_op jit(solution)/shard_map/ppermute | solution.py:166

commit v7 on v6

--- a/solution.py
+++ b/solution.py
@@ -9,7 +9,7 @@
 
 MIB = 1 << 20
 VMEM = pl.BlockSpec(memory_space=pltpu.VMEM)
-HBM = pl.BlockSpec(memory_space=pl.ANY)
+HBM = pl.BlockSpec(memory_space=pltpu.HBM)
 SMEM = pl.BlockSpec(memory_space=pltpu.SMEM)
 f32, bf16 = jnp.float32, jnp.bfloat16
 
@@ -54,22 +54,33 @@
         copy.wait()
 
 
-def norm_body(groups, place, *refs):
-    held, (gain, shift, own, mate, out, total, message) = refs[: 2 * groups], refs[2 * groups :]
+def early_body(groups, soon, *refs):
+    held, (gain, shift, near, far) = refs[: groups + soon], refs[groups + soon :]
     rows = held[0].shape[0]
-    for i in range(0, 2 * groups, 2):
-        pair = jnp.concatenate([held[i][...], held[i + 1][...]], axis=0)
-        out[i * rows : (i + 2) * rows, :] = normal(pair, gain[...], shift[...])
+    for out, some in ((near, held[:groups]), (far, held[groups:])):
+        for i in range(0, len(some), 2):
+            pair = jnp.concatenate([h[...] for h in some[i : i + 2]], axis=0)
+            out[i * rows : i * rows + pair.shape[0], :] = normal(pair, gain[...], shift[...])
+
+
+def norm_body(count, place, *refs):
+    held, (near, first, gain, shift, own, mate, far, total, message) = refs[:count], refs[count:]
+    rows, done = held[0].shape[0], first.shape[0]
+    far[:done, :] = first[...]
+    for i in range(0, count, 2):
+        pair = jnp.concatenate([h[...] for h in held[i : i + 2]], axis=0)
+        far[done + i * rows : done + i * rows + pair.shape[0], :] = normal(pair, gain[...], shift[...])
     share = own.shape[0]
     core = place[0] % 2
-    columns = out[:, window(place[0] // 2, 2 * share)].astype(f32)
+    at = window(place[0] // 2, 2 * share)
+    columns = jnp.concatenate([near[:, at].astype(f32), far[:, at].astype(f32)], axis=0)
     low, high = columns[:, :share], columns[:, share:]
     mine = jnp.where(core == 0, low, high).astype(bf16)
     other = jnp.where(core == 0, high, low).astype(bf16)
     sums = jnp.dot(mine, own[...], preferred_element_type=f32) + jnp.dot(
         other, mate[...], preferred_element_type=f32
     )
-    half = groups * rows
+    half = near.shape[0]
     total[...] = sums
     message[:half, :] = sums[half:].astype(bf16)
     message[half:, :] = sums[:half].astype(bf16)
@@ -81,14 +92,19 @@
     return jnp.concatenate([x[i * rows : (i + 1) * rows] for i in at], axis=0)
 
 
-def merge_body(groups, bit, total, got, out, message):
+def merge_body(groups, total, got, out, *messages):
     sums = total[...] + got[...].astype(f32)
     out[...] = sums
-    message[...] = turn(sums, groups, bit).astype(bf16)
-
-
-def up_body(groups, place, total, got, bias, own, mate, part, *outs):
-    hidden = jnp.maximum(total[...] + got[...].astype(f32) + bias[...], 0.0).astype(bf16)
+    for k in range(1, groups):
+        messages[k - 1][...] = turn(sums, groups, k).astype(bf16)
+
+
+def up_body(groups, place, total, bias, own, mate, part, *refs):
+    got, outs = refs[: groups - 1], refs[groups - 1 :]
+    sums = total[...]
+    for g in got:
+        sums = sums + g[...].astype(f32)
+    hidden = jnp.maximum(sums + bias[...], 0.0).astype(bf16)
     core = place[0] % 2
     mine = jnp.dot(hidden, own[...], preferred_element_type=f32)
     other = jnp.dot(hidden, mate[...], preferred_element_type=f32)
@@ -109,12 +125,13 @@
     out[...] = total.astype(bf16)
 
 
-def act_body(step, normed, w_own, w_mate, b_own, b_mate, mask, out):
+def act_body(step, near, far, w_own, w_mate, b_own, b_mate, mask, out):
     total = jnp.zeros(out.shape, f32)
-    for i in range(normed.shape[1] // step):
+    for i in range(near.shape[1] // step):
         at = slice(i * step, (i + 1) * step)
+        rows = jnp.concatenate([near[:, at], far[:, at]], axis=0)
         both = jnp.concatenate([w_own[at, :], w_mate[at, :]], axis=1)
-        total = total + jnp.dot(normed[:, at], both, preferred_element_type=f32)
+        total = total + jnp.dot(rows, both, preferred_element_type=f32)
     bias = jnp.concatenate([b_own[...], b_mate[...]], axis=1)
     out[...] = (jnp.maximum(total + bias, 0.0) * mask[...]).astype(bf16)
 
@@ -186,10 +203,12 @@
     mask = jnp.broadcast_to(live[None, :, None, :, None], (2, groups, row_dev, 2, block)).reshape(rows, 2 * block)
 
     held = [hidden] + [across(hidden, k) for k in range(1, groups)]
-    w_in_mate, low_in_mate = core(w_in), core(low_in)
-    held[1], low_in_mate, mask = lax.optimization_barrier((held[1], low_in_mate, mask))
+    w_in_mate = core(w_in)
+    held[1], low_in_sent, mask = lax.optimization_barrier((held[1], low_in, mask))
+    low_in_mate = core(low_in_sent)
+    beyond = [beside(h) for h in held]
     near = (hidden, gain, shift, low_in, w_in, w_out, low_out)
-    *near, mask = lax.optimization_barrier((*near, mask))
+    *near, mask, beyond[0] = lax.optimization_barrier((*near, mask, beyond[0]))
     near = call(
         functools.partial(load_body, len(near)),
         [shape(*x.shape, dtype=x.dtype) for x in near],
@@ -197,46 +216,48 @@
         16,
         [pltpu.SemaphoreType.DMA((len(near),))],
         8 * MIB,
-    )(*near)
-    held[2], *near = lax.optimization_barrier((held[2], *near))
+    )(*[pltpu.with_memory_space_constraint(x, pltpu.HBM) for x in near])
     hidden_near, gain, shift, low_in, w_in, w_out_near, low_out_near = near
     *_, w_in_mate, w_out_sent, low_out_sent, bias_sent = lax.optimization_barrier(
-        (*held, w_in_mate, w_out, low_out, bias)
+        (*held, *beyond[: groups // 2], w_in_mate, w_out, low_out, bias)
     )
     bias_mate, w_out_mate, low_out_mate = core(bias_sent), core(w_out_sent), core(low_out_sent)
-    beyond = [beside(h) for h in held]
-    held = [hidden_near] + held[1:] + beyond
-
-    normed, total, message = call(
-        functools.partial(norm_body, groups),
-        [shape(rows, width), shape(rows, rank, dtype=f32), shape(rows, rank)],
-        [SMEM] + [VMEM] * (2 * groups + 4),
-        16,
-        (),
-        6 * MIB,
-    )(place, *held, gain, shift, low_in, low_in_mate)
+    held[0] = hidden_near
+
+    soon = groups // 2
+    normed, first = call(
+        functools.partial(early_body, groups, soon),
+        [shape(some, width), shape(soon * row_dev, width)],
+        [VMEM] * (groups + soon + 2),
+        16,
+        (),
+        4 * MIB,
+    )(*held, *beyond[:soon], gain, shift)
+    far, total, message = call(
+        functools.partial(norm_body, groups - soon),
+        [shape(some, width), shape(rows, rank, dtype=f32), shape(rows, rank)],
+        [SMEM] + [VMEM] * (groups - soon + 6),
+        16,
+        (),
+        4 * MIB,
+    )(place, *beyond[soon:], normed, first, gain, shift, low_in, low_in_mate)
     got = beside(message)
     step = piece(width, 2048)
     act = call(
         functools.partial(act_body, step),
         [shape(rows, 2 * block)],
-        [VMEM] * 6,
-        16,
-        (),
-        6 * MIB,
-    )(normed, w_in, w_in_mate, bias, bias_mate, mask)[0]
-    bit = 1
-    while bit < groups:
-        total, message = call(
-            functools.partial(merge_body, groups, bit),
-            [shape(rows, rank, dtype=f32), shape(rows, rank)],
-            [VMEM] * 2,
-            16,
-        )(total, got)
-        if bit == 1:
-            message, act = lax.optimization_barrier((message, act))
-        got = across(message, bit)
-        bit *= 2
+        [VMEM] * 7,
+        16,
+        (),
+        4 * MIB,
+    )(normed, far, w_in, w_in_mate, bias, bias_mate, mask)[0]
+    total, *messages = call(
+        functools.partial(merge_body, groups),
+        [shape(rows, rank, dtype=f32)] + [shape(rows, rank)] * (groups - 1),
+        [VMEM] * 2,
+        16,
+    )(total, got)
+    got = [across(messages[k - 1], k) for k in range(1, groups)]
     part = call(
         functools.partial(part_body, step),
         [shape(rows, width, dtype=f32)],
@@ -245,15 +266,14 @@
         (),
         6 * MIB,
     )(act, w_out_near, w_out_mate)[0]
-    got, part = lax.optimization_barrier((got, part))
     parts = call(
         functools.partial(up_body, groups),
         [shape(row_dev, width, dtype=f32)] * groups + [shape(row_dev, width)] * groups,
-        [SMEM] + [VMEM] * 6,
+        [SMEM] + [VMEM] * (groups + 4),
         16,
         (),
         6 * MIB,
-    )(place, total, got, low_bias.reshape(1, rank), low_out_near, low_out_mate, part)
+    )(place, total, low_bias.reshape(1, rank), low_out_near, low_out_mate, part, *got)
 
     sums = []
     for k in range(groups - 1, -1, -1):

time: 64.8 us -> 52.6 us (0.81)
  local copies, waits for them, and re-layouts: 7.51 us -> 0.86 us
  starting transfers between devices: 27.2 us -> 23.5 us
  waiting for transfers between devices: 18.9 us -> 17.2 us
    unnamed x20 -> x6, local copies, waits for them, and re-layouts: 7.43 us -> 0.79 us
    ppermute x9, waiting for transfers between devices: 9.67 us -> 6.09 us  [beside(): return lax.ppermute(x, 'blk', [(i, i ^ 2) for i in range(devices)])]
    ppermute x8 -> x9, waiting for transfers between devices: 9.2 us -> 11.1 us  [across(): return lax.ppermute(x, 'blk', [(i, i ^ 4 * k) for i in range(devices)])]
    ppermute x9, starting transfers between devices: 10.6 us -> 8.72 us  [beside(): return lax.ppermute(x, 'blk', [(i, i ^ 2) for i in range(devices)])]
    ppermute x8 -> x9, starting transfers between devices: 15.5 us -> 13.6 us  [across(): return lax.ppermute(x, 'blk', [(i, i ^ 4 * k) for i in range(devices)])]
    pallas_call x1, Pallas kernels: 2.45 us -> 3.39 us  [shards(): call(functools.partial(load_body, len(near)), [shape(*x.shape, dtype=x.dt...]
    pallas_call x3, Pallas kernels: 2.41 us -> 1.63 us  [the longest x1 0.82 us: shards(): call(functools.partial(early_body, groups, soon), [shape(some, width), sh...]
  transfers between devices with their start and end apart: 22 -> 23, of which waited for: 12 -> 9; matrix products, arithmetic and copies ran while one was open for 5% -> 6% of each run, Pallas kernels for 11% -> 14%
where the time goes in v7:
time: 52.6 us; the launch traced here: 52.5 us
  starting transfers between devices  23.5 us (45%)
  waiting for transfers between devices  17.2 us (33%)
  Pallas kernels  8.55 us (16%)
  other arithmetic  2.23 us (4%)
  local copies, waits for them, and re-layouts  0.86 us (2%)
    ppermute x9, starting transfers between devices, across(): return lax.ppermute(x, 'blk', [(i, i ^ 4 * k) for i in range(devices)])  13.6 us
    ppermute x9, waiting for transfers between devices, across(): return lax.ppermute(x, 'blk', [(i, i ^ 4 * k) for i in range(devices)])  11.1 us
    ppermute x9, starting transfers between devices, beside(): return lax.ppermute(x, 'blk', [(i, i ^ 2) for i in range(devices)])  8.72 us
    ppermute x9, waiting for transfers between devices, beside(): return lax.ppermute(x, 'blk', [(i, i ^ 2) for i in range(devices)])  6.09 us
    pallas_call x1, Pallas kernels, shards(): call(functools.partial(load_body, len(near)), [shape(*x.shape, dtype=x.dt...  3.39 us
    pallas_call x1, Pallas kernels, shards(): call(functools.partial(part_body, step), [shape(rows, width, dtype=f32)],...  1.2 us
    pallas_call x1, Pallas kernels, shards(): call(functools.partial(act_body, step), [shape(rows, 2 * block)], [VMEM]...  1.19 us
    ppermute x5, starting transfers between devices, core(): return lax.ppermute(x, 'blk', [(i, i ^ 1) for i in range(devices)])  1.1 us
  transfers between devices with their start and end apart: 23, of which 9 were waited for; matrix products, arithmetic and copies ran while one was open for 6% of the time, Pallas kernels for 14%

profile of v7, /device:TPU:0, one launch (start us, length us, event | category | flops | bytes accessed | tf_op | source)
XLA Modules:
  0.0 52.5 jit_solution(3409154459728154124)
XLA Ops:
  0.5 2.6 %collective-permute-start.4 = (bf16[4,12288]{1,0:T(4,128)(2,1)}, bf16[4,12288]{1,0:T(4,128)(2,1)S(1)}, u32[]{:S(2)}, u32[]{:S(2)}) collective-permute-start(bf16[4,12288]{1,0:T(4,128)(2,1)} %refs_0_), channel_id=1, source_target_pairs={{0,4},{1,5},{2,6},{3,7},{4,0},{5,1},{6,2},{7,3},{8,12},{9,13},{10,... | collective-permute-start | bytes 294920 | tf_op jit(solution)/shard_map/ppermute | solution.py:183
  3.0 1.5 %collective-permute-start.5 = (bf16[4,12288]{1,0:T(4,128)(2,1)}, bf16[4,12288]{1,0:T(4,128)(2,1)S(1)}, u32[]{:S(2)}, u32[]{:S(2)}) collective-permute-start(bf16[4,12288]{1,0:T(4,128)(2,1)} %refs_0_), channel_id=1, source_target_pairs={{0,2},{1,3},{2,0},{3,1},{4,6},{5,7},{6,4},{7,5},{8,10},{9,11},{10,... | collective-permute-start | bytes 294920 | tf_op jit(solution)/shard_map/ppermute | solution.py:186
  4.5 2.6 %collective-permute-start = (bf16[4,12288]{1,0:T(4,128)(2,1)}, bf16[4,12288]{1,0:T(4,128)(2,1)S(1)}, u32[]{:S(2)}, u32[]{:S(2)}) collective-permute-start(bf16[4,12288]{1,0:T(4,128)(2,1)} %refs_0_), channel_id=1, source_target_pairs={{0,8},{1,9},{2,10},{3,11},{4,12},{5,13},{6,14},{7,15},{8,0},{9,1},... | collective-permute-start | bytes 294920 | tf_op jit(solution)/shard_map/ppermute | solution.py:183
  7.4 0.8 %copy.13 = s32[4,6]{0,1:T(8,128)S(1)} copy(s32[4,6]{1,0:T(4,128)} %param.15) | data formatting | bytes 192 | tf_op args[3]
  8.1 0.7 %fusion.1 = s32[4,6]{0,1:T(8,128)S(1)} fusion(s32[4]{0:T(128)} %param.16), kind=kLoop, calls=%fused_computation.12 | loop fusion | flops 48 | bytes 112 | tf_op jit(solution)/shard_map/convert_element_type | solution.py:150
  8.9 0.7 %fusion = s32[16,16]{1,0:T(8,128)S(1)} fusion(s32[16]{0:T(128)} %param.17), kind=kLoop, calls=%fused_computation.10 | loop fusion | flops 512 | bytes 1088 | tf_op jit(solution)/shard_map/convert_element_type | solution.py:153
  10.6 4.6 %collective-permute-done.refs_2_ = bf16[4,12288]{1,0:T(4,128)(2,1)S(1)} collective-permute-done((bf16[4,12288]{1,0:T(4,128)(2,1)}, bf16[4,12288]{1,0:T(4,128)(2,1)S(1)}, u32[]{:S(2)}, u32[]{:S(2)}) %collective-permute-start) | collective-permute-done | bytes 98336 | tf_op jit(solution)/shard_map/ppermute | solution.py:183
  15.9 0.7 %collective-permute-start.1 = (bf16[4,12288]{1,0:T(4,128)(2,1)S(1)}, bf16[4,12288]{1,0:T(4,128)(2,1)S(1)}, u32[]{:S(2)}, u32[]{:S(2)}) collective-permute-start(bf16[4,12288]{1,0:T(4,128)(2,1)S(1)} %collective-permute-done.refs_2_), channel_id=1, source_target_pairs={{0,2},{1,3},{2,0},{3,1},{4,6},{5,7},{6,4},{7,5},{8,10},{9,11},{10,... | collective-permute-start | bytes 294920 | tf_op jit(solution)/shard_map/ppermute | solution.py:186
  16.5 1.3 %collective-permute-start.3 = (bf16[4,12288]{1,0:T(4,128)(2,1)S(1)}, bf16[4,12288]{1,0:T(4,128)(2,1)S(1)}, u32[]{:S(2)}, u32[]{:S(2)}) collective-permute-start(bf16[4,12288]{1,0:T(4,128)(2,1)S(1)} %collective-permute-done.2.refs_3_), channel_id=1, source_target_pairs={{0,2},{1,3},{2,0},{3,1},{4,6},{5,7},{6,4},{7,5},{8,10},{9,11},{10,... | collective-permute-start | bytes 294920 | tf_op jit(solution)/shard_map/ppermute | solution.py:186
  17.9 3.4 %shard_map.118 = (bf16[4,12288]{1,0:T(4,128)(2,1)S(1)}, f32[1,12288]{1,0:T(1,128)S(1)}, f32[1,12288]{1,0:T(1,128)S(1)}, bf16[768,512]{1,0:T(8,128)(2,1)S(1)}, bf...) custom-call(bf16[4,12288]{1,0:T(4,128)(2,1)} %refs_0_, ...), custom_call_target="tpu_custom_call" | custom-call | bytes 8388608 | tf_op jit(solution)/shard_map/pallas_call | solution.py:212
  21.3 0.8 %shard_map.119 = (bf16[16,12288]{1,0:T(8,128)(2,1)S(1)}, bf16[8,12288]{1,0:T(8,128)(2,1)S(1)}) custom-call(bf16[4,12288]{1,0:T(4,128)(2,1)S(1)} %get-tuple-element.53.refs_0_, bf16[4,12288]{1,0:T(4,128)(2,1)S(1)} %collective-permute-done.4.refs_1_, bf16[4,12288]{1,0:T(4,128)(2,1)S(1)} %collective-permute-done.refs_2_, ...), custom_call_target="tpu_custom_call" | custom-call | bytes 4194304 | tf_op jit(solution)/shard_map/pallas_call | solution.py:228
  22.1 1.0 %collective-permute-done.3.refs_1_ = bf16[4,12288]{1,0:T(4,128)(2,1)S(1)} collective-permute-done((bf16[4,12288]{1,0:T(4,128)(2,1)S(1)}, bf16[4,12288]{1,0:T(4,128)(2,1)S(1)}, u32[]{:S(2)}, u32[]{:S(2)}) %collective-permute-start.3) | collective-permute-done | bytes 98336 | tf_op jit(solution)/shard_map/ppermute | solution.py:186
  23.1 0.8 %shard_map.120 = (bf16[16,12288]{1,0:T(8,128)(2,1)S(1)}, f32[32,512]{1,0:T(8,128)S(1)}, bf16[32,512]{1,0:T(8,128)(2,1)S(1)}) custom-call(s32[1]{0:T(128)} %bitcast.place, bf16[4,12288]{1,0:T(4,128)(2,1)S(1)} %collective-permute-done.1.refs_0_, bf16[4,12288]{1,0:T(4,128)(2,1)S(1)} %collective-permute-done.3.refs_1_, ...), custom_call_target="tpu_custom_call" | custom-call | bytes 4194304 | tf_op jit(solution)/shard_map/pallas_call | solution.py:236
  23.9 0.7 %collective-permute-start.8 = (bf16[32,512]{1,0:T(8,128)(2,1)S(1)}, bf16[32,512]{1,0:T(8,128)(2,1)S(1)}, u32[]{:S(2)}, u32[]{:S(2)}) collective-permute-start(bf16[32,512]{1,0:T(8,128)(2,1)S(1)} %get-tuple-element.63), channel_id=1, source_target_pairs={{0,2},{1,3},{2,0},{3,1},{4,6},{5,7},{6,4},{7,5},{8,10},{9,11},{10,... | collective-permute-start | bytes 98312 | tf_op jit(solution)/shard_map/ppermute | solution.py:186
  24.6 3.2 %collective-permute-done.8.got = bf16[32,512]{1,0:T(8,128)(2,1)S(1)} collective-permute-done((bf16[32,512]{1,0:T(8,128)(2,1)S(1)}, bf16[32,512]{1,0:T(8,128)(2,1)S(1)}, u32[]{:S(2)}, u32[]{:S(2)}) %collective-permute-start.8) | collective-permute-done | bytes 32800 | tf_op jit(solution)/shard_map/ppermute | solution.py:186
  27.9 2.0 %collective-permute-start.13 = (bf16[32,512]{1,0:T(8,128)(2,1)S(1)}, bf16[32,512]{1,0:T(8,128)(2,1)S(1)}, u32[]{:S(2)}, u32[]{:S(2)}) collective-permute-start(bf16[32,512]{1,0:T(8,128)(2,1)S(1)} %get-tuple-element.74), channel_id=1, source_target_pairs={{0,4},{1,5},{2,6},{3,7},{4,0},{5,1},{6,2},{7,3},{8,12},{9,13},{10,... | collective-permute-start | bytes 98312 | tf_op jit(solution)/shard_map/ppermute | solution.py:183
  29.9 1.9 %collective-permute-start.14 = (bf16[32,512]{1,0:T(8,128)(2,1)S(1)}, bf16[32,512]{1,0:T(8,128)(2,1)S(1)}, u32[]{:S(2)}, u32[]{:S(2)}) collective-permute-start(bf16[32,512]{1,0:T(8,128)(2,1)S(1)} %get-tuple-element.75), channel_id=1, source_target_pairs={{0,8},{1,9},{2,10},{3,11},{4,12},{5,13},{6,14},{7,15},{8,0},{9,1},... | collective-permute-start | bytes 98312 | tf_op jit(solution)/shard_map/ppermute | solution.py:183
  31.8 0.6 %collective-permute-start.15 = (bf16[32,512]{1,0:T(8,128)(2,1)S(1)}, bf16[32,512]{1,0:T(8,128)(2,1)S(1)}, u32[]{:S(2)}, u32[]{:S(2)}) collective-permute-start(bf16[32,512]{1,0:T(8,128)(2,1)S(1)} %get-tuple-element.76), channel_id=1, source_target_pairs={{0,12},{1,13},{2,14},{3,15},{4,8},{5,9},{6,10},{7,11},{8,4},{9,5},... | collective-permute-start | bytes 98312 | tf_op jit(solution)/shard_map/ppermute | solution.py:183
  32.3 1.2 %shard_map.122.act = bf16[32,256]{1,0:T(8,128)(2,1)S(1)} custom-call(bf16[16,12288]{1,0:T(8,128)(2,1)S(1)} %get-tuple-element.58.refs_2_.near, bf16[16,12288]{1,0:T(8,128)(2,1)S(1)} %get-tuple-element.67.far, bf16[12288,128]{1,0:T(8,128)(2,1)S(1)} %get-tuple-element.68.w_own, bf16[12288,128]{1,0:T(8,128)(2,1)S(1)} %collective-permute-done.9.w_mate, ...), custom_call_target="tpu_custom_call" | custom-call | bytes 4194304 | tf_op jit(solution)/shard_map/pallas_call | solution.py:246
  33.5 1.2 %shard_map.123.part = f32[32,12288]{1,0:T(8,128)S(1)} custom-call(bf16[32,256]{1,0:T(8,128)(2,1)S(1)} %shard_map.122.act, bf16[128,12288]{1,0:T(8,128)(2,1)S(1)} %get-tuple-element.72.w_own, bf16[128,12288]{1,0:T(8,128)(2,1)S(1)} %collective-permute-done.12.w_mate), custom_call_target="tpu_custom_call" | custom-call | bytes 6291456 | tf_op jit(solution)/shard_map/pallas_call | solution.py:261
  34.7 0.5 collective-permute-done.14.refs_1_
  35.3 2.2 %collective-permute-done.15.refs_2_ = bf16[32,512]{1,0:T(8,128)(2,1)S(1)} collective-permute-done((bf16[32,512]{1,0:T(8,128)(2,1)S(1)}, bf16[32,512]{1,0:T(8,128)(2,1)S(1)}, u32[]{:S(2)}, u32[]{:S(2)}) %collective-permute-start.15) | collective-permute-done | bytes 32800 | tf_op jit(solution)/shard_map/ppermute | solution.py:183
  37.9 0.6 %collective-permute-start.21 = (bf16[4,12288]{1,0:T(4,128)(2,1)S(1)}, bf16[4,12288]{1,0:T(4,128)(2,1)S(1)}, u32[]{:S(2)}, u32[]{:S(2)}) collective-permute-start(bf16[4,12288]{1,0:T(4,128)(2,1)S(1)} %get-tuple-element.84), channel_id=1, source_target_pairs={{0,2},{1,3},{2,0},{3,1},{4,6},{5,7},{6,4},{7,5},{8,10},{9,11},{10,... | collective-permute-start | bytes 294920 | tf_op jit(solution)/shard_map/ppermute | solution.py:186
  38.5 1.5 %collective-permute-start.19 = (bf16[4,12288]{1,0:T(4,128)(2,1)S(1)}, bf16[4,12288]{1,0:T(4,128)(2,1)S(1)}, u32[]{:S(2)}, u32[]{:S(2)}) collective-permute-start(bf16[4,12288]{1,0:T(4,128)(2,1)S(1)} %get-tuple-element.82), channel_id=1, source_target_pairs={{0,2},{1,3},{2,0},{3,1},{4,6},{5,7},{6,4},{7,5},{8,10},{9,11},{10,... | collective-permute-start | bytes 294920 | tf_op jit(solution)/shard_map/ppermute | solution.py:186
  40.5 1.5 %collective-permute-start.16 = (bf16[4,12288]{1,0:T(4,128)(2,1)S(1)}, bf16[4,12288]{1,0:T(4,128)(2,1)S(1)}, u32[]{:S(2)}, u32[]{:S(2)}) collective-permute-start(bf16[4,12288]{1,0:T(4,128)(2,1)S(1)} %get-tuple-element.78), channel_id=1, source_target_pairs={{0,2},{1,3},{2,0},{3,1},{4,6},{5,7},{6,4},{7,5},{8,10},{9,11},{10,... | collective-permute-start | bytes 294920 | tf_op jit(solution)/shard_map/ppermute | solution.py:186
  42.1 1.1 %collective-permute-done.21 = bf16[4,12288]{1,0:T(4,128)(2,1)S(1)} collective-permute-done((bf16[4,12288]{1,0:T(4,128)(2,1)S(1)}, bf16[4,12288]{1,0:T(4,128)(2,1)S(1)}, u32[]{:S(2)}, u32[]{:S(2)}) %collective-permute-start.21) | collective-permute-done | bytes 98336 | tf_op jit(solution)/shard_map/ppermute | solution.py:186
  43.2 1.1 %collective-permute-start.22 = (bf16[4,12288]{1,0:T(4,128)(2,1)S(1)}, bf16[4,12288]{1,0:T(4,128)(2,1)S(1)}, u32[]{:S(2)}, u32[]{:S(2)}) collective-permute-start(bf16[4,12288]{1,0:T(4,128)(2,1)S(1)} %add_convert_fusion), channel_id=1, source_target_pairs={{0,12},{1,13},{2,14},{3,15},{4,8},{5,9},{6,10},{7,11},{8,4},{9,5},... | collective-permute-start | bytes 294920 | tf_op jit(solution)/shard_map/ppermute | solution.py:183
  44.4 0.8 %collective-permute-done.17 = bf16[4,12288]{1,0:T(4,128)(2,1)S(1)} collective-permute-done((bf16[4,12288]{1,0:T(4,128)(2,1)S(1)}, bf16[4,12288]{1,0:T(4,128)(2,1)S(1)}, u32[]{:S(2)}, u32[]{:S(2)}) %collective-permute-start.17) | collective-permute-done | bytes 98336 | tf_op jit(solution)/shard_map/ppermute | solution.py:186
  45.3 2.6 %collective-permute-start.18 = (bf16[4,12288]{1,0:T(4,128)(2,1)S(1)}, bf16[4,12288]{1,0:T(4,128)(2,1)S(1)}, u32[]{:S(2)}, u32[]{:S(2)}) collective-permute-start(bf16[4,12288]{1,0:T(4,128)(2,1)S(1)} %add_convert_fusion.2), channel_id=1, source_target_pairs={{0,4},{1,5},{2,6},{3,7},{4,0},{5,1},{6,2},{7,3},{8,12},{9,13},{10,... | collective-permute-start | bytes 294920 | tf_op jit(solution)/shard_map/ppermute | solution.py:183
  47.9 1.8 %collective-permute-done.22.refs_3_ = bf16[4,12288]{1,0:T(4,128)(2,1)S(1)} collective-permute-done((bf16[4,12288]{1,0:T(4,128)(2,1)S(1)}, bf16[4,12288]{1,0:T(4,128)(2,1)S(1)}, u32[]{:S(2)}, u32[]{:S(2)}) %collective-permute-start.22) | collective-permute-done | bytes 98336 | tf_op jit(solution)/shard_map/ppermute | solution.py:183
  49.8 2.0 %collective-permute-done.20.refs_2_ = bf16[4,12288]{1,0:T(4,128)(2,1)S(1)} collective-permute-done((bf16[4,12288]{1,0:T(4,128)(2,1)S(1)}, bf16[4,12288]{1,0:T(4,128)(2,1)S(1)}, u32[]{:S(2)}, u32[]{:S(2)}) %collective-permute-start.20) | collective-permute-done | bytes 98336 | tf_op jit(solution)/shard_map/ppermute | solution.py:183
  51.8 0.7 %shard_map.125 = bf16[4,12288]{1,0:T(4,128)(2,1)} custom-call(f32[4,12288]{1,0:T(4,128)S(1)} %convert_add_fusion.refs_0_, bf16[4,12288]{1,0:T(4,128)(2,1)S(1)} %collective-permute-done.18.refs_1_, bf16[4,12288]{1,0:T(4,128)(2,1)S(1)} %collective-permute-done.20.refs_2_, bf16[4,12288]{1,0:T(4,128)(2,1)S(1)} %collective-permute-done.22.refs_3_), custom_call_target="tpu_custom_call" | custom-call | bytes 2097152 | tf_op jit(solution)/shard_map/pallas_call | solution.py:282
  (43 shorter events, 3.7 us)
Async XLA Ops:
  0.0 15.2 %collective-permute-start.9 = (bf16[12288,128]{1,0:T(8,128)(2,1)}, bf16[12288,128]{1,0:T(8,128)(2,1)S(1)}, u32[]{:S(2)}, u32[]{:S(2)}) collective-permute-start(bf16[12288,128]{1,0:T(8,128)(2,1)} %refs_4_), channel_id=1, source_target_pairs={{0,1},{1,0},{2,3},{3,2},{4,5},{5,4},{6,7},{7,6},{8,9},{9,8},{10,11... | collective-permute-start | bytes 9437192 | tf_op jit(solution)/shard_map/ppermute | solution.py:189
  0.5 9.8 %collective-permute-start.4 = (bf16[4,12288]{1,0:T(4,128)(2,1)}, bf16[4,12288]{1,0:T(4,128)(2,1)S(1)}, u32[]{:S(2)}, u32[]{:S(2)}) collective-permute-start(bf16[4,12288]{1,0:T(4,128)(2,1)} %refs_0_), channel_id=1, source_target_pairs={{0,4},{1,5},{2,6},{3,7},{4,0},{5,1},{6,2},{7,3},{8,12},{9,13},{10,... | collective-permute-start | bytes 294920 | tf_op jit(solution)/shard_map/ppermute | solution.py:183
  3.0 7.6 %collective-permute-start.5 = (bf16[4,12288]{1,0:T(4,128)(2,1)}, bf16[4,12288]{1,0:T(4,128)(2,1)S(1)}, u32[]{:S(2)}, u32[]{:S(2)}) collective-permute-start(bf16[4,12288]{1,0:T(4,128)(2,1)} %refs_0_), channel_id=1, source_target_pairs={{0,2},{1,3},{2,0},{3,1},{4,6},{5,7},{6,4},{7,5},{8,10},{9,11},{10,... | collective-permute-start | bytes 294920 | tf_op jit(solution)/shard_map/ppermute | solution.py:186
  4.5 10.6 %collective-permute-start = (bf16[4,12288]{1,0:T(4,128)(2,1)}, bf16[4,12288]{1,0:T(4,128)(2,1)S(1)}, u32[]{:S(2)}, u32[]{:S(2)}) collective-permute-start(bf16[4,12288]{1,0:T(4,128)(2,1)} %refs_0_), channel_id=1, source_target_pairs={{0,8},{1,9},{2,10},{3,11},{4,12},{5,13},{6,14},{7,15},{8,0},{9,1},... | collective-permute-start | bytes 294920 | tf_op jit(solution)/shard_map/ppermute | solution.py:183
  7.1 8.0 %collective-permute-start.2 = (bf16[4,12288]{1,0:T(4,128)(2,1)}, bf16[4,12288]{1,0:T(4,128)(2,1)S(1)}, u32[]{:S(2)}, u32[]{:S(2)}) collective-permute-start(bf16[4,12288]{1,0:T(4,128)(2,1)} %refs_0_), channel_id=1, source_target_pairs={{0,12},{1,13},{2,14},{3,15},{4,8},{5,9},{6,10},{7,11},{8,4},{9,5},... | collective-permute-start | bytes 294920 | tf_op jit(solution)/shard_map/ppermute | solution.py:183
  10.3 4.9 %collective-permute-start.6 = (bf16[4,12288]{1,0:T(4,128)(2,1)S(1)}, bf16[4,12288]{1,0:T(4,128)(2,1)S(1)}, u32[]{:S(2)}, u32[]{:S(2)}) collective-permute-start(bf16[4,12288]{1,0:T(4,128)(2,1)S(1)} %collective-permute-done.4.refs_1_), channel_id=1, source_target_pairs={{0,2},{1,3},{2,0},{3,1},{4,6},{5,7},{6,4},{7,5},{8,10},{9,11},{10,... | collective-permute-start | bytes 294920 | tf_op jit(solution)/shard_map/ppermute | solution.py:186
  15.2 18.3 %collective-permute-start.12 = (bf16[128,12288]{1,0:T(8,128)(2,1)}, bf16[128,12288]{1,0:T(8,128)(2,1)S(1)}, u32[]{:S(2)}, u32[]{:S(2)}) collective-permute-start(bf16[128,12288]{1,0:T(8,128)(2,1)} %refs_5_), channel_id=1, source_target_pairs={{0,1},{1,0},{2,3},{3,2},{4,5},{5,4},{6,7},{7,6},{8,9},{9,8},{10,11... | collective-permute-start | bytes 9437192 | tf_op jit(solution)/shard_map/ppermute | solution.py:189
  15.3 7.8 %collective-permute-start.7 = (bf16[768,512]{1,0:T(8,128)(2,1)}, bf16[768,512]{1,0:T(8,128)(2,1)S(1)}, u32[]{:S(2)}, u32[]{:S(2)}) collective-permute-start(bf16[768,512]{1,0:T(8,128)(2,1)} %refs_3_), channel_id=1, source_target_pairs={{0,1},{1,0},{2,3},{3,2},{4,5},{5,4},{6,7},{7,6},{8,9},{9,8},{10,11... | collective-permute-start | bytes 2359304 | tf_op jit(solution)/shard_map/ppermute | solution.py:189
  15.8 21.7 %collective-permute-start.10 = (bf16[512,768]{1,0:T(8,128)(2,1)}, bf16[512,768]{1,0:T(8,128)(2,1)S(1)}, u32[]{:S(2)}, u32[]{:S(2)}) collective-permute-start(bf16[512,768]{1,0:T(8,128)(2,1)} %refs_6_), channel_id=1, source_target_pairs={{0,1},{1,0},{2,3},{3,2},{4,5},{5,4},{6,7},{7,6},{8,9},{9,8},{10,11... | collective-permute-start | bytes 2359304 | tf_op jit(solution)/shard_map/ppermute | solution.py:189
  15.9 6.3 %collective-permute-start.1 = (bf16[4,12288]{1,0:T(4,128)(2,1)S(1)}, bf16[4,12288]{1,0:T(4,128)(2,1)S(1)}, u32[]{:S(2)}, u32[]{:S(2)}) collective-permute-start(bf16[4,12288]{1,0:T(4,128)(2,1)S(1)} %collective-permute-done.refs_2_), channel_id=1, source_target_pairs={{0,2},{1,3},{2,0},{3,1},{4,6},{5,7},{6,4},{7,5},{8,10},{9,11},{10,... | collective-permute-start | bytes 294920 | tf_op jit(solution)/shard_map/ppermute | solution.py:186
  16.5 6.6 %collective-permute-start.3 = (bf16[4,12288]{1,0:T(4,128)(2,1)S(1)}, bf16[4,12288]{1,0:T(4,128)(2,1)S(1)}, u32[]{:S(2)}, u32[]{:S(2)}) collective-permute-start(bf16[4,12288]{1,0:T(4,128)(2,1)S(1)} %collective-permute-done.2.refs_3_), channel_id=1, source_target_pairs={{0,2},{1,3},{2,0},{3,1},{4,6},{5,7},{6,4},{7,5},{8,10},{9,11},{10,... | collective-permute-start | bytes 294920 | tf_op jit(solution)/shard_map/ppermute | solution.py:186
  21.3 3.3 %copy-start.1 = (f32[128]{0:T(128)S(1)}, f32[128]{0:T(128)}, u32[]{:S(2)}) copy-start(f32[128]{0:T(128)} %param.19) | copy-start | bytes 1540
  23.9 3.9 %collective-permute-start.8 = (bf16[32,512]{1,0:T(8,128)(2,1)S(1)}, bf16[32,512]{1,0:T(8,128)(2,1)S(1)}, u32[]{:S(2)}, u32[]{:S(2)}) collective-permute-start(bf16[32,512]{1,0:T(8,128)(2,1)S(1)} %get-tuple-element.63), channel_id=1, source_target_pairs={{0,2},{1,3},{2,0},{3,1},{4,6},{5,7},{6,4},{7,5},{8,10},{9,11},{10,... | collective-permute-start | bytes 98312 | tf_op jit(solution)/shard_map/ppermute | solution.py:186
  24.6 7.2 %collective-permute-start.11 = (f32[1,128]{1,0:T(1,128)S(1)}, f32[1,128]{1,0:T(1,128)S(1)}, u32[]{:S(2)}, u32[]{:S(2)}) collective-permute-start(f32[1,128]{1,0:T(1,128)S(1)} %bitcast.12), channel_id=1, source_target_pairs={{0,1},{1,0},{2,3},{3,2},{4,5},{5,4},{6,7},{7,6},{8,9},{9,8},{10,11... | collective-permute-start | bytes 1544 | tf_op jit(solution)/shard_map/ppermute | solution.py:189
  27.9 6.9 %collective-permute-start.13 = (bf16[32,512]{1,0:T(8,128)(2,1)S(1)}, bf16[32,512]{1,0:T(8,128)(2,1)S(1)}, u32[]{:S(2)}, u32[]{:S(2)}) collective-permute-start(bf16[32,512]{1,0:T(8,128)(2,1)S(1)} %get-tuple-element.74), channel_id=1, source_target_pairs={{0,4},{1,5},{2,6},{3,7},{4,0},{5,1},{6,2},{7,3},{8,12},{9,13},{10,... | collective-permute-start | bytes 98312 | tf_op jit(solution)/shard_map/ppermute | solution.py:183
  29.9 5.4 %collective-permute-start.14 = (bf16[32,512]{1,0:T(8,128)(2,1)S(1)}, bf16[32,512]{1,0:T(8,128)(2,1)S(1)}, u32[]{:S(2)}, u32[]{:S(2)}) collective-permute-start(bf16[32,512]{1,0:T(8,128)(2,1)S(1)} %get-tuple-element.75), channel_id=1, source_target_pairs={{0,8},{1,9},{2,10},{3,11},{4,12},{5,13},{6,14},{7,15},{8,0},{9,1},... | collective-permute-start | bytes 98312 | tf_op jit(solution)/shard_map/ppermute | solution.py:183
  31.8 5.7 %collective-permute-start.15 = (bf16[32,512]{1,0:T(8,128)(2,1)S(1)}, bf16[32,512]{1,0:T(8,128)(2,1)S(1)}, u32[]{:S(2)}, u32[]{:S(2)}) collective-permute-start(bf16[32,512]{1,0:T(8,128)(2,1)S(1)} %get-tuple-element.76), channel_id=1, source_target_pairs={{0,12},{1,13},{2,14},{3,15},{4,8},{5,9},{6,10},{7,11},{8,4},{9,5},... | collective-permute-start | bytes 98312 | tf_op jit(solution)/shard_map/ppermute | solution.py:183
  33.5 3.9 %copy-start = (f32[512]{0:T(512)S(1)}, f32[512]{0:T(512)}, u32[]{:S(2)}) copy-start(f32[512]{0:T(512)} %param.22) | copy-start | bytes 6148
  37.9 5.2 %collective-permute-start.21 = (bf16[4,12288]{1,0:T(4,128)(2,1)S(1)}, bf16[4,12288]{1,0:T(4,128)(2,1)S(1)}, u32[]{:S(2)}, u32[]{:S(2)}) collective-permute-start(bf16[4,12288]{1,0:T(4,128)(2,1)S(1)} %get-tuple-element.84), channel_id=1, source_target_pairs={{0,2},{1,3},{2,0},{3,1},{4,6},{5,7},{6,4},{7,5},{8,10},{9,11},{10,... | collective-permute-start | bytes 294920 | tf_op jit(solution)/shard_map/ppermute | solution.py:186
  38.5 5.8 %collective-permute-start.19 = (bf16[4,12288]{1,0:T(4,128)(2,1)S(1)}, bf16[4,12288]{1,0:T(4,128)(2,1)S(1)}, u32[]{:S(2)}, u32[]{:S(2)}) collective-permute-start(bf16[4,12288]{1,0:T(4,128)(2,1)S(1)} %get-tuple-element.82), channel_id=1, source_target_pairs={{0,2},{1,3},{2,0},{3,1},{4,6},{5,7},{6,4},{7,5},{8,10},{9,11},{10,... | collective-permute-start | bytes 294920 | tf_op jit(solution)/shard_map/ppermute | solution.py:186
  40.0 5.2 %collective-permute-start.17 = (bf16[4,12288]{1,0:T(4,128)(2,1)S(1)}, bf16[4,12288]{1,0:T(4,128)(2,1)S(1)}, u32[]{:S(2)}, u32[]{:S(2)}) collective-permute-start(bf16[4,12288]{1,0:T(4,128)(2,1)S(1)} %get-tuple-element.80), channel_id=1, source_target_pairs={{0,2},{1,3},{2,0},{3,1},{4,6},{5,7},{6,4},{7,5},{8,10},{9,11},{10,... | collective-permute-start | bytes 294920 | tf_op jit(solution)/shard_map/ppermute | solution.py:186
  40.5 7.4 %collective-permute-start.16 = (bf16[4,12288]{1,0:T(4,128)(2,1)S(1)}, bf16[4,12288]{1,0:T(4,128)(2,1)S(1)}, u32[]{:S(2)}, u32[]{:S(2)}) collective-permute-start(bf16[4,12288]{1,0:T(4,128)(2,1)S(1)} %get-tuple-element.78), channel_id=1, source_target_pairs={{0,2},{1,3},{2,0},{3,1},{4,6},{5,7},{6,4},{7,5},{8,10},{9,11},{10,... | collective-permute-start | bytes 294920 | tf_op jit(solution)/shard_map/ppermute | solution.py:186
  43.2 6.6 %collective-permute-start.22 = (bf16[4,12288]{1,0:T(4,128)(2,1)S(1)}, bf16[4,12288]{1,0:T(4,128)(2,1)S(1)}, u32[]{:S(2)}, u32[]{:S(2)}) collective-permute-start(bf16[4,12288]{1,0:T(4,128)(2,1)S(1)} %add_convert_fusion), channel_id=1, source_target_pairs={{0,12},{1,13},{2,14},{3,15},{4,8},{5,9},{6,10},{7,11},{8,4},{9,5},... | collective-permute-start | bytes 294920 | tf_op jit(solution)/shard_map/ppermute | solution.py:183
  44.4 7.4 %collective-permute-start.20 = (bf16[4,12288]{1,0:T(4,128)(2,1)S(1)}, bf16[4,12288]{1,0:T(4,128)(2,1)S(1)}, u32[]{:S(2)}, u32[]{:S(2)}) collective-permute-start(bf16[4,12288]{1,0:T(4,128)(2,1)S(1)} %add_convert_fusion.1), channel_id=1, source_target_pairs={{0,8},{1,9},{2,10},{3,11},{4,12},{5,13},{6,14},{7,15},{8,0},{9,1},... | collective-permute-start | bytes 294920 | tf_op jit(solution)/shard_map/ppermute | solution.py:183
  45.3 6.5 %collective-permute-start.18 = (bf16[4,12288]{1,0:T(4,128)(2,1)S(1)}, bf16[4,12288]{1,0:T(4,128)(2,1)S(1)}, u32[]{:S(2)}, u32[]{:S(2)}) collective-permute-start(bf16[4,12288]{1,0:T(4,128)(2,1)S(1)} %add_convert_fusion.2), channel_id=1, source_target_pairs={{0,4},{1,5},{2,6},{3,7},{4,0},{5,1},{6,2},{7,3},{8,12},{9,13},{10,... | collective-permute-start | bytes 294920 | tf_op jit(solution)/shard_map/ppermute | solution.py:183

commit v8 on v7

--- a/solution.py
+++ b/solution.py
@@ -45,6 +45,13 @@
     return (centred * lax.rsqrt(variance + 1e-05) * gain + shift).astype(bf16)
 
 
+def normalise(held, gain, shift, out):
+    rows = held[0].shape[0]
+    for i in range(0, len(held), 2):
+        pair = jnp.concatenate([h[...] for h in held[i : i + 2]], axis=0)
+        out[i * rows : (i + 2) * rows, :] = normal(pair, gain[...], shift[...])
+
+
 def load_body(count, *refs):
     srcs, dsts, sems = refs[:count], refs[count : 2 * count], refs[2 * count]
     copies = [pltpu.make_async_copy(srcs[i], dsts[i], sems.at[i]) for i in range(count)]
@@ -54,33 +61,30 @@
         copy.wait()
 
 
-def early_body(groups, soon, *refs):
-    held, (gain, shift, near, far) = refs[: groups + soon], refs[groups + soon :]
-    rows = held[0].shape[0]
-    for out, some in ((near, held[:groups]), (far, held[groups:])):
-        for i in range(0, len(some), 2):
-            pair = jnp.concatenate([h[...] for h in some[i : i + 2]], axis=0)
-            out[i * rows : i * rows + pair.shape[0], :] = normal(pair, gain[...], shift[...])
-
-
-def norm_body(count, place, *refs):
-    held, (near, first, gain, shift, own, mate, far, total, message) = refs[:count], refs[count:]
-    rows, done = held[0].shape[0], first.shape[0]
-    far[:done, :] = first[...]
-    for i in range(0, count, 2):
-        pair = jnp.concatenate([h[...] for h in held[i : i + 2]], axis=0)
-        far[done + i * rows : done + i * rows + pair.shape[0], :] = normal(pair, gain[...], shift[...])
+def near_body(groups, place, *refs):
+    held, (gain, shift, near, keep, send) = refs[:groups], refs[groups:]
+    normalise(held, gain, shift, near)
+    span = keep.shape[1]
+    chip = place[0] // 2
+    keep[...] = near[:, window(chip, span)]
+    send[...] = near[:, window(chip ^ 1, span)]
+
+
+def far_body(groups, *refs):
+    normalise(refs[:groups], *refs[groups:])
+
+
+def down_body(place, keep, got, own, mate, total, message):
     share = own.shape[0]
     core = place[0] % 2
-    at = window(place[0] // 2, 2 * share)
-    columns = jnp.concatenate([near[:, at].astype(f32), far[:, at].astype(f32)], axis=0)
+    columns = jnp.concatenate([keep[...].astype(f32), got[...].astype(f32)], axis=0)
     low, high = columns[:, :share], columns[:, share:]
     mine = jnp.where(core == 0, low, high).astype(bf16)
     other = jnp.where(core == 0, high, low).astype(bf16)
     sums = jnp.dot(mine, own[...], preferred_element_type=f32) + jnp.dot(
         other, mate[...], preferred_element_type=f32
     )
-    half = near.shape[0]
+    half = keep.shape[0]
     total[...] = sums
     message[:half, :] = sums[half:].astype(bf16)
     message[half:, :] = sums[:half].astype(bf16)
@@ -204,11 +208,8 @@
 
     held = [hidden] + [across(hidden, k) for k in range(1, groups)]
     w_in_mate = core(w_in)
-    held[1], low_in_sent, mask = lax.optimization_barrier((held[1], low_in, mask))
-    low_in_mate = core(low_in_sent)
-    beyond = [beside(h) for h in held]
     near = (hidden, gain, shift, low_in, w_in, w_out, low_out)
-    *near, mask, beyond[0] = lax.optimization_barrier((*near, mask, beyond[0]))
+    *near, mask = lax.optimization_barrier((*near, mask))
     near = call(
         functools.partial(load_body, len(near)),
         [shape(*x.shape, dtype=x.dtype) for x in near],
@@ -217,30 +218,33 @@
         [pltpu.SemaphoreType.DMA((len(near),))],
         8 * MIB,
     )(*[pltpu.with_memory_space_constraint(x, pltpu.HBM) for x in near])
-    hidden_near, gain, shift, low_in, w_in, w_out_near, low_out_near = near
-    *_, w_in_mate, w_out_sent, low_out_sent, bias_sent = lax.optimization_barrier(
-        (*held, *beyond[: groups // 2], w_in_mate, w_out, low_out, bias)
+    held[1], *near = lax.optimization_barrier((held[1], *near))
+    hidden_near, gain, shift, low_in_near, w_in, w_out_near, low_out_near = near
+    soon = groups // 2
+    beyond = [beside(h) for h in held[:soon]]
+    *_, w_in_mate, low_in_sent, w_out_sent, low_out_sent, bias_sent = lax.optimization_barrier(
+        (*held, *beyond, w_in_mate, low_in, w_out, low_out, bias)
     )
-    bias_mate, w_out_mate, low_out_mate = core(bias_sent), core(w_out_sent), core(low_out_sent)
-    held[0] = hidden_near
-
-    soon = groups // 2
-    normed, first = call(
-        functools.partial(early_body, groups, soon),
-        [shape(some, width), shape(soon * row_dev, width)],
-        [VMEM] * (groups + soon + 2),
+    low_in_mate, bias_mate, w_out_mate, low_out_mate = map(core, (low_in_sent, bias_sent, w_out_sent, low_out_sent))
+
+    hidden_near, *beyond = lax.optimization_barrier((hidden_near, *beyond))
+    normed, keep, send = call(
+        functools.partial(near_body, groups),
+        [shape(some, width), shape(some, span), shape(some, span)],
+        [SMEM] + [VMEM] * (groups + 2),
         16,
         (),
         4 * MIB,
-    )(*held, *beyond[:soon], gain, shift)
-    far, total, message = call(
-        functools.partial(norm_body, groups - soon),
-        [shape(some, width), shape(rows, rank, dtype=f32), shape(rows, rank)],
-        [SMEM] + [VMEM] * (groups - soon + 6),
-        16,
-        (),
-        4 * MIB,
-    )(place, *beyond[soon:], normed, first, gain, shift, low_in, low_in_mate)
+    )(place, hidden_near, *held[1:], gain, shift)
+    send, *late = lax.optimization_barrier((send, *held[soon:]))
+    got = beside(send)
+    beyond = beyond + [beside(h) for h in late]
+    total, message = call(
+        down_body, [shape(rows, rank, dtype=f32), shape(rows, rank)], [SMEM] + [VMEM] * 4, 16
+    )(place, keep, got, low_in_near, low_in_mate)
+    far = call(
+        functools.partial(far_body, groups), [shape(some, width)], [VMEM] * (groups + 2), 16, (), 4 * MIB
+    )(*beyond, gain, shift)[0]
     got = beside(message)
     step = piece(width, 2048)
     act = call(

time: 52.6 us -> 57.6 us (1.095)
  waiting for transfers between devices: 17.2 us -> 23 us
  starting transfers between devices: 23.5 us -> 22.5 us
    ppermute x9 -> x10, waiting for transfers between devices: 6.09 us -> 15.2 us  [beside(): return lax.ppermute(x, 'blk', [(i, i ^ 2) for i in range(devices)])]
    ppermute x9, waiting for transfers between devices: 11.1 us -> 6.77 us  [across(): return lax.ppermute(x, 'blk', [(i, i ^ 4 * k) for i in range(devices)])]
    ppermute x9, starting transfers between devices: 13.6 us -> 12.4 us  [across(): return lax.ppermute(x, 'blk', [(i, i ^ 4 * k) for i in range(devices)])]
    ppermute x5, waiting for transfers between devices: 0.01 us -> 0.98 us  [core(): return lax.ppermute(x, 'blk', [(i, i ^ 1) for i in range(devices)])]
    ppermute x9 -> x10, starting transfers between devices: 8.72 us -> 9.15 us  [beside(): return lax.ppermute(x, 'blk', [(i, i ^ 2) for i in range(devices)])]
    pallas_call x2 -> x3, Pallas kernels: 1.62 us -> 1.55 us  [the longest x1 0.6 us: shards(): call(functools.partial(near_body, groups), [shape(some, width), shape(som...]
  transfers between devices with their start and end apart: 23 -> 24, of which waited for: 9 -> 9; matrix products, arithmetic and copies ran while one was open for 6% -> 5% of each run, Pallas kernels for 14% -> 13%
where the time goes in v8:
time: 57.6 us; the launch traced here: 57.4 us
  waiting for transfers between devices  23 us (40%)
  starting transfers between devices  22.5 us (39%)
  Pallas kernels  8.61 us (15%)
  other arithmetic  2.25 us (4%)
  local copies, waits for them, and re-layouts  0.88 us (2%)
    ppermute x10, waiting for transfers between devices, beside(): return lax.ppermute(x, 'blk', [(i, i ^ 2) for i in range(devices)])  15.2 us
    ppermute x9, starting transfers between devices, across(): return lax.ppermute(x, 'blk', [(i, i ^ 4 * k) for i in range(devices)])  12.4 us
    ppermute x10, starting transfers between devices, beside(): return lax.ppermute(x, 'blk', [(i, i ^ 2) for i in range(devices)])  9.15 us
    ppermute x9, waiting for transfers between devices, across(): return lax.ppermute(x, 'blk', [(i, i ^ 4 * k) for i in range(devices)])  6.77 us
    pallas_call x1, Pallas kernels, shards(): call(functools.partial(load_body, len(near)), [shape(*x.shape, dtype=x.dt...  3.52 us
    pallas_call x1, Pallas kernels, shards(): call(functools.partial(part_body, step), [shape(rows, width, dtype=f32)],...  1.19 us
    pallas_call x1, Pallas kernels, shards(): call(functools.partial(act_body, step), [shape(rows, 2 * block)], [VMEM]...  1.18 us
  transfers between devices with their start and end apart: 24, of which 9 were waited for; matrix products, arithmetic and copies ran while one was open for 5% of the time, Pallas kernels for 13%

profile of v8, /device:TPU:0, one launch (start us, length us, event | category | flops | bytes accessed | tf_op | source)
XLA Modules:
  0.0 57.4 jit_solution(10720235745235415952)
XLA Ops:
  0.5 3.6 %collective-permute-start.3 = (bf16[4,12288]{1,0:T(4,128)(2,1)}, bf16[4,12288]{1,0:T(4,128)(2,1)S(1)}, u32[]{:S(2)}, u32[]{:S(2)}) collective-permute-start(bf16[4,12288]{1,0:T(4,128)(2,1)} %refs_0_), channel_id=1, source_target_pairs={{0,8},{1,9},{2,10},{3,11},{4,12},{5,13},{6,14},{7,15},{8,0},{9,1},... | collective-permute-start | bytes 294920 | tf_op jit(solution)/shard_map/ppermute | solution.py:187
  4.0 1.5 %collective-permute-start.1 = (bf16[4,12288]{1,0:T(4,128)(2,1)}, bf16[4,12288]{1,0:T(4,128)(2,1)S(1)}, u32[]{:S(2)}, u32[]{:S(2)}) collective-permute-start(bf16[4,12288]{1,0:T(4,128)(2,1)} %refs_0_), channel_id=1, source_target_pairs={{0,2},{1,3},{2,0},{3,1},{4,6},{5,7},{6,4},{7,5},{8,10},{9,11},{10,... | collective-permute-start | bytes 294920 | tf_op jit(solution)/shard_map/ppermute | solution.py:190
  5.6 1.6 %collective-permute-start = (bf16[4,12288]{1,0:T(4,128)(2,1)}, bf16[4,12288]{1,0:T(4,128)(2,1)S(1)}, u32[]{:S(2)}, u32[]{:S(2)}) collective-permute-start(bf16[4,12288]{1,0:T(4,128)(2,1)} %refs_0_), channel_id=1, source_target_pairs={{0,4},{1,5},{2,6},{3,7},{4,0},{5,1},{6,2},{7,3},{8,12},{9,13},{10,... | collective-permute-start | bytes 294920 | tf_op jit(solution)/shard_map/ppermute | solution.py:187
  7.4 0.8 %copy.13 = s32[4,6]{0,1:T(8,128)S(1)} copy(s32[4,6]{1,0:T(4,128)} %param.15) | data formatting | bytes 192 | tf_op args[3]
  8.1 0.7 %fusion.1 = s32[4,6]{0,1:T(8,128)S(1)} fusion(s32[4]{0:T(128)} %param.16), kind=kLoop, calls=%fused_computation.12 | loop fusion | flops 48 | bytes 112 | tf_op jit(solution)/shard_map/convert_element_type | solution.py:154
  8.9 0.7 %fusion = s32[16,16]{1,0:T(8,128)S(1)} fusion(s32[16]{0:T(128)} %param.17), kind=kLoop, calls=%fused_computation.10 | loop fusion | flops 512 | bytes 1088 | tf_op jit(solution)/shard_map/convert_element_type | solution.py:157
  10.3 3.5 %shard_map.118 = (bf16[4,12288]{1,0:T(4,128)(2,1)S(1)}, f32[1,12288]{1,0:T(1,128)S(1)}, f32[1,12288]{1,0:T(1,128)S(1)}, bf16[768,512]{1,0:T(8,128)(2,1)S(1)}, bf...) custom-call(bf16[4,12288]{1,0:T(4,128)(2,1)} %refs_0_, ...), custom_call_target="tpu_custom_call" | custom-call | bytes 8388608 | tf_op jit(solution)/shard_map/pallas_call | solution.py:213
  14.2 4.3 %collective-permute-done.2.refs_1_ = bf16[4,12288]{1,0:T(4,128)(2,1)S(1)} collective-permute-done((bf16[4,12288]{1,0:T(4,128)(2,1)S(1)}, bf16[4,12288]{1,0:T(4,128)(2,1)S(1)}, u32[]{:S(2)}, u32[]{:S(2)}) %collective-permute-start.2) | collective-permute-done | bytes 98336 | tf_op jit(solution)/shard_map/ppermute | solution.py:190
  18.5 0.5 collective-permute-start.7
  19.1 0.6 %shard_map.119 = (bf16[16,12288]{1,0:T(8,128)(2,1)S(1)}, bf16[16,1536]{1,0:T(8,128)(2,1)S(1)}, bf16[16,1536]{1,0:T(8,128)(2,1)S(1)}) custom-call(s32[1]{0:T(128)} %bitcast.place, bf16[4,12288]{1,0:T(4,128)(2,1)S(1)} %get-tuple-element.72.refs_0_, bf16[4,12288]{1,0:T(4,128)(2,1)S(1)} %collective-permute-done.refs_1_, ...), custom_call_target="tpu_custom_call" | custom-call | bytes 4194304 | tf_op jit(solution)/shard_map/pallas_call | solution.py:231
  20.1 1.7 %collective-permute-start.10 = (bf16[4,12288]{1,0:T(4,128)(2,1)S(1)}, bf16[4,12288]{1,0:T(4,128)(2,1)S(1)}, u32[]{:S(2)}, u32[]{:S(2)}) collective-permute-start(bf16[4,12288]{1,0:T(4,128)(2,1)S(1)} %collective-permute-done.3.refs_2_), channel_id=1, source_target_pairs={{0,2},{1,3},{2,0},{3,1},{4,6},{5,7},{6,4},{7,5},{8,10},{9,11},{10,... | collective-permute-start | bytes 294920 | tf_op jit(solution)/shard_map/ppermute | solution.py:190
  21.8 2.5 %collective-permute-done.5.got = bf16[16,1536]{1,0:T(8,128)(2,1)S(1)} collective-permute-done((bf16[16,1536]{1,0:T(8,128)(2,1)S(1)}, bf16[16,1536]{1,0:T(8,128)(2,1)S(1)}, u32[]{:S(2)}, u32[]{:S(2)}) %collective-permute-start.5) | collective-permute-done | bytes 49184 | tf_op jit(solution)/shard_map/ppermute | solution.py:190
  24.3 1.0 %collective-permute-done.7.mate = bf16[768,512]{1,0:T(8,128)(2,1)S(1)} collective-permute-done((bf16[768,512]{1,0:T(8,128)(2,1)S(1)}, bf16[768,512]{1,0:T(8,128)(2,1)S(1)}, u32[]{:S(2)}, u32[]{:S(2)}) %collective-permute-start.7) | collective-permute-done | bytes 786464 | tf_op jit(solution)/shard_map/ppermute | solution.py:193
  25.7 1.1 %collective-permute-start.8 = (bf16[32,512]{1,0:T(8,128)(2,1)S(1)}, bf16[32,512]{1,0:T(8,128)(2,1)S(1)}, u32[]{:S(2)}, u32[]{:S(2)}) collective-permute-start(bf16[32,512]{1,0:T(8,128)(2,1)S(1)} %get-tuple-element.81), channel_id=1, source_target_pairs={{0,2},{1,3},{2,0},{3,1},{4,6},{5,7},{6,4},{7,5},{8,10},{9,11},{10,... | collective-permute-start | bytes 98312 | tf_op jit(solution)/shard_map/ppermute | solution.py:190
  26.7 2.9 %collective-permute-done.8.got = bf16[32,512]{1,0:T(8,128)(2,1)S(1)} collective-permute-done((bf16[32,512]{1,0:T(8,128)(2,1)S(1)}, bf16[32,512]{1,0:T(8,128)(2,1)S(1)}, u32[]{:S(2)}, u32[]{:S(2)}) %collective-permute-start.8) | collective-permute-done | bytes 32800 | tf_op jit(solution)/shard_map/ppermute | solution.py:190
  29.7 0.7 %collective-permute-start.14 = (bf16[32,512]{1,0:T(8,128)(2,1)S(1)}, bf16[32,512]{1,0:T(8,128)(2,1)S(1)}, u32[]{:S(2)}, u32[]{:S(2)}) collective-permute-start(bf16[32,512]{1,0:T(8,128)(2,1)S(1)} %get-tuple-element.96), channel_id=1, source_target_pairs={{0,4},{1,5},{2,6},{3,7},{4,0},{5,1},{6,2},{7,3},{8,12},{9,13},{10,... | collective-permute-start | bytes 98312 | tf_op jit(solution)/shard_map/ppermute | solution.py:187
  30.4 3.5 %collective-permute-start.15 = (bf16[32,512]{1,0:T(8,128)(2,1)S(1)}, bf16[32,512]{1,0:T(8,128)(2,1)S(1)}, u32[]{:S(2)}, u32[]{:S(2)}) collective-permute-start(bf16[32,512]{1,0:T(8,128)(2,1)S(1)} %get-tuple-element.97), channel_id=1, source_target_pairs={{0,8},{1,9},{2,10},{3,11},{4,12},{5,13},{6,14},{7,15},{8,0},{9,1},... | collective-permute-start | bytes 98312 | tf_op jit(solution)/shard_map/ppermute | solution.py:187
  33.9 0.5 collective-permute-start.16
  34.4 0.6 %shard_map.122.far = bf16[16,12288]{1,0:T(8,128)(2,1)S(1)} custom-call(bf16[4,12288]{1,0:T(4,128)(2,1)S(1)} %collective-permute-done.1.refs_0_, bf16[4,12288]{1,0:T(4,128)(2,1)S(1)} %collective-permute-done.2.refs_1_, bf16[4,12288]{1,0:T(4,128)(2,1)S(1)} %collective-permute-done.10.refs_2_, bf16[4,12288]{1,0:T(4,128)(2,1)S(1)} %collective-permute-done.11.refs_3_, ...), custom_call_target="tpu_custom_call" | custom-call | bytes 4194304 | tf_op jit(solution)/shard_map/pallas_call | solution.py:245
  35.0 1.2 %shard_map.123.act = bf16[32,256]{1,0:T(8,128)(2,1)S(1)} custom-call(bf16[16,12288]{1,0:T(8,128)(2,1)S(1)} %get-tuple-element.85.near, bf16[16,12288]{1,0:T(8,128)(2,1)S(1)} %shard_map.122.far, bf16[12288,128]{1,0:T(8,128)(2,1)S(1)} %get-tuple-element.90.w_own, bf16[12288,128]{1,0:T(8,128)(2,1)S(1)} %collective-permute-done.6.w_mate, f32[1,128]{1,0:T(1,128)S(1)} %bitcast.13, ...), custom_call_target="tpu_custom_call" | custom-call | bytes 4194304 | tf_op jit(solution)/shard_map/pallas_call | solution.py:250
  36.2 1.2 %shard_map.124.part = f32[32,12288]{1,0:T(8,128)S(1)} custom-call(bf16[32,256]{1,0:T(8,128)(2,1)S(1)} %shard_map.123.act, bf16[128,12288]{1,0:T(8,128)(2,1)S(1)} %get-tuple-element.94.w_own, bf16[128,12288]{1,0:T(8,128)(2,1)S(1)} %collective-permute-done.13.w_mate), custom_call_target="tpu_custom_call" | custom-call | bytes 6291456 | tf_op jit(solution)/shard_map/pallas_call | solution.py:265
  37.4 2.2 %collective-permute-done.16.refs_2_ = bf16[32,512]{1,0:T(8,128)(2,1)S(1)} collective-permute-done((bf16[32,512]{1,0:T(8,128)(2,1)S(1)}, bf16[32,512]{1,0:T(8,128)(2,1)S(1)}, u32[]{:S(2)}, u32[]{:S(2)}) %collective-permute-start.16) | collective-permute-done | bytes 32800 | tf_op jit(solution)/shard_map/ppermute | solution.py:187
  40.1 1.1 %collective-permute-start.18 = (bf16[4,12288]{1,0:T(4,128)(2,1)S(1)}, bf16[4,12288]{1,0:T(4,128)(2,1)S(1)}, u32[]{:S(2)}, u32[]{:S(2)}) collective-permute-start(bf16[4,12288]{1,0:T(4,128)(2,1)S(1)} %get-tuple-element.102), channel_id=1, source_target_pairs={{0,2},{1,3},{2,0},{3,1},{4,6},{5,7},{6,4},{7,5},{8,10},{9,11},{10,... | collective-permute-start | bytes 294920 | tf_op jit(solution)/shard_map/ppermute | solution.py:190
  41.2 1.0 %collective-permute-start.17 = (bf16[4,12288]{1,0:T(4,128)(2,1)S(1)}, bf16[4,12288]{1,0:T(4,128)(2,1)S(1)}, u32[]{:S(2)}, u32[]{:S(2)}) collective-permute-start(bf16[4,12288]{1,0:T(4,128)(2,1)S(1)} %get-tuple-element.100), channel_id=1, source_target_pairs={{0,2},{1,3},{2,0},{3,1},{4,6},{5,7},{6,4},{7,5},{8,10},{9,11},{10,... | collective-permute-start | bytes 294920 | tf_op jit(solution)/shard_map/ppermute | solution.py:190
  42.2 1.0 %collective-permute-start.20 = (bf16[4,12288]{1,0:T(4,128)(2,1)S(1)}, bf16[4,12288]{1,0:T(4,128)(2,1)S(1)}, u32[]{:S(2)}, u32[]{:S(2)}) collective-permute-start(bf16[4,12288]{1,0:T(4,128)(2,1)S(1)} %get-tuple-element.104), channel_id=1, source_target_pairs={{0,2},{1,3},{2,0},{3,1},{4,6},{5,7},{6,4},{7,5},{8,10},{9,11},{10,... | collective-permute-start | bytes 294920 | tf_op jit(solution)/shard_map/ppermute | solution.py:190
  43.2 1.0 %collective-permute-start.22 = (bf16[4,12288]{1,0:T(4,128)(2,1)S(1)}, bf16[4,12288]{1,0:T(4,128)(2,1)S(1)}, u32[]{:S(2)}, u32[]{:S(2)}) collective-permute-start(bf16[4,12288]{1,0:T(4,128)(2,1)S(1)} %get-tuple-element.106), channel_id=1, source_target_pairs={{0,2},{1,3},{2,0},{3,1},{4,6},{5,7},{6,4},{7,5},{8,10},{9,11},{10,... | collective-permute-start | bytes 294920 | tf_op jit(solution)/shard_map/ppermute | solution.py:190
  44.2 1.7 %collective-permute-done.18 = bf16[4,12288]{1,0:T(4,128)(2,1)S(1)} collective-permute-done((bf16[4,12288]{1,0:T(4,128)(2,1)S(1)}, bf16[4,12288]{1,0:T(4,128)(2,1)S(1)}, u32[]{:S(2)}, u32[]{:S(2)}) %collective-permute-start.18) | collective-permute-done | bytes 98336 | tf_op jit(solution)/shard_map/ppermute | solution.py:190
  46.0 2.9 %collective-permute-done.20 = bf16[4,12288]{1,0:T(4,128)(2,1)S(1)} collective-permute-done((bf16[4,12288]{1,0:T(4,128)(2,1)S(1)}, bf16[4,12288]{1,0:T(4,128)(2,1)S(1)}, u32[]{:S(2)}, u32[]{:S(2)}) %collective-permute-start.20) | collective-permute-done | bytes 98336 | tf_op jit(solution)/shard_map/ppermute | solution.py:190
  49.1 0.9 %collective-permute-done.22 = bf16[4,12288]{1,0:T(4,128)(2,1)S(1)} collective-permute-done((bf16[4,12288]{1,0:T(4,128)(2,1)S(1)}, bf16[4,12288]{1,0:T(4,128)(2,1)S(1)}, u32[]{:S(2)}, u32[]{:S(2)}) %collective-permute-start.22) | collective-permute-done | bytes 98336 | tf_op jit(solution)/shard_map/ppermute | solution.py:190
  50.0 2.1 %collective-permute-start.23 = (bf16[4,12288]{1,0:T(4,128)(2,1)S(1)}, bf16[4,12288]{1,0:T(4,128)(2,1)S(1)}, u32[]{:S(2)}, u32[]{:S(2)}) collective-permute-start(bf16[4,12288]{1,0:T(4,128)(2,1)S(1)} %add_convert_fusion), channel_id=1, source_target_pairs={{0,12},{1,13},{2,14},{3,15},{4,8},{5,9},{6,10},{7,11},{8,4},{9,5},... | collective-permute-start | bytes 294920 | tf_op jit(solution)/shard_map/ppermute | solution.py:187
  52.2 4.5 %collective-permute-done.21.refs_2_ = bf16[4,12288]{1,0:T(4,128)(2,1)S(1)} collective-permute-done((bf16[4,12288]{1,0:T(4,128)(2,1)S(1)}, bf16[4,12288]{1,0:T(4,128)(2,1)S(1)}, u32[]{:S(2)}, u32[]{:S(2)}) %collective-permute-start.21) | collective-permute-done | bytes 98336 | tf_op jit(solution)/shard_map/ppermute | solution.py:187
  56.7 0.7 %shard_map.126 = bf16[4,12288]{1,0:T(4,128)(2,1)} custom-call(f32[4,12288]{1,0:T(4,128)S(1)} %convert_add_fusion.refs_0_, bf16[4,12288]{1,0:T(4,128)(2,1)S(1)} %collective-permute-done.19.refs_1_, bf16[4,12288]{1,0:T(4,128)(2,1)S(1)} %collective-permute-done.21.refs_2_, bf16[4,12288]{1,0:T(4,128)(2,1)S(1)} %collective-permute-done.23.refs_3_), custom_call_target="tpu_custom_call" | custom-call | bytes 2097152 | tf_op jit(solution)/shard_map/pallas_call | solution.py:286
  (52 shorter events, 3.5 us)
Async XLA Ops:
  0.0 18.5 %collective-permute-start.6 = (bf16[12288,128]{1,0:T(8,128)(2,1)}, bf16[12288,128]{1,0:T(8,128)(2,1)S(1)}, u32[]{:S(2)}, u32[]{:S(2)}) collective-permute-start(bf16[12288,128]{1,0:T(8,128)(2,1)} %refs_4_), channel_id=1, source_target_pairs={{0,1},{1,0},{2,3},{3,2},{4,5},{5,4},{6,7},{7,6},{8,9},{9,8},{10,11... | collective-permute-start | bytes 9437192 | tf_op jit(solution)/shard_map/ppermute | solution.py:193
  0.5 13.7 %collective-permute-start.3 = (bf16[4,12288]{1,0:T(4,128)(2,1)}, bf16[4,12288]{1,0:T(4,128)(2,1)S(1)}, u32[]{:S(2)}, u32[]{:S(2)}) collective-permute-start(bf16[4,12288]{1,0:T(4,128)(2,1)} %refs_0_), channel_id=1, source_target_pairs={{0,8},{1,9},{2,10},{3,11},{4,12},{5,13},{6,14},{7,15},{8,0},{9,1},... | collective-permute-start | bytes 294920 | tf_op jit(solution)/shard_map/ppermute | solution.py:187
  4.0 10.2 %collective-permute-start.1 = (bf16[4,12288]{1,0:T(4,128)(2,1)}, bf16[4,12288]{1,0:T(4,128)(2,1)S(1)}, u32[]{:S(2)}, u32[]{:S(2)}) collective-permute-start(bf16[4,12288]{1,0:T(4,128)(2,1)} %refs_0_), channel_id=1, source_target_pairs={{0,2},{1,3},{2,0},{3,1},{4,6},{5,7},{6,4},{7,5},{8,10},{9,11},{10,... | collective-permute-start | bytes 294920 | tf_op jit(solution)/shard_map/ppermute | solution.py:190
  5.6 8.3 %collective-permute-start = (bf16[4,12288]{1,0:T(4,128)(2,1)}, bf16[4,12288]{1,0:T(4,128)(2,1)S(1)}, u32[]{:S(2)}, u32[]{:S(2)}) collective-permute-start(bf16[4,12288]{1,0:T(4,128)(2,1)} %refs_0_), channel_id=1, source_target_pairs={{0,4},{1,5},{2,6},{3,7},{4,0},{5,1},{6,2},{7,3},{8,12},{9,13},{10,... | collective-permute-start | bytes 294920 | tf_op jit(solution)/shard_map/ppermute | solution.py:187
  7.1 7.1 %collective-permute-start.4 = (bf16[4,12288]{1,0:T(4,128)(2,1)}, bf16[4,12288]{1,0:T(4,128)(2,1)S(1)}, u32[]{:S(2)}, u32[]{:S(2)}) collective-permute-start(bf16[4,12288]{1,0:T(4,128)(2,1)} %refs_0_), channel_id=1, source_target_pairs={{0,12},{1,13},{2,14},{3,15},{4,8},{5,9},{6,10},{7,11},{8,4},{9,5},... | collective-permute-start | bytes 294920 | tf_op jit(solution)/shard_map/ppermute | solution.py:187
  10.2 8.3 %copy-start.2 = (bf16[128,12288]{1,0:T(8,128)(2,1)S(1)}, bf16[128,12288]{1,0:T(8,128)(2,1)}, u32[]{:S(2)}) copy-start(bf16[128,12288]{1,0:T(8,128)(2,1)} %refs_5_) | copy-start | bytes 9437188
  10.3 8.3 %copy-start.3 = (bf16[768,512]{1,0:T(8,128)(2,1)S(1)}, bf16[768,512]{1,0:T(8,128)(2,1)}, u32[]{:S(2)}) copy-start(bf16[768,512]{1,0:T(8,128)(2,1)} %refs_3_) | copy-start | bytes 2359300
  10.3 8.8 %copy-start.4 = (bf16[512,768]{1,0:T(8,128)(2,1)S(1)}, bf16[512,768]{1,0:T(8,128)(2,1)}, u32[]{:S(2)}) copy-start(bf16[512,768]{1,0:T(8,128)(2,1)} %refs_6_) | copy-start | bytes 2359300
  10.3 19.4 %copy-start.1 = (f32[128]{0:T(128)S(1)}, f32[128]{0:T(128)}, u32[]{:S(2)}) copy-start(f32[128]{0:T(128)} %param.19) | copy-start | bytes 1540
  13.8 4.7 %collective-permute-start.2 = (bf16[4,12288]{1,0:T(4,128)(2,1)S(1)}, bf16[4,12288]{1,0:T(4,128)(2,1)S(1)}, u32[]{:S(2)}, u32[]{:S(2)}) collective-permute-start(bf16[4,12288]{1,0:T(4,128)(2,1)S(1)} %collective-permute-done.refs_1_), channel_id=1, source_target_pairs={{0,2},{1,3},{2,0},{3,1},{4,6},{5,7},{6,4},{7,5},{8,10},{9,11},{10,... | collective-permute-start | bytes 294920 | tf_op jit(solution)/shard_map/ppermute | solution.py:190
  18.5 17.7 %collective-permute-start.13 = (bf16[128,12288]{1,0:T(8,128)(2,1)S(1)}, bf16[128,12288]{1,0:T(8,128)(2,1)S(1)}, u32[]{:S(2)}, u32[]{:S(2)}) collective-permute-start(bf16[128,12288]{1,0:T(8,128)(2,1)S(1)} %copy-done.2), channel_id=1, source_target_pairs={{0,1},{1,0},{2,3},{3,2},{4,5},{5,4},{6,7},{7,6},{8,9},{9,8},{10,11... | collective-permute-start | bytes 9437192 | tf_op jit(solution)/shard_map/ppermute | solution.py:193
  18.5 6.8 %collective-permute-start.7 = (bf16[768,512]{1,0:T(8,128)(2,1)S(1)}, bf16[768,512]{1,0:T(8,128)(2,1)S(1)}, u32[]{:S(2)}, u32[]{:S(2)}) collective-permute-start(bf16[768,512]{1,0:T(8,128)(2,1)S(1)} %copy-done.3), channel_id=1, source_target_pairs={{0,1},{1,0},{2,3},{3,2},{4,5},{5,4},{6,7},{7,6},{8,9},{9,8},{10,11... | collective-permute-start | bytes 2359304 | tf_op jit(solution)/shard_map/ppermute | solution.py:193
  19.0 18.3 %collective-permute-start.9 = (bf16[512,768]{1,0:T(8,128)(2,1)S(1)}, bf16[512,768]{1,0:T(8,128)(2,1)S(1)}, u32[]{:S(2)}, u32[]{:S(2)}) collective-permute-start(bf16[512,768]{1,0:T(8,128)(2,1)S(1)} %copy-done.4), channel_id=1, source_target_pairs={{0,1},{1,0},{2,3},{3,2},{4,5},{5,4},{6,7},{7,6},{8,9},{9,8},{10,11... | collective-permute-start | bytes 2359304 | tf_op jit(solution)/shard_map/ppermute | solution.py:193
  19.7 4.6 %collective-permute-start.5 = (bf16[16,1536]{1,0:T(8,128)(2,1)S(1)}, bf16[16,1536]{1,0:T(8,128)(2,1)S(1)}, u32[]{:S(2)}, u32[]{:S(2)}) collective-permute-start(bf16[16,1536]{1,0:T(8,128)(2,1)S(1)} %get-tuple-element.77), channel_id=1, source_target_pairs={{0,2},{1,3},{2,0},{3,1},{4,6},{5,7},{6,4},{7,5},{8,10},{9,11},{10,... | collective-permute-start | bytes 147464 | tf_op jit(solution)/shard_map/ppermute | solution.py:190
  20.1 9.6 %collective-permute-start.10 = (bf16[4,12288]{1,0:T(4,128)(2,1)S(1)}, bf16[4,12288]{1,0:T(4,128)(2,1)S(1)}, u32[]{:S(2)}, u32[]{:S(2)}) collective-permute-start(bf16[4,12288]{1,0:T(4,128)(2,1)S(1)} %collective-permute-done.3.refs_2_), channel_id=1, source_target_pairs={{0,2},{1,3},{2,0},{3,1},{4,6},{5,7},{6,4},{7,5},{8,10},{9,11},{10,... | collective-permute-start | bytes 294920 | tf_op jit(solution)/shard_map/ppermute | solution.py:190
  24.3 6.1 %collective-permute-start.11 = (bf16[4,12288]{1,0:T(4,128)(2,1)S(1)}, bf16[4,12288]{1,0:T(4,128)(2,1)S(1)}, u32[]{:S(2)}, u32[]{:S(2)}) collective-permute-start(bf16[4,12288]{1,0:T(4,128)(2,1)S(1)} %collective-permute-done.4.refs_3_), channel_id=1, source_target_pairs={{0,2},{1,3},{2,0},{3,1},{4,6},{5,7},{6,4},{7,5},{8,10},{9,11},{10,... | collective-permute-start | bytes 294920 | tf_op jit(solution)/shard_map/ppermute | solution.py:190
  25.7 4.0 %collective-permute-start.8 = (bf16[32,512]{1,0:T(8,128)(2,1)S(1)}, bf16[32,512]{1,0:T(8,128)(2,1)S(1)}, u32[]{:S(2)}, u32[]{:S(2)}) collective-permute-start(bf16[32,512]{1,0:T(8,128)(2,1)S(1)} %get-tuple-element.81), channel_id=1, source_target_pairs={{0,2},{1,3},{2,0},{3,1},{4,6},{5,7},{6,4},{7,5},{8,10},{9,11},{10,... | collective-permute-start | bytes 98312 | tf_op jit(solution)/shard_map/ppermute | solution.py:190
  29.7 4.3 %collective-permute-start.12 = (f32[1,128]{1,0:T(1,128)S(1)}, f32[1,128]{1,0:T(1,128)S(1)}, u32[]{:S(2)}, u32[]{:S(2)}) collective-permute-start(f32[1,128]{1,0:T(1,128)S(1)} %bitcast.12), channel_id=1, source_target_pairs={{0,1},{1,0},{2,3},{3,2},{4,5},{5,4},{6,7},{7,6},{8,9},{9,8},{10,11... | collective-permute-start | bytes 1544 | tf_op jit(solution)/shard_map/ppermute | solution.py:193
  29.7 7.7 %collective-permute-start.14 = (bf16[32,512]{1,0:T(8,128)(2,1)S(1)}, bf16[32,512]{1,0:T(8,128)(2,1)S(1)}, u32[]{:S(2)}, u32[]{:S(2)}) collective-permute-start(bf16[32,512]{1,0:T(8,128)(2,1)S(1)} %get-tuple-element.96), channel_id=1, source_target_pairs={{0,4},{1,5},{2,6},{3,7},{4,0},{5,1},{6,2},{7,3},{8,12},{9,13},{10,... | collective-permute-start | bytes 98312 | tf_op jit(solution)/shard_map/ppermute | solution.py:187
  30.4 7.0 %collective-permute-start.15 = (bf16[32,512]{1,0:T(8,128)(2,1)S(1)}, bf16[32,512]{1,0:T(8,128)(2,1)S(1)}, u32[]{:S(2)}, u32[]{:S(2)}) collective-permute-start(bf16[32,512]{1,0:T(8,128)(2,1)S(1)} %get-tuple-element.97), channel_id=1, source_target_pairs={{0,8},{1,9},{2,10},{3,11},{4,12},{5,13},{6,14},{7,15},{8,0},{9,1},... | collective-permute-start | bytes 98312 | tf_op jit(solution)/shard_map/ppermute | solution.py:187
  33.9 5.7 %collective-permute-start.16 = (bf16[32,512]{1,0:T(8,128)(2,1)S(1)}, bf16[32,512]{1,0:T(8,128)(2,1)S(1)}, u32[]{:S(2)}, u32[]{:S(2)}) collective-permute-start(bf16[32,512]{1,0:T(8,128)(2,1)S(1)} %get-tuple-element.98), channel_id=1, source_target_pairs={{0,12},{1,13},{2,14},{3,15},{4,8},{5,9},{6,10},{7,11},{8,4},{9,5},... | collective-permute-start | bytes 98312 | tf_op jit(solution)/shard_map/ppermute | solution.py:187
  36.2 3.5 %copy-start = (f32[512]{0:T(512)S(1)}, f32[512]{0:T(512)}, u32[]{:S(2)}) copy-start(f32[512]{0:T(512)} %param.22) | copy-start | bytes 6148
  40.1 5.8 %collective-permute-start.18 = (bf16[4,12288]{1,0:T(4,128)(2,1)S(1)}, bf16[4,12288]{1,0:T(4,128)(2,1)S(1)}, u32[]{:S(2)}, u32[]{:S(2)}) collective-permute-start(bf16[4,12288]{1,0:T(4,128)(2,1)S(1)} %get-tuple-element.102), channel_id=1, source_target_pairs={{0,2},{1,3},{2,0},{3,1},{4,6},{5,7},{6,4},{7,5},{8,10},{9,11},{10,... | collective-permute-start | bytes 294920 | tf_op jit(solution)/shard_map/ppermute | solution.py:190
  41.2 11.0 %collective-permute-start.17 = (bf16[4,12288]{1,0:T(4,128)(2,1)S(1)}, bf16[4,12288]{1,0:T(4,128)(2,1)S(1)}, u32[]{:S(2)}, u32[]{:S(2)}) collective-permute-start(bf16[4,12288]{1,0:T(4,128)(2,1)S(1)} %get-tuple-element.100), channel_id=1, source_target_pairs={{0,2},{1,3},{2,0},{3,1},{4,6},{5,7},{6,4},{7,5},{8,10},{9,11},{10,... | collective-permute-start | bytes 294920 | tf_op jit(solution)/shard_map/ppermute | solution.py:190
  42.2 6.7 %collective-permute-start.20 = (bf16[4,12288]{1,0:T(4,128)(2,1)S(1)}, bf16[4,12288]{1,0:T(4,128)(2,1)S(1)}, u32[]{:S(2)}, u32[]{:S(2)}) collective-permute-start(bf16[4,12288]{1,0:T(4,128)(2,1)S(1)} %get-tuple-element.104), channel_id=1, source_target_pairs={{0,2},{1,3},{2,0},{3,1},{4,6},{5,7},{6,4},{7,5},{8,10},{9,11},{10,... | collective-permute-start | bytes 294920 | tf_op jit(solution)/shard_map/ppermute | solution.py:190
  43.2 6.8 %collective-permute-start.22 = (bf16[4,12288]{1,0:T(4,128)(2,1)S(1)}, bf16[4,12288]{1,0:T(4,128)(2,1)S(1)}, u32[]{:S(2)}, u32[]{:S(2)}) collective-permute-start(bf16[4,12288]{1,0:T(4,128)(2,1)S(1)} %get-tuple-element.106), channel_id=1, source_target_pairs={{0,2},{1,3},{2,0},{3,1},{4,6},{5,7},{6,4},{7,5},{8,10},{9,11},{10,... | collective-permute-start | bytes 294920 | tf_op jit(solution)/shard_map/ppermute | solution.py:190
  45.9 6.3 %collective-permute-start.19 = (bf16[4,12288]{1,0:T(4,128)(2,1)S(1)}, bf16[4,12288]{1,0:T(4,128)(2,1)S(1)}, u32[]{:S(2)}, u32[]{:S(2)}) collective-permute-start(bf16[4,12288]{1,0:T(4,128)(2,1)S(1)} %add_convert_fusion.2), channel_id=1, source_target_pairs={{0,4},{1,5},{2,6},{3,7},{4,0},{5,1},{6,2},{7,3},{8,12},{9,13},{10,... | collective-permute-start | bytes 294920 | tf_op jit(solution)/shard_map/ppermute | solution.py:187
  49.0 7.7 %collective-permute-start.21 = (bf16[4,12288]{1,0:T(4,128)(2,1)S(1)}, bf16[4,12288]{1,0:T(4,128)(2,1)S(1)}, u32[]{:S(2)}, u32[]{:S(2)}) collective-permute-start(bf16[4,12288]{1,0:T(4,128)(2,1)S(1)} %add_convert_fusion.1), channel_id=1, source_target_pairs={{0,8},{1,9},{2,10},{3,11},{4,12},{5,13},{6,14},{7,15},{8,0},{9,1},... | collective-permute-start | bytes 294920 | tf_op jit(solution)/shard_map/ppermute | solution.py:187
  50.0 6.7 %collective-permute-start.23 = (bf16[4,12288]{1,0:T(4,128)(2,1)S(1)}, bf16[4,12288]{1,0:T(4,128)(2,1)S(1)}, u32[]{:S(2)}, u32[]{:S(2)}) collective-permute-start(bf16[4,12288]{1,0:T(4,128)(2,1)S(1)} %add_convert_fusion), channel_id=1, source_target_pairs={{0,12},{1,13},{2,14},{3,15},{4,8},{5,9},{6,10},{7,11},{8,4},{9,5},... | collective-permute-start | bytes 294920 | tf_op jit(solution)/shard_map/ppermute | solution.py:187

commit v9 on v8

--- a/solution.py
+++ b/solution.py
@@ -62,8 +62,14 @@
 
 
 def near_body(groups, place, *refs):
-    held, (gain, shift, near, keep, send) = refs[:groups], refs[groups:]
-    normalise(held, gain, shift, near)
+    held, (own, gains, shifts, near, keep, send, gain, shift, first, sems) = refs[: groups - 1], refs[groups - 1 :]
+    pairs = ((own, first), (gains, gain), (shifts, shift))
+    copies = [pltpu.make_async_copy(src, dst, sems.at[i]) for i, (src, dst) in enumerate(pairs)]
+    for copy in copies:
+        copy.start()
+    for copy in copies:
+        copy.wait()
+    normalise((first, *held), gain, shift, near)
     span = keep.shape[1]
     chip = place[0] // 2
     keep[...] = near[:, window(chip, span)]
@@ -206,11 +212,30 @@
     live = jnp.sum(jnp.where(relate & choose, table[None, None], 0), axis=(2, 3)).astype(f32)
     mask = jnp.broadcast_to(live[None, :, None, :, None], (2, groups, row_dev, 2, block)).reshape(rows, 2 * block)
 
-    held = [hidden] + [across(hidden, k) for k in range(1, groups)]
+    held = [hidden] + [across(hidden, k) for k in range(groups - 1, 0, -1)][::-1]
     w_in_mate = core(w_in)
-    near = (hidden, gain, shift, low_in, w_in, w_out, low_out)
-    *near, mask = lax.optimization_barrier((*near, mask))
-    near = call(
+    first, _ = lax.optimization_barrier((hidden, held[1]))
+    beyond = [beside(first), beside(held[1])]
+    *_, w_in_mate, mask, low_in_sent, w_out_sent, bias_sent = lax.optimization_barrier(
+        (*held, *beyond, w_in_mate, mask, low_in, w_out, bias)
+    )
+    low_in_mate, bias_mate, w_out_mate = map(core, (low_in_sent, bias_sent, w_out_sent))
+
+    own, *beyond = lax.optimization_barrier((hidden, *beyond))
+    normed, keep, send, gain, shift = call(
+        functools.partial(near_body, groups),
+        [shape(some, width), shape(some, span), shape(some, span)] + [shape(1, width, dtype=f32)] * 2,
+        [SMEM] + [VMEM] * (groups - 1) + [HBM] * 3,
+        16,
+        [pltpu.VMEM((row_dev, width), bf16), pltpu.SemaphoreType.DMA((3,))],
+        4 * MIB,
+    )(place, *held[1:], *[pltpu.with_memory_space_constraint(x, pltpu.HBM) for x in (own, gain, shift)])
+    send, *late = lax.optimization_barrier((send, *held[2:]))
+    got, bias_mate = lax.optimization_barrier((beside(send), bias_mate))
+    beyond = beyond + [beside(h) for h in late]
+    near = (low_in, w_in, w_out, low_out)
+    *near, keep = lax.optimization_barrier((*near, keep))
+    low_in_near, w_in, w_out_near, low_out_near = call(
         functools.partial(load_body, len(near)),
         [shape(*x.shape, dtype=x.dtype) for x in near],
         [HBM] * len(near),
@@ -218,34 +243,14 @@
         [pltpu.SemaphoreType.DMA((len(near),))],
         8 * MIB,
     )(*[pltpu.with_memory_space_constraint(x, pltpu.HBM) for x in near])
-    held[1], *near = lax.optimization_barrier((held[1], *near))
-    hidden_near, gain, shift, low_in_near, w_in, w_out_near, low_out_near = near
-    soon = groups // 2
-    beyond = [beside(h) for h in held[:soon]]
-    *_, w_in_mate, low_in_sent, w_out_sent, low_out_sent, bias_sent = lax.optimization_barrier(
-        (*held, *beyond, w_in_mate, low_in, w_out, low_out, bias)
-    )
-    low_in_mate, bias_mate, w_out_mate, low_out_mate = map(core, (low_in_sent, bias_sent, w_out_sent, low_out_sent))
-
-    hidden_near, *beyond = lax.optimization_barrier((hidden_near, *beyond))
-    normed, keep, send = call(
-        functools.partial(near_body, groups),
-        [shape(some, width), shape(some, span), shape(some, span)],
-        [SMEM] + [VMEM] * (groups + 2),
-        16,
-        (),
-        4 * MIB,
-    )(place, hidden_near, *held[1:], gain, shift)
-    send, *late = lax.optimization_barrier((send, *held[soon:]))
-    got = beside(send)
-    beyond = beyond + [beside(h) for h in late]
     total, message = call(
         down_body, [shape(rows, rank, dtype=f32), shape(rows, rank)], [SMEM] + [VMEM] * 4, 16
     )(place, keep, got, low_in_near, low_in_mate)
     far = call(
         functools.partial(far_body, groups), [shape(some, width)], [VMEM] * (groups + 2), 16, (), 4 * MIB
     )(*beyond, gain, shift)[0]
-    got = beside(message)
+    got, low_out_sent, w_out_mate = lax.optimization_barrier((beside(message), low_out, w_out_mate))
+    low_out_mate = core(low_out_sent)
     step = piece(width, 2048)
     act = call(
         functools.partial(act_body, step),
@@ -261,7 +266,7 @@
         [VMEM] * 2,
         16,
     )(total, got)
-    got = [across(messages[k - 1], k) for k in range(1, groups)]
+    got = [across(messages[k - 1], k) for k in range(groups - 1, 0, -1)]
     part = call(
         functools.partial(part_body, step),
         [shape(rows, width, dtype=f32)],
@@ -279,11 +284,15 @@
         6 * MIB,
     )(place, total, low_bias.reshape(1, rank), low_out_near, low_out_mate, part, *got)
 
-    sums = []
+    sent, half = list(parts[groups:]), groups // 2
+    sums = [None] * groups
     for k in range(groups - 1, -1, -1):
-        here = parts[k] + beside(parts[groups + k]).astype(f32)
-        sums.append(across(here.astype(bf16), k) if k else here)
-    return call(functools.partial(last_body, groups), [shape(row_dev, width)], [VMEM] * groups, 16)(*sums[::-1])[0]
+        come = beside(sent[k])
+        if k == groups - 1:
+            come, *sent[:half] = lax.optimization_barrier((come, *sent[:half]))
+        here = parts[k] + come.astype(f32)
+        sums[k] = across(here.astype(bf16), k) if k else here
+    return call(functools.partial(last_body, groups), [shape(row_dev, width)], [VMEM] * groups, 16)(*sums)[0]
 
 
 def solution(mesh):

time: 57.6 us -> 56.9 us (0.988)
  waiting for transfers between devices: 23 us -> 18.3 us
  starting transfers between devices: 22.5 us -> 25.8 us
  Pallas kernels: 8.61 us -> 9.34 us
    ppermute x10, waiting for transfers between devices: 15.2 us -> 11.5 us  [beside(): return lax.ppermute(x, 'blk', [(i, i ^ 2) for i in range(devices)])]
    ppermute x10, starting transfers between devices: 9.15 us -> 11.5 us  [beside(): return lax.ppermute(x, 'blk', [(i, i ^ 2) for i in range(devices)])]
    ppermute x9, starting transfers between devices: 12.4 us -> 13.4 us  [across(): return lax.ppermute(x, 'blk', [(i, i ^ 4 * k) for i in range(devices)])]
    ppermute x5, waiting for transfers between devices: 0.98 us -> 0.07 us  [core(): return lax.ppermute(x, 'blk', [(i, i ^ 1) for i in range(devices)])]
    pallas_call x1, Pallas kernels: 0.6 us -> 1.49 us  [shards(): call(functools.partial(near_body, groups), [shape(some, width), shape(som...]
  transfers between devices with their start and end apart: 24 -> 24, of which waited for: 9 -> 12; matrix products, arithmetic and copies ran while one was open for 5% -> 5% of each run, Pallas kernels for 13% -> 14%
where the time goes in v9:
time: 56.9 us; the launch traced here: 56.7 us
  starting transfers between devices  25.8 us (45%)
  waiting for transfers between devices  18.3 us (32%)
  Pallas kernels  9.34 us (16%)
  other arithmetic  2.26 us (4%)
  local copies, waits for them, and re-layouts  0.87 us (2%)
    ppermute x9, starting transfers between devices, across(): return lax.ppermute(x, 'blk', [(i, i ^ 4 * k) for i in range(devices)])  13.4 us
    ppermute x10, waiting for transfers between devices, beside(): return lax.ppermute(x, 'blk', [(i, i ^ 2) for i in range(devices)])  11.5 us
    ppermute x10, starting transfers between devices, beside(): return lax.ppermute(x, 'blk', [(i, i ^ 2) for i in range(devices)])  11.5 us
    ppermute x9, waiting for transfers between devices, across(): return lax.ppermute(x, 'blk', [(i, i ^ 4 * k) for i in range(devices)])  6.71 us
    pallas_call x1, Pallas kernels, shards(): call(functools.partial(load_body, len(near)), [shape(*x.shape, dtype=x.dt...  3.32 us
    pallas_call x1, Pallas kernels, shards(): call(functools.partial(near_body, groups), [shape(some, width), shape(som...  1.49 us
    pallas_call x1, Pallas kernels, shards(): call(functools.partial(act_body, step), [shape(rows, 2 * block)], [VMEM]...  1.21 us
    pallas_call x1, Pallas kernels, shards(): call(functools.partial(part_body, step), [shape(rows, width, dtype=f32)],...  1.19 us
  transfers between devices with their start and end apart: 24, of which 12 were waited for; matrix products, arithmetic and copies ran while one was open for 5% of the time, Pallas kernels for 14%

profile of v9, /device:TPU:0, one launch (start us, length us, event | category | flops | bytes accessed | tf_op | source)
XLA Modules:
  0.0 56.7 jit_solution(10353723583265886079)
XLA Ops:
  0.5 2.6 %collective-permute-start = (bf16[4,12288]{1,0:T(4,128)(2,1)}, bf16[4,12288]{1,0:T(4,128)(2,1)S(1)}, u32[]{:S(2)}, u32[]{:S(2)}) collective-permute-start(bf16[4,12288]{1,0:T(4,128)(2,1)} %refs_3_), channel_id=1, source_target_pairs={{0,4},{1,5},{2,6},{3,7},{4,0},{5,1},{6,2},{7,3},{8,12},{9,13},{10,... | collective-permute-start | bytes 294920 | tf_op jit(solution)/shard_map/ppermute | solution.py:193
  3.0 2.6 %collective-permute-start.1 = (bf16[4,12288]{1,0:T(4,128)(2,1)}, bf16[4,12288]{1,0:T(4,128)(2,1)S(1)}, u32[]{:S(2)}, u32[]{:S(2)}) collective-permute-start(bf16[4,12288]{1,0:T(4,128)(2,1)} %refs_3_), channel_id=1, source_target_pairs={{0,8},{1,9},{2,10},{3,11},{4,12},{5,13},{6,14},{7,15},{8,0},{9,1},... | collective-permute-start | bytes 294920 | tf_op jit(solution)/shard_map/ppermute | solution.py:193
  5.6 0.8 %copy.13 = s32[4,6]{0,1:T(8,128)S(1)} copy(s32[4,6]{1,0:T(4,128)} %param.15) | data formatting | bytes 192 | tf_op args[3]
  6.4 0.7 %fusion.1 = s32[4,6]{0,1:T(8,128)S(1)} fusion(s32[4]{0:T(128)} %param.16), kind=kLoop, calls=%fused_computation.12 | loop fusion | flops 48 | bytes 112 | tf_op jit(solution)/shard_map/convert_element_type | solution.py:160
  7.3 0.7 %fusion = s32[16,16]{1,0:T(8,128)S(1)} fusion(s32[16]{0:T(128)} %param.17), kind=kLoop, calls=%fused_computation.10 | loop fusion | flops 512 | bytes 1088 | tf_op jit(solution)/shard_map/convert_element_type | solution.py:163
  8.1 1.8 %collective-permute-start.3 = (bf16[4,12288]{1,0:T(4,128)(2,1)}, bf16[4,12288]{1,0:T(4,128)(2,1)S(1)}, u32[]{:S(2)}, u32[]{:S(2)}) collective-permute-start(bf16[4,12288]{1,0:T(4,128)(2,1)} %refs_3_), channel_id=1, source_target_pairs={{0,2},{1,3},{2,0},{3,1},{4,6},{5,7},{6,4},{7,5},{8,10},{9,11},{10,... | collective-permute-start | bytes 294920 | tf_op jit(solution)/shard_map/ppermute | solution.py:196
  10.6 3.4 %collective-permute-done.1.refs_1_ = bf16[4,12288]{1,0:T(4,128)(2,1)S(1)} collective-permute-done((bf16[4,12288]{1,0:T(4,128)(2,1)}, bf16[4,12288]{1,0:T(4,128)(2,1)S(1)}, u32[]{:S(2)}, u32[]{:S(2)}) %collective-permute-start.1) | collective-permute-done | bytes 98336 | tf_op jit(solution)/shard_map/ppermute | solution.py:193
  14.1 1.1 %collective-permute-done.4.refs_1_ = bf16[4,12288]{1,0:T(4,128)(2,1)S(1)} collective-permute-done((bf16[4,12288]{1,0:T(4,128)(2,1)S(1)}, bf16[4,12288]{1,0:T(4,128)(2,1)S(1)}, u32[]{:S(2)}, u32[]{:S(2)}) %collective-permute-start.4) | collective-permute-done | bytes 98336 | tf_op jit(solution)/shard_map/ppermute | solution.py:196
  15.2 0.5 collective-permute-start.8
  15.7 1.5 %shard_map.118 = (bf16[16,12288]{1,0:T(8,128)(2,1)S(1)}, bf16[16,1536]{1,0:T(8,128)(2,1)S(1)}, bf16[16,1536]{1,0:T(8,128)(2,1)S(1)}, f32[1,12288]{1,0:T(1,128)S(1)}, f32[1,12288]{1,0:T(1,128)S(1)}) custom-call(s32[1]{0:T(128)} %bitcast.place, bf16[4,12288]{1,0:T(4,128)(2,1)S(1)} %collective-permute-done.refs_0_, ...), custom_call_target="tpu_custom_call" | custom-call | bytes 4194304 | tf_op jit(solution)/shard_map/pallas_call | solution.py:225
  17.2 1.6 %collective-permute-start.5 = (bf16[16,1536]{1,0:T(8,128)(2,1)S(1)}, bf16[16,1536]{1,0:T(8,128)(2,1)S(1)}, u32[]{:S(2)}, u32[]{:S(2)}) collective-permute-start(bf16[16,1536]{1,0:T(8,128)(2,1)S(1)} %get-tuple-element.58), channel_id=1, source_target_pairs={{0,2},{1,3},{2,0},{3,1},{4,6},{5,7},{6,4},{7,5},{8,10},{9,11},{10,... | collective-permute-start | bytes 147464 | tf_op jit(solution)/shard_map/ppermute | solution.py:196
  18.8 3.3 %shard_map.119 = (bf16[768,512]{1,0:T(8,128)(2,1)S(1)}, bf16[12288,128]{1,0:T(8,128)(2,1)S(1)}, bf16[128,12288]{1,0:T(8,128)(2,1)S(1)}, bf16[512,768]{1,0:T(8,128)(2,1)S(1)}) custom-call(bf16[768,512]{1,0:T(8,128)(2,1)} %refs_0_, bf16[12288,128]{1,0:T(8,128)(2,1)} %refs_1_, bf16[128,12288]{1,0:T(8,128)(2,1)} %refs_2_, bf16[512,768]{1,0:T(8,128)(2,1)} %refs_3_.1), custom_call_target="tpu_custom_call" | custom-call | bytes 8388608 | tf_op jit(solution)/shard_map/pallas_call | solution.py:238
  22.5 1.5 %collective-permute-start.9 = (bf16[32,512]{1,0:T(8,128)(2,1)S(1)}, bf16[32,512]{1,0:T(8,128)(2,1)S(1)}, u32[]{:S(2)}, u32[]{:S(2)}) collective-permute-start(bf16[32,512]{1,0:T(8,128)(2,1)S(1)} %get-tuple-element.68), channel_id=1, source_target_pairs={{0,2},{1,3},{2,0},{3,1},{4,6},{5,7},{6,4},{7,5},{8,10},{9,11},{10,... | collective-permute-start | bytes 98312 | tf_op jit(solution)/shard_map/ppermute | solution.py:196
  24.1 2.4 %collective-permute-done.9.got = bf16[32,512]{1,0:T(8,128)(2,1)S(1)} collective-permute-done((bf16[32,512]{1,0:T(8,128)(2,1)S(1)}, bf16[32,512]{1,0:T(8,128)(2,1)S(1)}, u32[]{:S(2)}, u32[]{:S(2)}) %collective-permute-start.9) | collective-permute-done | bytes 32800 | tf_op jit(solution)/shard_map/ppermute | solution.py:196
  26.5 1.6 %collective-permute-start.12 = (bf16[4,12288]{1,0:T(4,128)(2,1)S(1)}, bf16[4,12288]{1,0:T(4,128)(2,1)S(1)}, u32[]{:S(2)}, u32[]{:S(2)}) collective-permute-start(bf16[4,12288]{1,0:T(4,128)(2,1)S(1)} %collective-permute-done.1.refs_1_), channel_id=1, source_target_pairs={{0,2},{1,3},{2,0},{3,1},{4,6},{5,7},{6,4},{7,5},{8,10},{9,11},{10,... | collective-permute-start | bytes 294920 | tf_op jit(solution)/shard_map/ppermute | solution.py:196
  28.6 3.6 %collective-permute-start.14 = (bf16[32,512]{1,0:T(8,128)(2,1)S(1)}, bf16[32,512]{1,0:T(8,128)(2,1)S(1)}, u32[]{:S(2)}, u32[]{:S(2)}) collective-permute-start(bf16[32,512]{1,0:T(8,128)(2,1)S(1)} %get-tuple-element.87), channel_id=1, source_target_pairs={{0,12},{1,13},{2,14},{3,15},{4,8},{5,9},{6,10},{7,11},{8,4},{9,5},... | collective-permute-start | bytes 98312 | tf_op jit(solution)/shard_map/ppermute | solution.py:193
  32.2 0.8 %collective-permute-start.16 = (bf16[32,512]{1,0:T(8,128)(2,1)S(1)}, bf16[32,512]{1,0:T(8,128)(2,1)S(1)}, u32[]{:S(2)}, u32[]{:S(2)}) collective-permute-start(bf16[32,512]{1,0:T(8,128)(2,1)S(1)} %get-tuple-element.89), channel_id=1, source_target_pairs={{0,4},{1,5},{2,6},{3,7},{4,0},{5,1},{6,2},{7,3},{8,12},{9,13},{10,... | collective-permute-start | bytes 98312 | tf_op jit(solution)/shard_map/ppermute | solution.py:193
  33.0 0.7 %collective-permute-done.13.refs_3_ = bf16[4,12288]{1,0:T(4,128)(2,1)S(1)} collective-permute-done((bf16[4,12288]{1,0:T(4,128)(2,1)S(1)}, bf16[4,12288]{1,0:T(4,128)(2,1)S(1)}, u32[]{:S(2)}, u32[]{:S(2)}) %collective-permute-start.13) | collective-permute-done | bytes 98336 | tf_op jit(solution)/shard_map/ppermute | solution.py:196
  33.8 0.6 %shard_map.122.far = bf16[16,12288]{1,0:T(8,128)(2,1)S(1)} custom-call(bf16[4,12288]{1,0:T(4,128)(2,1)S(1)} %collective-permute-done.3.refs_0_, bf16[4,12288]{1,0:T(4,128)(2,1)S(1)} %collective-permute-done.4.refs_1_, bf16[4,12288]{1,0:T(4,128)(2,1)S(1)} %collective-permute-done.12.refs_2_, bf16[4,12288]{1,0:T(4,128)(2,1)S(1)} %collective-permute-done.13.refs_3_, ...), custom_call_target="tpu_custom_call" | custom-call | bytes 4194304 | tf_op jit(solution)/shard_map/pallas_call | solution.py:249
  34.4 1.2 %shard_map.123.act = bf16[32,256]{1,0:T(8,128)(2,1)S(1)} custom-call(bf16[16,12288]{1,0:T(8,128)(2,1)S(1)} %get-tuple-element.74.near, bf16[16,12288]{1,0:T(8,128)(2,1)S(1)} %shard_map.122.far, bf16[12288,128]{1,0:T(8,128)(2,1)S(1)} %get-tuple-element.81.w_own, bf16[12288,128]{1,0:T(8,128)(2,1)S(1)} %collective-permute-done.6.w_mate, f32[1,128]{1,0:T(1,128)S(1)} %bitcast.13, ...), custom_call_target="tpu_custom_call" | custom-call | bytes 4194304 | tf_op jit(solution)/shard_map/pallas_call | solution.py:255
  35.6 1.2 %shard_map.124.part = f32[32,12288]{1,0:T(8,128)S(1)} custom-call(bf16[32,256]{1,0:T(8,128)(2,1)S(1)} %shard_map.123.act, bf16[128,12288]{1,0:T(8,128)(2,1)S(1)} %get-tuple-element.85.w_own, bf16[128,12288]{1,0:T(8,128)(2,1)S(1)} %collective-permute-done.10.w_mate), custom_call_target="tpu_custom_call" | custom-call | bytes 6291456 | tf_op jit(solution)/shard_map/pallas_call | solution.py:270
  37.5 1.6 %collective-permute-start.17 = (bf16[4,12288]{1,0:T(4,128)(2,1)S(1)}, bf16[4,12288]{1,0:T(4,128)(2,1)S(1)}, u32[]{:S(2)}, u32[]{:S(2)}) collective-permute-start(bf16[4,12288]{1,0:T(4,128)(2,1)S(1)} %get-tuple-element.91), channel_id=1, source_target_pairs={{0,2},{1,3},{2,0},{3,1},{4,6},{5,7},{6,4},{7,5},{8,10},{9,11},{10,... | collective-permute-start | bytes 294920 | tf_op jit(solution)/shard_map/ppermute | solution.py:196
  39.0 0.5 collective-permute-start.21
  39.6 3.4 %collective-permute-done.17 = bf16[4,12288]{1,0:T(4,128)(2,1)S(1)} collective-permute-done((bf16[4,12288]{1,0:T(4,128)(2,1)S(1)}, bf16[4,12288]{1,0:T(4,128)(2,1)S(1)}, u32[]{:S(2)}, u32[]{:S(2)}) %collective-permute-start.17) | collective-permute-done | bytes 98336 | tf_op jit(solution)/shard_map/ppermute | solution.py:196
  43.0 3.6 %collective-permute-start.23 = (bf16[4,12288]{1,0:T(4,128)(2,1)S(1)}, bf16[4,12288]{1,0:T(4,128)(2,1)S(1)}, u32[]{:S(2)}, u32[]{:S(2)}) collective-permute-start(bf16[4,12288]{1,0:T(4,128)(2,1)S(1)} %add_convert_fusion), channel_id=1, source_target_pairs={{0,12},{1,13},{2,14},{3,15},{4,8},{5,9},{6,10},{7,11},{8,4},{9,5},... | collective-permute-start | bytes 294920 | tf_op jit(solution)/shard_map/ppermute | solution.py:193
  46.6 1.3 %collective-permute-start.19 = (bf16[4,12288]{1,0:T(4,128)(2,1)S(1)}, bf16[4,12288]{1,0:T(4,128)(2,1)S(1)}, u32[]{:S(2)}, u32[]{:S(2)}) collective-permute-start(bf16[4,12288]{1,0:T(4,128)(2,1)S(1)} %get-tuple-element.96), channel_id=1, source_target_pairs={{0,2},{1,3},{2,0},{3,1},{4,6},{5,7},{6,4},{7,5},{8,10},{9,11},{10,... | collective-permute-start | bytes 294920 | tf_op jit(solution)/shard_map/ppermute | solution.py:196
  48.1 0.8 %collective-permute-start.18 = (bf16[4,12288]{1,0:T(4,128)(2,1)S(1)}, bf16[4,12288]{1,0:T(4,128)(2,1)S(1)}, u32[]{:S(2)}, u32[]{:S(2)}) collective-permute-start(bf16[4,12288]{1,0:T(4,128)(2,1)S(1)} %get-tuple-element.94), channel_id=1, source_target_pairs={{0,2},{1,3},{2,0},{3,1},{4,6},{5,7},{6,4},{7,5},{8,10},{9,11},{10,... | collective-permute-start | bytes 294920 | tf_op jit(solution)/shard_map/ppermute | solution.py:196
  48.9 2.4 %collective-permute-done.19 = bf16[4,12288]{1,0:T(4,128)(2,1)S(1)} collective-permute-done((bf16[4,12288]{1,0:T(4,128)(2,1)S(1)}, bf16[4,12288]{1,0:T(4,128)(2,1)S(1)}, u32[]{:S(2)}, u32[]{:S(2)}) %collective-permute-start.19) | collective-permute-done | bytes 98336 | tf_op jit(solution)/shard_map/ppermute | solution.py:196
  51.4 1.4 %collective-permute-done.18 = bf16[4,12288]{1,0:T(4,128)(2,1)S(1)} collective-permute-done((bf16[4,12288]{1,0:T(4,128)(2,1)S(1)}, bf16[4,12288]{1,0:T(4,128)(2,1)S(1)}, u32[]{:S(2)}, u32[]{:S(2)}) %collective-permute-start.18) | collective-permute-done | bytes 98336 | tf_op jit(solution)/shard_map/ppermute | solution.py:196
  52.9 0.7 %collective-permute-done.22.refs_2_ = bf16[4,12288]{1,0:T(4,128)(2,1)S(1)} collective-permute-done((bf16[4,12288]{1,0:T(4,128)(2,1)S(1)}, bf16[4,12288]{1,0:T(4,128)(2,1)S(1)}, u32[]{:S(2)}, u32[]{:S(2)}) %collective-permute-start.22) | collective-permute-done | bytes 98336 | tf_op jit(solution)/shard_map/ppermute | solution.py:193
  53.6 2.4 %collective-permute-done.20.refs_1_ = bf16[4,12288]{1,0:T(4,128)(2,1)S(1)} collective-permute-done((bf16[4,12288]{1,0:T(4,128)(2,1)S(1)}, bf16[4,12288]{1,0:T(4,128)(2,1)S(1)}, u32[]{:S(2)}, u32[]{:S(2)}) %collective-permute-start.20) | collective-permute-done | bytes 98336 | tf_op jit(solution)/shard_map/ppermute | solution.py:193
  56.0 0.7 %shard_map.126 = bf16[4,12288]{1,0:T(4,128)(2,1)} custom-call(f32[4,12288]{1,0:T(4,128)S(1)} %convert_add_fusion.refs_0_, bf16[4,12288]{1,0:T(4,128)(2,1)S(1)} %collective-permute-done.20.refs_1_, bf16[4,12288]{1,0:T(4,128)(2,1)S(1)} %collective-permute-done.22.refs_2_, bf16[4,12288]{1,0:T(4,128)(2,1)S(1)} %collective-permute-done.23.refs_3_), custom_call_target="tpu_custom_call" | custom-call | bytes 2097152 | tf_op jit(solution)/shard_map/pallas_call | solution.py:295
  (48 shorter events, 3.5 us)
Async XLA Ops:
  0.0 15.1 %collective-permute-start.6 = (bf16[12288,128]{1,0:T(8,128)(2,1)}, bf16[12288,128]{1,0:T(8,128)(2,1)S(1)}, u32[]{:S(2)}, u32[]{:S(2)}) collective-permute-start(bf16[12288,128]{1,0:T(8,128)(2,1)} %refs_1_), channel_id=1, source_target_pairs={{0,1},{1,0},{2,3},{3,2},{4,5},{5,4},{6,7},{7,6},{8,9},{9,8},{10,11... | collective-permute-start | bytes 9437192 | tf_op jit(solution)/shard_map/ppermute | solution.py:199
  0.5 7.7 %collective-permute-start = (bf16[4,12288]{1,0:T(4,128)(2,1)}, bf16[4,12288]{1,0:T(4,128)(2,1)S(1)}, u32[]{:S(2)}, u32[]{:S(2)}) collective-permute-start(bf16[4,12288]{1,0:T(4,128)(2,1)} %refs_3_), channel_id=1, source_target_pairs={{0,4},{1,5},{2,6},{3,7},{4,0},{5,1},{6,2},{7,3},{8,12},{9,13},{10,... | collective-permute-start | bytes 294920 | tf_op jit(solution)/shard_map/ppermute | solution.py:193
  3.0 11.0 %collective-permute-start.1 = (bf16[4,12288]{1,0:T(4,128)(2,1)}, bf16[4,12288]{1,0:T(4,128)(2,1)S(1)}, u32[]{:S(2)}, u32[]{:S(2)}) collective-permute-start(bf16[4,12288]{1,0:T(4,128)(2,1)} %refs_3_), channel_id=1, source_target_pairs={{0,8},{1,9},{2,10},{3,11},{4,12},{5,13},{6,14},{7,15},{8,0},{9,1},... | collective-permute-start | bytes 294920 | tf_op jit(solution)/shard_map/ppermute | solution.py:193
  5.6 8.4 %collective-permute-start.2 = (bf16[4,12288]{1,0:T(4,128)(2,1)}, bf16[4,12288]{1,0:T(4,128)(2,1)S(1)}, u32[]{:S(2)}, u32[]{:S(2)}) collective-permute-start(bf16[4,12288]{1,0:T(4,128)(2,1)} %refs_3_), channel_id=1, source_target_pairs={{0,12},{1,13},{2,14},{3,15},{4,8},{5,9},{6,10},{7,11},{8,4},{9,5},... | collective-permute-start | bytes 294920 | tf_op jit(solution)/shard_map/ppermute | solution.py:193
  8.1 5.9 %collective-permute-start.3 = (bf16[4,12288]{1,0:T(4,128)(2,1)}, bf16[4,12288]{1,0:T(4,128)(2,1)S(1)}, u32[]{:S(2)}, u32[]{:S(2)}) collective-permute-start(bf16[4,12288]{1,0:T(4,128)(2,1)} %refs_3_), channel_id=1, source_target_pairs={{0,2},{1,3},{2,0},{3,1},{4,6},{5,7},{6,4},{7,5},{8,10},{9,11},{10,... | collective-permute-start | bytes 294920 | tf_op jit(solution)/shard_map/ppermute | solution.py:196
  9.9 5.2 %collective-permute-start.4 = (bf16[4,12288]{1,0:T(4,128)(2,1)S(1)}, bf16[4,12288]{1,0:T(4,128)(2,1)S(1)}, u32[]{:S(2)}, u32[]{:S(2)}) collective-permute-start(bf16[4,12288]{1,0:T(4,128)(2,1)S(1)} %collective-permute-done.refs_0_), channel_id=1, source_target_pairs={{0,2},{1,3},{2,0},{3,1},{4,6},{5,7},{6,4},{7,5},{8,10},{9,11},{10,... | collective-permute-start | bytes 294920 | tf_op jit(solution)/shard_map/ppermute | solution.py:196
  15.2 11.3 %collective-permute-start.10 = (bf16[128,12288]{1,0:T(8,128)(2,1)}, bf16[128,12288]{1,0:T(8,128)(2,1)S(1)}, u32[]{:S(2)}, u32[]{:S(2)}) collective-permute-start(bf16[128,12288]{1,0:T(8,128)(2,1)} %refs_2_), channel_id=1, source_target_pairs={{0,1},{1,0},{2,3},{3,2},{4,5},{5,4},{6,7},{7,6},{8,9},{9,8},{10,11... | collective-permute-start | bytes 9437192 | tf_op jit(solution)/shard_map/ppermute | solution.py:199
  15.2 7.0 %collective-permute-start.8 = (bf16[768,512]{1,0:T(8,128)(2,1)}, bf16[768,512]{1,0:T(8,128)(2,1)S(1)}, u32[]{:S(2)}, u32[]{:S(2)}) collective-permute-start(bf16[768,512]{1,0:T(8,128)(2,1)} %refs_0_), channel_id=1, source_target_pairs={{0,1},{1,0},{2,3},{3,2},{4,5},{5,4},{6,7},{7,6},{8,9},{9,8},{10,11... | collective-permute-start | bytes 2359304 | tf_op jit(solution)/shard_map/ppermute | solution.py:199
  17.2 4.9 %collective-permute-start.5 = (bf16[16,1536]{1,0:T(8,128)(2,1)S(1)}, bf16[16,1536]{1,0:T(8,128)(2,1)S(1)}, u32[]{:S(2)}, u32[]{:S(2)}) collective-permute-start(bf16[16,1536]{1,0:T(8,128)(2,1)S(1)} %get-tuple-element.58), channel_id=1, source_target_pairs={{0,2},{1,3},{2,0},{3,1},{4,6},{5,7},{6,4},{7,5},{8,10},{9,11},{10,... | collective-permute-start | bytes 147464 | tf_op jit(solution)/shard_map/ppermute | solution.py:196
  18.7 3.4 %collective-permute-start.7 = (f32[1,128]{1,0:T(1,128)}, f32[1,128]{1,0:T(1,128)S(1)}, u32[]{:S(2)}, u32[]{:S(2)}) collective-permute-start(f32[1,128]{1,0:T(1,128)} %bitcast.12), channel_id=1, source_target_pairs={{0,1},{1,0},{2,3},{3,2},{4,5},{5,4},{6,7},{7,6},{8,9},{9,8},{10,11... | collective-permute-start | bytes 1544 | tf_op jit(solution)/shard_map/ppermute | solution.py:199
  18.7 7.7 %copy-start.2 = (bf16[512,768]{1,0:T(8,128)(2,1)S(1)}, bf16[512,768]{1,0:T(8,128)(2,1)}, u32[]{:S(2)}) copy-start(bf16[512,768]{1,0:T(8,128)(2,1)} %refs_3_.1) | copy-start | bytes 2359300
  18.8 15.6 %copy-start.1 = (f32[128]{0:T(128)S(1)}, f32[128]{0:T(128)}, u32[]{:S(2)}) copy-start(f32[128]{0:T(128)} %param.19) | copy-start | bytes 1540
  22.5 3.9 %collective-permute-start.9 = (bf16[32,512]{1,0:T(8,128)(2,1)S(1)}, bf16[32,512]{1,0:T(8,128)(2,1)S(1)}, u32[]{:S(2)}, u32[]{:S(2)}) collective-permute-start(bf16[32,512]{1,0:T(8,128)(2,1)S(1)} %get-tuple-element.68), channel_id=1, source_target_pairs={{0,2},{1,3},{2,0},{3,1},{4,6},{5,7},{6,4},{7,5},{8,10},{9,11},{10,... | collective-permute-start | bytes 98312 | tf_op jit(solution)/shard_map/ppermute | solution.py:196
  26.5 10.5 %collective-permute-start.11 = (bf16[512,768]{1,0:T(8,128)(2,1)S(1)}, bf16[512,768]{1,0:T(8,128)(2,1)S(1)}, u32[]{:S(2)}, u32[]{:S(2)}) collective-permute-start(bf16[512,768]{1,0:T(8,128)(2,1)S(1)} %copy-done.2), channel_id=1, source_target_pairs={{0,1},{1,0},{2,3},{3,2},{4,5},{5,4},{6,7},{7,6},{8,9},{9,8},{10,11... | collective-permute-start | bytes 2359304 | tf_op jit(solution)/shard_map/ppermute | solution.py:199
  26.5 5.7 %collective-permute-start.12 = (bf16[4,12288]{1,0:T(4,128)(2,1)S(1)}, bf16[4,12288]{1,0:T(4,128)(2,1)S(1)}, u32[]{:S(2)}, u32[]{:S(2)}) collective-permute-start(bf16[4,12288]{1,0:T(4,128)(2,1)S(1)} %collective-permute-done.1.refs_1_), channel_id=1, source_target_pairs={{0,2},{1,3},{2,0},{3,1},{4,6},{5,7},{6,4},{7,5},{8,10},{9,11},{10,... | collective-permute-start | bytes 294920 | tf_op jit(solution)/shard_map/ppermute | solution.py:196
  28.0 5.7 %collective-permute-start.13 = (bf16[4,12288]{1,0:T(4,128)(2,1)S(1)}, bf16[4,12288]{1,0:T(4,128)(2,1)S(1)}, u32[]{:S(2)}, u32[]{:S(2)}) collective-permute-start(bf16[4,12288]{1,0:T(4,128)(2,1)S(1)} %collective-permute-done.2.refs_2_), channel_id=1, source_target_pairs={{0,2},{1,3},{2,0},{3,1},{4,6},{5,7},{6,4},{7,5},{8,10},{9,11},{10,... | collective-permute-start | bytes 294920 | tf_op jit(solution)/shard_map/ppermute | solution.py:196
  28.6 8.2 %collective-permute-start.14 = (bf16[32,512]{1,0:T(8,128)(2,1)S(1)}, bf16[32,512]{1,0:T(8,128)(2,1)S(1)}, u32[]{:S(2)}, u32[]{:S(2)}) collective-permute-start(bf16[32,512]{1,0:T(8,128)(2,1)S(1)} %get-tuple-element.87), channel_id=1, source_target_pairs={{0,12},{1,13},{2,14},{3,15},{4,8},{5,9},{6,10},{7,11},{8,4},{9,5},... | collective-permute-start | bytes 98312 | tf_op jit(solution)/shard_map/ppermute | solution.py:193
  32.2 4.8 %collective-permute-start.15 = (bf16[32,512]{1,0:T(8,128)(2,1)S(1)}, bf16[32,512]{1,0:T(8,128)(2,1)S(1)}, u32[]{:S(2)}, u32[]{:S(2)}) collective-permute-start(bf16[32,512]{1,0:T(8,128)(2,1)S(1)} %get-tuple-element.88), channel_id=1, source_target_pairs={{0,8},{1,9},{2,10},{3,11},{4,12},{5,13},{6,14},{7,15},{8,0},{9,1},... | collective-permute-start | bytes 98312 | tf_op jit(solution)/shard_map/ppermute | solution.py:193
  32.2 4.8 %collective-permute-start.16 = (bf16[32,512]{1,0:T(8,128)(2,1)S(1)}, bf16[32,512]{1,0:T(8,128)(2,1)S(1)}, u32[]{:S(2)}, u32[]{:S(2)}) collective-permute-start(bf16[32,512]{1,0:T(8,128)(2,1)S(1)} %get-tuple-element.89), channel_id=1, source_target_pairs={{0,4},{1,5},{2,6},{3,7},{4,0},{5,1},{6,2},{7,3},{8,12},{9,13},{10,... | collective-permute-start | bytes 98312 | tf_op jit(solution)/shard_map/ppermute | solution.py:193
  35.6 1.4 %copy-start = (f32[512]{0:T(512)S(1)}, f32[512]{0:T(512)}, u32[]{:S(2)}) copy-start(f32[512]{0:T(512)} %param.22) | copy-start | bytes 6148
  37.5 5.5 %collective-permute-start.17 = (bf16[4,12288]{1,0:T(4,128)(2,1)S(1)}, bf16[4,12288]{1,0:T(4,128)(2,1)S(1)}, u32[]{:S(2)}, u32[]{:S(2)}) collective-permute-start(bf16[4,12288]{1,0:T(4,128)(2,1)S(1)} %get-tuple-element.91), channel_id=1, source_target_pairs={{0,2},{1,3},{2,0},{3,1},{4,6},{5,7},{6,4},{7,5},{8,10},{9,11},{10,... | collective-permute-start | bytes 294920 | tf_op jit(solution)/shard_map/ppermute | solution.py:196
  39.0 8.9 %collective-permute-start.21 = (bf16[4,12288]{1,0:T(4,128)(2,1)S(1)}, bf16[4,12288]{1,0:T(4,128)(2,1)S(1)}, u32[]{:S(2)}, u32[]{:S(2)}) collective-permute-start(bf16[4,12288]{1,0:T(4,128)(2,1)S(1)} %get-tuple-element.98), channel_id=1, source_target_pairs={{0,2},{1,3},{2,0},{3,1},{4,6},{5,7},{6,4},{7,5},{8,10},{9,11},{10,... | collective-permute-start | bytes 294920 | tf_op jit(solution)/shard_map/ppermute | solution.py:196
  43.0 9.8 %collective-permute-start.23 = (bf16[4,12288]{1,0:T(4,128)(2,1)S(1)}, bf16[4,12288]{1,0:T(4,128)(2,1)S(1)}, u32[]{:S(2)}, u32[]{:S(2)}) collective-permute-start(bf16[4,12288]{1,0:T(4,128)(2,1)S(1)} %add_convert_fusion), channel_id=1, source_target_pairs={{0,12},{1,13},{2,14},{3,15},{4,8},{5,9},{6,10},{7,11},{8,4},{9,5},... | collective-permute-start | bytes 294920 | tf_op jit(solution)/shard_map/ppermute | solution.py:193
  46.6 4.6 %collective-permute-start.19 = (bf16[4,12288]{1,0:T(4,128)(2,1)S(1)}, bf16[4,12288]{1,0:T(4,128)(2,1)S(1)}, u32[]{:S(2)}, u32[]{:S(2)}) collective-permute-start(bf16[4,12288]{1,0:T(4,128)(2,1)S(1)} %get-tuple-element.96), channel_id=1, source_target_pairs={{0,2},{1,3},{2,0},{3,1},{4,6},{5,7},{6,4},{7,5},{8,10},{9,11},{10,... | collective-permute-start | bytes 294920 | tf_op jit(solution)/shard_map/ppermute | solution.py:196
  48.0 5.6 %collective-permute-start.22 = (bf16[4,12288]{1,0:T(4,128)(2,1)S(1)}, bf16[4,12288]{1,0:T(4,128)(2,1)S(1)}, u32[]{:S(2)}, u32[]{:S(2)}) collective-permute-start(bf16[4,12288]{1,0:T(4,128)(2,1)S(1)} %add_convert_fusion.1), channel_id=1, source_target_pairs={{0,8},{1,9},{2,10},{3,11},{4,12},{5,13},{6,14},{7,15},{8,0},{9,1},... | collective-permute-start | bytes 294920 | tf_op jit(solution)/shard_map/ppermute | solution.py:193
  48.1 4.7 %collective-permute-start.18 = (bf16[4,12288]{1,0:T(4,128)(2,1)S(1)}, bf16[4,12288]{1,0:T(4,128)(2,1)S(1)}, u32[]{:S(2)}, u32[]{:S(2)}) collective-permute-start(bf16[4,12288]{1,0:T(4,128)(2,1)S(1)} %get-tuple-element.94), channel_id=1, source_target_pairs={{0,2},{1,3},{2,0},{3,1},{4,6},{5,7},{6,4},{7,5},{8,10},{9,11},{10,... | collective-permute-start | bytes 294920 | tf_op jit(solution)/shard_map/ppermute | solution.py:196
  51.3 4.7 %collective-permute-start.20 = (bf16[4,12288]{1,0:T(4,128)(2,1)S(1)}, bf16[4,12288]{1,0:T(4,128)(2,1)S(1)}, u32[]{:S(2)}, u32[]{:S(2)}) collective-permute-start(bf16[4,12288]{1,0:T(4,128)(2,1)S(1)} %add_convert_fusion.2), channel_id=1, source_target_pairs={{0,4},{1,5},{2,6},{3,7},{4,0},{5,1},{6,2},{7,3},{8,12},{9,13},{10,... | collective-permute-start | bytes 294920 | tf_op jit(solution)/shard_map/ppermute | solution.py:193

commit v10 on v9

--- a/solution.py
+++ b/solution.py
@@ -214,12 +214,23 @@
 
     held = [hidden] + [across(hidden, k) for k in range(groups - 1, 0, -1)][::-1]
     w_in_mate = core(w_in)
-    first, _ = lax.optimization_barrier((hidden, held[1]))
+    near = (low_in, w_in, w_out, low_out)
+    *near, mask = lax.optimization_barrier((*near, mask))
+    loaded = call(
+        functools.partial(load_body, len(near)),
+        [shape(*x.shape, dtype=x.dtype) for x in near],
+        [HBM] * len(near),
+        16,
+        [pltpu.SemaphoreType.DMA((len(near),))],
+        8 * MIB,
+    )(*[pltpu.with_memory_space_constraint(x, pltpu.HBM) for x in near])
+    first, *loaded = lax.optimization_barrier((hidden, *loaded))
+    low_in_near, w_in, w_out_near, low_out_near = loaded
     beyond = [beside(first), beside(held[1])]
-    *_, w_in_mate, mask, low_in_sent, w_out_sent, bias_sent = lax.optimization_barrier(
-        (*held, *beyond, w_in_mate, mask, low_in, w_out, bias)
+    *_, w_in_mate, mask, low_in_sent, w_out_sent = lax.optimization_barrier(
+        (*held, *beyond, w_in_mate, mask, low_in, w_out)
     )
-    low_in_mate, bias_mate, w_out_mate = map(core, (low_in_sent, bias_sent, w_out_sent))
+    low_in_mate, w_out_mate = core(low_in_sent), core(w_out_sent)
 
     own, *beyond = lax.optimization_barrier((hidden, *beyond))
     normed, keep, send, gain, shift = call(
@@ -230,26 +241,16 @@
         [pltpu.VMEM((row_dev, width), bf16), pltpu.SemaphoreType.DMA((3,))],
         4 * MIB,
     )(place, *held[1:], *[pltpu.with_memory_space_constraint(x, pltpu.HBM) for x in (own, gain, shift)])
-    send, *late = lax.optimization_barrier((send, *held[2:]))
-    got, bias_mate = lax.optimization_barrier((beside(send), bias_mate))
+    send, bias_sent = lax.optimization_barrier((send, bias))
+    got, bias_mate, *late = lax.optimization_barrier((beside(send), core(bias_sent), *held[2:]))
     beyond = beyond + [beside(h) for h in late]
-    near = (low_in, w_in, w_out, low_out)
-    *near, keep = lax.optimization_barrier((*near, keep))
-    low_in_near, w_in, w_out_near, low_out_near = call(
-        functools.partial(load_body, len(near)),
-        [shape(*x.shape, dtype=x.dtype) for x in near],
-        [HBM] * len(near),
-        16,
-        [pltpu.SemaphoreType.DMA((len(near),))],
-        8 * MIB,
-    )(*[pltpu.with_memory_space_constraint(x, pltpu.HBM) for x in near])
     total, message = call(
         down_body, [shape(rows, rank, dtype=f32), shape(rows, rank)], [SMEM] + [VMEM] * 4, 16
     )(place, keep, got, low_in_near, low_in_mate)
     far = call(
         functools.partial(far_body, groups), [shape(some, width)], [VMEM] * (groups + 2), 16, (), 4 * MIB
     )(*beyond, gain, shift)[0]
-    got, low_out_sent, w_out_mate = lax.optimization_barrier((beside(message), low_out, w_out_mate))
+    got, low_out_sent, w_out_mate, *beyond = lax.optimization_barrier((beside(message), low_out, w_out_mate, *beyond))
     low_out_mate = core(low_out_sent)
     step = piece(width, 2048)
     act = call(
@@ -284,14 +285,15 @@
         6 * MIB,
     )(place, total, low_bias.reshape(1, rank), low_out_near, low_out_mate, part, *got)
 
-    sent, half = list(parts[groups:]), groups // 2
-    sums = [None] * groups
+    sums, here = [None] * groups, None
     for k in range(groups - 1, -1, -1):
-        come = beside(sent[k])
-        if k == groups - 1:
-            come, *sent[:half] = lax.optimization_barrier((come, *sent[:half]))
+        come = beside(parts[groups + k])
+        if here is not None:
+            come, here = lax.optimization_barrier((come, here))
+            sums[k + 1] = across(here, k + 1)
         here = parts[k] + come.astype(f32)
-        sums[k] = across(here.astype(bf16), k) if k else here
+        here = here.astype(bf16) if k else here
+    sums[0] = here
     return call(functools.partial(last_body, groups), [shape(row_dev, width)], [VMEM] * groups, 16)(*sums)[0]
 
 

time: 56.9 us -> 64.3 us (1.13)
  waiting for transfers between devices: 18.3 us -> 25 us
    ppermute x5, waiting for transfers between devices: 0.07 us -> 3.23 us  [core(): return lax.ppermute(x, 'blk', [(i, i ^ 1) for i in range(devices)])]
    ppermute x10, waiting for transfers between devices: 11.5 us -> 14.5 us  [beside(): return lax.ppermute(x, 'blk', [(i, i ^ 2) for i in range(devices)])]
    ppermute x9, starting transfers between devices: 13.4 us -> 14.1 us  [across(): return lax.ppermute(x, 'blk', [(i, i ^ 4 * k) for i in range(devices)])]
  transfers between devices with their start and end apart: 24 -> 24, of which waited for: 12 -> 11; matrix products, arithmetic and copies ran while one was open for 5% -> 5% of each run, Pallas kernels for 14% -> 13%
where the time goes in v10:
time: 64.3 us; the launch traced here: 64.1 us
  starting transfers between devices  26.4 us (41%)
  waiting for transfers between devices  25 us (39%)
  Pallas kernels  9.41 us (15%)
  other arithmetic  2.25 us (3%)
  local copies, waits for them, and re-layouts  0.89 us (1%)
    ppermute x10, waiting for transfers between devices, beside(): return lax.ppermute(x, 'blk', [(i, i ^ 2) for i in range(devices)])  14.5 us
    ppermute x9, starting transfers between devices, across(): return lax.ppermute(x, 'blk', [(i, i ^ 4 * k) for i in range(devices)])  14.1 us
    ppermute x10, starting transfers between devices, beside(): return lax.ppermute(x, 'blk', [(i, i ^ 2) for i in range(devices)])  11.3 us
    ppermute x9, waiting for transfers between devices, across(): return lax.ppermute(x, 'blk', [(i, i ^ 4 * k) for i in range(devices)])  7.28 us
    pallas_call x1, Pallas kernels, shards(): call(functools.partial(load_body, len(near)), [shape(*x.shape, dtype=x.dt...  3.4 us
    ppermute x5, waiting for transfers between devices, core(): return lax.ppermute(x, 'blk', [(i, i ^ 1) for i in range(devices)])  3.23 us
    pallas_call x1, Pallas kernels, shards(): call(functools.partial(near_body, groups), [shape(some, width), shape(som...  1.49 us
  transfers between devices with their start and end apart: 24, of which 11 were waited for; matrix products, arithmetic and copies ran while one was open for 5% of the time, Pallas kernels for 13%

profile of v10, /device:TPU:0, one launch (start us, length us, event | category | flops | bytes accessed | tf_op | source)
XLA Modules:
  0.0 64.1 jit_solution(10295890651409768576)
XLA Ops:
  0.5 4.6 %collective-permute-start.2 = (bf16[4,12288]{1,0:T(4,128)(2,1)}, bf16[4,12288]{1,0:T(4,128)(2,1)S(1)}, u32[]{:S(2)}, u32[]{:S(2)}) collective-permute-start(bf16[4,12288]{1,0:T(4,128)(2,1)} %refs_3_.1), channel_id=1, source_target_pairs={{0,12},{1,13},{2,14},{3,15},{4,8},{5,9},{6,10},{7,11},{8,4},{9,5},... | collective-permute-start | bytes 294920 | tf_op jit(solution)/shard_map/ppermute | solution.py:193
  5.1 0.6 collective-permute-start
  5.7 0.8 %copy.13 = s32[4,6]{0,1:T(8,128)S(1)} copy(s32[4,6]{1,0:T(4,128)} %param.15) | data formatting | bytes 192 | tf_op args[3]
  6.5 0.7 %fusion.1 = s32[4,6]{0,1:T(8,128)S(1)} fusion(s32[4]{0:T(128)} %param.16), kind=kLoop, calls=%fused_computation.12 | loop fusion | flops 48 | bytes 112 | tf_op jit(solution)/shard_map/convert_element_type | solution.py:160
  7.2 0.7 %fusion = s32[16,16]{1,0:T(8,128)S(1)} fusion(s32[16]{0:T(128)} %param.17), kind=kLoop, calls=%fused_computation.10 | loop fusion | flops 512 | bytes 1088 | tf_op jit(solution)/shard_map/convert_element_type | solution.py:163
  8.6 3.4 %shard_map.118 = (bf16[768,512]{1,0:T(8,128)(2,1)S(1)}, bf16[12288,128]{1,0:T(8,128)(2,1)S(1)}, bf16[128,12288]{1,0:T(8,128)(2,1)S(1)}, bf16[512,768]{1,0:T(8,128)(2,1)S(1)}) custom-call(bf16[768,512]{1,0:T(8,128)(2,1)} %refs_0_, bf16[12288,128]{1,0:T(8,128)(2,1)} %refs_1_, bf16[128,12288]{1,0:T(8,128)(2,1)} %refs_2_, bf16[512,768]{1,0:T(8,128)(2,1)} %refs_3_), custom_call_target="tpu_custom_call" | custom-call | bytes 8388608 | tf_op jit(solution)/shard_map/pallas_call | solution.py:219
  12.1 1.7 %collective-permute-start.3 = (bf16[4,12288]{1,0:T(4,128)(2,1)S(1)}, bf16[4,12288]{1,0:T(4,128)(2,1)S(1)}, u32[]{:S(2)}, u32[]{:S(2)}) collective-permute-start(bf16[4,12288]{1,0:T(4,128)(2,1)S(1)} %copy-done.5), channel_id=1, source_target_pairs={{0,2},{1,3},{2,0},{3,1},{4,6},{5,7},{6,4},{7,5},{8,10},{9,11},{10,... | collective-permute-start | bytes 294920 | tf_op jit(solution)/shard_map/ppermute | solution.py:196
  14.2 3.4 %collective-permute-done.3.refs_0_ = bf16[4,12288]{1,0:T(4,128)(2,1)S(1)} collective-permute-done((bf16[4,12288]{1,0:T(4,128)(2,1)S(1)}, bf16[4,12288]{1,0:T(4,128)(2,1)S(1)}, u32[]{:S(2)}, u32[]{:S(2)}) %collective-permute-start.3) | collective-permute-done | bytes 98336 | tf_op jit(solution)/shard_map/ppermute | solution.py:196
  17.6 1.2 %collective-permute-done.4.refs_1_ = bf16[4,12288]{1,0:T(4,128)(2,1)S(1)} collective-permute-done((bf16[4,12288]{1,0:T(4,128)(2,1)S(1)}, bf16[4,12288]{1,0:T(4,128)(2,1)S(1)}, u32[]{:S(2)}, u32[]{:S(2)}) %collective-permute-start.4) | collective-permute-done | bytes 98336 | tf_op jit(solution)/shard_map/ppermute | solution.py:196
  19.4 1.5 %shard_map.119 = (bf16[16,12288]{1,0:T(8,128)(2,1)S(1)}, bf16[16,1536]{1,0:T(8,128)(2,1)S(1)}, bf16[16,1536]{1,0:T(8,128)(2,1)S(1)}, f32[1,12288]{1,0:T(1,128)S(1)}, f32[1,12288]{1,0:T(1,128)S(1)}) custom-call(s32[1]{0:T(128)} %bitcast.place, bf16[4,12288]{1,0:T(4,128)(2,1)S(1)} %collective-permute-done.refs_0_, ...), custom_call_target="tpu_custom_call" | custom-call | bytes 4194304 | tf_op jit(solution)/shard_map/pallas_call | solution.py:236
  20.9 1.5 %collective-permute-start.5 = (bf16[16,1536]{1,0:T(8,128)(2,1)S(1)}, bf16[16,1536]{1,0:T(8,128)(2,1)S(1)}, u32[]{:S(2)}, u32[]{:S(2)}) collective-permute-start(bf16[16,1536]{1,0:T(8,128)(2,1)S(1)} %get-tuple-element.72), channel_id=1, source_target_pairs={{0,2},{1,3},{2,0},{3,1},{4,6},{5,7},{6,4},{7,5},{8,10},{9,11},{10,... | collective-permute-start | bytes 147464 | tf_op jit(solution)/shard_map/ppermute | solution.py:196
  22.4 3.2 %collective-permute-done.6.b_mate = f32[1,128]{1,0:T(1,128)S(1)} collective-permute-done((f32[1,128]{1,0:T(1,128)S(1)}, f32[1,128]{1,0:T(1,128)S(1)}, u32[]{:S(2)}, u32[]{:S(2)}) %collective-permute-start.6) | collective-permute-done | bytes 544 | tf_op jit(solution)/shard_map/ppermute | solution.py:199
  25.6 1.5 %collective-permute-start.11 = (bf16[4,12288]{1,0:T(4,128)(2,1)S(1)}, bf16[4,12288]{1,0:T(4,128)(2,1)S(1)}, u32[]{:S(2)}, u32[]{:S(2)}) collective-permute-start(bf16[4,12288]{1,0:T(4,128)(2,1)S(1)} %collective-permute-done.1.refs_1_), channel_id=1, source_target_pairs={{0,2},{1,3},{2,0},{3,1},{4,6},{5,7},{6,4},{7,5},{8,10},{9,11},{10,... | collective-permute-start | bytes 294920 | tf_op jit(solution)/shard_map/ppermute | solution.py:196
  28.0 1.5 %collective-permute-start.9 = (bf16[32,512]{1,0:T(8,128)(2,1)S(1)}, bf16[32,512]{1,0:T(8,128)(2,1)S(1)}, u32[]{:S(2)}, u32[]{:S(2)}) collective-permute-start(bf16[32,512]{1,0:T(8,128)(2,1)S(1)} %get-tuple-element.79), channel_id=1, source_target_pairs={{0,2},{1,3},{2,0},{3,1},{4,6},{5,7},{6,4},{7,5},{8,10},{9,11},{10,... | collective-permute-start | bytes 98312 | tf_op jit(solution)/shard_map/ppermute | solution.py:196
  29.5 1.7 %collective-permute-done.11.refs_2_ = bf16[4,12288]{1,0:T(4,128)(2,1)S(1)} collective-permute-done((bf16[4,12288]{1,0:T(4,128)(2,1)S(1)}, bf16[4,12288]{1,0:T(4,128)(2,1)S(1)}, u32[]{:S(2)}, u32[]{:S(2)}) %collective-permute-start.11) | collective-permute-done | bytes 98336 | tf_op jit(solution)/shard_map/ppermute | solution.py:196
  31.3 1.7 %collective-permute-done.12.refs_3_ = bf16[4,12288]{1,0:T(4,128)(2,1)S(1)} collective-permute-done((bf16[4,12288]{1,0:T(4,128)(2,1)S(1)}, bf16[4,12288]{1,0:T(4,128)(2,1)S(1)}, u32[]{:S(2)}, u32[]{:S(2)}) %collective-permute-start.12) | collective-permute-done | bytes 98336 | tf_op jit(solution)/shard_map/ppermute | solution.py:196
  33.3 3.8 %collective-permute-start.14 = (bf16[32,512]{1,0:T(8,128)(2,1)S(1)}, bf16[32,512]{1,0:T(8,128)(2,1)S(1)}, u32[]{:S(2)}, u32[]{:S(2)}) collective-permute-start(bf16[32,512]{1,0:T(8,128)(2,1)S(1)} %get-tuple-element.98), channel_id=1, source_target_pairs={{0,12},{1,13},{2,14},{3,15},{4,8},{5,9},{6,10},{7,11},{8,4},{9,5},... | collective-permute-start | bytes 98312 | tf_op jit(solution)/shard_map/ppermute | solution.py:193
  37.1 0.7 %collective-permute-start.16 = (bf16[32,512]{1,0:T(8,128)(2,1)S(1)}, bf16[32,512]{1,0:T(8,128)(2,1)S(1)}, u32[]{:S(2)}, u32[]{:S(2)}) collective-permute-start(bf16[32,512]{1,0:T(8,128)(2,1)S(1)} %get-tuple-element.100), channel_id=1, source_target_pairs={{0,4},{1,5},{2,6},{3,7},{4,0},{5,1},{6,2},{7,3},{8,12},{9,13},{10,... | collective-permute-start | bytes 98312 | tf_op jit(solution)/shard_map/ppermute | solution.py:193
  38.4 1.2 %shard_map.123.act = bf16[32,256]{1,0:T(8,128)(2,1)S(1)} custom-call(bf16[16,12288]{1,0:T(8,128)(2,1)S(1)} %get-tuple-element.89.near, bf16[16,12288]{1,0:T(8,128)(2,1)S(1)} %shard_map.122.far, bf16[12288,128]{1,0:T(8,128)(2,1)S(1)} %get-tuple-element.92.w_own, bf16[12288,128]{1,0:T(8,128)(2,1)S(1)} %collective-permute-done.7.w_mate, f32[1,128]{1,0:T(1,128)S(1)} %bitcast.13, ...), custom_call_target="tpu_custom_call" | custom-call | bytes 4194304 | tf_op jit(solution)/shard_map/pallas_call | solution.py:256
  39.6 1.2 %shard_map.124.part = f32[32,12288]{1,0:T(8,128)S(1)} custom-call(bf16[32,256]{1,0:T(8,128)(2,1)S(1)} %shard_map.123.act, bf16[128,12288]{1,0:T(8,128)(2,1)S(1)} %get-tuple-element.96.w_own, bf16[128,12288]{1,0:T(8,128)(2,1)S(1)} %collective-permute-done.10.w_mate), custom_call_target="tpu_custom_call" | custom-call | bytes 6291456 | tf_op jit(solution)/shard_map/pallas_call | solution.py:271
  40.8 1.1 %collective-permute-done.15.refs_1_ = bf16[32,512]{1,0:T(8,128)(2,1)S(1)} collective-permute-done((bf16[32,512]{1,0:T(8,128)(2,1)S(1)}, bf16[32,512]{1,0:T(8,128)(2,1)S(1)}, u32[]{:S(2)}, u32[]{:S(2)}) %collective-permute-start.15) | collective-permute-done | bytes 32800 | tf_op jit(solution)/shard_map/ppermute | solution.py:193
  42.4 1.4 %collective-permute-start.20 = (bf16[4,12288]{1,0:T(4,128)(2,1)S(1)}, bf16[4,12288]{1,0:T(4,128)(2,1)S(1)}, u32[]{:S(2)}, u32[]{:S(2)}) collective-permute-start(bf16[4,12288]{1,0:T(4,128)(2,1)S(1)} %get-tuple-element.108), channel_id=1, source_target_pairs={{0,2},{1,3},{2,0},{3,1},{4,6},{5,7},{6,4},{7,5},{8,10},{9,11},{10,... | collective-permute-start | bytes 294920 | tf_op jit(solution)/shard_map/ppermute | solution.py:196
  43.8 0.7 %collective-permute-start.17 = (bf16[4,12288]{1,0:T(4,128)(2,1)S(1)}, bf16[4,12288]{1,0:T(4,128)(2,1)S(1)}, u32[]{:S(2)}, u32[]{:S(2)}) collective-permute-start(bf16[4,12288]{1,0:T(4,128)(2,1)S(1)} %get-tuple-element.102), channel_id=1, source_target_pairs={{0,2},{1,3},{2,0},{3,1},{4,6},{5,7},{6,4},{7,5},{8,10},{9,11},{10,... | collective-permute-start | bytes 294920 | tf_op jit(solution)/shard_map/ppermute | solution.py:196
  44.5 1.3 %collective-permute-start.18 = (bf16[4,12288]{1,0:T(4,128)(2,1)S(1)}, bf16[4,12288]{1,0:T(4,128)(2,1)S(1)}, u32[]{:S(2)}, u32[]{:S(2)}) collective-permute-start(bf16[4,12288]{1,0:T(4,128)(2,1)S(1)} %get-tuple-element.104), channel_id=1, source_target_pairs={{0,2},{1,3},{2,0},{3,1},{4,6},{5,7},{6,4},{7,5},{8,10},{9,11},{10,... | collective-permute-start | bytes 294920 | tf_op jit(solution)/shard_map/ppermute | solution.py:196
  45.8 0.7 %collective-permute-start.19 = (bf16[4,12288]{1,0:T(4,128)(2,1)S(1)}, bf16[4,12288]{1,0:T(4,128)(2,1)S(1)}, u32[]{:S(2)}, u32[]{:S(2)}) collective-permute-start(bf16[4,12288]{1,0:T(4,128)(2,1)S(1)} %get-tuple-element.106), channel_id=1, source_target_pairs={{0,2},{1,3},{2,0},{3,1},{4,6},{5,7},{6,4},{7,5},{8,10},{9,11},{10,... | collective-permute-start | bytes 294920 | tf_op jit(solution)/shard_map/ppermute | solution.py:196
  46.5 1.7 %collective-permute-done.20 = bf16[4,12288]{1,0:T(4,128)(2,1)S(1)} collective-permute-done((bf16[4,12288]{1,0:T(4,128)(2,1)S(1)}, bf16[4,12288]{1,0:T(4,128)(2,1)S(1)}, u32[]{:S(2)}, u32[]{:S(2)}) %collective-permute-start.20) | collective-permute-done | bytes 98336 | tf_op jit(solution)/shard_map/ppermute | solution.py:196
  48.2 4.4 %collective-permute-done.19 = bf16[4,12288]{1,0:T(4,128)(2,1)S(1)} collective-permute-done((bf16[4,12288]{1,0:T(4,128)(2,1)S(1)}, bf16[4,12288]{1,0:T(4,128)(2,1)S(1)}, u32[]{:S(2)}, u32[]{:S(2)}) %collective-permute-start.19) | collective-permute-done | bytes 98336 | tf_op jit(solution)/shard_map/ppermute | solution.py:196
  52.8 1.1 %collective-permute-start.21 = (bf16[4,12288]{1,0:T(4,128)(2,1)S(1)}, bf16[4,12288]{1,0:T(4,128)(2,1)S(1)}, u32[]{:S(2)}, u32[]{:S(2)}) collective-permute-start(bf16[4,12288]{1,0:T(4,128)(2,1)S(1)} %add_convert_fusion), channel_id=1, source_target_pairs={{0,4},{1,5},{2,6},{3,7},{4,0},{5,1},{6,2},{7,3},{8,12},{9,13},{10,... | collective-permute-start | bytes 294920 | tf_op jit(solution)/shard_map/ppermute | solution.py:193
  53.9 2.6 %collective-permute-start.22 = (bf16[4,12288]{1,0:T(4,128)(2,1)S(1)}, bf16[4,12288]{1,0:T(4,128)(2,1)S(1)}, u32[]{:S(2)}, u32[]{:S(2)}) collective-permute-start(bf16[4,12288]{1,0:T(4,128)(2,1)S(1)} %add_convert_fusion.1), channel_id=1, source_target_pairs={{0,8},{1,9},{2,10},{3,11},{4,12},{5,13},{6,14},{7,15},{8,0},{9,1},... | collective-permute-start | bytes 294920 | tf_op jit(solution)/shard_map/ppermute | solution.py:193
  56.5 0.7 %collective-permute-start.23 = (bf16[4,12288]{1,0:T(4,128)(2,1)S(1)}, bf16[4,12288]{1,0:T(4,128)(2,1)S(1)}, u32[]{:S(2)}, u32[]{:S(2)}) collective-permute-start(bf16[4,12288]{1,0:T(4,128)(2,1)S(1)} %add_convert_fusion.2), channel_id=1, source_target_pairs={{0,12},{1,13},{2,14},{3,15},{4,8},{5,9},{6,10},{7,11},{8,4},{9,5},... | collective-permute-start | bytes 294920 | tf_op jit(solution)/shard_map/ppermute | solution.py:193
  57.8 5.6 %collective-permute-done.22.refs_2_ = bf16[4,12288]{1,0:T(4,128)(2,1)S(1)} collective-permute-done((bf16[4,12288]{1,0:T(4,128)(2,1)S(1)}, bf16[4,12288]{1,0:T(4,128)(2,1)S(1)}, u32[]{:S(2)}, u32[]{:S(2)}) %collective-permute-start.22) | collective-permute-done | bytes 98336 | tf_op jit(solution)/shard_map/ppermute | solution.py:193
  63.4 0.7 %shard_map.126 = bf16[4,12288]{1,0:T(4,128)(2,1)} custom-call(f32[4,12288]{1,0:T(4,128)S(1)} %convert_add_fusion.refs_0_, bf16[4,12288]{1,0:T(4,128)(2,1)S(1)} %collective-permute-done.21.refs_1_, bf16[4,12288]{1,0:T(4,128)(2,1)S(1)} %collective-permute-done.22.refs_2_, bf16[4,12288]{1,0:T(4,128)(2,1)S(1)} %collective-permute-done.23.refs_3_), custom_call_target="tpu_custom_call" | custom-call | bytes 2097152 | tf_op jit(solution)/shard_map/pallas_call | solution.py:297
  (54 shorter events, 5.2 us)
Async XLA Ops:
  0.0 18.8 %collective-permute-start.7 = (bf16[12288,128]{1,0:T(8,128)(2,1)}, bf16[12288,128]{1,0:T(8,128)(2,1)S(1)}, u32[]{:S(2)}, u32[]{:S(2)}) collective-permute-start(bf16[12288,128]{1,0:T(8,128)(2,1)} %refs_1_), channel_id=1, source_target_pairs={{0,1},{1,0},{2,3},{3,2},{4,5},{5,4},{6,7},{7,6},{8,9},{9,8},{10,11... | collective-permute-start | bytes 9437192 | tf_op jit(solution)/shard_map/ppermute | solution.py:199
  0.5 13.7 %collective-permute-start.2 = (bf16[4,12288]{1,0:T(4,128)(2,1)}, bf16[4,12288]{1,0:T(4,128)(2,1)S(1)}, u32[]{:S(2)}, u32[]{:S(2)}) collective-permute-start(bf16[4,12288]{1,0:T(4,128)(2,1)} %refs_3_.1), channel_id=1, source_target_pairs={{0,12},{1,13},{2,14},{3,15},{4,8},{5,9},{6,10},{7,11},{8,4},{9,5},... | collective-permute-start | bytes 294920 | tf_op jit(solution)/shard_map/ppermute | solution.py:193
  5.1 9.1 %collective-permute-start.1 = (bf16[4,12288]{1,0:T(4,128)(2,1)}, bf16[4,12288]{1,0:T(4,128)(2,1)S(1)}, u32[]{:S(2)}, u32[]{:S(2)}) collective-permute-start(bf16[4,12288]{1,0:T(4,128)(2,1)} %refs_3_.1), channel_id=1, source_target_pairs={{0,8},{1,9},{2,10},{3,11},{4,12},{5,13},{6,14},{7,15},{8,0},{9,1},... | collective-permute-start | bytes 294920 | tf_op jit(solution)/shard_map/ppermute | solution.py:193
  5.1 8.7 %collective-permute-start = (bf16[4,12288]{1,0:T(4,128)(2,1)}, bf16[4,12288]{1,0:T(4,128)(2,1)S(1)}, u32[]{:S(2)}, u32[]{:S(2)}) collective-permute-start(bf16[4,12288]{1,0:T(4,128)(2,1)} %refs_3_.1), channel_id=1, source_target_pairs={{0,4},{1,5},{2,6},{3,7},{4,0},{5,1},{6,2},{7,3},{8,12},{9,13},{10,... | collective-permute-start | bytes 294920 | tf_op jit(solution)/shard_map/ppermute | solution.py:193
  8.6 3.5 %copy-start.5 = (bf16[4,12288]{1,0:T(4,128)(2,1)S(1)}, bf16[4,12288]{1,0:T(4,128)(2,1)}, u32[]{:S(2)}) copy-start(bf16[4,12288]{1,0:T(4,128)(2,1)} %refs_3_.1) | copy-start | bytes 294916
  8.6 10.3 %copy-start.2 = (bf16[128,12288]{1,0:T(8,128)(2,1)S(1)}, bf16[128,12288]{1,0:T(8,128)(2,1)}, u32[]{:S(2)}) copy-start(bf16[128,12288]{1,0:T(8,128)(2,1)} %refs_2_) | copy-start | bytes 9437188
  8.6 10.3 %copy-start.3 = (bf16[768,512]{1,0:T(8,128)(2,1)S(1)}, bf16[768,512]{1,0:T(8,128)(2,1)}, u32[]{:S(2)}) copy-start(bf16[768,512]{1,0:T(8,128)(2,1)} %refs_0_) | copy-start | bytes 2359300
  8.6 13.8 %copy-start.1 = (f32[128]{0:T(128)S(1)}, f32[128]{0:T(128)}, u32[]{:S(2)}) copy-start(f32[128]{0:T(128)} %param.19) | copy-start | bytes 1540
  8.6 24.7 %copy-start.4 = (bf16[512,768]{1,0:T(8,128)(2,1)S(1)}, bf16[512,768]{1,0:T(8,128)(2,1)}, u32[]{:S(2)}) copy-start(bf16[512,768]{1,0:T(8,128)(2,1)} %refs_3_) | copy-start | bytes 2359300
  12.1 5.6 %collective-permute-start.3 = (bf16[4,12288]{1,0:T(4,128)(2,1)S(1)}, bf16[4,12288]{1,0:T(4,128)(2,1)S(1)}, u32[]{:S(2)}, u32[]{:S(2)}) collective-permute-start(bf16[4,12288]{1,0:T(4,128)(2,1)S(1)} %copy-done.5), channel_id=1, source_target_pairs={{0,2},{1,3},{2,0},{3,1},{4,6},{5,7},{6,4},{7,5},{8,10},{9,11},{10,... | collective-permute-start | bytes 294920 | tf_op jit(solution)/shard_map/ppermute | solution.py:196
  13.8 5.0 %collective-permute-start.4 = (bf16[4,12288]{1,0:T(4,128)(2,1)S(1)}, bf16[4,12288]{1,0:T(4,128)(2,1)S(1)}, u32[]{:S(2)}, u32[]{:S(2)}) collective-permute-start(bf16[4,12288]{1,0:T(4,128)(2,1)S(1)} %collective-permute-done.refs_0_), channel_id=1, source_target_pairs={{0,2},{1,3},{2,0},{3,1},{4,6},{5,7},{6,4},{7,5},{8,10},{9,11},{10,... | collective-permute-start | bytes 294920 | tf_op jit(solution)/shard_map/ppermute | solution.py:196
  18.8 14.4 %collective-permute-start.10 = (bf16[128,12288]{1,0:T(8,128)(2,1)S(1)}, bf16[128,12288]{1,0:T(8,128)(2,1)S(1)}, u32[]{:S(2)}, u32[]{:S(2)}) collective-permute-start(bf16[128,12288]{1,0:T(8,128)(2,1)S(1)} %copy-done.2), channel_id=1, source_target_pairs={{0,1},{1,0},{2,3},{3,2},{4,5},{5,4},{6,7},{7,6},{8,9},{9,8},{10,11... | collective-permute-start | bytes 9437192 | tf_op jit(solution)/shard_map/ppermute | solution.py:199
  18.9 8.8 %collective-permute-start.8 = (bf16[768,512]{1,0:T(8,128)(2,1)S(1)}, bf16[768,512]{1,0:T(8,128)(2,1)S(1)}, u32[]{:S(2)}, u32[]{:S(2)}) collective-permute-start(bf16[768,512]{1,0:T(8,128)(2,1)S(1)} %copy-done.3), channel_id=1, source_target_pairs={{0,1},{1,0},{2,3},{3,2},{4,5},{5,4},{6,7},{7,6},{8,9},{9,8},{10,11... | collective-permute-start | bytes 2359304 | tf_op jit(solution)/shard_map/ppermute | solution.py:199
  20.9 4.8 %collective-permute-start.5 = (bf16[16,1536]{1,0:T(8,128)(2,1)S(1)}, bf16[16,1536]{1,0:T(8,128)(2,1)S(1)}, u32[]{:S(2)}, u32[]{:S(2)}) collective-permute-start(bf16[16,1536]{1,0:T(8,128)(2,1)S(1)} %get-tuple-element.72), channel_id=1, source_target_pairs={{0,2},{1,3},{2,0},{3,1},{4,6},{5,7},{6,4},{7,5},{8,10},{9,11},{10,... | collective-permute-start | bytes 147464 | tf_op jit(solution)/shard_map/ppermute | solution.py:196
  22.4 3.2 %collective-permute-start.6 = (f32[1,128]{1,0:T(1,128)S(1)}, f32[1,128]{1,0:T(1,128)S(1)}, u32[]{:S(2)}, u32[]{:S(2)}) collective-permute-start(f32[1,128]{1,0:T(1,128)S(1)} %bitcast.12), channel_id=1, source_target_pairs={{0,1},{1,0},{2,3},{3,2},{4,5},{5,4},{6,7},{7,6},{8,9},{9,8},{10,11... | collective-permute-start | bytes 1544 | tf_op jit(solution)/shard_map/ppermute | solution.py:199
  25.6 5.6 %collective-permute-start.11 = (bf16[4,12288]{1,0:T(4,128)(2,1)S(1)}, bf16[4,12288]{1,0:T(4,128)(2,1)S(1)}, u32[]{:S(2)}, u32[]{:S(2)}) collective-permute-start(bf16[4,12288]{1,0:T(4,128)(2,1)S(1)} %collective-permute-done.1.refs_1_), channel_id=1, source_target_pairs={{0,2},{1,3},{2,0},{3,1},{4,6},{5,7},{6,4},{7,5},{8,10},{9,11},{10,... | collective-permute-start | bytes 294920 | tf_op jit(solution)/shard_map/ppermute | solution.py:196
  27.1 5.8 %collective-permute-start.12 = (bf16[4,12288]{1,0:T(4,128)(2,1)S(1)}, bf16[4,12288]{1,0:T(4,128)(2,1)S(1)}, u32[]{:S(2)}, u32[]{:S(2)}) collective-permute-start(bf16[4,12288]{1,0:T(4,128)(2,1)S(1)} %collective-permute-done.2.refs_2_), channel_id=1, source_target_pairs={{0,2},{1,3},{2,0},{3,1},{4,6},{5,7},{6,4},{7,5},{8,10},{9,11},{10,... | collective-permute-start | bytes 294920 | tf_op jit(solution)/shard_map/ppermute | solution.py:196
  28.0 5.3 %collective-permute-start.9 = (bf16[32,512]{1,0:T(8,128)(2,1)S(1)}, bf16[32,512]{1,0:T(8,128)(2,1)S(1)}, u32[]{:S(2)}, u32[]{:S(2)}) collective-permute-start(bf16[32,512]{1,0:T(8,128)(2,1)S(1)} %get-tuple-element.79), channel_id=1, source_target_pairs={{0,2},{1,3},{2,0},{3,1},{4,6},{5,7},{6,4},{7,5},{8,10},{9,11},{10,... | collective-permute-start | bytes 98312 | tf_op jit(solution)/shard_map/ppermute | solution.py:196
  33.3 8.6 %collective-permute-start.13 = (bf16[512,768]{1,0:T(8,128)(2,1)S(1)}, bf16[512,768]{1,0:T(8,128)(2,1)S(1)}, u32[]{:S(2)}, u32[]{:S(2)}) collective-permute-start(bf16[512,768]{1,0:T(8,128)(2,1)S(1)} %copy-done.4), channel_id=1, source_target_pairs={{0,1},{1,0},{2,3},{3,2},{4,5},{5,4},{6,7},{7,6},{8,9},{9,8},{10,11... | collective-permute-start | bytes 2359304 | tf_op jit(solution)/shard_map/ppermute | solution.py:199
  33.3 7.5 %collective-permute-start.14 = (bf16[32,512]{1,0:T(8,128)(2,1)S(1)}, bf16[32,512]{1,0:T(8,128)(2,1)S(1)}, u32[]{:S(2)}, u32[]{:S(2)}) collective-permute-start(bf16[32,512]{1,0:T(8,128)(2,1)S(1)} %get-tuple-element.98), channel_id=1, source_target_pairs={{0,12},{1,13},{2,14},{3,15},{4,8},{5,9},{6,10},{7,11},{8,4},{9,5},... | collective-permute-start | bytes 98312 | tf_op jit(solution)/shard_map/ppermute | solution.py:193
  37.1 4.8 %collective-permute-start.15 = (bf16[32,512]{1,0:T(8,128)(2,1)S(1)}, bf16[32,512]{1,0:T(8,128)(2,1)S(1)}, u32[]{:S(2)}, u32[]{:S(2)}) collective-permute-start(bf16[32,512]{1,0:T(8,128)(2,1)S(1)} %get-tuple-element.99), channel_id=1, source_target_pairs={{0,8},{1,9},{2,10},{3,11},{4,12},{5,13},{6,14},{7,15},{8,0},{9,1},... | collective-permute-start | bytes 98312 | tf_op jit(solution)/shard_map/ppermute | solution.py:193
  37.1 4.8 %collective-permute-start.16 = (bf16[32,512]{1,0:T(8,128)(2,1)S(1)}, bf16[32,512]{1,0:T(8,128)(2,1)S(1)}, u32[]{:S(2)}, u32[]{:S(2)}) collective-permute-start(bf16[32,512]{1,0:T(8,128)(2,1)S(1)} %get-tuple-element.100), channel_id=1, source_target_pairs={{0,4},{1,5},{2,6},{3,7},{4,0},{5,1},{6,2},{7,3},{8,12},{9,13},{10,... | collective-permute-start | bytes 98312 | tf_op jit(solution)/shard_map/ppermute | solution.py:193
  39.6 2.3 %copy-start = (f32[512]{0:T(512)S(1)}, f32[512]{0:T(512)}, u32[]{:S(2)}) copy-start(f32[512]{0:T(512)} %param.22) | copy-start | bytes 6148
  42.4 5.8 %collective-permute-start.20 = (bf16[4,12288]{1,0:T(4,128)(2,1)S(1)}, bf16[4,12288]{1,0:T(4,128)(2,1)S(1)}, u32[]{:S(2)}, u32[]{:S(2)}) collective-permute-start(bf16[4,12288]{1,0:T(4,128)(2,1)S(1)} %get-tuple-element.108), channel_id=1, source_target_pairs={{0,2},{1,3},{2,0},{3,1},{4,6},{5,7},{6,4},{7,5},{8,10},{9,11},{10,... | collective-permute-start | bytes 294920 | tf_op jit(solution)/shard_map/ppermute | solution.py:196
  43.8 9.0 %collective-permute-start.17 = (bf16[4,12288]{1,0:T(4,128)(2,1)S(1)}, bf16[4,12288]{1,0:T(4,128)(2,1)S(1)}, u32[]{:S(2)}, u32[]{:S(2)}) collective-permute-start(bf16[4,12288]{1,0:T(4,128)(2,1)S(1)} %get-tuple-element.102), channel_id=1, source_target_pairs={{0,2},{1,3},{2,0},{3,1},{4,6},{5,7},{6,4},{7,5},{8,10},{9,11},{10,... | collective-permute-start | bytes 294920 | tf_op jit(solution)/shard_map/ppermute | solution.py:196
  44.5 8.2 %collective-permute-start.18 = (bf16[4,12288]{1,0:T(4,128)(2,1)S(1)}, bf16[4,12288]{1,0:T(4,128)(2,1)S(1)}, u32[]{:S(2)}, u32[]{:S(2)}) collective-permute-start(bf16[4,12288]{1,0:T(4,128)(2,1)S(1)} %get-tuple-element.104), channel_id=1, source_target_pairs={{0,2},{1,3},{2,0},{3,1},{4,6},{5,7},{6,4},{7,5},{8,10},{9,11},{10,... | collective-permute-start | bytes 294920 | tf_op jit(solution)/shard_map/ppermute | solution.py:196
  45.8 6.8 %collective-permute-start.19 = (bf16[4,12288]{1,0:T(4,128)(2,1)S(1)}, bf16[4,12288]{1,0:T(4,128)(2,1)S(1)}, u32[]{:S(2)}, u32[]{:S(2)}) collective-permute-start(bf16[4,12288]{1,0:T(4,128)(2,1)S(1)} %get-tuple-element.106), channel_id=1, source_target_pairs={{0,2},{1,3},{2,0},{3,1},{4,6},{5,7},{6,4},{7,5},{8,10},{9,11},{10,... | collective-permute-start | bytes 294920 | tf_op jit(solution)/shard_map/ppermute | solution.py:196
  52.8 5.0 %collective-permute-start.21 = (bf16[4,12288]{1,0:T(4,128)(2,1)S(1)}, bf16[4,12288]{1,0:T(4,128)(2,1)S(1)}, u32[]{:S(2)}, u32[]{:S(2)}) collective-permute-start(bf16[4,12288]{1,0:T(4,128)(2,1)S(1)} %add_convert_fusion), channel_id=1, source_target_pairs={{0,4},{1,5},{2,6},{3,7},{4,0},{5,1},{6,2},{7,3},{8,12},{9,13},{10,... | collective-permute-start | bytes 294920 | tf_op jit(solution)/shard_map/ppermute | solution.py:193
  53.9 9.5 %collective-permute-start.22 = (bf16[4,12288]{1,0:T(4,128)(2,1)S(1)}, bf16[4,12288]{1,0:T(4,128)(2,1)S(1)}, u32[]{:S(2)}, u32[]{:S(2)}) collective-permute-start(bf16[4,12288]{1,0:T(4,128)(2,1)S(1)} %add_convert_fusion.1), channel_id=1, source_target_pairs={{0,8},{1,9},{2,10},{3,11},{4,12},{5,13},{6,14},{7,15},{8,0},{9,1},... | collective-permute-start | bytes 294920 | tf_op jit(solution)/shard_map/ppermute | solution.py:193
  56.5 6.9 %collective-permute-start.23 = (bf16[4,12288]{1,0:T(4,128)(2,1)S(1)}, bf16[4,12288]{1,0:T(4,128)(2,1)S(1)}, u32[]{:S(2)}, u32[]{:S(2)}) collective-permute-start(bf16[4,12288]{1,0:T(4,128)(2,1)S(1)} %add_convert_fusion.2), channel_id=1, source_target_pairs={{0,12},{1,13},{2,14},{3,15},{4,8},{5,9},{6,10},{7,11},{8,4},{9,5},... | collective-permute-start | bytes 294920 | tf_op jit(solution)/shard_map/ppermute | solution.py:193

commit v11 on v7

--- a/solution.py
+++ b/solution.py
@@ -63,8 +63,8 @@
             out[i * rows : i * rows + pair.shape[0], :] = normal(pair, gain[...], shift[...])
 
 
-def norm_body(count, place, *refs):
-    held, (near, first, gain, shift, own, mate, far, total, message) = refs[:count], refs[count:]
+def norm_body(groups, count, step, place, *refs):
+    held, (near, first, gain, shift, own, mate, far, total, *messages) = refs[:count], refs[count:]
     rows, done = held[0].shape[0], first.shape[0]
     far[:done, :] = first[...]
     for i in range(0, count, 2):
@@ -80,27 +80,39 @@
     sums = jnp.dot(mine, own[...], preferred_element_type=f32) + jnp.dot(
         other, mate[...], preferred_element_type=f32
     )
-    half = near.shape[0]
+    write(sums, groups, step, total, messages)
+
+
+def stages(groups):
+    bits = [(1, 0)]
+    while 1 << (len(bits) - 1) < groups:
+        bits.append((0, 1 << (len(bits) - 1)))
+    steps = []
+    for i in range(0, len(bits), 2):
+        step = list(bits[i : i + 2])
+        if len(step) == 2:
+            step.append((step[0][0] ^ step[1][0], step[0][1] ^ step[1][1]))
+        steps.append(step)
+    return steps
+
+
+def write(sums, groups, step, total, messages):
     total[...] = sums
-    message[:half, :] = sums[half:].astype(bf16)
-    message[half:, :] = sums[:half].astype(bf16)
-
-
-def turn(x, groups, bit):
-    rows = x.shape[0] // (2 * groups)
-    at = [h * groups + (k ^ bit) for h in range(2) for k in range(groups)]
-    return jnp.concatenate([x[i * rows : (i + 1) * rows] for i in at], axis=0)
-
-
-def merge_body(groups, total, got, out, *messages):
-    sums = total[...] + got[...].astype(f32)
-    out[...] = sums
-    for k in range(1, groups):
-        messages[k - 1][...] = turn(sums, groups, k).astype(bf16)
-
-
-def up_body(groups, place, total, bias, own, mate, part, *refs):
-    got, outs = refs[: groups - 1], refs[groups - 1 :]
+    rows = sums.shape[0] // (2 * groups)
+    for (other, offset), message in zip(step, messages):
+        at = [(h ^ other) * groups + (k ^ offset) for h in range(2) for k in range(groups)]
+        message[...] = jnp.concatenate([sums[i * rows : (i + 1) * rows] for i in at], axis=0).astype(bf16)
+
+
+def merge_body(groups, count, step, *refs):
+    sums = refs[0][...]
+    for got in refs[1 : count + 1]:
+        sums = sums + got[...].astype(f32)
+    write(sums, groups, step, refs[count + 1], refs[count + 2 :])
+
+
+def up_body(groups, count, place, total, bias, own, mate, part, *refs):
+    got, outs = refs[:count], refs[count:]
     sums = total[...]
     for g in got:
         sums = sums + g[...].astype(f32)
@@ -202,7 +214,7 @@
     live = jnp.sum(jnp.where(relate & choose, table[None, None], 0), axis=(2, 3)).astype(f32)
     mask = jnp.broadcast_to(live[None, :, None, :, None], (2, groups, row_dev, 2, block)).reshape(rows, 2 * block)
 
-    held = [hidden] + [across(hidden, k) for k in range(1, groups)]
+    held = [hidden] + [across(hidden, k) for k in range(groups - 1, 0, -1)][::-1]
     w_in_mate = core(w_in)
     held[1], low_in_sent, mask = lax.optimization_barrier((held[1], low_in, mask))
     low_in_mate = core(low_in_sent)
@@ -233,15 +245,21 @@
         (),
         4 * MIB,
     )(*held, *beyond[:soon], gain, shift)
-    far, total, message = call(
-        functools.partial(norm_body, groups - soon),
-        [shape(some, width), shape(rows, rank, dtype=f32), shape(rows, rank)],
+    steps = stages(groups)
+    far, total, *messages = call(
+        functools.partial(norm_body, groups, groups - soon, steps[0]),
+        [shape(some, width), shape(rows, rank, dtype=f32)] + [shape(rows, rank)] * len(steps[0]),
         [SMEM] + [VMEM] * (groups - soon + 6),
         16,
         (),
         4 * MIB,
     )(place, *beyond[soon:], normed, first, gain, shift, low_in, low_in_mate)
-    got = beside(message)
+
+    def swap(xs, step):
+        pairs = [[(i, i ^ (2 * other) ^ (4 * offset)) for i in range(devices)] for other, offset in step]
+        return [lax.ppermute(x, "blk", p) for x, p in zip(xs, pairs)]
+
+    got = swap(messages, steps[0])
     step = piece(width, 2048)
     act = call(
         functools.partial(act_body, step),
@@ -251,13 +269,14 @@
         (),
         4 * MIB,
     )(normed, far, w_in, w_in_mate, bias, bias_mate, mask)[0]
-    total, *messages = call(
-        functools.partial(merge_body, groups),
-        [shape(rows, rank, dtype=f32)] + [shape(rows, rank)] * (groups - 1),
-        [VMEM] * 2,
-        16,
-    )(total, got)
-    got = [across(messages[k - 1], k) for k in range(1, groups)]
+    for before, after in zip(steps, steps[1:]):
+        total, *messages = call(
+            functools.partial(merge_body, groups, len(before), after),
+            [shape(rows, rank, dtype=f32)] + [shape(rows, rank)] * len(after),
+            [VMEM] * (1 + len(before)),
+            16,
+        )(total, *got)
+        got = swap(messages, after)
     part = call(
         functools.partial(part_body, step),
         [shape(rows, width, dtype=f32)],
@@ -267,9 +286,9 @@
         6 * MIB,
     )(act, w_out_near, w_out_mate)[0]
     parts = call(
-        functools.partial(up_body, groups),
+        functools.partial(up_body, groups, len(got)),
         [shape(row_dev, width, dtype=f32)] * groups + [shape(row_dev, width)] * groups,
-        [SMEM] + [VMEM] * (groups + 4),
+        [SMEM] + [VMEM] * (len(got) + 5),
         16,
         (),
         6 * MIB,

time: 52.6 us -> 54.5 us (1.036)
  starting transfers between devices: 23.5 us -> 24.5 us
  waiting for transfers between devices: 17.2 us -> 17.9 us
    ppermute x0 -> x4, starting transfers between devices: none -> 5.52 us  [swap(): return [lax.ppermute(x, 'blk', p) for x, p in zip(xs, pairs)]]
    ppermute x0 -> x4, waiting for transfers between devices: none -> 3.83 us  [swap(): return [lax.ppermute(x, 'blk', p) for x, p in zip(xs, pairs)]]
    ppermute x9 -> x6, starting transfers between devices: 13.6 us -> 9.88 us  [across(): return lax.ppermute(x, 'blk', [(i, i ^ 4 * k) for i in range(devices)])]
    ppermute x9 -> x8, waiting for transfers between devices: 6.09 us -> 3.49 us  [beside(): return lax.ppermute(x, 'blk', [(i, i ^ 2) for i in range(devices)])]
    ppermute x9 -> x6, waiting for transfers between devices: 11.1 us -> 9.49 us  [across(): return lax.ppermute(x, 'blk', [(i, i ^ 4 * k) for i in range(devices)])]
    ppermute x5, waiting for transfers between devices: 0.01 us -> 1.13 us  [core(): return lax.ppermute(x, 'blk', [(i, i ^ 1) for i in range(devices)])]
    ppermute x9 -> x8, starting transfers between devices: 8.72 us -> 8.02 us  [beside(): return lax.ppermute(x, 'blk', [(i, i ^ 2) for i in range(devices)])]
  transfers between devices with their start and end apart: 23 -> 23, of which waited for: 9 -> 12; matrix products, arithmetic and copies ran while one was open for 6% -> 6% of each run, Pallas kernels for 14% -> 14%
where the time goes in v11:
time: 54.5 us; the launch traced here: 54.3 us
  starting transfers between devices  24.5 us (45%)
  waiting for transfers between devices  17.9 us (33%)
  Pallas kernels  8.58 us (16%)
  other arithmetic  2.23 us (4%)
  local copies, waits for them, and re-layouts  0.86 us (2%)
    ppermute x6, starting transfers between devices, across(): return lax.ppermute(x, 'blk', [(i, i ^ 4 * k) for i in range(devices)])  9.88 us
    ppermute x6, waiting for transfers between devices, across(): return lax.ppermute(x, 'blk', [(i, i ^ 4 * k) for i in range(devices)])  9.49 us
    ppermute x8, starting transfers between devices, beside(): return lax.ppermute(x, 'blk', [(i, i ^ 2) for i in range(devices)])  8.02 us
    ppermute x4, starting transfers between devices, swap(): return [lax.ppermute(x, 'blk', p) for x, p in zip(xs, pairs)]  5.52 us
    ppermute x4, waiting for transfers between devices, swap(): return [lax.ppermute(x, 'blk', p) for x, p in zip(xs, pairs)]  3.83 us
    ppermute x8, waiting for transfers between devices, beside(): return lax.ppermute(x, 'blk', [(i, i ^ 2) for i in range(devices)])  3.49 us
    pallas_call x1, Pallas kernels, shards(): call(functools.partial(load_body, len(near)), [shape(*x.shape, dtype=x.dt...  3.39 us
    pallas_call x1, Pallas kernels, shards(): call(functools.partial(part_body, step), [shape(rows, width, dtype=f32)],...  1.2 us
  transfers between devices with their start and end apart: 23, of which 12 were waited for; matrix products, arithmetic and copies ran while one was open for 6% of the time, Pallas kernels for 14%

profile of v11, /device:TPU:0, one launch (start us, length us, event | category | flops | bytes accessed | tf_op | source)
XLA Modules:
  0.0 54.3 jit_solution(4556052868466358577)
XLA Ops:
  0.5 2.6 %collective-permute-start.4 = (bf16[4,12288]{1,0:T(4,128)(2,1)}, bf16[4,12288]{1,0:T(4,128)(2,1)S(1)}, u32[]{:S(2)}, u32[]{:S(2)}) collective-permute-start(bf16[4,12288]{1,0:T(4,128)(2,1)} %refs_0_), channel_id=1, source_target_pairs={{0,4},{1,5},{2,6},{3,7},{4,0},{5,1},{6,2},{7,3},{8,12},{9,13},{10,... | collective-permute-start | bytes 294920 | tf_op jit(solution)/shard_map/ppermute | solution.py:195
  3.0 1.5 %collective-permute-start.5 = (bf16[4,12288]{1,0:T(4,128)(2,1)}, bf16[4,12288]{1,0:T(4,128)(2,1)S(1)}, u32[]{:S(2)}, u32[]{:S(2)}) collective-permute-start(bf16[4,12288]{1,0:T(4,128)(2,1)} %refs_0_), channel_id=1, source_target_pairs={{0,2},{1,3},{2,0},{3,1},{4,6},{5,7},{6,4},{7,5},{8,10},{9,11},{10,... | collective-permute-start | bytes 294920 | tf_op jit(solution)/shard_map/ppermute | solution.py:198
  4.5 2.6 %collective-permute-start = (bf16[4,12288]{1,0:T(4,128)(2,1)}, bf16[4,12288]{1,0:T(4,128)(2,1)S(1)}, u32[]{:S(2)}, u32[]{:S(2)}) collective-permute-start(bf16[4,12288]{1,0:T(4,128)(2,1)} %refs_0_), channel_id=1, source_target_pairs={{0,8},{1,9},{2,10},{3,11},{4,12},{5,13},{6,14},{7,15},{8,0},{9,1},... | collective-permute-start | bytes 294920 | tf_op jit(solution)/shard_map/ppermute | solution.py:195
  7.4 0.8 %copy.13 = s32[4,6]{0,1:T(8,128)S(1)} copy(s32[4,6]{1,0:T(4,128)} %param.15) | data formatting | bytes 192 | tf_op args[3]
  8.1 0.7 %fusion.1 = s32[4,6]{0,1:T(8,128)S(1)} fusion(s32[4]{0:T(128)} %param.16), kind=kLoop, calls=%fused_computation.12 | loop fusion | flops 48 | bytes 112 | tf_op jit(solution)/shard_map/convert_element_type | solution.py:162
  8.9 0.7 %fusion = s32[16,16]{1,0:T(8,128)S(1)} fusion(s32[16]{0:T(128)} %param.17), kind=kLoop, calls=%fused_computation.10 | loop fusion | flops 512 | bytes 1088 | tf_op jit(solution)/shard_map/convert_element_type | solution.py:165
  10.6 4.6 %collective-permute-done.refs_2_ = bf16[4,12288]{1,0:T(4,128)(2,1)S(1)} collective-permute-done((bf16[4,12288]{1,0:T(4,128)(2,1)}, bf16[4,12288]{1,0:T(4,128)(2,1)S(1)}, u32[]{:S(2)}, u32[]{:S(2)}) %collective-permute-start) | collective-permute-done | bytes 98336 | tf_op jit(solution)/shard_map/ppermute | solution.py:195
  15.9 0.7 %collective-permute-start.1 = (bf16[4,12288]{1,0:T(4,128)(2,1)S(1)}, bf16[4,12288]{1,0:T(4,128)(2,1)S(1)}, u32[]{:S(2)}, u32[]{:S(2)}) collective-permute-start(bf16[4,12288]{1,0:T(4,128)(2,1)S(1)} %collective-permute-done.refs_2_), channel_id=1, source_target_pairs={{0,2},{1,3},{2,0},{3,1},{4,6},{5,7},{6,4},{7,5},{8,10},{9,11},{10,... | collective-permute-start | bytes 294920 | tf_op jit(solution)/shard_map/ppermute | solution.py:198
  16.5 1.3 %collective-permute-start.3 = (bf16[4,12288]{1,0:T(4,128)(2,1)S(1)}, bf16[4,12288]{1,0:T(4,128)(2,1)S(1)}, u32[]{:S(2)}, u32[]{:S(2)}) collective-permute-start(bf16[4,12288]{1,0:T(4,128)(2,1)S(1)} %collective-permute-done.2.refs_3_), channel_id=1, source_target_pairs={{0,2},{1,3},{2,0},{3,1},{4,6},{5,7},{6,4},{7,5},{8,10},{9,11},{10,... | collective-permute-start | bytes 294920 | tf_op jit(solution)/shard_map/ppermute | solution.py:198
  17.9 3.4 %shard_map.118 = (bf16[4,12288]{1,0:T(4,128)(2,1)S(1)}, f32[1,12288]{1,0:T(1,128)S(1)}, f32[1,12288]{1,0:T(1,128)S(1)}, bf16[768,512]{1,0:T(8,128)(2,1)S(1)}, bf...) custom-call(bf16[4,12288]{1,0:T(4,128)(2,1)} %refs_0_, ...), custom_call_target="tpu_custom_call" | custom-call | bytes 8388608 | tf_op jit(solution)/shard_map/pallas_call | solution.py:224
  21.3 0.8 %shard_map.119 = (bf16[16,12288]{1,0:T(8,128)(2,1)S(1)}, bf16[8,12288]{1,0:T(8,128)(2,1)S(1)}) custom-call(bf16[4,12288]{1,0:T(4,128)(2,1)S(1)} %get-tuple-element.53.refs_0_, bf16[4,12288]{1,0:T(4,128)(2,1)S(1)} %collective-permute-done.4.refs_1_, bf16[4,12288]{1,0:T(4,128)(2,1)S(1)} %collective-permute-done.refs_2_, ...), custom_call_target="tpu_custom_call" | custom-call | bytes 4194304 | tf_op jit(solution)/shard_map/pallas_call | solution.py:240
  22.1 1.0 %collective-permute-done.3.refs_1_ = bf16[4,12288]{1,0:T(4,128)(2,1)S(1)} collective-permute-done((bf16[4,12288]{1,0:T(4,128)(2,1)S(1)}, bf16[4,12288]{1,0:T(4,128)(2,1)S(1)}, u32[]{:S(2)}, u32[]{:S(2)}) %collective-permute-start.3) | collective-permute-done | bytes 98336 | tf_op jit(solution)/shard_map/ppermute | solution.py:198
  23.1 0.8 %shard_map.120 = (bf16[16,12288]{1,0:T(8,128)(2,1)S(1)}, f32[32,512]{1,0:T(8,128)S(1)}, bf16[32,512]{1,0:T(8,128)(2,1)S(1)}, bf16[32,512]{1,0:T(8,128)(2,1)S(1)}, bf16[32,512]{1,0:T(8,128)(2,1)S(1)}) custom-call(s32[1]{0:T(128)} %bitcast.place, bf16[4,12288]{1,0:T(4,128)(2,1)S(1)} %collective-permute-done.1.refs_0_, ...), custom_call_target="tpu_custom_call" | custom-call | bytes 4194304 | tf_op jit(solution)/shard_map/pallas_call | solution.py:249
  23.9 1.9 %collective-permute-start.10 = (bf16[32,512]{1,0:T(8,128)(2,1)S(1)}, bf16[32,512]{1,0:T(8,128)(2,1)S(1)}, u32[]{:S(2)}, u32[]{:S(2)}) collective-permute-start(bf16[32,512]{1,0:T(8,128)(2,1)S(1)} %get-tuple-element.65), channel_id=1, source_target_pairs={{0,6},{1,7},{2,4},{3,5},{4,2},{5,3},{6,0},{7,1},{8,14},{9,15},{10,... | collective-permute-start | bytes 98312 | tf_op jit(solution)/shard_map/ppermute | solution.py:260
  25.9 1.5 %collective-permute-start.8 = (bf16[32,512]{1,0:T(8,128)(2,1)S(1)}, bf16[32,512]{1,0:T(8,128)(2,1)S(1)}, u32[]{:S(2)}, u32[]{:S(2)}) collective-permute-start(bf16[32,512]{1,0:T(8,128)(2,1)S(1)} %get-tuple-element.63), channel_id=1, source_target_pairs={{0,2},{1,3},{2,0},{3,1},{4,6},{5,7},{6,4},{7,5},{8,10},{9,11},{10,... | collective-permute-start | bytes 98312 | tf_op jit(solution)/shard_map/ppermute | solution.py:260
  27.5 1.3 %collective-permute-done.10.refs_3_ = bf16[32,512]{1,0:T(8,128)(2,1)S(1)} collective-permute-done((bf16[32,512]{1,0:T(8,128)(2,1)S(1)}, bf16[32,512]{1,0:T(8,128)(2,1)S(1)}, u32[]{:S(2)}, u32[]{:S(2)}) %collective-permute-start.10) | collective-permute-done | bytes 32800 | tf_op jit(solution)/shard_map/ppermute | solution.py:260
  28.8 1.0 %collective-permute-done.8.refs_1_ = bf16[32,512]{1,0:T(8,128)(2,1)S(1)} collective-permute-done((bf16[32,512]{1,0:T(8,128)(2,1)S(1)}, bf16[32,512]{1,0:T(8,128)(2,1)S(1)}, u32[]{:S(2)}, u32[]{:S(2)}) %collective-permute-start.8) | collective-permute-done | bytes 32800 | tf_op jit(solution)/shard_map/ppermute | solution.py:260
  29.8 1.5 %collective-permute-done.9.refs_2_ = bf16[32,512]{1,0:T(8,128)(2,1)S(1)} collective-permute-done((bf16[32,512]{1,0:T(8,128)(2,1)S(1)}, bf16[32,512]{1,0:T(8,128)(2,1)S(1)}, u32[]{:S(2)}, u32[]{:S(2)}) %collective-permute-start.9) | collective-permute-done | bytes 32800 | tf_op jit(solution)/shard_map/ppermute | solution.py:260
  31.3 2.0 %collective-permute-start.15 = (bf16[32,512]{1,0:T(8,128)(2,1)S(1)}, bf16[32,512]{1,0:T(8,128)(2,1)S(1)}, u32[]{:S(2)}, u32[]{:S(2)}) collective-permute-start(bf16[32,512]{1,0:T(8,128)(2,1)S(1)} %get-tuple-element.76), channel_id=1, source_target_pairs={{0,8},{1,9},{2,10},{3,11},{4,12},{5,13},{6,14},{7,15},{8,0},{9,1},... | collective-permute-start | bytes 98312 | tf_op jit(solution)/shard_map/ppermute | solution.py:260
  33.3 1.1 %collective-permute-done.13.b_mate = f32[1,128]{1,0:T(1,128)S(1)} collective-permute-done((f32[1,128]{1,0:T(1,128)S(1)}, f32[1,128]{1,0:T(1,128)S(1)}, u32[]{:S(2)}, u32[]{:S(2)}) %collective-permute-start.13) | collective-permute-done | bytes 544 | tf_op jit(solution)/shard_map/ppermute | solution.py:201
  34.4 1.2 %shard_map.122.act = bf16[32,256]{1,0:T(8,128)(2,1)S(1)} custom-call(bf16[16,12288]{1,0:T(8,128)(2,1)S(1)} %get-tuple-element.58.refs_2_.near, bf16[16,12288]{1,0:T(8,128)(2,1)S(1)} %get-tuple-element.69.far, bf16[12288,128]{1,0:T(8,128)(2,1)S(1)} %get-tuple-element.70.w_own, bf16[12288,128]{1,0:T(8,128)(2,1)S(1)} %collective-permute-done.11.w_mate, ...), custom_call_target="tpu_custom_call" | custom-call | bytes 4194304 | tf_op jit(solution)/shard_map/pallas_call | solution.py:264
  35.6 1.2 %shard_map.123.part = f32[32,12288]{1,0:T(8,128)S(1)} custom-call(bf16[32,256]{1,0:T(8,128)(2,1)S(1)} %shard_map.122.act, bf16[128,12288]{1,0:T(8,128)(2,1)S(1)} %get-tuple-element.74.w_own, bf16[128,12288]{1,0:T(8,128)(2,1)S(1)} %collective-permute-done.14.w_mate), custom_call_target="tpu_custom_call" | custom-call | bytes 6291456 | tf_op jit(solution)/shard_map/pallas_call | solution.py:280
  37.9 1.5 %collective-permute-start.19 = (bf16[4,12288]{1,0:T(4,128)(2,1)S(1)}, bf16[4,12288]{1,0:T(4,128)(2,1)S(1)}, u32[]{:S(2)}, u32[]{:S(2)}) collective-permute-start(bf16[4,12288]{1,0:T(4,128)(2,1)S(1)} %get-tuple-element.82), channel_id=1, source_target_pairs={{0,2},{1,3},{2,0},{3,1},{4,6},{5,7},{6,4},{7,5},{8,10},{9,11},{10,... | collective-permute-start | bytes 294920 | tf_op jit(solution)/shard_map/ppermute | solution.py:198
  39.9 1.5 %collective-permute-start.16 = (bf16[4,12288]{1,0:T(4,128)(2,1)S(1)}, bf16[4,12288]{1,0:T(4,128)(2,1)S(1)}, u32[]{:S(2)}, u32[]{:S(2)}) collective-permute-start(bf16[4,12288]{1,0:T(4,128)(2,1)S(1)} %get-tuple-element.78), channel_id=1, source_target_pairs={{0,2},{1,3},{2,0},{3,1},{4,6},{5,7},{6,4},{7,5},{8,10},{9,11},{10,... | collective-permute-start | bytes 294920 | tf_op jit(solution)/shard_map/ppermute | solution.py:198
  41.4 1.6 %collective-permute-done.21 = bf16[4,12288]{1,0:T(4,128)(2,1)S(1)} collective-permute-done((bf16[4,12288]{1,0:T(4,128)(2,1)S(1)}, bf16[4,12288]{1,0:T(4,128)(2,1)S(1)}, u32[]{:S(2)}, u32[]{:S(2)}) %collective-permute-start.21) | collective-permute-done | bytes 98336 | tf_op jit(solution)/shard_map/ppermute | solution.py:198
  43.1 2.0 %collective-permute-start.22 = (bf16[4,12288]{1,0:T(4,128)(2,1)S(1)}, bf16[4,12288]{1,0:T(4,128)(2,1)S(1)}, u32[]{:S(2)}, u32[]{:S(2)}) collective-permute-start(bf16[4,12288]{1,0:T(4,128)(2,1)S(1)} %add_convert_fusion), channel_id=1, source_target_pairs={{0,12},{1,13},{2,14},{3,15},{4,8},{5,9},{6,10},{7,11},{8,4},{9,5},... | collective-permute-start | bytes 294920 | tf_op jit(solution)/shard_map/ppermute | solution.py:195
  45.2 1.3 %collective-permute-start.20 = (bf16[4,12288]{1,0:T(4,128)(2,1)S(1)}, bf16[4,12288]{1,0:T(4,128)(2,1)S(1)}, u32[]{:S(2)}, u32[]{:S(2)}) collective-permute-start(bf16[4,12288]{1,0:T(4,128)(2,1)S(1)} %add_convert_fusion.1), channel_id=1, source_target_pairs={{0,8},{1,9},{2,10},{3,11},{4,12},{5,13},{6,14},{7,15},{8,0},{9,1},... | collective-permute-start | bytes 294920 | tf_op jit(solution)/shard_map/ppermute | solution.py:195
  46.5 0.7 %collective-permute-done.17 = bf16[4,12288]{1,0:T(4,128)(2,1)S(1)} collective-permute-done((bf16[4,12288]{1,0:T(4,128)(2,1)S(1)}, bf16[4,12288]{1,0:T(4,128)(2,1)S(1)}, u32[]{:S(2)}, u32[]{:S(2)}) %collective-permute-start.17) | collective-permute-done | bytes 98336 | tf_op jit(solution)/shard_map/ppermute | solution.py:198
  47.3 1.2 %collective-permute-start.18 = (bf16[4,12288]{1,0:T(4,128)(2,1)S(1)}, bf16[4,12288]{1,0:T(4,128)(2,1)S(1)}, u32[]{:S(2)}, u32[]{:S(2)}) collective-permute-start(bf16[4,12288]{1,0:T(4,128)(2,1)S(1)} %add_convert_fusion.2), channel_id=1, source_target_pairs={{0,4},{1,5},{2,6},{3,7},{4,0},{5,1},{6,2},{7,3},{8,12},{9,13},{10,... | collective-permute-start | bytes 294920 | tf_op jit(solution)/shard_map/ppermute | solution.py:195
  48.7 1.9 %collective-permute-done.22.refs_3_ = bf16[4,12288]{1,0:T(4,128)(2,1)S(1)} collective-permute-done((bf16[4,12288]{1,0:T(4,128)(2,1)S(1)}, bf16[4,12288]{1,0:T(4,128)(2,1)S(1)}, u32[]{:S(2)}, u32[]{:S(2)}) %collective-permute-start.22) | collective-permute-done | bytes 98336 | tf_op jit(solution)/shard_map/ppermute | solution.py:195
  50.6 3.0 %collective-permute-done.20.refs_2_ = bf16[4,12288]{1,0:T(4,128)(2,1)S(1)} collective-permute-done((bf16[4,12288]{1,0:T(4,128)(2,1)S(1)}, bf16[4,12288]{1,0:T(4,128)(2,1)S(1)}, u32[]{:S(2)}, u32[]{:S(2)}) %collective-permute-start.20) | collective-permute-done | bytes 98336 | tf_op jit(solution)/shard_map/ppermute | solution.py:195
  53.6 0.7 %shard_map.125 = bf16[4,12288]{1,0:T(4,128)(2,1)} custom-call(f32[4,12288]{1,0:T(4,128)S(1)} %convert_add_fusion.refs_0_, bf16[4,12288]{1,0:T(4,128)(2,1)S(1)} %collective-permute-done.18.refs_1_, bf16[4,12288]{1,0:T(4,128)(2,1)S(1)} %collective-permute-done.20.refs_2_, bf16[4,12288]{1,0:T(4,128)(2,1)S(1)} %collective-permute-done.22.refs_3_), custom_call_target="tpu_custom_call" | custom-call | bytes 2097152 | tf_op jit(solution)/shard_map/pallas_call | solution.py:301
  (43 shorter events, 4.5 us)
Async XLA Ops:
  0.0 15.2 %collective-permute-start.11 = (bf16[12288,128]{1,0:T(8,128)(2,1)}, bf16[12288,128]{1,0:T(8,128)(2,1)S(1)}, u32[]{:S(2)}, u32[]{:S(2)}) collective-permute-start(bf16[12288,128]{1,0:T(8,128)(2,1)} %refs_4_), channel_id=1, source_target_pairs={{0,1},{1,0},{2,3},{3,2},{4,5},{5,4},{6,7},{7,6},{8,9},{9,8},{10,11... | collective-permute-start | bytes 9437192 | tf_op jit(solution)/shard_map/ppermute | solution.py:201
  0.5 9.8 %collective-permute-start.4 = (bf16[4,12288]{1,0:T(4,128)(2,1)}, bf16[4,12288]{1,0:T(4,128)(2,1)S(1)}, u32[]{:S(2)}, u32[]{:S(2)}) collective-permute-start(bf16[4,12288]{1,0:T(4,128)(2,1)} %refs_0_), channel_id=1, source_target_pairs={{0,4},{1,5},{2,6},{3,7},{4,0},{5,1},{6,2},{7,3},{8,12},{9,13},{10,... | collective-permute-start | bytes 294920 | tf_op jit(solution)/shard_map/ppermute | solution.py:195
  3.0 7.6 %collective-permute-start.5 = (bf16[4,12288]{1,0:T(4,128)(2,1)}, bf16[4,12288]{1,0:T(4,128)(2,1)S(1)}, u32[]{:S(2)}, u32[]{:S(2)}) collective-permute-start(bf16[4,12288]{1,0:T(4,128)(2,1)} %refs_0_), channel_id=1, source_target_pairs={{0,2},{1,3},{2,0},{3,1},{4,6},{5,7},{6,4},{7,5},{8,10},{9,11},{10,... | collective-permute-start | bytes 294920 | tf_op jit(solution)/shard_map/ppermute | solution.py:198
  4.5 10.6 %collective-permute-start = (bf16[4,12288]{1,0:T(4,128)(2,1)}, bf16[4,12288]{1,0:T(4,128)(2,1)S(1)}, u32[]{:S(2)}, u32[]{:S(2)}) collective-permute-start(bf16[4,12288]{1,0:T(4,128)(2,1)} %refs_0_), channel_id=1, source_target_pairs={{0,8},{1,9},{2,10},{3,11},{4,12},{5,13},{6,14},{7,15},{8,0},{9,1},... | collective-permute-start | bytes 294920 | tf_op jit(solution)/shard_map/ppermute | solution.py:195
  7.1 8.0 %collective-permute-start.2 = (bf16[4,12288]{1,0:T(4,128)(2,1)}, bf16[4,12288]{1,0:T(4,128)(2,1)S(1)}, u32[]{:S(2)}, u32[]{:S(2)}) collective-permute-start(bf16[4,12288]{1,0:T(4,128)(2,1)} %refs_0_), channel_id=1, source_target_pairs={{0,12},{1,13},{2,14},{3,15},{4,8},{5,9},{6,10},{7,11},{8,4},{9,5},... | collective-permute-start | bytes 294920 | tf_op jit(solution)/shard_map/ppermute | solution.py:195
  10.3 4.9 %collective-permute-start.6 = (bf16[4,12288]{1,0:T(4,128)(2,1)S(1)}, bf16[4,12288]{1,0:T(4,128)(2,1)S(1)}, u32[]{:S(2)}, u32[]{:S(2)}) collective-permute-start(bf16[4,12288]{1,0:T(4,128)(2,1)S(1)} %collective-permute-done.4.refs_1_), channel_id=1, source_target_pairs={{0,2},{1,3},{2,0},{3,1},{4,6},{5,7},{6,4},{7,5},{8,10},{9,11},{10,... | collective-permute-start | bytes 294920 | tf_op jit(solution)/shard_map/ppermute | solution.py:198
  15.2 20.4 %collective-permute-start.14 = (bf16[128,12288]{1,0:T(8,128)(2,1)}, bf16[128,12288]{1,0:T(8,128)(2,1)S(1)}, u32[]{:S(2)}, u32[]{:S(2)}) collective-permute-start(bf16[128,12288]{1,0:T(8,128)(2,1)} %refs_5_), channel_id=1, source_target_pairs={{0,1},{1,0},{2,3},{3,2},{4,5},{5,4},{6,7},{7,6},{8,9},{9,8},{10,11... | collective-permute-start | bytes 9437192 | tf_op jit(solution)/shard_map/ppermute | solution.py:201
  15.3 7.8 %collective-permute-start.7 = (bf16[768,512]{1,0:T(8,128)(2,1)}, bf16[768,512]{1,0:T(8,128)(2,1)S(1)}, u32[]{:S(2)}, u32[]{:S(2)}) collective-permute-start(bf16[768,512]{1,0:T(8,128)(2,1)} %refs_3_), channel_id=1, source_target_pairs={{0,1},{1,0},{2,3},{3,2},{4,5},{5,4},{6,7},{7,6},{8,9},{9,8},{10,11... | collective-permute-start | bytes 2359304 | tf_op jit(solution)/shard_map/ppermute | solution.py:201
  15.8 21.1 %collective-permute-start.12 = (bf16[512,768]{1,0:T(8,128)(2,1)}, bf16[512,768]{1,0:T(8,128)(2,1)S(1)}, u32[]{:S(2)}, u32[]{:S(2)}) collective-permute-start(bf16[512,768]{1,0:T(8,128)(2,1)} %refs_6_), channel_id=1, source_target_pairs={{0,1},{1,0},{2,3},{3,2},{4,5},{5,4},{6,7},{7,6},{8,9},{9,8},{10,11... | collective-permute-start | bytes 2359304 | tf_op jit(solution)/shard_map/ppermute | solution.py:201
  15.9 6.3 %collective-permute-start.1 = (bf16[4,12288]{1,0:T(4,128)(2,1)S(1)}, bf16[4,12288]{1,0:T(4,128)(2,1)S(1)}, u32[]{:S(2)}, u32[]{:S(2)}) collective-permute-start(bf16[4,12288]{1,0:T(4,128)(2,1)S(1)} %collective-permute-done.refs_2_), channel_id=1, source_target_pairs={{0,2},{1,3},{2,0},{3,1},{4,6},{5,7},{6,4},{7,5},{8,10},{9,11},{10,... | collective-permute-start | bytes 294920 | tf_op jit(solution)/shard_map/ppermute | solution.py:198
  16.5 6.6 %collective-permute-start.3 = (bf16[4,12288]{1,0:T(4,128)(2,1)S(1)}, bf16[4,12288]{1,0:T(4,128)(2,1)S(1)}, u32[]{:S(2)}, u32[]{:S(2)}) collective-permute-start(bf16[4,12288]{1,0:T(4,128)(2,1)S(1)} %collective-permute-done.2.refs_3_), channel_id=1, source_target_pairs={{0,2},{1,3},{2,0},{3,1},{4,6},{5,7},{6,4},{7,5},{8,10},{9,11},{10,... | collective-permute-start | bytes 294920 | tf_op jit(solution)/shard_map/ppermute | solution.py:198
  21.3 12.0 %copy-start.1 = (f32[128]{0:T(128)S(1)}, f32[128]{0:T(128)}, u32[]{:S(2)}) copy-start(f32[128]{0:T(128)} %param.19) | copy-start | bytes 1540
  23.9 4.9 %collective-permute-start.10 = (bf16[32,512]{1,0:T(8,128)(2,1)S(1)}, bf16[32,512]{1,0:T(8,128)(2,1)S(1)}, u32[]{:S(2)}, u32[]{:S(2)}) collective-permute-start(bf16[32,512]{1,0:T(8,128)(2,1)S(1)} %get-tuple-element.65), channel_id=1, source_target_pairs={{0,6},{1,7},{2,4},{3,5},{4,2},{5,3},{6,0},{7,1},{8,14},{9,15},{10,... | collective-permute-start | bytes 98312 | tf_op jit(solution)/shard_map/ppermute | solution.py:260
  25.9 3.9 %collective-permute-start.8 = (bf16[32,512]{1,0:T(8,128)(2,1)S(1)}, bf16[32,512]{1,0:T(8,128)(2,1)S(1)}, u32[]{:S(2)}, u32[]{:S(2)}) collective-permute-start(bf16[32,512]{1,0:T(8,128)(2,1)S(1)} %get-tuple-element.63), channel_id=1, source_target_pairs={{0,2},{1,3},{2,0},{3,1},{4,6},{5,7},{6,4},{7,5},{8,10},{9,11},{10,... | collective-permute-start | bytes 98312 | tf_op jit(solution)/shard_map/ppermute | solution.py:260
  27.4 3.9 %collective-permute-start.9 = (bf16[32,512]{1,0:T(8,128)(2,1)S(1)}, bf16[32,512]{1,0:T(8,128)(2,1)S(1)}, u32[]{:S(2)}, u32[]{:S(2)}) collective-permute-start(bf16[32,512]{1,0:T(8,128)(2,1)S(1)} %get-tuple-element.64), channel_id=1, source_target_pairs={{0,4},{1,5},{2,6},{3,7},{4,0},{5,1},{6,2},{7,3},{8,12},{9,13},{10,... | collective-permute-start | bytes 98312 | tf_op jit(solution)/shard_map/ppermute | solution.py:260
  31.3 5.5 %collective-permute-start.15 = (bf16[32,512]{1,0:T(8,128)(2,1)S(1)}, bf16[32,512]{1,0:T(8,128)(2,1)S(1)}, u32[]{:S(2)}, u32[]{:S(2)}) collective-permute-start(bf16[32,512]{1,0:T(8,128)(2,1)S(1)} %get-tuple-element.76), channel_id=1, source_target_pairs={{0,8},{1,9},{2,10},{3,11},{4,12},{5,13},{6,14},{7,15},{8,0},{9,1},... | collective-permute-start | bytes 98312 | tf_op jit(solution)/shard_map/ppermute | solution.py:260
  33.3 1.1 %collective-permute-start.13 = (f32[1,128]{1,0:T(1,128)S(1)}, f32[1,128]{1,0:T(1,128)S(1)}, u32[]{:S(2)}, u32[]{:S(2)}) collective-permute-start(f32[1,128]{1,0:T(1,128)S(1)} %bitcast.12), channel_id=1, source_target_pairs={{0,1},{1,0},{2,3},{3,2},{4,5},{5,4},{6,7},{7,6},{8,9},{9,8},{10,11... | collective-permute-start | bytes 1544 | tf_op jit(solution)/shard_map/ppermute | solution.py:201
  35.6 1.2 %copy-start = (f32[512]{0:T(512)S(1)}, f32[512]{0:T(512)}, u32[]{:S(2)}) copy-start(f32[512]{0:T(512)} %param.22) | copy-start | bytes 6148
  37.3 5.7 %collective-permute-start.21 = (bf16[4,12288]{1,0:T(4,128)(2,1)S(1)}, bf16[4,12288]{1,0:T(4,128)(2,1)S(1)}, u32[]{:S(2)}, u32[]{:S(2)}) collective-permute-start(bf16[4,12288]{1,0:T(4,128)(2,1)S(1)} %get-tuple-element.84), channel_id=1, source_target_pairs={{0,2},{1,3},{2,0},{3,1},{4,6},{5,7},{6,4},{7,5},{8,10},{9,11},{10,... | collective-permute-start | bytes 294920 | tf_op jit(solution)/shard_map/ppermute | solution.py:198
  37.9 7.2 %collective-permute-start.19 = (bf16[4,12288]{1,0:T(4,128)(2,1)S(1)}, bf16[4,12288]{1,0:T(4,128)(2,1)S(1)}, u32[]{:S(2)}, u32[]{:S(2)}) collective-permute-start(bf16[4,12288]{1,0:T(4,128)(2,1)S(1)} %get-tuple-element.82), channel_id=1, source_target_pairs={{0,2},{1,3},{2,0},{3,1},{4,6},{5,7},{6,4},{7,5},{8,10},{9,11},{10,... | collective-permute-start | bytes 294920 | tf_op jit(solution)/shard_map/ppermute | solution.py:198
  39.4 7.8 %collective-permute-start.17 = (bf16[4,12288]{1,0:T(4,128)(2,1)S(1)}, bf16[4,12288]{1,0:T(4,128)(2,1)S(1)}, u32[]{:S(2)}, u32[]{:S(2)}) collective-permute-start(bf16[4,12288]{1,0:T(4,128)(2,1)S(1)} %get-tuple-element.80), channel_id=1, source_target_pairs={{0,2},{1,3},{2,0},{3,1},{4,6},{5,7},{6,4},{7,5},{8,10},{9,11},{10,... | collective-permute-start | bytes 294920 | tf_op jit(solution)/shard_map/ppermute | solution.py:198
  39.9 8.7 %collective-permute-start.16 = (bf16[4,12288]{1,0:T(4,128)(2,1)S(1)}, bf16[4,12288]{1,0:T(4,128)(2,1)S(1)}, u32[]{:S(2)}, u32[]{:S(2)}) collective-permute-start(bf16[4,12288]{1,0:T(4,128)(2,1)S(1)} %get-tuple-element.78), channel_id=1, source_target_pairs={{0,2},{1,3},{2,0},{3,1},{4,6},{5,7},{6,4},{7,5},{8,10},{9,11},{10,... | collective-permute-start | bytes 294920 | tf_op jit(solution)/shard_map/ppermute | solution.py:198
  43.1 7.5 %collective-permute-start.22 = (bf16[4,12288]{1,0:T(4,128)(2,1)S(1)}, bf16[4,12288]{1,0:T(4,128)(2,1)S(1)}, u32[]{:S(2)}, u32[]{:S(2)}) collective-permute-start(bf16[4,12288]{1,0:T(4,128)(2,1)S(1)} %add_convert_fusion), channel_id=1, source_target_pairs={{0,12},{1,13},{2,14},{3,15},{4,8},{5,9},{6,10},{7,11},{8,4},{9,5},... | collective-permute-start | bytes 294920 | tf_op jit(solution)/shard_map/ppermute | solution.py:195
  45.2 8.4 %collective-permute-start.20 = (bf16[4,12288]{1,0:T(4,128)(2,1)S(1)}, bf16[4,12288]{1,0:T(4,128)(2,1)S(1)}, u32[]{:S(2)}, u32[]{:S(2)}) collective-permute-start(bf16[4,12288]{1,0:T(4,128)(2,1)S(1)} %add_convert_fusion.1), channel_id=1, source_target_pairs={{0,8},{1,9},{2,10},{3,11},{4,12},{5,13},{6,14},{7,15},{8,0},{9,1},... | collective-permute-start | bytes 294920 | tf_op jit(solution)/shard_map/ppermute | solution.py:195
  47.3 6.3 %collective-permute-start.18 = (bf16[4,12288]{1,0:T(4,128)(2,1)S(1)}, bf16[4,12288]{1,0:T(4,128)(2,1)S(1)}, u32[]{:S(2)}, u32[]{:S(2)}) collective-permute-start(bf16[4,12288]{1,0:T(4,128)(2,1)S(1)} %add_convert_fusion.2), channel_id=1, source_target_pairs={{0,4},{1,5},{2,6},{3,7},{4,0},{5,1},{6,2},{7,3},{8,12},{9,13},{10,... | collective-permute-start | bytes 294920 | tf_op jit(solution)/shard_map/ppermute | solution.py:195

commit v12 on v8

--- a/solution.py
+++ b/solution.py
@@ -218,15 +218,12 @@
         [pltpu.SemaphoreType.DMA((len(near),))],
         8 * MIB,
     )(*[pltpu.with_memory_space_constraint(x, pltpu.HBM) for x in near])
-    held[1], *near = lax.optimization_barrier((held[1], *near))
+    beyond = [beside(hidden)]
+    *_, w_in_mate, low_in_sent, w_out_sent = lax.optimization_barrier(
+        (*held, *near, *beyond, w_in_mate, low_in, w_out)
+    )
     hidden_near, gain, shift, low_in_near, w_in, w_out_near, low_out_near = near
-    soon = groups // 2
-    beyond = [beside(h) for h in held[:soon]]
-    *_, w_in_mate, low_in_sent, w_out_sent, low_out_sent, bias_sent = lax.optimization_barrier(
-        (*held, *beyond, w_in_mate, low_in, w_out, low_out, bias)
-    )
-    low_in_mate, bias_mate, w_out_mate, low_out_mate = map(core, (low_in_sent, bias_sent, w_out_sent, low_out_sent))
-
+    low_in_mate, w_out_mate = core(low_in_sent), core(w_out_sent)
     hidden_near, *beyond = lax.optimization_barrier((hidden_near, *beyond))
     normed, keep, send = call(
         functools.partial(near_body, groups),
@@ -236,8 +233,9 @@
         (),
         4 * MIB,
     )(place, hidden_near, *held[1:], gain, shift)
-    send, *late = lax.optimization_barrier((send, *held[soon:]))
-    got = beside(send)
+    send, bias_sent, *late = lax.optimization_barrier((send, bias, *held[2:]))
+    beyond.append(beside(held[1]))
+    got, bias_mate, beyond[1] = lax.optimization_barrier((beside(send), core(bias_sent), beyond[1]))
     beyond = beyond + [beside(h) for h in late]
     total, message = call(
         down_body, [shape(rows, rank, dtype=f32), shape(rows, rank)], [SMEM] + [VMEM] * 4, 16
@@ -245,7 +243,8 @@
     far = call(
         functools.partial(far_body, groups), [shape(some, width)], [VMEM] * (groups + 2), 16, (), 4 * MIB
     )(*beyond, gain, shift)[0]
-    got = beside(message)
+    got, w_out_mate, low_out_sent = lax.optimization_barrier((beside(message), w_out_mate, low_out))
+    low_out_mate = core(low_out_sent)
     step = piece(width, 2048)
     act = call(
         functools.partial(act_body, step),
@@ -261,7 +260,7 @@
         [VMEM] * 2,
         16,
     )(total, got)
-    got = [across(messages[k - 1], k) for k in range(1, groups)]
+    got = [across(messages[k - 1], k) for k in range(groups - 1, 0, -1)]
     part = call(
         functools.partial(part_body, step),
         [shape(rows, width, dtype=f32)],
@@ -279,10 +278,18 @@
         6 * MIB,
     )(place, total, low_bias.reshape(1, rank), low_out_near, low_out_mate, part, *got)
 
-    sums = []
+    sums, here, mark = [], None, None
     for k in range(groups - 1, -1, -1):
-        here = parts[k] + beside(parts[groups + k]).astype(f32)
-        sums.append(across(here.astype(bf16), k) if k else here)
+        mine = parts[groups + k]
+        if k == 0:
+            mine, _ = lax.optimization_barrier((mine, mark))
+        come = beside(mine)
+        if here is not None:
+            come, _ = lax.optimization_barrier((come, here))
+        here = parts[k] + come.astype(f32)
+        here = here.astype(bf16) if k else here
+        mark = here if k == groups // 2 else mark
+        sums.append(across(here, k) if k else here)
     return call(functools.partial(last_body, groups), [shape(row_dev, width)], [VMEM] * groups, 16)(*sums[::-1])[0]
 
 

time: 57.6 us -> 54.5 us (0.946)
  waiting for transfers between devices: 23 us -> 15.7 us
  starting transfers between devices: 22.5 us -> 25.9 us
  local copies, waits for them, and re-layouts: 0.88 us -> 1.72 us
    ppermute x10, waiting for transfers between devices: 15.2 us -> 9.32 us  [beside(): return lax.ppermute(x, 'blk', [(i, i ^ 2) for i in range(devices)])]
    ppermute x9, waiting for transfers between devices: 6.77 us -> 2.8 us  [across(): return lax.ppermute(x, 'blk', [(i, i ^ 4 * k) for i in range(devices)])]
    ppermute x9, starting transfers between devices: 12.4 us -> 15 us  [across(): return lax.ppermute(x, 'blk', [(i, i ^ 4 * k) for i in range(devices)])]
    ppermute x5, waiting for transfers between devices: 0.98 us -> 3.58 us  [core(): return lax.ppermute(x, 'blk', [(i, i ^ 1) for i in range(devices)])]
    ppermute x10, starting transfers between devices: 9.15 us -> 10.2 us  [beside(): return lax.ppermute(x, 'blk', [(i, i ^ 2) for i in range(devices)])]
    unnamed x12, local copies, waits for them, and re-layouts: 0.81 us -> 1.64 us
  transfers between devices with their start and end apart: 24 -> 24, of which waited for: 9 -> 8; matrix products, arithmetic and copies ran while one was open for 5% -> 6% of each run, Pallas kernels for 13% -> 14%
where the time goes in v12:
time: 54.5 us; the launch traced here: 54.4 us
  starting transfers between devices  25.9 us (48%)
  waiting for transfers between devices  15.7 us (29%)
  Pallas kernels  8.62 us (16%)
  other arithmetic  2.24 us (4%)
  local copies, waits for them, and re-layouts  1.72 us (3%)
    ppermute x9, starting transfers between devices, across(): return lax.ppermute(x, 'blk', [(i, i ^ 4 * k) for i in range(devices)])  15 us
    ppermute x10, starting transfers between devices, beside(): return lax.ppermute(x, 'blk', [(i, i ^ 2) for i in range(devices)])  10.2 us
    ppermute x10, waiting for transfers between devices, beside(): return lax.ppermute(x, 'blk', [(i, i ^ 2) for i in range(devices)])  9.32 us
    ppermute x5, waiting for transfers between devices, core(): return lax.ppermute(x, 'blk', [(i, i ^ 1) for i in range(devices)])  3.58 us
    pallas_call x1, Pallas kernels, shards(): call(functools.partial(load_body, len(near)), [shape(*x.shape, dtype=x.dt...  3.52 us
    ppermute x9, waiting for transfers between devices, across(): return lax.ppermute(x, 'blk', [(i, i ^ 4 * k) for i in range(devices)])  2.8 us
    unnamed x12, local copies, waits for them, and re-layouts  1.64 us
    pallas_call x1, Pallas kernels, shards(): call(functools.partial(part_body, step), [shape(rows, width, dtype=f32)],...  1.19 us
  transfers between devices with their start and end apart: 24, of which 8 were waited for; matrix products, arithmetic and copies ran while one was open for 6% of the time, Pallas kernels for 14%

profile of v12, /device:TPU:0, one launch (start us, length us, event | category | flops | bytes accessed | tf_op | source)
XLA Modules:
  0.0 54.4 jit_solution(10424204790616186035)
XLA Ops:
  0.5 3.6 %collective-permute-start.2 = (bf16[4,12288]{1,0:T(4,128)(2,1)}, bf16[4,12288]{1,0:T(4,128)(2,1)S(1)}, u32[]{:S(2)}, u32[]{:S(2)}) collective-permute-start(bf16[4,12288]{1,0:T(4,128)(2,1)} %refs_0_), channel_id=1, source_target_pairs={{0,8},{1,9},{2,10},{3,11},{4,12},{5,13},{6,14},{7,15},{8,0},{9,1},... | collective-permute-start | bytes 294920 | tf_op jit(solution)/shard_map/ppermute | solution.py:187
  4.0 1.6 %collective-permute-start.1 = (bf16[4,12288]{1,0:T(4,128)(2,1)}, bf16[4,12288]{1,0:T(4,128)(2,1)S(1)}, u32[]{:S(2)}, u32[]{:S(2)}) collective-permute-start(bf16[4,12288]{1,0:T(4,128)(2,1)} %refs_0_), channel_id=1, source_target_pairs={{0,4},{1,5},{2,6},{3,7},{4,0},{5,1},{6,2},{7,3},{8,12},{9,13},{10,... | collective-permute-start | bytes 294920 | tf_op jit(solution)/shard_map/ppermute | solution.py:187
  5.6 1.5 %collective-permute-start = (bf16[4,12288]{1,0:T(4,128)(2,1)}, bf16[4,12288]{1,0:T(4,128)(2,1)S(1)}, u32[]{:S(2)}, u32[]{:S(2)}) collective-permute-start(bf16[4,12288]{1,0:T(4,128)(2,1)} %refs_0_), channel_id=1, source_target_pairs={{0,2},{1,3},{2,0},{3,1},{4,6},{5,7},{6,4},{7,5},{8,10},{9,11},{10,... | collective-permute-start | bytes 294920 | tf_op jit(solution)/shard_map/ppermute | solution.py:190
  7.4 0.8 %copy.13 = s32[4,6]{0,1:T(8,128)S(1)} copy(s32[4,6]{1,0:T(4,128)} %param.15) | data formatting | bytes 192 | tf_op args[3]
  8.1 0.7 %fusion.1 = s32[4,6]{0,1:T(8,128)S(1)} fusion(s32[4]{0:T(128)} %param.16), kind=kLoop, calls=%fused_computation.12 | loop fusion | flops 48 | bytes 112 | tf_op jit(solution)/shard_map/convert_element_type | solution.py:154
  8.9 0.7 %fusion = s32[16,16]{1,0:T(8,128)S(1)} fusion(s32[16]{0:T(128)} %param.17), kind=kLoop, calls=%fused_computation.10 | loop fusion | flops 512 | bytes 1088 | tf_op jit(solution)/shard_map/convert_element_type | solution.py:157
  10.3 3.5 %shard_map.118 = (bf16[4,12288]{1,0:T(4,128)(2,1)S(1)}, f32[1,12288]{1,0:T(1,128)S(1)}, f32[1,12288]{1,0:T(1,128)S(1)}, bf16[768,512]{1,0:T(8,128)(2,1)S(1)}, bf...) custom-call(bf16[4,12288]{1,0:T(4,128)(2,1)} %refs_0_, ...), custom_call_target="tpu_custom_call" | custom-call | bytes 8388608 | tf_op jit(solution)/shard_map/pallas_call | solution.py:213
  13.9 0.7 %copy-done.2 = bf16[128,12288]{1,0:T(8,128)(2,1)S(1)} copy-done((bf16[128,12288]{1,0:T(8,128)(2,1)S(1)}, bf16[128,12288]{1,0:T(8,128)(2,1)}, u32[]{:S(2)}) %copy-start.2) | copy-done | bytes 3145752
  15.3 0.6 %shard_map.119 = (bf16[16,12288]{1,0:T(8,128)(2,1)S(1)}, bf16[16,1536]{1,0:T(8,128)(2,1)S(1)}, bf16[16,1536]{1,0:T(8,128)(2,1)S(1)}) custom-call(s32[1]{0:T(128)} %bitcast.place, bf16[4,12288]{1,0:T(4,128)(2,1)S(1)} %get-tuple-element.64.refs_0_, bf16[4,12288]{1,0:T(4,128)(2,1)S(1)} %collective-permute-done.1.refs_1_, ...), custom_call_target="tpu_custom_call" | custom-call | bytes 4194304 | tf_op jit(solution)/shard_map/pallas_call | solution.py:228
  15.9 1.8 %collective-permute-start.4 = (bf16[16,1536]{1,0:T(8,128)(2,1)S(1)}, bf16[16,1536]{1,0:T(8,128)(2,1)S(1)}, u32[]{:S(2)}, u32[]{:S(2)}) collective-permute-start(bf16[16,1536]{1,0:T(8,128)(2,1)S(1)} %get-tuple-element.69), channel_id=1, source_target_pairs={{0,2},{1,3},{2,0},{3,1},{4,6},{5,7},{6,4},{7,5},{8,10},{9,11},{10,... | collective-permute-start | bytes 147464 | tf_op jit(solution)/shard_map/ppermute | solution.py:190
  17.8 3.6 %collective-permute-done.5.b_mate = f32[1,128]{1,0:T(1,128)S(1)} collective-permute-done((f32[1,128]{1,0:T(1,128)S(1)}, f32[1,128]{1,0:T(1,128)S(1)}, u32[]{:S(2)}, u32[]{:S(2)}) %collective-permute-start.5) | collective-permute-done | bytes 544 | tf_op jit(solution)/shard_map/ppermute | solution.py:193
  21.7 0.5 collective-permute-start.9
  22.2 3.4 %collective-permute-done.9.got = bf16[32,512]{1,0:T(8,128)(2,1)S(1)} collective-permute-done((bf16[32,512]{1,0:T(8,128)(2,1)S(1)}, bf16[32,512]{1,0:T(8,128)(2,1)S(1)}, u32[]{:S(2)}, u32[]{:S(2)}) %collective-permute-start.9) | collective-permute-done | bytes 32800 | tf_op jit(solution)/shard_map/ppermute | solution.py:190
  25.6 0.6 %collective-permute-start.12 = (bf16[4,12288]{1,0:T(4,128)(2,1)S(1)}, bf16[4,12288]{1,0:T(4,128)(2,1)S(1)}, u32[]{:S(2)}, u32[]{:S(2)}) collective-permute-start(bf16[4,12288]{1,0:T(4,128)(2,1)S(1)} %collective-permute-done.2.refs_2_), channel_id=1, source_target_pairs={{0,2},{1,3},{2,0},{3,1},{4,6},{5,7},{6,4},{7,5},{8,10},{9,11},{10,... | collective-permute-start | bytes 294920 | tf_op jit(solution)/shard_map/ppermute | solution.py:190
  26.2 1.5 %collective-permute-start.13 = (bf16[4,12288]{1,0:T(4,128)(2,1)S(1)}, bf16[4,12288]{1,0:T(4,128)(2,1)S(1)}, u32[]{:S(2)}, u32[]{:S(2)}) collective-permute-start(bf16[4,12288]{1,0:T(4,128)(2,1)S(1)} %collective-permute-done.3.refs_3_), channel_id=1, source_target_pairs={{0,2},{1,3},{2,0},{3,1},{4,6},{5,7},{6,4},{7,5},{8,10},{9,11},{10,... | collective-permute-start | bytes 294920 | tf_op jit(solution)/shard_map/ppermute | solution.py:190
  27.8 3.7 %collective-permute-start.14 = (bf16[32,512]{1,0:T(8,128)(2,1)S(1)}, bf16[32,512]{1,0:T(8,128)(2,1)S(1)}, u32[]{:S(2)}, u32[]{:S(2)}) collective-permute-start(bf16[32,512]{1,0:T(8,128)(2,1)S(1)} %get-tuple-element.92), channel_id=1, source_target_pairs={{0,12},{1,13},{2,14},{3,15},{4,8},{5,9},{6,10},{7,11},{8,4},{9,5},... | collective-permute-start | bytes 98312 | tf_op jit(solution)/shard_map/ppermute | solution.py:187
  31.4 0.8 %collective-permute-start.16 = (bf16[32,512]{1,0:T(8,128)(2,1)S(1)}, bf16[32,512]{1,0:T(8,128)(2,1)S(1)}, u32[]{:S(2)}, u32[]{:S(2)}) collective-permute-start(bf16[32,512]{1,0:T(8,128)(2,1)S(1)} %get-tuple-element.94), channel_id=1, source_target_pairs={{0,4},{1,5},{2,6},{3,7},{4,0},{5,1},{6,2},{7,3},{8,12},{9,13},{10,... | collective-permute-start | bytes 98312 | tf_op jit(solution)/shard_map/ppermute | solution.py:187
  32.2 0.7 %collective-permute-done.13.refs_3_ = bf16[4,12288]{1,0:T(4,128)(2,1)S(1)} collective-permute-done((bf16[4,12288]{1,0:T(4,128)(2,1)S(1)}, bf16[4,12288]{1,0:T(4,128)(2,1)S(1)}, u32[]{:S(2)}, u32[]{:S(2)}) %collective-permute-start.13) | collective-permute-done | bytes 98336 | tf_op jit(solution)/shard_map/ppermute | solution.py:190
  33.0 0.6 %shard_map.122.far = bf16[16,12288]{1,0:T(8,128)(2,1)S(1)} custom-call(bf16[4,12288]{1,0:T(4,128)(2,1)S(1)} %collective-permute-done.refs_0_, bf16[4,12288]{1,0:T(4,128)(2,1)S(1)} %collective-permute-done.6.refs_1_, bf16[4,12288]{1,0:T(4,128)(2,1)S(1)} %collective-permute-done.12.refs_2_, bf16[4,12288]{1,0:T(4,128)(2,1)S(1)} %collective-permute-done.13.refs_3_, ...), custom_call_target="tpu_custom_call" | custom-call | bytes 4194304 | tf_op jit(solution)/shard_map/pallas_call | solution.py:243
  33.6 1.2 %shard_map.123.act = bf16[32,256]{1,0:T(8,128)(2,1)S(1)} custom-call(bf16[16,12288]{1,0:T(8,128)(2,1)S(1)} %get-tuple-element.83.near, bf16[16,12288]{1,0:T(8,128)(2,1)S(1)} %shard_map.122.far, bf16[12288,128]{1,0:T(8,128)(2,1)S(1)} %get-tuple-element.73.w_own, bf16[12288,128]{1,0:T(8,128)(2,1)S(1)} %collective-permute-done.7.w_mate, f32[1,128]{1,0:T(1,128)S(1)} %bitcast.13, ...), custom_call_target="tpu_custom_call" | custom-call | bytes 4194304 | tf_op jit(solution)/shard_map/pallas_call | solution.py:249
  34.8 1.2 %shard_map.124.part = f32[32,12288]{1,0:T(8,128)S(1)} custom-call(bf16[32,256]{1,0:T(8,128)(2,1)S(1)} %shard_map.123.act, bf16[128,12288]{1,0:T(8,128)(2,1)S(1)} %get-tuple-element.74.w_own, bf16[128,12288]{1,0:T(8,128)(2,1)S(1)} %collective-permute-done.10.w_mate), custom_call_target="tpu_custom_call" | custom-call | bytes 6291456 | tf_op jit(solution)/shard_map/pallas_call | solution.py:264
  36.7 0.6 %collective-permute-start.18 = (bf16[4,12288]{1,0:T(4,128)(2,1)S(1)}, bf16[4,12288]{1,0:T(4,128)(2,1)S(1)}, u32[]{:S(2)}, u32[]{:S(2)}) collective-permute-start(bf16[4,12288]{1,0:T(4,128)(2,1)S(1)} %get-tuple-element.100), channel_id=1, source_target_pairs={{0,2},{1,3},{2,0},{3,1},{4,6},{5,7},{6,4},{7,5},{8,10},{9,11},{10,... | collective-permute-start | bytes 294920 | tf_op jit(solution)/shard_map/ppermute | solution.py:190
  37.3 1.5 %collective-permute-start.17 = (bf16[4,12288]{1,0:T(4,128)(2,1)S(1)}, bf16[4,12288]{1,0:T(4,128)(2,1)S(1)}, u32[]{:S(2)}, u32[]{:S(2)}) collective-permute-start(bf16[4,12288]{1,0:T(4,128)(2,1)S(1)} %get-tuple-element.98), channel_id=1, source_target_pairs={{0,2},{1,3},{2,0},{3,1},{4,6},{5,7},{6,4},{7,5},{8,10},{9,11},{10,... | collective-permute-start | bytes 294920 | tf_op jit(solution)/shard_map/ppermute | solution.py:190
  38.8 0.5 collective-permute-start.20
  39.3 3.2 %collective-permute-done.18 = bf16[4,12288]{1,0:T(4,128)(2,1)S(1)} collective-permute-done((bf16[4,12288]{1,0:T(4,128)(2,1)S(1)}, bf16[4,12288]{1,0:T(4,128)(2,1)S(1)}, u32[]{:S(2)}, u32[]{:S(2)}) %collective-permute-start.18) | collective-permute-done | bytes 98336 | tf_op jit(solution)/shard_map/ppermute | solution.py:190
  42.6 3.4 %collective-permute-start.23 = (bf16[4,12288]{1,0:T(4,128)(2,1)S(1)}, bf16[4,12288]{1,0:T(4,128)(2,1)S(1)}, u32[]{:S(2)}, u32[]{:S(2)}) collective-permute-start(bf16[4,12288]{1,0:T(4,128)(2,1)S(1)} %add_convert_fusion.2), channel_id=1, source_target_pairs={{0,12},{1,13},{2,14},{3,15},{4,8},{5,9},{6,10},{7,11},{8,4},{9,5},... | collective-permute-start | bytes 294920 | tf_op jit(solution)/shard_map/ppermute | solution.py:187
  46.5 1.3 %collective-permute-start.19 = (bf16[4,12288]{1,0:T(4,128)(2,1)S(1)}, bf16[4,12288]{1,0:T(4,128)(2,1)S(1)}, u32[]{:S(2)}, u32[]{:S(2)}) collective-permute-start(bf16[4,12288]{1,0:T(4,128)(2,1)S(1)} %get-tuple-element.102), channel_id=1, source_target_pairs={{0,2},{1,3},{2,0},{3,1},{4,6},{5,7},{6,4},{7,5},{8,10},{9,11},{10,... | collective-permute-start | bytes 294920 | tf_op jit(solution)/shard_map/ppermute | solution.py:190
  47.9 1.3 %collective-permute-start.21 = (bf16[4,12288]{1,0:T(4,128)(2,1)S(1)}, bf16[4,12288]{1,0:T(4,128)(2,1)S(1)}, u32[]{:S(2)}, u32[]{:S(2)}) collective-permute-start(bf16[4,12288]{1,0:T(4,128)(2,1)S(1)} %add_convert_fusion), channel_id=1, source_target_pairs={{0,4},{1,5},{2,6},{3,7},{4,0},{5,1},{6,2},{7,3},{8,12},{9,13},{10,... | collective-permute-start | bytes 294920 | tf_op jit(solution)/shard_map/ppermute | solution.py:187
  49.1 2.0 %collective-permute-done.19 = bf16[4,12288]{1,0:T(4,128)(2,1)S(1)} collective-permute-done((bf16[4,12288]{1,0:T(4,128)(2,1)S(1)}, bf16[4,12288]{1,0:T(4,128)(2,1)S(1)}, u32[]{:S(2)}, u32[]{:S(2)}) %collective-permute-start.19) | collective-permute-done | bytes 98336 | tf_op jit(solution)/shard_map/ppermute | solution.py:190
  51.2 1.6 %collective-permute-done.22.refs_2_ = bf16[4,12288]{1,0:T(4,128)(2,1)S(1)} collective-permute-done((bf16[4,12288]{1,0:T(4,128)(2,1)S(1)}, bf16[4,12288]{1,0:T(4,128)(2,1)S(1)}, u32[]{:S(2)}, u32[]{:S(2)}) %collective-permute-start.22) | collective-permute-done | bytes 98336 | tf_op jit(solution)/shard_map/ppermute | solution.py:187
  52.7 0.9 %collective-permute-done.21.refs_1_ = bf16[4,12288]{1,0:T(4,128)(2,1)S(1)} collective-permute-done((bf16[4,12288]{1,0:T(4,128)(2,1)S(1)}, bf16[4,12288]{1,0:T(4,128)(2,1)S(1)}, u32[]{:S(2)}, u32[]{:S(2)}) %collective-permute-start.21) | collective-permute-done | bytes 98336 | tf_op jit(solution)/shard_map/ppermute | solution.py:187
  53.7 0.7 %shard_map.126 = bf16[4,12288]{1,0:T(4,128)(2,1)} custom-call(f32[4,12288]{1,0:T(4,128)S(1)} %convert_add_fusion.refs_0_, bf16[4,12288]{1,0:T(4,128)(2,1)S(1)} %collective-permute-done.21.refs_1_, bf16[4,12288]{1,0:T(4,128)(2,1)S(1)} %collective-permute-done.22.refs_2_, bf16[4,12288]{1,0:T(4,128)(2,1)S(1)} %collective-permute-done.23.refs_3_), custom_call_target="tpu_custom_call" | custom-call | bytes 2097152 | tf_op jit(solution)/shard_map/pallas_call | solution.py:293
  (52 shorter events, 4.1 us)
Async XLA Ops:
  0.0 13.9 %collective-permute-start.7 = (bf16[12288,128]{1,0:T(8,128)(2,1)}, bf16[12288,128]{1,0:T(8,128)(2,1)S(1)}, u32[]{:S(2)}, u32[]{:S(2)}) collective-permute-start(bf16[12288,128]{1,0:T(8,128)(2,1)} %refs_4_), channel_id=1, source_target_pairs={{0,1},{1,0},{2,3},{3,2},{4,5},{5,4},{6,7},{7,6},{8,9},{9,8},{10,11... | collective-permute-start | bytes 9437192 | tf_op jit(solution)/shard_map/ppermute | solution.py:193
  0.5 13.4 %collective-permute-start.2 = (bf16[4,12288]{1,0:T(4,128)(2,1)}, bf16[4,12288]{1,0:T(4,128)(2,1)S(1)}, u32[]{:S(2)}, u32[]{:S(2)}) collective-permute-start(bf16[4,12288]{1,0:T(4,128)(2,1)} %refs_0_), channel_id=1, source_target_pairs={{0,8},{1,9},{2,10},{3,11},{4,12},{5,13},{6,14},{7,15},{8,0},{9,1},... | collective-permute-start | bytes 294920 | tf_op jit(solution)/shard_map/ppermute | solution.py:187
  4.0 9.8 %collective-permute-start.1 = (bf16[4,12288]{1,0:T(4,128)(2,1)}, bf16[4,12288]{1,0:T(4,128)(2,1)S(1)}, u32[]{:S(2)}, u32[]{:S(2)}) collective-permute-start(bf16[4,12288]{1,0:T(4,128)(2,1)} %refs_0_), channel_id=1, source_target_pairs={{0,4},{1,5},{2,6},{3,7},{4,0},{5,1},{6,2},{7,3},{8,12},{9,13},{10,... | collective-permute-start | bytes 294920 | tf_op jit(solution)/shard_map/ppermute | solution.py:187
  5.6 8.2 %collective-permute-start = (bf16[4,12288]{1,0:T(4,128)(2,1)}, bf16[4,12288]{1,0:T(4,128)(2,1)S(1)}, u32[]{:S(2)}, u32[]{:S(2)}) collective-permute-start(bf16[4,12288]{1,0:T(4,128)(2,1)} %refs_0_), channel_id=1, source_target_pairs={{0,2},{1,3},{2,0},{3,1},{4,6},{5,7},{6,4},{7,5},{8,10},{9,11},{10,... | collective-permute-start | bytes 294920 | tf_op jit(solution)/shard_map/ppermute | solution.py:190
  7.1 6.7 %collective-permute-start.3 = (bf16[4,12288]{1,0:T(4,128)(2,1)}, bf16[4,12288]{1,0:T(4,128)(2,1)S(1)}, u32[]{:S(2)}, u32[]{:S(2)}) collective-permute-start(bf16[4,12288]{1,0:T(4,128)(2,1)} %refs_0_), channel_id=1, source_target_pairs={{0,12},{1,13},{2,14},{3,15},{4,8},{5,9},{6,10},{7,11},{8,4},{9,5},... | collective-permute-start | bytes 294920 | tf_op jit(solution)/shard_map/ppermute | solution.py:187
  10.2 4.3 %copy-start.2 = (bf16[128,12288]{1,0:T(8,128)(2,1)S(1)}, bf16[128,12288]{1,0:T(8,128)(2,1)}, u32[]{:S(2)}) copy-start(bf16[128,12288]{1,0:T(8,128)(2,1)} %refs_5_) | copy-start | bytes 9437188
  10.3 4.5 %copy-start.3 = (bf16[768,512]{1,0:T(8,128)(2,1)S(1)}, bf16[768,512]{1,0:T(8,128)(2,1)}, u32[]{:S(2)}) copy-start(bf16[768,512]{1,0:T(8,128)(2,1)} %refs_3_) | copy-start | bytes 2359300
  10.3 7.5 %copy-start.1 = (f32[128]{0:T(128)S(1)}, f32[128]{0:T(128)}, u32[]{:S(2)}) copy-start(f32[128]{0:T(128)} %param.19) | copy-start | bytes 1540
  10.3 15.4 %copy-start.4 = (bf16[512,768]{1,0:T(8,128)(2,1)S(1)}, bf16[512,768]{1,0:T(8,128)(2,1)}, u32[]{:S(2)}) copy-start(bf16[512,768]{1,0:T(8,128)(2,1)} %refs_6_) | copy-start | bytes 2359300
  14.5 11.1 %collective-permute-start.10 = (bf16[128,12288]{1,0:T(8,128)(2,1)S(1)}, bf16[128,12288]{1,0:T(8,128)(2,1)S(1)}, u32[]{:S(2)}, u32[]{:S(2)}) collective-permute-start(bf16[128,12288]{1,0:T(8,128)(2,1)S(1)} %copy-done.2), channel_id=1, source_target_pairs={{0,1},{1,0},{2,3},{3,2},{4,5},{5,4},{6,7},{7,6},{8,9},{9,8},{10,11... | collective-permute-start | bytes 9437192 | tf_op jit(solution)/shard_map/ppermute | solution.py:193
  14.7 6.6 %collective-permute-start.8 = (bf16[768,512]{1,0:T(8,128)(2,1)S(1)}, bf16[768,512]{1,0:T(8,128)(2,1)S(1)}, u32[]{:S(2)}, u32[]{:S(2)}) collective-permute-start(bf16[768,512]{1,0:T(8,128)(2,1)S(1)} %copy-done.3), channel_id=1, source_target_pairs={{0,1},{1,0},{2,3},{3,2},{4,5},{5,4},{6,7},{7,6},{8,9},{9,8},{10,11... | collective-permute-start | bytes 2359304 | tf_op jit(solution)/shard_map/ppermute | solution.py:193
  15.0 6.3 %collective-permute-start.6 = (bf16[4,12288]{1,0:T(4,128)(2,1)S(1)}, bf16[4,12288]{1,0:T(4,128)(2,1)S(1)}, u32[]{:S(2)}, u32[]{:S(2)}) collective-permute-start(bf16[4,12288]{1,0:T(4,128)(2,1)S(1)} %collective-permute-done.1.refs_1_), channel_id=1, source_target_pairs={{0,2},{1,3},{2,0},{3,1},{4,6},{5,7},{6,4},{7,5},{8,10},{9,11},{10,... | collective-permute-start | bytes 294920 | tf_op jit(solution)/shard_map/ppermute | solution.py:190
  15.9 5.4 %collective-permute-start.4 = (bf16[16,1536]{1,0:T(8,128)(2,1)S(1)}, bf16[16,1536]{1,0:T(8,128)(2,1)S(1)}, u32[]{:S(2)}, u32[]{:S(2)}) collective-permute-start(bf16[16,1536]{1,0:T(8,128)(2,1)S(1)} %get-tuple-element.69), channel_id=1, source_target_pairs={{0,2},{1,3},{2,0},{3,1},{4,6},{5,7},{6,4},{7,5},{8,10},{9,11},{10,... | collective-permute-start | bytes 147464 | tf_op jit(solution)/shard_map/ppermute | solution.py:190
  17.7 3.6 %collective-permute-start.5 = (f32[1,128]{1,0:T(1,128)S(1)}, f32[1,128]{1,0:T(1,128)S(1)}, u32[]{:S(2)}, u32[]{:S(2)}) collective-permute-start(f32[1,128]{1,0:T(1,128)S(1)} %bitcast.12), channel_id=1, source_target_pairs={{0,1},{1,0},{2,3},{3,2},{4,5},{5,4},{6,7},{7,6},{8,9},{9,8},{10,11... | collective-permute-start | bytes 1544 | tf_op jit(solution)/shard_map/ppermute | solution.py:193
  21.7 3.9 %collective-permute-start.9 = (bf16[32,512]{1,0:T(8,128)(2,1)S(1)}, bf16[32,512]{1,0:T(8,128)(2,1)S(1)}, u32[]{:S(2)}, u32[]{:S(2)}) collective-permute-start(bf16[32,512]{1,0:T(8,128)(2,1)S(1)} %get-tuple-element.78), channel_id=1, source_target_pairs={{0,2},{1,3},{2,0},{3,1},{4,6},{5,7},{6,4},{7,5},{8,10},{9,11},{10,... | collective-permute-start | bytes 98312 | tf_op jit(solution)/shard_map/ppermute | solution.py:190
  25.6 10.6 %collective-permute-start.11 = (bf16[512,768]{1,0:T(8,128)(2,1)S(1)}, bf16[512,768]{1,0:T(8,128)(2,1)S(1)}, u32[]{:S(2)}, u32[]{:S(2)}) collective-permute-start(bf16[512,768]{1,0:T(8,128)(2,1)S(1)} %copy-done.4), channel_id=1, source_target_pairs={{0,1},{1,0},{2,3},{3,2},{4,5},{5,4},{6,7},{7,6},{8,9},{9,8},{10,11... | collective-permute-start | bytes 2359304 | tf_op jit(solution)/shard_map/ppermute | solution.py:193
  25.6 5.8 %collective-permute-start.12 = (bf16[4,12288]{1,0:T(4,128)(2,1)S(1)}, bf16[4,12288]{1,0:T(4,128)(2,1)S(1)}, u32[]{:S(2)}, u32[]{:S(2)}) collective-permute-start(bf16[4,12288]{1,0:T(4,128)(2,1)S(1)} %collective-permute-done.2.refs_2_), channel_id=1, source_target_pairs={{0,2},{1,3},{2,0},{3,1},{4,6},{5,7},{6,4},{7,5},{8,10},{9,11},{10,... | collective-permute-start | bytes 294920 | tf_op jit(solution)/shard_map/ppermute | solution.py:190
  26.2 6.7 %collective-permute-start.13 = (bf16[4,12288]{1,0:T(4,128)(2,1)S(1)}, bf16[4,12288]{1,0:T(4,128)(2,1)S(1)}, u32[]{:S(2)}, u32[]{:S(2)}) collective-permute-start(bf16[4,12288]{1,0:T(4,128)(2,1)S(1)} %collective-permute-done.3.refs_3_), channel_id=1, source_target_pairs={{0,2},{1,3},{2,0},{3,1},{4,6},{5,7},{6,4},{7,5},{8,10},{9,11},{10,... | collective-permute-start | bytes 294920 | tf_op jit(solution)/shard_map/ppermute | solution.py:190
  27.8 8.2 %collective-permute-start.14 = (bf16[32,512]{1,0:T(8,128)(2,1)S(1)}, bf16[32,512]{1,0:T(8,128)(2,1)S(1)}, u32[]{:S(2)}, u32[]{:S(2)}) collective-permute-start(bf16[32,512]{1,0:T(8,128)(2,1)S(1)} %get-tuple-element.92), channel_id=1, source_target_pairs={{0,12},{1,13},{2,14},{3,15},{4,8},{5,9},{6,10},{7,11},{8,4},{9,5},... | collective-permute-start | bytes 98312 | tf_op jit(solution)/shard_map/ppermute | solution.py:187
  31.4 4.8 %collective-permute-start.15 = (bf16[32,512]{1,0:T(8,128)(2,1)S(1)}, bf16[32,512]{1,0:T(8,128)(2,1)S(1)}, u32[]{:S(2)}, u32[]{:S(2)}) collective-permute-start(bf16[32,512]{1,0:T(8,128)(2,1)S(1)} %get-tuple-element.93), channel_id=1, source_target_pairs={{0,8},{1,9},{2,10},{3,11},{4,12},{5,13},{6,14},{7,15},{8,0},{9,1},... | collective-permute-start | bytes 98312 | tf_op jit(solution)/shard_map/ppermute | solution.py:187
  31.4 4.8 %collective-permute-start.16 = (bf16[32,512]{1,0:T(8,128)(2,1)S(1)}, bf16[32,512]{1,0:T(8,128)(2,1)S(1)}, u32[]{:S(2)}, u32[]{:S(2)}) collective-permute-start(bf16[32,512]{1,0:T(8,128)(2,1)S(1)} %get-tuple-element.94), channel_id=1, source_target_pairs={{0,4},{1,5},{2,6},{3,7},{4,0},{5,1},{6,2},{7,3},{8,12},{9,13},{10,... | collective-permute-start | bytes 98312 | tf_op jit(solution)/shard_map/ppermute | solution.py:187
  34.7 1.5 %copy-start = (f32[512]{0:T(512)S(1)}, f32[512]{0:T(512)}, u32[]{:S(2)}) copy-start(f32[512]{0:T(512)} %param.22) | copy-start | bytes 6148
  36.7 5.8 %collective-permute-start.18 = (bf16[4,12288]{1,0:T(4,128)(2,1)S(1)}, bf16[4,12288]{1,0:T(4,128)(2,1)S(1)}, u32[]{:S(2)}, u32[]{:S(2)}) collective-permute-start(bf16[4,12288]{1,0:T(4,128)(2,1)S(1)} %get-tuple-element.100), channel_id=1, source_target_pairs={{0,2},{1,3},{2,0},{3,1},{4,6},{5,7},{6,4},{7,5},{8,10},{9,11},{10,... | collective-permute-start | bytes 294920 | tf_op jit(solution)/shard_map/ppermute | solution.py:190
  37.3 8.7 %collective-permute-start.17 = (bf16[4,12288]{1,0:T(4,128)(2,1)S(1)}, bf16[4,12288]{1,0:T(4,128)(2,1)S(1)}, u32[]{:S(2)}, u32[]{:S(2)}) collective-permute-start(bf16[4,12288]{1,0:T(4,128)(2,1)S(1)} %get-tuple-element.98), channel_id=1, source_target_pairs={{0,2},{1,3},{2,0},{3,1},{4,6},{5,7},{6,4},{7,5},{8,10},{9,11},{10,... | collective-permute-start | bytes 294920 | tf_op jit(solution)/shard_map/ppermute | solution.py:190
  38.8 9.0 %collective-permute-start.20 = (bf16[4,12288]{1,0:T(4,128)(2,1)S(1)}, bf16[4,12288]{1,0:T(4,128)(2,1)S(1)}, u32[]{:S(2)}, u32[]{:S(2)}) collective-permute-start(bf16[4,12288]{1,0:T(4,128)(2,1)S(1)} %get-tuple-element.104), channel_id=1, source_target_pairs={{0,2},{1,3},{2,0},{3,1},{4,6},{5,7},{6,4},{7,5},{8,10},{9,11},{10,... | collective-permute-start | bytes 294920 | tf_op jit(solution)/shard_map/ppermute | solution.py:190
  42.6 10.2 %collective-permute-start.23 = (bf16[4,12288]{1,0:T(4,128)(2,1)S(1)}, bf16[4,12288]{1,0:T(4,128)(2,1)S(1)}, u32[]{:S(2)}, u32[]{:S(2)}) collective-permute-start(bf16[4,12288]{1,0:T(4,128)(2,1)S(1)} %add_convert_fusion.2), channel_id=1, source_target_pairs={{0,12},{1,13},{2,14},{3,15},{4,8},{5,9},{6,10},{7,11},{8,4},{9,5},... | collective-permute-start | bytes 294920 | tf_op jit(solution)/shard_map/ppermute | solution.py:187
  46.0 6.7 %collective-permute-start.22 = (bf16[4,12288]{1,0:T(4,128)(2,1)S(1)}, bf16[4,12288]{1,0:T(4,128)(2,1)S(1)}, u32[]{:S(2)}, u32[]{:S(2)}) collective-permute-start(bf16[4,12288]{1,0:T(4,128)(2,1)S(1)} %add_convert_fusion.1), channel_id=1, source_target_pairs={{0,8},{1,9},{2,10},{3,11},{4,12},{5,13},{6,14},{7,15},{8,0},{9,1},... | collective-permute-start | bytes 294920 | tf_op jit(solution)/shard_map/ppermute | solution.py:187
  46.5 4.6 %collective-permute-start.19 = (bf16[4,12288]{1,0:T(4,128)(2,1)S(1)}, bf16[4,12288]{1,0:T(4,128)(2,1)S(1)}, u32[]{:S(2)}, u32[]{:S(2)}) collective-permute-start(bf16[4,12288]{1,0:T(4,128)(2,1)S(1)} %get-tuple-element.102), channel_id=1, source_target_pairs={{0,2},{1,3},{2,0},{3,1},{4,6},{5,7},{6,4},{7,5},{8,10},{9,11},{10,... | collective-permute-start | bytes 294920 | tf_op jit(solution)/shard_map/ppermute | solution.py:190
  47.9 5.8 %collective-permute-start.21 = (bf16[4,12288]{1,0:T(4,128)(2,1)S(1)}, bf16[4,12288]{1,0:T(4,128)(2,1)S(1)}, u32[]{:S(2)}, u32[]{:S(2)}) collective-permute-start(bf16[4,12288]{1,0:T(4,128)(2,1)S(1)} %add_convert_fusion), channel_id=1, source_target_pairs={{0,4},{1,5},{2,6},{3,7},{4,0},{5,1},{6,2},{7,3},{8,12},{9,13},{10,... | collective-permute-start | bytes 294920 | tf_op jit(solution)/shard_map/ppermute | solution.py:187

commit v13 on v12

--- a/solution.py
+++ b/solution.py
@@ -218,7 +218,8 @@
         [pltpu.SemaphoreType.DMA((len(near),))],
         8 * MIB,
     )(*[pltpu.with_memory_space_constraint(x, pltpu.HBM) for x in near])
-    beyond = [beside(hidden)]
+    early, bias_mate = lax.optimization_barrier((hidden, core(bias)))
+    beyond = [beside(early)]
     *_, w_in_mate, low_in_sent, w_out_sent = lax.optimization_barrier(
         (*held, *near, *beyond, w_in_mate, low_in, w_out)
     )
@@ -233,9 +234,9 @@
         (),
         4 * MIB,
     )(place, hidden_near, *held[1:], gain, shift)
-    send, bias_sent, *late = lax.optimization_barrier((send, bias, *held[2:]))
+    send, *late = lax.optimization_barrier((send, *held[2:]))
     beyond.append(beside(held[1]))
-    got, bias_mate, beyond[1] = lax.optimization_barrier((beside(send), core(bias_sent), beyond[1]))
+    got, beyond[1] = lax.optimization_barrier((beside(send), beyond[1]))
     beyond = beyond + [beside(h) for h in late]
     total, message = call(
         down_body, [shape(rows, rank, dtype=f32), shape(rows, rank)], [SMEM] + [VMEM] * 4, 16

time: 54.5 us -> 54.6 us (level)
  starting transfers between devices: 25.9 us -> 26.7 us
    ppermute x5, waiting for transfers between devices: 3.58 us -> 0.3 us  [core(): return lax.ppermute(x, 'blk', [(i, i ^ 1) for i in range(devices)])]
    ppermute x10, waiting for transfers between devices: 9.32 us -> 12.1 us  [beside(): return lax.ppermute(x, 'blk', [(i, i ^ 2) for i in range(devices)])]
    ppermute x10, starting transfers between devices: 10.2 us -> 10.9 us  [beside(): return lax.ppermute(x, 'blk', [(i, i ^ 2) for i in range(devices)])]
  transfers between devices with their start and end apart: 24 -> 24, of which waited for: 8 -> 9; matrix products, arithmetic and copies ran while one was open for 6% -> 6% of each run, Pallas kernels for 14% -> 14%
where the time goes in v13:
time: 54.6 us; the launch traced here: 54.4 us
  starting transfers between devices  26.7 us (49%)
  waiting for transfers between devices  15.2 us (28%)
  Pallas kernels  8.61 us (16%)
  other arithmetic  2.24 us (4%)
  local copies, waits for them, and re-layouts  1.54 us (3%)
    ppermute x9, starting transfers between devices, across(): return lax.ppermute(x, 'blk', [(i, i ^ 4 * k) for i in range(devices)])  14.8 us
    ppermute x10, waiting for transfers between devices, beside(): return lax.ppermute(x, 'blk', [(i, i ^ 2) for i in range(devices)])  12.1 us
    ppermute x10, starting transfers between devices, beside(): return lax.ppermute(x, 'blk', [(i, i ^ 2) for i in range(devices)])  10.9 us
    pallas_call x1, Pallas kernels, shards(): call(functools.partial(load_body, len(near)), [shape(*x.shape, dtype=x.dt...  3.52 us
    ppermute x9, waiting for transfers between devices, across(): return lax.ppermute(x, 'blk', [(i, i ^ 4 * k) for i in range(devices)])  2.79 us
    unnamed x12, local copies, waits for them, and re-layouts  1.46 us
    pallas_call x1, Pallas kernels, shards(): call(functools.partial(part_body, step), [shape(rows, width, dtype=f32)],...  1.19 us
    pallas_call x1, Pallas kernels, shards(): call(functools.partial(act_body, step), [shape(rows, 2 * block)], [VMEM]...  1.18 us
  transfers between devices with their start and end apart: 24, of which 9 were waited for; matrix products, arithmetic and copies ran while one was open for 6% of the time, Pallas kernels for 14%

profile of v13, /device:TPU:0, one launch (start us, length us, event | category | flops | bytes accessed | tf_op | source)
XLA Modules:
  0.0 54.4 jit_solution(11164880825318827565)
XLA Ops:
  0.5 3.6 %collective-permute-start.3 = (bf16[4,12288]{1,0:T(4,128)(2,1)}, bf16[4,12288]{1,0:T(4,128)(2,1)S(1)}, u32[]{:S(2)}, u32[]{:S(2)}) collective-permute-start(bf16[4,12288]{1,0:T(4,128)(2,1)} %refs_0_), channel_id=1, source_target_pairs={{0,8},{1,9},{2,10},{3,11},{4,12},{5,13},{6,14},{7,15},{8,0},{9,1},... | collective-permute-start | bytes 294920 | tf_op jit(solution)/shard_map/ppermute | solution.py:187
  4.0 1.6 %collective-permute-start.2 = (bf16[4,12288]{1,0:T(4,128)(2,1)}, bf16[4,12288]{1,0:T(4,128)(2,1)S(1)}, u32[]{:S(2)}, u32[]{:S(2)}) collective-permute-start(bf16[4,12288]{1,0:T(4,128)(2,1)} %refs_0_), channel_id=1, source_target_pairs={{0,4},{1,5},{2,6},{3,7},{4,0},{5,1},{6,2},{7,3},{8,12},{9,13},{10,... | collective-permute-start | bytes 294920 | tf_op jit(solution)/shard_map/ppermute | solution.py:187
  5.6 0.8 %copy.13 = s32[4,6]{0,1:T(8,128)S(1)} copy(s32[4,6]{1,0:T(4,128)} %param.15) | data formatting | bytes 192 | tf_op args[3]
  6.4 0.7 %fusion.1 = s32[4,6]{0,1:T(8,128)S(1)} fusion(s32[4]{0:T(128)} %param.16), kind=kLoop, calls=%fused_computation.12 | loop fusion | flops 48 | bytes 112 | tf_op jit(solution)/shard_map/convert_element_type | solution.py:154
  7.3 0.7 %fusion = s32[16,16]{1,0:T(8,128)S(1)} fusion(s32[16]{0:T(128)} %param.17), kind=kLoop, calls=%fused_computation.10 | loop fusion | flops 512 | bytes 1088 | tf_op jit(solution)/shard_map/convert_element_type | solution.py:157
  8.1 1.8 %collective-permute-start.1 = (bf16[4,12288]{1,0:T(4,128)(2,1)}, bf16[4,12288]{1,0:T(4,128)(2,1)S(1)}, u32[]{:S(2)}, u32[]{:S(2)}) collective-permute-start(bf16[4,12288]{1,0:T(4,128)(2,1)} %refs_0_), channel_id=1, source_target_pairs={{0,2},{1,3},{2,0},{3,1},{4,6},{5,7},{6,4},{7,5},{8,10},{9,11},{10,... | collective-permute-start | bytes 294920 | tf_op jit(solution)/shard_map/ppermute | solution.py:190
  10.4 3.5 %shard_map.118 = (bf16[4,12288]{1,0:T(4,128)(2,1)S(1)}, f32[1,12288]{1,0:T(1,128)S(1)}, f32[1,12288]{1,0:T(1,128)S(1)}, bf16[768,512]{1,0:T(8,128)(2,1)S(1)}, bf...) custom-call(bf16[4,12288]{1,0:T(4,128)(2,1)} %refs_0_, ...), custom_call_target="tpu_custom_call" | custom-call | bytes 8388608 | tf_op jit(solution)/shard_map/pallas_call | solution.py:213
  13.9 0.7 %copy-done.2 = bf16[128,12288]{1,0:T(8,128)(2,1)S(1)} copy-done((bf16[128,12288]{1,0:T(8,128)(2,1)S(1)}, bf16[128,12288]{1,0:T(8,128)(2,1)}, u32[]{:S(2)}) %copy-start.2) | copy-done | bytes 3145752
  15.1 0.7 %collective-permute-start.6 = (bf16[4,12288]{1,0:T(4,128)(2,1)S(1)}, bf16[4,12288]{1,0:T(4,128)(2,1)S(1)}, u32[]{:S(2)}, u32[]{:S(2)}) collective-permute-start(bf16[4,12288]{1,0:T(4,128)(2,1)S(1)} %collective-permute-done.2.refs_1_), channel_id=1, source_target_pairs={{0,2},{1,3},{2,0},{3,1},{4,6},{5,7},{6,4},{7,5},{8,10},{9,11},{10,... | collective-permute-start | bytes 294920 | tf_op jit(solution)/shard_map/ppermute | solution.py:190
  15.9 0.6 %shard_map.119 = (bf16[16,12288]{1,0:T(8,128)(2,1)S(1)}, bf16[16,1536]{1,0:T(8,128)(2,1)S(1)}, bf16[16,1536]{1,0:T(8,128)(2,1)S(1)}) custom-call(s32[1]{0:T(128)} %bitcast.place, bf16[4,12288]{1,0:T(4,128)(2,1)S(1)} %get-tuple-element.65.refs_0_, bf16[4,12288]{1,0:T(4,128)(2,1)S(1)} %collective-permute-done.2.refs_1_, ...), custom_call_target="tpu_custom_call" | custom-call | bytes 4194304 | tf_op jit(solution)/shard_map/pallas_call | solution.py:229
  16.5 1.3 %collective-permute-start.5 = (bf16[16,1536]{1,0:T(8,128)(2,1)S(1)}, bf16[16,1536]{1,0:T(8,128)(2,1)S(1)}, u32[]{:S(2)}, u32[]{:S(2)}) collective-permute-start(bf16[16,1536]{1,0:T(8,128)(2,1)S(1)} %get-tuple-element.70), channel_id=1, source_target_pairs={{0,2},{1,3},{2,0},{3,1},{4,6},{5,7},{6,4},{7,5},{8,10},{9,11},{10,... | collective-permute-start | bytes 147464 | tf_op jit(solution)/shard_map/ppermute | solution.py:190
  17.8 3.3 %collective-permute-done.5.got = bf16[16,1536]{1,0:T(8,128)(2,1)S(1)} collective-permute-done((bf16[16,1536]{1,0:T(8,128)(2,1)S(1)}, bf16[16,1536]{1,0:T(8,128)(2,1)S(1)}, u32[]{:S(2)}, u32[]{:S(2)}) %collective-permute-start.5) | collective-permute-done | bytes 49184 | tf_op jit(solution)/shard_map/ppermute | solution.py:190
  21.8 0.8 %collective-permute-start.9 = (bf16[32,512]{1,0:T(8,128)(2,1)S(1)}, bf16[32,512]{1,0:T(8,128)(2,1)S(1)}, u32[]{:S(2)}, u32[]{:S(2)}) collective-permute-start(bf16[32,512]{1,0:T(8,128)(2,1)S(1)} %get-tuple-element.78), channel_id=1, source_target_pairs={{0,2},{1,3},{2,0},{3,1},{4,6},{5,7},{6,4},{7,5},{8,10},{9,11},{10,... | collective-permute-start | bytes 98312 | tf_op jit(solution)/shard_map/ppermute | solution.py:190
  22.5 3.2 %collective-permute-done.9.got = bf16[32,512]{1,0:T(8,128)(2,1)S(1)} collective-permute-done((bf16[32,512]{1,0:T(8,128)(2,1)S(1)}, bf16[32,512]{1,0:T(8,128)(2,1)S(1)}, u32[]{:S(2)}, u32[]{:S(2)}) %collective-permute-start.9) | collective-permute-done | bytes 32800 | tf_op jit(solution)/shard_map/ppermute | solution.py:190
  25.7 0.8 %collective-permute-start.12 = (bf16[4,12288]{1,0:T(4,128)(2,1)S(1)}, bf16[4,12288]{1,0:T(4,128)(2,1)S(1)}, u32[]{:S(2)}, u32[]{:S(2)}) collective-permute-start(bf16[4,12288]{1,0:T(4,128)(2,1)S(1)} %collective-permute-done.3.refs_2_), channel_id=1, source_target_pairs={{0,2},{1,3},{2,0},{3,1},{4,6},{5,7},{6,4},{7,5},{8,10},{9,11},{10,... | collective-permute-start | bytes 294920 | tf_op jit(solution)/shard_map/ppermute | solution.py:190
  26.5 1.3 %collective-permute-start.13 = (bf16[4,12288]{1,0:T(4,128)(2,1)S(1)}, bf16[4,12288]{1,0:T(4,128)(2,1)S(1)}, u32[]{:S(2)}, u32[]{:S(2)}) collective-permute-start(bf16[4,12288]{1,0:T(4,128)(2,1)S(1)} %collective-permute-done.4.refs_3_), channel_id=1, source_target_pairs={{0,2},{1,3},{2,0},{3,1},{4,6},{5,7},{6,4},{7,5},{8,10},{9,11},{10,... | collective-permute-start | bytes 294920 | tf_op jit(solution)/shard_map/ppermute | solution.py:190
  27.8 3.7 %collective-permute-start.14 = (bf16[32,512]{1,0:T(8,128)(2,1)S(1)}, bf16[32,512]{1,0:T(8,128)(2,1)S(1)}, u32[]{:S(2)}, u32[]{:S(2)}) collective-permute-start(bf16[32,512]{1,0:T(8,128)(2,1)S(1)} %get-tuple-element.92), channel_id=1, source_target_pairs={{0,12},{1,13},{2,14},{3,15},{4,8},{5,9},{6,10},{7,11},{8,4},{9,5},... | collective-permute-start | bytes 98312 | tf_op jit(solution)/shard_map/ppermute | solution.py:187
  31.5 0.8 %collective-permute-start.16 = (bf16[32,512]{1,0:T(8,128)(2,1)S(1)}, bf16[32,512]{1,0:T(8,128)(2,1)S(1)}, u32[]{:S(2)}, u32[]{:S(2)}) collective-permute-start(bf16[32,512]{1,0:T(8,128)(2,1)S(1)} %get-tuple-element.94), channel_id=1, source_target_pairs={{0,4},{1,5},{2,6},{3,7},{4,0},{5,1},{6,2},{7,3},{8,12},{9,13},{10,... | collective-permute-start | bytes 98312 | tf_op jit(solution)/shard_map/ppermute | solution.py:187
  32.3 0.7 %collective-permute-done.13.refs_3_ = bf16[4,12288]{1,0:T(4,128)(2,1)S(1)} collective-permute-done((bf16[4,12288]{1,0:T(4,128)(2,1)S(1)}, bf16[4,12288]{1,0:T(4,128)(2,1)S(1)}, u32[]{:S(2)}, u32[]{:S(2)}) %collective-permute-start.13) | collective-permute-done | bytes 98336 | tf_op jit(solution)/shard_map/ppermute | solution.py:190
  33.6 1.2 %shard_map.123.act = bf16[32,256]{1,0:T(8,128)(2,1)S(1)} custom-call(bf16[16,12288]{1,0:T(8,128)(2,1)S(1)} %get-tuple-element.83.near, bf16[16,12288]{1,0:T(8,128)(2,1)S(1)} %shard_map.122.far, bf16[12288,128]{1,0:T(8,128)(2,1)S(1)} %get-tuple-element.73.w_own, bf16[12288,128]{1,0:T(8,128)(2,1)S(1)} %collective-permute-done.7.w_mate, f32[1,128]{1,0:T(1,128)S(1)} %bitcast.13, ...), custom_call_target="tpu_custom_call" | custom-call | bytes 4194304 | tf_op jit(solution)/shard_map/pallas_call | solution.py:250
  34.8 1.2 %shard_map.124.part = f32[32,12288]{1,0:T(8,128)S(1)} custom-call(bf16[32,256]{1,0:T(8,128)(2,1)S(1)} %shard_map.123.act, bf16[128,12288]{1,0:T(8,128)(2,1)S(1)} %get-tuple-element.74.w_own, bf16[128,12288]{1,0:T(8,128)(2,1)S(1)} %collective-permute-done.10.w_mate), custom_call_target="tpu_custom_call" | custom-call | bytes 6291456 | tf_op jit(solution)/shard_map/pallas_call | solution.py:265
  36.8 0.8 %collective-permute-start.18 = (bf16[4,12288]{1,0:T(4,128)(2,1)S(1)}, bf16[4,12288]{1,0:T(4,128)(2,1)S(1)}, u32[]{:S(2)}, u32[]{:S(2)}) collective-permute-start(bf16[4,12288]{1,0:T(4,128)(2,1)S(1)} %get-tuple-element.100), channel_id=1, source_target_pairs={{0,2},{1,3},{2,0},{3,1},{4,6},{5,7},{6,4},{7,5},{8,10},{9,11},{10,... | collective-permute-start | bytes 294920 | tf_op jit(solution)/shard_map/ppermute | solution.py:190
  37.6 1.3 %collective-permute-start.17 = (bf16[4,12288]{1,0:T(4,128)(2,1)S(1)}, bf16[4,12288]{1,0:T(4,128)(2,1)S(1)}, u32[]{:S(2)}, u32[]{:S(2)}) collective-permute-start(bf16[4,12288]{1,0:T(4,128)(2,1)S(1)} %get-tuple-element.98), channel_id=1, source_target_pairs={{0,2},{1,3},{2,0},{3,1},{4,6},{5,7},{6,4},{7,5},{8,10},{9,11},{10,... | collective-permute-start | bytes 294920 | tf_op jit(solution)/shard_map/ppermute | solution.py:190
  38.9 0.7 %collective-permute-start.20 = (bf16[4,12288]{1,0:T(4,128)(2,1)S(1)}, bf16[4,12288]{1,0:T(4,128)(2,1)S(1)}, u32[]{:S(2)}, u32[]{:S(2)}) collective-permute-start(bf16[4,12288]{1,0:T(4,128)(2,1)S(1)} %get-tuple-element.104), channel_id=1, source_target_pairs={{0,2},{1,3},{2,0},{3,1},{4,6},{5,7},{6,4},{7,5},{8,10},{9,11},{10,... | collective-permute-start | bytes 294920 | tf_op jit(solution)/shard_map/ppermute | solution.py:190
  39.6 3.0 %collective-permute-done.18 = bf16[4,12288]{1,0:T(4,128)(2,1)S(1)} collective-permute-done((bf16[4,12288]{1,0:T(4,128)(2,1)S(1)}, bf16[4,12288]{1,0:T(4,128)(2,1)S(1)}, u32[]{:S(2)}, u32[]{:S(2)}) %collective-permute-start.18) | collective-permute-done | bytes 98336 | tf_op jit(solution)/shard_map/ppermute | solution.py:190
  42.6 3.4 %collective-permute-start.23 = (bf16[4,12288]{1,0:T(4,128)(2,1)S(1)}, bf16[4,12288]{1,0:T(4,128)(2,1)S(1)}, u32[]{:S(2)}, u32[]{:S(2)}) collective-permute-start(bf16[4,12288]{1,0:T(4,128)(2,1)S(1)} %add_convert_fusion.2), channel_id=1, source_target_pairs={{0,12},{1,13},{2,14},{3,15},{4,8},{5,9},{6,10},{7,11},{8,4},{9,5},... | collective-permute-start | bytes 294920 | tf_op jit(solution)/shard_map/ppermute | solution.py:187
  46.6 1.3 %collective-permute-start.19 = (bf16[4,12288]{1,0:T(4,128)(2,1)S(1)}, bf16[4,12288]{1,0:T(4,128)(2,1)S(1)}, u32[]{:S(2)}, u32[]{:S(2)}) collective-permute-start(bf16[4,12288]{1,0:T(4,128)(2,1)S(1)} %get-tuple-element.102), channel_id=1, source_target_pairs={{0,2},{1,3},{2,0},{3,1},{4,6},{5,7},{6,4},{7,5},{8,10},{9,11},{10,... | collective-permute-start | bytes 294920 | tf_op jit(solution)/shard_map/ppermute | solution.py:190
  48.0 1.3 %collective-permute-start.21 = (bf16[4,12288]{1,0:T(4,128)(2,1)S(1)}, bf16[4,12288]{1,0:T(4,128)(2,1)S(1)}, u32[]{:S(2)}, u32[]{:S(2)}) collective-permute-start(bf16[4,12288]{1,0:T(4,128)(2,1)S(1)} %add_convert_fusion), channel_id=1, source_target_pairs={{0,4},{1,5},{2,6},{3,7},{4,0},{5,1},{6,2},{7,3},{8,12},{9,13},{10,... | collective-permute-start | bytes 294920 | tf_op jit(solution)/shard_map/ppermute | solution.py:187
  49.3 1.9 %collective-permute-done.19 = bf16[4,12288]{1,0:T(4,128)(2,1)S(1)} collective-permute-done((bf16[4,12288]{1,0:T(4,128)(2,1)S(1)}, bf16[4,12288]{1,0:T(4,128)(2,1)S(1)}, u32[]{:S(2)}, u32[]{:S(2)}) %collective-permute-start.19) | collective-permute-done | bytes 98336 | tf_op jit(solution)/shard_map/ppermute | solution.py:190
  51.2 1.6 %collective-permute-done.22.refs_2_ = bf16[4,12288]{1,0:T(4,128)(2,1)S(1)} collective-permute-done((bf16[4,12288]{1,0:T(4,128)(2,1)S(1)}, bf16[4,12288]{1,0:T(4,128)(2,1)S(1)}, u32[]{:S(2)}, u32[]{:S(2)}) %collective-permute-start.22) | collective-permute-done | bytes 98336 | tf_op jit(solution)/shard_map/ppermute | solution.py:187
  52.8 0.9 %collective-permute-done.21.refs_1_ = bf16[4,12288]{1,0:T(4,128)(2,1)S(1)} collective-permute-done((bf16[4,12288]{1,0:T(4,128)(2,1)S(1)}, bf16[4,12288]{1,0:T(4,128)(2,1)S(1)}, u32[]{:S(2)}, u32[]{:S(2)}) %collective-permute-start.21) | collective-permute-done | bytes 98336 | tf_op jit(solution)/shard_map/ppermute | solution.py:187
  53.7 0.7 %shard_map.126 = bf16[4,12288]{1,0:T(4,128)(2,1)} custom-call(f32[4,12288]{1,0:T(4,128)S(1)} %convert_add_fusion.refs_0_, bf16[4,12288]{1,0:T(4,128)(2,1)S(1)} %collective-permute-done.21.refs_1_, bf16[4,12288]{1,0:T(4,128)(2,1)S(1)} %collective-permute-done.22.refs_2_, bf16[4,12288]{1,0:T(4,128)(2,1)S(1)} %collective-permute-done.23.refs_3_), custom_call_target="tpu_custom_call" | custom-call | bytes 2097152 | tf_op jit(solution)/shard_map/pallas_call | solution.py:294
  (52 shorter events, 4.4 us)
Async XLA Ops:
  0.0 13.9 %collective-permute-start.7 = (bf16[12288,128]{1,0:T(8,128)(2,1)}, bf16[12288,128]{1,0:T(8,128)(2,1)S(1)}, u32[]{:S(2)}, u32[]{:S(2)}) collective-permute-start(bf16[12288,128]{1,0:T(8,128)(2,1)} %refs_4_), channel_id=1, source_target_pairs={{0,1},{1,0},{2,3},{3,2},{4,5},{5,4},{6,7},{7,6},{8,9},{9,8},{10,11... | collective-permute-start | bytes 9437192 | tf_op jit(solution)/shard_map/ppermute | solution.py:193
  0.5 13.4 %collective-permute-start.3 = (bf16[4,12288]{1,0:T(4,128)(2,1)}, bf16[4,12288]{1,0:T(4,128)(2,1)S(1)}, u32[]{:S(2)}, u32[]{:S(2)}) collective-permute-start(bf16[4,12288]{1,0:T(4,128)(2,1)} %refs_0_), channel_id=1, source_target_pairs={{0,8},{1,9},{2,10},{3,11},{4,12},{5,13},{6,14},{7,15},{8,0},{9,1},... | collective-permute-start | bytes 294920 | tf_op jit(solution)/shard_map/ppermute | solution.py:187
  4.0 9.9 %collective-permute-start.2 = (bf16[4,12288]{1,0:T(4,128)(2,1)}, bf16[4,12288]{1,0:T(4,128)(2,1)S(1)}, u32[]{:S(2)}, u32[]{:S(2)}) collective-permute-start(bf16[4,12288]{1,0:T(4,128)(2,1)} %refs_0_), channel_id=1, source_target_pairs={{0,4},{1,5},{2,6},{3,7},{4,0},{5,1},{6,2},{7,3},{8,12},{9,13},{10,... | collective-permute-start | bytes 294920 | tf_op jit(solution)/shard_map/ppermute | solution.py:187
  5.6 8.3 %collective-permute-start.4 = (bf16[4,12288]{1,0:T(4,128)(2,1)}, bf16[4,12288]{1,0:T(4,128)(2,1)S(1)}, u32[]{:S(2)}, u32[]{:S(2)}) collective-permute-start(bf16[4,12288]{1,0:T(4,128)(2,1)} %refs_0_), channel_id=1, source_target_pairs={{0,12},{1,13},{2,14},{3,15},{4,8},{5,9},{6,10},{7,11},{8,4},{9,5},... | collective-permute-start | bytes 294920 | tf_op jit(solution)/shard_map/ppermute | solution.py:187
  5.6 2.5 %collective-permute-start = (f32[1,128]{1,0:T(1,128)}, f32[1,128]{1,0:T(1,128)S(1)}, u32[]{:S(2)}, u32[]{:S(2)}) collective-permute-start(f32[1,128]{1,0:T(1,128)} %bitcast.12), channel_id=1, source_target_pairs={{0,1},{1,0},{2,3},{3,2},{4,5},{5,4},{6,7},{7,6},{8,9},{9,8},{10,11... | collective-permute-start | bytes 1544 | tf_op jit(solution)/shard_map/ppermute | solution.py:193
  8.1 5.8 %collective-permute-start.1 = (bf16[4,12288]{1,0:T(4,128)(2,1)}, bf16[4,12288]{1,0:T(4,128)(2,1)S(1)}, u32[]{:S(2)}, u32[]{:S(2)}) collective-permute-start(bf16[4,12288]{1,0:T(4,128)(2,1)} %refs_0_), channel_id=1, source_target_pairs={{0,2},{1,3},{2,0},{3,1},{4,6},{5,7},{6,4},{7,5},{8,10},{9,11},{10,... | collective-permute-start | bytes 294920 | tf_op jit(solution)/shard_map/ppermute | solution.py:190
  10.3 4.3 %copy-start.2 = (bf16[128,12288]{1,0:T(8,128)(2,1)S(1)}, bf16[128,12288]{1,0:T(8,128)(2,1)}, u32[]{:S(2)}) copy-start(bf16[128,12288]{1,0:T(8,128)(2,1)} %refs_5_) | copy-start | bytes 9437188
  10.3 4.5 %copy-start.3 = (bf16[768,512]{1,0:T(8,128)(2,1)S(1)}, bf16[768,512]{1,0:T(8,128)(2,1)}, u32[]{:S(2)}) copy-start(bf16[768,512]{1,0:T(8,128)(2,1)} %refs_3_) | copy-start | bytes 2359300
  10.3 15.3 %copy-start.4 = (bf16[512,768]{1,0:T(8,128)(2,1)S(1)}, bf16[512,768]{1,0:T(8,128)(2,1)}, u32[]{:S(2)}) copy-start(bf16[512,768]{1,0:T(8,128)(2,1)} %refs_6_) | copy-start | bytes 2359300
  13.9 19.7 %copy-start.1 = (f32[128]{0:T(128)S(1)}, f32[128]{0:T(128)}, u32[]{:S(2)}) copy-start(f32[128]{0:T(128)} %param.19) | copy-start | bytes 1540
  14.6 11.1 %collective-permute-start.10 = (bf16[128,12288]{1,0:T(8,128)(2,1)S(1)}, bf16[128,12288]{1,0:T(8,128)(2,1)S(1)}, u32[]{:S(2)}, u32[]{:S(2)}) collective-permute-start(bf16[128,12288]{1,0:T(8,128)(2,1)S(1)} %copy-done.2), channel_id=1, source_target_pairs={{0,1},{1,0},{2,3},{3,2},{4,5},{5,4},{6,7},{7,6},{8,9},{9,8},{10,11... | collective-permute-start | bytes 9437192 | tf_op jit(solution)/shard_map/ppermute | solution.py:193
  14.8 6.6 %collective-permute-start.8 = (bf16[768,512]{1,0:T(8,128)(2,1)S(1)}, bf16[768,512]{1,0:T(8,128)(2,1)S(1)}, u32[]{:S(2)}, u32[]{:S(2)}) collective-permute-start(bf16[768,512]{1,0:T(8,128)(2,1)S(1)} %copy-done.3), channel_id=1, source_target_pairs={{0,1},{1,0},{2,3},{3,2},{4,5},{5,4},{6,7},{7,6},{8,9},{9,8},{10,11... | collective-permute-start | bytes 2359304 | tf_op jit(solution)/shard_map/ppermute | solution.py:193
  15.1 6.0 %collective-permute-start.6 = (bf16[4,12288]{1,0:T(4,128)(2,1)S(1)}, bf16[4,12288]{1,0:T(4,128)(2,1)S(1)}, u32[]{:S(2)}, u32[]{:S(2)}) collective-permute-start(bf16[4,12288]{1,0:T(4,128)(2,1)S(1)} %collective-permute-done.2.refs_1_), channel_id=1, source_target_pairs={{0,2},{1,3},{2,0},{3,1},{4,6},{5,7},{6,4},{7,5},{8,10},{9,11},{10,... | collective-permute-start | bytes 294920 | tf_op jit(solution)/shard_map/ppermute | solution.py:190
  16.5 4.6 %collective-permute-start.5 = (bf16[16,1536]{1,0:T(8,128)(2,1)S(1)}, bf16[16,1536]{1,0:T(8,128)(2,1)S(1)}, u32[]{:S(2)}, u32[]{:S(2)}) collective-permute-start(bf16[16,1536]{1,0:T(8,128)(2,1)S(1)} %get-tuple-element.70), channel_id=1, source_target_pairs={{0,2},{1,3},{2,0},{3,1},{4,6},{5,7},{6,4},{7,5},{8,10},{9,11},{10,... | collective-permute-start | bytes 147464 | tf_op jit(solution)/shard_map/ppermute | solution.py:190
  21.8 3.9 %collective-permute-start.9 = (bf16[32,512]{1,0:T(8,128)(2,1)S(1)}, bf16[32,512]{1,0:T(8,128)(2,1)S(1)}, u32[]{:S(2)}, u32[]{:S(2)}) collective-permute-start(bf16[32,512]{1,0:T(8,128)(2,1)S(1)} %get-tuple-element.78), channel_id=1, source_target_pairs={{0,2},{1,3},{2,0},{3,1},{4,6},{5,7},{6,4},{7,5},{8,10},{9,11},{10,... | collective-permute-start | bytes 98312 | tf_op jit(solution)/shard_map/ppermute | solution.py:190
  25.7 10.6 %collective-permute-start.11 = (bf16[512,768]{1,0:T(8,128)(2,1)S(1)}, bf16[512,768]{1,0:T(8,128)(2,1)S(1)}, u32[]{:S(2)}, u32[]{:S(2)}) collective-permute-start(bf16[512,768]{1,0:T(8,128)(2,1)S(1)} %copy-done.4), channel_id=1, source_target_pairs={{0,1},{1,0},{2,3},{3,2},{4,5},{5,4},{6,7},{7,6},{8,9},{9,8},{10,11... | collective-permute-start | bytes 2359304 | tf_op jit(solution)/shard_map/ppermute | solution.py:193
  25.7 5.8 %collective-permute-start.12 = (bf16[4,12288]{1,0:T(4,128)(2,1)S(1)}, bf16[4,12288]{1,0:T(4,128)(2,1)S(1)}, u32[]{:S(2)}, u32[]{:S(2)}) collective-permute-start(bf16[4,12288]{1,0:T(4,128)(2,1)S(1)} %collective-permute-done.3.refs_2_), channel_id=1, source_target_pairs={{0,2},{1,3},{2,0},{3,1},{4,6},{5,7},{6,4},{7,5},{8,10},{9,11},{10,... | collective-permute-start | bytes 294920 | tf_op jit(solution)/shard_map/ppermute | solution.py:190
  26.5 6.5 %collective-permute-start.13 = (bf16[4,12288]{1,0:T(4,128)(2,1)S(1)}, bf16[4,12288]{1,0:T(4,128)(2,1)S(1)}, u32[]{:S(2)}, u32[]{:S(2)}) collective-permute-start(bf16[4,12288]{1,0:T(4,128)(2,1)S(1)} %collective-permute-done.4.refs_3_), channel_id=1, source_target_pairs={{0,2},{1,3},{2,0},{3,1},{4,6},{5,7},{6,4},{7,5},{8,10},{9,11},{10,... | collective-permute-start | bytes 294920 | tf_op jit(solution)/shard_map/ppermute | solution.py:190
  27.8 8.2 %collective-permute-start.14 = (bf16[32,512]{1,0:T(8,128)(2,1)S(1)}, bf16[32,512]{1,0:T(8,128)(2,1)S(1)}, u32[]{:S(2)}, u32[]{:S(2)}) collective-permute-start(bf16[32,512]{1,0:T(8,128)(2,1)S(1)} %get-tuple-element.92), channel_id=1, source_target_pairs={{0,12},{1,13},{2,14},{3,15},{4,8},{5,9},{6,10},{7,11},{8,4},{9,5},... | collective-permute-start | bytes 98312 | tf_op jit(solution)/shard_map/ppermute | solution.py:187
  31.5 4.8 %collective-permute-start.15 = (bf16[32,512]{1,0:T(8,128)(2,1)S(1)}, bf16[32,512]{1,0:T(8,128)(2,1)S(1)}, u32[]{:S(2)}, u32[]{:S(2)}) collective-permute-start(bf16[32,512]{1,0:T(8,128)(2,1)S(1)} %get-tuple-element.93), channel_id=1, source_target_pairs={{0,8},{1,9},{2,10},{3,11},{4,12},{5,13},{6,14},{7,15},{8,0},{9,1},... | collective-permute-start | bytes 98312 | tf_op jit(solution)/shard_map/ppermute | solution.py:187
  31.5 4.8 %collective-permute-start.16 = (bf16[32,512]{1,0:T(8,128)(2,1)S(1)}, bf16[32,512]{1,0:T(8,128)(2,1)S(1)}, u32[]{:S(2)}, u32[]{:S(2)}) collective-permute-start(bf16[32,512]{1,0:T(8,128)(2,1)S(1)} %get-tuple-element.94), channel_id=1, source_target_pairs={{0,4},{1,5},{2,6},{3,7},{4,0},{5,1},{6,2},{7,3},{8,12},{9,13},{10,... | collective-permute-start | bytes 98312 | tf_op jit(solution)/shard_map/ppermute | solution.py:187
  34.8 1.5 %copy-start = (f32[512]{0:T(512)S(1)}, f32[512]{0:T(512)}, u32[]{:S(2)}) copy-start(f32[512]{0:T(512)} %param.22) | copy-start | bytes 6148
  36.8 5.8 %collective-permute-start.18 = (bf16[4,12288]{1,0:T(4,128)(2,1)S(1)}, bf16[4,12288]{1,0:T(4,128)(2,1)S(1)}, u32[]{:S(2)}, u32[]{:S(2)}) collective-permute-start(bf16[4,12288]{1,0:T(4,128)(2,1)S(1)} %get-tuple-element.100), channel_id=1, source_target_pairs={{0,2},{1,3},{2,0},{3,1},{4,6},{5,7},{6,4},{7,5},{8,10},{9,11},{10,... | collective-permute-start | bytes 294920 | tf_op jit(solution)/shard_map/ppermute | solution.py:190
  37.6 8.5 %collective-permute-start.17 = (bf16[4,12288]{1,0:T(4,128)(2,1)S(1)}, bf16[4,12288]{1,0:T(4,128)(2,1)S(1)}, u32[]{:S(2)}, u32[]{:S(2)}) collective-permute-start(bf16[4,12288]{1,0:T(4,128)(2,1)S(1)} %get-tuple-element.98), channel_id=1, source_target_pairs={{0,2},{1,3},{2,0},{3,1},{4,6},{5,7},{6,4},{7,5},{8,10},{9,11},{10,... | collective-permute-start | bytes 294920 | tf_op jit(solution)/shard_map/ppermute | solution.py:190
  38.9 9.0 %collective-permute-start.20 = (bf16[4,12288]{1,0:T(4,128)(2,1)S(1)}, bf16[4,12288]{1,0:T(4,128)(2,1)S(1)}, u32[]{:S(2)}, u32[]{:S(2)}) collective-permute-start(bf16[4,12288]{1,0:T(4,128)(2,1)S(1)} %get-tuple-element.104), channel_id=1, source_target_pairs={{0,2},{1,3},{2,0},{3,1},{4,6},{5,7},{6,4},{7,5},{8,10},{9,11},{10,... | collective-permute-start | bytes 294920 | tf_op jit(solution)/shard_map/ppermute | solution.py:190
  42.6 10.2 %collective-permute-start.23 = (bf16[4,12288]{1,0:T(4,128)(2,1)S(1)}, bf16[4,12288]{1,0:T(4,128)(2,1)S(1)}, u32[]{:S(2)}, u32[]{:S(2)}) collective-permute-start(bf16[4,12288]{1,0:T(4,128)(2,1)S(1)} %add_convert_fusion.2), channel_id=1, source_target_pairs={{0,12},{1,13},{2,14},{3,15},{4,8},{5,9},{6,10},{7,11},{8,4},{9,5},... | collective-permute-start | bytes 294920 | tf_op jit(solution)/shard_map/ppermute | solution.py:187
  46.1 6.7 %collective-permute-start.22 = (bf16[4,12288]{1,0:T(4,128)(2,1)S(1)}, bf16[4,12288]{1,0:T(4,128)(2,1)S(1)}, u32[]{:S(2)}, u32[]{:S(2)}) collective-permute-start(bf16[4,12288]{1,0:T(4,128)(2,1)S(1)} %add_convert_fusion.1), channel_id=1, source_target_pairs={{0,8},{1,9},{2,10},{3,11},{4,12},{5,13},{6,14},{7,15},{8,0},{9,1},... | collective-permute-start | bytes 294920 | tf_op jit(solution)/shard_map/ppermute | solution.py:187
  46.6 4.6 %collective-permute-start.19 = (bf16[4,12288]{1,0:T(4,128)(2,1)S(1)}, bf16[4,12288]{1,0:T(4,128)(2,1)S(1)}, u32[]{:S(2)}, u32[]{:S(2)}) collective-permute-start(bf16[4,12288]{1,0:T(4,128)(2,1)S(1)} %get-tuple-element.102), channel_id=1, source_target_pairs={{0,2},{1,3},{2,0},{3,1},{4,6},{5,7},{6,4},{7,5},{8,10},{9,11},{10,... | collective-permute-start | bytes 294920 | tf_op jit(solution)/shard_map/ppermute | solution.py:190
  48.0 5.8 %collective-permute-start.21 = (bf16[4,12288]{1,0:T(4,128)(2,1)S(1)}, bf16[4,12288]{1,0:T(4,128)(2,1)S(1)}, u32[]{:S(2)}, u32[]{:S(2)}) collective-permute-start(bf16[4,12288]{1,0:T(4,128)(2,1)S(1)} %add_convert_fusion), channel_id=1, source_target_pairs={{0,4},{1,5},{2,6},{3,7},{4,0},{5,1},{6,2},{7,3},{8,12},{9,13},{10,... | collective-permute-start | bytes 294920 | tf_op jit(solution)/shard_map/ppermute | solution.py:187

commit v14 on v10

--- a/solution.py
+++ b/solution.py
@@ -45,13 +45,6 @@
     return (centred * lax.rsqrt(variance + 1e-05) * gain + shift).astype(bf16)
 
 
-def normalise(held, gain, shift, out):
-    rows = held[0].shape[0]
-    for i in range(0, len(held), 2):
-        pair = jnp.concatenate([h[...] for h in held[i : i + 2]], axis=0)
-        out[i * rows : (i + 2) * rows, :] = normal(pair, gain[...], shift[...])
-
-
 def load_body(count, *refs):
     srcs, dsts, sems = refs[:count], refs[count : 2 * count], refs[2 * count]
     copies = [pltpu.make_async_copy(srcs[i], dsts[i], sems.at[i]) for i in range(count)]
@@ -61,23 +54,28 @@
         copy.wait()
 
 
-def near_body(groups, place, *refs):
-    held, (own, gains, shifts, near, keep, send, gain, shift, first, sems) = refs[: groups - 1], refs[groups - 1 :]
-    pairs = ((own, first), (gains, gain), (shifts, shift))
+def head_body(groups, place, hidden, gain, shift, out, *refs):
+    strips, (rows, gains, shifts, sems) = refs[:groups], refs[groups:]
+    pairs = ((hidden, rows), (gain, gains), (shift, shifts))
     copies = [pltpu.make_async_copy(src, dst, sems.at[i]) for i, (src, dst) in enumerate(pairs)]
     for copy in copies:
         copy.start()
     for copy in copies:
         copy.wait()
-    normalise((first, *held), gain, shift, near)
+    out[...] = normal(rows[...], gains[...], shifts[...])
+    span = strips[0].shape[1]
+    for k in range(groups):
+        strips[k][...] = out[:, window((place[0] // 4) ^ k, span)]
+
+
+def sort_body(groups, place, *refs):
+    strips, (keep, send) = refs[:groups], refs[groups:]
     span = keep.shape[1]
-    chip = place[0] // 2
-    keep[...] = near[:, window(chip, span)]
-    send[...] = near[:, window(chip ^ 1, span)]
-
-
-def far_body(groups, *refs):
-    normalise(refs[:groups], *refs[groups:])
+    upper = (place[0] // 2) % 2
+    rows = jnp.concatenate([s[...].astype(f32) for s in strips], axis=0)
+    low, high = rows[:, :span], rows[:, span:]
+    keep[...] = jnp.where(upper == 0, low, high).astype(bf16)
+    send[...] = jnp.where(upper == 0, high, low).astype(bf16)
 
 
 def down_body(place, keep, got, own, mate, total, message):
@@ -135,15 +133,33 @@
     out[...] = total.astype(bf16)
 
 
-def act_body(step, near, far, w_own, w_mate, b_own, b_mate, mask, out):
+def act_body(groups, step, place, lists, counts, block_slot, *refs):
+    x, (w_own, w_mate, b_own, b_mate, out) = refs[: 2 * groups], refs[2 * groups :]
+    block, row_dev = w_own.shape[1], x[0].shape[0]
     total = jnp.zeros(out.shape, f32)
-    for i in range(near.shape[1] // step):
+    for i in range(w_own.shape[0] // step):
         at = slice(i * step, (i + 1) * step)
-        rows = jnp.concatenate([near[:, at], far[:, at]], axis=0)
+        rows = jnp.concatenate([r[:, at] for r in x], axis=0)
         both = jnp.concatenate([w_own[at, :], w_mate[at, :]], axis=1)
         total = total + jnp.dot(rows, both, preferred_element_type=f32)
     bias = jnp.concatenate([b_own[...], b_mate[...]], axis=1)
-    out[...] = (jnp.maximum(total + bias, 0.0) * mask[...]).astype(bf16)
+    act = jnp.maximum(total + bias, 0.0)
+    row_k = (lax.broadcasted_iota(jnp.int32, out.shape, 0) // row_dev) % groups
+    column_b = lax.broadcasted_iota(jnp.int32, out.shape, 1) // block
+    uses = jnp.zeros(out.shape, jnp.int32)
+    for k in range(groups):
+        group = (place[0] // 4) ^ k
+
+        def hit(e, found):
+            slot = block_slot[lists[group, e]]
+            live = e < counts[group]
+            own = jnp.where(live & (slot == place[0]), 1, 0)
+            mate = jnp.where(live & (slot == place[0] ^ 1), 1, 0)
+            return found[0] + own, found[1] + mate
+
+        own, mate = lax.fori_loop(0, lists.shape[1], hit, (jnp.int32(0), jnp.int32(0)))
+        uses = jnp.where(row_k == k, jnp.where(column_b == 0, own, mate), uses)
+    out[...] = jnp.where(uses > 0, act, 0.0).astype(bf16)
 
 
 def part_body(step, act, w_own, w_mate, out):
@@ -151,17 +167,6 @@
         at = slice(i * step, (i + 1) * step)
         both = jnp.concatenate([w_own[:, at], w_mate[:, at]], axis=0)
         out[:, at] = jnp.dot(act[...], both, preferred_element_type=f32)
-
-
-def activity(lists, counts, block_slot):
-    groups, top = lists.shape
-    nblocks = block_slot.shape[0]
-    names = jnp.arange(nblocks, dtype=jnp.int32)
-    live = (jnp.arange(top, dtype=jnp.int32)[None, :] < counts[:, None]).astype(jnp.int32)
-    hits = (lists[:, :, None] == names[None, None, :]).astype(jnp.int32) * live[:, :, None]
-    by_block = jnp.sum(hits, axis=1)
-    placed = (block_slot[:, None] == names[None, :]).astype(jnp.int32)
-    return jnp.sum(by_block[:, :, None] * placed[None, :, :], axis=1)
 
 
 def shards(
@@ -204,63 +209,60 @@
     gain, shift, bias = ln_gain.reshape(1, width), ln_shift.reshape(1, width), b_in.reshape(1, block)
     span = 2 * share
 
-    table = activity(lists, counts, block_slot)
-    by = plane ^ jnp.arange(groups)
-    at = position ^ jnp.arange(2)
-    relate = (by[:, None] == jnp.arange(groups)[None, :])[:, None, :, None]
-    choose = (at[:, None] == jnp.arange(devices)[None, :])[None, :, None, :]
-    live = jnp.sum(jnp.where(relate & choose, table[None, None], 0), axis=(2, 3)).astype(f32)
-    mask = jnp.broadcast_to(live[None, :, None, :, None], (2, groups, row_dev, 2, block)).reshape(rows, 2 * block)
-
-    held = [hidden] + [across(hidden, k) for k in range(groups - 1, 0, -1)][::-1]
-    w_in_mate = core(w_in)
+    hbm = lambda *xs: [pltpu.with_memory_space_constraint(x, pltpu.HBM) for x in xs]
+    normed, *strips = call(
+        functools.partial(head_body, groups),
+        [shape(row_dev, width)] + [shape(row_dev, 2 * span)] * groups,
+        [SMEM] + [HBM] * 3,
+        16,
+        [
+            pltpu.VMEM((row_dev, width), bf16),
+            pltpu.VMEM((1, width), f32),
+            pltpu.VMEM((1, width), f32),
+            pltpu.SemaphoreType.DMA((3,)),
+        ],
+        4 * MIB,
+    )(place, *hbm(hidden, gain, shift))
+
+    low_in_mate, bias_mate = core(low_in), core(bias)
+    *strips, low_in_mate, bias_mate = lax.optimization_barrier((*strips, low_in_mate, bias_mate))
+    strips = [strips[0]] + [across(strips[k], k) for k in range(groups - 1, 0, -1)][::-1]
+    normed_sent, *strips = lax.optimization_barrier((normed, *strips))
+    held = [normed] + [across(normed_sent, k) for k in range(groups - 1, 0, -1)][::-1]
+    beyond = [beside(h) for h in held]
+
     near = (low_in, w_in, w_out, low_out)
-    *near, mask = lax.optimization_barrier((*near, mask))
-    loaded = call(
+    low_in_near, w_in_near, w_out_near, low_out_near = call(
         functools.partial(load_body, len(near)),
         [shape(*x.shape, dtype=x.dtype) for x in near],
         [HBM] * len(near),
         16,
         [pltpu.SemaphoreType.DMA((len(near),))],
         8 * MIB,
-    )(*[pltpu.with_memory_space_constraint(x, pltpu.HBM) for x in near])
-    first, *loaded = lax.optimization_barrier((hidden, *loaded))
-    low_in_near, w_in, w_out_near, low_out_near = loaded
-    beyond = [beside(first), beside(held[1])]
-    *_, w_in_mate, mask, low_in_sent, w_out_sent = lax.optimization_barrier(
-        (*held, *beyond, w_in_mate, mask, low_in, w_out)
-    )
-    low_in_mate, w_out_mate = core(low_in_sent), core(w_out_sent)
-
-    own, *beyond = lax.optimization_barrier((hidden, *beyond))
-    normed, keep, send, gain, shift = call(
-        functools.partial(near_body, groups),
-        [shape(some, width), shape(some, span), shape(some, span)] + [shape(1, width, dtype=f32)] * 2,
-        [SMEM] + [VMEM] * (groups - 1) + [HBM] * 3,
-        16,
-        [pltpu.VMEM((row_dev, width), bf16), pltpu.SemaphoreType.DMA((3,))],
-        4 * MIB,
-    )(place, *held[1:], *[pltpu.with_memory_space_constraint(x, pltpu.HBM) for x in (own, gain, shift)])
-    send, bias_sent = lax.optimization_barrier((send, bias))
-    got, bias_mate, *late = lax.optimization_barrier((beside(send), core(bias_sent), *held[2:]))
-    beyond = beyond + [beside(h) for h in late]
+    )(*hbm(*near))
+
+    keep, send = call(
+        functools.partial(sort_body, groups), [shape(some, span)] * 2, [SMEM] + [VMEM] * groups, 16
+    )(place, *strips)
+    send, w_in_sent = lax.optimization_barrier((send, w_in))
+    w_in_mate = core(w_in_sent)
+    got, beyond[0] = lax.optimization_barrier((beside(send), beyond[0]))
     total, message = call(
         down_body, [shape(rows, rank, dtype=f32), shape(rows, rank)], [SMEM] + [VMEM] * 4, 16
     )(place, keep, got, low_in_near, low_in_mate)
-    far = call(
-        functools.partial(far_body, groups), [shape(some, width)], [VMEM] * (groups + 2), 16, (), 4 * MIB
-    )(*beyond, gain, shift)[0]
-    got, low_out_sent, w_out_mate, *beyond = lax.optimization_barrier((beside(message), low_out, w_out_mate, *beyond))
+    *_, w_out_sent = lax.optimization_barrier((*held, message, w_in_mate, w_out))
+    w_out_mate = core(w_out_sent)
+    got, low_out_sent, beyond[1] = lax.optimization_barrier((beside(message), low_out, beyond[1]))
     low_out_mate = core(low_out_sent)
     step = piece(width, 2048)
     act = call(
-        functools.partial(act_body, step),
+        functools.partial(act_body, groups, step),
         [shape(rows, 2 * block)],
-        [VMEM] * 7,
+        [SMEM] * 4 + [VMEM] * (2 * groups + 4),
         16,
         (),
         4 * MIB,
-    )(normed, far, w_in, w_in_mate, bias, bias_mate, mask)[0]
+    )(place, lists, counts, block_slot, *held, *beyond, w_in_near, w_in_mate, bias, bias_mate)[0]
     total, *messages = call(
         functools.partial(merge_body, groups),
         [shape(rows, rank, dtype=f32)] + [shape(rows, rank)] * (groups - 1),
@@ -285,16 +287,19 @@
         6 * MIB,
     )(place, total, low_bias.reshape(1, rank), low_out_near, low_out_mate, part, *got)
 
-    sums, here = [None] * groups, None
+    sums, here, mark = [], None, None
     for k in range(groups - 1, -1, -1):
-        come = beside(parts[groups + k])
+        mine = parts[groups + k]
+        if k == 0:
+            mine, _ = lax.optimization_barrier((mine, mark))
+        come = beside(mine)
         if here is not None:
-            come, here = lax.optimization_barrier((come, here))
-            sums[k + 1] = across(here, k + 1)
+            come, _ = lax.optimization_barrier((come, here))
         here = parts[k] + come.astype(f32)
         here = here.astype(bf16) if k else here
-    sums[0] = here
-    return call(functools.partial(last_body, groups), [shape(row_dev, width)], [VMEM] * groups, 16)(*sums)[0]
+        mark = here if k == groups // 2 else mark
+        sums.append(across(here, k) if k else here)
+    return call(functools.partial(last_body, groups), [shape(row_dev, width)], [VMEM] * groups, 16)(*sums[::-1])[0]
 
 
 def solution(mesh):

time: 64.3 us -> 61 us (0.949)
  waiting for transfers between devices: 25 us -> 22 us
  starting transfers between devices: 26.4 us -> 29.1 us
  other arithmetic: 2.25 us -> 0.22 us
  local copies, waits for them, and re-layouts: 0.89 us -> 0.04 us
    ppermute x9 -> x12, starting transfers between devices: 14.1 us -> 18.8 us  [across(): return lax.ppermute(x, 'blk', [(i, i ^ 4 * k) for i in range(devices)])]
    ppermute x10, waiting for transfers between devices: 14.5 us -> 11.6 us  [beside(): return lax.ppermute(x, 'blk', [(i, i ^ 2) for i in range(devices)])]
    ppermute x5, waiting for transfers between devices: 3.23 us -> 0.73 us  [core(): return lax.ppermute(x, 'blk', [(i, i ^ 1) for i in range(devices)])]
    ppermute x9 -> x12, waiting for transfers between devices: 7.28 us -> 9.69 us  [across(): return lax.ppermute(x, 'blk', [(i, i ^ 4 * k) for i in range(devices)])]
    ppermute x10, starting transfers between devices: 11.3 us -> 9.55 us  [beside(): return lax.ppermute(x, 'blk', [(i, i ^ 2) for i in range(devices)])]
    convert_element_type x3 -> x0, other arithmetic: 1.39 us -> none  [the longest x1 0.73 us: activity(): placed = (block_slot[:, None] == names[None, :]).astype(jnp.int32)]
    unnamed x14, local copies, waits for them, and re-layouts: 0.81 us -> 0.04 us
  transfers between devices with their start and end apart: 24 -> 27, of which waited for: 11 -> 11; matrix products, arithmetic and copies ran while one was open for 5% -> 0% of each run, Pallas kernels for 13% -> 13%
where the time goes in v14:
time: 61 us; the launch traced here: 60.8 us
  starting transfers between devices  29.1 us (48%)
  waiting for transfers between devices  22 us (36%)
  Pallas kernels  9.27 us (15%)
    ppermute x12, starting transfers between devices, across(): return lax.ppermute(x, 'blk', [(i, i ^ 4 * k) for i in range(devices)])  18.8 us
    ppermute x10, waiting for transfers between devices, beside(): return lax.ppermute(x, 'blk', [(i, i ^ 2) for i in range(devices)])  11.6 us
    ppermute x12, waiting for transfers between devices, across(): return lax.ppermute(x, 'blk', [(i, i ^ 4 * k) for i in range(devices)])  9.69 us
    ppermute x10, starting transfers between devices, beside(): return lax.ppermute(x, 'blk', [(i, i ^ 2) for i in range(devices)])  9.55 us
    pallas_call x1, Pallas kernels, shards(): call(functools.partial(load_body, len(near)), [shape(*x.shape, dtype=x.dt...  3.25 us
    pallas_call x1, Pallas kernels, shards(): call(functools.partial(act_body, groups, step), [shape(rows, 2 * block)],...  1.93 us
    pallas_call x1, Pallas kernels, shards(): call(functools.partial(head_body, groups), [shape(row_dev, width)] + [sha...  1.34 us
  transfers between devices with their start and end apart: 27, of which 11 were waited for; matrix products, arithmetic and copies ran while one was open for 0% of the time, Pallas kernels for 13%

profile of v14, /device:TPU:0, one launch (start us, length us, event | category | flops | bytes accessed | tf_op | source)
XLA Modules:
  0.0 60.8 jit_solution(5735451315937084674)
XLA Ops:
  0.5 1.3 %shard_map.118 = (bf16[4,12288]{1,0:T(4,128)(2,1)S(1)}, bf16[4,3072]{1,0:T(4,128)(2,1)S(1)}, bf16[4,3072]{1,0:T(4,128)(2,1)S(1)}, bf16[4,3072]{1,0:T(4,128)(2,1)S(1)}, bf16[4,3072]{1,0:T(4,128)(2,1)S(1)}) custom-call(s32[1]{0:T(128)} %bitcast.place, bf16[4,12288]{1,0:T(4,128)(2,1)} %hidden.1, f32[1,12288]{1,0:T(1,128)} %bitcast.8, f32[1,12288]{1,0:T(1,128)} %bitcast.9), custom_call_target="tpu_custom_call" | custom-call | bytes 4194304 | tf_op jit(solution)/shard_map/pallas_call | solution.py:213
  1.9 0.7 %collective-permute-done.1.refs_11_ = f32[1,128]{1,0:T(1,128)S(1)} collective-permute-done((f32[1,128]{1,0:T(1,128)}, f32[1,128]{1,0:T(1,128)S(1)}, u32[]{:S(2)}, u32[]{:S(2)}) %collective-permute-start.1) | collective-permute-done | bytes 544 | tf_op jit(solution)/shard_map/ppermute | solution.py:204
  2.6 2.9 %collective-permute-start.2 = (bf16[4,3072]{1,0:T(4,128)(2,1)S(1)}, bf16[4,3072]{1,0:T(4,128)(2,1)S(1)}, u32[]{:S(2)}, u32[]{:S(2)}) collective-permute-start(bf16[4,3072]{1,0:T(4,128)(2,1)S(1)} %get-tuple-element.59), channel_id=1, source_target_pairs={{0,4},{1,5},{2,6},{3,7},{4,0},{5,1},{6,2},{7,3},{8,12},{9,13},{10,... | collective-permute-start | bytes 73736 | tf_op jit(solution)/shard_map/ppermute | solution.py:198
  5.5 2.6 %collective-permute-start.3 = (bf16[4,3072]{1,0:T(4,128)(2,1)S(1)}, bf16[4,3072]{1,0:T(4,128)(2,1)S(1)}, u32[]{:S(2)}, u32[]{:S(2)}) collective-permute-start(bf16[4,3072]{1,0:T(4,128)(2,1)S(1)} %get-tuple-element.60), channel_id=1, source_target_pairs={{0,8},{1,9},{2,10},{3,11},{4,12},{5,13},{6,14},{7,15},{8,0},{9,1},... | collective-permute-start | bytes 73736 | tf_op jit(solution)/shard_map/ppermute | solution.py:198
  8.1 2.4 %collective-permute-done.3.refs_2_ = bf16[4,3072]{1,0:T(4,128)(2,1)S(1)} collective-permute-done((bf16[4,3072]{1,0:T(4,128)(2,1)S(1)}, bf16[4,3072]{1,0:T(4,128)(2,1)S(1)}, u32[]{:S(2)}, u32[]{:S(2)}) %collective-permute-start.3) | collective-permute-done | bytes 24608 | tf_op jit(solution)/shard_map/ppermute | solution.py:198
  10.5 3.3 %collective-permute-done.4.refs_3_ = bf16[4,3072]{1,0:T(4,128)(2,1)S(1)} collective-permute-done((bf16[4,3072]{1,0:T(4,128)(2,1)S(1)}, bf16[4,3072]{1,0:T(4,128)(2,1)S(1)}, u32[]{:S(2)}, u32[]{:S(2)}) %collective-permute-start.4) | collective-permute-done | bytes 24608 | tf_op jit(solution)/shard_map/ppermute | solution.py:198
  13.9 1.6 %collective-permute-start.6 = (bf16[4,12288]{1,0:T(4,128)(2,1)S(1)}, bf16[4,12288]{1,0:T(4,128)(2,1)S(1)}, u32[]{:S(2)}, u32[]{:S(2)}) collective-permute-start(bf16[4,12288]{1,0:T(4,128)(2,1)S(1)} %get-tuple-element.74.refs_0_), channel_id=1, source_target_pairs={{0,2},{1,3},{2,0},{3,1},{4,6},{5,7},{6,4},{7,5},{8,10},{9,11},{10,... | collective-permute-start | bytes 294920 | tf_op jit(solution)/shard_map/ppermute | solution.py:201
  15.5 0.8 %collective-permute-start.11 = (bf16[4,12288]{1,0:T(4,128)(2,1)S(1)}, bf16[4,12288]{1,0:T(4,128)(2,1)S(1)}, u32[]{:S(2)}, u32[]{:S(2)}) collective-permute-start(bf16[4,12288]{1,0:T(4,128)(2,1)S(1)} %get-tuple-element.74.refs_0_), channel_id=1, source_target_pairs={{0,8},{1,9},{2,10},{3,11},{4,12},{5,13},{6,14},{7,15},{8,0},{9,1},... | collective-permute-start | bytes 294920 | tf_op jit(solution)/shard_map/ppermute | solution.py:198
  16.3 3.6 %collective-permute-start.12 = (bf16[4,12288]{1,0:T(4,128)(2,1)S(1)}, bf16[4,12288]{1,0:T(4,128)(2,1)S(1)}, u32[]{:S(2)}, u32[]{:S(2)}) collective-permute-start(bf16[4,12288]{1,0:T(4,128)(2,1)S(1)} %get-tuple-element.74.refs_0_), channel_id=1, source_target_pairs={{0,12},{1,13},{2,14},{3,15},{4,8},{5,9},{6,10},{7,11},{8,4},{9,5},... | collective-permute-start | bytes 294920 | tf_op jit(solution)/shard_map/ppermute | solution.py:198
  19.9 0.8 %collective-permute-start.5 = (bf16[16,1536]{1,0:T(8,128)(2,1)S(1)}, bf16[16,1536]{1,0:T(8,128)(2,1)S(1)}, u32[]{:S(2)}, u32[]{:S(2)}) collective-permute-start(bf16[16,1536]{1,0:T(8,128)(2,1)S(1)} %get-tuple-element.68), channel_id=1, source_target_pairs={{0,2},{1,3},{2,0},{3,1},{4,6},{5,7},{6,4},{7,5},{8,10},{9,11},{10,... | collective-permute-start | bytes 147464 | tf_op jit(solution)/shard_map/ppermute | solution.py:201
  20.7 3.2 %shard_map.120 = (bf16[768,512]{1,0:T(8,128)(2,1)S(1)}, bf16[12288,128]{1,0:T(8,128)(2,1)S(1)}, bf16[128,12288]{1,0:T(8,128)(2,1)S(1)}, bf16[512,768]{1,0:T(8,128)(2,1)S(1)}) custom-call(bf16[768,512]{1,0:T(8,128)(2,1)} %refs_0_.1, bf16[12288,128]{1,0:T(8,128)(2,1)} %refs_1_.1, bf16[128,12288]{1,0:T(8,128)(2,1)} %refs_2_.1, bf16[512,768]{1,0:T(8,128)(2,1)} %refs_3_.1), custom_call_target="tpu_custom_call" | custom-call | bytes 8388608 | tf_op jit(solution)/shard_map/pallas_call | solution.py:235
  24.4 1.9 %collective-permute-done.11.refs_2_ = bf16[4,12288]{1,0:T(4,128)(2,1)S(1)} collective-permute-done((bf16[4,12288]{1,0:T(4,128)(2,1)S(1)}, bf16[4,12288]{1,0:T(4,128)(2,1)S(1)}, u32[]{:S(2)}, u32[]{:S(2)}) %collective-permute-start.11) | collective-permute-done | bytes 98336 | tf_op jit(solution)/shard_map/ppermute | solution.py:198
  26.4 0.6 collective-permute-start.9
  27.0 1.5 %collective-permute-start.7 = (bf16[32,512]{1,0:T(8,128)(2,1)S(1)}, bf16[32,512]{1,0:T(8,128)(2,1)S(1)}, u32[]{:S(2)}, u32[]{:S(2)}) collective-permute-start(bf16[32,512]{1,0:T(8,128)(2,1)S(1)} %get-tuple-element.73), channel_id=1, source_target_pairs={{0,2},{1,3},{2,0},{3,1},{4,6},{5,7},{6,4},{7,5},{8,10},{9,11},{10,... | collective-permute-start | bytes 98312 | tf_op jit(solution)/shard_map/ppermute | solution.py:201
  28.5 3.8 %collective-permute-done.7.got = bf16[32,512]{1,0:T(8,128)(2,1)S(1)} collective-permute-done((bf16[32,512]{1,0:T(8,128)(2,1)S(1)}, bf16[32,512]{1,0:T(8,128)(2,1)S(1)}, u32[]{:S(2)}, u32[]{:S(2)}) %collective-permute-start.7) | collective-permute-done | bytes 32800 | tf_op jit(solution)/shard_map/ppermute | solution.py:201
  32.3 0.6 collective-permute-start.13
  32.9 1.5 %collective-permute-start.14 = (bf16[4,12288]{1,0:T(4,128)(2,1)S(1)}, bf16[4,12288]{1,0:T(4,128)(2,1)S(1)}, u32[]{:S(2)}, u32[]{:S(2)}) collective-permute-start(bf16[4,12288]{1,0:T(4,128)(2,1)S(1)} %collective-permute-done.12.refs_3_), channel_id=1, source_target_pairs={{0,2},{1,3},{2,0},{3,1},{4,6},{5,7},{6,4},{7,5},{8,10},{9,11},{10,... | collective-permute-start | bytes 294920 | tf_op jit(solution)/shard_map/ppermute | solution.py:201
  34.4 1.5 %collective-permute-start.17 = (bf16[32,512]{1,0:T(8,128)(2,1)S(1)}, bf16[32,512]{1,0:T(8,128)(2,1)S(1)}, u32[]{:S(2)}, u32[]{:S(2)}) collective-permute-start(bf16[32,512]{1,0:T(8,128)(2,1)S(1)} %get-tuple-element.86), channel_id=1, source_target_pairs={{0,12},{1,13},{2,14},{3,15},{4,8},{5,9},{6,10},{7,11},{8,4},{9,5},... | collective-permute-start | bytes 98312 | tf_op jit(solution)/shard_map/ppermute | solution.py:198
  35.9 2.1 %collective-permute-done.13.refs_6_ = bf16[4,12288]{1,0:T(4,128)(2,1)S(1)} collective-permute-done((bf16[4,12288]{1,0:T(4,128)(2,1)S(1)}, bf16[4,12288]{1,0:T(4,128)(2,1)S(1)}, u32[]{:S(2)}, u32[]{:S(2)}) %collective-permute-start.13) | collective-permute-done | bytes 98336 | tf_op jit(solution)/shard_map/ppermute | solution.py:201
  38.0 1.8 %collective-permute-start.18 = (bf16[32,512]{1,0:T(8,128)(2,1)S(1)}, bf16[32,512]{1,0:T(8,128)(2,1)S(1)}, u32[]{:S(2)}, u32[]{:S(2)}) collective-permute-start(bf16[32,512]{1,0:T(8,128)(2,1)S(1)} %get-tuple-element.87), channel_id=1, source_target_pairs={{0,8},{1,9},{2,10},{3,11},{4,12},{5,13},{6,14},{7,15},{8,0},{9,1},... | collective-permute-start | bytes 98312 | tf_op jit(solution)/shard_map/ppermute | solution.py:198
  39.8 1.7 %collective-permute-start.19 = (bf16[32,512]{1,0:T(8,128)(2,1)S(1)}, bf16[32,512]{1,0:T(8,128)(2,1)S(1)}, u32[]{:S(2)}, u32[]{:S(2)}) collective-permute-start(bf16[32,512]{1,0:T(8,128)(2,1)S(1)} %get-tuple-element.88), channel_id=1, source_target_pairs={{0,4},{1,5},{2,6},{3,7},{4,0},{5,1},{6,2},{7,3},{8,12},{9,13},{10,... | collective-permute-start | bytes 98312 | tf_op jit(solution)/shard_map/ppermute | solution.py:198
  41.5 1.9 %shard_map.123.act = bf16[32,256]{1,0:T(8,128)(2,1)S(1)} custom-call(s32[1]{0:T(128)} %bitcast.place, s32[4,6]{1,0:T(4,128)S(1)} %copy-done, s32[4]{0:T(128)S(1)} %copy-done.2, s32[16]{0:T(128)S(1)} %copy-done.3, bf16[4,12288]{1,0:T(4,128)(2,1)S(1)} %get-tuple-element.74.refs_0_, bf16[4,12288]{1,0:T(4,128)(2,1)S(1)} %collective-permute-done.8.refs_1_, ...), custom_call_target="tpu_custom_call" | custom-call | bytes 4194304 | tf_op jit(solution)/shard_map/pallas_call | solution.py:258
  43.4 1.2 %shard_map.124.part = f32[32,12288]{1,0:T(8,128)S(1)} custom-call(bf16[32,256]{1,0:T(8,128)(2,1)S(1)} %shard_map.123.act, bf16[128,12288]{1,0:T(8,128)(2,1)S(1)} %get-tuple-element.84.w_own, bf16[128,12288]{1,0:T(8,128)(2,1)S(1)} %collective-permute-done.16.w_mate), custom_call_target="tpu_custom_call" | custom-call | bytes 6291456 | tf_op jit(solution)/shard_map/pallas_call | solution.py:273
  45.1 0.6 collective-permute-start.21
  45.7 1.5 %collective-permute-start.20 = (bf16[4,12288]{1,0:T(4,128)(2,1)S(1)}, bf16[4,12288]{1,0:T(4,128)(2,1)S(1)}, u32[]{:S(2)}, u32[]{:S(2)}) collective-permute-start(bf16[4,12288]{1,0:T(4,128)(2,1)S(1)} %get-tuple-element.92), channel_id=1, source_target_pairs={{0,2},{1,3},{2,0},{3,1},{4,6},{5,7},{6,4},{7,5},{8,10},{9,11},{10,... | collective-permute-start | bytes 294920 | tf_op jit(solution)/shard_map/ppermute | solution.py:201
  47.7 3.2 %collective-permute-done.21 = bf16[4,12288]{1,0:T(4,128)(2,1)S(1)} collective-permute-done((bf16[4,12288]{1,0:T(4,128)(2,1)S(1)}, bf16[4,12288]{1,0:T(4,128)(2,1)S(1)}, u32[]{:S(2)}, u32[]{:S(2)}) %collective-permute-start.21) | collective-permute-done | bytes 98336 | tf_op jit(solution)/shard_map/ppermute | solution.py:201
  51.0 1.5 %collective-permute-start.26 = (bf16[4,12288]{1,0:T(4,128)(2,1)S(1)}, bf16[4,12288]{1,0:T(4,128)(2,1)S(1)}, u32[]{:S(2)}, u32[]{:S(2)}) collective-permute-start(bf16[4,12288]{1,0:T(4,128)(2,1)S(1)} %add_convert_fusion.2), channel_id=1, source_target_pairs={{0,12},{1,13},{2,14},{3,15},{4,8},{5,9},{6,10},{7,11},{8,4},{9,5},... | collective-permute-start | bytes 294920 | tf_op jit(solution)/shard_map/ppermute | solution.py:198
  52.5 0.8 %collective-permute-start.25 = (bf16[4,12288]{1,0:T(4,128)(2,1)S(1)}, bf16[4,12288]{1,0:T(4,128)(2,1)S(1)}, u32[]{:S(2)}, u32[]{:S(2)}) collective-permute-start(bf16[4,12288]{1,0:T(4,128)(2,1)S(1)} %add_convert_fusion.1), channel_id=1, source_target_pairs={{0,8},{1,9},{2,10},{3,11},{4,12},{5,13},{6,14},{7,15},{8,0},{9,1},... | collective-permute-start | bytes 294920 | tf_op jit(solution)/shard_map/ppermute | solution.py:198
  54.3 1.7 %collective-permute-start.24 = (bf16[4,12288]{1,0:T(4,128)(2,1)S(1)}, bf16[4,12288]{1,0:T(4,128)(2,1)S(1)}, u32[]{:S(2)}, u32[]{:S(2)}) collective-permute-start(bf16[4,12288]{1,0:T(4,128)(2,1)S(1)} %add_convert_fusion), channel_id=1, source_target_pairs={{0,4},{1,5},{2,6},{3,7},{4,0},{5,1},{6,2},{7,3},{8,12},{9,13},{10,... | collective-permute-start | bytes 294920 | tf_op jit(solution)/shard_map/ppermute | solution.py:198
  56.0 1.9 %collective-permute-done.22 = bf16[4,12288]{1,0:T(4,128)(2,1)S(1)} collective-permute-done((bf16[4,12288]{1,0:T(4,128)(2,1)S(1)}, bf16[4,12288]{1,0:T(4,128)(2,1)S(1)}, u32[]{:S(2)}, u32[]{:S(2)}) %collective-permute-start.22) | collective-permute-done | bytes 98336 | tf_op jit(solution)/shard_map/ppermute | solution.py:201
  58.0 2.1 %collective-permute-done.24.refs_1_ = bf16[4,12288]{1,0:T(4,128)(2,1)S(1)} collective-permute-done((bf16[4,12288]{1,0:T(4,128)(2,1)S(1)}, bf16[4,12288]{1,0:T(4,128)(2,1)S(1)}, u32[]{:S(2)}, u32[]{:S(2)}) %collective-permute-start.24) | collective-permute-done | bytes 98336 | tf_op jit(solution)/shard_map/ppermute | solution.py:198
  60.1 0.7 %shard_map.126 = bf16[4,12288]{1,0:T(4,128)(2,1)} custom-call(f32[4,12288]{1,0:T(4,128)S(1)} %convert_add_fusion.refs_0_, bf16[4,12288]{1,0:T(4,128)(2,1)S(1)} %collective-permute-done.24.refs_1_, bf16[4,12288]{1,0:T(4,128)(2,1)S(1)} %collective-permute-done.25.refs_2_, bf16[4,12288]{1,0:T(4,128)(2,1)S(1)} %collective-permute-done.26.refs_3_), custom_call_target="tpu_custom_call" | custom-call | bytes 2097152 | tf_op jit(solution)/shard_map/pallas_call | solution.py:302
  (49 shorter events, 3.4 us)
Async XLA Ops:
  0.0 2.6 %collective-permute-start = (bf16[768,512]{1,0:T(8,128)(2,1)}, bf16[768,512]{1,0:T(8,128)(2,1)S(1)}, u32[]{:S(2)}, u32[]{:S(2)}) collective-permute-start(bf16[768,512]{1,0:T(8,128)(2,1)} %refs_0_.1), channel_id=1, source_target_pairs={{0,1},{1,0},{2,3},{3,2},{4,5},{5,4},{6,7},{7,6},{8,9},{9,8},{10,11... | collective-permute-start | bytes 2359304 | tf_op jit(solution)/shard_map/ppermute | solution.py:204
  0.5 2.1 %collective-permute-start.1 = (f32[1,128]{1,0:T(1,128)}, f32[1,128]{1,0:T(1,128)S(1)}, u32[]{:S(2)}, u32[]{:S(2)}) collective-permute-start(f32[1,128]{1,0:T(1,128)} %bitcast.6), channel_id=1, source_target_pairs={{0,1},{1,0},{2,3},{3,2},{4,5},{5,4},{6,7},{7,6},{8,9},{9,8},{10,11... | collective-permute-start | bytes 1544 | tf_op jit(solution)/shard_map/ppermute | solution.py:204
  2.6 5.5 %collective-permute-start.2 = (bf16[4,3072]{1,0:T(4,128)(2,1)S(1)}, bf16[4,3072]{1,0:T(4,128)(2,1)S(1)}, u32[]{:S(2)}, u32[]{:S(2)}) collective-permute-start(bf16[4,3072]{1,0:T(4,128)(2,1)S(1)} %get-tuple-element.59), channel_id=1, source_target_pairs={{0,4},{1,5},{2,6},{3,7},{4,0},{5,1},{6,2},{7,3},{8,12},{9,13},{10,... | collective-permute-start | bytes 73736 | tf_op jit(solution)/shard_map/ppermute | solution.py:198
  5.5 5.0 %collective-permute-start.3 = (bf16[4,3072]{1,0:T(4,128)(2,1)S(1)}, bf16[4,3072]{1,0:T(4,128)(2,1)S(1)}, u32[]{:S(2)}, u32[]{:S(2)}) collective-permute-start(bf16[4,3072]{1,0:T(4,128)(2,1)S(1)} %get-tuple-element.60), channel_id=1, source_target_pairs={{0,8},{1,9},{2,10},{3,11},{4,12},{5,13},{6,14},{7,15},{8,0},{9,1},... | collective-permute-start | bytes 73736 | tf_op jit(solution)/shard_map/ppermute | solution.py:198
  8.1 5.6 %collective-permute-start.4 = (bf16[4,3072]{1,0:T(4,128)(2,1)S(1)}, bf16[4,3072]{1,0:T(4,128)(2,1)S(1)}, u32[]{:S(2)}, u32[]{:S(2)}) collective-permute-start(bf16[4,3072]{1,0:T(4,128)(2,1)S(1)} %get-tuple-element.61), channel_id=1, source_target_pairs={{0,12},{1,13},{2,14},{3,15},{4,8},{5,9},{6,10},{7,11},{8,4},{9,5},... | collective-permute-start | bytes 73736 | tf_op jit(solution)/shard_map/ppermute | solution.py:198
  13.8 18.5 %copy-start.6 = (bf16[512,768]{1,0:T(8,128)(2,1)S(1)}, bf16[512,768]{1,0:T(8,128)(2,1)}, u32[]{:S(2)}) copy-start(bf16[512,768]{1,0:T(8,128)(2,1)} %refs_3_.1) | copy-start | bytes 2359300
  13.8 27.7 %copy-start = (s32[4,6]{1,0:T(4,128)S(1)}, s32[4,6]{1,0:T(4,128)}, u32[]{:S(2)}) copy-start(s32[4,6]{1,0:T(4,128)} %lists.1) | copy-start | bytes 292
  13.8 27.6 %copy-start.2 = (s32[4]{0:T(128)S(1)}, s32[4]{0:T(128)}, u32[]{:S(2)}) copy-start(s32[4]{0:T(128)} %counts.1) | copy-start | bytes 52
  13.8 27.6 %copy-start.3 = (s32[16]{0:T(128)S(1)}, s32[16]{0:T(128)}, u32[]{:S(2)}) copy-start(s32[16]{0:T(128)} %block_slot.1) | copy-start | bytes 196
  13.8 27.6 %copy-start.4 = (f32[128]{0:T(128)S(1)}, f32[128]{0:T(128)}, u32[]{:S(2)}) copy-start(f32[128]{0:T(128)} %param.19) | copy-start | bytes 1540
  13.8 12.5 %collective-permute-start.15 = (bf16[12288,128]{1,0:T(8,128)(2,1)}, bf16[12288,128]{1,0:T(8,128)(2,1)S(1)}, u32[]{:S(2)}, u32[]{:S(2)}) collective-permute-start(bf16[12288,128]{1,0:T(8,128)(2,1)} %refs_1_.1), channel_id=1, source_target_pairs={{0,1},{1,0},{2,3},{3,2},{4,5},{5,4},{6,7},{7,6},{8,9},{9,8},{10,11... | collective-permute-start | bytes 9437192 | tf_op jit(solution)/shard_map/ppermute | solution.py:204
  13.9 6.0 %collective-permute-start.6 = (bf16[4,12288]{1,0:T(4,128)(2,1)S(1)}, bf16[4,12288]{1,0:T(4,128)(2,1)S(1)}, u32[]{:S(2)}, u32[]{:S(2)}) collective-permute-start(bf16[4,12288]{1,0:T(4,128)(2,1)S(1)} %get-tuple-element.74.refs_0_), channel_id=1, source_target_pairs={{0,2},{1,3},{2,0},{3,1},{4,6},{5,7},{6,4},{7,5},{8,10},{9,11},{10,... | collective-permute-start | bytes 294920 | tf_op jit(solution)/shard_map/ppermute | solution.py:201
  15.5 8.9 %collective-permute-start.8 = (bf16[4,12288]{1,0:T(4,128)(2,1)S(1)}, bf16[4,12288]{1,0:T(4,128)(2,1)S(1)}, u32[]{:S(2)}, u32[]{:S(2)}) collective-permute-start(bf16[4,12288]{1,0:T(4,128)(2,1)S(1)} %get-tuple-element.74.refs_0_), channel_id=1, source_target_pairs={{0,4},{1,5},{2,6},{3,7},{4,0},{5,1},{6,2},{7,3},{8,12},{9,13},{10,... | collective-permute-start | bytes 294920 | tf_op jit(solution)/shard_map/ppermute | solution.py:198
  15.5 10.8 %collective-permute-start.11 = (bf16[4,12288]{1,0:T(4,128)(2,1)S(1)}, bf16[4,12288]{1,0:T(4,128)(2,1)S(1)}, u32[]{:S(2)}, u32[]{:S(2)}) collective-permute-start(bf16[4,12288]{1,0:T(4,128)(2,1)S(1)} %get-tuple-element.74.refs_0_), channel_id=1, source_target_pairs={{0,8},{1,9},{2,10},{3,11},{4,12},{5,13},{6,14},{7,15},{8,0},{9,1},... | collective-permute-start | bytes 294920 | tf_op jit(solution)/shard_map/ppermute | solution.py:198
  16.3 10.0 %collective-permute-start.12 = (bf16[4,12288]{1,0:T(4,128)(2,1)S(1)}, bf16[4,12288]{1,0:T(4,128)(2,1)S(1)}, u32[]{:S(2)}, u32[]{:S(2)}) collective-permute-start(bf16[4,12288]{1,0:T(4,128)(2,1)S(1)} %get-tuple-element.74.refs_0_), channel_id=1, source_target_pairs={{0,12},{1,13},{2,14},{3,15},{4,8},{5,9},{6,10},{7,11},{8,4},{9,5},... | collective-permute-start | bytes 294920 | tf_op jit(solution)/shard_map/ppermute | solution.py:198
  19.9 4.1 %collective-permute-start.5 = (bf16[16,1536]{1,0:T(8,128)(2,1)S(1)}, bf16[16,1536]{1,0:T(8,128)(2,1)S(1)}, u32[]{:S(2)}, u32[]{:S(2)}) collective-permute-start(bf16[16,1536]{1,0:T(8,128)(2,1)S(1)} %get-tuple-element.68), channel_id=1, source_target_pairs={{0,2},{1,3},{2,0},{3,1},{4,6},{5,7},{6,4},{7,5},{8,10},{9,11},{10,... | collective-permute-start | bytes 147464 | tf_op jit(solution)/shard_map/ppermute | solution.py:201
  26.3 17.1 %collective-permute-start.16 = (bf16[128,12288]{1,0:T(8,128)(2,1)S(1)}, bf16[128,12288]{1,0:T(8,128)(2,1)S(1)}, u32[]{:S(2)}, u32[]{:S(2)}) collective-permute-start(bf16[128,12288]{1,0:T(8,128)(2,1)S(1)} %copy-done.5), channel_id=1, source_target_pairs={{0,1},{1,0},{2,3},{3,2},{4,5},{5,4},{6,7},{7,6},{8,9},{9,8},{10,11... | collective-permute-start | bytes 9437192 | tf_op jit(solution)/shard_map/ppermute | solution.py:204
  26.4 5.9 %collective-permute-start.9 = (bf16[4,12288]{1,0:T(4,128)(2,1)S(1)}, bf16[4,12288]{1,0:T(4,128)(2,1)S(1)}, u32[]{:S(2)}, u32[]{:S(2)}) collective-permute-start(bf16[4,12288]{1,0:T(4,128)(2,1)S(1)} %collective-permute-done.8.refs_1_), channel_id=1, source_target_pairs={{0,2},{1,3},{2,0},{3,1},{4,6},{5,7},{6,4},{7,5},{8,10},{9,11},{10,... | collective-permute-start | bytes 294920 | tf_op jit(solution)/shard_map/ppermute | solution.py:201
  27.0 5.3 %collective-permute-start.7 = (bf16[32,512]{1,0:T(8,128)(2,1)S(1)}, bf16[32,512]{1,0:T(8,128)(2,1)S(1)}, u32[]{:S(2)}, u32[]{:S(2)}) collective-permute-start(bf16[32,512]{1,0:T(8,128)(2,1)S(1)} %get-tuple-element.73), channel_id=1, source_target_pairs={{0,2},{1,3},{2,0},{3,1},{4,6},{5,7},{6,4},{7,5},{8,10},{9,11},{10,... | collective-permute-start | bytes 98312 | tf_op jit(solution)/shard_map/ppermute | solution.py:201
  32.3 12.3 %collective-permute-start.10 = (bf16[512,768]{1,0:T(8,128)(2,1)S(1)}, bf16[512,768]{1,0:T(8,128)(2,1)S(1)}, u32[]{:S(2)}, u32[]{:S(2)}) collective-permute-start(bf16[512,768]{1,0:T(8,128)(2,1)S(1)} %copy-done.6), channel_id=1, source_target_pairs={{0,1},{1,0},{2,3},{3,2},{4,5},{5,4},{6,7},{7,6},{8,9},{9,8},{10,11... | collective-permute-start | bytes 2359304 | tf_op jit(solution)/shard_map/ppermute | solution.py:204
  32.3 5.7 %collective-permute-start.13 = (bf16[4,12288]{1,0:T(4,128)(2,1)S(1)}, bf16[4,12288]{1,0:T(4,128)(2,1)S(1)}, u32[]{:S(2)}, u32[]{:S(2)}) collective-permute-start(bf16[4,12288]{1,0:T(4,128)(2,1)S(1)} %collective-permute-done.11.refs_2_), channel_id=1, source_target_pairs={{0,2},{1,3},{2,0},{3,1},{4,6},{5,7},{6,4},{7,5},{8,10},{9,11},{10,... | collective-permute-start | bytes 294920 | tf_op jit(solution)/shard_map/ppermute | solution.py:201
  32.9 6.9 %collective-permute-start.14 = (bf16[4,12288]{1,0:T(4,128)(2,1)S(1)}, bf16[4,12288]{1,0:T(4,128)(2,1)S(1)}, u32[]{:S(2)}, u32[]{:S(2)}) collective-permute-start(bf16[4,12288]{1,0:T(4,128)(2,1)S(1)} %collective-permute-done.12.refs_3_), channel_id=1, source_target_pairs={{0,2},{1,3},{2,0},{3,1},{4,6},{5,7},{6,4},{7,5},{8,10},{9,11},{10,... | collective-permute-start | bytes 294920 | tf_op jit(solution)/shard_map/ppermute | solution.py:201
  34.4 10.2 %collective-permute-start.17 = (bf16[32,512]{1,0:T(8,128)(2,1)S(1)}, bf16[32,512]{1,0:T(8,128)(2,1)S(1)}, u32[]{:S(2)}, u32[]{:S(2)}) collective-permute-start(bf16[32,512]{1,0:T(8,128)(2,1)S(1)} %get-tuple-element.86), channel_id=1, source_target_pairs={{0,12},{1,13},{2,14},{3,15},{4,8},{5,9},{6,10},{7,11},{8,4},{9,5},... | collective-permute-start | bytes 98312 | tf_op jit(solution)/shard_map/ppermute | solution.py:198
  38.0 6.6 %collective-permute-start.18 = (bf16[32,512]{1,0:T(8,128)(2,1)S(1)}, bf16[32,512]{1,0:T(8,128)(2,1)S(1)}, u32[]{:S(2)}, u32[]{:S(2)}) collective-permute-start(bf16[32,512]{1,0:T(8,128)(2,1)S(1)} %get-tuple-element.87), channel_id=1, source_target_pairs={{0,8},{1,9},{2,10},{3,11},{4,12},{5,13},{6,14},{7,15},{8,0},{9,1},... | collective-permute-start | bytes 98312 | tf_op jit(solution)/shard_map/ppermute | solution.py:198
  39.8 4.9 %collective-permute-start.19 = (bf16[32,512]{1,0:T(8,128)(2,1)S(1)}, bf16[32,512]{1,0:T(8,128)(2,1)S(1)}, u32[]{:S(2)}, u32[]{:S(2)}) collective-permute-start(bf16[32,512]{1,0:T(8,128)(2,1)S(1)} %get-tuple-element.88), channel_id=1, source_target_pairs={{0,4},{1,5},{2,6},{3,7},{4,0},{5,1},{6,2},{7,3},{8,12},{9,13},{10,... | collective-permute-start | bytes 98312 | tf_op jit(solution)/shard_map/ppermute | solution.py:198
  45.1 5.8 %collective-permute-start.21 = (bf16[4,12288]{1,0:T(4,128)(2,1)S(1)}, bf16[4,12288]{1,0:T(4,128)(2,1)S(1)}, u32[]{:S(2)}, u32[]{:S(2)}) collective-permute-start(bf16[4,12288]{1,0:T(4,128)(2,1)S(1)} %get-tuple-element.94), channel_id=1, source_target_pairs={{0,2},{1,3},{2,0},{3,1},{4,6},{5,7},{6,4},{7,5},{8,10},{9,11},{10,... | collective-permute-start | bytes 294920 | tf_op jit(solution)/shard_map/ppermute | solution.py:201
  45.7 6.8 %collective-permute-start.20 = (bf16[4,12288]{1,0:T(4,128)(2,1)S(1)}, bf16[4,12288]{1,0:T(4,128)(2,1)S(1)}, u32[]{:S(2)}, u32[]{:S(2)}) collective-permute-start(bf16[4,12288]{1,0:T(4,128)(2,1)S(1)} %get-tuple-element.92), channel_id=1, source_target_pairs={{0,2},{1,3},{2,0},{3,1},{4,6},{5,7},{6,4},{7,5},{8,10},{9,11},{10,... | collective-permute-start | bytes 294920 | tf_op jit(solution)/shard_map/ppermute | solution.py:201
  47.2 7.1 %collective-permute-start.23 = (bf16[4,12288]{1,0:T(4,128)(2,1)S(1)}, bf16[4,12288]{1,0:T(4,128)(2,1)S(1)}, u32[]{:S(2)}, u32[]{:S(2)}) collective-permute-start(bf16[4,12288]{1,0:T(4,128)(2,1)S(1)} %get-tuple-element.98), channel_id=1, source_target_pairs={{0,2},{1,3},{2,0},{3,1},{4,6},{5,7},{6,4},{7,5},{8,10},{9,11},{10,... | collective-permute-start | bytes 294920 | tf_op jit(solution)/shard_map/ppermute | solution.py:201
  51.0 9.1 %collective-permute-start.26 = (bf16[4,12288]{1,0:T(4,128)(2,1)S(1)}, bf16[4,12288]{1,0:T(4,128)(2,1)S(1)}, u32[]{:S(2)}, u32[]{:S(2)}) collective-permute-start(bf16[4,12288]{1,0:T(4,128)(2,1)S(1)} %add_convert_fusion.2), channel_id=1, source_target_pairs={{0,12},{1,13},{2,14},{3,15},{4,8},{5,9},{6,10},{7,11},{8,4},{9,5},... | collective-permute-start | bytes 294920 | tf_op jit(solution)/shard_map/ppermute | solution.py:198
  52.5 7.6 %collective-permute-start.25 = (bf16[4,12288]{1,0:T(4,128)(2,1)S(1)}, bf16[4,12288]{1,0:T(4,128)(2,1)S(1)}, u32[]{:S(2)}, u32[]{:S(2)}) collective-permute-start(bf16[4,12288]{1,0:T(4,128)(2,1)S(1)} %add_convert_fusion.1), channel_id=1, source_target_pairs={{0,8},{1,9},{2,10},{3,11},{4,12},{5,13},{6,14},{7,15},{8,0},{9,1},... | collective-permute-start | bytes 294920 | tf_op jit(solution)/shard_map/ppermute | solution.py:198
  53.3 4.6 %collective-permute-start.22 = (bf16[4,12288]{1,0:T(4,128)(2,1)S(1)}, bf16[4,12288]{1,0:T(4,128)(2,1)S(1)}, u32[]{:S(2)}, u32[]{:S(2)}) collective-permute-start(bf16[4,12288]{1,0:T(4,128)(2,1)S(1)} %get-tuple-element.96), channel_id=1, source_target_pairs={{0,2},{1,3},{2,0},{3,1},{4,6},{5,7},{6,4},{7,5},{8,10},{9,11},{10,... | collective-permute-start | bytes 294920 | tf_op jit(solution)/shard_map/ppermute | solution.py:201
  54.3 5.8 %collective-permute-start.24 = (bf16[4,12288]{1,0:T(4,128)(2,1)S(1)}, bf16[4,12288]{1,0:T(4,128)(2,1)S(1)}, u32[]{:S(2)}, u32[]{:S(2)}) collective-permute-start(bf16[4,12288]{1,0:T(4,128)(2,1)S(1)} %add_convert_fusion), channel_id=1, source_target_pairs={{0,4},{1,5},{2,6},{3,7},{4,0},{5,1},{6,2},{7,3},{8,12},{9,13},{10,... | collective-permute-start | bytes 294920 | tf_op jit(solution)/shard_map/ppermute | solution.py:198
  (2 other events, 13.8 us)

commit v15 on v13

--- a/solution.py
+++ b/solution.py
@@ -61,30 +61,24 @@
         copy.wait()
 
 
-def near_body(groups, place, *refs):
-    held, (gain, shift, near, keep, send) = refs[:groups], refs[groups:]
-    normalise(held, gain, shift, near)
-    span = keep.shape[1]
-    chip = place[0] // 2
-    keep[...] = near[:, window(chip, span)]
-    send[...] = near[:, window(chip ^ 1, span)]
-
-
-def far_body(groups, *refs):
+def near_body(groups, *refs):
     normalise(refs[:groups], *refs[groups:])
 
 
-def down_body(place, keep, got, own, mate, total, message):
+def far_body(groups, place, *refs):
+    held, (near, gain, shift, own, mate, far, total, message) = refs[:groups], refs[groups:]
+    normalise(held, gain, shift, far)
     share = own.shape[0]
     core = place[0] % 2
-    columns = jnp.concatenate([keep[...].astype(f32), got[...].astype(f32)], axis=0)
+    at = window(place[0] // 2, 2 * share)
+    columns = jnp.concatenate([near[:, at].astype(f32), far[:, at].astype(f32)], axis=0)
     low, high = columns[:, :share], columns[:, share:]
     mine = jnp.where(core == 0, low, high).astype(bf16)
     other = jnp.where(core == 0, high, low).astype(bf16)
     sums = jnp.dot(mine, own[...], preferred_element_type=f32) + jnp.dot(
         other, mate[...], preferred_element_type=f32
     )
-    half = keep.shape[0]
+    half = near.shape[0]
     total[...] = sums
     message[:half, :] = sums[half:].astype(bf16)
     message[half:, :] = sums[:half].astype(bf16)
@@ -219,31 +213,24 @@
         8 * MIB,
     )(*[pltpu.with_memory_space_constraint(x, pltpu.HBM) for x in near])
     early, bias_mate = lax.optimization_barrier((hidden, core(bias)))
-    beyond = [beside(early)]
+    beyond = [beside(early), beside(held[1])]
     *_, w_in_mate, low_in_sent, w_out_sent = lax.optimization_barrier(
         (*held, *near, *beyond, w_in_mate, low_in, w_out)
     )
     hidden_near, gain, shift, low_in_near, w_in, w_out_near, low_out_near = near
     low_in_mate, w_out_mate = core(low_in_sent), core(w_out_sent)
-    hidden_near, *beyond = lax.optimization_barrier((hidden_near, *beyond))
-    normed, keep, send = call(
-        functools.partial(near_body, groups),
-        [shape(some, width), shape(some, span), shape(some, span)],
-        [SMEM] + [VMEM] * (groups + 2),
+    normed = call(
+        functools.partial(near_body, groups), [shape(some, width)], [VMEM] * (groups + 2), 16, (), 4 * MIB
+    )(hidden_near, *held[1:], gain, shift)[0]
+    beyond = beyond + [beside(h) for h in held[len(beyond) :]]
+    far, total, message = call(
+        functools.partial(far_body, groups),
+        [shape(some, width), shape(rows, rank, dtype=f32), shape(rows, rank)],
+        [SMEM] + [VMEM] * (groups + 5),
         16,
         (),
         4 * MIB,
-    )(place, hidden_near, *held[1:], gain, shift)
-    send, *late = lax.optimization_barrier((send, *held[2:]))
-    beyond.append(beside(held[1]))
-    got, beyond[1] = lax.optimization_barrier((beside(send), beyond[1]))
-    beyond = beyond + [beside(h) for h in late]
-    total, message = call(
-        down_body, [shape(rows, rank, dtype=f32), shape(rows, rank)], [SMEM] + [VMEM] * 4, 16
-    )(place, keep, got, low_in_near, low_in_mate)
-    far = call(
-        functools.partial(far_body, groups), [shape(some, width)], [VMEM] * (groups + 2), 16, (), 4 * MIB
-    )(*beyond, gain, shift)[0]
+    )(place, *beyond, normed, gain, shift, low_in_near, low_in_mate)
     got, w_out_mate, low_out_sent = lax.optimization_barrier((beside(message), w_out_mate, low_out))
     low_out_mate = core(low_out_sent)
     step = piece(width, 2048)

time: 54.6 us -> 55.6 us (1.018)
  waiting for transfers between devices: 15.2 us -> 19.8 us
  starting transfers between devices: 26.7 us -> 22.9 us
    ppermute x9, waiting for transfers between devices: 2.79 us -> 6.35 us  [across(): return lax.ppermute(x, 'blk', [(i, i ^ 4 * k) for i in range(devices)])]
    ppermute x10 -> x9, starting transfers between devices: 10.9 us -> 9.09 us  [beside(): return lax.ppermute(x, 'blk', [(i, i ^ 2) for i in range(devices)])]
    ppermute x9, starting transfers between devices: 14.8 us -> 13 us  [across(): return lax.ppermute(x, 'blk', [(i, i ^ 4 * k) for i in range(devices)])]
    ppermute x10 -> x9, waiting for transfers between devices: 12.1 us -> 13.5 us  [beside(): return lax.ppermute(x, 'blk', [(i, i ^ 2) for i in range(devices)])]
    pallas_call x3 -> x2, Pallas kernels: 1.55 us -> 1.47 us  [the longest x1 0.88 us: shards(): call(functools.partial(far_body, groups), [shape(some, width), shape(rows...]
  transfers between devices with their start and end apart: 24 -> 23, of which waited for: 9 -> 11; matrix products, arithmetic and copies ran while one was open for 6% -> 6% of each run, Pallas kernels for 14% -> 13%
where the time goes in v15:
time: 55.6 us; the launch traced here: 55.4 us
  starting transfers between devices  22.9 us (41%)
  waiting for transfers between devices  19.8 us (36%)
  Pallas kernels  8.54 us (15%)
  other arithmetic  2.24 us (4%)
  local copies, waits for them, and re-layouts  1.72 us (3%)
    ppermute x9, waiting for transfers between devices, beside(): return lax.ppermute(x, 'blk', [(i, i ^ 2) for i in range(devices)])  13.5 us
    ppermute x9, starting transfers between devices, across(): return lax.ppermute(x, 'blk', [(i, i ^ 4 * k) for i in range(devices)])  13 us
    ppermute x9, starting transfers between devices, beside(): return lax.ppermute(x, 'blk', [(i, i ^ 2) for i in range(devices)])  9.09 us
    ppermute x9, waiting for transfers between devices, across(): return lax.ppermute(x, 'blk', [(i, i ^ 4 * k) for i in range(devices)])  6.35 us
    pallas_call x1, Pallas kernels, shards(): call(functools.partial(load_body, len(near)), [shape(*x.shape, dtype=x.dt...  3.52 us
    unnamed x12, local copies, waits for them, and re-layouts  1.64 us
    pallas_call x1, Pallas kernels, shards(): call(functools.partial(part_body, step), [shape(rows, width, dtype=f32)],...  1.19 us
    pallas_call x1, Pallas kernels, shards(): call(functools.partial(act_body, step), [shape(rows, 2 * block)], [VMEM]...  1.19 us
  transfers between devices with their start and end apart: 23, of which 11 were waited for; matrix products, arithmetic and copies ran while one was open for 6% of the time, Pallas kernels for 13%

profile of v15, /device:TPU:0, one launch (start us, length us, event | category | flops | bytes accessed | tf_op | source)
XLA Modules:
  0.0 55.4 jit_solution(11084506666406250896)
XLA Ops:
  0.5 4.6 %collective-permute-start.6 = (bf16[4,12288]{1,0:T(4,128)(2,1)}, bf16[4,12288]{1,0:T(4,128)(2,1)S(1)}, u32[]{:S(2)}, u32[]{:S(2)}) collective-permute-start(bf16[4,12288]{1,0:T(4,128)(2,1)} %refs_0_), channel_id=1, source_target_pairs={{0,12},{1,13},{2,14},{3,15},{4,8},{5,9},{6,10},{7,11},{8,4},{9,5},... | collective-permute-start | bytes 294920 | tf_op jit(solution)/shard_map/ppermute | solution.py:181
  5.1 0.6 %collective-permute-start.2 = (bf16[4,12288]{1,0:T(4,128)(2,1)}, bf16[4,12288]{1,0:T(4,128)(2,1)S(1)}, u32[]{:S(2)}, u32[]{:S(2)}) collective-permute-start(bf16[4,12288]{1,0:T(4,128)(2,1)} %refs_0_), channel_id=1, source_target_pairs={{0,4},{1,5},{2,6},{3,7},{4,0},{5,1},{6,2},{7,3},{8,12},{9,13},{10,... | collective-permute-start | bytes 294920 | tf_op jit(solution)/shard_map/ppermute | solution.py:181
  5.7 0.8 %copy.13 = s32[4,6]{0,1:T(8,128)S(1)} copy(s32[4,6]{1,0:T(4,128)} %param.15) | data formatting | bytes 192 | tf_op args[3]
  6.5 0.7 %fusion.1 = s32[4,6]{0,1:T(8,128)S(1)} fusion(s32[4]{0:T(128)} %param.16), kind=kLoop, calls=%fused_computation.12 | loop fusion | flops 48 | bytes 112 | tf_op jit(solution)/shard_map/convert_element_type | solution.py:148
  7.4 0.7 %fusion = s32[16,16]{1,0:T(8,128)S(1)} fusion(s32[16]{0:T(128)} %param.17), kind=kLoop, calls=%fused_computation.10 | loop fusion | flops 512 | bytes 1088 | tf_op jit(solution)/shard_map/convert_element_type | solution.py:151
  8.2 1.7 %collective-permute-start.1 = (bf16[4,12288]{1,0:T(4,128)(2,1)}, bf16[4,12288]{1,0:T(4,128)(2,1)S(1)}, u32[]{:S(2)}, u32[]{:S(2)}) collective-permute-start(bf16[4,12288]{1,0:T(4,128)(2,1)} %refs_0_), channel_id=1, source_target_pairs={{0,2},{1,3},{2,0},{3,1},{4,6},{5,7},{6,4},{7,5},{8,10},{9,11},{10,... | collective-permute-start | bytes 294920 | tf_op jit(solution)/shard_map/ppermute | solution.py:184
  9.9 2.4 %collective-permute-done.2.refs_1_ = bf16[4,12288]{1,0:T(4,128)(2,1)S(1)} collective-permute-done((bf16[4,12288]{1,0:T(4,128)(2,1)}, bf16[4,12288]{1,0:T(4,128)(2,1)S(1)}, u32[]{:S(2)}, u32[]{:S(2)}) %collective-permute-start.2) | collective-permute-done | bytes 98336 | tf_op jit(solution)/shard_map/ppermute | solution.py:181
  12.4 1.5 %collective-permute-start.3 = (bf16[4,12288]{1,0:T(4,128)(2,1)S(1)}, bf16[4,12288]{1,0:T(4,128)(2,1)S(1)}, u32[]{:S(2)}, u32[]{:S(2)}) collective-permute-start(bf16[4,12288]{1,0:T(4,128)(2,1)S(1)} %collective-permute-done.2.refs_1_), channel_id=1, source_target_pairs={{0,2},{1,3},{2,0},{3,1},{4,6},{5,7},{6,4},{7,5},{8,10},{9,11},{10,... | collective-permute-start | bytes 294920 | tf_op jit(solution)/shard_map/ppermute | solution.py:184
  14.3 3.5 %shard_map.118 = (bf16[4,12288]{1,0:T(4,128)(2,1)S(1)}, f32[1,12288]{1,0:T(1,128)S(1)}, f32[1,12288]{1,0:T(1,128)S(1)}, bf16[768,512]{1,0:T(8,128)(2,1)S(1)}, bf...) custom-call(bf16[4,12288]{1,0:T(4,128)(2,1)} %refs_0_, ...), custom_call_target="tpu_custom_call" | custom-call | bytes 8388608 | tf_op jit(solution)/shard_map/pallas_call | solution.py:207
  17.9 0.7 %copy-done.2 = bf16[128,12288]{1,0:T(8,128)(2,1)S(1)} copy-done((bf16[128,12288]{1,0:T(8,128)(2,1)S(1)}, bf16[128,12288]{1,0:T(8,128)(2,1)}, u32[]{:S(2)}) %copy-start.2) | copy-done | bytes 3145752
  19.6 1.5 %collective-permute-start.5 = (bf16[4,12288]{1,0:T(4,128)(2,1)S(1)}, bf16[4,12288]{1,0:T(4,128)(2,1)S(1)}, u32[]{:S(2)}, u32[]{:S(2)}) collective-permute-start(bf16[4,12288]{1,0:T(4,128)(2,1)S(1)} %collective-permute-done.4.refs_2_), channel_id=1, source_target_pairs={{0,2},{1,3},{2,0},{3,1},{4,6},{5,7},{6,4},{7,5},{8,10},{9,11},{10,... | collective-permute-start | bytes 294920 | tf_op jit(solution)/shard_map/ppermute | solution.py:184
  21.1 0.6 %shard_map.119.refs_4_.near = bf16[16,12288]{1,0:T(8,128)(2,1)S(1)} custom-call(bf16[4,12288]{1,0:T(4,128)(2,1)S(1)} %get-tuple-element.55.refs_0_, bf16[4,12288]{1,0:T(4,128)(2,1)S(1)} %collective-permute-done.2.refs_1_, bf16[4,12288]{1,0:T(4,128)(2,1)S(1)} %collective-permute-done.4.refs_2_, bf16[4,12288]{1,0:T(4,128)(2,1)S(1)} %collective-permute-done.6.refs_3_, ...), custom_call_target="tpu_custom_call" | custom-call | bytes 4194304 | tf_op jit(solution)/shard_map/pallas_call | solution.py:222
  21.7 3.0 %collective-permute-done.7.refs_3_ = bf16[4,12288]{1,0:T(4,128)(2,1)S(1)} collective-permute-done((bf16[4,12288]{1,0:T(4,128)(2,1)S(1)}, bf16[4,12288]{1,0:T(4,128)(2,1)S(1)}, u32[]{:S(2)}, u32[]{:S(2)}) %collective-permute-start.7) | collective-permute-done | bytes 98336 | tf_op jit(solution)/shard_map/ppermute | solution.py:184
  24.7 1.4 %collective-permute-done.5.refs_2_ = bf16[4,12288]{1,0:T(4,128)(2,1)S(1)} collective-permute-done((bf16[4,12288]{1,0:T(4,128)(2,1)S(1)}, bf16[4,12288]{1,0:T(4,128)(2,1)S(1)}, u32[]{:S(2)}, u32[]{:S(2)}) %collective-permute-start.5) | collective-permute-done | bytes 98336 | tf_op jit(solution)/shard_map/ppermute | solution.py:184
  26.1 0.9 %shard_map.120 = (bf16[16,12288]{1,0:T(8,128)(2,1)S(1)}, f32[32,512]{1,0:T(8,128)S(1)}, bf16[32,512]{1,0:T(8,128)(2,1)S(1)}) custom-call(s32[1]{0:T(128)} %bitcast.place, bf16[4,12288]{1,0:T(4,128)(2,1)S(1)} %collective-permute-done.1.refs_0_, bf16[4,12288]{1,0:T(4,128)(2,1)S(1)} %collective-permute-done.3.refs_1_, ...), custom_call_target="tpu_custom_call" | custom-call | bytes 4194304 | tf_op jit(solution)/shard_map/pallas_call | solution.py:226
  27.5 3.4 %collective-permute-done.10.got = bf16[32,512]{1,0:T(8,128)(2,1)S(1)} collective-permute-done((bf16[32,512]{1,0:T(8,128)(2,1)S(1)}, bf16[32,512]{1,0:T(8,128)(2,1)S(1)}, u32[]{:S(2)}, u32[]{:S(2)}) %collective-permute-start.10) | collective-permute-done | bytes 32800 | tf_op jit(solution)/shard_map/ppermute | solution.py:184
  30.9 2.3 %collective-permute-start.13 = (bf16[32,512]{1,0:T(8,128)(2,1)S(1)}, bf16[32,512]{1,0:T(8,128)(2,1)S(1)}, u32[]{:S(2)}, u32[]{:S(2)}) collective-permute-start(bf16[32,512]{1,0:T(8,128)(2,1)S(1)} %get-tuple-element.74), channel_id=1, source_target_pairs={{0,12},{1,13},{2,14},{3,15},{4,8},{5,9},{6,10},{7,11},{8,4},{9,5},... | collective-permute-start | bytes 98312 | tf_op jit(solution)/shard_map/ppermute | solution.py:181
  33.2 1.6 %collective-permute-start.14 = (bf16[32,512]{1,0:T(8,128)(2,1)S(1)}, bf16[32,512]{1,0:T(8,128)(2,1)S(1)}, u32[]{:S(2)}, u32[]{:S(2)}) collective-permute-start(bf16[32,512]{1,0:T(8,128)(2,1)S(1)} %get-tuple-element.75), channel_id=1, source_target_pairs={{0,8},{1,9},{2,10},{3,11},{4,12},{5,13},{6,14},{7,15},{8,0},{9,1},... | collective-permute-start | bytes 98312 | tf_op jit(solution)/shard_map/ppermute | solution.py:181
  34.8 0.5 collective-permute-start.15
  35.4 1.2 %shard_map.122.act = bf16[32,256]{1,0:T(8,128)(2,1)S(1)} custom-call(bf16[16,12288]{1,0:T(8,128)(2,1)S(1)} %shard_map.119.refs_4_.near, bf16[16,12288]{1,0:T(8,128)(2,1)S(1)} %get-tuple-element.69.far, bf16[12288,128]{1,0:T(8,128)(2,1)S(1)} %get-tuple-element.59.w_own, bf16[12288,128]{1,0:T(8,128)(2,1)S(1)} %collective-permute-done.8.w_mate, ...), custom_call_target="tpu_custom_call" | custom-call | bytes 4194304 | tf_op jit(solution)/shard_map/pallas_call | solution.py:237
  36.6 1.2 %shard_map.123.part = f32[32,12288]{1,0:T(8,128)S(1)} custom-call(bf16[32,256]{1,0:T(8,128)(2,1)S(1)} %shard_map.122.act, bf16[128,12288]{1,0:T(8,128)(2,1)S(1)} %get-tuple-element.60.w_own, bf16[128,12288]{1,0:T(8,128)(2,1)S(1)} %collective-permute-done.11.w_mate), custom_call_target="tpu_custom_call" | custom-call | bytes 6291456 | tf_op jit(solution)/shard_map/pallas_call | solution.py:252
  37.8 0.9 %collective-permute-done.14.refs_1_ = bf16[32,512]{1,0:T(8,128)(2,1)S(1)} collective-permute-done((bf16[32,512]{1,0:T(8,128)(2,1)S(1)}, bf16[32,512]{1,0:T(8,128)(2,1)S(1)}, u32[]{:S(2)}, u32[]{:S(2)}) %collective-permute-start.14) | collective-permute-done | bytes 32800 | tf_op jit(solution)/shard_map/ppermute | solution.py:181
  39.5 0.6 %collective-permute-start.17 = (bf16[4,12288]{1,0:T(4,128)(2,1)S(1)}, bf16[4,12288]{1,0:T(4,128)(2,1)S(1)}, u32[]{:S(2)}, u32[]{:S(2)}) collective-permute-start(bf16[4,12288]{1,0:T(4,128)(2,1)S(1)} %get-tuple-element.82), channel_id=1, source_target_pairs={{0,2},{1,3},{2,0},{3,1},{4,6},{5,7},{6,4},{7,5},{8,10},{9,11},{10,... | collective-permute-start | bytes 294920 | tf_op jit(solution)/shard_map/ppermute | solution.py:184
  40.1 1.5 %collective-permute-start.16 = (bf16[4,12288]{1,0:T(4,128)(2,1)S(1)}, bf16[4,12288]{1,0:T(4,128)(2,1)S(1)}, u32[]{:S(2)}, u32[]{:S(2)}) collective-permute-start(bf16[4,12288]{1,0:T(4,128)(2,1)S(1)} %get-tuple-element.80), channel_id=1, source_target_pairs={{0,2},{1,3},{2,0},{3,1},{4,6},{5,7},{6,4},{7,5},{8,10},{9,11},{10,... | collective-permute-start | bytes 294920 | tf_op jit(solution)/shard_map/ppermute | solution.py:184
  42.1 3.2 %collective-permute-done.17 = bf16[4,12288]{1,0:T(4,128)(2,1)S(1)} collective-permute-done((bf16[4,12288]{1,0:T(4,128)(2,1)S(1)}, bf16[4,12288]{1,0:T(4,128)(2,1)S(1)}, u32[]{:S(2)}, u32[]{:S(2)}) %collective-permute-start.17) | collective-permute-done | bytes 98336 | tf_op jit(solution)/shard_map/ppermute | solution.py:184
  45.3 1.2 %collective-permute-start.22 = (bf16[4,12288]{1,0:T(4,128)(2,1)S(1)}, bf16[4,12288]{1,0:T(4,128)(2,1)S(1)}, u32[]{:S(2)}, u32[]{:S(2)}) collective-permute-start(bf16[4,12288]{1,0:T(4,128)(2,1)S(1)} %add_convert_fusion.2), channel_id=1, source_target_pairs={{0,12},{1,13},{2,14},{3,15},{4,8},{5,9},{6,10},{7,11},{8,4},{9,5},... | collective-permute-start | bytes 294920 | tf_op jit(solution)/shard_map/ppermute | solution.py:181
  47.4 0.7 %collective-permute-start.18 = (bf16[4,12288]{1,0:T(4,128)(2,1)S(1)}, bf16[4,12288]{1,0:T(4,128)(2,1)S(1)}, u32[]{:S(2)}, u32[]{:S(2)}) collective-permute-start(bf16[4,12288]{1,0:T(4,128)(2,1)S(1)} %get-tuple-element.84), channel_id=1, source_target_pairs={{0,2},{1,3},{2,0},{3,1},{4,6},{5,7},{6,4},{7,5},{8,10},{9,11},{10,... | collective-permute-start | bytes 294920 | tf_op jit(solution)/shard_map/ppermute | solution.py:184
  48.0 0.6 %collective-permute-done.19 = bf16[4,12288]{1,0:T(4,128)(2,1)S(1)} collective-permute-done((bf16[4,12288]{1,0:T(4,128)(2,1)S(1)}, bf16[4,12288]{1,0:T(4,128)(2,1)S(1)}, u32[]{:S(2)}, u32[]{:S(2)}) %collective-permute-start.19) | collective-permute-done | bytes 98336 | tf_op jit(solution)/shard_map/ppermute | solution.py:184
  48.7 1.8 %collective-permute-start.20 = (bf16[4,12288]{1,0:T(4,128)(2,1)S(1)}, bf16[4,12288]{1,0:T(4,128)(2,1)S(1)}, u32[]{:S(2)}, u32[]{:S(2)}) collective-permute-start(bf16[4,12288]{1,0:T(4,128)(2,1)S(1)} %add_convert_fusion), channel_id=1, source_target_pairs={{0,4},{1,5},{2,6},{3,7},{4,0},{5,1},{6,2},{7,3},{8,12},{9,13},{10,... | collective-permute-start | bytes 294920 | tf_op jit(solution)/shard_map/ppermute | solution.py:181
  50.5 1.5 %collective-permute-done.18 = bf16[4,12288]{1,0:T(4,128)(2,1)S(1)} collective-permute-done((bf16[4,12288]{1,0:T(4,128)(2,1)S(1)}, bf16[4,12288]{1,0:T(4,128)(2,1)S(1)}, u32[]{:S(2)}, u32[]{:S(2)}) %collective-permute-start.18) | collective-permute-done | bytes 98336 | tf_op jit(solution)/shard_map/ppermute | solution.py:184
  52.0 2.6 %collective-permute-done.21.refs_2_ = bf16[4,12288]{1,0:T(4,128)(2,1)S(1)} collective-permute-done((bf16[4,12288]{1,0:T(4,128)(2,1)S(1)}, bf16[4,12288]{1,0:T(4,128)(2,1)S(1)}, u32[]{:S(2)}, u32[]{:S(2)}) %collective-permute-start.21) | collective-permute-done | bytes 98336 | tf_op jit(solution)/shard_map/ppermute | solution.py:181
  54.7 0.7 %shard_map.125 = bf16[4,12288]{1,0:T(4,128)(2,1)} custom-call(f32[4,12288]{1,0:T(4,128)S(1)} %convert_add_fusion.refs_0_, bf16[4,12288]{1,0:T(4,128)(2,1)S(1)} %collective-permute-done.20.refs_1_, bf16[4,12288]{1,0:T(4,128)(2,1)S(1)} %collective-permute-done.21.refs_2_, bf16[4,12288]{1,0:T(4,128)(2,1)S(1)} %collective-permute-done.22.refs_3_), custom_call_target="tpu_custom_call" | custom-call | bytes 2097152 | tf_op jit(solution)/shard_map/pallas_call | solution.py:281
  (49 shorter events, 5.0 us)
Async XLA Ops:
  0.0 17.9 %collective-permute-start.8 = (bf16[12288,128]{1,0:T(8,128)(2,1)}, bf16[12288,128]{1,0:T(8,128)(2,1)S(1)}, u32[]{:S(2)}, u32[]{:S(2)}) collective-permute-start(bf16[12288,128]{1,0:T(8,128)(2,1)} %refs_4_), channel_id=1, source_target_pairs={{0,1},{1,0},{2,3},{3,2},{4,5},{5,4},{6,7},{7,6},{8,9},{9,8},{10,11... | collective-permute-start | bytes 9437192 | tf_op jit(solution)/shard_map/ppermute | solution.py:187
  0.5 17.4 %collective-permute-start.6 = (bf16[4,12288]{1,0:T(4,128)(2,1)}, bf16[4,12288]{1,0:T(4,128)(2,1)S(1)}, u32[]{:S(2)}, u32[]{:S(2)}) collective-permute-start(bf16[4,12288]{1,0:T(4,128)(2,1)} %refs_0_), channel_id=1, source_target_pairs={{0,12},{1,13},{2,14},{3,15},{4,8},{5,9},{6,10},{7,11},{8,4},{9,5},... | collective-permute-start | bytes 294920 | tf_op jit(solution)/shard_map/ppermute | solution.py:181
  5.1 12.8 %collective-permute-start.4 = (bf16[4,12288]{1,0:T(4,128)(2,1)}, bf16[4,12288]{1,0:T(4,128)(2,1)S(1)}, u32[]{:S(2)}, u32[]{:S(2)}) collective-permute-start(bf16[4,12288]{1,0:T(4,128)(2,1)} %refs_0_), channel_id=1, source_target_pairs={{0,8},{1,9},{2,10},{3,11},{4,12},{5,13},{6,14},{7,15},{8,0},{9,1},... | collective-permute-start | bytes 294920 | tf_op jit(solution)/shard_map/ppermute | solution.py:181
  5.1 7.3 %collective-permute-start.2 = (bf16[4,12288]{1,0:T(4,128)(2,1)}, bf16[4,12288]{1,0:T(4,128)(2,1)S(1)}, u32[]{:S(2)}, u32[]{:S(2)}) collective-permute-start(bf16[4,12288]{1,0:T(4,128)(2,1)} %refs_0_), channel_id=1, source_target_pairs={{0,4},{1,5},{2,6},{3,7},{4,0},{5,1},{6,2},{7,3},{8,12},{9,13},{10,... | collective-permute-start | bytes 294920 | tf_op jit(solution)/shard_map/ppermute | solution.py:181
  5.7 2.5 %collective-permute-start = (f32[1,128]{1,0:T(1,128)}, f32[1,128]{1,0:T(1,128)S(1)}, u32[]{:S(2)}, u32[]{:S(2)}) collective-permute-start(f32[1,128]{1,0:T(1,128)} %bitcast.12), channel_id=1, source_target_pairs={{0,1},{1,0},{2,3},{3,2},{4,5},{5,4},{6,7},{7,6},{8,9},{9,8},{10,11... | collective-permute-start | bytes 1544 | tf_op jit(solution)/shard_map/ppermute | solution.py:187
  8.2 9.7 %collective-permute-start.1 = (bf16[4,12288]{1,0:T(4,128)(2,1)}, bf16[4,12288]{1,0:T(4,128)(2,1)S(1)}, u32[]{:S(2)}, u32[]{:S(2)}) collective-permute-start(bf16[4,12288]{1,0:T(4,128)(2,1)} %refs_0_), channel_id=1, source_target_pairs={{0,2},{1,3},{2,0},{3,1},{4,6},{5,7},{6,4},{7,5},{8,10},{9,11},{10,... | collective-permute-start | bytes 294920 | tf_op jit(solution)/shard_map/ppermute | solution.py:184
  12.4 5.5 %collective-permute-start.3 = (bf16[4,12288]{1,0:T(4,128)(2,1)S(1)}, bf16[4,12288]{1,0:T(4,128)(2,1)S(1)}, u32[]{:S(2)}, u32[]{:S(2)}) collective-permute-start(bf16[4,12288]{1,0:T(4,128)(2,1)S(1)} %collective-permute-done.2.refs_1_), channel_id=1, source_target_pairs={{0,2},{1,3},{2,0},{3,1},{4,6},{5,7},{6,4},{7,5},{8,10},{9,11},{10,... | collective-permute-start | bytes 294920 | tf_op jit(solution)/shard_map/ppermute | solution.py:184
  14.3 4.3 %copy-start.2 = (bf16[128,12288]{1,0:T(8,128)(2,1)S(1)}, bf16[128,12288]{1,0:T(8,128)(2,1)}, u32[]{:S(2)}) copy-start(bf16[128,12288]{1,0:T(8,128)(2,1)} %refs_5_) | copy-start | bytes 9437188
  14.3 4.5 %copy-start.3 = (bf16[768,512]{1,0:T(8,128)(2,1)S(1)}, bf16[768,512]{1,0:T(8,128)(2,1)}, u32[]{:S(2)}) copy-start(bf16[768,512]{1,0:T(8,128)(2,1)} %refs_3_) | copy-start | bytes 2359300
  17.8 13.1 %copy-start.4 = (bf16[512,768]{1,0:T(8,128)(2,1)S(1)}, bf16[512,768]{1,0:T(8,128)(2,1)}, u32[]{:S(2)}) copy-start(bf16[512,768]{1,0:T(8,128)(2,1)} %refs_6_) | copy-start | bytes 2359300
  17.8 17.5 %copy-start.1 = (f32[128]{0:T(128)S(1)}, f32[128]{0:T(128)}, u32[]{:S(2)}) copy-start(f32[128]{0:T(128)} %param.19) | copy-start | bytes 1540
  18.6 12.3 %collective-permute-start.11 = (bf16[128,12288]{1,0:T(8,128)(2,1)S(1)}, bf16[128,12288]{1,0:T(8,128)(2,1)S(1)}, u32[]{:S(2)}, u32[]{:S(2)}) collective-permute-start(bf16[128,12288]{1,0:T(8,128)(2,1)S(1)} %copy-done.2), channel_id=1, source_target_pairs={{0,1},{1,0},{2,3},{3,2},{4,5},{5,4},{6,7},{7,6},{8,9},{9,8},{10,11... | collective-permute-start | bytes 9437192 | tf_op jit(solution)/shard_map/ppermute | solution.py:187
  18.7 7.3 %collective-permute-start.9 = (bf16[768,512]{1,0:T(8,128)(2,1)S(1)}, bf16[768,512]{1,0:T(8,128)(2,1)S(1)}, u32[]{:S(2)}, u32[]{:S(2)}) collective-permute-start(bf16[768,512]{1,0:T(8,128)(2,1)S(1)} %copy-done.3), channel_id=1, source_target_pairs={{0,1},{1,0},{2,3},{3,2},{4,5},{5,4},{6,7},{7,6},{8,9},{9,8},{10,11... | collective-permute-start | bytes 2359304 | tf_op jit(solution)/shard_map/ppermute | solution.py:187
  19.1 5.6 %collective-permute-start.7 = (bf16[4,12288]{1,0:T(4,128)(2,1)S(1)}, bf16[4,12288]{1,0:T(4,128)(2,1)S(1)}, u32[]{:S(2)}, u32[]{:S(2)}) collective-permute-start(bf16[4,12288]{1,0:T(4,128)(2,1)S(1)} %collective-permute-done.6.refs_3_), channel_id=1, source_target_pairs={{0,2},{1,3},{2,0},{3,1},{4,6},{5,7},{6,4},{7,5},{8,10},{9,11},{10,... | collective-permute-start | bytes 294920 | tf_op jit(solution)/shard_map/ppermute | solution.py:184
  19.6 6.5 %collective-permute-start.5 = (bf16[4,12288]{1,0:T(4,128)(2,1)S(1)}, bf16[4,12288]{1,0:T(4,128)(2,1)S(1)}, u32[]{:S(2)}, u32[]{:S(2)}) collective-permute-start(bf16[4,12288]{1,0:T(4,128)(2,1)S(1)} %collective-permute-done.4.refs_2_), channel_id=1, source_target_pairs={{0,2},{1,3},{2,0},{3,1},{4,6},{5,7},{6,4},{7,5},{8,10},{9,11},{10,... | collective-permute-start | bytes 294920 | tf_op jit(solution)/shard_map/ppermute | solution.py:184
  26.9 3.9 %collective-permute-start.10 = (bf16[32,512]{1,0:T(8,128)(2,1)S(1)}, bf16[32,512]{1,0:T(8,128)(2,1)S(1)}, u32[]{:S(2)}, u32[]{:S(2)}) collective-permute-start(bf16[32,512]{1,0:T(8,128)(2,1)S(1)} %get-tuple-element.64), channel_id=1, source_target_pairs={{0,2},{1,3},{2,0},{3,1},{4,6},{5,7},{6,4},{7,5},{8,10},{9,11},{10,... | collective-permute-start | bytes 98312 | tf_op jit(solution)/shard_map/ppermute | solution.py:184
  30.9 8.2 %collective-permute-start.12 = (bf16[512,768]{1,0:T(8,128)(2,1)S(1)}, bf16[512,768]{1,0:T(8,128)(2,1)S(1)}, u32[]{:S(2)}, u32[]{:S(2)}) collective-permute-start(bf16[512,768]{1,0:T(8,128)(2,1)S(1)} %copy-done.4), channel_id=1, source_target_pairs={{0,1},{1,0},{2,3},{3,2},{4,5},{5,4},{6,7},{7,6},{8,9},{9,8},{10,11... | collective-permute-start | bytes 2359304 | tf_op jit(solution)/shard_map/ppermute | solution.py:187
  30.9 6.9 %collective-permute-start.13 = (bf16[32,512]{1,0:T(8,128)(2,1)S(1)}, bf16[32,512]{1,0:T(8,128)(2,1)S(1)}, u32[]{:S(2)}, u32[]{:S(2)}) collective-permute-start(bf16[32,512]{1,0:T(8,128)(2,1)S(1)} %get-tuple-element.74), channel_id=1, source_target_pairs={{0,12},{1,13},{2,14},{3,15},{4,8},{5,9},{6,10},{7,11},{8,4},{9,5},... | collective-permute-start | bytes 98312 | tf_op jit(solution)/shard_map/ppermute | solution.py:181
  33.2 5.5 %collective-permute-start.14 = (bf16[32,512]{1,0:T(8,128)(2,1)S(1)}, bf16[32,512]{1,0:T(8,128)(2,1)S(1)}, u32[]{:S(2)}, u32[]{:S(2)}) collective-permute-start(bf16[32,512]{1,0:T(8,128)(2,1)S(1)} %get-tuple-element.75), channel_id=1, source_target_pairs={{0,8},{1,9},{2,10},{3,11},{4,12},{5,13},{6,14},{7,15},{8,0},{9,1},... | collective-permute-start | bytes 98312 | tf_op jit(solution)/shard_map/ppermute | solution.py:181
  34.8 4.2 %collective-permute-start.15 = (bf16[32,512]{1,0:T(8,128)(2,1)S(1)}, bf16[32,512]{1,0:T(8,128)(2,1)S(1)}, u32[]{:S(2)}, u32[]{:S(2)}) collective-permute-start(bf16[32,512]{1,0:T(8,128)(2,1)S(1)} %get-tuple-element.76), channel_id=1, source_target_pairs={{0,4},{1,5},{2,6},{3,7},{4,0},{5,1},{6,2},{7,3},{8,12},{9,13},{10,... | collective-permute-start | bytes 98312 | tf_op jit(solution)/shard_map/ppermute | solution.py:181
  36.6 2.5 %copy-start = (f32[512]{0:T(512)S(1)}, f32[512]{0:T(512)}, u32[]{:S(2)}) copy-start(f32[512]{0:T(512)} %param.22) | copy-start | bytes 6148
  39.5 5.8 %collective-permute-start.17 = (bf16[4,12288]{1,0:T(4,128)(2,1)S(1)}, bf16[4,12288]{1,0:T(4,128)(2,1)S(1)}, u32[]{:S(2)}, u32[]{:S(2)}) collective-permute-start(bf16[4,12288]{1,0:T(4,128)(2,1)S(1)} %get-tuple-element.82), channel_id=1, source_target_pairs={{0,2},{1,3},{2,0},{3,1},{4,6},{5,7},{6,4},{7,5},{8,10},{9,11},{10,... | collective-permute-start | bytes 294920 | tf_op jit(solution)/shard_map/ppermute | solution.py:184
  40.1 7.0 %collective-permute-start.16 = (bf16[4,12288]{1,0:T(4,128)(2,1)S(1)}, bf16[4,12288]{1,0:T(4,128)(2,1)S(1)}, u32[]{:S(2)}, u32[]{:S(2)}) collective-permute-start(bf16[4,12288]{1,0:T(4,128)(2,1)S(1)} %get-tuple-element.80), channel_id=1, source_target_pairs={{0,2},{1,3},{2,0},{3,1},{4,6},{5,7},{6,4},{7,5},{8,10},{9,11},{10,... | collective-permute-start | bytes 294920 | tf_op jit(solution)/shard_map/ppermute | solution.py:184
  41.6 7.0 %collective-permute-start.19 = (bf16[4,12288]{1,0:T(4,128)(2,1)S(1)}, bf16[4,12288]{1,0:T(4,128)(2,1)S(1)}, u32[]{:S(2)}, u32[]{:S(2)}) collective-permute-start(bf16[4,12288]{1,0:T(4,128)(2,1)S(1)} %get-tuple-element.86), channel_id=1, source_target_pairs={{0,2},{1,3},{2,0},{3,1},{4,6},{5,7},{6,4},{7,5},{8,10},{9,11},{10,... | collective-permute-start | bytes 294920 | tf_op jit(solution)/shard_map/ppermute | solution.py:184
  45.3 9.3 %collective-permute-start.22 = (bf16[4,12288]{1,0:T(4,128)(2,1)S(1)}, bf16[4,12288]{1,0:T(4,128)(2,1)S(1)}, u32[]{:S(2)}, u32[]{:S(2)}) collective-permute-start(bf16[4,12288]{1,0:T(4,128)(2,1)S(1)} %add_convert_fusion.2), channel_id=1, source_target_pairs={{0,12},{1,13},{2,14},{3,15},{4,8},{5,9},{6,10},{7,11},{8,4},{9,5},... | collective-permute-start | bytes 294920 | tf_op jit(solution)/shard_map/ppermute | solution.py:181
  47.1 7.5 %collective-permute-start.21 = (bf16[4,12288]{1,0:T(4,128)(2,1)S(1)}, bf16[4,12288]{1,0:T(4,128)(2,1)S(1)}, u32[]{:S(2)}, u32[]{:S(2)}) collective-permute-start(bf16[4,12288]{1,0:T(4,128)(2,1)S(1)} %add_convert_fusion.1), channel_id=1, source_target_pairs={{0,8},{1,9},{2,10},{3,11},{4,12},{5,13},{6,14},{7,15},{8,0},{9,1},... | collective-permute-start | bytes 294920 | tf_op jit(solution)/shard_map/ppermute | solution.py:181
  47.4 4.6 %collective-permute-start.18 = (bf16[4,12288]{1,0:T(4,128)(2,1)S(1)}, bf16[4,12288]{1,0:T(4,128)(2,1)S(1)}, u32[]{:S(2)}, u32[]{:S(2)}) collective-permute-start(bf16[4,12288]{1,0:T(4,128)(2,1)S(1)} %get-tuple-element.84), channel_id=1, source_target_pairs={{0,2},{1,3},{2,0},{3,1},{4,6},{5,7},{6,4},{7,5},{8,10},{9,11},{10,... | collective-permute-start | bytes 294920 | tf_op jit(solution)/shard_map/ppermute | solution.py:184
  48.7 6.0 %collective-permute-start.20 = (bf16[4,12288]{1,0:T(4,128)(2,1)S(1)}, bf16[4,12288]{1,0:T(4,128)(2,1)S(1)}, u32[]{:S(2)}, u32[]{:S(2)}) collective-permute-start(bf16[4,12288]{1,0:T(4,128)(2,1)S(1)} %add_convert_fusion), channel_id=1, source_target_pairs={{0,4},{1,5},{2,6},{3,7},{4,0},{5,1},{6,2},{7,3},{8,12},{9,13},{10,... | collective-permute-start | bytes 294920 | tf_op jit(solution)/shard_map/ppermute | solution.py:181

commit v16 on v15

--- a/solution.py
+++ b/solution.py
@@ -123,15 +123,32 @@
     out[...] = total.astype(bf16)
 
 
-def act_body(step, near, far, w_own, w_mate, b_own, b_mate, mask, out):
+def act_body(groups, step, place, lists, counts, block_slot, near, far, w_own, w_mate, b_own, b_mate, out):
+    block, row_dev = w_own.shape[1], near.shape[0] // groups
     total = jnp.zeros(out.shape, f32)
-    for i in range(near.shape[1] // step):
+    for i in range(w_own.shape[0] // step):
         at = slice(i * step, (i + 1) * step)
         rows = jnp.concatenate([near[:, at], far[:, at]], axis=0)
         both = jnp.concatenate([w_own[at, :], w_mate[at, :]], axis=1)
         total = total + jnp.dot(rows, both, preferred_element_type=f32)
     bias = jnp.concatenate([b_own[...], b_mate[...]], axis=1)
-    out[...] = (jnp.maximum(total + bias, 0.0) * mask[...]).astype(bf16)
+    act = jnp.maximum(total + bias, 0.0)
+    row_k = (lax.broadcasted_iota(jnp.int32, out.shape, 0) // row_dev) % groups
+    column_b = lax.broadcasted_iota(jnp.int32, out.shape, 1) // block
+    uses = jnp.zeros(out.shape, jnp.int32)
+    for k in range(groups):
+        group = (place[0] // 4) ^ k
+
+        def hit(e, found):
+            slot = block_slot[lists[group, e]]
+            live = e < counts[group]
+            own = jnp.where(live & (slot == place[0]), 1, 0)
+            mate = jnp.where(live & (slot == place[0] ^ 1), 1, 0)
+            return found[0] + own, found[1] + mate
+
+        own, mate = lax.fori_loop(0, lists.shape[1], hit, (jnp.int32(0), jnp.int32(0)))
+        uses = jnp.where(row_k == k, jnp.where(column_b == 0, own, mate), uses)
+    out[...] = jnp.where(uses > 0, act, 0.0).astype(bf16)
 
 
 def part_body(step, act, w_own, w_mate, out):
@@ -139,17 +156,6 @@
         at = slice(i * step, (i + 1) * step)
         both = jnp.concatenate([w_own[:, at], w_mate[:, at]], axis=0)
         out[:, at] = jnp.dot(act[...], both, preferred_element_type=f32)
-
-
-def activity(lists, counts, block_slot):
-    groups, top = lists.shape
-    nblocks = block_slot.shape[0]
-    names = jnp.arange(nblocks, dtype=jnp.int32)
-    live = (jnp.arange(top, dtype=jnp.int32)[None, :] < counts[:, None]).astype(jnp.int32)
-    hits = (lists[:, :, None] == names[None, None, :]).astype(jnp.int32) * live[:, :, None]
-    by_block = jnp.sum(hits, axis=1)
-    placed = (block_slot[:, None] == names[None, :]).astype(jnp.int32)
-    return jnp.sum(by_block[:, :, None] * placed[None, :, :], axis=1)
 
 
 def shards(
@@ -192,18 +198,9 @@
     gain, shift, bias = ln_gain.reshape(1, width), ln_shift.reshape(1, width), b_in.reshape(1, block)
     span = 2 * share
 
-    table = activity(lists, counts, block_slot)
-    by = plane ^ jnp.arange(groups)
-    at = position ^ jnp.arange(2)
-    relate = (by[:, None] == jnp.arange(groups)[None, :])[:, None, :, None]
-    choose = (at[:, None] == jnp.arange(devices)[None, :])[None, :, None, :]
-    live = jnp.sum(jnp.where(relate & choose, table[None, None], 0), axis=(2, 3)).astype(f32)
-    mask = jnp.broadcast_to(live[None, :, None, :, None], (2, groups, row_dev, 2, block)).reshape(rows, 2 * block)
-
     held = [hidden] + [across(hidden, k) for k in range(1, groups)]
     w_in_mate = core(w_in)
     near = (hidden, gain, shift, low_in, w_in, w_out, low_out)
-    *near, mask = lax.optimization_barrier((*near, mask))
     near = call(
         functools.partial(load_body, len(near)),
         [shape(*x.shape, dtype=x.dtype) for x in near],
@@ -213,6 +210,7 @@
         8 * MIB,
     )(*[pltpu.with_memory_space_constraint(x, pltpu.HBM) for x in near])
     early, bias_mate = lax.optimization_barrier((hidden, core(bias)))
+    held[1], *near = lax.optimization_barrier((held[1], *near))
     beyond = [beside(early), beside(held[1])]
     *_, w_in_mate, low_in_sent, w_out_sent = lax.optimization_barrier(
         (*held, *near, *beyond, w_in_mate, low_in, w_out)
@@ -235,13 +233,13 @@
     low_out_mate = core(low_out_sent)
     step = piece(width, 2048)
     act = call(
-        functools.partial(act_body, step),
+        functools.partial(act_body, groups, step),
         [shape(rows, 2 * block)],
-        [VMEM] * 7,
+        [SMEM] * 4 + [VMEM] * 6,
         16,
         (),
         4 * MIB,
-    )(normed, far, w_in, w_in_mate, bias, bias_mate, mask)[0]
+    )(place, lists, counts, block_slot, normed, far, w_in, w_in_mate, bias, bias_mate)[0]
     total, *messages = call(
         functools.partial(merge_body, groups),
         [shape(rows, rank, dtype=f32)] + [shape(rows, rank)] * (groups - 1),

time: 55.6 us -> 68.4 us (1.23)
  local copies, waits for them, and re-layouts: 1.72 us -> 11.5 us
  starting transfers between devices: 22.9 us -> 27.7 us
  Pallas kernels: 8.54 us -> 12.4 us
  waiting for transfers between devices: 19.8 us -> 16.1 us
  other arithmetic: 2.24 us -> 0.22 us
    unnamed x12 -> x44, local copies, waits for them, and re-layouts: 1.64 us -> 11.5 us
    ppermute x9, waiting for transfers between devices: 6.35 us -> 2.67 us  [across(): return lax.ppermute(x, 'blk', [(i, i ^ 4 * k) for i in range(devices)])]
    ppermute x9, starting transfers between devices: 13 us -> 15.9 us  [across(): return lax.ppermute(x, 'blk', [(i, i ^ 4 * k) for i in range(devices)])]
    pallas_call x1, Pallas kernels: 1.19 us -> 3.15 us  [shards(): call(functools.partial(part_body, step), [shape(rows, width, dtype=f32)],...]
    ppermute x9, starting transfers between devices: 9.09 us -> 10.7 us  [beside(): return lax.ppermute(x, 'blk', [(i, i ^ 2) for i in range(devices)])]
    convert_element_type x3 -> x0, other arithmetic: 1.39 us -> none  [the longest x1 0.73 us: activity(): placed = (block_slot[:, None] == names[None, :]).astype(jnp.int32)]
    pallas_call x1, Pallas kernels: 0.88 us -> 2.08 us  [shards(): call(functools.partial(far_body, groups), [shape(some, width), shape(rows...]
    pallas_call x1, Pallas kernels: 1.19 us -> 2.03 us  [shards(): call(functools.partial(act_body, groups, step), [shape(rows, 2 * block)],...]
  transfers between devices with their start and end apart: 23 -> 23, of which waited for: 11 -> 9; matrix products, arithmetic and copies ran while one was open for 6% -> 0% of each run, Pallas kernels for 13% -> 17%
where the time goes in v16:
time: 68.4 us; the launch traced here: 68.2 us
  starting transfers between devices  27.7 us (40%)
  waiting for transfers between devices  16.1 us (24%)
  Pallas kernels  12.4 us (18%)
  local copies, waits for them, and re-layouts  11.5 us (17%)
    ppermute x9, starting transfers between devices, across(): return lax.ppermute(x, 'blk', [(i, i ^ 4 * k) for i in range(devices)])  15.9 us
    ppermute x9, waiting for transfers between devices, beside(): return lax.ppermute(x, 'blk', [(i, i ^ 2) for i in range(devices)])  13.4 us
    unnamed x44, local copies, waits for them, and re-layouts  11.5 us
    ppermute x9, starting transfers between devices, beside(): return lax.ppermute(x, 'blk', [(i, i ^ 2) for i in range(devices)])  10.7 us
    pallas_call x1, Pallas kernels, shards(): call(functools.partial(load_body, len(near)), [shape(*x.shape, dtype=x.dt...  3.41 us
    pallas_call x1, Pallas kernels, shards(): call(functools.partial(part_body, step), [shape(rows, width, dtype=f32)],...  3.15 us
    ppermute x9, waiting for transfers between devices, across(): return lax.ppermute(x, 'blk', [(i, i ^ 4 * k) for i in range(devices)])  2.67 us
    pallas_call x1, Pallas kernels, shards(): call(functools.partial(far_body, groups), [shape(some, width), shape(rows...  2.08 us
  transfers between devices with their start and end apart: 23, of which 9 were waited for; matrix products, arithmetic and copies ran while one was open for 0% of the time, Pallas kernels for 17%

profile of v16, /device:TPU:0, one launch (start us, length us, event | category | flops | bytes accessed | tf_op | source)
XLA Modules:
  0.0 68.2 jit_solution(13032023371695132436)
XLA Ops:
  0.5 2.6 %collective-permute-start.2 = (bf16[4,12288]{1,0:T(4,128)(2,1)}, bf16[4,12288]{1,0:T(4,128)(2,1)S(1)}, u32[]{:S(2)}, u32[]{:S(2)}) collective-permute-start(bf16[4,12288]{1,0:T(4,128)(2,1)} %refs_0_.1), channel_id=1, source_target_pairs={{0,4},{1,5},{2,6},{3,7},{4,0},{5,1},{6,2},{7,3},{8,12},{9,13},{10,... | collective-permute-start | bytes 294920 | tf_op jit(solution)/shard_map/ppermute | solution.py:187
  3.3 2.6 %collective-permute-start.4 = (bf16[4,12288]{1,0:T(4,128)(2,1)}, bf16[4,12288]{1,0:T(4,128)(2,1)S(1)}, u32[]{:S(2)}, u32[]{:S(2)}) collective-permute-start(bf16[4,12288]{1,0:T(4,128)(2,1)} %refs_0_.1), channel_id=1, source_target_pairs={{0,8},{1,9},{2,10},{3,11},{4,12},{5,13},{6,14},{7,15},{8,0},{9,1},... | collective-permute-start | bytes 294920 | tf_op jit(solution)/shard_map/ppermute | solution.py:187
  5.9 3.4 %shard_map.118 = (bf16[4,12288]{1,0:T(4,128)(2,1)S(1)}, f32[1,12288]{1,0:T(1,128)S(1)}, f32[1,12288]{1,0:T(1,128)S(1)}, bf16[768,512]{1,0:T(8,128)(2,1)S(1)}, bf...) custom-call(bf16[4,12288]{1,0:T(4,128)(2,1)} %refs_0_.1, ...), custom_call_target="tpu_custom_call" | custom-call | bytes 8388608 | tf_op jit(solution)/shard_map/pallas_call | solution.py:204
  9.3 1.7 %copy-done = bf16[12288,128]{1,0:T(8,128)(2,1)} copy-done((bf16[12288,128]{1,0:T(8,128)(2,1)}, bf16[12288,128]{1,0:T(8,128)(2,1)S(1)}, u32[]{:S(2)}) %copy-start) | copy-done | bytes 3145752
  11.0 1.6 %copy-done.2 = bf16[128,12288]{1,0:T(8,128)(2,1)} copy-done((bf16[128,12288]{1,0:T(8,128)(2,1)}, bf16[128,12288]{1,0:T(8,128)(2,1)S(1)}, u32[]{:S(2)}) %copy-start.2) | copy-done | bytes 3145752
  12.6 0.9 %copy-done.4 = bf16[512,768]{1,0:T(8,128)(2,1)} copy-done((bf16[512,768]{1,0:T(8,128)(2,1)}, bf16[512,768]{1,0:T(8,128)(2,1)S(1)}, u32[]{:S(2)}) %copy-start.4) | copy-done | bytes 786456
  13.6 0.9 %copy-done.6 = bf16[768,512]{1,0:T(8,128)(2,1)} copy-done((bf16[768,512]{1,0:T(8,128)(2,1)}, bf16[768,512]{1,0:T(8,128)(2,1)S(1)}, u32[]{:S(2)}) %copy-start.6) | copy-done | bytes 786456
  15.1 1.8 %collective-permute-start.1 = (bf16[4,12288]{1,0:T(4,128)(2,1)S(1)}, bf16[4,12288]{1,0:T(4,128)(2,1)S(1)}, u32[]{:S(2)}, u32[]{:S(2)}) collective-permute-start(bf16[4,12288]{1,0:T(4,128)(2,1)S(1)} %copy-done.21), channel_id=1, source_target_pairs={{0,2},{1,3},{2,0},{3,1},{4,6},{5,7},{6,4},{7,5},{8,10},{9,11},{10,... | collective-permute-start | bytes 294920 | tf_op jit(solution)/shard_map/ppermute | solution.py:190
  17.2 3.5 %collective-permute-done.1.refs_0_ = bf16[4,12288]{1,0:T(4,128)(2,1)S(1)} collective-permute-done((bf16[4,12288]{1,0:T(4,128)(2,1)S(1)}, bf16[4,12288]{1,0:T(4,128)(2,1)S(1)}, u32[]{:S(2)}, u32[]{:S(2)}) %collective-permute-start.1) | collective-permute-done | bytes 98336 | tf_op jit(solution)/shard_map/ppermute | solution.py:190
  23.1 1.5 %collective-permute-start.5 = (bf16[4,12288]{1,0:T(4,128)(2,1)S(1)}, bf16[4,12288]{1,0:T(4,128)(2,1)}, u32[]{:S(2)}, u32[]{:S(2)}) collective-permute-start(bf16[4,12288]{1,0:T(4,128)(2,1)S(1)} %collective-permute-done.4.refs_2_), channel_id=1, source_target_pairs={{0,2},{1,3},{2,0},{3,1},{4,6},{5,7},{6,4},{7,5},{8,10},{9,11},{10,... | collective-permute-start | bytes 294920 | tf_op jit(solution)/shard_map/ppermute | solution.py:190
  25.1 0.9 %copy-done.9 = bf16[4,12288]{1,0:T(4,128)(2,1)S(1)} copy-done((bf16[4,12288]{1,0:T(4,128)(2,1)S(1)}, bf16[4,12288]{1,0:T(4,128)(2,1)}, u32[]{:S(2)}) %copy-start.9) | copy-done | bytes 98328
  26.6 2.1 %collective-permute-done.5.refs_2_ = bf16[4,12288]{1,0:T(4,128)(2,1)} collective-permute-done((bf16[4,12288]{1,0:T(4,128)(2,1)S(1)}, bf16[4,12288]{1,0:T(4,128)(2,1)}, u32[]{:S(2)}, u32[]{:S(2)}) %collective-permute-start.5) | collective-permute-done | bytes 98336 | tf_op jit(solution)/shard_map/ppermute | solution.py:190
  28.8 1.2 %collective-permute-done.7.refs_3_ = bf16[4,12288]{1,0:T(4,128)(2,1)} collective-permute-done((bf16[4,12288]{1,0:T(4,128)(2,1)S(1)}, bf16[4,12288]{1,0:T(4,128)(2,1)}, u32[]{:S(2)}, u32[]{:S(2)}) %collective-permute-start.7) | collective-permute-done | bytes 98336 | tf_op jit(solution)/shard_map/ppermute | solution.py:190
  30.0 1.1 %copy-done.7 = bf16[768,512]{1,0:T(8,128)(2,1)S(1)} copy-done((bf16[768,512]{1,0:T(8,128)(2,1)S(1)}, bf16[768,512]{1,0:T(8,128)(2,1)}, u32[]{:S(2)}) %copy-start.7) | copy-done | bytes 786456
  31.2 0.9 %copy-done.11 = bf16[4,12288]{1,0:T(4,128)(2,1)S(1)} copy-done((bf16[4,12288]{1,0:T(4,128)(2,1)S(1)}, bf16[4,12288]{1,0:T(4,128)(2,1)}, u32[]{:S(2)}) %copy-start.11) | copy-done | bytes 98328
  32.1 0.9 %copy-done.13 = bf16[4,12288]{1,0:T(4,128)(2,1)S(1)} copy-done((bf16[4,12288]{1,0:T(4,128)(2,1)S(1)}, bf16[4,12288]{1,0:T(4,128)(2,1)}, u32[]{:S(2)}) %copy-start.13) | copy-done | bytes 98328
  33.0 2.1 %shard_map.120 = (bf16[16,12288]{1,0:T(8,128)(2,1)S(1)}, f32[32,512]{1,0:T(8,128)S(1)}, bf16[32,512]{1,0:T(8,128)(2,1)S(1)}) custom-call(s32[1]{0:T(128)} %bitcast.place, bf16[4,12288]{1,0:T(4,128)(2,1)S(1)} %copy-done.11, bf16[4,12288]{1,0:T(4,128)(2,1)S(1)} %copy-done.13, bf16[4,12288]{1,0:T(4,128)(2,1)} %collective-permute-done.5.refs_2_, ...), custom_call_target="tpu_custom_call" | custom-call | bytes 4194304 | tf_op jit(solution)/shard_map/pallas_call | solution.py:224
  35.0 1.6 %collective-permute-start.10 = (bf16[32,512]{1,0:T(8,128)(2,1)S(1)}, bf16[32,512]{1,0:T(8,128)(2,1)S(1)}, u32[]{:S(2)}, u32[]{:S(2)}) collective-permute-start(bf16[32,512]{1,0:T(8,128)(2,1)S(1)} %get-tuple-element.65), channel_id=1, source_target_pairs={{0,2},{1,3},{2,0},{3,1},{4,6},{5,7},{6,4},{7,5},{8,10},{9,11},{10,... | collective-permute-start | bytes 98312 | tf_op jit(solution)/shard_map/ppermute | solution.py:190
  36.6 2.4 %collective-permute-done.10.got = bf16[32,512]{1,0:T(8,128)(2,1)S(1)} collective-permute-done((bf16[32,512]{1,0:T(8,128)(2,1)S(1)}, bf16[32,512]{1,0:T(8,128)(2,1)S(1)}, u32[]{:S(2)}, u32[]{:S(2)}) %collective-permute-start.10) | collective-permute-done | bytes 32800 | tf_op jit(solution)/shard_map/ppermute | solution.py:190
  39.0 3.8 %collective-permute-start.13 = (bf16[32,512]{1,0:T(8,128)(2,1)S(1)}, bf16[32,512]{1,0:T(8,128)(2,1)S(1)}, u32[]{:S(2)}, u32[]{:S(2)}) collective-permute-start(bf16[32,512]{1,0:T(8,128)(2,1)S(1)} %get-tuple-element.74), channel_id=1, source_target_pairs={{0,12},{1,13},{2,14},{3,15},{4,8},{5,9},{6,10},{7,11},{8,4},{9,5},... | collective-permute-start | bytes 98312 | tf_op jit(solution)/shard_map/ppermute | solution.py:187
  44.2 2.0 %shard_map.122.act = bf16[32,256]{1,0:T(8,128)(2,1)S(1)} custom-call(s32[1]{0:T(128)} %bitcast.place, s32[4,6]{1,0:T(4,128)S(1)} %copy-done.14, s32[4]{0:T(128)S(1)} %copy-done.16, s32[16]{0:T(128)S(1)} %copy-done.17, bf16[16,12288]{1,0:T(8,128)(2,1)S(1)} %shard_map.119.refs_4_.near, bf16[16,12288]{1,0:T(8,128)(2,1)S(1)} %get-tuple-element.70.far, ...), custom_call_target="tpu_custom_call" | custom-call | bytes 4194304 | tf_op jit(solution)/shard_map/pallas_call | solution.py:235
  46.2 3.1 %shard_map.123.part = f32[32,12288]{1,0:T(8,128)S(1)} custom-call(bf16[32,256]{1,0:T(8,128)(2,1)S(1)} %shard_map.122.act, bf16[128,12288]{1,0:T(8,128)(2,1)S(1)} %copy-done.3, bf16[128,12288]{1,0:T(8,128)(2,1)} %collective-permute-done.11.w_mate), custom_call_target="tpu_custom_call" | custom-call | bytes 6291456 | tf_op jit(solution)/shard_map/pallas_call | solution.py:250
  49.9 1.6 %collective-permute-start.17 = (bf16[4,12288]{1,0:T(4,128)(2,1)S(1)}, bf16[4,12288]{1,0:T(4,128)(2,1)S(1)}, u32[]{:S(2)}, u32[]{:S(2)}) collective-permute-start(bf16[4,12288]{1,0:T(4,128)(2,1)S(1)} %get-tuple-element.82), channel_id=1, source_target_pairs={{0,2},{1,3},{2,0},{3,1},{4,6},{5,7},{6,4},{7,5},{8,10},{9,11},{10,... | collective-permute-start | bytes 294920 | tf_op jit(solution)/shard_map/ppermute | solution.py:190
  52.0 1.5 %collective-permute-start.19 = (bf16[4,12288]{1,0:T(4,128)(2,1)S(1)}, bf16[4,12288]{1,0:T(4,128)(2,1)S(1)}, u32[]{:S(2)}, u32[]{:S(2)}) collective-permute-start(bf16[4,12288]{1,0:T(4,128)(2,1)S(1)} %get-tuple-element.86), channel_id=1, source_target_pairs={{0,2},{1,3},{2,0},{3,1},{4,6},{5,7},{6,4},{7,5},{8,10},{9,11},{10,... | collective-permute-start | bytes 294920 | tf_op jit(solution)/shard_map/ppermute | solution.py:190
  53.5 2.1 %collective-permute-done.17 = bf16[4,12288]{1,0:T(4,128)(2,1)S(1)} collective-permute-done((bf16[4,12288]{1,0:T(4,128)(2,1)S(1)}, bf16[4,12288]{1,0:T(4,128)(2,1)S(1)}, u32[]{:S(2)}, u32[]{:S(2)}) %collective-permute-start.17) | collective-permute-done | bytes 98336 | tf_op jit(solution)/shard_map/ppermute | solution.py:190
  55.7 3.8 %collective-permute-start.22 = (bf16[4,12288]{1,0:T(4,128)(2,1)S(1)}, bf16[4,12288]{1,0:T(4,128)(2,1)S(1)}, u32[]{:S(2)}, u32[]{:S(2)}) collective-permute-start(bf16[4,12288]{1,0:T(4,128)(2,1)S(1)} %add_convert_fusion.2), channel_id=1, source_target_pairs={{0,12},{1,13},{2,14},{3,15},{4,8},{5,9},{6,10},{7,11},{8,4},{9,5},... | collective-permute-start | bytes 294920 | tf_op jit(solution)/shard_map/ppermute | solution.py:187
  60.1 1.3 %collective-permute-start.18 = (bf16[4,12288]{1,0:T(4,128)(2,1)S(1)}, bf16[4,12288]{1,0:T(4,128)(2,1)S(1)}, u32[]{:S(2)}, u32[]{:S(2)}) collective-permute-start(bf16[4,12288]{1,0:T(4,128)(2,1)S(1)} %get-tuple-element.84), channel_id=1, source_target_pairs={{0,2},{1,3},{2,0},{3,1},{4,6},{5,7},{6,4},{7,5},{8,10},{9,11},{10,... | collective-permute-start | bytes 294920 | tf_op jit(solution)/shard_map/ppermute | solution.py:190
  61.5 1.8 %collective-permute-start.20 = (bf16[4,12288]{1,0:T(4,128)(2,1)S(1)}, bf16[4,12288]{1,0:T(4,128)(2,1)S(1)}, u32[]{:S(2)}, u32[]{:S(2)}) collective-permute-start(bf16[4,12288]{1,0:T(4,128)(2,1)S(1)} %add_convert_fusion), channel_id=1, source_target_pairs={{0,4},{1,5},{2,6},{3,7},{4,0},{5,1},{6,2},{7,3},{8,12},{9,13},{10,... | collective-permute-start | bytes 294920 | tf_op jit(solution)/shard_map/ppermute | solution.py:187
  63.4 1.4 %collective-permute-done.18 = bf16[4,12288]{1,0:T(4,128)(2,1)S(1)} collective-permute-done((bf16[4,12288]{1,0:T(4,128)(2,1)S(1)}, bf16[4,12288]{1,0:T(4,128)(2,1)S(1)}, u32[]{:S(2)}, u32[]{:S(2)}) %collective-permute-start.18) | collective-permute-done | bytes 98336 | tf_op jit(solution)/shard_map/ppermute | solution.py:190
  64.8 1.7 %collective-permute-done.21.refs_2_ = bf16[4,12288]{1,0:T(4,128)(2,1)S(1)} collective-permute-done((bf16[4,12288]{1,0:T(4,128)(2,1)S(1)}, bf16[4,12288]{1,0:T(4,128)(2,1)S(1)}, u32[]{:S(2)}, u32[]{:S(2)}) %collective-permute-start.21) | collective-permute-done | bytes 98336 | tf_op jit(solution)/shard_map/ppermute | solution.py:187
  66.5 1.0 %collective-permute-done.20.refs_1_ = bf16[4,12288]{1,0:T(4,128)(2,1)S(1)} collective-permute-done((bf16[4,12288]{1,0:T(4,128)(2,1)S(1)}, bf16[4,12288]{1,0:T(4,128)(2,1)S(1)}, u32[]{:S(2)}, u32[]{:S(2)}) %collective-permute-start.20) | collective-permute-done | bytes 98336 | tf_op jit(solution)/shard_map/ppermute | solution.py:187
  67.5 0.7 %shard_map.125 = bf16[4,12288]{1,0:T(4,128)(2,1)} custom-call(f32[4,12288]{1,0:T(4,128)S(1)} %convert_add_fusion.refs_0_, bf16[4,12288]{1,0:T(4,128)(2,1)S(1)} %collective-permute-done.20.refs_1_, bf16[4,12288]{1,0:T(4,128)(2,1)S(1)} %collective-permute-done.21.refs_2_, bf16[4,12288]{1,0:T(4,128)(2,1)S(1)} %collective-permute-done.22.refs_3_), custom_call_target="tpu_custom_call" | custom-call | bytes 2097152 | tf_op jit(solution)/shard_map/pallas_call | solution.py:279
  (70 shorter events, 8.3 us)
Async XLA Ops:
  0.0 22.6 %collective-permute-start.8 = (bf16[12288,128]{1,0:T(8,128)(2,1)}, bf16[12288,128]{1,0:T(8,128)(2,1)S(1)}, u32[]{:S(2)}, u32[]{:S(2)}) collective-permute-start(bf16[12288,128]{1,0:T(8,128)(2,1)} %refs_4_.1), channel_id=1, source_target_pairs={{0,1},{1,0},{2,3},{3,2},{4,5},{5,4},{6,7},{7,6},{8,9},{9,8},{10,11... | collective-permute-start | bytes 9437192 | tf_op jit(solution)/shard_map/ppermute | solution.py:193
  0.5 16.4 %collective-permute-start.2 = (bf16[4,12288]{1,0:T(4,128)(2,1)}, bf16[4,12288]{1,0:T(4,128)(2,1)S(1)}, u32[]{:S(2)}, u32[]{:S(2)}) collective-permute-start(bf16[4,12288]{1,0:T(4,128)(2,1)} %refs_0_.1), channel_id=1, source_target_pairs={{0,4},{1,5},{2,6},{3,7},{4,0},{5,1},{6,2},{7,3},{8,12},{9,13},{10,... | collective-permute-start | bytes 294920 | tf_op jit(solution)/shard_map/ppermute | solution.py:187
  3.0 12.1 %collective-permute-start = (f32[1,128]{1,0:T(1,128)}, f32[1,128]{1,0:T(1,128)S(1)}, u32[]{:S(2)}, u32[]{:S(2)}) collective-permute-start(f32[1,128]{1,0:T(1,128)} %bitcast.6), channel_id=1, source_target_pairs={{0,1},{1,0},{2,3},{3,2},{4,5},{5,4},{6,7},{7,6},{8,9},{9,8},{10,11... | collective-permute-start | bytes 1544 | tf_op jit(solution)/shard_map/ppermute | solution.py:193
  3.3 14.0 %collective-permute-start.4 = (bf16[4,12288]{1,0:T(4,128)(2,1)}, bf16[4,12288]{1,0:T(4,128)(2,1)S(1)}, u32[]{:S(2)}, u32[]{:S(2)}) collective-permute-start(bf16[4,12288]{1,0:T(4,128)(2,1)} %refs_0_.1), channel_id=1, source_target_pairs={{0,8},{1,9},{2,10},{3,11},{4,12},{5,13},{6,14},{7,15},{8,0},{9,1},... | collective-permute-start | bytes 294920 | tf_op jit(solution)/shard_map/ppermute | solution.py:187
  5.8 11.4 %collective-permute-start.6 = (bf16[4,12288]{1,0:T(4,128)(2,1)}, bf16[4,12288]{1,0:T(4,128)(2,1)S(1)}, u32[]{:S(2)}, u32[]{:S(2)}) collective-permute-start(bf16[4,12288]{1,0:T(4,128)(2,1)} %refs_0_.1), channel_id=1, source_target_pairs={{0,12},{1,13},{2,14},{3,15},{4,8},{5,9},{6,10},{7,11},{8,4},{9,5},... | collective-permute-start | bytes 294920 | tf_op jit(solution)/shard_map/ppermute | solution.py:187
  5.9 9.2 %copy-start.21 = (bf16[4,12288]{1,0:T(4,128)(2,1)S(1)}, bf16[4,12288]{1,0:T(4,128)(2,1)}, u32[]{:S(2)}) copy-start(bf16[4,12288]{1,0:T(4,128)(2,1)} %refs_0_.1) | copy-start | bytes 294916
  15.1 28.4 %copy-start.14 = (s32[4,6]{1,0:T(4,128)S(1)}, s32[4,6]{1,0:T(4,128)}, u32[]{:S(2)}) copy-start(s32[4,6]{1,0:T(4,128)} %lists.1) | copy-start | bytes 292
  15.1 28.4 %copy-start.16 = (s32[4]{0:T(128)S(1)}, s32[4]{0:T(128)}, u32[]{:S(2)}) copy-start(s32[4]{0:T(128)} %counts.1) | copy-start | bytes 52
  15.1 28.4 %copy-start.17 = (s32[16]{0:T(128)S(1)}, s32[16]{0:T(128)}, u32[]{:S(2)}) copy-start(s32[16]{0:T(128)} %block_slot.1) | copy-start | bytes 196
  15.1 28.4 %copy-start.18 = (f32[128]{0:T(128)S(1)}, f32[128]{0:T(128)}, u32[]{:S(2)}) copy-start(f32[128]{0:T(128)} %param.19) | copy-start | bytes 1540
  15.1 8.0 %copy-start.19 = (f32[1,128]{1,0:T(1,128)}, f32[1,128]{1,0:T(1,128)S(1)}, u32[]{:S(2)}) copy-start(f32[1,128]{1,0:T(1,128)S(1)} %collective-permute-done.b_mate) | copy-start | bytes 1540
  15.1 5.6 %collective-permute-start.1 = (bf16[4,12288]{1,0:T(4,128)(2,1)S(1)}, bf16[4,12288]{1,0:T(4,128)(2,1)S(1)}, u32[]{:S(2)}, u32[]{:S(2)}) collective-permute-start(bf16[4,12288]{1,0:T(4,128)(2,1)S(1)} %copy-done.21), channel_id=1, source_target_pairs={{0,2},{1,3},{2,0},{3,1},{4,6},{5,7},{6,4},{7,5},{8,10},{9,11},{10,... | collective-permute-start | bytes 294920 | tf_op jit(solution)/shard_map/ppermute | solution.py:190
  16.9 5.1 %collective-permute-start.3 = (bf16[4,12288]{1,0:T(4,128)(2,1)S(1)}, bf16[4,12288]{1,0:T(4,128)(2,1)S(1)}, u32[]{:S(2)}, u32[]{:S(2)}) collective-permute-start(bf16[4,12288]{1,0:T(4,128)(2,1)S(1)} %collective-permute-done.2.refs_1_), channel_id=1, source_target_pairs={{0,2},{1,3},{2,0},{3,1},{4,6},{5,7},{6,4},{7,5},{8,10},{9,11},{10,... | collective-permute-start | bytes 294920 | tf_op jit(solution)/shard_map/ppermute | solution.py:190
  22.6 16.4 %collective-permute-start.11 = (bf16[128,12288]{1,0:T(8,128)(2,1)}, bf16[128,12288]{1,0:T(8,128)(2,1)}, u32[]{:S(2)}, u32[]{:S(2)}) collective-permute-start(bf16[128,12288]{1,0:T(8,128)(2,1)} %refs_5_.1), channel_id=1, source_target_pairs={{0,1},{1,0},{2,3},{3,2},{4,5},{5,4},{6,7},{7,6},{8,9},{9,8},{10,11... | collective-permute-start | bytes 9437192 | tf_op jit(solution)/shard_map/ppermute | solution.py:193
  22.6 7.4 %collective-permute-start.9 = (bf16[768,512]{1,0:T(8,128)(2,1)}, bf16[768,512]{1,0:T(8,128)(2,1)}, u32[]{:S(2)}, u32[]{:S(2)}) collective-permute-start(bf16[768,512]{1,0:T(8,128)(2,1)} %refs_3_.1), channel_id=1, source_target_pairs={{0,1},{1,0},{2,3},{3,2},{4,5},{5,4},{6,7},{7,6},{8,9},{9,8},{10,11... | collective-permute-start | bytes 2359304 | tf_op jit(solution)/shard_map/ppermute | solution.py:193
  23.1 5.7 %collective-permute-start.5 = (bf16[4,12288]{1,0:T(4,128)(2,1)S(1)}, bf16[4,12288]{1,0:T(4,128)(2,1)}, u32[]{:S(2)}, u32[]{:S(2)}) collective-permute-start(bf16[4,12288]{1,0:T(4,128)(2,1)S(1)} %collective-permute-done.4.refs_2_), channel_id=1, source_target_pairs={{0,2},{1,3},{2,0},{3,1},{4,6},{5,7},{6,4},{7,5},{8,10},{9,11},{10,... | collective-permute-start | bytes 294920 | tf_op jit(solution)/shard_map/ppermute | solution.py:190
  24.6 5.4 %collective-permute-start.7 = (bf16[4,12288]{1,0:T(4,128)(2,1)S(1)}, bf16[4,12288]{1,0:T(4,128)(2,1)}, u32[]{:S(2)}, u32[]{:S(2)}) collective-permute-start(bf16[4,12288]{1,0:T(4,128)(2,1)S(1)} %collective-permute-done.6.refs_3_), channel_id=1, source_target_pairs={{0,2},{1,3},{2,0},{3,1},{4,6},{5,7},{6,4},{7,5},{8,10},{9,11},{10,... | collective-permute-start | bytes 294920 | tf_op jit(solution)/shard_map/ppermute | solution.py:190
  26.0 17.5 %copy-start.1 = (bf16[12288,128]{1,0:T(8,128)(2,1)S(1)}, bf16[12288,128]{1,0:T(8,128)(2,1)}, u32[]{:S(2)}) copy-start(bf16[12288,128]{1,0:T(8,128)(2,1)} %copy-done) | copy-start | bytes 9437188
  35.0 4.0 %collective-permute-start.10 = (bf16[32,512]{1,0:T(8,128)(2,1)S(1)}, bf16[32,512]{1,0:T(8,128)(2,1)S(1)}, u32[]{:S(2)}, u32[]{:S(2)}) collective-permute-start(bf16[32,512]{1,0:T(8,128)(2,1)S(1)} %get-tuple-element.65), channel_id=1, source_target_pairs={{0,2},{1,3},{2,0},{3,1},{4,6},{5,7},{6,4},{7,5},{8,10},{9,11},{10,... | collective-permute-start | bytes 98312 | tf_op jit(solution)/shard_map/ppermute | solution.py:190
  39.0 10.4 %collective-permute-start.12 = (bf16[512,768]{1,0:T(8,128)(2,1)}, bf16[512,768]{1,0:T(8,128)(2,1)S(1)}, u32[]{:S(2)}, u32[]{:S(2)}) collective-permute-start(bf16[512,768]{1,0:T(8,128)(2,1)} %refs_6_.1), channel_id=1, source_target_pairs={{0,1},{1,0},{2,3},{3,2},{4,5},{5,4},{6,7},{7,6},{8,9},{9,8},{10,11... | collective-permute-start | bytes 2359304 | tf_op jit(solution)/shard_map/ppermute | solution.py:193
  39.0 10.3 %collective-permute-start.13 = (bf16[32,512]{1,0:T(8,128)(2,1)S(1)}, bf16[32,512]{1,0:T(8,128)(2,1)S(1)}, u32[]{:S(2)}, u32[]{:S(2)}) collective-permute-start(bf16[32,512]{1,0:T(8,128)(2,1)S(1)} %get-tuple-element.74), channel_id=1, source_target_pairs={{0,12},{1,13},{2,14},{3,15},{4,8},{5,9},{6,10},{7,11},{8,4},{9,5},... | collective-permute-start | bytes 98312 | tf_op jit(solution)/shard_map/ppermute | solution.py:187
  42.8 6.5 %collective-permute-start.14 = (bf16[32,512]{1,0:T(8,128)(2,1)S(1)}, bf16[32,512]{1,0:T(8,128)(2,1)S(1)}, u32[]{:S(2)}, u32[]{:S(2)}) collective-permute-start(bf16[32,512]{1,0:T(8,128)(2,1)S(1)} %get-tuple-element.75), channel_id=1, source_target_pairs={{0,8},{1,9},{2,10},{3,11},{4,12},{5,13},{6,14},{7,15},{8,0},{9,1},... | collective-permute-start | bytes 98312 | tf_op jit(solution)/shard_map/ppermute | solution.py:187
  42.8 6.5 %collective-permute-start.15 = (bf16[32,512]{1,0:T(8,128)(2,1)S(1)}, bf16[32,512]{1,0:T(8,128)(2,1)S(1)}, u32[]{:S(2)}, u32[]{:S(2)}) collective-permute-start(bf16[32,512]{1,0:T(8,128)(2,1)S(1)} %get-tuple-element.76), channel_id=1, source_target_pairs={{0,4},{1,5},{2,6},{3,7},{4,0},{5,1},{6,2},{7,3},{8,12},{9,13},{10,... | collective-permute-start | bytes 98312 | tf_op jit(solution)/shard_map/ppermute | solution.py:187
  46.2 3.2 %copy-start.5 = (bf16[512,768]{1,0:T(8,128)(2,1)S(1)}, bf16[512,768]{1,0:T(8,128)(2,1)}, u32[]{:S(2)}) copy-start(bf16[512,768]{1,0:T(8,128)(2,1)} %copy-done.4) | copy-start | bytes 2359300
  46.2 3.2 %copy-start.15 = (f32[512]{0:T(512)S(1)}, f32[512]{0:T(512)}, u32[]{:S(2)}) copy-start(f32[512]{0:T(512)} %param.22) | copy-start | bytes 6148
  49.9 5.7 %collective-permute-start.17 = (bf16[4,12288]{1,0:T(4,128)(2,1)S(1)}, bf16[4,12288]{1,0:T(4,128)(2,1)S(1)}, u32[]{:S(2)}, u32[]{:S(2)}) collective-permute-start(bf16[4,12288]{1,0:T(4,128)(2,1)S(1)} %get-tuple-element.82), channel_id=1, source_target_pairs={{0,2},{1,3},{2,0},{3,1},{4,6},{5,7},{6,4},{7,5},{8,10},{9,11},{10,... | collective-permute-start | bytes 294920 | tf_op jit(solution)/shard_map/ppermute | solution.py:190
  51.5 8.0 %collective-permute-start.16 = (bf16[4,12288]{1,0:T(4,128)(2,1)S(1)}, bf16[4,12288]{1,0:T(4,128)(2,1)S(1)}, u32[]{:S(2)}, u32[]{:S(2)}) collective-permute-start(bf16[4,12288]{1,0:T(4,128)(2,1)S(1)} %get-tuple-element.80), channel_id=1, source_target_pairs={{0,2},{1,3},{2,0},{3,1},{4,6},{5,7},{6,4},{7,5},{8,10},{9,11},{10,... | collective-permute-start | bytes 294920 | tf_op jit(solution)/shard_map/ppermute | solution.py:190
  52.0 9.5 %collective-permute-start.19 = (bf16[4,12288]{1,0:T(4,128)(2,1)S(1)}, bf16[4,12288]{1,0:T(4,128)(2,1)S(1)}, u32[]{:S(2)}, u32[]{:S(2)}) collective-permute-start(bf16[4,12288]{1,0:T(4,128)(2,1)S(1)} %get-tuple-element.86), channel_id=1, source_target_pairs={{0,2},{1,3},{2,0},{3,1},{4,6},{5,7},{6,4},{7,5},{8,10},{9,11},{10,... | collective-permute-start | bytes 294920 | tf_op jit(solution)/shard_map/ppermute | solution.py:190
  55.7 10.8 %collective-permute-start.22 = (bf16[4,12288]{1,0:T(4,128)(2,1)S(1)}, bf16[4,12288]{1,0:T(4,128)(2,1)S(1)}, u32[]{:S(2)}, u32[]{:S(2)}) collective-permute-start(bf16[4,12288]{1,0:T(4,128)(2,1)S(1)} %add_convert_fusion.2), channel_id=1, source_target_pairs={{0,12},{1,13},{2,14},{3,15},{4,8},{5,9},{6,10},{7,11},{8,4},{9,5},... | collective-permute-start | bytes 294920 | tf_op jit(solution)/shard_map/ppermute | solution.py:187
  59.6 6.9 %collective-permute-start.21 = (bf16[4,12288]{1,0:T(4,128)(2,1)S(1)}, bf16[4,12288]{1,0:T(4,128)(2,1)S(1)}, u32[]{:S(2)}, u32[]{:S(2)}) collective-permute-start(bf16[4,12288]{1,0:T(4,128)(2,1)S(1)} %add_convert_fusion.1), channel_id=1, source_target_pairs={{0,8},{1,9},{2,10},{3,11},{4,12},{5,13},{6,14},{7,15},{8,0},{9,1},... | collective-permute-start | bytes 294920 | tf_op jit(solution)/shard_map/ppermute | solution.py:187
  60.1 4.6 %collective-permute-start.18 = (bf16[4,12288]{1,0:T(4,128)(2,1)S(1)}, bf16[4,12288]{1,0:T(4,128)(2,1)S(1)}, u32[]{:S(2)}, u32[]{:S(2)}) collective-permute-start(bf16[4,12288]{1,0:T(4,128)(2,1)S(1)} %get-tuple-element.84), channel_id=1, source_target_pairs={{0,2},{1,3},{2,0},{3,1},{4,6},{5,7},{6,4},{7,5},{8,10},{9,11},{10,... | collective-permute-start | bytes 294920 | tf_op jit(solution)/shard_map/ppermute | solution.py:190
  61.5 5.9 %collective-permute-start.20 = (bf16[4,12288]{1,0:T(4,128)(2,1)S(1)}, bf16[4,12288]{1,0:T(4,128)(2,1)S(1)}, u32[]{:S(2)}, u32[]{:S(2)}) collective-permute-start(bf16[4,12288]{1,0:T(4,128)(2,1)S(1)} %add_convert_fusion), channel_id=1, source_target_pairs={{0,4},{1,5},{2,6},{3,7},{4,0},{5,1},{6,2},{7,3},{8,12},{9,13},{10,... | collective-permute-start | bytes 294920 | tf_op jit(solution)/shard_map/ppermute | solution.py:187
  (13 other events, 13.5 us)

commit v17 on v16

--- a/solution.py
+++ b/solution.py
@@ -201,6 +201,7 @@
     held = [hidden] + [across(hidden, k) for k in range(1, groups)]
     w_in_mate = core(w_in)
     near = (hidden, gain, shift, low_in, w_in, w_out, low_out)
+    place, *near = lax.optimization_barrier((place, *near))
     near = call(
         functools.partial(load_body, len(near)),
         [shape(*x.shape, dtype=x.dtype) for x in near],

time: 68.4 us -> 55.6 us (0.81)
  local copies, waits for them, and re-layouts: 11.5 us -> 0.05 us
  Pallas kernels: 12.4 us -> 9.36 us
  waiting for transfers between devices: 16.1 us -> 18.6 us
  starting transfers between devices: 27.7 us -> 27 us
    unnamed x44 -> x18, local copies, waits for them, and re-layouts: 11.5 us -> 0.05 us
    ppermute x9, waiting for transfers between devices: 2.67 us -> 6.03 us  [across(): return lax.ppermute(x, 'blk', [(i, i ^ 4 * k) for i in range(devices)])]
    pallas_call x1, Pallas kernels: 3.15 us -> 1.19 us  [shards(): call(functools.partial(part_body, step), [shape(rows, width, dtype=f32)],...]
    pallas_call x1, Pallas kernels: 2.08 us -> 0.88 us  [shards(): call(functools.partial(far_body, groups), [shape(some, width), shape(rows...]
    ppermute x9, waiting for transfers between devices: 13.4 us -> 12.6 us  [beside(): return lax.ppermute(x, 'blk', [(i, i ^ 2) for i in range(devices)])]
  transfers between devices with their start and end apart: 23 -> 23, of which waited for: 9 -> 11; matrix products, arithmetic and copies ran while one was open for 0% -> 0% of each run, Pallas kernels for 17% -> 15%
where the time goes in v17:
time: 55.6 us; the launch traced here: 55.5 us
  starting transfers between devices  27 us (49%)
  waiting for transfers between devices  18.6 us (33%)
  Pallas kernels  9.36 us (17%)
    ppermute x9, starting transfers between devices, across(): return lax.ppermute(x, 'blk', [(i, i ^ 4 * k) for i in range(devices)])  15.3 us
    ppermute x9, waiting for transfers between devices, beside(): return lax.ppermute(x, 'blk', [(i, i ^ 2) for i in range(devices)])  12.6 us
    ppermute x9, starting transfers between devices, beside(): return lax.ppermute(x, 'blk', [(i, i ^ 2) for i in range(devices)])  10.8 us
    ppermute x9, waiting for transfers between devices, across(): return lax.ppermute(x, 'blk', [(i, i ^ 4 * k) for i in range(devices)])  6.03 us
    pallas_call x1, Pallas kernels, shards(): call(functools.partial(load_body, len(near)), [shape(*x.shape, dtype=x.dt...  3.52 us
    pallas_call x1, Pallas kernels, shards(): call(functools.partial(act_body, groups, step), [shape(rows, 2 * block)],...  2.02 us
    pallas_call x1, Pallas kernels, shards(): call(functools.partial(part_body, step), [shape(rows, width, dtype=f32)],...  1.19 us
  transfers between devices with their start and end apart: 23, of which 11 were waited for; matrix products, arithmetic and copies ran while one was open for 0% of the time, Pallas kernels for 15%

profile of v17, /device:TPU:0, one launch (start us, length us, event | category | flops | bytes accessed | tf_op | source)
XLA Modules:
  0.0 55.5 jit_solution(17558399223681943720)
XLA Ops:
  0.5 2.6 %collective-permute-start.2 = (bf16[4,12288]{1,0:T(4,128)(2,1)}, bf16[4,12288]{1,0:T(4,128)(2,1)S(1)}, u32[]{:S(2)}, u32[]{:S(2)}) collective-permute-start(bf16[4,12288]{1,0:T(4,128)(2,1)} %refs_0_), channel_id=1, source_target_pairs={{0,4},{1,5},{2,6},{3,7},{4,0},{5,1},{6,2},{7,3},{8,12},{9,13},{10,... | collective-permute-start | bytes 294920 | tf_op jit(solution)/shard_map/ppermute | solution.py:187
  3.0 2.6 %collective-permute-start.4 = (bf16[4,12288]{1,0:T(4,128)(2,1)}, bf16[4,12288]{1,0:T(4,128)(2,1)S(1)}, u32[]{:S(2)}, u32[]{:S(2)}) collective-permute-start(bf16[4,12288]{1,0:T(4,128)(2,1)} %refs_0_), channel_id=1, source_target_pairs={{0,8},{1,9},{2,10},{3,11},{4,12},{5,13},{6,14},{7,15},{8,0},{9,1},... | collective-permute-start | bytes 294920 | tf_op jit(solution)/shard_map/ppermute | solution.py:187
  5.6 3.5 %shard_map.118 = (bf16[4,12288]{1,0:T(4,128)(2,1)S(1)}, f32[1,12288]{1,0:T(1,128)S(1)}, f32[1,12288]{1,0:T(1,128)S(1)}, bf16[768,512]{1,0:T(8,128)(2,1)S(1)}, bf...) custom-call(bf16[4,12288]{1,0:T(4,128)(2,1)} %refs_0_, ...), custom_call_target="tpu_custom_call" | custom-call | bytes 8388608 | tf_op jit(solution)/shard_map/pallas_call | solution.py:205
  9.3 1.8 %collective-permute-start.1 = (bf16[4,12288]{1,0:T(4,128)(2,1)S(1)}, bf16[4,12288]{1,0:T(4,128)(2,1)S(1)}, u32[]{:S(2)}, u32[]{:S(2)}) collective-permute-start(bf16[4,12288]{1,0:T(4,128)(2,1)S(1)} %copy-done.8), channel_id=1, source_target_pairs={{0,2},{1,3},{2,0},{3,1},{4,6},{5,7},{6,4},{7,5},{8,10},{9,11},{10,... | collective-permute-start | bytes 294920 | tf_op jit(solution)/shard_map/ppermute | solution.py:190
  11.4 2.6 %collective-permute-done.4.refs_2_ = bf16[4,12288]{1,0:T(4,128)(2,1)S(1)} collective-permute-done((bf16[4,12288]{1,0:T(4,128)(2,1)}, bf16[4,12288]{1,0:T(4,128)(2,1)S(1)}, u32[]{:S(2)}, u32[]{:S(2)}) %collective-permute-start.4) | collective-permute-done | bytes 98336 | tf_op jit(solution)/shard_map/ppermute | solution.py:187
  14.0 0.9 %collective-permute-done.1.refs_0_ = bf16[4,12288]{1,0:T(4,128)(2,1)S(1)} collective-permute-done((bf16[4,12288]{1,0:T(4,128)(2,1)S(1)}, bf16[4,12288]{1,0:T(4,128)(2,1)S(1)}, u32[]{:S(2)}, u32[]{:S(2)}) %collective-permute-start.1) | collective-permute-done | bytes 98336 | tf_op jit(solution)/shard_map/ppermute | solution.py:190
  14.9 1.7 %collective-permute-done.3.refs_1_ = bf16[4,12288]{1,0:T(4,128)(2,1)S(1)} collective-permute-done((bf16[4,12288]{1,0:T(4,128)(2,1)S(1)}, bf16[4,12288]{1,0:T(4,128)(2,1)S(1)}, u32[]{:S(2)}, u32[]{:S(2)}) %collective-permute-start.3) | collective-permute-done | bytes 98336 | tf_op jit(solution)/shard_map/ppermute | solution.py:190
  16.6 0.5 collective-permute-start.9
  17.1 1.7 %collective-permute-start.5 = (bf16[4,12288]{1,0:T(4,128)(2,1)S(1)}, bf16[4,12288]{1,0:T(4,128)(2,1)S(1)}, u32[]{:S(2)}, u32[]{:S(2)}) collective-permute-start(bf16[4,12288]{1,0:T(4,128)(2,1)S(1)} %collective-permute-done.4.refs_2_), channel_id=1, source_target_pairs={{0,2},{1,3},{2,0},{3,1},{4,6},{5,7},{6,4},{7,5},{8,10},{9,11},{10,... | collective-permute-start | bytes 294920 | tf_op jit(solution)/shard_map/ppermute | solution.py:190
  19.2 0.6 %shard_map.119.refs_4_.near = bf16[16,12288]{1,0:T(8,128)(2,1)S(1)} custom-call(bf16[4,12288]{1,0:T(4,128)(2,1)S(1)} %get-tuple-element.72.refs_0_, bf16[4,12288]{1,0:T(4,128)(2,1)S(1)} %collective-permute-done.2.refs_1_, bf16[4,12288]{1,0:T(4,128)(2,1)S(1)} %collective-permute-done.4.refs_2_, bf16[4,12288]{1,0:T(4,128)(2,1)S(1)} %collective-permute-done.6.refs_3_, ...), custom_call_target="tpu_custom_call" | custom-call | bytes 4194304 | tf_op jit(solution)/shard_map/pallas_call | solution.py:221
  19.8 2.9 %collective-permute-done.5.refs_2_ = bf16[4,12288]{1,0:T(4,128)(2,1)S(1)} collective-permute-done((bf16[4,12288]{1,0:T(4,128)(2,1)S(1)}, bf16[4,12288]{1,0:T(4,128)(2,1)S(1)}, u32[]{:S(2)}, u32[]{:S(2)}) %collective-permute-start.5) | collective-permute-done | bytes 98336 | tf_op jit(solution)/shard_map/ppermute | solution.py:190
  22.6 1.4 %collective-permute-done.7.refs_3_ = bf16[4,12288]{1,0:T(4,128)(2,1)S(1)} collective-permute-done((bf16[4,12288]{1,0:T(4,128)(2,1)S(1)}, bf16[4,12288]{1,0:T(4,128)(2,1)S(1)}, u32[]{:S(2)}, u32[]{:S(2)}) %collective-permute-start.7) | collective-permute-done | bytes 98336 | tf_op jit(solution)/shard_map/ppermute | solution.py:190
  24.0 0.9 %shard_map.120 = (bf16[16,12288]{1,0:T(8,128)(2,1)S(1)}, f32[32,512]{1,0:T(8,128)S(1)}, bf16[32,512]{1,0:T(8,128)(2,1)S(1)}) custom-call(s32[1]{0:T(128)} %bitcast.place, bf16[4,12288]{1,0:T(4,128)(2,1)S(1)} %collective-permute-done.1.refs_0_, bf16[4,12288]{1,0:T(4,128)(2,1)S(1)} %collective-permute-done.3.refs_1_, ...), custom_call_target="tpu_custom_call" | custom-call | bytes 4194304 | tf_op jit(solution)/shard_map/pallas_call | solution.py:225
  24.9 1.8 %collective-permute-start.10 = (bf16[32,512]{1,0:T(8,128)(2,1)S(1)}, bf16[32,512]{1,0:T(8,128)(2,1)S(1)}, u32[]{:S(2)}, u32[]{:S(2)}) collective-permute-start(bf16[32,512]{1,0:T(8,128)(2,1)S(1)} %get-tuple-element.81), channel_id=1, source_target_pairs={{0,2},{1,3},{2,0},{3,1},{4,6},{5,7},{6,4},{7,5},{8,10},{9,11},{10,... | collective-permute-start | bytes 98312 | tf_op jit(solution)/shard_map/ppermute | solution.py:190
  26.7 2.2 %collective-permute-done.10.got = bf16[32,512]{1,0:T(8,128)(2,1)S(1)} collective-permute-done((bf16[32,512]{1,0:T(8,128)(2,1)S(1)}, bf16[32,512]{1,0:T(8,128)(2,1)S(1)}, u32[]{:S(2)}, u32[]{:S(2)}) %collective-permute-start.10) | collective-permute-done | bytes 32800 | tf_op jit(solution)/shard_map/ppermute | solution.py:190
  28.9 3.9 %collective-permute-start.13 = (bf16[32,512]{1,0:T(8,128)(2,1)S(1)}, bf16[32,512]{1,0:T(8,128)(2,1)S(1)}, u32[]{:S(2)}, u32[]{:S(2)}) collective-permute-start(bf16[32,512]{1,0:T(8,128)(2,1)S(1)} %get-tuple-element.90), channel_id=1, source_target_pairs={{0,12},{1,13},{2,14},{3,15},{4,8},{5,9},{6,10},{7,11},{8,4},{9,5},... | collective-permute-start | bytes 98312 | tf_op jit(solution)/shard_map/ppermute | solution.py:187
  32.8 0.6 %collective-permute-start.15 = (bf16[32,512]{1,0:T(8,128)(2,1)S(1)}, bf16[32,512]{1,0:T(8,128)(2,1)S(1)}, u32[]{:S(2)}, u32[]{:S(2)}) collective-permute-start(bf16[32,512]{1,0:T(8,128)(2,1)S(1)} %get-tuple-element.92), channel_id=1, source_target_pairs={{0,4},{1,5},{2,6},{3,7},{4,0},{5,1},{6,2},{7,3},{8,12},{9,13},{10,... | collective-permute-start | bytes 98312 | tf_op jit(solution)/shard_map/ppermute | solution.py:187
  33.4 2.0 %shard_map.122.act = bf16[32,256]{1,0:T(8,128)(2,1)S(1)} custom-call(s32[1]{0:T(128)} %bitcast.place, s32[4,6]{1,0:T(4,128)S(1)} %copy-done, s32[4]{0:T(128)S(1)} %copy-done.2, s32[16]{0:T(128)S(1)} %copy-done.3, bf16[16,12288]{1,0:T(8,128)(2,1)S(1)} %shard_map.119.refs_4_.near, bf16[16,12288]{1,0:T(8,128)(2,1)S(1)} %get-tuple-element.86.far, ...), custom_call_target="tpu_custom_call" | custom-call | bytes 4194304 | tf_op jit(solution)/shard_map/pallas_call | solution.py:236
  35.5 1.2 %shard_map.123.part = f32[32,12288]{1,0:T(8,128)S(1)} custom-call(bf16[32,256]{1,0:T(8,128)(2,1)S(1)} %shard_map.122.act, bf16[128,12288]{1,0:T(8,128)(2,1)S(1)} %get-tuple-element.77.w_own, bf16[128,12288]{1,0:T(8,128)(2,1)S(1)} %collective-permute-done.11.w_mate), custom_call_target="tpu_custom_call" | custom-call | bytes 6291456 | tf_op jit(solution)/shard_map/pallas_call | solution.py:251
  36.7 0.9 %collective-permute-done.14.refs_1_ = bf16[32,512]{1,0:T(8,128)(2,1)S(1)} collective-permute-done((bf16[32,512]{1,0:T(8,128)(2,1)S(1)}, bf16[32,512]{1,0:T(8,128)(2,1)S(1)}, u32[]{:S(2)}, u32[]{:S(2)}) %collective-permute-start.14) | collective-permute-done | bytes 32800 | tf_op jit(solution)/shard_map/ppermute | solution.py:187
  38.0 1.6 %collective-permute-start.17 = (bf16[4,12288]{1,0:T(4,128)(2,1)S(1)}, bf16[4,12288]{1,0:T(4,128)(2,1)S(1)}, u32[]{:S(2)}, u32[]{:S(2)}) collective-permute-start(bf16[4,12288]{1,0:T(4,128)(2,1)S(1)} %get-tuple-element.98), channel_id=1, source_target_pairs={{0,2},{1,3},{2,0},{3,1},{4,6},{5,7},{6,4},{7,5},{8,10},{9,11},{10,... | collective-permute-start | bytes 294920 | tf_op jit(solution)/shard_map/ppermute | solution.py:190
  39.6 0.5 collective-permute-start.16
  40.1 1.5 %collective-permute-start.19 = (bf16[4,12288]{1,0:T(4,128)(2,1)S(1)}, bf16[4,12288]{1,0:T(4,128)(2,1)S(1)}, u32[]{:S(2)}, u32[]{:S(2)}) collective-permute-start(bf16[4,12288]{1,0:T(4,128)(2,1)S(1)} %get-tuple-element.102), channel_id=1, source_target_pairs={{0,2},{1,3},{2,0},{3,1},{4,6},{5,7},{6,4},{7,5},{8,10},{9,11},{10,... | collective-permute-start | bytes 294920 | tf_op jit(solution)/shard_map/ppermute | solution.py:190
  41.7 2.1 %collective-permute-done.17 = bf16[4,12288]{1,0:T(4,128)(2,1)S(1)} collective-permute-done((bf16[4,12288]{1,0:T(4,128)(2,1)S(1)}, bf16[4,12288]{1,0:T(4,128)(2,1)S(1)}, u32[]{:S(2)}, u32[]{:S(2)}) %collective-permute-start.17) | collective-permute-done | bytes 98336 | tf_op jit(solution)/shard_map/ppermute | solution.py:190
  43.8 3.0 %collective-permute-start.22 = (bf16[4,12288]{1,0:T(4,128)(2,1)S(1)}, bf16[4,12288]{1,0:T(4,128)(2,1)S(1)}, u32[]{:S(2)}, u32[]{:S(2)}) collective-permute-start(bf16[4,12288]{1,0:T(4,128)(2,1)S(1)} %add_convert_fusion.2), channel_id=1, source_target_pairs={{0,12},{1,13},{2,14},{3,15},{4,8},{5,9},{6,10},{7,11},{8,4},{9,5},... | collective-permute-start | bytes 294920 | tf_op jit(solution)/shard_map/ppermute | solution.py:187
  46.8 0.8 %collective-permute-start.21 = (bf16[4,12288]{1,0:T(4,128)(2,1)S(1)}, bf16[4,12288]{1,0:T(4,128)(2,1)S(1)}, u32[]{:S(2)}, u32[]{:S(2)}) collective-permute-start(bf16[4,12288]{1,0:T(4,128)(2,1)S(1)} %add_convert_fusion.1), channel_id=1, source_target_pairs={{0,8},{1,9},{2,10},{3,11},{4,12},{5,13},{6,14},{7,15},{8,0},{9,1},... | collective-permute-start | bytes 294920 | tf_op jit(solution)/shard_map/ppermute | solution.py:187
  47.6 1.3 %collective-permute-start.18 = (bf16[4,12288]{1,0:T(4,128)(2,1)S(1)}, bf16[4,12288]{1,0:T(4,128)(2,1)S(1)}, u32[]{:S(2)}, u32[]{:S(2)}) collective-permute-start(bf16[4,12288]{1,0:T(4,128)(2,1)S(1)} %get-tuple-element.100), channel_id=1, source_target_pairs={{0,2},{1,3},{2,0},{3,1},{4,6},{5,7},{6,4},{7,5},{8,10},{9,11},{10,... | collective-permute-start | bytes 294920 | tf_op jit(solution)/shard_map/ppermute | solution.py:190
  49.0 1.8 %collective-permute-start.20 = (bf16[4,12288]{1,0:T(4,128)(2,1)S(1)}, bf16[4,12288]{1,0:T(4,128)(2,1)S(1)}, u32[]{:S(2)}, u32[]{:S(2)}) collective-permute-start(bf16[4,12288]{1,0:T(4,128)(2,1)S(1)} %add_convert_fusion), channel_id=1, source_target_pairs={{0,4},{1,5},{2,6},{3,7},{4,0},{5,1},{6,2},{7,3},{8,12},{9,13},{10,... | collective-permute-start | bytes 294920 | tf_op jit(solution)/shard_map/ppermute | solution.py:187
  50.8 1.4 %collective-permute-done.18 = bf16[4,12288]{1,0:T(4,128)(2,1)S(1)} collective-permute-done((bf16[4,12288]{1,0:T(4,128)(2,1)S(1)}, bf16[4,12288]{1,0:T(4,128)(2,1)S(1)}, u32[]{:S(2)}, u32[]{:S(2)}) %collective-permute-start.18) | collective-permute-done | bytes 98336 | tf_op jit(solution)/shard_map/ppermute | solution.py:190
  52.3 1.5 %collective-permute-done.21.refs_2_ = bf16[4,12288]{1,0:T(4,128)(2,1)S(1)} collective-permute-done((bf16[4,12288]{1,0:T(4,128)(2,1)S(1)}, bf16[4,12288]{1,0:T(4,128)(2,1)S(1)}, u32[]{:S(2)}, u32[]{:S(2)}) %collective-permute-start.21) | collective-permute-done | bytes 98336 | tf_op jit(solution)/shard_map/ppermute | solution.py:187
  53.8 1.0 %collective-permute-done.20.refs_1_ = bf16[4,12288]{1,0:T(4,128)(2,1)S(1)} collective-permute-done((bf16[4,12288]{1,0:T(4,128)(2,1)S(1)}, bf16[4,12288]{1,0:T(4,128)(2,1)S(1)}, u32[]{:S(2)}, u32[]{:S(2)}) %collective-permute-start.20) | collective-permute-done | bytes 98336 | tf_op jit(solution)/shard_map/ppermute | solution.py:187
  54.8 0.7 %shard_map.125 = bf16[4,12288]{1,0:T(4,128)(2,1)} custom-call(f32[4,12288]{1,0:T(4,128)S(1)} %convert_add_fusion.refs_0_, bf16[4,12288]{1,0:T(4,128)(2,1)S(1)} %collective-permute-done.20.refs_1_, bf16[4,12288]{1,0:T(4,128)(2,1)S(1)} %collective-permute-done.21.refs_2_, bf16[4,12288]{1,0:T(4,128)(2,1)S(1)} %collective-permute-done.22.refs_3_), custom_call_target="tpu_custom_call" | custom-call | bytes 2097152 | tf_op jit(solution)/shard_map/pallas_call | solution.py:280
  (44 shorter events, 1.8 us)
Async XLA Ops:
  0.0 16.6 %collective-permute-start.8 = (bf16[12288,128]{1,0:T(8,128)(2,1)}, bf16[12288,128]{1,0:T(8,128)(2,1)S(1)}, u32[]{:S(2)}, u32[]{:S(2)}) collective-permute-start(bf16[12288,128]{1,0:T(8,128)(2,1)} %refs_4_), channel_id=1, source_target_pairs={{0,1},{1,0},{2,3},{3,2},{4,5},{5,4},{6,7},{7,6},{8,9},{9,8},{10,11... | collective-permute-start | bytes 9437192 | tf_op jit(solution)/shard_map/ppermute | solution.py:193
  0.5 10.6 %collective-permute-start.2 = (bf16[4,12288]{1,0:T(4,128)(2,1)}, bf16[4,12288]{1,0:T(4,128)(2,1)S(1)}, u32[]{:S(2)}, u32[]{:S(2)}) collective-permute-start(bf16[4,12288]{1,0:T(4,128)(2,1)} %refs_0_), channel_id=1, source_target_pairs={{0,4},{1,5},{2,6},{3,7},{4,0},{5,1},{6,2},{7,3},{8,12},{9,13},{10,... | collective-permute-start | bytes 294920 | tf_op jit(solution)/shard_map/ppermute | solution.py:187
  3.0 11.0 %collective-permute-start.4 = (bf16[4,12288]{1,0:T(4,128)(2,1)}, bf16[4,12288]{1,0:T(4,128)(2,1)S(1)}, u32[]{:S(2)}, u32[]{:S(2)}) collective-permute-start(bf16[4,12288]{1,0:T(4,128)(2,1)} %refs_0_), channel_id=1, source_target_pairs={{0,8},{1,9},{2,10},{3,11},{4,12},{5,13},{6,14},{7,15},{8,0},{9,1},... | collective-permute-start | bytes 294920 | tf_op jit(solution)/shard_map/ppermute | solution.py:187
  5.6 8.4 %collective-permute-start.6 = (bf16[4,12288]{1,0:T(4,128)(2,1)}, bf16[4,12288]{1,0:T(4,128)(2,1)S(1)}, u32[]{:S(2)}, u32[]{:S(2)}) collective-permute-start(bf16[4,12288]{1,0:T(4,128)(2,1)} %refs_0_), channel_id=1, source_target_pairs={{0,12},{1,13},{2,14},{3,15},{4,8},{5,9},{6,10},{7,11},{8,4},{9,5},... | collective-permute-start | bytes 294920 | tf_op jit(solution)/shard_map/ppermute | solution.py:187
  5.6 3.6 %collective-permute-start = (f32[1,128]{1,0:T(1,128)}, f32[1,128]{1,0:T(1,128)S(1)}, u32[]{:S(2)}, u32[]{:S(2)}) collective-permute-start(f32[1,128]{1,0:T(1,128)} %bitcast.6), channel_id=1, source_target_pairs={{0,1},{1,0},{2,3},{3,2},{4,5},{5,4},{6,7},{7,6},{8,9},{9,8},{10,11... | collective-permute-start | bytes 1544 | tf_op jit(solution)/shard_map/ppermute | solution.py:193
  5.6 3.6 %copy-start.8 = (bf16[4,12288]{1,0:T(4,128)(2,1)S(1)}, bf16[4,12288]{1,0:T(4,128)(2,1)}, u32[]{:S(2)}) copy-start(bf16[4,12288]{1,0:T(4,128)(2,1)} %refs_0_) | copy-start | bytes 294916
  5.6 11.0 %copy-start.5 = (bf16[128,12288]{1,0:T(8,128)(2,1)S(1)}, bf16[128,12288]{1,0:T(8,128)(2,1)}, u32[]{:S(2)}) copy-start(bf16[128,12288]{1,0:T(8,128)(2,1)} %refs_5_) | copy-start | bytes 9437188
  5.6 11.0 %copy-start.6 = (bf16[768,512]{1,0:T(8,128)(2,1)S(1)}, bf16[768,512]{1,0:T(8,128)(2,1)}, u32[]{:S(2)}) copy-start(bf16[768,512]{1,0:T(8,128)(2,1)} %refs_3_) | copy-start | bytes 2359300
  9.2 19.7 %copy-start.7 = (bf16[512,768]{1,0:T(8,128)(2,1)S(1)}, bf16[512,768]{1,0:T(8,128)(2,1)}, u32[]{:S(2)}) copy-start(bf16[512,768]{1,0:T(8,128)(2,1)} %refs_6_) | copy-start | bytes 2359300
  9.2 24.2 %copy-start = (s32[4,6]{1,0:T(4,128)S(1)}, s32[4,6]{1,0:T(4,128)}, u32[]{:S(2)}) copy-start(s32[4,6]{1,0:T(4,128)} %lists.1) | copy-start | bytes 292
  9.2 24.2 %copy-start.2 = (s32[4]{0:T(128)S(1)}, s32[4]{0:T(128)}, u32[]{:S(2)}) copy-start(s32[4]{0:T(128)} %counts.1) | copy-start | bytes 52
  9.2 24.2 %copy-start.3 = (s32[16]{0:T(128)S(1)}, s32[16]{0:T(128)}, u32[]{:S(2)}) copy-start(s32[16]{0:T(128)} %block_slot.1) | copy-start | bytes 196
  9.2 24.2 %copy-start.4 = (f32[128]{0:T(128)S(1)}, f32[128]{0:T(128)}, u32[]{:S(2)}) copy-start(f32[128]{0:T(128)} %param.19) | copy-start | bytes 1540
  9.3 5.7 %collective-permute-start.1 = (bf16[4,12288]{1,0:T(4,128)(2,1)S(1)}, bf16[4,12288]{1,0:T(4,128)(2,1)S(1)}, u32[]{:S(2)}, u32[]{:S(2)}) collective-permute-start(bf16[4,12288]{1,0:T(4,128)(2,1)S(1)} %copy-done.8), channel_id=1, source_target_pairs={{0,2},{1,3},{2,0},{3,1},{4,6},{5,7},{6,4},{7,5},{8,10},{9,11},{10,... | collective-permute-start | bytes 294920 | tf_op jit(solution)/shard_map/ppermute | solution.py:190
  11.0 5.6 %collective-permute-start.3 = (bf16[4,12288]{1,0:T(4,128)(2,1)S(1)}, bf16[4,12288]{1,0:T(4,128)(2,1)S(1)}, u32[]{:S(2)}, u32[]{:S(2)}) collective-permute-start(bf16[4,12288]{1,0:T(4,128)(2,1)S(1)} %collective-permute-done.2.refs_1_), channel_id=1, source_target_pairs={{0,2},{1,3},{2,0},{3,1},{4,6},{5,7},{6,4},{7,5},{8,10},{9,11},{10,... | collective-permute-start | bytes 294920 | tf_op jit(solution)/shard_map/ppermute | solution.py:190
  16.6 12.2 %collective-permute-start.11 = (bf16[128,12288]{1,0:T(8,128)(2,1)S(1)}, bf16[128,12288]{1,0:T(8,128)(2,1)S(1)}, u32[]{:S(2)}, u32[]{:S(2)}) collective-permute-start(bf16[128,12288]{1,0:T(8,128)(2,1)S(1)} %copy-done.5), channel_id=1, source_target_pairs={{0,1},{1,0},{2,3},{3,2},{4,5},{5,4},{6,7},{7,6},{8,9},{9,8},{10,11... | collective-permute-start | bytes 9437192 | tf_op jit(solution)/shard_map/ppermute | solution.py:193
  16.6 7.4 %collective-permute-start.9 = (bf16[768,512]{1,0:T(8,128)(2,1)S(1)}, bf16[768,512]{1,0:T(8,128)(2,1)S(1)}, u32[]{:S(2)}, u32[]{:S(2)}) collective-permute-start(bf16[768,512]{1,0:T(8,128)(2,1)S(1)} %copy-done.6), channel_id=1, source_target_pairs={{0,1},{1,0},{2,3},{3,2},{4,5},{5,4},{6,7},{7,6},{8,9},{9,8},{10,11... | collective-permute-start | bytes 2359304 | tf_op jit(solution)/shard_map/ppermute | solution.py:193
  17.1 5.5 %collective-permute-start.5 = (bf16[4,12288]{1,0:T(4,128)(2,1)S(1)}, bf16[4,12288]{1,0:T(4,128)(2,1)S(1)}, u32[]{:S(2)}, u32[]{:S(2)}) collective-permute-start(bf16[4,12288]{1,0:T(4,128)(2,1)S(1)} %collective-permute-done.4.refs_2_), channel_id=1, source_target_pairs={{0,2},{1,3},{2,0},{3,1},{4,6},{5,7},{6,4},{7,5},{8,10},{9,11},{10,... | collective-permute-start | bytes 294920 | tf_op jit(solution)/shard_map/ppermute | solution.py:190
  18.9 5.1 %collective-permute-start.7 = (bf16[4,12288]{1,0:T(4,128)(2,1)S(1)}, bf16[4,12288]{1,0:T(4,128)(2,1)S(1)}, u32[]{:S(2)}, u32[]{:S(2)}) collective-permute-start(bf16[4,12288]{1,0:T(4,128)(2,1)S(1)} %collective-permute-done.6.refs_3_), channel_id=1, source_target_pairs={{0,2},{1,3},{2,0},{3,1},{4,6},{5,7},{6,4},{7,5},{8,10},{9,11},{10,... | collective-permute-start | bytes 294920 | tf_op jit(solution)/shard_map/ppermute | solution.py:190
  24.9 3.9 %collective-permute-start.10 = (bf16[32,512]{1,0:T(8,128)(2,1)S(1)}, bf16[32,512]{1,0:T(8,128)(2,1)S(1)}, u32[]{:S(2)}, u32[]{:S(2)}) collective-permute-start(bf16[32,512]{1,0:T(8,128)(2,1)S(1)} %get-tuple-element.81), channel_id=1, source_target_pairs={{0,2},{1,3},{2,0},{3,1},{4,6},{5,7},{6,4},{7,5},{8,10},{9,11},{10,... | collective-permute-start | bytes 98312 | tf_op jit(solution)/shard_map/ppermute | solution.py:190
  28.8 8.7 %collective-permute-start.12 = (bf16[512,768]{1,0:T(8,128)(2,1)S(1)}, bf16[512,768]{1,0:T(8,128)(2,1)S(1)}, u32[]{:S(2)}, u32[]{:S(2)}) collective-permute-start(bf16[512,768]{1,0:T(8,128)(2,1)S(1)} %copy-done.7), channel_id=1, source_target_pairs={{0,1},{1,0},{2,3},{3,2},{4,5},{5,4},{6,7},{7,6},{8,9},{9,8},{10,11... | collective-permute-start | bytes 2359304 | tf_op jit(solution)/shard_map/ppermute | solution.py:193
  28.9 7.8 %collective-permute-start.13 = (bf16[32,512]{1,0:T(8,128)(2,1)S(1)}, bf16[32,512]{1,0:T(8,128)(2,1)S(1)}, u32[]{:S(2)}, u32[]{:S(2)}) collective-permute-start(bf16[32,512]{1,0:T(8,128)(2,1)S(1)} %get-tuple-element.90), channel_id=1, source_target_pairs={{0,12},{1,13},{2,14},{3,15},{4,8},{5,9},{6,10},{7,11},{8,4},{9,5},... | collective-permute-start | bytes 98312 | tf_op jit(solution)/shard_map/ppermute | solution.py:187
  32.8 4.8 %collective-permute-start.14 = (bf16[32,512]{1,0:T(8,128)(2,1)S(1)}, bf16[32,512]{1,0:T(8,128)(2,1)S(1)}, u32[]{:S(2)}, u32[]{:S(2)}) collective-permute-start(bf16[32,512]{1,0:T(8,128)(2,1)S(1)} %get-tuple-element.91), channel_id=1, source_target_pairs={{0,8},{1,9},{2,10},{3,11},{4,12},{5,13},{6,14},{7,15},{8,0},{9,1},... | collective-permute-start | bytes 98312 | tf_op jit(solution)/shard_map/ppermute | solution.py:187
  32.8 4.8 %collective-permute-start.15 = (bf16[32,512]{1,0:T(8,128)(2,1)S(1)}, bf16[32,512]{1,0:T(8,128)(2,1)S(1)}, u32[]{:S(2)}, u32[]{:S(2)}) collective-permute-start(bf16[32,512]{1,0:T(8,128)(2,1)S(1)} %get-tuple-element.92), channel_id=1, source_target_pairs={{0,4},{1,5},{2,6},{3,7},{4,0},{5,1},{6,2},{7,3},{8,12},{9,13},{10,... | collective-permute-start | bytes 98312 | tf_op jit(solution)/shard_map/ppermute | solution.py:187
  35.5 2.1 %copy-start.1 = (f32[512]{0:T(512)S(1)}, f32[512]{0:T(512)}, u32[]{:S(2)}) copy-start(f32[512]{0:T(512)} %param.22) | copy-start | bytes 6148
  38.0 5.7 %collective-permute-start.17 = (bf16[4,12288]{1,0:T(4,128)(2,1)S(1)}, bf16[4,12288]{1,0:T(4,128)(2,1)S(1)}, u32[]{:S(2)}, u32[]{:S(2)}) collective-permute-start(bf16[4,12288]{1,0:T(4,128)(2,1)S(1)} %get-tuple-element.98), channel_id=1, source_target_pairs={{0,2},{1,3},{2,0},{3,1},{4,6},{5,7},{6,4},{7,5},{8,10},{9,11},{10,... | collective-permute-start | bytes 294920 | tf_op jit(solution)/shard_map/ppermute | solution.py:190
  39.6 7.1 %collective-permute-start.16 = (bf16[4,12288]{1,0:T(4,128)(2,1)S(1)}, bf16[4,12288]{1,0:T(4,128)(2,1)S(1)}, u32[]{:S(2)}, u32[]{:S(2)}) collective-permute-start(bf16[4,12288]{1,0:T(4,128)(2,1)S(1)} %get-tuple-element.96), channel_id=1, source_target_pairs={{0,2},{1,3},{2,0},{3,1},{4,6},{5,7},{6,4},{7,5},{8,10},{9,11},{10,... | collective-permute-start | bytes 294920 | tf_op jit(solution)/shard_map/ppermute | solution.py:190
  40.1 8.8 %collective-permute-start.19 = (bf16[4,12288]{1,0:T(4,128)(2,1)S(1)}, bf16[4,12288]{1,0:T(4,128)(2,1)S(1)}, u32[]{:S(2)}, u32[]{:S(2)}) collective-permute-start(bf16[4,12288]{1,0:T(4,128)(2,1)S(1)} %get-tuple-element.102), channel_id=1, source_target_pairs={{0,2},{1,3},{2,0},{3,1},{4,6},{5,7},{6,4},{7,5},{8,10},{9,11},{10,... | collective-permute-start | bytes 294920 | tf_op jit(solution)/shard_map/ppermute | solution.py:190
  43.8 10.0 %collective-permute-start.22 = (bf16[4,12288]{1,0:T(4,128)(2,1)S(1)}, bf16[4,12288]{1,0:T(4,128)(2,1)S(1)}, u32[]{:S(2)}, u32[]{:S(2)}) collective-permute-start(bf16[4,12288]{1,0:T(4,128)(2,1)S(1)} %add_convert_fusion.2), channel_id=1, source_target_pairs={{0,12},{1,13},{2,14},{3,15},{4,8},{5,9},{6,10},{7,11},{8,4},{9,5},... | collective-permute-start | bytes 294920 | tf_op jit(solution)/shard_map/ppermute | solution.py:187
  46.8 7.0 %collective-permute-start.21 = (bf16[4,12288]{1,0:T(4,128)(2,1)S(1)}, bf16[4,12288]{1,0:T(4,128)(2,1)S(1)}, u32[]{:S(2)}, u32[]{:S(2)}) collective-permute-start(bf16[4,12288]{1,0:T(4,128)(2,1)S(1)} %add_convert_fusion.1), channel_id=1, source_target_pairs={{0,8},{1,9},{2,10},{3,11},{4,12},{5,13},{6,14},{7,15},{8,0},{9,1},... | collective-permute-start | bytes 294920 | tf_op jit(solution)/shard_map/ppermute | solution.py:187
  47.6 4.6 %collective-permute-start.18 = (bf16[4,12288]{1,0:T(4,128)(2,1)S(1)}, bf16[4,12288]{1,0:T(4,128)(2,1)S(1)}, u32[]{:S(2)}, u32[]{:S(2)}) collective-permute-start(bf16[4,12288]{1,0:T(4,128)(2,1)S(1)} %get-tuple-element.100), channel_id=1, source_target_pairs={{0,2},{1,3},{2,0},{3,1},{4,6},{5,7},{6,4},{7,5},{8,10},{9,11},{10,... | collective-permute-start | bytes 294920 | tf_op jit(solution)/shard_map/ppermute | solution.py:190
  49.0 5.7 %collective-permute-start.20 = (bf16[4,12288]{1,0:T(4,128)(2,1)S(1)}, bf16[4,12288]{1,0:T(4,128)(2,1)S(1)}, u32[]{:S(2)}, u32[]{:S(2)}) collective-permute-start(bf16[4,12288]{1,0:T(4,128)(2,1)S(1)} %add_convert_fusion), channel_id=1, source_target_pairs={{0,4},{1,5},{2,6},{3,7},{4,0},{5,1},{6,2},{7,3},{8,12},{9,13},{10,... | collective-permute-start | bytes 294920 | tf_op jit(solution)/shard_map/ppermute | solution.py:187

commit v18 on v7

--- a/solution.py
+++ b/solution.py
@@ -206,7 +206,8 @@
     w_in_mate = core(w_in)
     held[1], low_in_sent, mask = lax.optimization_barrier((held[1], low_in, mask))
     low_in_mate = core(low_in_sent)
-    beyond = [beside(h) for h in held]
+    early, bias_mate = lax.optimization_barrier((hidden, core(bias)))
+    beyond = [beside(h) for h in [early] + held[1:]]
     near = (hidden, gain, shift, low_in, w_in, w_out, low_out)
     *near, mask, beyond[0] = lax.optimization_barrier((*near, mask, beyond[0]))
     near = call(
@@ -218,10 +219,10 @@
         8 * MIB,
     )(*[pltpu.with_memory_space_constraint(x, pltpu.HBM) for x in near])
     hidden_near, gain, shift, low_in, w_in, w_out_near, low_out_near = near
-    *_, w_in_mate, w_out_sent, low_out_sent, bias_sent = lax.optimization_barrier(
-        (*held, *beyond[: groups // 2], w_in_mate, w_out, low_out, bias)
+    *_, w_in_mate, w_out_sent, low_out_sent = lax.optimization_barrier(
+        (*held, *beyond[: groups // 2], w_in_mate, w_out, low_out)
     )
-    bias_mate, w_out_mate, low_out_mate = core(bias_sent), core(w_out_sent), core(low_out_sent)
+    w_out_mate, low_out_mate = core(w_out_sent), core(low_out_sent)
     held[0] = hidden_near
 
     soon = groups // 2
@@ -257,7 +258,7 @@
         [VMEM] * 2,
         16,
     )(total, got)
-    got = [across(messages[k - 1], k) for k in range(1, groups)]
+    got = [across(messages[k - 1], k) for k in range(groups - 1, 0, -1)]
     part = call(
         functools.partial(part_body, step),
         [shape(rows, width, dtype=f32)],

time: 52.6 us -> 52.6 us (level)
  waiting for transfers between devices: 17.2 us -> 15.3 us
  starting transfers between devices: 23.5 us -> 25.3 us
    ppermute x9, waiting for transfers between devices: 11.1 us -> 5.59 us  [across(): return lax.ppermute(x, 'blk', [(i, i ^ 4 * k) for i in range(devices)])]
    ppermute x9, waiting for transfers between devices: 6.09 us -> 9.67 us  [beside(): return lax.ppermute(x, 'blk', [(i, i ^ 2) for i in range(devices)])]
    ppermute x9, starting transfers between devices: 8.72 us -> 10.1 us  [beside(): return lax.ppermute(x, 'blk', [(i, i ^ 2) for i in range(devices)])]
    ppermute x9, starting transfers between devices: 13.6 us -> 14.3 us  [across(): return lax.ppermute(x, 'blk', [(i, i ^ 4 * k) for i in range(devices)])]
  transfers between devices with their start and end apart: 23 -> 23, of which waited for: 9 -> 8; matrix products, arithmetic and copies ran while one was open for 6% -> 6% of each run, Pallas kernels for 14% -> 14%
where the time goes in v18:
time: 52.6 us; the launch traced here: 52.4 us
  starting transfers between devices  25.3 us (48%)
  waiting for transfers between devices  15.3 us (29%)
  Pallas kernels  8.58 us (16%)
  other arithmetic  2.23 us (4%)
  local copies, waits for them, and re-layouts  0.86 us (2%)
    ppermute x9, starting transfers between devices, across(): return lax.ppermute(x, 'blk', [(i, i ^ 4 * k) for i in range(devices)])  14.3 us
    ppermute x9, starting transfers between devices, beside(): return lax.ppermute(x, 'blk', [(i, i ^ 2) for i in range(devices)])  10.1 us
    ppermute x9, waiting for transfers between devices, beside(): return lax.ppermute(x, 'blk', [(i, i ^ 2) for i in range(devices)])  9.67 us
    ppermute x9, waiting for transfers between devices, across(): return lax.ppermute(x, 'blk', [(i, i ^ 4 * k) for i in range(devices)])  5.59 us
    pallas_call x1, Pallas kernels, shards(): call(functools.partial(load_body, len(near)), [shape(*x.shape, dtype=x.dt...  3.39 us
    pallas_call x1, Pallas kernels, shards(): call(functools.partial(act_body, step), [shape(rows, 2 * block)], [VMEM]...  1.21 us
    pallas_call x1, Pallas kernels, shards(): call(functools.partial(part_body, step), [shape(rows, width, dtype=f32)],...  1.19 us
  transfers between devices with their start and end apart: 23, of which 8 were waited for; matrix products, arithmetic and copies ran while one was open for 6% of the time, Pallas kernels for 14%

profile of v18, /device:TPU:0, one launch (start us, length us, event | category | flops | bytes accessed | tf_op | source)
XLA Modules:
  0.0 52.4 jit_solution(6923960923065274841)
XLA Ops:
  0.0 0.5 collective-permute-start.10
  0.5 2.6 %collective-permute-start.4 = (bf16[4,12288]{1,0:T(4,128)(2,1)}, bf16[4,12288]{1,0:T(4,128)(2,1)S(1)}, u32[]{:S(2)}, u32[]{:S(2)}) collective-permute-start(bf16[4,12288]{1,0:T(4,128)(2,1)} %refs_0_), channel_id=1, source_target_pairs={{0,4},{1,5},{2,6},{3,7},{4,0},{5,1},{6,2},{7,3},{8,12},{9,13},{10,... | collective-permute-start | bytes 294920 | tf_op jit(solution)/shard_map/ppermute | solution.py:183
  3.0 2.6 %collective-permute-start = (bf16[4,12288]{1,0:T(4,128)(2,1)}, bf16[4,12288]{1,0:T(4,128)(2,1)S(1)}, u32[]{:S(2)}, u32[]{:S(2)}) collective-permute-start(bf16[4,12288]{1,0:T(4,128)(2,1)} %refs_0_), channel_id=1, source_target_pairs={{0,8},{1,9},{2,10},{3,11},{4,12},{5,13},{6,14},{7,15},{8,0},{9,1},... | collective-permute-start | bytes 294920 | tf_op jit(solution)/shard_map/ppermute | solution.py:183
  5.6 0.8 %copy.13 = s32[4,6]{0,1:T(8,128)S(1)} copy(s32[4,6]{1,0:T(4,128)} %param.15) | data formatting | bytes 192 | tf_op args[3]
  6.4 0.7 %fusion.1 = s32[4,6]{0,1:T(8,128)S(1)} fusion(s32[4]{0:T(128)} %param.16), kind=kLoop, calls=%fused_computation.12 | loop fusion | flops 48 | bytes 112 | tf_op jit(solution)/shard_map/convert_element_type | solution.py:150
  7.3 0.7 %fusion = s32[16,16]{1,0:T(8,128)S(1)} fusion(s32[16]{0:T(128)} %param.17), kind=kLoop, calls=%fused_computation.10 | loop fusion | flops 512 | bytes 1088 | tf_op jit(solution)/shard_map/convert_element_type | solution.py:153
  8.1 1.8 %collective-permute-start.6 = (bf16[4,12288]{1,0:T(4,128)(2,1)}, bf16[4,12288]{1,0:T(4,128)(2,1)S(1)}, u32[]{:S(2)}, u32[]{:S(2)}) collective-permute-start(bf16[4,12288]{1,0:T(4,128)(2,1)} %refs_0_), channel_id=1, source_target_pairs={{0,2},{1,3},{2,0},{3,1},{4,6},{5,7},{6,4},{7,5},{8,10},{9,11},{10,... | collective-permute-start | bytes 294920 | tf_op jit(solution)/shard_map/ppermute | solution.py:186
  10.7 3.3 %collective-permute-done.6.refs_4_ = bf16[4,12288]{1,0:T(4,128)(2,1)S(1)} collective-permute-done((bf16[4,12288]{1,0:T(4,128)(2,1)}, bf16[4,12288]{1,0:T(4,128)(2,1)S(1)}, u32[]{:S(2)}, u32[]{:S(2)}) %collective-permute-start.6) | collective-permute-done | bytes 98336 | tf_op jit(solution)/shard_map/ppermute | solution.py:186
  14.0 1.7 %collective-permute-done.7.refs_5_ = bf16[4,12288]{1,0:T(4,128)(2,1)S(1)} collective-permute-done((bf16[4,12288]{1,0:T(4,128)(2,1)S(1)}, bf16[4,12288]{1,0:T(4,128)(2,1)S(1)}, u32[]{:S(2)}, u32[]{:S(2)}) %collective-permute-start.7) | collective-permute-done | bytes 98336 | tf_op jit(solution)/shard_map/ppermute | solution.py:186
  15.7 0.5 collective-permute-start.8
  16.2 1.7 %collective-permute-start.1 = (bf16[4,12288]{1,0:T(4,128)(2,1)S(1)}, bf16[4,12288]{1,0:T(4,128)(2,1)S(1)}, u32[]{:S(2)}, u32[]{:S(2)}) collective-permute-start(bf16[4,12288]{1,0:T(4,128)(2,1)S(1)} %collective-permute-done.refs_2_), channel_id=1, source_target_pairs={{0,2},{1,3},{2,0},{3,1},{4,6},{5,7},{6,4},{7,5},{8,10},{9,11},{10,... | collective-permute-start | bytes 294920 | tf_op jit(solution)/shard_map/ppermute | solution.py:186
  18.3 3.4 %shard_map.118 = (bf16[4,12288]{1,0:T(4,128)(2,1)S(1)}, f32[1,12288]{1,0:T(1,128)S(1)}, f32[1,12288]{1,0:T(1,128)S(1)}, bf16[768,512]{1,0:T(8,128)(2,1)S(1)}, bf...) custom-call(bf16[4,12288]{1,0:T(4,128)(2,1)} %refs_0_, ...), custom_call_target="tpu_custom_call" | custom-call | bytes 8388608 | tf_op jit(solution)/shard_map/pallas_call | solution.py:213
  21.7 0.8 %shard_map.119 = (bf16[16,12288]{1,0:T(8,128)(2,1)S(1)}, bf16[8,12288]{1,0:T(8,128)(2,1)S(1)}) custom-call(bf16[4,12288]{1,0:T(4,128)(2,1)S(1)} %get-tuple-element.55.refs_0_, bf16[4,12288]{1,0:T(4,128)(2,1)S(1)} %collective-permute-done.4.refs_1_, bf16[4,12288]{1,0:T(4,128)(2,1)S(1)} %collective-permute-done.refs_2_, ...), custom_call_target="tpu_custom_call" | custom-call | bytes 4194304 | tf_op jit(solution)/shard_map/pallas_call | solution.py:229
  22.5 1.0 %collective-permute-done.3.refs_1_ = bf16[4,12288]{1,0:T(4,128)(2,1)S(1)} collective-permute-done((bf16[4,12288]{1,0:T(4,128)(2,1)S(1)}, bf16[4,12288]{1,0:T(4,128)(2,1)S(1)}, u32[]{:S(2)}, u32[]{:S(2)}) %collective-permute-start.3) | collective-permute-done | bytes 98336 | tf_op jit(solution)/shard_map/ppermute | solution.py:186
  23.5 0.8 %shard_map.120 = (bf16[16,12288]{1,0:T(8,128)(2,1)S(1)}, f32[32,512]{1,0:T(8,128)S(1)}, bf16[32,512]{1,0:T(8,128)(2,1)S(1)}) custom-call(s32[1]{0:T(128)} %bitcast.place, bf16[4,12288]{1,0:T(4,128)(2,1)S(1)} %collective-permute-done.1.refs_0_, bf16[4,12288]{1,0:T(4,128)(2,1)S(1)} %collective-permute-done.3.refs_1_, ...), custom_call_target="tpu_custom_call" | custom-call | bytes 4194304 | tf_op jit(solution)/shard_map/pallas_call | solution.py:237
  24.3 1.8 %collective-permute-start.9 = (bf16[32,512]{1,0:T(8,128)(2,1)S(1)}, bf16[32,512]{1,0:T(8,128)(2,1)S(1)}, u32[]{:S(2)}, u32[]{:S(2)}) collective-permute-start(bf16[32,512]{1,0:T(8,128)(2,1)S(1)} %get-tuple-element.65), channel_id=1, source_target_pairs={{0,2},{1,3},{2,0},{3,1},{4,6},{5,7},{6,4},{7,5},{8,10},{9,11},{10,... | collective-permute-start | bytes 98312 | tf_op jit(solution)/shard_map/ppermute | solution.py:186
  26.1 2.2 %collective-permute-done.9.got = bf16[32,512]{1,0:T(8,128)(2,1)S(1)} collective-permute-done((bf16[32,512]{1,0:T(8,128)(2,1)S(1)}, bf16[32,512]{1,0:T(8,128)(2,1)S(1)}, u32[]{:S(2)}, u32[]{:S(2)}) %collective-permute-start.9) | collective-permute-done | bytes 32800 | tf_op jit(solution)/shard_map/ppermute | solution.py:186
  28.3 3.9 %collective-permute-start.13 = (bf16[32,512]{1,0:T(8,128)(2,1)S(1)}, bf16[32,512]{1,0:T(8,128)(2,1)S(1)}, u32[]{:S(2)}, u32[]{:S(2)}) collective-permute-start(bf16[32,512]{1,0:T(8,128)(2,1)S(1)} %get-tuple-element.76), channel_id=1, source_target_pairs={{0,12},{1,13},{2,14},{3,15},{4,8},{5,9},{6,10},{7,11},{8,4},{9,5},... | collective-permute-start | bytes 98312 | tf_op jit(solution)/shard_map/ppermute | solution.py:183
  32.2 0.6 %collective-permute-start.15 = (bf16[32,512]{1,0:T(8,128)(2,1)S(1)}, bf16[32,512]{1,0:T(8,128)(2,1)S(1)}, u32[]{:S(2)}, u32[]{:S(2)}) collective-permute-start(bf16[32,512]{1,0:T(8,128)(2,1)S(1)} %get-tuple-element.78), channel_id=1, source_target_pairs={{0,4},{1,5},{2,6},{3,7},{4,0},{5,1},{6,2},{7,3},{8,12},{9,13},{10,... | collective-permute-start | bytes 98312 | tf_op jit(solution)/shard_map/ppermute | solution.py:183
  32.8 1.2 %shard_map.122.act = bf16[32,256]{1,0:T(8,128)(2,1)S(1)} custom-call(bf16[16,12288]{1,0:T(8,128)(2,1)S(1)} %get-tuple-element.60.refs_2_.near, bf16[16,12288]{1,0:T(8,128)(2,1)S(1)} %get-tuple-element.69.far, bf16[12288,128]{1,0:T(8,128)(2,1)S(1)} %get-tuple-element.70.w_own, bf16[12288,128]{1,0:T(8,128)(2,1)S(1)} %collective-permute-done.10.w_mate, ...), custom_call_target="tpu_custom_call" | custom-call | bytes 4194304 | tf_op jit(solution)/shard_map/pallas_call | solution.py:247
  34.1 1.2 %shard_map.123.part = f32[32,12288]{1,0:T(8,128)S(1)} custom-call(bf16[32,256]{1,0:T(8,128)(2,1)S(1)} %shard_map.122.act, bf16[128,12288]{1,0:T(8,128)(2,1)S(1)} %get-tuple-element.74.w_own, bf16[128,12288]{1,0:T(8,128)(2,1)S(1)} %collective-permute-done.12.w_mate), custom_call_target="tpu_custom_call" | custom-call | bytes 6291456 | tf_op jit(solution)/shard_map/pallas_call | solution.py:262
  35.3 1.7 %collective-permute-done.14.refs_1_ = bf16[32,512]{1,0:T(8,128)(2,1)S(1)} collective-permute-done((bf16[32,512]{1,0:T(8,128)(2,1)S(1)}, bf16[32,512]{1,0:T(8,128)(2,1)S(1)}, u32[]{:S(2)}, u32[]{:S(2)}) %collective-permute-start.14) | collective-permute-done | bytes 32800 | tf_op jit(solution)/shard_map/ppermute | solution.py:183
  37.5 1.6 %collective-permute-start.21 = (bf16[4,12288]{1,0:T(4,128)(2,1)S(1)}, bf16[4,12288]{1,0:T(4,128)(2,1)S(1)}, u32[]{:S(2)}, u32[]{:S(2)}) collective-permute-start(bf16[4,12288]{1,0:T(4,128)(2,1)S(1)} %get-tuple-element.86), channel_id=1, source_target_pairs={{0,2},{1,3},{2,0},{3,1},{4,6},{5,7},{6,4},{7,5},{8,10},{9,11},{10,... | collective-permute-start | bytes 294920 | tf_op jit(solution)/shard_map/ppermute | solution.py:186
  39.0 0.5 collective-permute-start.19
  39.5 1.5 %collective-permute-start.17 = (bf16[4,12288]{1,0:T(4,128)(2,1)S(1)}, bf16[4,12288]{1,0:T(4,128)(2,1)S(1)}, u32[]{:S(2)}, u32[]{:S(2)}) collective-permute-start(bf16[4,12288]{1,0:T(4,128)(2,1)S(1)} %get-tuple-element.82), channel_id=1, source_target_pairs={{0,2},{1,3},{2,0},{3,1},{4,6},{5,7},{6,4},{7,5},{8,10},{9,11},{10,... | collective-permute-start | bytes 294920 | tf_op jit(solution)/shard_map/ppermute | solution.py:186
  41.1 0.5 collective-permute-start.16
  41.6 1.5 %collective-permute-done.21 = bf16[4,12288]{1,0:T(4,128)(2,1)S(1)} collective-permute-done((bf16[4,12288]{1,0:T(4,128)(2,1)S(1)}, bf16[4,12288]{1,0:T(4,128)(2,1)S(1)}, u32[]{:S(2)}, u32[]{:S(2)}) %collective-permute-start.21) | collective-permute-done | bytes 98336 | tf_op jit(solution)/shard_map/ppermute | solution.py:186
  43.1 2.3 %collective-permute-start.22 = (bf16[4,12288]{1,0:T(4,128)(2,1)S(1)}, bf16[4,12288]{1,0:T(4,128)(2,1)S(1)}, u32[]{:S(2)}, u32[]{:S(2)}) collective-permute-start(bf16[4,12288]{1,0:T(4,128)(2,1)S(1)} %add_convert_fusion), channel_id=1, source_target_pairs={{0,12},{1,13},{2,14},{3,15},{4,8},{5,9},{6,10},{7,11},{8,4},{9,5},... | collective-permute-start | bytes 294920 | tf_op jit(solution)/shard_map/ppermute | solution.py:183
  45.9 1.9 %collective-permute-start.18 = (bf16[4,12288]{1,0:T(4,128)(2,1)S(1)}, bf16[4,12288]{1,0:T(4,128)(2,1)S(1)}, u32[]{:S(2)}, u32[]{:S(2)}) collective-permute-start(bf16[4,12288]{1,0:T(4,128)(2,1)S(1)} %add_convert_fusion.2), channel_id=1, source_target_pairs={{0,4},{1,5},{2,6},{3,7},{4,0},{5,1},{6,2},{7,3},{8,12},{9,13},{10,... | collective-permute-start | bytes 294920 | tf_op jit(solution)/shard_map/ppermute | solution.py:183
  47.9 1.7 %collective-permute-done.22.refs_3_ = bf16[4,12288]{1,0:T(4,128)(2,1)S(1)} collective-permute-done((bf16[4,12288]{1,0:T(4,128)(2,1)S(1)}, bf16[4,12288]{1,0:T(4,128)(2,1)S(1)}, u32[]{:S(2)}, u32[]{:S(2)}) %collective-permute-start.22) | collective-permute-done | bytes 98336 | tf_op jit(solution)/shard_map/ppermute | solution.py:183
  49.6 2.1 %collective-permute-done.20.refs_2_ = bf16[4,12288]{1,0:T(4,128)(2,1)S(1)} collective-permute-done((bf16[4,12288]{1,0:T(4,128)(2,1)S(1)}, bf16[4,12288]{1,0:T(4,128)(2,1)S(1)}, u32[]{:S(2)}, u32[]{:S(2)}) %collective-permute-start.20) | collective-permute-done | bytes 98336 | tf_op jit(solution)/shard_map/ppermute | solution.py:183
  51.7 0.7 %shard_map.125 = bf16[4,12288]{1,0:T(4,128)(2,1)} custom-call(f32[4,12288]{1,0:T(4,128)S(1)} %convert_add_fusion.refs_0_, bf16[4,12288]{1,0:T(4,128)(2,1)S(1)} %collective-permute-done.18.refs_1_, bf16[4,12288]{1,0:T(4,128)(2,1)S(1)} %collective-permute-done.20.refs_2_, bf16[4,12288]{1,0:T(4,128)(2,1)S(1)} %collective-permute-done.22.refs_3_), custom_call_target="tpu_custom_call" | custom-call | bytes 2097152 | tf_op jit(solution)/shard_map/pallas_call | solution.py:283
  (43 shorter events, 2.4 us)
Async XLA Ops:
  0.0 15.7 %collective-permute-start.10 = (bf16[12288,128]{1,0:T(8,128)(2,1)}, bf16[12288,128]{1,0:T(8,128)(2,1)S(1)}, u32[]{:S(2)}, u32[]{:S(2)}) collective-permute-start(bf16[12288,128]{1,0:T(8,128)(2,1)} %refs_4_), channel_id=1, source_target_pairs={{0,1},{1,0},{2,3},{3,2},{4,5},{5,4},{6,7},{7,6},{8,9},{9,8},{10,11... | collective-permute-start | bytes 9437192 | tf_op jit(solution)/shard_map/ppermute | solution.py:189
  0.5 9.9 %collective-permute-start.4 = (bf16[4,12288]{1,0:T(4,128)(2,1)}, bf16[4,12288]{1,0:T(4,128)(2,1)S(1)}, u32[]{:S(2)}, u32[]{:S(2)}) collective-permute-start(bf16[4,12288]{1,0:T(4,128)(2,1)} %refs_0_), channel_id=1, source_target_pairs={{0,4},{1,5},{2,6},{3,7},{4,0},{5,1},{6,2},{7,3},{8,12},{9,13},{10,... | collective-permute-start | bytes 294920 | tf_op jit(solution)/shard_map/ppermute | solution.py:183
  3.0 11.0 %collective-permute-start = (bf16[4,12288]{1,0:T(4,128)(2,1)}, bf16[4,12288]{1,0:T(4,128)(2,1)S(1)}, u32[]{:S(2)}, u32[]{:S(2)}) collective-permute-start(bf16[4,12288]{1,0:T(4,128)(2,1)} %refs_0_), channel_id=1, source_target_pairs={{0,8},{1,9},{2,10},{3,11},{4,12},{5,13},{6,14},{7,15},{8,0},{9,1},... | collective-permute-start | bytes 294920 | tf_op jit(solution)/shard_map/ppermute | solution.py:183
  5.6 8.4 %collective-permute-start.2 = (bf16[4,12288]{1,0:T(4,128)(2,1)}, bf16[4,12288]{1,0:T(4,128)(2,1)S(1)}, u32[]{:S(2)}, u32[]{:S(2)}) collective-permute-start(bf16[4,12288]{1,0:T(4,128)(2,1)} %refs_0_), channel_id=1, source_target_pairs={{0,12},{1,13},{2,14},{3,15},{4,8},{5,9},{6,10},{7,11},{8,4},{9,5},... | collective-permute-start | bytes 294920 | tf_op jit(solution)/shard_map/ppermute | solution.py:183
  5.6 2.5 %collective-permute-start.5 = (f32[1,128]{1,0:T(1,128)}, f32[1,128]{1,0:T(1,128)S(1)}, u32[]{:S(2)}, u32[]{:S(2)}) collective-permute-start(f32[1,128]{1,0:T(1,128)} %bitcast.12), channel_id=1, source_target_pairs={{0,1},{1,0},{2,3},{3,2},{4,5},{5,4},{6,7},{7,6},{8,9},{9,8},{10,11... | collective-permute-start | bytes 1544 | tf_op jit(solution)/shard_map/ppermute | solution.py:189
  8.1 5.8 %collective-permute-start.6 = (bf16[4,12288]{1,0:T(4,128)(2,1)}, bf16[4,12288]{1,0:T(4,128)(2,1)S(1)}, u32[]{:S(2)}, u32[]{:S(2)}) collective-permute-start(bf16[4,12288]{1,0:T(4,128)(2,1)} %refs_0_), channel_id=1, source_target_pairs={{0,2},{1,3},{2,0},{3,1},{4,6},{5,7},{6,4},{7,5},{8,10},{9,11},{10,... | collective-permute-start | bytes 294920 | tf_op jit(solution)/shard_map/ppermute | solution.py:186
  10.3 5.4 %collective-permute-start.7 = (bf16[4,12288]{1,0:T(4,128)(2,1)S(1)}, bf16[4,12288]{1,0:T(4,128)(2,1)S(1)}, u32[]{:S(2)}, u32[]{:S(2)}) collective-permute-start(bf16[4,12288]{1,0:T(4,128)(2,1)S(1)} %collective-permute-done.4.refs_1_), channel_id=1, source_target_pairs={{0,2},{1,3},{2,0},{3,1},{4,6},{5,7},{6,4},{7,5},{8,10},{9,11},{10,... | collective-permute-start | bytes 294920 | tf_op jit(solution)/shard_map/ppermute | solution.py:186
  15.7 18.3 %collective-permute-start.12 = (bf16[128,12288]{1,0:T(8,128)(2,1)}, bf16[128,12288]{1,0:T(8,128)(2,1)S(1)}, u32[]{:S(2)}, u32[]{:S(2)}) collective-permute-start(bf16[128,12288]{1,0:T(8,128)(2,1)} %refs_5_), channel_id=1, source_target_pairs={{0,1},{1,0},{2,3},{3,2},{4,5},{5,4},{6,7},{7,6},{8,9},{9,8},{10,11... | collective-permute-start | bytes 9437192 | tf_op jit(solution)/shard_map/ppermute | solution.py:189
  15.7 7.8 %collective-permute-start.8 = (bf16[768,512]{1,0:T(8,128)(2,1)}, bf16[768,512]{1,0:T(8,128)(2,1)S(1)}, u32[]{:S(2)}, u32[]{:S(2)}) collective-permute-start(bf16[768,512]{1,0:T(8,128)(2,1)} %refs_3_), channel_id=1, source_target_pairs={{0,1},{1,0},{2,3},{3,2},{4,5},{5,4},{6,7},{7,6},{8,9},{9,8},{10,11... | collective-permute-start | bytes 2359304 | tf_op jit(solution)/shard_map/ppermute | solution.py:189
  16.2 20.8 %collective-permute-start.11 = (bf16[512,768]{1,0:T(8,128)(2,1)}, bf16[512,768]{1,0:T(8,128)(2,1)S(1)}, u32[]{:S(2)}, u32[]{:S(2)}) collective-permute-start(bf16[512,768]{1,0:T(8,128)(2,1)} %refs_6_), channel_id=1, source_target_pairs={{0,1},{1,0},{2,3},{3,2},{4,5},{5,4},{6,7},{7,6},{8,9},{9,8},{10,11... | collective-permute-start | bytes 2359304 | tf_op jit(solution)/shard_map/ppermute | solution.py:189
  16.2 6.3 %collective-permute-start.1 = (bf16[4,12288]{1,0:T(4,128)(2,1)S(1)}, bf16[4,12288]{1,0:T(4,128)(2,1)S(1)}, u32[]{:S(2)}, u32[]{:S(2)}) collective-permute-start(bf16[4,12288]{1,0:T(4,128)(2,1)S(1)} %collective-permute-done.refs_2_), channel_id=1, source_target_pairs={{0,2},{1,3},{2,0},{3,1},{4,6},{5,7},{6,4},{7,5},{8,10},{9,11},{10,... | collective-permute-start | bytes 294920 | tf_op jit(solution)/shard_map/ppermute | solution.py:186
  18.0 5.6 %collective-permute-start.3 = (bf16[4,12288]{1,0:T(4,128)(2,1)S(1)}, bf16[4,12288]{1,0:T(4,128)(2,1)S(1)}, u32[]{:S(2)}, u32[]{:S(2)}) collective-permute-start(bf16[4,12288]{1,0:T(4,128)(2,1)S(1)} %collective-permute-done.2.refs_3_), channel_id=1, source_target_pairs={{0,2},{1,3},{2,0},{3,1},{4,6},{5,7},{6,4},{7,5},{8,10},{9,11},{10,... | collective-permute-start | bytes 294920 | tf_op jit(solution)/shard_map/ppermute | solution.py:186
  21.7 11.2 %copy-start.1 = (f32[128]{0:T(128)S(1)}, f32[128]{0:T(128)}, u32[]{:S(2)}) copy-start(f32[128]{0:T(128)} %param.19) | copy-start | bytes 1540
  24.3 3.9 %collective-permute-start.9 = (bf16[32,512]{1,0:T(8,128)(2,1)S(1)}, bf16[32,512]{1,0:T(8,128)(2,1)S(1)}, u32[]{:S(2)}, u32[]{:S(2)}) collective-permute-start(bf16[32,512]{1,0:T(8,128)(2,1)S(1)} %get-tuple-element.65), channel_id=1, source_target_pairs={{0,2},{1,3},{2,0},{3,1},{4,6},{5,7},{6,4},{7,5},{8,10},{9,11},{10,... | collective-permute-start | bytes 98312 | tf_op jit(solution)/shard_map/ppermute | solution.py:186
  28.3 7.0 %collective-permute-start.13 = (bf16[32,512]{1,0:T(8,128)(2,1)S(1)}, bf16[32,512]{1,0:T(8,128)(2,1)S(1)}, u32[]{:S(2)}, u32[]{:S(2)}) collective-permute-start(bf16[32,512]{1,0:T(8,128)(2,1)S(1)} %get-tuple-element.76), channel_id=1, source_target_pairs={{0,12},{1,13},{2,14},{3,15},{4,8},{5,9},{6,10},{7,11},{8,4},{9,5},... | collective-permute-start | bytes 98312 | tf_op jit(solution)/shard_map/ppermute | solution.py:183
  32.2 4.8 %collective-permute-start.14 = (bf16[32,512]{1,0:T(8,128)(2,1)S(1)}, bf16[32,512]{1,0:T(8,128)(2,1)S(1)}, u32[]{:S(2)}, u32[]{:S(2)}) collective-permute-start(bf16[32,512]{1,0:T(8,128)(2,1)S(1)} %get-tuple-element.77), channel_id=1, source_target_pairs={{0,8},{1,9},{2,10},{3,11},{4,12},{5,13},{6,14},{7,15},{8,0},{9,1},... | collective-permute-start | bytes 98312 | tf_op jit(solution)/shard_map/ppermute | solution.py:183
  32.2 4.8 %collective-permute-start.15 = (bf16[32,512]{1,0:T(8,128)(2,1)S(1)}, bf16[32,512]{1,0:T(8,128)(2,1)S(1)}, u32[]{:S(2)}, u32[]{:S(2)}) collective-permute-start(bf16[32,512]{1,0:T(8,128)(2,1)S(1)} %get-tuple-element.78), channel_id=1, source_target_pairs={{0,4},{1,5},{2,6},{3,7},{4,0},{5,1},{6,2},{7,3},{8,12},{9,13},{10,... | collective-permute-start | bytes 98312 | tf_op jit(solution)/shard_map/ppermute | solution.py:183
  34.1 2.9 %copy-start = (f32[512]{0:T(512)S(1)}, f32[512]{0:T(512)}, u32[]{:S(2)}) copy-start(f32[512]{0:T(512)} %param.22) | copy-start | bytes 6148
  37.5 5.6 %collective-permute-start.21 = (bf16[4,12288]{1,0:T(4,128)(2,1)S(1)}, bf16[4,12288]{1,0:T(4,128)(2,1)S(1)}, u32[]{:S(2)}, u32[]{:S(2)}) collective-permute-start(bf16[4,12288]{1,0:T(4,128)(2,1)S(1)} %get-tuple-element.86), channel_id=1, source_target_pairs={{0,2},{1,3},{2,0},{3,1},{4,6},{5,7},{6,4},{7,5},{8,10},{9,11},{10,... | collective-permute-start | bytes 294920 | tf_op jit(solution)/shard_map/ppermute | solution.py:186
  39.0 6.4 %collective-permute-start.19 = (bf16[4,12288]{1,0:T(4,128)(2,1)S(1)}, bf16[4,12288]{1,0:T(4,128)(2,1)S(1)}, u32[]{:S(2)}, u32[]{:S(2)}) collective-permute-start(bf16[4,12288]{1,0:T(4,128)(2,1)S(1)} %get-tuple-element.84), channel_id=1, source_target_pairs={{0,2},{1,3},{2,0},{3,1},{4,6},{5,7},{6,4},{7,5},{8,10},{9,11},{10,... | collective-permute-start | bytes 294920 | tf_op jit(solution)/shard_map/ppermute | solution.py:186
  39.5 6.2 %collective-permute-start.17 = (bf16[4,12288]{1,0:T(4,128)(2,1)S(1)}, bf16[4,12288]{1,0:T(4,128)(2,1)S(1)}, u32[]{:S(2)}, u32[]{:S(2)}) collective-permute-start(bf16[4,12288]{1,0:T(4,128)(2,1)S(1)} %get-tuple-element.82), channel_id=1, source_target_pairs={{0,2},{1,3},{2,0},{3,1},{4,6},{5,7},{6,4},{7,5},{8,10},{9,11},{10,... | collective-permute-start | bytes 294920 | tf_op jit(solution)/shard_map/ppermute | solution.py:186
  41.1 6.7 %collective-permute-start.16 = (bf16[4,12288]{1,0:T(4,128)(2,1)S(1)}, bf16[4,12288]{1,0:T(4,128)(2,1)S(1)}, u32[]{:S(2)}, u32[]{:S(2)}) collective-permute-start(bf16[4,12288]{1,0:T(4,128)(2,1)S(1)} %get-tuple-element.80), channel_id=1, source_target_pairs={{0,2},{1,3},{2,0},{3,1},{4,6},{5,7},{6,4},{7,5},{8,10},{9,11},{10,... | collective-permute-start | bytes 294920 | tf_op jit(solution)/shard_map/ppermute | solution.py:186
  43.1 6.5 %collective-permute-start.22 = (bf16[4,12288]{1,0:T(4,128)(2,1)S(1)}, bf16[4,12288]{1,0:T(4,128)(2,1)S(1)}, u32[]{:S(2)}, u32[]{:S(2)}) collective-permute-start(bf16[4,12288]{1,0:T(4,128)(2,1)S(1)} %add_convert_fusion), channel_id=1, source_target_pairs={{0,12},{1,13},{2,14},{3,15},{4,8},{5,9},{6,10},{7,11},{8,4},{9,5},... | collective-permute-start | bytes 294920 | tf_op jit(solution)/shard_map/ppermute | solution.py:183
  45.5 6.2 %collective-permute-start.20 = (bf16[4,12288]{1,0:T(4,128)(2,1)S(1)}, bf16[4,12288]{1,0:T(4,128)(2,1)S(1)}, u32[]{:S(2)}, u32[]{:S(2)}) collective-permute-start(bf16[4,12288]{1,0:T(4,128)(2,1)S(1)} %add_convert_fusion.1), channel_id=1, source_target_pairs={{0,8},{1,9},{2,10},{3,11},{4,12},{5,13},{6,14},{7,15},{8,0},{9,1},... | collective-permute-start | bytes 294920 | tf_op jit(solution)/shard_map/ppermute | solution.py:183
  45.9 5.8 %collective-permute-start.18 = (bf16[4,12288]{1,0:T(4,128)(2,1)S(1)}, bf16[4,12288]{1,0:T(4,128)(2,1)S(1)}, u32[]{:S(2)}, u32[]{:S(2)}) collective-permute-start(bf16[4,12288]{1,0:T(4,128)(2,1)S(1)} %add_convert_fusion.2), channel_id=1, source_target_pairs={{0,4},{1,5},{2,6},{3,7},{4,0},{5,1},{6,2},{7,3},{8,12},{9,13},{10,... | collective-permute-start | bytes 294920 | tf_op jit(solution)/shard_map/ppermute | solution.py:183

commit v19 on v18

--- a/solution.py
+++ b/solution.py
@@ -202,12 +202,12 @@
     live = jnp.sum(jnp.where(relate & choose, table[None, None], 0), axis=(2, 3)).astype(f32)
     mask = jnp.broadcast_to(live[None, :, None, :, None], (2, groups, row_dev, 2, block)).reshape(rows, 2 * block)
 
-    held = [hidden] + [across(hidden, k) for k in range(1, groups)]
+    start, bias_mate = lax.optimization_barrier((hidden, core(bias)))
+    held = [hidden] + [across(start, k) for k in range(1, groups)]
     w_in_mate = core(w_in)
     held[1], low_in_sent, mask = lax.optimization_barrier((held[1], low_in, mask))
     low_in_mate = core(low_in_sent)
-    early, bias_mate = lax.optimization_barrier((hidden, core(bias)))
-    beyond = [beside(h) for h in [early] + held[1:]]
+    beyond = [beside(h) for h in [start] + held[1:]]
     near = (hidden, gain, shift, low_in, w_in, w_out, low_out)
     *near, mask, beyond[0] = lax.optimization_barrier((*near, mask, beyond[0]))
     near = call(

time: 52.6 us -> 57.5 us (1.093)
  waiting for transfers between devices: 15.3 us -> 20.3 us
    ppermute x9, waiting for transfers between devices: 5.59 us -> 12.1 us  [across(): return lax.ppermute(x, 'blk', [(i, i ^ 4 * k) for i in range(devices)])]
    ppermute x9, waiting for transfers between devices: 9.67 us -> 5.21 us  [beside(): return lax.ppermute(x, 'blk', [(i, i ^ 2) for i in range(devices)])]
    ppermute x5, waiting for transfers between devices: 0.01 us -> 2.96 us  [core(): return lax.ppermute(x, 'blk', [(i, i ^ 1) for i in range(devices)])]
    ppermute x9, starting transfers between devices: 10.1 us -> 9.21 us  [beside(): return lax.ppermute(x, 'blk', [(i, i ^ 2) for i in range(devices)])]
    ppermute x9, starting transfers between devices: 14.3 us -> 14.9 us  [across(): return lax.ppermute(x, 'blk', [(i, i ^ 4 * k) for i in range(devices)])]
  transfers between devices with their start and end apart: 23 -> 23, of which waited for: 8 -> 9; matrix products, arithmetic and copies ran while one was open for 6% -> 5% of each run, Pallas kernels for 14% -> 13%
where the time goes in v19:
time: 57.5 us; the launch traced here: 57.3 us
  starting transfers between devices  25.2 us (44%)
  waiting for transfers between devices  20.3 us (35%)
  Pallas kernels  8.58 us (15%)
  other arithmetic  2.22 us (4%)
  local copies, waits for them, and re-layouts  0.86 us (1%)
    ppermute x9, starting transfers between devices, across(): return lax.ppermute(x, 'blk', [(i, i ^ 4 * k) for i in range(devices)])  14.9 us
    ppermute x9, waiting for transfers between devices, across(): return lax.ppermute(x, 'blk', [(i, i ^ 4 * k) for i in range(devices)])  12.1 us
    ppermute x9, starting transfers between devices, beside(): return lax.ppermute(x, 'blk', [(i, i ^ 2) for i in range(devices)])  9.21 us
    ppermute x9, waiting for transfers between devices, beside(): return lax.ppermute(x, 'blk', [(i, i ^ 2) for i in range(devices)])  5.21 us
    pallas_call x1, Pallas kernels, shards(): call(functools.partial(load_body, len(near)), [shape(*x.shape, dtype=x.dt...  3.39 us
    ppermute x5, waiting for transfers between devices, core(): return lax.ppermute(x, 'blk', [(i, i ^ 1) for i in range(devices)])  2.96 us
    pallas_call x1, Pallas kernels, shards(): call(functools.partial(act_body, step), [shape(rows, 2 * block)], [VMEM]...  1.21 us
    pallas_call x1, Pallas kernels, shards(): call(functools.partial(part_body, step), [shape(rows, width, dtype=f32)],...  1.19 us
  transfers between devices with their start and end apart: 23, of which 9 were waited for; matrix products, arithmetic and copies ran while one was open for 5% of the time, Pallas kernels for 13%

profile of v19, /device:TPU:0, one launch (start us, length us, event | category | flops | bytes accessed | tf_op | source)
XLA Modules:
  0.0 57.3 jit_solution(11563537599232249367)
XLA Ops:
  0.5 0.8 %copy.13 = s32[4,6]{0,1:T(8,128)S(1)} copy(s32[4,6]{1,0:T(4,128)} %param.15) | data formatting | bytes 192 | tf_op args[3]
  1.3 0.7 %fusion.1 = s32[4,6]{0,1:T(8,128)S(1)} fusion(s32[4]{0:T(128)} %param.16), kind=kLoop, calls=%fused_computation.12 | loop fusion | flops 48 | bytes 112 | tf_op jit(solution)/shard_map/convert_element_type | solution.py:150
  2.2 0.7 %fusion = s32[16,16]{1,0:T(8,128)S(1)} fusion(s32[16]{0:T(128)} %param.17), kind=kLoop, calls=%fused_computation.10 | loop fusion | flops 512 | bytes 1088 | tf_op jit(solution)/shard_map/convert_element_type | solution.py:153
  3.0 3.0 %collective-permute-done.b_mate = f32[1,128]{1,0:T(1,128)S(1)} collective-permute-done((f32[1,128]{1,0:T(1,128)}, f32[1,128]{1,0:T(1,128)S(1)}, u32[]{:S(2)}, u32[]{:S(2)}) %collective-permute-start) | collective-permute-done | bytes 544 | tf_op jit(solution)/shard_map/ppermute | solution.py:189
  6.0 2.9 %collective-permute-start.5 = (bf16[4,12288]{1,0:T(4,128)(2,1)}, bf16[4,12288]{1,0:T(4,128)(2,1)S(1)}, u32[]{:S(2)}, u32[]{:S(2)}) collective-permute-start(bf16[4,12288]{1,0:T(4,128)(2,1)} %refs_0_), channel_id=1, source_target_pairs={{0,4},{1,5},{2,6},{3,7},{4,0},{5,1},{6,2},{7,3},{8,12},{9,13},{10,... | collective-permute-start | bytes 294920 | tf_op jit(solution)/shard_map/ppermute | solution.py:183
  9.2 1.6 %collective-permute-start.6 = (bf16[4,12288]{1,0:T(4,128)(2,1)}, bf16[4,12288]{1,0:T(4,128)(2,1)S(1)}, u32[]{:S(2)}, u32[]{:S(2)}) collective-permute-start(bf16[4,12288]{1,0:T(4,128)(2,1)} %refs_0_), channel_id=1, source_target_pairs={{0,2},{1,3},{2,0},{3,1},{4,6},{5,7},{6,4},{7,5},{8,10},{9,11},{10,... | collective-permute-start | bytes 294920 | tf_op jit(solution)/shard_map/ppermute | solution.py:186
  10.9 2.7 %collective-permute-start.1 = (bf16[4,12288]{1,0:T(4,128)(2,1)}, bf16[4,12288]{1,0:T(4,128)(2,1)S(1)}, u32[]{:S(2)}, u32[]{:S(2)}) collective-permute-start(bf16[4,12288]{1,0:T(4,128)(2,1)} %refs_0_), channel_id=1, source_target_pairs={{0,8},{1,9},{2,10},{3,11},{4,12},{5,13},{6,14},{7,15},{8,0},{9,1},... | collective-permute-start | bytes 294920 | tf_op jit(solution)/shard_map/ppermute | solution.py:183
  14.1 6.7 %collective-permute-done.1.refs_2_ = bf16[4,12288]{1,0:T(4,128)(2,1)S(1)} collective-permute-done((bf16[4,12288]{1,0:T(4,128)(2,1)}, bf16[4,12288]{1,0:T(4,128)(2,1)S(1)}, u32[]{:S(2)}, u32[]{:S(2)}) %collective-permute-start.1) | collective-permute-done | bytes 98336 | tf_op jit(solution)/shard_map/ppermute | solution.py:183
  20.9 0.5 collective-permute-start.8
  21.5 1.2 %collective-permute-start.2 = (bf16[4,12288]{1,0:T(4,128)(2,1)S(1)}, bf16[4,12288]{1,0:T(4,128)(2,1)S(1)}, u32[]{:S(2)}, u32[]{:S(2)}) collective-permute-start(bf16[4,12288]{1,0:T(4,128)(2,1)S(1)} %collective-permute-done.1.refs_2_), channel_id=1, source_target_pairs={{0,2},{1,3},{2,0},{3,1},{4,6},{5,7},{6,4},{7,5},{8,10},{9,11},{10,... | collective-permute-start | bytes 294920 | tf_op jit(solution)/shard_map/ppermute | solution.py:186
  22.7 0.8 %collective-permute-start.4 = (bf16[4,12288]{1,0:T(4,128)(2,1)S(1)}, bf16[4,12288]{1,0:T(4,128)(2,1)S(1)}, u32[]{:S(2)}, u32[]{:S(2)}) collective-permute-start(bf16[4,12288]{1,0:T(4,128)(2,1)S(1)} %collective-permute-done.3.refs_3_), channel_id=1, source_target_pairs={{0,2},{1,3},{2,0},{3,1},{4,6},{5,7},{6,4},{7,5},{8,10},{9,11},{10,... | collective-permute-start | bytes 294920 | tf_op jit(solution)/shard_map/ppermute | solution.py:186
  23.5 3.4 %shard_map.118 = (bf16[4,12288]{1,0:T(4,128)(2,1)S(1)}, f32[1,12288]{1,0:T(1,128)S(1)}, f32[1,12288]{1,0:T(1,128)S(1)}, bf16[768,512]{1,0:T(8,128)(2,1)S(1)}, bf...) custom-call(bf16[4,12288]{1,0:T(4,128)(2,1)} %refs_0_, ...), custom_call_target="tpu_custom_call" | custom-call | bytes 8388608 | tf_op jit(solution)/shard_map/pallas_call | solution.py:213
  26.9 0.8 %shard_map.119 = (bf16[16,12288]{1,0:T(8,128)(2,1)S(1)}, bf16[8,12288]{1,0:T(8,128)(2,1)S(1)}) custom-call(bf16[4,12288]{1,0:T(4,128)(2,1)S(1)} %get-tuple-element.55.refs_0_, bf16[4,12288]{1,0:T(4,128)(2,1)S(1)} %collective-permute-done.5.refs_1_, bf16[4,12288]{1,0:T(4,128)(2,1)S(1)} %collective-permute-done.1.refs_2_, ...), custom_call_target="tpu_custom_call" | custom-call | bytes 4194304 | tf_op jit(solution)/shard_map/pallas_call | solution.py:229
  27.8 1.0 %collective-permute-done.4.refs_1_ = bf16[4,12288]{1,0:T(4,128)(2,1)S(1)} collective-permute-done((bf16[4,12288]{1,0:T(4,128)(2,1)S(1)}, bf16[4,12288]{1,0:T(4,128)(2,1)S(1)}, u32[]{:S(2)}, u32[]{:S(2)}) %collective-permute-start.4) | collective-permute-done | bytes 98336 | tf_op jit(solution)/shard_map/ppermute | solution.py:186
  28.7 0.8 %shard_map.120 = (bf16[16,12288]{1,0:T(8,128)(2,1)S(1)}, f32[32,512]{1,0:T(8,128)S(1)}, bf16[32,512]{1,0:T(8,128)(2,1)S(1)}) custom-call(s32[1]{0:T(128)} %bitcast.place, bf16[4,12288]{1,0:T(4,128)(2,1)S(1)} %collective-permute-done.2.refs_0_, bf16[4,12288]{1,0:T(4,128)(2,1)S(1)} %collective-permute-done.4.refs_1_, ...), custom_call_target="tpu_custom_call" | custom-call | bytes 4194304 | tf_op jit(solution)/shard_map/pallas_call | solution.py:237
  29.5 1.2 %collective-permute-start.9 = (bf16[32,512]{1,0:T(8,128)(2,1)S(1)}, bf16[32,512]{1,0:T(8,128)(2,1)S(1)}, u32[]{:S(2)}, u32[]{:S(2)}) collective-permute-start(bf16[32,512]{1,0:T(8,128)(2,1)S(1)} %get-tuple-element.65), channel_id=1, source_target_pairs={{0,2},{1,3},{2,0},{3,1},{4,6},{5,7},{6,4},{7,5},{8,10},{9,11},{10,... | collective-permute-start | bytes 98312 | tf_op jit(solution)/shard_map/ppermute | solution.py:186
  30.7 2.7 %collective-permute-done.9.got = bf16[32,512]{1,0:T(8,128)(2,1)S(1)} collective-permute-done((bf16[32,512]{1,0:T(8,128)(2,1)S(1)}, bf16[32,512]{1,0:T(8,128)(2,1)S(1)}, u32[]{:S(2)}, u32[]{:S(2)}) %collective-permute-start.9) | collective-permute-done | bytes 32800 | tf_op jit(solution)/shard_map/ppermute | solution.py:186
  33.5 3.3 %collective-permute-start.13 = (bf16[32,512]{1,0:T(8,128)(2,1)S(1)}, bf16[32,512]{1,0:T(8,128)(2,1)S(1)}, u32[]{:S(2)}, u32[]{:S(2)}) collective-permute-start(bf16[32,512]{1,0:T(8,128)(2,1)S(1)} %get-tuple-element.76), channel_id=1, source_target_pairs={{0,12},{1,13},{2,14},{3,15},{4,8},{5,9},{6,10},{7,11},{8,4},{9,5},... | collective-permute-start | bytes 98312 | tf_op jit(solution)/shard_map/ppermute | solution.py:183
  37.3 0.7 %collective-permute-start.15 = (bf16[32,512]{1,0:T(8,128)(2,1)S(1)}, bf16[32,512]{1,0:T(8,128)(2,1)S(1)}, u32[]{:S(2)}, u32[]{:S(2)}) collective-permute-start(bf16[32,512]{1,0:T(8,128)(2,1)S(1)} %get-tuple-element.78), channel_id=1, source_target_pairs={{0,4},{1,5},{2,6},{3,7},{4,0},{5,1},{6,2},{7,3},{8,12},{9,13},{10,... | collective-permute-start | bytes 98312 | tf_op jit(solution)/shard_map/ppermute | solution.py:183
  37.9 1.2 %shard_map.122.act = bf16[32,256]{1,0:T(8,128)(2,1)S(1)} custom-call(bf16[16,12288]{1,0:T(8,128)(2,1)S(1)} %get-tuple-element.60.refs_2_.near, bf16[16,12288]{1,0:T(8,128)(2,1)S(1)} %get-tuple-element.69.far, bf16[12288,128]{1,0:T(8,128)(2,1)S(1)} %get-tuple-element.70.w_own, bf16[12288,128]{1,0:T(8,128)(2,1)S(1)} %collective-permute-done.10.w_mate, ...), custom_call_target="tpu_custom_call" | custom-call | bytes 4194304 | tf_op jit(solution)/shard_map/pallas_call | solution.py:247
  39.2 1.2 %shard_map.123.part = f32[32,12288]{1,0:T(8,128)S(1)} custom-call(bf16[32,256]{1,0:T(8,128)(2,1)S(1)} %shard_map.122.act, bf16[128,12288]{1,0:T(8,128)(2,1)S(1)} %get-tuple-element.74.w_own, bf16[128,12288]{1,0:T(8,128)(2,1)S(1)} %collective-permute-done.12.w_mate), custom_call_target="tpu_custom_call" | custom-call | bytes 6291456 | tf_op jit(solution)/shard_map/pallas_call | solution.py:262
  40.4 1.6 %collective-permute-done.14.refs_1_ = bf16[32,512]{1,0:T(8,128)(2,1)S(1)} collective-permute-done((bf16[32,512]{1,0:T(8,128)(2,1)S(1)}, bf16[32,512]{1,0:T(8,128)(2,1)S(1)}, u32[]{:S(2)}, u32[]{:S(2)}) %collective-permute-start.14) | collective-permute-done | bytes 32800 | tf_op jit(solution)/shard_map/ppermute | solution.py:183
  42.4 0.6 %collective-permute-start.21 = (bf16[4,12288]{1,0:T(4,128)(2,1)S(1)}, bf16[4,12288]{1,0:T(4,128)(2,1)S(1)}, u32[]{:S(2)}, u32[]{:S(2)}) collective-permute-start(bf16[4,12288]{1,0:T(4,128)(2,1)S(1)} %get-tuple-element.86), channel_id=1, source_target_pairs={{0,2},{1,3},{2,0},{3,1},{4,6},{5,7},{6,4},{7,5},{8,10},{9,11},{10,... | collective-permute-start | bytes 294920 | tf_op jit(solution)/shard_map/ppermute | solution.py:186
  43.0 1.5 %collective-permute-start.19 = (bf16[4,12288]{1,0:T(4,128)(2,1)S(1)}, bf16[4,12288]{1,0:T(4,128)(2,1)S(1)}, u32[]{:S(2)}, u32[]{:S(2)}) collective-permute-start(bf16[4,12288]{1,0:T(4,128)(2,1)S(1)} %get-tuple-element.84), channel_id=1, source_target_pairs={{0,2},{1,3},{2,0},{3,1},{4,6},{5,7},{6,4},{7,5},{8,10},{9,11},{10,... | collective-permute-start | bytes 294920 | tf_op jit(solution)/shard_map/ppermute | solution.py:186
  44.5 0.6 collective-permute-start.17
  45.1 1.5 %collective-permute-start.16 = (bf16[4,12288]{1,0:T(4,128)(2,1)S(1)}, bf16[4,12288]{1,0:T(4,128)(2,1)S(1)}, u32[]{:S(2)}, u32[]{:S(2)}) collective-permute-start(bf16[4,12288]{1,0:T(4,128)(2,1)S(1)} %get-tuple-element.80), channel_id=1, source_target_pairs={{0,2},{1,3},{2,0},{3,1},{4,6},{5,7},{6,4},{7,5},{8,10},{9,11},{10,... | collective-permute-start | bytes 294920 | tf_op jit(solution)/shard_map/ppermute | solution.py:186
  46.5 1.4 %collective-permute-done.21 = bf16[4,12288]{1,0:T(4,128)(2,1)S(1)} collective-permute-done((bf16[4,12288]{1,0:T(4,128)(2,1)S(1)}, bf16[4,12288]{1,0:T(4,128)(2,1)S(1)}, u32[]{:S(2)}, u32[]{:S(2)}) %collective-permute-start.21) | collective-permute-done | bytes 98336 | tf_op jit(solution)/shard_map/ppermute | solution.py:186
  48.0 1.8 %collective-permute-start.22 = (bf16[4,12288]{1,0:T(4,128)(2,1)S(1)}, bf16[4,12288]{1,0:T(4,128)(2,1)S(1)}, u32[]{:S(2)}, u32[]{:S(2)}) collective-permute-start(bf16[4,12288]{1,0:T(4,128)(2,1)S(1)} %add_convert_fusion), channel_id=1, source_target_pairs={{0,12},{1,13},{2,14},{3,15},{4,8},{5,9},{6,10},{7,11},{8,4},{9,5},... | collective-permute-start | bytes 294920 | tf_op jit(solution)/shard_map/ppermute | solution.py:183
  50.3 2.4 %collective-permute-start.18 = (bf16[4,12288]{1,0:T(4,128)(2,1)S(1)}, bf16[4,12288]{1,0:T(4,128)(2,1)S(1)}, u32[]{:S(2)}, u32[]{:S(2)}) collective-permute-start(bf16[4,12288]{1,0:T(4,128)(2,1)S(1)} %add_convert_fusion.2), channel_id=1, source_target_pairs={{0,4},{1,5},{2,6},{3,7},{4,0},{5,1},{6,2},{7,3},{8,12},{9,13},{10,... | collective-permute-start | bytes 294920 | tf_op jit(solution)/shard_map/ppermute | solution.py:183
  52.8 1.7 %collective-permute-done.22.refs_3_ = bf16[4,12288]{1,0:T(4,128)(2,1)S(1)} collective-permute-done((bf16[4,12288]{1,0:T(4,128)(2,1)S(1)}, bf16[4,12288]{1,0:T(4,128)(2,1)S(1)}, u32[]{:S(2)}, u32[]{:S(2)}) %collective-permute-start.22) | collective-permute-done | bytes 98336 | tf_op jit(solution)/shard_map/ppermute | solution.py:183
  54.5 2.1 %collective-permute-done.20.refs_2_ = bf16[4,12288]{1,0:T(4,128)(2,1)S(1)} collective-permute-done((bf16[4,12288]{1,0:T(4,128)(2,1)S(1)}, bf16[4,12288]{1,0:T(4,128)(2,1)S(1)}, u32[]{:S(2)}, u32[]{:S(2)}) %collective-permute-start.20) | collective-permute-done | bytes 98336 | tf_op jit(solution)/shard_map/ppermute | solution.py:183
  56.6 0.7 %shard_map.125 = bf16[4,12288]{1,0:T(4,128)(2,1)} custom-call(f32[4,12288]{1,0:T(4,128)S(1)} %convert_add_fusion.refs_0_, bf16[4,12288]{1,0:T(4,128)(2,1)S(1)} %collective-permute-done.18.refs_1_, bf16[4,12288]{1,0:T(4,128)(2,1)S(1)} %collective-permute-done.20.refs_2_, bf16[4,12288]{1,0:T(4,128)(2,1)S(1)} %collective-permute-done.22.refs_3_), custom_call_target="tpu_custom_call" | custom-call | bytes 2097152 | tf_op jit(solution)/shard_map/pallas_call | solution.py:283
  (43 shorter events, 3.5 us)
Async XLA Ops:
  0.0 20.8 %collective-permute-start.10 = (bf16[12288,128]{1,0:T(8,128)(2,1)}, bf16[12288,128]{1,0:T(8,128)(2,1)S(1)}, u32[]{:S(2)}, u32[]{:S(2)}) collective-permute-start(bf16[12288,128]{1,0:T(8,128)(2,1)} %refs_4_), channel_id=1, source_target_pairs={{0,1},{1,0},{2,3},{3,2},{4,5},{5,4},{6,7},{7,6},{8,9},{9,8},{10,11... | collective-permute-start | bytes 9437192 | tf_op jit(solution)/shard_map/ppermute | solution.py:189
  0.5 5.5 %collective-permute-start = (f32[1,128]{1,0:T(1,128)}, f32[1,128]{1,0:T(1,128)S(1)}, u32[]{:S(2)}, u32[]{:S(2)}) collective-permute-start(f32[1,128]{1,0:T(1,128)} %bitcast.12), channel_id=1, source_target_pairs={{0,1},{1,0},{2,3},{3,2},{4,5},{5,4},{6,7},{7,6},{8,9},{9,8},{10,11... | collective-permute-start | bytes 1544 | tf_op jit(solution)/shard_map/ppermute | solution.py:189
  6.0 7.8 %collective-permute-start.5 = (bf16[4,12288]{1,0:T(4,128)(2,1)}, bf16[4,12288]{1,0:T(4,128)(2,1)S(1)}, u32[]{:S(2)}, u32[]{:S(2)}) collective-permute-start(bf16[4,12288]{1,0:T(4,128)(2,1)} %refs_0_), channel_id=1, source_target_pairs={{0,4},{1,5},{2,6},{3,7},{4,0},{5,1},{6,2},{7,3},{8,12},{9,13},{10,... | collective-permute-start | bytes 294920 | tf_op jit(solution)/shard_map/ppermute | solution.py:183
  9.2 4.9 %collective-permute-start.6 = (bf16[4,12288]{1,0:T(4,128)(2,1)}, bf16[4,12288]{1,0:T(4,128)(2,1)S(1)}, u32[]{:S(2)}, u32[]{:S(2)}) collective-permute-start(bf16[4,12288]{1,0:T(4,128)(2,1)} %refs_0_), channel_id=1, source_target_pairs={{0,2},{1,3},{2,0},{3,1},{4,6},{5,7},{6,4},{7,5},{8,10},{9,11},{10,... | collective-permute-start | bytes 294920 | tf_op jit(solution)/shard_map/ppermute | solution.py:186
  10.9 9.9 %collective-permute-start.1 = (bf16[4,12288]{1,0:T(4,128)(2,1)}, bf16[4,12288]{1,0:T(4,128)(2,1)S(1)}, u32[]{:S(2)}, u32[]{:S(2)}) collective-permute-start(bf16[4,12288]{1,0:T(4,128)(2,1)} %refs_0_), channel_id=1, source_target_pairs={{0,8},{1,9},{2,10},{3,11},{4,12},{5,13},{6,14},{7,15},{8,0},{9,1},... | collective-permute-start | bytes 294920 | tf_op jit(solution)/shard_map/ppermute | solution.py:183
  13.5 7.3 %collective-permute-start.3 = (bf16[4,12288]{1,0:T(4,128)(2,1)}, bf16[4,12288]{1,0:T(4,128)(2,1)S(1)}, u32[]{:S(2)}, u32[]{:S(2)}) collective-permute-start(bf16[4,12288]{1,0:T(4,128)(2,1)} %refs_0_), channel_id=1, source_target_pairs={{0,12},{1,13},{2,14},{3,15},{4,8},{5,9},{6,10},{7,11},{8,4},{9,5},... | collective-permute-start | bytes 294920 | tf_op jit(solution)/shard_map/ppermute | solution.py:183
  13.7 7.1 %collective-permute-start.7 = (bf16[4,12288]{1,0:T(4,128)(2,1)S(1)}, bf16[4,12288]{1,0:T(4,128)(2,1)S(1)}, u32[]{:S(2)}, u32[]{:S(2)}) collective-permute-start(bf16[4,12288]{1,0:T(4,128)(2,1)S(1)} %collective-permute-done.5.refs_1_), channel_id=1, source_target_pairs={{0,2},{1,3},{2,0},{3,1},{4,6},{5,7},{6,4},{7,5},{8,10},{9,11},{10,... | collective-permute-start | bytes 294920 | tf_op jit(solution)/shard_map/ppermute | solution.py:186
  20.8 18.3 %collective-permute-start.12 = (bf16[128,12288]{1,0:T(8,128)(2,1)}, bf16[128,12288]{1,0:T(8,128)(2,1)S(1)}, u32[]{:S(2)}, u32[]{:S(2)}) collective-permute-start(bf16[128,12288]{1,0:T(8,128)(2,1)} %refs_5_), channel_id=1, source_target_pairs={{0,1},{1,0},{2,3},{3,2},{4,5},{5,4},{6,7},{7,6},{8,9},{9,8},{10,11... | collective-permute-start | bytes 9437192 | tf_op jit(solution)/shard_map/ppermute | solution.py:189
  20.9 7.8 %collective-permute-start.8 = (bf16[768,512]{1,0:T(8,128)(2,1)}, bf16[768,512]{1,0:T(8,128)(2,1)S(1)}, u32[]{:S(2)}, u32[]{:S(2)}) collective-permute-start(bf16[768,512]{1,0:T(8,128)(2,1)} %refs_3_), channel_id=1, source_target_pairs={{0,1},{1,0},{2,3},{3,2},{4,5},{5,4},{6,7},{7,6},{8,9},{9,8},{10,11... | collective-permute-start | bytes 2359304 | tf_op jit(solution)/shard_map/ppermute | solution.py:189
  21.4 20.6 %collective-permute-start.11 = (bf16[512,768]{1,0:T(8,128)(2,1)}, bf16[512,768]{1,0:T(8,128)(2,1)S(1)}, u32[]{:S(2)}, u32[]{:S(2)}) collective-permute-start(bf16[512,768]{1,0:T(8,128)(2,1)} %refs_6_), channel_id=1, source_target_pairs={{0,1},{1,0},{2,3},{3,2},{4,5},{5,4},{6,7},{7,6},{8,9},{9,8},{10,11... | collective-permute-start | bytes 2359304 | tf_op jit(solution)/shard_map/ppermute | solution.py:189
  21.5 6.3 %collective-permute-start.2 = (bf16[4,12288]{1,0:T(4,128)(2,1)S(1)}, bf16[4,12288]{1,0:T(4,128)(2,1)S(1)}, u32[]{:S(2)}, u32[]{:S(2)}) collective-permute-start(bf16[4,12288]{1,0:T(4,128)(2,1)S(1)} %collective-permute-done.1.refs_2_), channel_id=1, source_target_pairs={{0,2},{1,3},{2,0},{3,1},{4,6},{5,7},{6,4},{7,5},{8,10},{9,11},{10,... | collective-permute-start | bytes 294920 | tf_op jit(solution)/shard_map/ppermute | solution.py:186
  22.7 6.1 %collective-permute-start.4 = (bf16[4,12288]{1,0:T(4,128)(2,1)S(1)}, bf16[4,12288]{1,0:T(4,128)(2,1)S(1)}, u32[]{:S(2)}, u32[]{:S(2)}) collective-permute-start(bf16[4,12288]{1,0:T(4,128)(2,1)S(1)} %collective-permute-done.3.refs_3_), channel_id=1, source_target_pairs={{0,2},{1,3},{2,0},{3,1},{4,6},{5,7},{6,4},{7,5},{8,10},{9,11},{10,... | collective-permute-start | bytes 294920 | tf_op jit(solution)/shard_map/ppermute | solution.py:186
  26.9 11.0 %copy-start.1 = (f32[128]{0:T(128)S(1)}, f32[128]{0:T(128)}, u32[]{:S(2)}) copy-start(f32[128]{0:T(128)} %param.19) | copy-start | bytes 1540
  29.5 3.9 %collective-permute-start.9 = (bf16[32,512]{1,0:T(8,128)(2,1)S(1)}, bf16[32,512]{1,0:T(8,128)(2,1)S(1)}, u32[]{:S(2)}, u32[]{:S(2)}) collective-permute-start(bf16[32,512]{1,0:T(8,128)(2,1)S(1)} %get-tuple-element.65), channel_id=1, source_target_pairs={{0,2},{1,3},{2,0},{3,1},{4,6},{5,7},{6,4},{7,5},{8,10},{9,11},{10,... | collective-permute-start | bytes 98312 | tf_op jit(solution)/shard_map/ppermute | solution.py:186
  33.5 6.9 %collective-permute-start.13 = (bf16[32,512]{1,0:T(8,128)(2,1)S(1)}, bf16[32,512]{1,0:T(8,128)(2,1)S(1)}, u32[]{:S(2)}, u32[]{:S(2)}) collective-permute-start(bf16[32,512]{1,0:T(8,128)(2,1)S(1)} %get-tuple-element.76), channel_id=1, source_target_pairs={{0,12},{1,13},{2,14},{3,15},{4,8},{5,9},{6,10},{7,11},{8,4},{9,5},... | collective-permute-start | bytes 98312 | tf_op jit(solution)/shard_map/ppermute | solution.py:183
  36.8 5.2 %collective-permute-start.14 = (bf16[32,512]{1,0:T(8,128)(2,1)S(1)}, bf16[32,512]{1,0:T(8,128)(2,1)S(1)}, u32[]{:S(2)}, u32[]{:S(2)}) collective-permute-start(bf16[32,512]{1,0:T(8,128)(2,1)S(1)} %get-tuple-element.77), channel_id=1, source_target_pairs={{0,8},{1,9},{2,10},{3,11},{4,12},{5,13},{6,14},{7,15},{8,0},{9,1},... | collective-permute-start | bytes 98312 | tf_op jit(solution)/shard_map/ppermute | solution.py:183
  37.3 4.7 %collective-permute-start.15 = (bf16[32,512]{1,0:T(8,128)(2,1)S(1)}, bf16[32,512]{1,0:T(8,128)(2,1)S(1)}, u32[]{:S(2)}, u32[]{:S(2)}) collective-permute-start(bf16[32,512]{1,0:T(8,128)(2,1)S(1)} %get-tuple-element.78), channel_id=1, source_target_pairs={{0,4},{1,5},{2,6},{3,7},{4,0},{5,1},{6,2},{7,3},{8,12},{9,13},{10,... | collective-permute-start | bytes 98312 | tf_op jit(solution)/shard_map/ppermute | solution.py:183
  39.2 2.8 %copy-start = (f32[512]{0:T(512)S(1)}, f32[512]{0:T(512)}, u32[]{:S(2)}) copy-start(f32[512]{0:T(512)} %param.22) | copy-start | bytes 6148
  42.4 5.6 %collective-permute-start.21 = (bf16[4,12288]{1,0:T(4,128)(2,1)S(1)}, bf16[4,12288]{1,0:T(4,128)(2,1)S(1)}, u32[]{:S(2)}, u32[]{:S(2)}) collective-permute-start(bf16[4,12288]{1,0:T(4,128)(2,1)S(1)} %get-tuple-element.86), channel_id=1, source_target_pairs={{0,2},{1,3},{2,0},{3,1},{4,6},{5,7},{6,4},{7,5},{8,10},{9,11},{10,... | collective-permute-start | bytes 294920 | tf_op jit(solution)/shard_map/ppermute | solution.py:186
  43.0 6.8 %collective-permute-start.19 = (bf16[4,12288]{1,0:T(4,128)(2,1)S(1)}, bf16[4,12288]{1,0:T(4,128)(2,1)S(1)}, u32[]{:S(2)}, u32[]{:S(2)}) collective-permute-start(bf16[4,12288]{1,0:T(4,128)(2,1)S(1)} %get-tuple-element.84), channel_id=1, source_target_pairs={{0,2},{1,3},{2,0},{3,1},{4,6},{5,7},{6,4},{7,5},{8,10},{9,11},{10,... | collective-permute-start | bytes 294920 | tf_op jit(solution)/shard_map/ppermute | solution.py:186
  44.5 5.8 %collective-permute-start.17 = (bf16[4,12288]{1,0:T(4,128)(2,1)S(1)}, bf16[4,12288]{1,0:T(4,128)(2,1)S(1)}, u32[]{:S(2)}, u32[]{:S(2)}) collective-permute-start(bf16[4,12288]{1,0:T(4,128)(2,1)S(1)} %get-tuple-element.82), channel_id=1, source_target_pairs={{0,2},{1,3},{2,0},{3,1},{4,6},{5,7},{6,4},{7,5},{8,10},{9,11},{10,... | collective-permute-start | bytes 294920 | tf_op jit(solution)/shard_map/ppermute | solution.py:186
  45.1 7.7 %collective-permute-start.16 = (bf16[4,12288]{1,0:T(4,128)(2,1)S(1)}, bf16[4,12288]{1,0:T(4,128)(2,1)S(1)}, u32[]{:S(2)}, u32[]{:S(2)}) collective-permute-start(bf16[4,12288]{1,0:T(4,128)(2,1)S(1)} %get-tuple-element.80), channel_id=1, source_target_pairs={{0,2},{1,3},{2,0},{3,1},{4,6},{5,7},{6,4},{7,5},{8,10},{9,11},{10,... | collective-permute-start | bytes 294920 | tf_op jit(solution)/shard_map/ppermute | solution.py:186
  48.0 6.5 %collective-permute-start.22 = (bf16[4,12288]{1,0:T(4,128)(2,1)S(1)}, bf16[4,12288]{1,0:T(4,128)(2,1)S(1)}, u32[]{:S(2)}, u32[]{:S(2)}) collective-permute-start(bf16[4,12288]{1,0:T(4,128)(2,1)S(1)} %add_convert_fusion), channel_id=1, source_target_pairs={{0,12},{1,13},{2,14},{3,15},{4,8},{5,9},{6,10},{7,11},{8,4},{9,5},... | collective-permute-start | bytes 294920 | tf_op jit(solution)/shard_map/ppermute | solution.py:183
  49.9 6.7 %collective-permute-start.20 = (bf16[4,12288]{1,0:T(4,128)(2,1)S(1)}, bf16[4,12288]{1,0:T(4,128)(2,1)S(1)}, u32[]{:S(2)}, u32[]{:S(2)}) collective-permute-start(bf16[4,12288]{1,0:T(4,128)(2,1)S(1)} %add_convert_fusion.1), channel_id=1, source_target_pairs={{0,8},{1,9},{2,10},{3,11},{4,12},{5,13},{6,14},{7,15},{8,0},{9,1},... | collective-permute-start | bytes 294920 | tf_op jit(solution)/shard_map/ppermute | solution.py:183
  50.3 6.3 %collective-permute-start.18 = (bf16[4,12288]{1,0:T(4,128)(2,1)S(1)}, bf16[4,12288]{1,0:T(4,128)(2,1)S(1)}, u32[]{:S(2)}, u32[]{:S(2)}) collective-permute-start(bf16[4,12288]{1,0:T(4,128)(2,1)S(1)} %add_convert_fusion.2), channel_id=1, source_target_pairs={{0,4},{1,5},{2,6},{3,7},{4,0},{5,1},{6,2},{7,3},{8,12},{9,13},{10,... | collective-permute-start | bytes 294920 | tf_op jit(solution)/shard_map/ppermute | solution.py:183

commit v20 on v7

--- a/solution.py
+++ b/solution.py
@@ -257,7 +257,7 @@
         [VMEM] * 2,
         16,
     )(total, got)
-    got = [across(messages[k - 1], k) for k in range(1, groups)]
+    got = [across(messages[k - 1], k) for k in range(groups - 1, 0, -1)]
     part = call(
         functools.partial(part_body, step),
         [shape(rows, width, dtype=f32)],

time: 52.6 us -> 51.7 us (0.983)
  waiting for transfers between devices: 17.2 us -> 15.5 us
  starting transfers between devices: 23.5 us -> 24.2 us
    ppermute x9, waiting for transfers between devices: 11.1 us -> 9.69 us  [across(): return lax.ppermute(x, 'blk', [(i, i ^ 4 * k) for i in range(devices)])]
    ppermute x9, starting transfers between devices: 13.6 us -> 14.4 us  [across(): return lax.ppermute(x, 'blk', [(i, i ^ 4 * k) for i in range(devices)])]
  transfers between devices with their start and end apart: 23 -> 23, of which waited for: 9 -> 7; matrix products, arithmetic and copies ran while one was open for 6% -> 6% of each run, Pallas kernels for 14% -> 14%
where the time goes in v20:
time: 51.7 us; the launch traced here: 51.5 us
  starting transfers between devices  24.2 us (47%)
  waiting for transfers between devices  15.5 us (30%)
  Pallas kernels  8.56 us (17%)
  other arithmetic  2.23 us (4%)
  local copies, waits for them, and re-layouts  0.86 us (2%)
    ppermute x9, starting transfers between devices, across(): return lax.ppermute(x, 'blk', [(i, i ^ 4 * k) for i in range(devices)])  14.4 us
    ppermute x9, waiting for transfers between devices, across(): return lax.ppermute(x, 'blk', [(i, i ^ 4 * k) for i in range(devices)])  9.69 us
    ppermute x9, starting transfers between devices, beside(): return lax.ppermute(x, 'blk', [(i, i ^ 2) for i in range(devices)])  8.72 us
    ppermute x9, waiting for transfers between devices, beside(): return lax.ppermute(x, 'blk', [(i, i ^ 2) for i in range(devices)])  5.79 us
    pallas_call x1, Pallas kernels, shards(): call(functools.partial(load_body, len(near)), [shape(*x.shape, dtype=x.dt...  3.39 us
    pallas_call x1, Pallas kernels, shards(): call(functools.partial(part_body, step), [shape(rows, width, dtype=f32)],...  1.2 us
    pallas_call x1, Pallas kernels, shards(): call(functools.partial(act_body, step), [shape(rows, 2 * block)], [VMEM]...  1.19 us
    ppermute x5, starting transfers between devices, core(): return lax.ppermute(x, 'blk', [(i, i ^ 1) for i in range(devices)])  1.1 us
  transfers between devices with their start and end apart: 23, of which 7 were waited for; matrix products, arithmetic and copies ran while one was open for 6% of the time, Pallas kernels for 14%

profile of v20, /device:TPU:0, one launch (start us, length us, event | category | flops | bytes accessed | tf_op | source)
XLA Modules:
  0.0 51.5 jit_solution(2270883189183488062)
XLA Ops:
  0.0 0.5 collective-permute-start.9
  0.5 2.6 %collective-permute-start.4 = (bf16[4,12288]{1,0:T(4,128)(2,1)}, bf16[4,12288]{1,0:T(4,128)(2,1)S(1)}, u32[]{:S(2)}, u32[]{:S(2)}) collective-permute-start(bf16[4,12288]{1,0:T(4,128)(2,1)} %refs_0_), channel_id=1, source_target_pairs={{0,4},{1,5},{2,6},{3,7},{4,0},{5,1},{6,2},{7,3},{8,12},{9,13},{10,... | collective-permute-start | bytes 294920 | tf_op jit(solution)/shard_map/ppermute | solution.py:183
  3.0 1.5 %collective-permute-start.5 = (bf16[4,12288]{1,0:T(4,128)(2,1)}, bf16[4,12288]{1,0:T(4,128)(2,1)S(1)}, u32[]{:S(2)}, u32[]{:S(2)}) collective-permute-start(bf16[4,12288]{1,0:T(4,128)(2,1)} %refs_0_), channel_id=1, source_target_pairs={{0,2},{1,3},{2,0},{3,1},{4,6},{5,7},{6,4},{7,5},{8,10},{9,11},{10,... | collective-permute-start | bytes 294920 | tf_op jit(solution)/shard_map/ppermute | solution.py:186
  4.5 2.6 %collective-permute-start = (bf16[4,12288]{1,0:T(4,128)(2,1)}, bf16[4,12288]{1,0:T(4,128)(2,1)S(1)}, u32[]{:S(2)}, u32[]{:S(2)}) collective-permute-start(bf16[4,12288]{1,0:T(4,128)(2,1)} %refs_0_), channel_id=1, source_target_pairs={{0,8},{1,9},{2,10},{3,11},{4,12},{5,13},{6,14},{7,15},{8,0},{9,1},... | collective-permute-start | bytes 294920 | tf_op jit(solution)/shard_map/ppermute | solution.py:183
  7.4 0.8 %copy.13 = s32[4,6]{0,1:T(8,128)S(1)} copy(s32[4,6]{1,0:T(4,128)} %param.15) | data formatting | bytes 192 | tf_op args[3]
  8.1 0.7 %fusion.1 = s32[4,6]{0,1:T(8,128)S(1)} fusion(s32[4]{0:T(128)} %param.16), kind=kLoop, calls=%fused_computation.12 | loop fusion | flops 48 | bytes 112 | tf_op jit(solution)/shard_map/convert_element_type | solution.py:150
  8.9 0.7 %fusion = s32[16,16]{1,0:T(8,128)S(1)} fusion(s32[16]{0:T(128)} %param.17), kind=kLoop, calls=%fused_computation.10 | loop fusion | flops 512 | bytes 1088 | tf_op jit(solution)/shard_map/convert_element_type | solution.py:153
  10.6 4.6 %collective-permute-done.refs_2_ = bf16[4,12288]{1,0:T(4,128)(2,1)S(1)} collective-permute-done((bf16[4,12288]{1,0:T(4,128)(2,1)}, bf16[4,12288]{1,0:T(4,128)(2,1)S(1)}, u32[]{:S(2)}, u32[]{:S(2)}) %collective-permute-start) | collective-permute-done | bytes 98336 | tf_op jit(solution)/shard_map/ppermute | solution.py:183
  15.3 0.5 collective-permute-start.7
  15.9 0.7 %collective-permute-start.1 = (bf16[4,12288]{1,0:T(4,128)(2,1)S(1)}, bf16[4,12288]{1,0:T(4,128)(2,1)S(1)}, u32[]{:S(2)}, u32[]{:S(2)}) collective-permute-start(bf16[4,12288]{1,0:T(4,128)(2,1)S(1)} %collective-permute-done.refs_2_), channel_id=1, source_target_pairs={{0,2},{1,3},{2,0},{3,1},{4,6},{5,7},{6,4},{7,5},{8,10},{9,11},{10,... | collective-permute-start | bytes 294920 | tf_op jit(solution)/shard_map/ppermute | solution.py:186
  16.5 1.3 %collective-permute-start.3 = (bf16[4,12288]{1,0:T(4,128)(2,1)S(1)}, bf16[4,12288]{1,0:T(4,128)(2,1)S(1)}, u32[]{:S(2)}, u32[]{:S(2)}) collective-permute-start(bf16[4,12288]{1,0:T(4,128)(2,1)S(1)} %collective-permute-done.2.refs_3_), channel_id=1, source_target_pairs={{0,2},{1,3},{2,0},{3,1},{4,6},{5,7},{6,4},{7,5},{8,10},{9,11},{10,... | collective-permute-start | bytes 294920 | tf_op jit(solution)/shard_map/ppermute | solution.py:186
  17.9 3.4 %shard_map.118 = (bf16[4,12288]{1,0:T(4,128)(2,1)S(1)}, f32[1,12288]{1,0:T(1,128)S(1)}, f32[1,12288]{1,0:T(1,128)S(1)}, bf16[768,512]{1,0:T(8,128)(2,1)S(1)}, bf...) custom-call(bf16[4,12288]{1,0:T(4,128)(2,1)} %refs_0_, ...), custom_call_target="tpu_custom_call" | custom-call | bytes 8388608 | tf_op jit(solution)/shard_map/pallas_call | solution.py:212
  21.3 0.8 %shard_map.119 = (bf16[16,12288]{1,0:T(8,128)(2,1)S(1)}, bf16[8,12288]{1,0:T(8,128)(2,1)S(1)}) custom-call(bf16[4,12288]{1,0:T(4,128)(2,1)S(1)} %get-tuple-element.53.refs_0_, bf16[4,12288]{1,0:T(4,128)(2,1)S(1)} %collective-permute-done.4.refs_1_, bf16[4,12288]{1,0:T(4,128)(2,1)S(1)} %collective-permute-done.refs_2_, ...), custom_call_target="tpu_custom_call" | custom-call | bytes 4194304 | tf_op jit(solution)/shard_map/pallas_call | solution.py:228
  22.1 1.0 %collective-permute-done.3.refs_1_ = bf16[4,12288]{1,0:T(4,128)(2,1)S(1)} collective-permute-done((bf16[4,12288]{1,0:T(4,128)(2,1)S(1)}, bf16[4,12288]{1,0:T(4,128)(2,1)S(1)}, u32[]{:S(2)}, u32[]{:S(2)}) %collective-permute-start.3) | collective-permute-done | bytes 98336 | tf_op jit(solution)/shard_map/ppermute | solution.py:186
  23.1 0.8 %shard_map.120 = (bf16[16,12288]{1,0:T(8,128)(2,1)S(1)}, f32[32,512]{1,0:T(8,128)S(1)}, bf16[32,512]{1,0:T(8,128)(2,1)S(1)}) custom-call(s32[1]{0:T(128)} %bitcast.place, bf16[4,12288]{1,0:T(4,128)(2,1)S(1)} %collective-permute-done.1.refs_0_, bf16[4,12288]{1,0:T(4,128)(2,1)S(1)} %collective-permute-done.3.refs_1_, ...), custom_call_target="tpu_custom_call" | custom-call | bytes 4194304 | tf_op jit(solution)/shard_map/pallas_call | solution.py:236
  23.9 0.7 %collective-permute-start.8 = (bf16[32,512]{1,0:T(8,128)(2,1)S(1)}, bf16[32,512]{1,0:T(8,128)(2,1)S(1)}, u32[]{:S(2)}, u32[]{:S(2)}) collective-permute-start(bf16[32,512]{1,0:T(8,128)(2,1)S(1)} %get-tuple-element.63), channel_id=1, source_target_pairs={{0,2},{1,3},{2,0},{3,1},{4,6},{5,7},{6,4},{7,5},{8,10},{9,11},{10,... | collective-permute-start | bytes 98312 | tf_op jit(solution)/shard_map/ppermute | solution.py:186
  24.6 3.2 %collective-permute-done.8.got = bf16[32,512]{1,0:T(8,128)(2,1)S(1)} collective-permute-done((bf16[32,512]{1,0:T(8,128)(2,1)S(1)}, bf16[32,512]{1,0:T(8,128)(2,1)S(1)}, u32[]{:S(2)}, u32[]{:S(2)}) %collective-permute-start.8) | collective-permute-done | bytes 32800 | tf_op jit(solution)/shard_map/ppermute | solution.py:186
  27.9 3.3 %collective-permute-start.13 = (bf16[32,512]{1,0:T(8,128)(2,1)S(1)}, bf16[32,512]{1,0:T(8,128)(2,1)S(1)}, u32[]{:S(2)}, u32[]{:S(2)}) collective-permute-start(bf16[32,512]{1,0:T(8,128)(2,1)S(1)} %get-tuple-element.74), channel_id=1, source_target_pairs={{0,12},{1,13},{2,14},{3,15},{4,8},{5,9},{6,10},{7,11},{8,4},{9,5},... | collective-permute-start | bytes 98312 | tf_op jit(solution)/shard_map/ppermute | solution.py:183
  31.3 1.0 %collective-permute-start.15 = (bf16[32,512]{1,0:T(8,128)(2,1)S(1)}, bf16[32,512]{1,0:T(8,128)(2,1)S(1)}, u32[]{:S(2)}, u32[]{:S(2)}) collective-permute-start(bf16[32,512]{1,0:T(8,128)(2,1)S(1)} %get-tuple-element.76), channel_id=1, source_target_pairs={{0,4},{1,5},{2,6},{3,7},{4,0},{5,1},{6,2},{7,3},{8,12},{9,13},{10,... | collective-permute-start | bytes 98312 | tf_op jit(solution)/shard_map/ppermute | solution.py:183
  32.3 1.2 %shard_map.122.act = bf16[32,256]{1,0:T(8,128)(2,1)S(1)} custom-call(bf16[16,12288]{1,0:T(8,128)(2,1)S(1)} %get-tuple-element.58.refs_2_.near, bf16[16,12288]{1,0:T(8,128)(2,1)S(1)} %get-tuple-element.67.far, bf16[12288,128]{1,0:T(8,128)(2,1)S(1)} %get-tuple-element.68.w_own, bf16[12288,128]{1,0:T(8,128)(2,1)S(1)} %collective-permute-done.9.w_mate, ...), custom_call_target="tpu_custom_call" | custom-call | bytes 4194304 | tf_op jit(solution)/shard_map/pallas_call | solution.py:246
  33.5 1.2 %shard_map.123.part = f32[32,12288]{1,0:T(8,128)S(1)} custom-call(bf16[32,256]{1,0:T(8,128)(2,1)S(1)} %shard_map.122.act, bf16[128,12288]{1,0:T(8,128)(2,1)S(1)} %get-tuple-element.72.w_own, bf16[128,12288]{1,0:T(8,128)(2,1)S(1)} %collective-permute-done.12.w_mate), custom_call_target="tpu_custom_call" | custom-call | bytes 6291456 | tf_op jit(solution)/shard_map/pallas_call | solution.py:261
  34.7 1.3 %collective-permute-done.14.refs_1_ = bf16[32,512]{1,0:T(8,128)(2,1)S(1)} collective-permute-done((bf16[32,512]{1,0:T(8,128)(2,1)S(1)}, bf16[32,512]{1,0:T(8,128)(2,1)S(1)}, u32[]{:S(2)}, u32[]{:S(2)}) %collective-permute-start.14) | collective-permute-done | bytes 32800 | tf_op jit(solution)/shard_map/ppermute | solution.py:183
  36.5 0.6 %collective-permute-start.21 = (bf16[4,12288]{1,0:T(4,128)(2,1)S(1)}, bf16[4,12288]{1,0:T(4,128)(2,1)S(1)}, u32[]{:S(2)}, u32[]{:S(2)}) collective-permute-start(bf16[4,12288]{1,0:T(4,128)(2,1)S(1)} %get-tuple-element.84), channel_id=1, source_target_pairs={{0,2},{1,3},{2,0},{3,1},{4,6},{5,7},{6,4},{7,5},{8,10},{9,11},{10,... | collective-permute-start | bytes 294920 | tf_op jit(solution)/shard_map/ppermute | solution.py:186
  37.1 1.5 %collective-permute-start.19 = (bf16[4,12288]{1,0:T(4,128)(2,1)S(1)}, bf16[4,12288]{1,0:T(4,128)(2,1)S(1)}, u32[]{:S(2)}, u32[]{:S(2)}) collective-permute-start(bf16[4,12288]{1,0:T(4,128)(2,1)S(1)} %get-tuple-element.82), channel_id=1, source_target_pairs={{0,2},{1,3},{2,0},{3,1},{4,6},{5,7},{6,4},{7,5},{8,10},{9,11},{10,... | collective-permute-start | bytes 294920 | tf_op jit(solution)/shard_map/ppermute | solution.py:186
  38.6 0.6 %collective-permute-start.17 = (bf16[4,12288]{1,0:T(4,128)(2,1)S(1)}, bf16[4,12288]{1,0:T(4,128)(2,1)S(1)}, u32[]{:S(2)}, u32[]{:S(2)}) collective-permute-start(bf16[4,12288]{1,0:T(4,128)(2,1)S(1)} %get-tuple-element.80), channel_id=1, source_target_pairs={{0,2},{1,3},{2,0},{3,1},{4,6},{5,7},{6,4},{7,5},{8,10},{9,11},{10,... | collective-permute-start | bytes 294920 | tf_op jit(solution)/shard_map/ppermute | solution.py:186
  39.1 1.5 %collective-permute-start.16 = (bf16[4,12288]{1,0:T(4,128)(2,1)S(1)}, bf16[4,12288]{1,0:T(4,128)(2,1)S(1)}, u32[]{:S(2)}, u32[]{:S(2)}) collective-permute-start(bf16[4,12288]{1,0:T(4,128)(2,1)S(1)} %get-tuple-element.78), channel_id=1, source_target_pairs={{0,2},{1,3},{2,0},{3,1},{4,6},{5,7},{6,4},{7,5},{8,10},{9,11},{10,... | collective-permute-start | bytes 294920 | tf_op jit(solution)/shard_map/ppermute | solution.py:186
  40.6 1.6 %collective-permute-done.21 = bf16[4,12288]{1,0:T(4,128)(2,1)S(1)} collective-permute-done((bf16[4,12288]{1,0:T(4,128)(2,1)S(1)}, bf16[4,12288]{1,0:T(4,128)(2,1)S(1)}, u32[]{:S(2)}, u32[]{:S(2)}) %collective-permute-start.21) | collective-permute-done | bytes 98336 | tf_op jit(solution)/shard_map/ppermute | solution.py:186
  42.2 2.1 %collective-permute-start.22 = (bf16[4,12288]{1,0:T(4,128)(2,1)S(1)}, bf16[4,12288]{1,0:T(4,128)(2,1)S(1)}, u32[]{:S(2)}, u32[]{:S(2)}) collective-permute-start(bf16[4,12288]{1,0:T(4,128)(2,1)S(1)} %add_convert_fusion), channel_id=1, source_target_pairs={{0,12},{1,13},{2,14},{3,15},{4,8},{5,9},{6,10},{7,11},{8,4},{9,5},... | collective-permute-start | bytes 294920 | tf_op jit(solution)/shard_map/ppermute | solution.py:183
  44.5 2.4 %collective-permute-start.18 = (bf16[4,12288]{1,0:T(4,128)(2,1)S(1)}, bf16[4,12288]{1,0:T(4,128)(2,1)S(1)}, u32[]{:S(2)}, u32[]{:S(2)}) collective-permute-start(bf16[4,12288]{1,0:T(4,128)(2,1)S(1)} %add_convert_fusion.2), channel_id=1, source_target_pairs={{0,4},{1,5},{2,6},{3,7},{4,0},{5,1},{6,2},{7,3},{8,12},{9,13},{10,... | collective-permute-start | bytes 294920 | tf_op jit(solution)/shard_map/ppermute | solution.py:183
  47.0 1.7 %collective-permute-done.22.refs_3_ = bf16[4,12288]{1,0:T(4,128)(2,1)S(1)} collective-permute-done((bf16[4,12288]{1,0:T(4,128)(2,1)S(1)}, bf16[4,12288]{1,0:T(4,128)(2,1)S(1)}, u32[]{:S(2)}, u32[]{:S(2)}) %collective-permute-start.22) | collective-permute-done | bytes 98336 | tf_op jit(solution)/shard_map/ppermute | solution.py:183
  48.7 2.1 %collective-permute-done.20.refs_2_ = bf16[4,12288]{1,0:T(4,128)(2,1)S(1)} collective-permute-done((bf16[4,12288]{1,0:T(4,128)(2,1)S(1)}, bf16[4,12288]{1,0:T(4,128)(2,1)S(1)}, u32[]{:S(2)}, u32[]{:S(2)}) %collective-permute-start.20) | collective-permute-done | bytes 98336 | tf_op jit(solution)/shard_map/ppermute | solution.py:183
  50.8 0.7 %shard_map.125 = bf16[4,12288]{1,0:T(4,128)(2,1)} custom-call(f32[4,12288]{1,0:T(4,128)S(1)} %convert_add_fusion.refs_0_, bf16[4,12288]{1,0:T(4,128)(2,1)S(1)} %collective-permute-done.18.refs_1_, bf16[4,12288]{1,0:T(4,128)(2,1)S(1)} %collective-permute-done.20.refs_2_, bf16[4,12288]{1,0:T(4,128)(2,1)S(1)} %collective-permute-done.22.refs_3_), custom_call_target="tpu_custom_call" | custom-call | bytes 2097152 | tf_op jit(solution)/shard_map/pallas_call | solution.py:282
  (43 shorter events, 2.4 us)
Async XLA Ops:
  0.0 15.2 %collective-permute-start.9 = (bf16[12288,128]{1,0:T(8,128)(2,1)}, bf16[12288,128]{1,0:T(8,128)(2,1)S(1)}, u32[]{:S(2)}, u32[]{:S(2)}) collective-permute-start(bf16[12288,128]{1,0:T(8,128)(2,1)} %refs_4_), channel_id=1, source_target_pairs={{0,1},{1,0},{2,3},{3,2},{4,5},{5,4},{6,7},{7,6},{8,9},{9,8},{10,11... | collective-permute-start | bytes 9437192 | tf_op jit(solution)/shard_map/ppermute | solution.py:189
  0.5 9.8 %collective-permute-start.4 = (bf16[4,12288]{1,0:T(4,128)(2,1)}, bf16[4,12288]{1,0:T(4,128)(2,1)S(1)}, u32[]{:S(2)}, u32[]{:S(2)}) collective-permute-start(bf16[4,12288]{1,0:T(4,128)(2,1)} %refs_0_), channel_id=1, source_target_pairs={{0,4},{1,5},{2,6},{3,7},{4,0},{5,1},{6,2},{7,3},{8,12},{9,13},{10,... | collective-permute-start | bytes 294920 | tf_op jit(solution)/shard_map/ppermute | solution.py:183
  3.0 7.6 %collective-permute-start.5 = (bf16[4,12288]{1,0:T(4,128)(2,1)}, bf16[4,12288]{1,0:T(4,128)(2,1)S(1)}, u32[]{:S(2)}, u32[]{:S(2)}) collective-permute-start(bf16[4,12288]{1,0:T(4,128)(2,1)} %refs_0_), channel_id=1, source_target_pairs={{0,2},{1,3},{2,0},{3,1},{4,6},{5,7},{6,4},{7,5},{8,10},{9,11},{10,... | collective-permute-start | bytes 294920 | tf_op jit(solution)/shard_map/ppermute | solution.py:186
  4.5 10.6 %collective-permute-start = (bf16[4,12288]{1,0:T(4,128)(2,1)}, bf16[4,12288]{1,0:T(4,128)(2,1)S(1)}, u32[]{:S(2)}, u32[]{:S(2)}) collective-permute-start(bf16[4,12288]{1,0:T(4,128)(2,1)} %refs_0_), channel_id=1, source_target_pairs={{0,8},{1,9},{2,10},{3,11},{4,12},{5,13},{6,14},{7,15},{8,0},{9,1},... | collective-permute-start | bytes 294920 | tf_op jit(solution)/shard_map/ppermute | solution.py:183
  7.1 8.0 %collective-permute-start.2 = (bf16[4,12288]{1,0:T(4,128)(2,1)}, bf16[4,12288]{1,0:T(4,128)(2,1)S(1)}, u32[]{:S(2)}, u32[]{:S(2)}) collective-permute-start(bf16[4,12288]{1,0:T(4,128)(2,1)} %refs_0_), channel_id=1, source_target_pairs={{0,12},{1,13},{2,14},{3,15},{4,8},{5,9},{6,10},{7,11},{8,4},{9,5},... | collective-permute-start | bytes 294920 | tf_op jit(solution)/shard_map/ppermute | solution.py:183
  10.3 4.9 %collective-permute-start.6 = (bf16[4,12288]{1,0:T(4,128)(2,1)S(1)}, bf16[4,12288]{1,0:T(4,128)(2,1)S(1)}, u32[]{:S(2)}, u32[]{:S(2)}) collective-permute-start(bf16[4,12288]{1,0:T(4,128)(2,1)S(1)} %collective-permute-done.4.refs_1_), channel_id=1, source_target_pairs={{0,2},{1,3},{2,0},{3,1},{4,6},{5,7},{6,4},{7,5},{8,10},{9,11},{10,... | collective-permute-start | bytes 294920 | tf_op jit(solution)/shard_map/ppermute | solution.py:186
  15.2 18.3 %collective-permute-start.12 = (bf16[128,12288]{1,0:T(8,128)(2,1)}, bf16[128,12288]{1,0:T(8,128)(2,1)S(1)}, u32[]{:S(2)}, u32[]{:S(2)}) collective-permute-start(bf16[128,12288]{1,0:T(8,128)(2,1)} %refs_5_), channel_id=1, source_target_pairs={{0,1},{1,0},{2,3},{3,2},{4,5},{5,4},{6,7},{7,6},{8,9},{9,8},{10,11... | collective-permute-start | bytes 9437192 | tf_op jit(solution)/shard_map/ppermute | solution.py:189
  15.3 7.8 %collective-permute-start.7 = (bf16[768,512]{1,0:T(8,128)(2,1)}, bf16[768,512]{1,0:T(8,128)(2,1)S(1)}, u32[]{:S(2)}, u32[]{:S(2)}) collective-permute-start(bf16[768,512]{1,0:T(8,128)(2,1)} %refs_3_), channel_id=1, source_target_pairs={{0,1},{1,0},{2,3},{3,2},{4,5},{5,4},{6,7},{7,6},{8,9},{9,8},{10,11... | collective-permute-start | bytes 2359304 | tf_op jit(solution)/shard_map/ppermute | solution.py:189
  15.8 20.3 %collective-permute-start.10 = (bf16[512,768]{1,0:T(8,128)(2,1)}, bf16[512,768]{1,0:T(8,128)(2,1)S(1)}, u32[]{:S(2)}, u32[]{:S(2)}) collective-permute-start(bf16[512,768]{1,0:T(8,128)(2,1)} %refs_6_), channel_id=1, source_target_pairs={{0,1},{1,0},{2,3},{3,2},{4,5},{5,4},{6,7},{7,6},{8,9},{9,8},{10,11... | collective-permute-start | bytes 2359304 | tf_op jit(solution)/shard_map/ppermute | solution.py:189
  15.9 6.3 %collective-permute-start.1 = (bf16[4,12288]{1,0:T(4,128)(2,1)S(1)}, bf16[4,12288]{1,0:T(4,128)(2,1)S(1)}, u32[]{:S(2)}, u32[]{:S(2)}) collective-permute-start(bf16[4,12288]{1,0:T(4,128)(2,1)S(1)} %collective-permute-done.refs_2_), channel_id=1, source_target_pairs={{0,2},{1,3},{2,0},{3,1},{4,6},{5,7},{6,4},{7,5},{8,10},{9,11},{10,... | collective-permute-start | bytes 294920 | tf_op jit(solution)/shard_map/ppermute | solution.py:186
  16.5 6.6 %collective-permute-start.3 = (bf16[4,12288]{1,0:T(4,128)(2,1)S(1)}, bf16[4,12288]{1,0:T(4,128)(2,1)S(1)}, u32[]{:S(2)}, u32[]{:S(2)}) collective-permute-start(bf16[4,12288]{1,0:T(4,128)(2,1)S(1)} %collective-permute-done.2.refs_3_), channel_id=1, source_target_pairs={{0,2},{1,3},{2,0},{3,1},{4,6},{5,7},{6,4},{7,5},{8,10},{9,11},{10,... | collective-permute-start | bytes 294920 | tf_op jit(solution)/shard_map/ppermute | solution.py:186
  21.3 3.3 %copy-start.1 = (f32[128]{0:T(128)S(1)}, f32[128]{0:T(128)}, u32[]{:S(2)}) copy-start(f32[128]{0:T(128)} %param.19) | copy-start | bytes 1540
  23.9 3.9 %collective-permute-start.8 = (bf16[32,512]{1,0:T(8,128)(2,1)S(1)}, bf16[32,512]{1,0:T(8,128)(2,1)S(1)}, u32[]{:S(2)}, u32[]{:S(2)}) collective-permute-start(bf16[32,512]{1,0:T(8,128)(2,1)S(1)} %get-tuple-element.63), channel_id=1, source_target_pairs={{0,2},{1,3},{2,0},{3,1},{4,6},{5,7},{6,4},{7,5},{8,10},{9,11},{10,... | collective-permute-start | bytes 98312 | tf_op jit(solution)/shard_map/ppermute | solution.py:186
  24.6 6.7 %collective-permute-start.11 = (f32[1,128]{1,0:T(1,128)S(1)}, f32[1,128]{1,0:T(1,128)S(1)}, u32[]{:S(2)}, u32[]{:S(2)}) collective-permute-start(f32[1,128]{1,0:T(1,128)S(1)} %bitcast.12), channel_id=1, source_target_pairs={{0,1},{1,0},{2,3},{3,2},{4,5},{5,4},{6,7},{7,6},{8,9},{9,8},{10,11... | collective-permute-start | bytes 1544 | tf_op jit(solution)/shard_map/ppermute | solution.py:189
  27.9 6.9 %collective-permute-start.13 = (bf16[32,512]{1,0:T(8,128)(2,1)S(1)}, bf16[32,512]{1,0:T(8,128)(2,1)S(1)}, u32[]{:S(2)}, u32[]{:S(2)}) collective-permute-start(bf16[32,512]{1,0:T(8,128)(2,1)S(1)} %get-tuple-element.74), channel_id=1, source_target_pairs={{0,12},{1,13},{2,14},{3,15},{4,8},{5,9},{6,10},{7,11},{8,4},{9,5},... | collective-permute-start | bytes 98312 | tf_op jit(solution)/shard_map/ppermute | solution.py:183
  31.2 4.8 %collective-permute-start.14 = (bf16[32,512]{1,0:T(8,128)(2,1)S(1)}, bf16[32,512]{1,0:T(8,128)(2,1)S(1)}, u32[]{:S(2)}, u32[]{:S(2)}) collective-permute-start(bf16[32,512]{1,0:T(8,128)(2,1)S(1)} %get-tuple-element.75), channel_id=1, source_target_pairs={{0,8},{1,9},{2,10},{3,11},{4,12},{5,13},{6,14},{7,15},{8,0},{9,1},... | collective-permute-start | bytes 98312 | tf_op jit(solution)/shard_map/ppermute | solution.py:183
  31.3 4.7 %collective-permute-start.15 = (bf16[32,512]{1,0:T(8,128)(2,1)S(1)}, bf16[32,512]{1,0:T(8,128)(2,1)S(1)}, u32[]{:S(2)}, u32[]{:S(2)}) collective-permute-start(bf16[32,512]{1,0:T(8,128)(2,1)S(1)} %get-tuple-element.76), channel_id=1, source_target_pairs={{0,4},{1,5},{2,6},{3,7},{4,0},{5,1},{6,2},{7,3},{8,12},{9,13},{10,... | collective-permute-start | bytes 98312 | tf_op jit(solution)/shard_map/ppermute | solution.py:183
  33.5 2.5 %copy-start = (f32[512]{0:T(512)S(1)}, f32[512]{0:T(512)}, u32[]{:S(2)}) copy-start(f32[512]{0:T(512)} %param.22) | copy-start | bytes 6148
  36.5 5.7 %collective-permute-start.21 = (bf16[4,12288]{1,0:T(4,128)(2,1)S(1)}, bf16[4,12288]{1,0:T(4,128)(2,1)S(1)}, u32[]{:S(2)}, u32[]{:S(2)}) collective-permute-start(bf16[4,12288]{1,0:T(4,128)(2,1)S(1)} %get-tuple-element.84), channel_id=1, source_target_pairs={{0,2},{1,3},{2,0},{3,1},{4,6},{5,7},{6,4},{7,5},{8,10},{9,11},{10,... | collective-permute-start | bytes 294920 | tf_op jit(solution)/shard_map/ppermute | solution.py:186
  37.1 7.2 %collective-permute-start.19 = (bf16[4,12288]{1,0:T(4,128)(2,1)S(1)}, bf16[4,12288]{1,0:T(4,128)(2,1)S(1)}, u32[]{:S(2)}, u32[]{:S(2)}) collective-permute-start(bf16[4,12288]{1,0:T(4,128)(2,1)S(1)} %get-tuple-element.82), channel_id=1, source_target_pairs={{0,2},{1,3},{2,0},{3,1},{4,6},{5,7},{6,4},{7,5},{8,10},{9,11},{10,... | collective-permute-start | bytes 294920 | tf_op jit(solution)/shard_map/ppermute | solution.py:186
  38.6 5.9 %collective-permute-start.17 = (bf16[4,12288]{1,0:T(4,128)(2,1)S(1)}, bf16[4,12288]{1,0:T(4,128)(2,1)S(1)}, u32[]{:S(2)}, u32[]{:S(2)}) collective-permute-start(bf16[4,12288]{1,0:T(4,128)(2,1)S(1)} %get-tuple-element.80), channel_id=1, source_target_pairs={{0,2},{1,3},{2,0},{3,1},{4,6},{5,7},{6,4},{7,5},{8,10},{9,11},{10,... | collective-permute-start | bytes 294920 | tf_op jit(solution)/shard_map/ppermute | solution.py:186
  39.1 7.8 %collective-permute-start.16 = (bf16[4,12288]{1,0:T(4,128)(2,1)S(1)}, bf16[4,12288]{1,0:T(4,128)(2,1)S(1)}, u32[]{:S(2)}, u32[]{:S(2)}) collective-permute-start(bf16[4,12288]{1,0:T(4,128)(2,1)S(1)} %get-tuple-element.78), channel_id=1, source_target_pairs={{0,2},{1,3},{2,0},{3,1},{4,6},{5,7},{6,4},{7,5},{8,10},{9,11},{10,... | collective-permute-start | bytes 294920 | tf_op jit(solution)/shard_map/ppermute | solution.py:186
  42.2 6.5 %collective-permute-start.22 = (bf16[4,12288]{1,0:T(4,128)(2,1)S(1)}, bf16[4,12288]{1,0:T(4,128)(2,1)S(1)}, u32[]{:S(2)}, u32[]{:S(2)}) collective-permute-start(bf16[4,12288]{1,0:T(4,128)(2,1)S(1)} %add_convert_fusion), channel_id=1, source_target_pairs={{0,12},{1,13},{2,14},{3,15},{4,8},{5,9},{6,10},{7,11},{8,4},{9,5},... | collective-permute-start | bytes 294920 | tf_op jit(solution)/shard_map/ppermute | solution.py:183
  44.4 6.5 %collective-permute-start.20 = (bf16[4,12288]{1,0:T(4,128)(2,1)S(1)}, bf16[4,12288]{1,0:T(4,128)(2,1)S(1)}, u32[]{:S(2)}, u32[]{:S(2)}) collective-permute-start(bf16[4,12288]{1,0:T(4,128)(2,1)S(1)} %add_convert_fusion.1), channel_id=1, source_target_pairs={{0,8},{1,9},{2,10},{3,11},{4,12},{5,13},{6,14},{7,15},{8,0},{9,1},... | collective-permute-start | bytes 294920 | tf_op jit(solution)/shard_map/ppermute | solution.py:183
  44.5 6.3 %collective-permute-start.18 = (bf16[4,12288]{1,0:T(4,128)(2,1)S(1)}, bf16[4,12288]{1,0:T(4,128)(2,1)S(1)}, u32[]{:S(2)}, u32[]{:S(2)}) collective-permute-start(bf16[4,12288]{1,0:T(4,128)(2,1)S(1)} %add_convert_fusion.2), channel_id=1, source_target_pairs={{0,4},{1,5},{2,6},{3,7},{4,0},{5,1},{6,2},{7,3},{8,12},{9,13},{10,... | collective-permute-start | bytes 294920 | tf_op jit(solution)/shard_map/ppermute | solution.py:183

commit v21 on v18

--- a/solution.py
+++ b/solution.py
@@ -194,6 +194,10 @@
     gain, shift, bias = ln_gain.reshape(1, width), ln_shift.reshape(1, width), b_in.reshape(1, block)
     span = 2 * share
 
+    held = [hidden] + [across(hidden, k) for k in range(1, groups)]
+    w_in_mate = core(w_in)
+    held[1], lists, counts, block_slot = lax.optimization_barrier((held[1], lists, counts, block_slot))
+
     table = activity(lists, counts, block_slot)
     by = plane ^ jnp.arange(groups)
     at = position ^ jnp.arange(2)
@@ -202,9 +206,7 @@
     live = jnp.sum(jnp.where(relate & choose, table[None, None], 0), axis=(2, 3)).astype(f32)
     mask = jnp.broadcast_to(live[None, :, None, :, None], (2, groups, row_dev, 2, block)).reshape(rows, 2 * block)
 
-    held = [hidden] + [across(hidden, k) for k in range(1, groups)]
-    w_in_mate = core(w_in)
-    held[1], low_in_sent, mask = lax.optimization_barrier((held[1], low_in, mask))
+    low_in_sent, mask = lax.optimization_barrier((low_in, mask))
     low_in_mate = core(low_in_sent)
     early, bias_mate = lax.optimization_barrier((hidden, core(bias)))
     beyond = [beside(h) for h in [early] + held[1:]]

time: 52.6 us -> 51.1 us (0.971)
  waiting for transfers between devices: 15.3 us -> 13.9 us
    ppermute x9, waiting for transfers between devices: 9.67 us -> 5.61 us  [beside(): return lax.ppermute(x, 'blk', [(i, i ^ 2) for i in range(devices)])]
    ppermute x9, waiting for transfers between devices: 5.59 us -> 7.24 us  [across(): return lax.ppermute(x, 'blk', [(i, i ^ 4 * k) for i in range(devices)])]
    ppermute x5, waiting for transfers between devices: 0.01 us -> 1.1 us  [core(): return lax.ppermute(x, 'blk', [(i, i ^ 1) for i in range(devices)])]
    optimization_barrier x0 -> x1, local copies, waits for them, and re-layouts: none -> 0.77 us  [shards(): lax.optimization_barrier((held[1], lists, counts, block_slot))]
    unnamed x6 -> x5, local copies, waits for them, and re-layouts: 0.79 us -> 0.02 us
  transfers between devices with their start and end apart: 23 -> 23, of which waited for: 8 -> 10; matrix products, arithmetic and copies ran while one was open for 6% -> 6% of each run, Pallas kernels for 14% -> 15%
where the time goes in v21:
time: 51.1 us; the launch traced here: 50.9 us
  starting transfers between devices  25.2 us (49%)
  waiting for transfers between devices  13.9 us (27%)
  Pallas kernels  8.57 us (17%)
  other arithmetic  2.23 us (4%)
  local copies, waits for them, and re-layouts  0.86 us (2%)
    ppermute x9, starting transfers between devices, across(): return lax.ppermute(x, 'blk', [(i, i ^ 4 * k) for i in range(devices)])  14.3 us
    ppermute x9, starting transfers between devices, beside(): return lax.ppermute(x, 'blk', [(i, i ^ 2) for i in range(devices)])  9.93 us
    ppermute x9, waiting for transfers between devices, across(): return lax.ppermute(x, 'blk', [(i, i ^ 4 * k) for i in range(devices)])  7.24 us
    ppermute x9, waiting for transfers between devices, beside(): return lax.ppermute(x, 'blk', [(i, i ^ 2) for i in range(devices)])  5.61 us
    pallas_call x1, Pallas kernels, shards(): call(functools.partial(load_body, len(near)), [shape(*x.shape, dtype=x.dt...  3.39 us
    pallas_call x1, Pallas kernels, shards(): call(functools.partial(act_body, step), [shape(rows, 2 * block)], [VMEM]...  1.21 us
    pallas_call x1, Pallas kernels, shards(): call(functools.partial(part_body, step), [shape(rows, width, dtype=f32)],...  1.19 us
    ppermute x5, waiting for transfers between devices, core(): return lax.ppermute(x, 'blk', [(i, i ^ 1) for i in range(devices)])  1.1 us
  transfers between devices with their start and end apart: 23, of which 10 were waited for; matrix products, arithmetic and copies ran while one was open for 6% of the time, Pallas kernels for 15%

profile of v21, /device:TPU:0, one launch (start us, length us, event | category | flops | bytes accessed | tf_op | source)
XLA Modules:
  0.0 50.9 jit_solution(4326677886285336367)
XLA Ops:
  0.5 2.6 %collective-permute-start.4 = (bf16[4,12288]{1,0:T(4,128)(2,1)}, bf16[4,12288]{1,0:T(4,128)(2,1)S(1)}, u32[]{:S(2)}, u32[]{:S(2)}) collective-permute-start(bf16[4,12288]{1,0:T(4,128)(2,1)} %refs_0_), channel_id=1, source_target_pairs={{0,4},{1,5},{2,6},{3,7},{4,0},{5,1},{6,2},{7,3},{8,12},{9,13},{10,... | collective-permute-start | bytes 294920 | tf_op jit(solution)/shard_map/ppermute | solution.py:183
  3.0 2.6 %collective-permute-start = (bf16[4,12288]{1,0:T(4,128)(2,1)}, bf16[4,12288]{1,0:T(4,128)(2,1)S(1)}, u32[]{:S(2)}, u32[]{:S(2)}) collective-permute-start(bf16[4,12288]{1,0:T(4,128)(2,1)} %refs_0_), channel_id=1, source_target_pairs={{0,8},{1,9},{2,10},{3,11},{4,12},{5,13},{6,14},{7,15},{8,0},{9,1},... | collective-permute-start | bytes 294920 | tf_op jit(solution)/shard_map/ppermute | solution.py:183
  5.8 1.1 %collective-permute-done.5.b_mate = f32[1,128]{1,0:T(1,128)S(1)} collective-permute-done((f32[1,128]{1,0:T(1,128)}, f32[1,128]{1,0:T(1,128)S(1)}, u32[]{:S(2)}, u32[]{:S(2)}) %collective-permute-start.5) | collective-permute-done | bytes 544 | tf_op jit(solution)/shard_map/ppermute | solution.py:189
  6.9 2.0 %collective-permute-start.6 = (bf16[4,12288]{1,0:T(4,128)(2,1)}, bf16[4,12288]{1,0:T(4,128)(2,1)S(1)}, u32[]{:S(2)}, u32[]{:S(2)}) collective-permute-start(bf16[4,12288]{1,0:T(4,128)(2,1)} %refs_0_), channel_id=1, source_target_pairs={{0,2},{1,3},{2,0},{3,1},{4,6},{5,7},{6,4},{7,5},{8,10},{9,11},{10,... | collective-permute-start | bytes 294920 | tf_op jit(solution)/shard_map/ppermute | solution.py:186
  8.8 0.8 %copy.13 = s32[4,6]{0,1:T(8,128)S(1)} copy(s32[4,6]{1,0:T(4,128)} %param.15) | data formatting | bytes 192 | tf_op jit(solution)/shard_map/optimization_barrier | solution.py:199
  9.7 0.7 %fusion.1 = s32[4,6]{0,1:T(8,128)S(1)} fusion(s32[4]{0:T(128)} %param.16), kind=kLoop, calls=%fused_computation.12 | loop fusion | flops 48 | bytes 112 | tf_op jit(solution)/shard_map/convert_element_type | solution.py:150
  10.4 0.7 %fusion = s32[16,16]{1,0:T(8,128)S(1)} fusion(s32[16]{0:T(128)} %param.17), kind=kLoop, calls=%fused_computation.10 | loop fusion | flops 512 | bytes 1088 | tf_op jit(solution)/shard_map/convert_element_type | solution.py:153
  11.6 0.7 %collective-permute-done.6.refs_4_ = bf16[4,12288]{1,0:T(4,128)(2,1)S(1)} collective-permute-done((bf16[4,12288]{1,0:T(4,128)(2,1)}, bf16[4,12288]{1,0:T(4,128)(2,1)S(1)}, u32[]{:S(2)}, u32[]{:S(2)}) %collective-permute-start.6) | collective-permute-done | bytes 98336 | tf_op jit(solution)/shard_map/ppermute | solution.py:186
  12.3 1.7 %collective-permute-done.refs_2_ = bf16[4,12288]{1,0:T(4,128)(2,1)S(1)} collective-permute-done((bf16[4,12288]{1,0:T(4,128)(2,1)}, bf16[4,12288]{1,0:T(4,128)(2,1)S(1)}, u32[]{:S(2)}, u32[]{:S(2)}) %collective-permute-start) | collective-permute-done | bytes 98336 | tf_op jit(solution)/shard_map/ppermute | solution.py:183
  14.3 0.5 collective-permute-start.8
  14.8 1.7 %collective-permute-start.1 = (bf16[4,12288]{1,0:T(4,128)(2,1)S(1)}, bf16[4,12288]{1,0:T(4,128)(2,1)S(1)}, u32[]{:S(2)}, u32[]{:S(2)}) collective-permute-start(bf16[4,12288]{1,0:T(4,128)(2,1)S(1)} %collective-permute-done.refs_2_), channel_id=1, source_target_pairs={{0,2},{1,3},{2,0},{3,1},{4,6},{5,7},{6,4},{7,5},{8,10},{9,11},{10,... | collective-permute-start | bytes 294920 | tf_op jit(solution)/shard_map/ppermute | solution.py:186
  16.8 3.4 %shard_map.118 = (bf16[4,12288]{1,0:T(4,128)(2,1)S(1)}, f32[1,12288]{1,0:T(1,128)S(1)}, f32[1,12288]{1,0:T(1,128)S(1)}, bf16[768,512]{1,0:T(8,128)(2,1)S(1)}, bf...) custom-call(bf16[4,12288]{1,0:T(4,128)(2,1)} %refs_0_, ...), custom_call_target="tpu_custom_call" | custom-call | bytes 8388608 | tf_op jit(solution)/shard_map/pallas_call | solution.py:215
  20.2 0.8 %shard_map.119 = (bf16[16,12288]{1,0:T(8,128)(2,1)S(1)}, bf16[8,12288]{1,0:T(8,128)(2,1)S(1)}) custom-call(bf16[4,12288]{1,0:T(4,128)(2,1)S(1)} %get-tuple-element.61.refs_0_, bf16[4,12288]{1,0:T(4,128)(2,1)S(1)} %collective-permute-done.4.refs_1_, bf16[4,12288]{1,0:T(4,128)(2,1)S(1)} %collective-permute-done.refs_2_, ...), custom_call_target="tpu_custom_call" | custom-call | bytes 4194304 | tf_op jit(solution)/shard_map/pallas_call | solution.py:231
  21.0 1.0 %collective-permute-done.3.refs_1_ = bf16[4,12288]{1,0:T(4,128)(2,1)S(1)} collective-permute-done((bf16[4,12288]{1,0:T(4,128)(2,1)S(1)}, bf16[4,12288]{1,0:T(4,128)(2,1)S(1)}, u32[]{:S(2)}, u32[]{:S(2)}) %collective-permute-start.3) | collective-permute-done | bytes 98336 | tf_op jit(solution)/shard_map/ppermute | solution.py:186
  22.1 0.8 %shard_map.120 = (bf16[16,12288]{1,0:T(8,128)(2,1)S(1)}, f32[32,512]{1,0:T(8,128)S(1)}, bf16[32,512]{1,0:T(8,128)(2,1)S(1)}) custom-call(s32[1]{0:T(128)} %bitcast.place, bf16[4,12288]{1,0:T(4,128)(2,1)S(1)} %collective-permute-done.1.refs_0_, bf16[4,12288]{1,0:T(4,128)(2,1)S(1)} %collective-permute-done.3.refs_1_, ...), custom_call_target="tpu_custom_call" | custom-call | bytes 4194304 | tf_op jit(solution)/shard_map/pallas_call | solution.py:239
  22.9 1.8 %collective-permute-start.9 = (bf16[32,512]{1,0:T(8,128)(2,1)S(1)}, bf16[32,512]{1,0:T(8,128)(2,1)S(1)}, u32[]{:S(2)}, u32[]{:S(2)}) collective-permute-start(bf16[32,512]{1,0:T(8,128)(2,1)S(1)} %get-tuple-element.71), channel_id=1, source_target_pairs={{0,2},{1,3},{2,0},{3,1},{4,6},{5,7},{6,4},{7,5},{8,10},{9,11},{10,... | collective-permute-start | bytes 98312 | tf_op jit(solution)/shard_map/ppermute | solution.py:186
  24.6 2.2 %collective-permute-done.9.got = bf16[32,512]{1,0:T(8,128)(2,1)S(1)} collective-permute-done((bf16[32,512]{1,0:T(8,128)(2,1)S(1)}, bf16[32,512]{1,0:T(8,128)(2,1)S(1)}, u32[]{:S(2)}, u32[]{:S(2)}) %collective-permute-start.9) | collective-permute-done | bytes 32800 | tf_op jit(solution)/shard_map/ppermute | solution.py:186
  26.8 3.9 %collective-permute-start.13 = (bf16[32,512]{1,0:T(8,128)(2,1)S(1)}, bf16[32,512]{1,0:T(8,128)(2,1)S(1)}, u32[]{:S(2)}, u32[]{:S(2)}) collective-permute-start(bf16[32,512]{1,0:T(8,128)(2,1)S(1)} %get-tuple-element.82), channel_id=1, source_target_pairs={{0,12},{1,13},{2,14},{3,15},{4,8},{5,9},{6,10},{7,11},{8,4},{9,5},... | collective-permute-start | bytes 98312 | tf_op jit(solution)/shard_map/ppermute | solution.py:183
  30.7 0.6 %collective-permute-start.15 = (bf16[32,512]{1,0:T(8,128)(2,1)S(1)}, bf16[32,512]{1,0:T(8,128)(2,1)S(1)}, u32[]{:S(2)}, u32[]{:S(2)}) collective-permute-start(bf16[32,512]{1,0:T(8,128)(2,1)S(1)} %get-tuple-element.84), channel_id=1, source_target_pairs={{0,4},{1,5},{2,6},{3,7},{4,0},{5,1},{6,2},{7,3},{8,12},{9,13},{10,... | collective-permute-start | bytes 98312 | tf_op jit(solution)/shard_map/ppermute | solution.py:183
  31.4 1.2 %shard_map.122.act = bf16[32,256]{1,0:T(8,128)(2,1)S(1)} custom-call(bf16[16,12288]{1,0:T(8,128)(2,1)S(1)} %get-tuple-element.66.refs_2_.near, bf16[16,12288]{1,0:T(8,128)(2,1)S(1)} %get-tuple-element.75.far, bf16[12288,128]{1,0:T(8,128)(2,1)S(1)} %get-tuple-element.76.w_own, bf16[12288,128]{1,0:T(8,128)(2,1)S(1)} %collective-permute-done.10.w_mate, ...), custom_call_target="tpu_custom_call" | custom-call | bytes 4194304 | tf_op jit(solution)/shard_map/pallas_call | solution.py:249
  32.6 1.2 %shard_map.123.part = f32[32,12288]{1,0:T(8,128)S(1)} custom-call(bf16[32,256]{1,0:T(8,128)(2,1)S(1)} %shard_map.122.act, bf16[128,12288]{1,0:T(8,128)(2,1)S(1)} %get-tuple-element.80.w_own, bf16[128,12288]{1,0:T(8,128)(2,1)S(1)} %collective-permute-done.12.w_mate), custom_call_target="tpu_custom_call" | custom-call | bytes 6291456 | tf_op jit(solution)/shard_map/pallas_call | solution.py:264
  33.8 1.7 %collective-permute-done.14.refs_1_ = bf16[32,512]{1,0:T(8,128)(2,1)S(1)} collective-permute-done((bf16[32,512]{1,0:T(8,128)(2,1)S(1)}, bf16[32,512]{1,0:T(8,128)(2,1)S(1)}, u32[]{:S(2)}, u32[]{:S(2)}) %collective-permute-start.14) | collective-permute-done | bytes 32800 | tf_op jit(solution)/shard_map/ppermute | solution.py:183
  36.0 1.6 %collective-permute-start.21 = (bf16[4,12288]{1,0:T(4,128)(2,1)S(1)}, bf16[4,12288]{1,0:T(4,128)(2,1)S(1)}, u32[]{:S(2)}, u32[]{:S(2)}) collective-permute-start(bf16[4,12288]{1,0:T(4,128)(2,1)S(1)} %get-tuple-element.92), channel_id=1, source_target_pairs={{0,2},{1,3},{2,0},{3,1},{4,6},{5,7},{6,4},{7,5},{8,10},{9,11},{10,... | collective-permute-start | bytes 294920 | tf_op jit(solution)/shard_map/ppermute | solution.py:186
  37.6 0.5 %collective-permute-start.19 = (bf16[4,12288]{1,0:T(4,128)(2,1)S(1)}, bf16[4,12288]{1,0:T(4,128)(2,1)S(1)}, u32[]{:S(2)}, u32[]{:S(2)}) collective-permute-start(bf16[4,12288]{1,0:T(4,128)(2,1)S(1)} %get-tuple-element.90), channel_id=1, source_target_pairs={{0,2},{1,3},{2,0},{3,1},{4,6},{5,7},{6,4},{7,5},{8,10},{9,11},{10,... | collective-permute-start | bytes 294920 | tf_op jit(solution)/shard_map/ppermute | solution.py:186
  38.1 1.5 %collective-permute-start.17 = (bf16[4,12288]{1,0:T(4,128)(2,1)S(1)}, bf16[4,12288]{1,0:T(4,128)(2,1)S(1)}, u32[]{:S(2)}, u32[]{:S(2)}) collective-permute-start(bf16[4,12288]{1,0:T(4,128)(2,1)S(1)} %get-tuple-element.88), channel_id=1, source_target_pairs={{0,2},{1,3},{2,0},{3,1},{4,6},{5,7},{6,4},{7,5},{8,10},{9,11},{10,... | collective-permute-start | bytes 294920 | tf_op jit(solution)/shard_map/ppermute | solution.py:186
  39.6 0.5 %collective-permute-start.16 = (bf16[4,12288]{1,0:T(4,128)(2,1)S(1)}, bf16[4,12288]{1,0:T(4,128)(2,1)S(1)}, u32[]{:S(2)}, u32[]{:S(2)}) collective-permute-start(bf16[4,12288]{1,0:T(4,128)(2,1)S(1)} %get-tuple-element.86), channel_id=1, source_target_pairs={{0,2},{1,3},{2,0},{3,1},{4,6},{5,7},{6,4},{7,5},{8,10},{9,11},{10,... | collective-permute-start | bytes 294920 | tf_op jit(solution)/shard_map/ppermute | solution.py:186
  40.1 1.5 %collective-permute-done.21 = bf16[4,12288]{1,0:T(4,128)(2,1)S(1)} collective-permute-done((bf16[4,12288]{1,0:T(4,128)(2,1)S(1)}, bf16[4,12288]{1,0:T(4,128)(2,1)S(1)}, u32[]{:S(2)}, u32[]{:S(2)}) %collective-permute-start.21) | collective-permute-done | bytes 98336 | tf_op jit(solution)/shard_map/ppermute | solution.py:186
  41.6 2.3 %collective-permute-start.22 = (bf16[4,12288]{1,0:T(4,128)(2,1)S(1)}, bf16[4,12288]{1,0:T(4,128)(2,1)S(1)}, u32[]{:S(2)}, u32[]{:S(2)}) collective-permute-start(bf16[4,12288]{1,0:T(4,128)(2,1)S(1)} %add_convert_fusion), channel_id=1, source_target_pairs={{0,12},{1,13},{2,14},{3,15},{4,8},{5,9},{6,10},{7,11},{8,4},{9,5},... | collective-permute-start | bytes 294920 | tf_op jit(solution)/shard_map/ppermute | solution.py:183
  44.4 1.9 %collective-permute-start.18 = (bf16[4,12288]{1,0:T(4,128)(2,1)S(1)}, bf16[4,12288]{1,0:T(4,128)(2,1)S(1)}, u32[]{:S(2)}, u32[]{:S(2)}) collective-permute-start(bf16[4,12288]{1,0:T(4,128)(2,1)S(1)} %add_convert_fusion.2), channel_id=1, source_target_pairs={{0,4},{1,5},{2,6},{3,7},{4,0},{5,1},{6,2},{7,3},{8,12},{9,13},{10,... | collective-permute-start | bytes 294920 | tf_op jit(solution)/shard_map/ppermute | solution.py:183
  46.4 1.7 %collective-permute-done.22.refs_3_ = bf16[4,12288]{1,0:T(4,128)(2,1)S(1)} collective-permute-done((bf16[4,12288]{1,0:T(4,128)(2,1)S(1)}, bf16[4,12288]{1,0:T(4,128)(2,1)S(1)}, u32[]{:S(2)}, u32[]{:S(2)}) %collective-permute-start.22) | collective-permute-done | bytes 98336 | tf_op jit(solution)/shard_map/ppermute | solution.py:183
  48.1 2.1 %collective-permute-done.20.refs_2_ = bf16[4,12288]{1,0:T(4,128)(2,1)S(1)} collective-permute-done((bf16[4,12288]{1,0:T(4,128)(2,1)S(1)}, bf16[4,12288]{1,0:T(4,128)(2,1)S(1)}, u32[]{:S(2)}, u32[]{:S(2)}) %collective-permute-start.20) | collective-permute-done | bytes 98336 | tf_op jit(solution)/shard_map/ppermute | solution.py:183
  50.2 0.7 %shard_map.125 = bf16[4,12288]{1,0:T(4,128)(2,1)} custom-call(f32[4,12288]{1,0:T(4,128)S(1)} %convert_add_fusion.refs_0_, bf16[4,12288]{1,0:T(4,128)(2,1)S(1)} %collective-permute-done.18.refs_1_, bf16[4,12288]{1,0:T(4,128)(2,1)S(1)} %collective-permute-done.20.refs_2_, bf16[4,12288]{1,0:T(4,128)(2,1)S(1)} %collective-permute-done.22.refs_3_), custom_call_target="tpu_custom_call" | custom-call | bytes 2097152 | tf_op jit(solution)/shard_map/pallas_call | solution.py:285
  (43 shorter events, 2.8 us)
Async XLA Ops:
  0.0 14.3 %collective-permute-start.10 = (bf16[12288,128]{1,0:T(8,128)(2,1)}, bf16[12288,128]{1,0:T(8,128)(2,1)S(1)}, u32[]{:S(2)}, u32[]{:S(2)}) collective-permute-start(bf16[12288,128]{1,0:T(8,128)(2,1)} %refs_4_), channel_id=1, source_target_pairs={{0,1},{1,0},{2,3},{3,2},{4,5},{5,4},{6,7},{7,6},{8,9},{9,8},{10,11... | collective-permute-start | bytes 9437192 | tf_op jit(solution)/shard_map/ppermute | solution.py:189
  0.5 8.4 %collective-permute-start.4 = (bf16[4,12288]{1,0:T(4,128)(2,1)}, bf16[4,12288]{1,0:T(4,128)(2,1)S(1)}, u32[]{:S(2)}, u32[]{:S(2)}) collective-permute-start(bf16[4,12288]{1,0:T(4,128)(2,1)} %refs_0_), channel_id=1, source_target_pairs={{0,4},{1,5},{2,6},{3,7},{4,0},{5,1},{6,2},{7,3},{8,12},{9,13},{10,... | collective-permute-start | bytes 294920 | tf_op jit(solution)/shard_map/ppermute | solution.py:183
  3.0 11.0 %collective-permute-start = (bf16[4,12288]{1,0:T(4,128)(2,1)}, bf16[4,12288]{1,0:T(4,128)(2,1)S(1)}, u32[]{:S(2)}, u32[]{:S(2)}) collective-permute-start(bf16[4,12288]{1,0:T(4,128)(2,1)} %refs_0_), channel_id=1, source_target_pairs={{0,8},{1,9},{2,10},{3,11},{4,12},{5,13},{6,14},{7,15},{8,0},{9,1},... | collective-permute-start | bytes 294920 | tf_op jit(solution)/shard_map/ppermute | solution.py:183
  5.6 8.4 %collective-permute-start.2 = (bf16[4,12288]{1,0:T(4,128)(2,1)}, bf16[4,12288]{1,0:T(4,128)(2,1)S(1)}, u32[]{:S(2)}, u32[]{:S(2)}) collective-permute-start(bf16[4,12288]{1,0:T(4,128)(2,1)} %refs_0_), channel_id=1, source_target_pairs={{0,12},{1,13},{2,14},{3,15},{4,8},{5,9},{6,10},{7,11},{8,4},{9,5},... | collective-permute-start | bytes 294920 | tf_op jit(solution)/shard_map/ppermute | solution.py:183
  5.6 1.3 %collective-permute-start.5 = (f32[1,128]{1,0:T(1,128)}, f32[1,128]{1,0:T(1,128)S(1)}, u32[]{:S(2)}, u32[]{:S(2)}) collective-permute-start(f32[1,128]{1,0:T(1,128)} %bitcast.12), channel_id=1, source_target_pairs={{0,1},{1,0},{2,3},{3,2},{4,5},{5,4},{6,7},{7,6},{8,9},{9,8},{10,11... | collective-permute-start | bytes 1544 | tf_op jit(solution)/shard_map/ppermute | solution.py:189
  6.9 5.4 %collective-permute-start.6 = (bf16[4,12288]{1,0:T(4,128)(2,1)}, bf16[4,12288]{1,0:T(4,128)(2,1)S(1)}, u32[]{:S(2)}, u32[]{:S(2)}) collective-permute-start(bf16[4,12288]{1,0:T(4,128)(2,1)} %refs_0_), channel_id=1, source_target_pairs={{0,2},{1,3},{2,0},{3,1},{4,6},{5,7},{6,4},{7,5},{8,10},{9,11},{10,... | collective-permute-start | bytes 294920 | tf_op jit(solution)/shard_map/ppermute | solution.py:186
  9.6 4.6 %collective-permute-start.7 = (bf16[4,12288]{1,0:T(4,128)(2,1)S(1)}, bf16[4,12288]{1,0:T(4,128)(2,1)S(1)}, u32[]{:S(2)}, u32[]{:S(2)}) collective-permute-start(bf16[4,12288]{1,0:T(4,128)(2,1)S(1)} %collective-permute-done.4.refs_1_), channel_id=1, source_target_pairs={{0,2},{1,3},{2,0},{3,1},{4,6},{5,7},{6,4},{7,5},{8,10},{9,11},{10,... | collective-permute-start | bytes 294920 | tf_op jit(solution)/shard_map/ppermute | solution.py:186
  14.3 18.3 %collective-permute-start.12 = (bf16[128,12288]{1,0:T(8,128)(2,1)}, bf16[128,12288]{1,0:T(8,128)(2,1)S(1)}, u32[]{:S(2)}, u32[]{:S(2)}) collective-permute-start(bf16[128,12288]{1,0:T(8,128)(2,1)} %refs_5_), channel_id=1, source_target_pairs={{0,1},{1,0},{2,3},{3,2},{4,5},{5,4},{6,7},{7,6},{8,9},{9,8},{10,11... | collective-permute-start | bytes 9437192 | tf_op jit(solution)/shard_map/ppermute | solution.py:189
  14.3 7.8 %collective-permute-start.8 = (bf16[768,512]{1,0:T(8,128)(2,1)}, bf16[768,512]{1,0:T(8,128)(2,1)S(1)}, u32[]{:S(2)}, u32[]{:S(2)}) collective-permute-start(bf16[768,512]{1,0:T(8,128)(2,1)} %refs_3_), channel_id=1, source_target_pairs={{0,1},{1,0},{2,3},{3,2},{4,5},{5,4},{6,7},{7,6},{8,9},{9,8},{10,11... | collective-permute-start | bytes 2359304 | tf_op jit(solution)/shard_map/ppermute | solution.py:189
  14.8 20.8 %collective-permute-start.11 = (bf16[512,768]{1,0:T(8,128)(2,1)}, bf16[512,768]{1,0:T(8,128)(2,1)S(1)}, u32[]{:S(2)}, u32[]{:S(2)}) collective-permute-start(bf16[512,768]{1,0:T(8,128)(2,1)} %refs_6_), channel_id=1, source_target_pairs={{0,1},{1,0},{2,3},{3,2},{4,5},{5,4},{6,7},{7,6},{8,9},{9,8},{10,11... | collective-permute-start | bytes 2359304 | tf_op jit(solution)/shard_map/ppermute | solution.py:189
  14.8 6.3 %collective-permute-start.1 = (bf16[4,12288]{1,0:T(4,128)(2,1)S(1)}, bf16[4,12288]{1,0:T(4,128)(2,1)S(1)}, u32[]{:S(2)}, u32[]{:S(2)}) collective-permute-start(bf16[4,12288]{1,0:T(4,128)(2,1)S(1)} %collective-permute-done.refs_2_), channel_id=1, source_target_pairs={{0,2},{1,3},{2,0},{3,1},{4,6},{5,7},{6,4},{7,5},{8,10},{9,11},{10,... | collective-permute-start | bytes 294920 | tf_op jit(solution)/shard_map/ppermute | solution.py:186
  16.5 5.6 %collective-permute-start.3 = (bf16[4,12288]{1,0:T(4,128)(2,1)S(1)}, bf16[4,12288]{1,0:T(4,128)(2,1)S(1)}, u32[]{:S(2)}, u32[]{:S(2)}) collective-permute-start(bf16[4,12288]{1,0:T(4,128)(2,1)S(1)} %collective-permute-done.2.refs_3_), channel_id=1, source_target_pairs={{0,2},{1,3},{2,0},{3,1},{4,6},{5,7},{6,4},{7,5},{8,10},{9,11},{10,... | collective-permute-start | bytes 294920 | tf_op jit(solution)/shard_map/ppermute | solution.py:186
  20.2 11.2 %copy-start.1 = (f32[128]{0:T(128)S(1)}, f32[128]{0:T(128)}, u32[]{:S(2)}) copy-start(f32[128]{0:T(128)} %param.19) | copy-start | bytes 1540
  22.9 3.9 %collective-permute-start.9 = (bf16[32,512]{1,0:T(8,128)(2,1)S(1)}, bf16[32,512]{1,0:T(8,128)(2,1)S(1)}, u32[]{:S(2)}, u32[]{:S(2)}) collective-permute-start(bf16[32,512]{1,0:T(8,128)(2,1)S(1)} %get-tuple-element.71), channel_id=1, source_target_pairs={{0,2},{1,3},{2,0},{3,1},{4,6},{5,7},{6,4},{7,5},{8,10},{9,11},{10,... | collective-permute-start | bytes 98312 | tf_op jit(solution)/shard_map/ppermute | solution.py:186
  26.8 7.0 %collective-permute-start.13 = (bf16[32,512]{1,0:T(8,128)(2,1)S(1)}, bf16[32,512]{1,0:T(8,128)(2,1)S(1)}, u32[]{:S(2)}, u32[]{:S(2)}) collective-permute-start(bf16[32,512]{1,0:T(8,128)(2,1)S(1)} %get-tuple-element.82), channel_id=1, source_target_pairs={{0,12},{1,13},{2,14},{3,15},{4,8},{5,9},{6,10},{7,11},{8,4},{9,5},... | collective-permute-start | bytes 98312 | tf_op jit(solution)/shard_map/ppermute | solution.py:183
  30.7 4.8 %collective-permute-start.14 = (bf16[32,512]{1,0:T(8,128)(2,1)S(1)}, bf16[32,512]{1,0:T(8,128)(2,1)S(1)}, u32[]{:S(2)}, u32[]{:S(2)}) collective-permute-start(bf16[32,512]{1,0:T(8,128)(2,1)S(1)} %get-tuple-element.83), channel_id=1, source_target_pairs={{0,8},{1,9},{2,10},{3,11},{4,12},{5,13},{6,14},{7,15},{8,0},{9,1},... | collective-permute-start | bytes 98312 | tf_op jit(solution)/shard_map/ppermute | solution.py:183
  30.7 4.8 %collective-permute-start.15 = (bf16[32,512]{1,0:T(8,128)(2,1)S(1)}, bf16[32,512]{1,0:T(8,128)(2,1)S(1)}, u32[]{:S(2)}, u32[]{:S(2)}) collective-permute-start(bf16[32,512]{1,0:T(8,128)(2,1)S(1)} %get-tuple-element.84), channel_id=1, source_target_pairs={{0,4},{1,5},{2,6},{3,7},{4,0},{5,1},{6,2},{7,3},{8,12},{9,13},{10,... | collective-permute-start | bytes 98312 | tf_op jit(solution)/shard_map/ppermute | solution.py:183
  32.6 2.9 %copy-start = (f32[512]{0:T(512)S(1)}, f32[512]{0:T(512)}, u32[]{:S(2)}) copy-start(f32[512]{0:T(512)} %param.22) | copy-start | bytes 6148
  36.0 5.6 %collective-permute-start.21 = (bf16[4,12288]{1,0:T(4,128)(2,1)S(1)}, bf16[4,12288]{1,0:T(4,128)(2,1)S(1)}, u32[]{:S(2)}, u32[]{:S(2)}) collective-permute-start(bf16[4,12288]{1,0:T(4,128)(2,1)S(1)} %get-tuple-element.92), channel_id=1, source_target_pairs={{0,2},{1,3},{2,0},{3,1},{4,6},{5,7},{6,4},{7,5},{8,10},{9,11},{10,... | collective-permute-start | bytes 294920 | tf_op jit(solution)/shard_map/ppermute | solution.py:186
  37.6 6.4 %collective-permute-start.19 = (bf16[4,12288]{1,0:T(4,128)(2,1)S(1)}, bf16[4,12288]{1,0:T(4,128)(2,1)S(1)}, u32[]{:S(2)}, u32[]{:S(2)}) collective-permute-start(bf16[4,12288]{1,0:T(4,128)(2,1)S(1)} %get-tuple-element.90), channel_id=1, source_target_pairs={{0,2},{1,3},{2,0},{3,1},{4,6},{5,7},{6,4},{7,5},{8,10},{9,11},{10,... | collective-permute-start | bytes 294920 | tf_op jit(solution)/shard_map/ppermute | solution.py:186
  38.1 6.2 %collective-permute-start.17 = (bf16[4,12288]{1,0:T(4,128)(2,1)S(1)}, bf16[4,12288]{1,0:T(4,128)(2,1)S(1)}, u32[]{:S(2)}, u32[]{:S(2)}) collective-permute-start(bf16[4,12288]{1,0:T(4,128)(2,1)S(1)} %get-tuple-element.88), channel_id=1, source_target_pairs={{0,2},{1,3},{2,0},{3,1},{4,6},{5,7},{6,4},{7,5},{8,10},{9,11},{10,... | collective-permute-start | bytes 294920 | tf_op jit(solution)/shard_map/ppermute | solution.py:186
  39.6 6.7 %collective-permute-start.16 = (bf16[4,12288]{1,0:T(4,128)(2,1)S(1)}, bf16[4,12288]{1,0:T(4,128)(2,1)S(1)}, u32[]{:S(2)}, u32[]{:S(2)}) collective-permute-start(bf16[4,12288]{1,0:T(4,128)(2,1)S(1)} %get-tuple-element.86), channel_id=1, source_target_pairs={{0,2},{1,3},{2,0},{3,1},{4,6},{5,7},{6,4},{7,5},{8,10},{9,11},{10,... | collective-permute-start | bytes 294920 | tf_op jit(solution)/shard_map/ppermute | solution.py:186
  41.6 6.5 %collective-permute-start.22 = (bf16[4,12288]{1,0:T(4,128)(2,1)S(1)}, bf16[4,12288]{1,0:T(4,128)(2,1)S(1)}, u32[]{:S(2)}, u32[]{:S(2)}) collective-permute-start(bf16[4,12288]{1,0:T(4,128)(2,1)S(1)} %add_convert_fusion), channel_id=1, source_target_pairs={{0,12},{1,13},{2,14},{3,15},{4,8},{5,9},{6,10},{7,11},{8,4},{9,5},... | collective-permute-start | bytes 294920 | tf_op jit(solution)/shard_map/ppermute | solution.py:183
  44.0 6.2 %collective-permute-start.20 = (bf16[4,12288]{1,0:T(4,128)(2,1)S(1)}, bf16[4,12288]{1,0:T(4,128)(2,1)S(1)}, u32[]{:S(2)}, u32[]{:S(2)}) collective-permute-start(bf16[4,12288]{1,0:T(4,128)(2,1)S(1)} %add_convert_fusion.1), channel_id=1, source_target_pairs={{0,8},{1,9},{2,10},{3,11},{4,12},{5,13},{6,14},{7,15},{8,0},{9,1},... | collective-permute-start | bytes 294920 | tf_op jit(solution)/shard_map/ppermute | solution.py:183
  44.4 5.8 %collective-permute-start.18 = (bf16[4,12288]{1,0:T(4,128)(2,1)S(1)}, bf16[4,12288]{1,0:T(4,128)(2,1)S(1)}, u32[]{:S(2)}, u32[]{:S(2)}) collective-permute-start(bf16[4,12288]{1,0:T(4,128)(2,1)S(1)} %add_convert_fusion.2), channel_id=1, source_target_pairs={{0,4},{1,5},{2,6},{3,7},{4,0},{5,1},{6,2},{7,3},{8,12},{9,13},{10,... | collective-permute-start | bytes 294920 | tf_op jit(solution)/shard_map/ppermute | solution.py:183

commit v22 on v21

--- a/solution.py
+++ b/solution.py
@@ -196,7 +196,9 @@
 
     held = [hidden] + [across(hidden, k) for k in range(1, groups)]
     w_in_mate = core(w_in)
-    held[1], lists, counts, block_slot = lax.optimization_barrier((held[1], lists, counts, block_slot))
+    held[1], lists, counts, block_slot, w_in_mate = lax.optimization_barrier(
+        (held[1], lists, counts, block_slot, w_in_mate)
+    )
 
     table = activity(lists, counts, block_slot)
     by = plane ^ jnp.arange(groups)

time: 51.1 us -> 59.1 us (1.16)
  waiting for transfers between devices: 13.9 us -> 18.7 us
  other arithmetic: 2.23 us -> 4.71 us
    ppermute x9, waiting for transfers between devices: 7.24 us -> 10.8 us  [across(): return lax.ppermute(x, 'blk', [(i, i ^ 4 * k) for i in range(devices)])]
    ppermute x9, waiting for transfers between devices: 5.61 us -> 7.85 us  [beside(): return lax.ppermute(x, 'blk', [(i, i ^ 2) for i in range(devices)])]
    ppermute x9, starting transfers between devices: 9.93 us -> 11.2 us  [beside(): return lax.ppermute(x, 'blk', [(i, i ^ 2) for i in range(devices)])]
    ppermute x9, starting transfers between devices: 14.3 us -> 13.1 us  [across(): return lax.ppermute(x, 'blk', [(i, i ^ 4 * k) for i in range(devices)])]
    ppermute x5, waiting for transfers between devices: 1.1 us -> 0.01 us  [core(): return lax.ppermute(x, 'blk', [(i, i ^ 1) for i in range(devices)])]
    reduce_sum x1, other arithmetic: 0.09 us -> 0.77 us  [activity(): by_block = jnp.sum(hits, axis=1)]
    reduce_sum x1, other arithmetic: 0.29 us -> 0.97 us  [shards(): jnp.sum(jnp.where(relate & choose, table[None, None], 0), axis=(2, 3))]
  transfers between devices with their start and end apart: 23 -> 23, of which waited for: 10 -> 9; matrix products, arithmetic and copies ran while one was open for 6% -> 10% of each run, Pallas kernels for 15% -> 13%
where the time goes in v22:
time: 59.1 us; the launch traced here: 58.9 us
  starting transfers between devices  25.3 us (43%)
  waiting for transfers between devices  18.7 us (32%)
  Pallas kernels  8.58 us (15%)
  other arithmetic  4.71 us (8%)
  local copies, waits for them, and re-layouts  1.45 us (2%)
    ppermute x9, starting transfers between devices, across(): return lax.ppermute(x, 'blk', [(i, i ^ 4 * k) for i in range(devices)])  13.1 us
    ppermute x9, starting transfers between devices, beside(): return lax.ppermute(x, 'blk', [(i, i ^ 2) for i in range(devices)])  11.2 us
    ppermute x9, waiting for transfers between devices, across(): return lax.ppermute(x, 'blk', [(i, i ^ 4 * k) for i in range(devices)])  10.8 us
    ppermute x9, waiting for transfers between devices, beside(): return lax.ppermute(x, 'blk', [(i, i ^ 2) for i in range(devices)])  7.85 us
    pallas_call x1, Pallas kernels, shards(): call(functools.partial(load_body, len(near)), [shape(*x.shape, dtype=x.dt...  3.39 us
    optimization_barrier x1, local copies, waits for them, and re-layouts, shards(): lax.optimization_barrier((held[1], lists, counts, block_slot, w_in_mate))  1.35 us
    pallas_call x1, Pallas kernels, shards(): call(functools.partial(act_body, step), [shape(rows, 2 * block)], [VMEM]...  1.21 us
    pallas_call x1, Pallas kernels, shards(): call(functools.partial(part_body, step), [shape(rows, width, dtype=f32)],...  1.19 us
  transfers between devices with their start and end apart: 23, of which 9 were waited for; matrix products, arithmetic and copies ran while one was open for 10% of the time, Pallas kernels for 13%

profile of v22, /device:TPU:0, one launch (start us, length us, event | category | flops | bytes accessed | tf_op | source)
XLA Modules:
  0.0 58.9 jit_solution(15093782181330065259)
XLA Ops:
  0.5 3.6 %collective-permute-start = (bf16[4,12288]{1,0:T(4,128)(2,1)}, bf16[4,12288]{1,0:T(4,128)(2,1)S(1)}, u32[]{:S(2)}, u32[]{:S(2)}) collective-permute-start(bf16[4,12288]{1,0:T(4,128)(2,1)} %refs_0_), channel_id=1, source_target_pairs={{0,8},{1,9},{2,10},{3,11},{4,12},{5,13},{6,14},{7,15},{8,0},{9,1},... | collective-permute-start | bytes 294920 | tf_op jit(solution)/shard_map/ppermute | solution.py:183
  4.0 1.3 %collective-permute-start.2 = (bf16[4,12288]{1,0:T(4,128)(2,1)}, bf16[4,12288]{1,0:T(4,128)(2,1)S(1)}, u32[]{:S(2)}, u32[]{:S(2)}) collective-permute-start(bf16[4,12288]{1,0:T(4,128)(2,1)} %refs_0_), channel_id=1, source_target_pairs={{0,12},{1,13},{2,14},{3,15},{4,8},{5,9},{6,10},{7,11},{8,4},{9,5},... | collective-permute-start | bytes 294920 | tf_op jit(solution)/shard_map/ppermute | solution.py:183
  6.9 1.9 %collective-permute-start.7 = (bf16[4,12288]{1,0:T(4,128)(2,1)}, bf16[4,12288]{1,0:T(4,128)(2,1)S(1)}, u32[]{:S(2)}, u32[]{:S(2)}) collective-permute-start(bf16[4,12288]{1,0:T(4,128)(2,1)} %refs_0_), channel_id=1, source_target_pairs={{0,2},{1,3},{2,0},{3,1},{4,6},{5,7},{6,4},{7,5},{8,10},{9,11},{10,... | collective-permute-start | bytes 294920 | tf_op jit(solution)/shard_map/ppermute | solution.py:186
  8.8 4.5 %collective-permute-done.4.refs_1_ = bf16[4,12288]{1,0:T(4,128)(2,1)S(1)} collective-permute-done((bf16[4,12288]{1,0:T(4,128)(2,1)}, bf16[4,12288]{1,0:T(4,128)(2,1)S(1)}, u32[]{:S(2)}, u32[]{:S(2)}) %collective-permute-start.4) | collective-permute-done | bytes 98336 | tf_op jit(solution)/shard_map/ppermute | solution.py:183
  13.3 0.7 %fusion = s32[16,16]{1,0:T(8,128)S(1)} fusion(s32[16]{0:T(128)} %param.17), kind=kLoop, calls=%fused_computation.10 | loop fusion | flops 512 | bytes 1088 | tf_op jit(solution)/shard_map/convert_element_type | solution.py:153
  14.0 0.7 %fusion.1 = s32[4,6]{0,1:T(8,128)S(1)} fusion(s32[4]{0:T(128)} %param.16), kind=kLoop, calls=%fused_computation.12 | loop fusion | flops 48 | bytes 112 | tf_op jit(solution)/shard_map/convert_element_type | solution.py:150
  14.7 1.4 %copy.13 = s32[4,6]{0,1:T(8,128)} copy(s32[4,6]{1,0:T(4,128)} %param.15) | data formatting | bytes 192 | tf_op jit(solution)/shard_map/optimization_barrier | solution.py:199
  16.0 1.6 %collective-permute-start.8 = (bf16[4,12288]{1,0:T(4,128)(2,1)S(1)}, bf16[4,12288]{1,0:T(4,128)(2,1)S(1)}, u32[]{:S(2)}, u32[]{:S(2)}) collective-permute-start(bf16[4,12288]{1,0:T(4,128)(2,1)S(1)} %collective-permute-done.4.refs_1_), channel_id=1, source_target_pairs={{0,2},{1,3},{2,0},{3,1},{4,6},{5,7},{6,4},{7,5},{8,10},{9,11},{10,... | collective-permute-start | bytes 294920 | tf_op jit(solution)/shard_map/ppermute | solution.py:186
  17.6 0.8 %select_reduce_fusion.1 = s32[4,16]{1,0:T(4,128)S(1)} fusion(s32[4,6]{0,1:T(8,128)S(1)} %fusion.1, s32[4,6]{0,1:T(8,128)} %copy.13), kind=kLoop, calls=%fused_computation.7 | loop fusion | flops 1088 | bytes 448 | tf_op jit(solution)/shard_map/reduce_sum | solution.py:152
  18.5 1.0 %select_reduce_fusion = s32[4,2]{1,0:T(4,128)S(1)} fusion(s32[4,16]{1,0:T(4,128)S(1)} %multiply_reduce_fusion, pred[2,16]{1,0:T(4,128)(4,1)} %iota_compare_fusion.4, pred[4,4]{1,0:T(4,128)(4,1)} %iota_compare_fusion.3), kind=kLoop, calls=%fused_computation.6 | loop fusion | flops 1528 | bytes 336 | tf_op jit(solution)/shard_map/reduce_sum | solution.py:208
  19.6 1.1 %collective-permute-done.8.refs_5_ = bf16[4,12288]{1,0:T(4,128)(2,1)S(1)} collective-permute-done((bf16[4,12288]{1,0:T(4,128)(2,1)S(1)}, bf16[4,12288]{1,0:T(4,128)(2,1)S(1)}, u32[]{:S(2)}, u32[]{:S(2)}) %collective-permute-start.8) | collective-permute-done | bytes 98336 | tf_op jit(solution)/shard_map/ppermute | solution.py:186
  21.2 1.6 %collective-permute-start.1 = (bf16[4,12288]{1,0:T(4,128)(2,1)S(1)}, bf16[4,12288]{1,0:T(4,128)(2,1)S(1)}, u32[]{:S(2)}, u32[]{:S(2)}) collective-permute-start(bf16[4,12288]{1,0:T(4,128)(2,1)S(1)} %collective-permute-done.refs_2_), channel_id=1, source_target_pairs={{0,2},{1,3},{2,0},{3,1},{4,6},{5,7},{6,4},{7,5},{8,10},{9,11},{10,... | collective-permute-start | bytes 294920 | tf_op jit(solution)/shard_map/ppermute | solution.py:186
  23.2 3.4 %shard_map.118 = (bf16[4,12288]{1,0:T(4,128)(2,1)S(1)}, f32[1,12288]{1,0:T(1,128)S(1)}, f32[1,12288]{1,0:T(1,128)S(1)}, bf16[768,512]{1,0:T(8,128)(2,1)S(1)}, bf...) custom-call(bf16[4,12288]{1,0:T(4,128)(2,1)} %refs_0_, ...), custom_call_target="tpu_custom_call" | custom-call | bytes 8388608 | tf_op jit(solution)/shard_map/pallas_call | solution.py:217
  26.6 0.8 %shard_map.119 = (bf16[16,12288]{1,0:T(8,128)(2,1)S(1)}, bf16[8,12288]{1,0:T(8,128)(2,1)S(1)}) custom-call(bf16[4,12288]{1,0:T(4,128)(2,1)S(1)} %get-tuple-element.62.refs_0_, bf16[4,12288]{1,0:T(4,128)(2,1)S(1)} %collective-permute-done.4.refs_1_, bf16[4,12288]{1,0:T(4,128)(2,1)S(1)} %collective-permute-done.refs_2_, ...), custom_call_target="tpu_custom_call" | custom-call | bytes 4194304 | tf_op jit(solution)/shard_map/pallas_call | solution.py:233
  27.4 1.0 %collective-permute-done.3.refs_1_ = bf16[4,12288]{1,0:T(4,128)(2,1)S(1)} collective-permute-done((bf16[4,12288]{1,0:T(4,128)(2,1)S(1)}, bf16[4,12288]{1,0:T(4,128)(2,1)S(1)}, u32[]{:S(2)}, u32[]{:S(2)}) %collective-permute-start.3) | collective-permute-done | bytes 98336 | tf_op jit(solution)/shard_map/ppermute | solution.py:186
  28.5 0.8 %shard_map.120 = (bf16[16,12288]{1,0:T(8,128)(2,1)S(1)}, f32[32,512]{1,0:T(8,128)S(1)}, bf16[32,512]{1,0:T(8,128)(2,1)S(1)}) custom-call(s32[1]{0:T(128)} %bitcast.place, bf16[4,12288]{1,0:T(4,128)(2,1)S(1)} %collective-permute-done.1.refs_0_, bf16[4,12288]{1,0:T(4,128)(2,1)S(1)} %collective-permute-done.3.refs_1_, ...), custom_call_target="tpu_custom_call" | custom-call | bytes 4194304 | tf_op jit(solution)/shard_map/pallas_call | solution.py:241
  29.3 1.6 %collective-permute-start.10 = (bf16[32,512]{1,0:T(8,128)(2,1)S(1)}, bf16[32,512]{1,0:T(8,128)(2,1)S(1)}, u32[]{:S(2)}, u32[]{:S(2)}) collective-permute-start(bf16[32,512]{1,0:T(8,128)(2,1)S(1)} %get-tuple-element.72), channel_id=1, source_target_pairs={{0,2},{1,3},{2,0},{3,1},{4,6},{5,7},{6,4},{7,5},{8,10},{9,11},{10,... | collective-permute-start | bytes 98312 | tf_op jit(solution)/shard_map/ppermute | solution.py:186
  30.9 2.3 %collective-permute-done.10.got = bf16[32,512]{1,0:T(8,128)(2,1)S(1)} collective-permute-done((bf16[32,512]{1,0:T(8,128)(2,1)S(1)}, bf16[32,512]{1,0:T(8,128)(2,1)S(1)}, u32[]{:S(2)}, u32[]{:S(2)}) %collective-permute-start.10) | collective-permute-done | bytes 32800 | tf_op jit(solution)/shard_map/ppermute | solution.py:186
  33.2 3.6 %collective-permute-start.13 = (bf16[32,512]{1,0:T(8,128)(2,1)S(1)}, bf16[32,512]{1,0:T(8,128)(2,1)S(1)}, u32[]{:S(2)}, u32[]{:S(2)}) collective-permute-start(bf16[32,512]{1,0:T(8,128)(2,1)S(1)} %get-tuple-element.84), channel_id=1, source_target_pairs={{0,12},{1,13},{2,14},{3,15},{4,8},{5,9},{6,10},{7,11},{8,4},{9,5},... | collective-permute-start | bytes 98312 | tf_op jit(solution)/shard_map/ppermute | solution.py:183
  36.8 0.8 %collective-permute-start.15 = (bf16[32,512]{1,0:T(8,128)(2,1)S(1)}, bf16[32,512]{1,0:T(8,128)(2,1)S(1)}, u32[]{:S(2)}, u32[]{:S(2)}) collective-permute-start(bf16[32,512]{1,0:T(8,128)(2,1)S(1)} %get-tuple-element.86), channel_id=1, source_target_pairs={{0,4},{1,5},{2,6},{3,7},{4,0},{5,1},{6,2},{7,3},{8,12},{9,13},{10,... | collective-permute-start | bytes 98312 | tf_op jit(solution)/shard_map/ppermute | solution.py:183
  37.7 1.2 %shard_map.122.act = bf16[32,256]{1,0:T(8,128)(2,1)S(1)} custom-call(bf16[16,12288]{1,0:T(8,128)(2,1)S(1)} %get-tuple-element.67.refs_2_.near, bf16[16,12288]{1,0:T(8,128)(2,1)S(1)} %get-tuple-element.77.far, bf16[12288,128]{1,0:T(8,128)(2,1)S(1)} %get-tuple-element.78.w_own, bf16[12288,128]{1,0:T(8,128)(2,1)S(1)} %collective-permute-done.5.w_mate, ...), custom_call_target="tpu_custom_call" | custom-call | bytes 4194304 | tf_op jit(solution)/shard_map/pallas_call | solution.py:251
  38.9 1.2 %shard_map.123.part = f32[32,12288]{1,0:T(8,128)S(1)} custom-call(bf16[32,256]{1,0:T(8,128)(2,1)S(1)} %shard_map.122.act, bf16[128,12288]{1,0:T(8,128)(2,1)S(1)} %get-tuple-element.82.w_own, bf16[128,12288]{1,0:T(8,128)(2,1)S(1)} %collective-permute-done.12.w_mate), custom_call_target="tpu_custom_call" | custom-call | bytes 6291456 | tf_op jit(solution)/shard_map/pallas_call | solution.py:266
  40.1 1.5 %collective-permute-done.14.refs_1_ = bf16[32,512]{1,0:T(8,128)(2,1)S(1)} collective-permute-done((bf16[32,512]{1,0:T(8,128)(2,1)S(1)}, bf16[32,512]{1,0:T(8,128)(2,1)S(1)}, u32[]{:S(2)}, u32[]{:S(2)}) %collective-permute-start.14) | collective-permute-done | bytes 32800 | tf_op jit(solution)/shard_map/ppermute | solution.py:183
  42.1 1.6 %collective-permute-start.17 = (bf16[4,12288]{1,0:T(4,128)(2,1)S(1)}, bf16[4,12288]{1,0:T(4,128)(2,1)S(1)}, u32[]{:S(2)}, u32[]{:S(2)}) collective-permute-start(bf16[4,12288]{1,0:T(4,128)(2,1)S(1)} %get-tuple-element.90), channel_id=1, source_target_pairs={{0,2},{1,3},{2,0},{3,1},{4,6},{5,7},{6,4},{7,5},{8,10},{9,11},{10,... | collective-permute-start | bytes 294920 | tf_op jit(solution)/shard_map/ppermute | solution.py:186
  44.2 1.5 %collective-permute-start.19 = (bf16[4,12288]{1,0:T(4,128)(2,1)S(1)}, bf16[4,12288]{1,0:T(4,128)(2,1)S(1)}, u32[]{:S(2)}, u32[]{:S(2)}) collective-permute-start(bf16[4,12288]{1,0:T(4,128)(2,1)S(1)} %get-tuple-element.92), channel_id=1, source_target_pairs={{0,2},{1,3},{2,0},{3,1},{4,6},{5,7},{6,4},{7,5},{8,10},{9,11},{10,... | collective-permute-start | bytes 294920 | tf_op jit(solution)/shard_map/ppermute | solution.py:186
  46.2 1.5 %collective-permute-done.17 = bf16[4,12288]{1,0:T(4,128)(2,1)S(1)} collective-permute-done((bf16[4,12288]{1,0:T(4,128)(2,1)S(1)}, bf16[4,12288]{1,0:T(4,128)(2,1)S(1)}, u32[]{:S(2)}, u32[]{:S(2)}) %collective-permute-start.17) | collective-permute-done | bytes 98336 | tf_op jit(solution)/shard_map/ppermute | solution.py:186
  48.0 1.9 %collective-permute-done.19 = bf16[4,12288]{1,0:T(4,128)(2,1)S(1)} collective-permute-done((bf16[4,12288]{1,0:T(4,128)(2,1)S(1)}, bf16[4,12288]{1,0:T(4,128)(2,1)S(1)}, u32[]{:S(2)}, u32[]{:S(2)}) %collective-permute-start.19) | collective-permute-done | bytes 98336 | tf_op jit(solution)/shard_map/ppermute | solution.py:186
  49.9 1.6 %collective-permute-start.20 = (bf16[4,12288]{1,0:T(4,128)(2,1)S(1)}, bf16[4,12288]{1,0:T(4,128)(2,1)S(1)}, u32[]{:S(2)}, u32[]{:S(2)}) collective-permute-start(bf16[4,12288]{1,0:T(4,128)(2,1)S(1)} %add_convert_fusion.1), channel_id=1, source_target_pairs={{0,8},{1,9},{2,10},{3,11},{4,12},{5,13},{6,14},{7,15},{8,0},{9,1},... | collective-permute-start | bytes 294920 | tf_op jit(solution)/shard_map/ppermute | solution.py:183
  51.6 1.7 %collective-permute-start.22 = (bf16[4,12288]{1,0:T(4,128)(2,1)S(1)}, bf16[4,12288]{1,0:T(4,128)(2,1)S(1)}, u32[]{:S(2)}, u32[]{:S(2)}) collective-permute-start(bf16[4,12288]{1,0:T(4,128)(2,1)S(1)} %add_convert_fusion), channel_id=1, source_target_pairs={{0,12},{1,13},{2,14},{3,15},{4,8},{5,9},{6,10},{7,11},{8,4},{9,5},... | collective-permute-start | bytes 294920 | tf_op jit(solution)/shard_map/ppermute | solution.py:183
  53.4 3.1 %collective-permute-done.20.refs_2_ = bf16[4,12288]{1,0:T(4,128)(2,1)S(1)} collective-permute-done((bf16[4,12288]{1,0:T(4,128)(2,1)S(1)}, bf16[4,12288]{1,0:T(4,128)(2,1)S(1)}, u32[]{:S(2)}, u32[]{:S(2)}) %collective-permute-start.20) | collective-permute-done | bytes 98336 | tf_op jit(solution)/shard_map/ppermute | solution.py:183
  56.4 1.7 %collective-permute-done.22.refs_3_ = bf16[4,12288]{1,0:T(4,128)(2,1)S(1)} collective-permute-done((bf16[4,12288]{1,0:T(4,128)(2,1)S(1)}, bf16[4,12288]{1,0:T(4,128)(2,1)S(1)}, u32[]{:S(2)}, u32[]{:S(2)}) %collective-permute-start.22) | collective-permute-done | bytes 98336 | tf_op jit(solution)/shard_map/ppermute | solution.py:183
  58.2 0.7 %shard_map.125 = bf16[4,12288]{1,0:T(4,128)(2,1)} custom-call(f32[4,12288]{1,0:T(4,128)S(1)} %convert_add_fusion.refs_0_, bf16[4,12288]{1,0:T(4,128)(2,1)S(1)} %collective-permute-done.18.refs_1_, bf16[4,12288]{1,0:T(4,128)(2,1)S(1)} %collective-permute-done.20.refs_2_, bf16[4,12288]{1,0:T(4,128)(2,1)S(1)} %collective-permute-done.22.refs_3_), custom_call_target="tpu_custom_call" | custom-call | bytes 2097152 | tf_op jit(solution)/shard_map/pallas_call | solution.py:287
  (43 shorter events, 5.0 us)
Async XLA Ops:
  0.0 13.3 %collective-permute-start.5 = (bf16[12288,128]{1,0:T(8,128)(2,1)}, bf16[12288,128]{1,0:T(8,128)(2,1)S(1)}, u32[]{:S(2)}, u32[]{:S(2)}) collective-permute-start(bf16[12288,128]{1,0:T(8,128)(2,1)} %refs_4_), channel_id=1, source_target_pairs={{0,1},{1,0},{2,3},{3,2},{4,5},{5,4},{6,7},{7,6},{8,9},{9,8},{10,11... | collective-permute-start | bytes 9437192 | tf_op jit(solution)/shard_map/ppermute | solution.py:189
  0.5 19.1 %collective-permute-start = (bf16[4,12288]{1,0:T(4,128)(2,1)}, bf16[4,12288]{1,0:T(4,128)(2,1)S(1)}, u32[]{:S(2)}, u32[]{:S(2)}) collective-permute-start(bf16[4,12288]{1,0:T(4,128)(2,1)} %refs_0_), channel_id=1, source_target_pairs={{0,8},{1,9},{2,10},{3,11},{4,12},{5,13},{6,14},{7,15},{8,0},{9,1},... | collective-permute-start | bytes 294920 | tf_op jit(solution)/shard_map/ppermute | solution.py:183
  4.0 15.5 %collective-permute-start.2 = (bf16[4,12288]{1,0:T(4,128)(2,1)}, bf16[4,12288]{1,0:T(4,128)(2,1)S(1)}, u32[]{:S(2)}, u32[]{:S(2)}) collective-permute-start(bf16[4,12288]{1,0:T(4,128)(2,1)} %refs_0_), channel_id=1, source_target_pairs={{0,12},{1,13},{2,14},{3,15},{4,8},{5,9},{6,10},{7,11},{8,4},{9,5},... | collective-permute-start | bytes 294920 | tf_op jit(solution)/shard_map/ppermute | solution.py:183
  5.4 7.9 %collective-permute-start.4 = (bf16[4,12288]{1,0:T(4,128)(2,1)}, bf16[4,12288]{1,0:T(4,128)(2,1)S(1)}, u32[]{:S(2)}, u32[]{:S(2)}) collective-permute-start(bf16[4,12288]{1,0:T(4,128)(2,1)} %refs_0_), channel_id=1, source_target_pairs={{0,4},{1,5},{2,6},{3,7},{4,0},{5,1},{6,2},{7,3},{8,12},{9,13},{10,... | collective-permute-start | bytes 294920 | tf_op jit(solution)/shard_map/ppermute | solution.py:183
  5.6 1.3 %collective-permute-start.6 = (f32[1,128]{1,0:T(1,128)}, f32[1,128]{1,0:T(1,128)S(1)}, u32[]{:S(2)}, u32[]{:S(2)}) collective-permute-start(f32[1,128]{1,0:T(1,128)} %bitcast.12), channel_id=1, source_target_pairs={{0,1},{1,0},{2,3},{3,2},{4,5},{5,4},{6,7},{7,6},{8,9},{9,8},{10,11... | collective-permute-start | bytes 1544 | tf_op jit(solution)/shard_map/ppermute | solution.py:189
  6.9 12.7 %collective-permute-start.7 = (bf16[4,12288]{1,0:T(4,128)(2,1)}, bf16[4,12288]{1,0:T(4,128)(2,1)S(1)}, u32[]{:S(2)}, u32[]{:S(2)}) collective-permute-start(bf16[4,12288]{1,0:T(4,128)(2,1)} %refs_0_), channel_id=1, source_target_pairs={{0,2},{1,3},{2,0},{3,1},{4,6},{5,7},{6,4},{7,5},{8,10},{9,11},{10,... | collective-permute-start | bytes 294920 | tf_op jit(solution)/shard_map/ppermute | solution.py:186
  16.0 4.6 %collective-permute-start.8 = (bf16[4,12288]{1,0:T(4,128)(2,1)S(1)}, bf16[4,12288]{1,0:T(4,128)(2,1)S(1)}, u32[]{:S(2)}, u32[]{:S(2)}) collective-permute-start(bf16[4,12288]{1,0:T(4,128)(2,1)S(1)} %collective-permute-done.4.refs_1_), channel_id=1, source_target_pairs={{0,2},{1,3},{2,0},{3,1},{4,6},{5,7},{6,4},{7,5},{8,10},{9,11},{10,... | collective-permute-start | bytes 294920 | tf_op jit(solution)/shard_map/ppermute | solution.py:186
  20.7 18.3 %collective-permute-start.12 = (bf16[128,12288]{1,0:T(8,128)(2,1)}, bf16[128,12288]{1,0:T(8,128)(2,1)S(1)}, u32[]{:S(2)}, u32[]{:S(2)}) collective-permute-start(bf16[128,12288]{1,0:T(8,128)(2,1)} %refs_5_), channel_id=1, source_target_pairs={{0,1},{1,0},{2,3},{3,2},{4,5},{5,4},{6,7},{7,6},{8,9},{9,8},{10,11... | collective-permute-start | bytes 9437192 | tf_op jit(solution)/shard_map/ppermute | solution.py:189
  20.7 7.8 %collective-permute-start.9 = (bf16[768,512]{1,0:T(8,128)(2,1)}, bf16[768,512]{1,0:T(8,128)(2,1)S(1)}, u32[]{:S(2)}, u32[]{:S(2)}) collective-permute-start(bf16[768,512]{1,0:T(8,128)(2,1)} %refs_3_), channel_id=1, source_target_pairs={{0,1},{1,0},{2,3},{3,2},{4,5},{5,4},{6,7},{7,6},{8,9},{9,8},{10,11... | collective-permute-start | bytes 2359304 | tf_op jit(solution)/shard_map/ppermute | solution.py:189
  21.2 20.5 %collective-permute-start.11 = (bf16[512,768]{1,0:T(8,128)(2,1)}, bf16[512,768]{1,0:T(8,128)(2,1)S(1)}, u32[]{:S(2)}, u32[]{:S(2)}) collective-permute-start(bf16[512,768]{1,0:T(8,128)(2,1)} %refs_6_), channel_id=1, source_target_pairs={{0,1},{1,0},{2,3},{3,2},{4,5},{5,4},{6,7},{7,6},{8,9},{9,8},{10,11... | collective-permute-start | bytes 2359304 | tf_op jit(solution)/shard_map/ppermute | solution.py:189
  21.2 6.3 %collective-permute-start.1 = (bf16[4,12288]{1,0:T(4,128)(2,1)S(1)}, bf16[4,12288]{1,0:T(4,128)(2,1)S(1)}, u32[]{:S(2)}, u32[]{:S(2)}) collective-permute-start(bf16[4,12288]{1,0:T(4,128)(2,1)S(1)} %collective-permute-done.refs_2_), channel_id=1, source_target_pairs={{0,2},{1,3},{2,0},{3,1},{4,6},{5,7},{6,4},{7,5},{8,10},{9,11},{10,... | collective-permute-start | bytes 294920 | tf_op jit(solution)/shard_map/ppermute | solution.py:186
  22.7 5.7 %collective-permute-start.3 = (bf16[4,12288]{1,0:T(4,128)(2,1)S(1)}, bf16[4,12288]{1,0:T(4,128)(2,1)S(1)}, u32[]{:S(2)}, u32[]{:S(2)}) collective-permute-start(bf16[4,12288]{1,0:T(4,128)(2,1)S(1)} %collective-permute-done.2.refs_3_), channel_id=1, source_target_pairs={{0,2},{1,3},{2,0},{3,1},{4,6},{5,7},{6,4},{7,5},{8,10},{9,11},{10,... | collective-permute-start | bytes 294920 | tf_op jit(solution)/shard_map/ppermute | solution.py:186
  26.6 11.1 %copy-start.1 = (f32[128]{0:T(128)S(1)}, f32[128]{0:T(128)}, u32[]{:S(2)}) copy-start(f32[128]{0:T(128)} %param.19) | copy-start | bytes 1540
  29.3 3.9 %collective-permute-start.10 = (bf16[32,512]{1,0:T(8,128)(2,1)S(1)}, bf16[32,512]{1,0:T(8,128)(2,1)S(1)}, u32[]{:S(2)}, u32[]{:S(2)}) collective-permute-start(bf16[32,512]{1,0:T(8,128)(2,1)S(1)} %get-tuple-element.72), channel_id=1, source_target_pairs={{0,2},{1,3},{2,0},{3,1},{4,6},{5,7},{6,4},{7,5},{8,10},{9,11},{10,... | collective-permute-start | bytes 98312 | tf_op jit(solution)/shard_map/ppermute | solution.py:186
  33.2 6.9 %collective-permute-start.13 = (bf16[32,512]{1,0:T(8,128)(2,1)S(1)}, bf16[32,512]{1,0:T(8,128)(2,1)S(1)}, u32[]{:S(2)}, u32[]{:S(2)}) collective-permute-start(bf16[32,512]{1,0:T(8,128)(2,1)S(1)} %get-tuple-element.84), channel_id=1, source_target_pairs={{0,12},{1,13},{2,14},{3,15},{4,8},{5,9},{6,10},{7,11},{8,4},{9,5},... | collective-permute-start | bytes 98312 | tf_op jit(solution)/shard_map/ppermute | solution.py:183
  36.8 4.8 %collective-permute-start.14 = (bf16[32,512]{1,0:T(8,128)(2,1)S(1)}, bf16[32,512]{1,0:T(8,128)(2,1)S(1)}, u32[]{:S(2)}, u32[]{:S(2)}) collective-permute-start(bf16[32,512]{1,0:T(8,128)(2,1)S(1)} %get-tuple-element.85), channel_id=1, source_target_pairs={{0,8},{1,9},{2,10},{3,11},{4,12},{5,13},{6,14},{7,15},{8,0},{9,1},... | collective-permute-start | bytes 98312 | tf_op jit(solution)/shard_map/ppermute | solution.py:183
  36.8 4.8 %collective-permute-start.15 = (bf16[32,512]{1,0:T(8,128)(2,1)S(1)}, bf16[32,512]{1,0:T(8,128)(2,1)S(1)}, u32[]{:S(2)}, u32[]{:S(2)}) collective-permute-start(bf16[32,512]{1,0:T(8,128)(2,1)S(1)} %get-tuple-element.86), channel_id=1, source_target_pairs={{0,4},{1,5},{2,6},{3,7},{4,0},{5,1},{6,2},{7,3},{8,12},{9,13},{10,... | collective-permute-start | bytes 98312 | tf_op jit(solution)/shard_map/ppermute | solution.py:183
  38.9 2.8 %copy-start = (f32[512]{0:T(512)S(1)}, f32[512]{0:T(512)}, u32[]{:S(2)}) copy-start(f32[512]{0:T(512)} %param.22) | copy-start | bytes 6148
  42.1 5.6 %collective-permute-start.17 = (bf16[4,12288]{1,0:T(4,128)(2,1)S(1)}, bf16[4,12288]{1,0:T(4,128)(2,1)S(1)}, u32[]{:S(2)}, u32[]{:S(2)}) collective-permute-start(bf16[4,12288]{1,0:T(4,128)(2,1)S(1)} %get-tuple-element.90), channel_id=1, source_target_pairs={{0,2},{1,3},{2,0},{3,1},{4,6},{5,7},{6,4},{7,5},{8,10},{9,11},{10,... | collective-permute-start | bytes 294920 | tf_op jit(solution)/shard_map/ppermute | solution.py:186
  43.7 9.6 %collective-permute-start.16 = (bf16[4,12288]{1,0:T(4,128)(2,1)S(1)}, bf16[4,12288]{1,0:T(4,128)(2,1)S(1)}, u32[]{:S(2)}, u32[]{:S(2)}) collective-permute-start(bf16[4,12288]{1,0:T(4,128)(2,1)S(1)} %get-tuple-element.88), channel_id=1, source_target_pairs={{0,2},{1,3},{2,0},{3,1},{4,6},{5,7},{6,4},{7,5},{8,10},{9,11},{10,... | collective-permute-start | bytes 294920 | tf_op jit(solution)/shard_map/ppermute | solution.py:186
  44.2 5.6 %collective-permute-start.19 = (bf16[4,12288]{1,0:T(4,128)(2,1)S(1)}, bf16[4,12288]{1,0:T(4,128)(2,1)S(1)}, u32[]{:S(2)}, u32[]{:S(2)}) collective-permute-start(bf16[4,12288]{1,0:T(4,128)(2,1)S(1)} %get-tuple-element.92), channel_id=1, source_target_pairs={{0,2},{1,3},{2,0},{3,1},{4,6},{5,7},{6,4},{7,5},{8,10},{9,11},{10,... | collective-permute-start | bytes 294920 | tf_op jit(solution)/shard_map/ppermute | solution.py:186
  45.7 5.8 %collective-permute-start.21 = (bf16[4,12288]{1,0:T(4,128)(2,1)S(1)}, bf16[4,12288]{1,0:T(4,128)(2,1)S(1)}, u32[]{:S(2)}, u32[]{:S(2)}) collective-permute-start(bf16[4,12288]{1,0:T(4,128)(2,1)S(1)} %get-tuple-element.94), channel_id=1, source_target_pairs={{0,2},{1,3},{2,0},{3,1},{4,6},{5,7},{6,4},{7,5},{8,10},{9,11},{10,... | collective-permute-start | bytes 294920 | tf_op jit(solution)/shard_map/ppermute | solution.py:186
  47.8 5.5 %collective-permute-start.18 = (bf16[4,12288]{1,0:T(4,128)(2,1)S(1)}, bf16[4,12288]{1,0:T(4,128)(2,1)S(1)}, u32[]{:S(2)}, u32[]{:S(2)}) collective-permute-start(bf16[4,12288]{1,0:T(4,128)(2,1)S(1)} %add_convert_fusion.2), channel_id=1, source_target_pairs={{0,4},{1,5},{2,6},{3,7},{4,0},{5,1},{6,2},{7,3},{8,12},{9,13},{10,... | collective-permute-start | bytes 294920 | tf_op jit(solution)/shard_map/ppermute | solution.py:183
  49.9 6.5 %collective-permute-start.20 = (bf16[4,12288]{1,0:T(4,128)(2,1)S(1)}, bf16[4,12288]{1,0:T(4,128)(2,1)S(1)}, u32[]{:S(2)}, u32[]{:S(2)}) collective-permute-start(bf16[4,12288]{1,0:T(4,128)(2,1)S(1)} %add_convert_fusion.1), channel_id=1, source_target_pairs={{0,8},{1,9},{2,10},{3,11},{4,12},{5,13},{6,14},{7,15},{8,0},{9,1},... | collective-permute-start | bytes 294920 | tf_op jit(solution)/shard_map/ppermute | solution.py:183
  51.6 6.6 %collective-permute-start.22 = (bf16[4,12288]{1,0:T(4,128)(2,1)S(1)}, bf16[4,12288]{1,0:T(4,128)(2,1)S(1)}, u32[]{:S(2)}, u32[]{:S(2)}) collective-permute-start(bf16[4,12288]{1,0:T(4,128)(2,1)S(1)} %add_convert_fusion), channel_id=1, source_target_pairs={{0,12},{1,13},{2,14},{3,15},{4,8},{5,9},{6,10},{7,11},{8,4},{9,5},... | collective-permute-start | bytes 294920 | tf_op jit(solution)/shard_map/ppermute | solution.py:183

commit v23 on v21

--- a/solution.py
+++ b/solution.py
@@ -64,7 +64,7 @@
 
 
 def norm_body(count, place, *refs):
-    held, (near, first, gain, shift, own, mate, far, total, message) = refs[:count], refs[count:]
+    held, (near, first, gain, shift, own, mate, far, total, *messages) = refs[:count], refs[count:]
     rows, done = held[0].shape[0], first.shape[0]
     far[:done, :] = first[...]
     for i in range(0, count, 2):
@@ -80,10 +80,9 @@
     sums = jnp.dot(mine, own[...], preferred_element_type=f32) + jnp.dot(
         other, mate[...], preferred_element_type=f32
     )
-    half = near.shape[0]
     total[...] = sums
-    message[:half, :] = sums[half:].astype(bf16)
-    message[half:, :] = sums[:half].astype(bf16)
+    for k, message in enumerate(messages, 1):
+        message[...] = turn(sums, len(messages) + 1, k).astype(bf16)
 
 
 def turn(x, groups, bit):
@@ -92,18 +91,19 @@
     return jnp.concatenate([x[i * rows : (i + 1) * rows] for i in at], axis=0)
 
 
-def merge_body(groups, total, got, out, *messages):
-    sums = total[...] + got[...].astype(f32)
-    out[...] = sums
-    for k in range(1, groups):
-        messages[k - 1][...] = turn(sums, groups, k).astype(bf16)
-
-
-def up_body(groups, place, total, bias, own, mate, part, *refs):
-    got, outs = refs[: groups - 1], refs[groups - 1 :]
+def merge_body(groups, total, *refs):
+    got, (out, message) = refs[: groups - 1], refs[groups - 1 :]
     sums = total[...]
     for g in got:
         sums = sums + g[...].astype(f32)
+    out[...] = sums
+    half = sums.shape[0] // 2
+    message[:half, :] = sums[half:].astype(bf16)
+    message[half:, :] = sums[:half].astype(bf16)
+
+
+def up_body(groups, place, total, bias, own, mate, part, got, *outs):
+    sums = total[...] + got[...].astype(f32)
     hidden = jnp.maximum(sums + bias[...], 0.0).astype(bf16)
     core = place[0] % 2
     mine = jnp.dot(hidden, own[...], preferred_element_type=f32)
@@ -236,15 +236,15 @@
         (),
         4 * MIB,
     )(*held, *beyond[:soon], gain, shift)
-    far, total, message = call(
+    far, total, *messages = call(
         functools.partial(norm_body, groups - soon),
-        [shape(some, width), shape(rows, rank, dtype=f32), shape(rows, rank)],
+        [shape(some, width), shape(rows, rank, dtype=f32)] + [shape(rows, rank)] * (groups - 1),
         [SMEM] + [VMEM] * (groups - soon + 6),
         16,
         (),
         4 * MIB,
     )(place, *beyond[soon:], normed, first, gain, shift, low_in, low_in_mate)
-    got = beside(message)
+    got = [across(messages[k - 1], k) for k in (1, *range(groups - 1, 1, -1))]
     step = piece(width, 2048)
     act = call(
         functools.partial(act_body, step),
@@ -254,13 +254,13 @@
         (),
         4 * MIB,
     )(normed, far, w_in, w_in_mate, bias, bias_mate, mask)[0]
-    total, *messages = call(
+    total, message = call(
         functools.partial(merge_body, groups),
-        [shape(rows, rank, dtype=f32)] + [shape(rows, rank)] * (groups - 1),
-        [VMEM] * 2,
-        16,
-    )(total, got)
-    got = [across(messages[k - 1], k) for k in range(groups - 1, 0, -1)]
+        [shape(rows, rank, dtype=f32), shape(rows, rank)],
+        [VMEM] * groups,
+        16,
+    )(total, *got)
+    got = beside(message)
     part = call(
         functools.partial(part_body, step),
         [shape(rows, width, dtype=f32)],
@@ -272,11 +272,11 @@
     parts = call(
         functools.partial(up_body, groups),
         [shape(row_dev, width, dtype=f32)] * groups + [shape(row_dev, width)] * groups,
-        [SMEM] + [VMEM] * (groups + 4),
+        [SMEM] + [VMEM] * 6,
         16,
         (),
         6 * MIB,
-    )(place, total, low_bias.reshape(1, rank), low_out_near, low_out_mate, part, *got)
+    )(place, total, low_bias.reshape(1, rank), low_out_near, low_out_mate, part, got)
 
     sums = []
     for k in range(groups - 1, -1, -1):

time: 51.1 us -> 51.8 us (1.014)
  waiting for transfers between devices: 13.9 us -> 14.7 us
    ppermute x9, waiting for transfers between devices: 7.24 us -> 9.98 us  [across(): return lax.ppermute(x, 'blk', [(i, i ^ 4 * k) for i in range(devices)])]
    ppermute x9, waiting for transfers between devices: 5.61 us -> 3.66 us  [beside(): return lax.ppermute(x, 'blk', [(i, i ^ 2) for i in range(devices)])]
  transfers between devices with their start and end apart: 23 -> 23, of which waited for: 10 -> 11; matrix products, arithmetic and copies ran while one was open for 6% -> 6% of each run, Pallas kernels for 15% -> 14%
where the time goes in v23:
time: 51.8 us; the launch traced here: 51.6 us
  starting transfers between devices  25 us (48%)
  waiting for transfers between devices  14.7 us (28%)
  Pallas kernels  8.59 us (17%)
  other arithmetic  2.23 us (4%)
  local copies, waits for them, and re-layouts  0.86 us (2%)
    ppermute x9, starting transfers between devices, across(): return lax.ppermute(x, 'blk', [(i, i ^ 4 * k) for i in range(devices)])  14.3 us
    ppermute x9, waiting for transfers between devices, across(): return lax.ppermute(x, 'blk', [(i, i ^ 4 * k) for i in range(devices)])  9.98 us
    ppermute x9, starting transfers between devices, beside(): return lax.ppermute(x, 'blk', [(i, i ^ 2) for i in range(devices)])  9.75 us
    ppermute x9, waiting for transfers between devices, beside(): return lax.ppermute(x, 'blk', [(i, i ^ 2) for i in range(devices)])  3.66 us
    pallas_call x1, Pallas kernels, shards(): call(functools.partial(load_body, len(near)), [shape(*x.shape, dtype=x.dt...  3.39 us
    pallas_call x1, Pallas kernels, shards(): call(functools.partial(act_body, step), [shape(rows, 2 * block)], [VMEM]...  1.21 us
    pallas_call x1, Pallas kernels, shards(): call(functools.partial(part_body, step), [shape(rows, width, dtype=f32)],...  1.19 us
    ppermute x5, waiting for transfers between devices, core(): return lax.ppermute(x, 'blk', [(i, i ^ 1) for i in range(devices)])  1.11 us
  transfers between devices with their start and end apart: 23, of which 11 were waited for; matrix products, arithmetic and copies ran while one was open for 6% of the time, Pallas kernels for 14%

profile of v23, /device:TPU:0, one launch (start us, length us, event | category | flops | bytes accessed | tf_op | source)
XLA Modules:
  0.0 51.6 jit_solution(12478303630995460221)
XLA Ops:
  0.5 2.6 %collective-permute-start.4 = (bf16[4,12288]{1,0:T(4,128)(2,1)}, bf16[4,12288]{1,0:T(4,128)(2,1)S(1)}, u32[]{:S(2)}, u32[]{:S(2)}) collective-permute-start(bf16[4,12288]{1,0:T(4,128)(2,1)} %refs_0_), channel_id=1, source_target_pairs={{0,4},{1,5},{2,6},{3,7},{4,0},{5,1},{6,2},{7,3},{8,12},{9,13},{10,... | collective-permute-start | bytes 294920 | tf_op jit(solution)/shard_map/ppermute | solution.py:183
  3.0 2.6 %collective-permute-start = (bf16[4,12288]{1,0:T(4,128)(2,1)}, bf16[4,12288]{1,0:T(4,128)(2,1)S(1)}, u32[]{:S(2)}, u32[]{:S(2)}) collective-permute-start(bf16[4,12288]{1,0:T(4,128)(2,1)} %refs_0_), channel_id=1, source_target_pairs={{0,8},{1,9},{2,10},{3,11},{4,12},{5,13},{6,14},{7,15},{8,0},{9,1},... | collective-permute-start | bytes 294920 | tf_op jit(solution)/shard_map/ppermute | solution.py:183
  5.8 1.1 %collective-permute-done.5.b_mate = f32[1,128]{1,0:T(1,128)S(1)} collective-permute-done((f32[1,128]{1,0:T(1,128)}, f32[1,128]{1,0:T(1,128)S(1)}, u32[]{:S(2)}, u32[]{:S(2)}) %collective-permute-start.5) | collective-permute-done | bytes 544 | tf_op jit(solution)/shard_map/ppermute | solution.py:189
  6.9 2.0 %collective-permute-start.6 = (bf16[4,12288]{1,0:T(4,128)(2,1)}, bf16[4,12288]{1,0:T(4,128)(2,1)S(1)}, u32[]{:S(2)}, u32[]{:S(2)}) collective-permute-start(bf16[4,12288]{1,0:T(4,128)(2,1)} %refs_0_), channel_id=1, source_target_pairs={{0,2},{1,3},{2,0},{3,1},{4,6},{5,7},{6,4},{7,5},{8,10},{9,11},{10,... | collective-permute-start | bytes 294920 | tf_op jit(solution)/shard_map/ppermute | solution.py:186
  8.8 0.8 %copy.13 = s32[4,6]{0,1:T(8,128)S(1)} copy(s32[4,6]{1,0:T(4,128)} %param.15) | data formatting | bytes 192 | tf_op jit(solution)/shard_map/optimization_barrier | solution.py:199
  9.7 0.7 %fusion.1 = s32[4,6]{0,1:T(8,128)S(1)} fusion(s32[4]{0:T(128)} %param.16), kind=kLoop, calls=%fused_computation.12 | loop fusion | flops 48 | bytes 112 | tf_op jit(solution)/shard_map/convert_element_type | solution.py:150
  10.4 0.7 %fusion = s32[16,16]{1,0:T(8,128)S(1)} fusion(s32[16]{0:T(128)} %param.17), kind=kLoop, calls=%fused_computation.10 | loop fusion | flops 512 | bytes 1088 | tf_op jit(solution)/shard_map/convert_element_type | solution.py:153
  11.6 0.7 %collective-permute-done.6.refs_4_ = bf16[4,12288]{1,0:T(4,128)(2,1)S(1)} collective-permute-done((bf16[4,12288]{1,0:T(4,128)(2,1)}, bf16[4,12288]{1,0:T(4,128)(2,1)S(1)}, u32[]{:S(2)}, u32[]{:S(2)}) %collective-permute-start.6) | collective-permute-done | bytes 98336 | tf_op jit(solution)/shard_map/ppermute | solution.py:186
  12.3 1.7 %collective-permute-done.refs_2_ = bf16[4,12288]{1,0:T(4,128)(2,1)S(1)} collective-permute-done((bf16[4,12288]{1,0:T(4,128)(2,1)}, bf16[4,12288]{1,0:T(4,128)(2,1)S(1)}, u32[]{:S(2)}, u32[]{:S(2)}) %collective-permute-start) | collective-permute-done | bytes 98336 | tf_op jit(solution)/shard_map/ppermute | solution.py:183
  14.8 1.7 %collective-permute-start.1 = (bf16[4,12288]{1,0:T(4,128)(2,1)S(1)}, bf16[4,12288]{1,0:T(4,128)(2,1)S(1)}, u32[]{:S(2)}, u32[]{:S(2)}) collective-permute-start(bf16[4,12288]{1,0:T(4,128)(2,1)S(1)} %collective-permute-done.refs_2_), channel_id=1, source_target_pairs={{0,2},{1,3},{2,0},{3,1},{4,6},{5,7},{6,4},{7,5},{8,10},{9,11},{10,... | collective-permute-start | bytes 294920 | tf_op jit(solution)/shard_map/ppermute | solution.py:186
  16.8 3.4 %shard_map.118 = (bf16[4,12288]{1,0:T(4,128)(2,1)S(1)}, f32[1,12288]{1,0:T(1,128)S(1)}, f32[1,12288]{1,0:T(1,128)S(1)}, bf16[768,512]{1,0:T(8,128)(2,1)S(1)}, bf...) custom-call(bf16[4,12288]{1,0:T(4,128)(2,1)} %refs_0_, ...), custom_call_target="tpu_custom_call" | custom-call | bytes 8388608 | tf_op jit(solution)/shard_map/pallas_call | solution.py:215
  20.2 0.8 %shard_map.119 = (bf16[16,12288]{1,0:T(8,128)(2,1)S(1)}, bf16[8,12288]{1,0:T(8,128)(2,1)S(1)}) custom-call(bf16[4,12288]{1,0:T(4,128)(2,1)S(1)} %get-tuple-element.61.refs_0_, bf16[4,12288]{1,0:T(4,128)(2,1)S(1)} %collective-permute-done.4.refs_1_, bf16[4,12288]{1,0:T(4,128)(2,1)S(1)} %collective-permute-done.refs_2_, ...), custom_call_target="tpu_custom_call" | custom-call | bytes 4194304 | tf_op jit(solution)/shard_map/pallas_call | solution.py:231
  21.0 1.0 %collective-permute-done.3.refs_1_ = bf16[4,12288]{1,0:T(4,128)(2,1)S(1)} collective-permute-done((bf16[4,12288]{1,0:T(4,128)(2,1)S(1)}, bf16[4,12288]{1,0:T(4,128)(2,1)S(1)}, u32[]{:S(2)}, u32[]{:S(2)}) %collective-permute-start.3) | collective-permute-done | bytes 98336 | tf_op jit(solution)/shard_map/ppermute | solution.py:186
  22.1 0.8 %shard_map.120 = (bf16[16,12288]{1,0:T(8,128)(2,1)S(1)}, f32[32,512]{1,0:T(8,128)S(1)}, bf16[32,512]{1,0:T(8,128)(2,1)S(1)}, bf16[32,512]{1,0:T(8,128)(2,1)S(1)}, bf16[32,512]{1,0:T(8,128)(2,1)S(1)}) custom-call(s32[1]{0:T(128)} %bitcast.place, bf16[4,12288]{1,0:T(4,128)(2,1)S(1)} %collective-permute-done.1.refs_0_, ...), custom_call_target="tpu_custom_call" | custom-call | bytes 4194304 | tf_op jit(solution)/shard_map/pallas_call | solution.py:239
  22.9 3.9 %collective-permute-start.10 = (bf16[32,512]{1,0:T(8,128)(2,1)S(1)}, bf16[32,512]{1,0:T(8,128)(2,1)S(1)}, u32[]{:S(2)}, u32[]{:S(2)}) collective-permute-start(bf16[32,512]{1,0:T(8,128)(2,1)S(1)} %get-tuple-element.72), channel_id=1, source_target_pairs={{0,12},{1,13},{2,14},{3,15},{4,8},{5,9},{6,10},{7,11},{8,4},{9,5},... | collective-permute-start | bytes 98312 | tf_op jit(solution)/shard_map/ppermute | solution.py:183
  26.8 0.6 %collective-permute-start.9 = (bf16[32,512]{1,0:T(8,128)(2,1)S(1)}, bf16[32,512]{1,0:T(8,128)(2,1)S(1)}, u32[]{:S(2)}, u32[]{:S(2)}) collective-permute-start(bf16[32,512]{1,0:T(8,128)(2,1)S(1)} %get-tuple-element.71), channel_id=1, source_target_pairs={{0,4},{1,5},{2,6},{3,7},{4,0},{5,1},{6,2},{7,3},{8,12},{9,13},{10,... | collective-permute-start | bytes 98312 | tf_op jit(solution)/shard_map/ppermute | solution.py:183
  27.4 1.3 %collective-permute-done.10.refs_1_ = bf16[32,512]{1,0:T(8,128)(2,1)S(1)} collective-permute-done((bf16[32,512]{1,0:T(8,128)(2,1)S(1)}, bf16[32,512]{1,0:T(8,128)(2,1)S(1)}, u32[]{:S(2)}, u32[]{:S(2)}) %collective-permute-start.10) | collective-permute-done | bytes 32800 | tf_op jit(solution)/shard_map/ppermute | solution.py:183
  28.7 2.9 %collective-permute-done.11.refs_2_ = bf16[32,512]{1,0:T(8,128)(2,1)S(1)} collective-permute-done((bf16[32,512]{1,0:T(8,128)(2,1)S(1)}, bf16[32,512]{1,0:T(8,128)(2,1)S(1)}, u32[]{:S(2)}, u32[]{:S(2)}) %collective-permute-start.11) | collective-permute-done | bytes 32800 | tf_op jit(solution)/shard_map/ppermute | solution.py:183
  31.6 1.6 %collective-permute-start.15 = (bf16[32,512]{1,0:T(8,128)(2,1)S(1)}, bf16[32,512]{1,0:T(8,128)(2,1)S(1)}, u32[]{:S(2)}, u32[]{:S(2)}) collective-permute-start(bf16[32,512]{1,0:T(8,128)(2,1)S(1)} %get-tuple-element.84), channel_id=1, source_target_pairs={{0,2},{1,3},{2,0},{3,1},{4,6},{5,7},{6,4},{7,5},{8,10},{9,11},{10,... | collective-permute-start | bytes 98312 | tf_op jit(solution)/shard_map/ppermute | solution.py:186
  33.2 1.2 %shard_map.122.act = bf16[32,256]{1,0:T(8,128)(2,1)S(1)} custom-call(bf16[16,12288]{1,0:T(8,128)(2,1)S(1)} %get-tuple-element.66.refs_2_.near, bf16[16,12288]{1,0:T(8,128)(2,1)S(1)} %get-tuple-element.77.far, bf16[12288,128]{1,0:T(8,128)(2,1)S(1)} %get-tuple-element.78.w_own, bf16[12288,128]{1,0:T(8,128)(2,1)S(1)} %collective-permute-done.12.w_mate, ...), custom_call_target="tpu_custom_call" | custom-call | bytes 4194304 | tf_op jit(solution)/shard_map/pallas_call | solution.py:249
  34.5 1.2 %shard_map.123.part = f32[32,12288]{1,0:T(8,128)S(1)} custom-call(bf16[32,256]{1,0:T(8,128)(2,1)S(1)} %shard_map.122.act, bf16[128,12288]{1,0:T(8,128)(2,1)S(1)} %get-tuple-element.82.w_own, bf16[128,12288]{1,0:T(8,128)(2,1)S(1)} %collective-permute-done.14.w_mate), custom_call_target="tpu_custom_call" | custom-call | bytes 6291456 | tf_op jit(solution)/shard_map/pallas_call | solution.py:264
  36.1 1.5 %collective-permute-start.21 = (bf16[4,12288]{1,0:T(4,128)(2,1)S(1)}, bf16[4,12288]{1,0:T(4,128)(2,1)S(1)}, u32[]{:S(2)}, u32[]{:S(2)}) collective-permute-start(bf16[4,12288]{1,0:T(4,128)(2,1)S(1)} %get-tuple-element.92), channel_id=1, source_target_pairs={{0,2},{1,3},{2,0},{3,1},{4,6},{5,7},{6,4},{7,5},{8,10},{9,11},{10,... | collective-permute-start | bytes 294920 | tf_op jit(solution)/shard_map/ppermute | solution.py:186
  37.7 0.6 %collective-permute-start.19 = (bf16[4,12288]{1,0:T(4,128)(2,1)S(1)}, bf16[4,12288]{1,0:T(4,128)(2,1)S(1)}, u32[]{:S(2)}, u32[]{:S(2)}) collective-permute-start(bf16[4,12288]{1,0:T(4,128)(2,1)S(1)} %get-tuple-element.90), channel_id=1, source_target_pairs={{0,2},{1,3},{2,0},{3,1},{4,6},{5,7},{6,4},{7,5},{8,10},{9,11},{10,... | collective-permute-start | bytes 294920 | tf_op jit(solution)/shard_map/ppermute | solution.py:186
  38.2 1.5 %collective-permute-start.17 = (bf16[4,12288]{1,0:T(4,128)(2,1)S(1)}, bf16[4,12288]{1,0:T(4,128)(2,1)S(1)}, u32[]{:S(2)}, u32[]{:S(2)}) collective-permute-start(bf16[4,12288]{1,0:T(4,128)(2,1)S(1)} %get-tuple-element.88), channel_id=1, source_target_pairs={{0,2},{1,3},{2,0},{3,1},{4,6},{5,7},{6,4},{7,5},{8,10},{9,11},{10,... | collective-permute-start | bytes 294920 | tf_op jit(solution)/shard_map/ppermute | solution.py:186
  39.7 0.6 %collective-permute-start.16 = (bf16[4,12288]{1,0:T(4,128)(2,1)S(1)}, bf16[4,12288]{1,0:T(4,128)(2,1)S(1)}, u32[]{:S(2)}, u32[]{:S(2)}) collective-permute-start(bf16[4,12288]{1,0:T(4,128)(2,1)S(1)} %get-tuple-element.86), channel_id=1, source_target_pairs={{0,2},{1,3},{2,0},{3,1},{4,6},{5,7},{6,4},{7,5},{8,10},{9,11},{10,... | collective-permute-start | bytes 294920 | tf_op jit(solution)/shard_map/ppermute | solution.py:186
  40.3 1.7 %collective-permute-done.21 = bf16[4,12288]{1,0:T(4,128)(2,1)S(1)} collective-permute-done((bf16[4,12288]{1,0:T(4,128)(2,1)S(1)}, bf16[4,12288]{1,0:T(4,128)(2,1)S(1)}, u32[]{:S(2)}, u32[]{:S(2)}) %collective-permute-start.21) | collective-permute-done | bytes 98336 | tf_op jit(solution)/shard_map/ppermute | solution.py:186
  42.0 1.5 %collective-permute-start.22 = (bf16[4,12288]{1,0:T(4,128)(2,1)S(1)}, bf16[4,12288]{1,0:T(4,128)(2,1)S(1)}, u32[]{:S(2)}, u32[]{:S(2)}) collective-permute-start(bf16[4,12288]{1,0:T(4,128)(2,1)S(1)} %add_convert_fusion), channel_id=1, source_target_pairs={{0,12},{1,13},{2,14},{3,15},{4,8},{5,9},{6,10},{7,11},{8,4},{9,5},... | collective-permute-start | bytes 294920 | tf_op jit(solution)/shard_map/ppermute | solution.py:183
  43.6 1.7 %collective-permute-start.20 = (bf16[4,12288]{1,0:T(4,128)(2,1)S(1)}, bf16[4,12288]{1,0:T(4,128)(2,1)S(1)}, u32[]{:S(2)}, u32[]{:S(2)}) collective-permute-start(bf16[4,12288]{1,0:T(4,128)(2,1)S(1)} %add_convert_fusion.1), channel_id=1, source_target_pairs={{0,8},{1,9},{2,10},{3,11},{4,12},{5,13},{6,14},{7,15},{8,0},{9,1},... | collective-permute-start | bytes 294920 | tf_op jit(solution)/shard_map/ppermute | solution.py:183
  45.3 1.3 %collective-permute-start.18 = (bf16[4,12288]{1,0:T(4,128)(2,1)S(1)}, bf16[4,12288]{1,0:T(4,128)(2,1)S(1)}, u32[]{:S(2)}, u32[]{:S(2)}) collective-permute-start(bf16[4,12288]{1,0:T(4,128)(2,1)S(1)} %add_convert_fusion.2), channel_id=1, source_target_pairs={{0,4},{1,5},{2,6},{3,7},{4,0},{5,1},{6,2},{7,3},{8,12},{9,13},{10,... | collective-permute-start | bytes 294920 | tf_op jit(solution)/shard_map/ppermute | solution.py:183
  46.8 1.8 %collective-permute-done.22.refs_3_ = bf16[4,12288]{1,0:T(4,128)(2,1)S(1)} collective-permute-done((bf16[4,12288]{1,0:T(4,128)(2,1)S(1)}, bf16[4,12288]{1,0:T(4,128)(2,1)S(1)}, u32[]{:S(2)}, u32[]{:S(2)}) %collective-permute-start.22) | collective-permute-done | bytes 98336 | tf_op jit(solution)/shard_map/ppermute | solution.py:183
  48.5 2.2 %collective-permute-done.20.refs_2_ = bf16[4,12288]{1,0:T(4,128)(2,1)S(1)} collective-permute-done((bf16[4,12288]{1,0:T(4,128)(2,1)S(1)}, bf16[4,12288]{1,0:T(4,128)(2,1)S(1)}, u32[]{:S(2)}, u32[]{:S(2)}) %collective-permute-start.20) | collective-permute-done | bytes 98336 | tf_op jit(solution)/shard_map/ppermute | solution.py:183
  50.9 0.7 %shard_map.125 = bf16[4,12288]{1,0:T(4,128)(2,1)} custom-call(f32[4,12288]{1,0:T(4,128)S(1)} %convert_add_fusion.refs_0_, bf16[4,12288]{1,0:T(4,128)(2,1)S(1)} %collective-permute-done.18.refs_1_, bf16[4,12288]{1,0:T(4,128)(2,1)S(1)} %collective-permute-done.20.refs_2_, bf16[4,12288]{1,0:T(4,128)(2,1)S(1)} %collective-permute-done.22.refs_3_), custom_call_target="tpu_custom_call" | custom-call | bytes 2097152 | tf_op jit(solution)/shard_map/pallas_call | solution.py:285
  (43 shorter events, 3.2 us)
Async XLA Ops:
  0.0 14.3 %collective-permute-start.12 = (bf16[12288,128]{1,0:T(8,128)(2,1)}, bf16[12288,128]{1,0:T(8,128)(2,1)S(1)}, u32[]{:S(2)}, u32[]{:S(2)}) collective-permute-start(bf16[12288,128]{1,0:T(8,128)(2,1)} %refs_4_), channel_id=1, source_target_pairs={{0,1},{1,0},{2,3},{3,2},{4,5},{5,4},{6,7},{7,6},{8,9},{9,8},{10,11... | collective-permute-start | bytes 9437192 | tf_op jit(solution)/shard_map/ppermute | solution.py:189
  0.5 8.4 %collective-permute-start.4 = (bf16[4,12288]{1,0:T(4,128)(2,1)}, bf16[4,12288]{1,0:T(4,128)(2,1)S(1)}, u32[]{:S(2)}, u32[]{:S(2)}) collective-permute-start(bf16[4,12288]{1,0:T(4,128)(2,1)} %refs_0_), channel_id=1, source_target_pairs={{0,4},{1,5},{2,6},{3,7},{4,0},{5,1},{6,2},{7,3},{8,12},{9,13},{10,... | collective-permute-start | bytes 294920 | tf_op jit(solution)/shard_map/ppermute | solution.py:183
  3.0 11.0 %collective-permute-start = (bf16[4,12288]{1,0:T(4,128)(2,1)}, bf16[4,12288]{1,0:T(4,128)(2,1)S(1)}, u32[]{:S(2)}, u32[]{:S(2)}) collective-permute-start(bf16[4,12288]{1,0:T(4,128)(2,1)} %refs_0_), channel_id=1, source_target_pairs={{0,8},{1,9},{2,10},{3,11},{4,12},{5,13},{6,14},{7,15},{8,0},{9,1},... | collective-permute-start | bytes 294920 | tf_op jit(solution)/shard_map/ppermute | solution.py:183
  5.6 8.4 %collective-permute-start.2 = (bf16[4,12288]{1,0:T(4,128)(2,1)}, bf16[4,12288]{1,0:T(4,128)(2,1)S(1)}, u32[]{:S(2)}, u32[]{:S(2)}) collective-permute-start(bf16[4,12288]{1,0:T(4,128)(2,1)} %refs_0_), channel_id=1, source_target_pairs={{0,12},{1,13},{2,14},{3,15},{4,8},{5,9},{6,10},{7,11},{8,4},{9,5},... | collective-permute-start | bytes 294920 | tf_op jit(solution)/shard_map/ppermute | solution.py:183
  5.6 1.3 %collective-permute-start.5 = (f32[1,128]{1,0:T(1,128)}, f32[1,128]{1,0:T(1,128)S(1)}, u32[]{:S(2)}, u32[]{:S(2)}) collective-permute-start(f32[1,128]{1,0:T(1,128)} %bitcast.12), channel_id=1, source_target_pairs={{0,1},{1,0},{2,3},{3,2},{4,5},{5,4},{6,7},{7,6},{8,9},{9,8},{10,11... | collective-permute-start | bytes 1544 | tf_op jit(solution)/shard_map/ppermute | solution.py:189
  6.9 5.4 %collective-permute-start.6 = (bf16[4,12288]{1,0:T(4,128)(2,1)}, bf16[4,12288]{1,0:T(4,128)(2,1)S(1)}, u32[]{:S(2)}, u32[]{:S(2)}) collective-permute-start(bf16[4,12288]{1,0:T(4,128)(2,1)} %refs_0_), channel_id=1, source_target_pairs={{0,2},{1,3},{2,0},{3,1},{4,6},{5,7},{6,4},{7,5},{8,10},{9,11},{10,... | collective-permute-start | bytes 294920 | tf_op jit(solution)/shard_map/ppermute | solution.py:186
  9.6 4.6 %collective-permute-start.7 = (bf16[4,12288]{1,0:T(4,128)(2,1)S(1)}, bf16[4,12288]{1,0:T(4,128)(2,1)S(1)}, u32[]{:S(2)}, u32[]{:S(2)}) collective-permute-start(bf16[4,12288]{1,0:T(4,128)(2,1)S(1)} %collective-permute-done.4.refs_1_), channel_id=1, source_target_pairs={{0,2},{1,3},{2,0},{3,1},{4,6},{5,7},{6,4},{7,5},{8,10},{9,11},{10,... | collective-permute-start | bytes 294920 | tf_op jit(solution)/shard_map/ppermute | solution.py:186
  14.3 20.2 %collective-permute-start.14 = (bf16[128,12288]{1,0:T(8,128)(2,1)}, bf16[128,12288]{1,0:T(8,128)(2,1)S(1)}, u32[]{:S(2)}, u32[]{:S(2)}) collective-permute-start(bf16[128,12288]{1,0:T(8,128)(2,1)} %refs_5_), channel_id=1, source_target_pairs={{0,1},{1,0},{2,3},{3,2},{4,5},{5,4},{6,7},{7,6},{8,9},{9,8},{10,11... | collective-permute-start | bytes 9437192 | tf_op jit(solution)/shard_map/ppermute | solution.py:189
  14.3 7.8 %collective-permute-start.8 = (bf16[768,512]{1,0:T(8,128)(2,1)}, bf16[768,512]{1,0:T(8,128)(2,1)S(1)}, u32[]{:S(2)}, u32[]{:S(2)}) collective-permute-start(bf16[768,512]{1,0:T(8,128)(2,1)} %refs_3_), channel_id=1, source_target_pairs={{0,1},{1,0},{2,3},{3,2},{4,5},{5,4},{6,7},{7,6},{8,9},{9,8},{10,11... | collective-permute-start | bytes 2359304 | tf_op jit(solution)/shard_map/ppermute | solution.py:189
  14.8 20.9 %collective-permute-start.13 = (bf16[512,768]{1,0:T(8,128)(2,1)}, bf16[512,768]{1,0:T(8,128)(2,1)S(1)}, u32[]{:S(2)}, u32[]{:S(2)}) collective-permute-start(bf16[512,768]{1,0:T(8,128)(2,1)} %refs_6_), channel_id=1, source_target_pairs={{0,1},{1,0},{2,3},{3,2},{4,5},{5,4},{6,7},{7,6},{8,9},{9,8},{10,11... | collective-permute-start | bytes 2359304 | tf_op jit(solution)/shard_map/ppermute | solution.py:189
  14.8 6.3 %collective-permute-start.1 = (bf16[4,12288]{1,0:T(4,128)(2,1)S(1)}, bf16[4,12288]{1,0:T(4,128)(2,1)S(1)}, u32[]{:S(2)}, u32[]{:S(2)}) collective-permute-start(bf16[4,12288]{1,0:T(4,128)(2,1)S(1)} %collective-permute-done.refs_2_), channel_id=1, source_target_pairs={{0,2},{1,3},{2,0},{3,1},{4,6},{5,7},{6,4},{7,5},{8,10},{9,11},{10,... | collective-permute-start | bytes 294920 | tf_op jit(solution)/shard_map/ppermute | solution.py:186
  16.5 5.6 %collective-permute-start.3 = (bf16[4,12288]{1,0:T(4,128)(2,1)S(1)}, bf16[4,12288]{1,0:T(4,128)(2,1)S(1)}, u32[]{:S(2)}, u32[]{:S(2)}) collective-permute-start(bf16[4,12288]{1,0:T(4,128)(2,1)S(1)} %collective-permute-done.2.refs_3_), channel_id=1, source_target_pairs={{0,2},{1,3},{2,0},{3,1},{4,6},{5,7},{6,4},{7,5},{8,10},{9,11},{10,... | collective-permute-start | bytes 294920 | tf_op jit(solution)/shard_map/ppermute | solution.py:186
  20.2 13.0 %copy-start.1 = (f32[128]{0:T(128)S(1)}, f32[128]{0:T(128)}, u32[]{:S(2)}) copy-start(f32[128]{0:T(128)} %param.19) | copy-start | bytes 1540
  22.9 5.8 %collective-permute-start.10 = (bf16[32,512]{1,0:T(8,128)(2,1)S(1)}, bf16[32,512]{1,0:T(8,128)(2,1)S(1)}, u32[]{:S(2)}, u32[]{:S(2)}) collective-permute-start(bf16[32,512]{1,0:T(8,128)(2,1)S(1)} %get-tuple-element.72), channel_id=1, source_target_pairs={{0,12},{1,13},{2,14},{3,15},{4,8},{5,9},{6,10},{7,11},{8,4},{9,5},... | collective-permute-start | bytes 98312 | tf_op jit(solution)/shard_map/ppermute | solution.py:183
  26.8 4.8 %collective-permute-start.11 = (bf16[32,512]{1,0:T(8,128)(2,1)S(1)}, bf16[32,512]{1,0:T(8,128)(2,1)S(1)}, u32[]{:S(2)}, u32[]{:S(2)}) collective-permute-start(bf16[32,512]{1,0:T(8,128)(2,1)S(1)} %get-tuple-element.73), channel_id=1, source_target_pairs={{0,8},{1,9},{2,10},{3,11},{4,12},{5,13},{6,14},{7,15},{8,0},{9,1},... | collective-permute-start | bytes 98312 | tf_op jit(solution)/shard_map/ppermute | solution.py:183
  26.8 4.8 %collective-permute-start.9 = (bf16[32,512]{1,0:T(8,128)(2,1)S(1)}, bf16[32,512]{1,0:T(8,128)(2,1)S(1)}, u32[]{:S(2)}, u32[]{:S(2)}) collective-permute-start(bf16[32,512]{1,0:T(8,128)(2,1)S(1)} %get-tuple-element.71), channel_id=1, source_target_pairs={{0,4},{1,5},{2,6},{3,7},{4,0},{5,1},{6,2},{7,3},{8,12},{9,13},{10,... | collective-permute-start | bytes 98312 | tf_op jit(solution)/shard_map/ppermute | solution.py:183
  31.6 4.0 %collective-permute-start.15 = (bf16[32,512]{1,0:T(8,128)(2,1)S(1)}, bf16[32,512]{1,0:T(8,128)(2,1)S(1)}, u32[]{:S(2)}, u32[]{:S(2)}) collective-permute-start(bf16[32,512]{1,0:T(8,128)(2,1)S(1)} %get-tuple-element.84), channel_id=1, source_target_pairs={{0,2},{1,3},{2,0},{3,1},{4,6},{5,7},{6,4},{7,5},{8,10},{9,11},{10,... | collective-permute-start | bytes 98312 | tf_op jit(solution)/shard_map/ppermute | solution.py:186
  34.4 1.2 %copy-start = (f32[512]{0:T(512)S(1)}, f32[512]{0:T(512)}, u32[]{:S(2)}) copy-start(f32[512]{0:T(512)} %param.22) | copy-start | bytes 6148
  36.1 5.8 %collective-permute-start.21 = (bf16[4,12288]{1,0:T(4,128)(2,1)S(1)}, bf16[4,12288]{1,0:T(4,128)(2,1)S(1)}, u32[]{:S(2)}, u32[]{:S(2)}) collective-permute-start(bf16[4,12288]{1,0:T(4,128)(2,1)S(1)} %get-tuple-element.92), channel_id=1, source_target_pairs={{0,2},{1,3},{2,0},{3,1},{4,6},{5,7},{6,4},{7,5},{8,10},{9,11},{10,... | collective-permute-start | bytes 294920 | tf_op jit(solution)/shard_map/ppermute | solution.py:186
  37.7 5.9 %collective-permute-start.19 = (bf16[4,12288]{1,0:T(4,128)(2,1)S(1)}, bf16[4,12288]{1,0:T(4,128)(2,1)S(1)}, u32[]{:S(2)}, u32[]{:S(2)}) collective-permute-start(bf16[4,12288]{1,0:T(4,128)(2,1)S(1)} %get-tuple-element.90), channel_id=1, source_target_pairs={{0,2},{1,3},{2,0},{3,1},{4,6},{5,7},{6,4},{7,5},{8,10},{9,11},{10,... | collective-permute-start | bytes 294920 | tf_op jit(solution)/shard_map/ppermute | solution.py:186
  38.2 7.1 %collective-permute-start.17 = (bf16[4,12288]{1,0:T(4,128)(2,1)S(1)}, bf16[4,12288]{1,0:T(4,128)(2,1)S(1)}, u32[]{:S(2)}, u32[]{:S(2)}) collective-permute-start(bf16[4,12288]{1,0:T(4,128)(2,1)S(1)} %get-tuple-element.88), channel_id=1, source_target_pairs={{0,2},{1,3},{2,0},{3,1},{4,6},{5,7},{6,4},{7,5},{8,10},{9,11},{10,... | collective-permute-start | bytes 294920 | tf_op jit(solution)/shard_map/ppermute | solution.py:186
  39.7 7.0 %collective-permute-start.16 = (bf16[4,12288]{1,0:T(4,128)(2,1)S(1)}, bf16[4,12288]{1,0:T(4,128)(2,1)S(1)}, u32[]{:S(2)}, u32[]{:S(2)}) collective-permute-start(bf16[4,12288]{1,0:T(4,128)(2,1)S(1)} %get-tuple-element.86), channel_id=1, source_target_pairs={{0,2},{1,3},{2,0},{3,1},{4,6},{5,7},{6,4},{7,5},{8,10},{9,11},{10,... | collective-permute-start | bytes 294920 | tf_op jit(solution)/shard_map/ppermute | solution.py:186
  42.0 6.5 %collective-permute-start.22 = (bf16[4,12288]{1,0:T(4,128)(2,1)S(1)}, bf16[4,12288]{1,0:T(4,128)(2,1)S(1)}, u32[]{:S(2)}, u32[]{:S(2)}) collective-permute-start(bf16[4,12288]{1,0:T(4,128)(2,1)S(1)} %add_convert_fusion), channel_id=1, source_target_pairs={{0,12},{1,13},{2,14},{3,15},{4,8},{5,9},{6,10},{7,11},{8,4},{9,5},... | collective-permute-start | bytes 294920 | tf_op jit(solution)/shard_map/ppermute | solution.py:183
  43.6 7.1 %collective-permute-start.20 = (bf16[4,12288]{1,0:T(4,128)(2,1)S(1)}, bf16[4,12288]{1,0:T(4,128)(2,1)S(1)}, u32[]{:S(2)}, u32[]{:S(2)}) collective-permute-start(bf16[4,12288]{1,0:T(4,128)(2,1)S(1)} %add_convert_fusion.1), channel_id=1, source_target_pairs={{0,8},{1,9},{2,10},{3,11},{4,12},{5,13},{6,14},{7,15},{8,0},{9,1},... | collective-permute-start | bytes 294920 | tf_op jit(solution)/shard_map/ppermute | solution.py:183
  45.3 5.5 %collective-permute-start.18 = (bf16[4,12288]{1,0:T(4,128)(2,1)S(1)}, bf16[4,12288]{1,0:T(4,128)(2,1)S(1)}, u32[]{:S(2)}, u32[]{:S(2)}) collective-permute-start(bf16[4,12288]{1,0:T(4,128)(2,1)S(1)} %add_convert_fusion.2), channel_id=1, source_target_pairs={{0,4},{1,5},{2,6},{3,7},{4,0},{5,1},{6,2},{7,3},{8,12},{9,13},{10,... | collective-permute-start | bytes 294920 | tf_op jit(solution)/shard_map/ppermute | solution.py:183

commit v24 on v21

--- a/solution.py
+++ b/solution.py
@@ -82,8 +82,8 @@
     )
     half = near.shape[0]
     total[...] = sums
-    message[:half, :] = sums[half:].astype(bf16)
-    message[half:, :] = sums[:half].astype(bf16)
+    message[:half, :] = sums[half:]
+    message[half:, :] = sums[:half]
 
 
 def turn(x, groups, bit):
@@ -93,17 +93,17 @@
 
 
 def merge_body(groups, total, got, out, *messages):
-    sums = total[...] + got[...].astype(f32)
+    sums = total[...] + got[...]
     out[...] = sums
     for k in range(1, groups):
-        messages[k - 1][...] = turn(sums, groups, k).astype(bf16)
+        messages[k - 1][...] = turn(sums, groups, k)
 
 
 def up_body(groups, place, total, bias, own, mate, part, *refs):
     got, outs = refs[: groups - 1], refs[groups - 1 :]
     sums = total[...]
     for g in got:
-        sums = sums + g[...].astype(f32)
+        sums = sums + g[...]
     hidden = jnp.maximum(sums + bias[...], 0.0).astype(bf16)
     core = place[0] % 2
     mine = jnp.dot(hidden, own[...], preferred_element_type=f32)
@@ -238,7 +238,7 @@
     )(*held, *beyond[:soon], gain, shift)
     far, total, message = call(
         functools.partial(norm_body, groups - soon),
-        [shape(some, width), shape(rows, rank, dtype=f32), shape(rows, rank)],
+        [shape(some, width), shape(rows, rank, dtype=f32), shape(rows, rank, dtype=f32)],
         [SMEM] + [VMEM] * (groups - soon + 6),
         16,
         (),
@@ -256,7 +256,7 @@
     )(normed, far, w_in, w_in_mate, bias, bias_mate, mask)[0]
     total, *messages = call(
         functools.partial(merge_body, groups),
-        [shape(rows, rank, dtype=f32)] + [shape(rows, rank)] * (groups - 1),
+        [shape(rows, rank, dtype=f32)] * groups,
         [VMEM] * 2,
         16,
     )(total, got)

time: 51.1 us -> 52.1 us (1.020)
  waiting for transfers between devices: 13.9 us -> 14.9 us
    ppermute x9, waiting for transfers between devices: 5.61 us -> 6.18 us  [beside(): return lax.ppermute(x, 'blk', [(i, i ^ 2) for i in range(devices)])]
  transfers between devices with their start and end apart: 23 -> 23, of which waited for: 10 -> 10; matrix products, arithmetic and copies ran while one was open for 6% -> 6% of each run, Pallas kernels for 15% -> 14%
where the time goes in v24:
time: 52.1 us; the launch traced here: 51.9 us
  starting transfers between devices  25.2 us (48%)
  waiting for transfers between devices  14.9 us (29%)
  Pallas kernels  8.58 us (16%)
  other arithmetic  2.23 us (4%)
  local copies, waits for them, and re-layouts  0.86 us (2%)
    ppermute x9, starting transfers between devices, across(): return lax.ppermute(x, 'blk', [(i, i ^ 4 * k) for i in range(devices)])  14.3 us
    ppermute x9, starting transfers between devices, beside(): return lax.ppermute(x, 'blk', [(i, i ^ 2) for i in range(devices)])  9.96 us
    ppermute x9, waiting for transfers between devices, across(): return lax.ppermute(x, 'blk', [(i, i ^ 4 * k) for i in range(devices)])  7.59 us
    ppermute x9, waiting for transfers between devices, beside(): return lax.ppermute(x, 'blk', [(i, i ^ 2) for i in range(devices)])  6.18 us
    pallas_call x1, Pallas kernels, shards(): call(functools.partial(load_body, len(near)), [shape(*x.shape, dtype=x.dt...  3.39 us
    pallas_call x1, Pallas kernels, shards(): call(functools.partial(act_body, step), [shape(rows, 2 * block)], [VMEM]...  1.21 us
    pallas_call x1, Pallas kernels, shards(): call(functools.partial(part_body, step), [shape(rows, width, dtype=f32)],...  1.19 us
    ppermute x5, waiting for transfers between devices, core(): return lax.ppermute(x, 'blk', [(i, i ^ 1) for i in range(devices)])  1.1 us
  transfers between devices with their start and end apart: 23, of which 10 were waited for; matrix products, arithmetic and copies ran while one was open for 6% of the time, Pallas kernels for 14%

profile of v24, /device:TPU:0, one launch (start us, length us, event | category | flops | bytes accessed | tf_op | source)
XLA Modules:
  0.0 51.9 jit_solution(12305339267597489071)
XLA Ops:
  0.5 2.6 %collective-permute-start.4 = (bf16[4,12288]{1,0:T(4,128)(2,1)}, bf16[4,12288]{1,0:T(4,128)(2,1)S(1)}, u32[]{:S(2)}, u32[]{:S(2)}) collective-permute-start(bf16[4,12288]{1,0:T(4,128)(2,1)} %refs_0_), channel_id=1, source_target_pairs={{0,4},{1,5},{2,6},{3,7},{4,0},{5,1},{6,2},{7,3},{8,12},{9,13},{10,... | collective-permute-start | bytes 294920 | tf_op jit(solution)/shard_map/ppermute | solution.py:183
  3.0 2.6 %collective-permute-start = (bf16[4,12288]{1,0:T(4,128)(2,1)}, bf16[4,12288]{1,0:T(4,128)(2,1)S(1)}, u32[]{:S(2)}, u32[]{:S(2)}) collective-permute-start(bf16[4,12288]{1,0:T(4,128)(2,1)} %refs_0_), channel_id=1, source_target_pairs={{0,8},{1,9},{2,10},{3,11},{4,12},{5,13},{6,14},{7,15},{8,0},{9,1},... | collective-permute-start | bytes 294920 | tf_op jit(solution)/shard_map/ppermute | solution.py:183
  5.8 1.1 %collective-permute-done.5.b_mate = f32[1,128]{1,0:T(1,128)S(1)} collective-permute-done((f32[1,128]{1,0:T(1,128)}, f32[1,128]{1,0:T(1,128)S(1)}, u32[]{:S(2)}, u32[]{:S(2)}) %collective-permute-start.5) | collective-permute-done | bytes 544 | tf_op jit(solution)/shard_map/ppermute | solution.py:189
  6.9 2.0 %collective-permute-start.6 = (bf16[4,12288]{1,0:T(4,128)(2,1)}, bf16[4,12288]{1,0:T(4,128)(2,1)S(1)}, u32[]{:S(2)}, u32[]{:S(2)}) collective-permute-start(bf16[4,12288]{1,0:T(4,128)(2,1)} %refs_0_), channel_id=1, source_target_pairs={{0,2},{1,3},{2,0},{3,1},{4,6},{5,7},{6,4},{7,5},{8,10},{9,11},{10,... | collective-permute-start | bytes 294920 | tf_op jit(solution)/shard_map/ppermute | solution.py:186
  8.8 0.8 %copy.13 = s32[4,6]{0,1:T(8,128)S(1)} copy(s32[4,6]{1,0:T(4,128)} %param.15) | data formatting | bytes 192 | tf_op jit(solution)/shard_map/optimization_barrier | solution.py:199
  9.7 0.7 %fusion.1 = s32[4,6]{0,1:T(8,128)S(1)} fusion(s32[4]{0:T(128)} %param.16), kind=kLoop, calls=%fused_computation.12 | loop fusion | flops 48 | bytes 112 | tf_op jit(solution)/shard_map/convert_element_type | solution.py:150
  10.4 0.7 %fusion = s32[16,16]{1,0:T(8,128)S(1)} fusion(s32[16]{0:T(128)} %param.17), kind=kLoop, calls=%fused_computation.10 | loop fusion | flops 512 | bytes 1088 | tf_op jit(solution)/shard_map/convert_element_type | solution.py:153
  11.6 0.7 %collective-permute-done.6.refs_4_ = bf16[4,12288]{1,0:T(4,128)(2,1)S(1)} collective-permute-done((bf16[4,12288]{1,0:T(4,128)(2,1)}, bf16[4,12288]{1,0:T(4,128)(2,1)S(1)}, u32[]{:S(2)}, u32[]{:S(2)}) %collective-permute-start.6) | collective-permute-done | bytes 98336 | tf_op jit(solution)/shard_map/ppermute | solution.py:186
  12.3 1.7 %collective-permute-done.refs_2_ = bf16[4,12288]{1,0:T(4,128)(2,1)S(1)} collective-permute-done((bf16[4,12288]{1,0:T(4,128)(2,1)}, bf16[4,12288]{1,0:T(4,128)(2,1)S(1)}, u32[]{:S(2)}, u32[]{:S(2)}) %collective-permute-start) | collective-permute-done | bytes 98336 | tf_op jit(solution)/shard_map/ppermute | solution.py:183
  14.8 1.7 %collective-permute-start.1 = (bf16[4,12288]{1,0:T(4,128)(2,1)S(1)}, bf16[4,12288]{1,0:T(4,128)(2,1)S(1)}, u32[]{:S(2)}, u32[]{:S(2)}) collective-permute-start(bf16[4,12288]{1,0:T(4,128)(2,1)S(1)} %collective-permute-done.refs_2_), channel_id=1, source_target_pairs={{0,2},{1,3},{2,0},{3,1},{4,6},{5,7},{6,4},{7,5},{8,10},{9,11},{10,... | collective-permute-start | bytes 294920 | tf_op jit(solution)/shard_map/ppermute | solution.py:186
  16.8 3.4 %shard_map.118 = (bf16[4,12288]{1,0:T(4,128)(2,1)S(1)}, f32[1,12288]{1,0:T(1,128)S(1)}, f32[1,12288]{1,0:T(1,128)S(1)}, bf16[768,512]{1,0:T(8,128)(2,1)S(1)}, bf...) custom-call(bf16[4,12288]{1,0:T(4,128)(2,1)} %refs_0_, ...), custom_call_target="tpu_custom_call" | custom-call | bytes 8388608 | tf_op jit(solution)/shard_map/pallas_call | solution.py:215
  20.2 0.8 %shard_map.119 = (bf16[16,12288]{1,0:T(8,128)(2,1)S(1)}, bf16[8,12288]{1,0:T(8,128)(2,1)S(1)}) custom-call(bf16[4,12288]{1,0:T(4,128)(2,1)S(1)} %get-tuple-element.61.refs_0_, bf16[4,12288]{1,0:T(4,128)(2,1)S(1)} %collective-permute-done.4.refs_1_, bf16[4,12288]{1,0:T(4,128)(2,1)S(1)} %collective-permute-done.refs_2_, ...), custom_call_target="tpu_custom_call" | custom-call | bytes 4194304 | tf_op jit(solution)/shard_map/pallas_call | solution.py:231
  21.0 1.0 %collective-permute-done.3.refs_1_ = bf16[4,12288]{1,0:T(4,128)(2,1)S(1)} collective-permute-done((bf16[4,12288]{1,0:T(4,128)(2,1)S(1)}, bf16[4,12288]{1,0:T(4,128)(2,1)S(1)}, u32[]{:S(2)}, u32[]{:S(2)}) %collective-permute-start.3) | collective-permute-done | bytes 98336 | tf_op jit(solution)/shard_map/ppermute | solution.py:186
  22.1 0.8 %shard_map.120 = (bf16[16,12288]{1,0:T(8,128)(2,1)S(1)}, f32[32,512]{1,0:T(8,128)S(1)}, f32[32,512]{1,0:T(8,128)S(1)}) custom-call(s32[1]{0:T(128)} %bitcast.place, bf16[4,12288]{1,0:T(4,128)(2,1)S(1)} %collective-permute-done.1.refs_0_, bf16[4,12288]{1,0:T(4,128)(2,1)S(1)} %collective-permute-done.3.refs_1_, ...), custom_call_target="tpu_custom_call" | custom-call | bytes 4194304 | tf_op jit(solution)/shard_map/pallas_call | solution.py:239
  22.9 1.8 %collective-permute-start.9 = (f32[32,512]{1,0:T(8,128)S(1)}, f32[32,512]{1,0:T(8,128)S(1)}, u32[]{:S(2)}, u32[]{:S(2)}) collective-permute-start(f32[32,512]{1,0:T(8,128)S(1)} %get-tuple-element.71), channel_id=1, source_target_pairs={{0,2},{1,3},{2,0},{3,1},{4,6},{5,7},{6,4},{7,5},{8,10},{9,11},{10,... | collective-permute-start | bytes 196616 | tf_op jit(solution)/shard_map/ppermute | solution.py:186
  24.7 2.5 %collective-permute-done.9.got = f32[32,512]{1,0:T(8,128)S(1)} collective-permute-done((f32[32,512]{1,0:T(8,128)S(1)}, f32[32,512]{1,0:T(8,128)S(1)}, u32[]{:S(2)}, u32[]{:S(2)}) %collective-permute-start.9) | collective-permute-done | bytes 65568 | tf_op jit(solution)/shard_map/ppermute | solution.py:186
  27.2 3.9 %collective-permute-start.13 = (f32[32,512]{1,0:T(8,128)S(1)}, f32[32,512]{1,0:T(8,128)S(1)}, u32[]{:S(2)}, u32[]{:S(2)}) collective-permute-start(f32[32,512]{1,0:T(8,128)S(1)} %get-tuple-element.82), channel_id=1, source_target_pairs={{0,12},{1,13},{2,14},{3,15},{4,8},{5,9},{6,10},{7,11},{8,4},{9,5},... | collective-permute-start | bytes 196616 | tf_op jit(solution)/shard_map/ppermute | solution.py:183
  31.1 0.6 %collective-permute-start.15 = (f32[32,512]{1,0:T(8,128)S(1)}, f32[32,512]{1,0:T(8,128)S(1)}, u32[]{:S(2)}, u32[]{:S(2)}) collective-permute-start(f32[32,512]{1,0:T(8,128)S(1)} %get-tuple-element.84), channel_id=1, source_target_pairs={{0,4},{1,5},{2,6},{3,7},{4,0},{5,1},{6,2},{7,3},{8,12},{9,13},{10,... | collective-permute-start | bytes 196616 | tf_op jit(solution)/shard_map/ppermute | solution.py:183
  31.8 1.2 %shard_map.122.act = bf16[32,256]{1,0:T(8,128)(2,1)S(1)} custom-call(bf16[16,12288]{1,0:T(8,128)(2,1)S(1)} %get-tuple-element.66.refs_2_.near, bf16[16,12288]{1,0:T(8,128)(2,1)S(1)} %get-tuple-element.75.far, bf16[12288,128]{1,0:T(8,128)(2,1)S(1)} %get-tuple-element.76.w_own, bf16[12288,128]{1,0:T(8,128)(2,1)S(1)} %collective-permute-done.10.w_mate, ...), custom_call_target="tpu_custom_call" | custom-call | bytes 4194304 | tf_op jit(solution)/shard_map/pallas_call | solution.py:249
  33.0 1.2 %shard_map.123.part = f32[32,12288]{1,0:T(8,128)S(1)} custom-call(bf16[32,256]{1,0:T(8,128)(2,1)S(1)} %shard_map.122.act, bf16[128,12288]{1,0:T(8,128)(2,1)S(1)} %get-tuple-element.80.w_own, bf16[128,12288]{1,0:T(8,128)(2,1)S(1)} %collective-permute-done.12.w_mate), custom_call_target="tpu_custom_call" | custom-call | bytes 6291456 | tf_op jit(solution)/shard_map/pallas_call | solution.py:264
  34.2 2.1 %collective-permute-done.14.refs_1_ = f32[32,512]{1,0:T(8,128)S(1)} collective-permute-done((f32[32,512]{1,0:T(8,128)S(1)}, f32[32,512]{1,0:T(8,128)S(1)}, u32[]{:S(2)}, u32[]{:S(2)}) %collective-permute-start.14) | collective-permute-done | bytes 65568 | tf_op jit(solution)/shard_map/ppermute | solution.py:183
  36.7 1.6 %collective-permute-start.21 = (bf16[4,12288]{1,0:T(4,128)(2,1)S(1)}, bf16[4,12288]{1,0:T(4,128)(2,1)S(1)}, u32[]{:S(2)}, u32[]{:S(2)}) collective-permute-start(bf16[4,12288]{1,0:T(4,128)(2,1)S(1)} %get-tuple-element.92), channel_id=1, source_target_pairs={{0,2},{1,3},{2,0},{3,1},{4,6},{5,7},{6,4},{7,5},{8,10},{9,11},{10,... | collective-permute-start | bytes 294920 | tf_op jit(solution)/shard_map/ppermute | solution.py:186
  38.3 0.5 collective-permute-start.19
  38.8 1.5 %collective-permute-start.17 = (bf16[4,12288]{1,0:T(4,128)(2,1)S(1)}, bf16[4,12288]{1,0:T(4,128)(2,1)S(1)}, u32[]{:S(2)}, u32[]{:S(2)}) collective-permute-start(bf16[4,12288]{1,0:T(4,128)(2,1)S(1)} %get-tuple-element.88), channel_id=1, source_target_pairs={{0,2},{1,3},{2,0},{3,1},{4,6},{5,7},{6,4},{7,5},{8,10},{9,11},{10,... | collective-permute-start | bytes 294920 | tf_op jit(solution)/shard_map/ppermute | solution.py:186
  40.4 0.5 collective-permute-start.16
  40.9 1.7 %collective-permute-done.21 = bf16[4,12288]{1,0:T(4,128)(2,1)S(1)} collective-permute-done((bf16[4,12288]{1,0:T(4,128)(2,1)S(1)}, bf16[4,12288]{1,0:T(4,128)(2,1)S(1)}, u32[]{:S(2)}, u32[]{:S(2)}) %collective-permute-start.21) | collective-permute-done | bytes 98336 | tf_op jit(solution)/shard_map/ppermute | solution.py:186
  42.6 1.8 %collective-permute-start.22 = (bf16[4,12288]{1,0:T(4,128)(2,1)S(1)}, bf16[4,12288]{1,0:T(4,128)(2,1)S(1)}, u32[]{:S(2)}, u32[]{:S(2)}) collective-permute-start(bf16[4,12288]{1,0:T(4,128)(2,1)S(1)} %add_convert_fusion), channel_id=1, source_target_pairs={{0,12},{1,13},{2,14},{3,15},{4,8},{5,9},{6,10},{7,11},{8,4},{9,5},... | collective-permute-start | bytes 294920 | tf_op jit(solution)/shard_map/ppermute | solution.py:183
  44.5 0.7 %collective-permute-start.20 = (bf16[4,12288]{1,0:T(4,128)(2,1)S(1)}, bf16[4,12288]{1,0:T(4,128)(2,1)S(1)}, u32[]{:S(2)}, u32[]{:S(2)}) collective-permute-start(bf16[4,12288]{1,0:T(4,128)(2,1)S(1)} %add_convert_fusion.1), channel_id=1, source_target_pairs={{0,8},{1,9},{2,10},{3,11},{4,12},{5,13},{6,14},{7,15},{8,0},{9,1},... | collective-permute-start | bytes 294920 | tf_op jit(solution)/shard_map/ppermute | solution.py:183
  45.3 2.0 %collective-permute-start.18 = (bf16[4,12288]{1,0:T(4,128)(2,1)S(1)}, bf16[4,12288]{1,0:T(4,128)(2,1)S(1)}, u32[]{:S(2)}, u32[]{:S(2)}) collective-permute-start(bf16[4,12288]{1,0:T(4,128)(2,1)S(1)} %add_convert_fusion.2), channel_id=1, source_target_pairs={{0,4},{1,5},{2,6},{3,7},{4,0},{5,1},{6,2},{7,3},{8,12},{9,13},{10,... | collective-permute-start | bytes 294920 | tf_op jit(solution)/shard_map/ppermute | solution.py:183
  47.4 1.7 %collective-permute-done.22.refs_3_ = bf16[4,12288]{1,0:T(4,128)(2,1)S(1)} collective-permute-done((bf16[4,12288]{1,0:T(4,128)(2,1)S(1)}, bf16[4,12288]{1,0:T(4,128)(2,1)S(1)}, u32[]{:S(2)}, u32[]{:S(2)}) %collective-permute-start.22) | collective-permute-done | bytes 98336 | tf_op jit(solution)/shard_map/ppermute | solution.py:183
  49.1 2.1 %collective-permute-done.20.refs_2_ = bf16[4,12288]{1,0:T(4,128)(2,1)S(1)} collective-permute-done((bf16[4,12288]{1,0:T(4,128)(2,1)S(1)}, bf16[4,12288]{1,0:T(4,128)(2,1)S(1)}, u32[]{:S(2)}, u32[]{:S(2)}) %collective-permute-start.20) | collective-permute-done | bytes 98336 | tf_op jit(solution)/shard_map/ppermute | solution.py:183
  51.2 0.7 %shard_map.125 = bf16[4,12288]{1,0:T(4,128)(2,1)} custom-call(f32[4,12288]{1,0:T(4,128)S(1)} %convert_add_fusion.refs_0_, bf16[4,12288]{1,0:T(4,128)(2,1)S(1)} %collective-permute-done.18.refs_1_, bf16[4,12288]{1,0:T(4,128)(2,1)S(1)} %collective-permute-done.20.refs_2_, bf16[4,12288]{1,0:T(4,128)(2,1)S(1)} %collective-permute-done.22.refs_3_), custom_call_target="tpu_custom_call" | custom-call | bytes 2097152 | tf_op jit(solution)/shard_map/pallas_call | solution.py:285
  (43 shorter events, 3.0 us)
Async XLA Ops:
  0.0 14.3 %collective-permute-start.10 = (bf16[12288,128]{1,0:T(8,128)(2,1)}, bf16[12288,128]{1,0:T(8,128)(2,1)S(1)}, u32[]{:S(2)}, u32[]{:S(2)}) collective-permute-start(bf16[12288,128]{1,0:T(8,128)(2,1)} %refs_4_), channel_id=1, source_target_pairs={{0,1},{1,0},{2,3},{3,2},{4,5},{5,4},{6,7},{7,6},{8,9},{9,8},{10,11... | collective-permute-start | bytes 9437192 | tf_op jit(solution)/shard_map/ppermute | solution.py:189
  0.5 8.4 %collective-permute-start.4 = (bf16[4,12288]{1,0:T(4,128)(2,1)}, bf16[4,12288]{1,0:T(4,128)(2,1)S(1)}, u32[]{:S(2)}, u32[]{:S(2)}) collective-permute-start(bf16[4,12288]{1,0:T(4,128)(2,1)} %refs_0_), channel_id=1, source_target_pairs={{0,4},{1,5},{2,6},{3,7},{4,0},{5,1},{6,2},{7,3},{8,12},{9,13},{10,... | collective-permute-start | bytes 294920 | tf_op jit(solution)/shard_map/ppermute | solution.py:183
  3.0 11.0 %collective-permute-start = (bf16[4,12288]{1,0:T(4,128)(2,1)}, bf16[4,12288]{1,0:T(4,128)(2,1)S(1)}, u32[]{:S(2)}, u32[]{:S(2)}) collective-permute-start(bf16[4,12288]{1,0:T(4,128)(2,1)} %refs_0_), channel_id=1, source_target_pairs={{0,8},{1,9},{2,10},{3,11},{4,12},{5,13},{6,14},{7,15},{8,0},{9,1},... | collective-permute-start | bytes 294920 | tf_op jit(solution)/shard_map/ppermute | solution.py:183
  5.6 8.4 %collective-permute-start.2 = (bf16[4,12288]{1,0:T(4,128)(2,1)}, bf16[4,12288]{1,0:T(4,128)(2,1)S(1)}, u32[]{:S(2)}, u32[]{:S(2)}) collective-permute-start(bf16[4,12288]{1,0:T(4,128)(2,1)} %refs_0_), channel_id=1, source_target_pairs={{0,12},{1,13},{2,14},{3,15},{4,8},{5,9},{6,10},{7,11},{8,4},{9,5},... | collective-permute-start | bytes 294920 | tf_op jit(solution)/shard_map/ppermute | solution.py:183
  5.6 1.3 %collective-permute-start.5 = (f32[1,128]{1,0:T(1,128)}, f32[1,128]{1,0:T(1,128)S(1)}, u32[]{:S(2)}, u32[]{:S(2)}) collective-permute-start(f32[1,128]{1,0:T(1,128)} %bitcast.12), channel_id=1, source_target_pairs={{0,1},{1,0},{2,3},{3,2},{4,5},{5,4},{6,7},{7,6},{8,9},{9,8},{10,11... | collective-permute-start | bytes 1544 | tf_op jit(solution)/shard_map/ppermute | solution.py:189
  6.9 5.4 %collective-permute-start.6 = (bf16[4,12288]{1,0:T(4,128)(2,1)}, bf16[4,12288]{1,0:T(4,128)(2,1)S(1)}, u32[]{:S(2)}, u32[]{:S(2)}) collective-permute-start(bf16[4,12288]{1,0:T(4,128)(2,1)} %refs_0_), channel_id=1, source_target_pairs={{0,2},{1,3},{2,0},{3,1},{4,6},{5,7},{6,4},{7,5},{8,10},{9,11},{10,... | collective-permute-start | bytes 294920 | tf_op jit(solution)/shard_map/ppermute | solution.py:186
  9.6 4.6 %collective-permute-start.7 = (bf16[4,12288]{1,0:T(4,128)(2,1)S(1)}, bf16[4,12288]{1,0:T(4,128)(2,1)S(1)}, u32[]{:S(2)}, u32[]{:S(2)}) collective-permute-start(bf16[4,12288]{1,0:T(4,128)(2,1)S(1)} %collective-permute-done.4.refs_1_), channel_id=1, source_target_pairs={{0,2},{1,3},{2,0},{3,1},{4,6},{5,7},{6,4},{7,5},{8,10},{9,11},{10,... | collective-permute-start | bytes 294920 | tf_op jit(solution)/shard_map/ppermute | solution.py:186
  14.3 18.7 %collective-permute-start.12 = (bf16[128,12288]{1,0:T(8,128)(2,1)}, bf16[128,12288]{1,0:T(8,128)(2,1)S(1)}, u32[]{:S(2)}, u32[]{:S(2)}) collective-permute-start(bf16[128,12288]{1,0:T(8,128)(2,1)} %refs_5_), channel_id=1, source_target_pairs={{0,1},{1,0},{2,3},{3,2},{4,5},{5,4},{6,7},{7,6},{8,9},{9,8},{10,11... | collective-permute-start | bytes 9437192 | tf_op jit(solution)/shard_map/ppermute | solution.py:189
  14.3 7.8 %collective-permute-start.8 = (bf16[768,512]{1,0:T(8,128)(2,1)}, bf16[768,512]{1,0:T(8,128)(2,1)S(1)}, u32[]{:S(2)}, u32[]{:S(2)}) collective-permute-start(bf16[768,512]{1,0:T(8,128)(2,1)} %refs_3_), channel_id=1, source_target_pairs={{0,1},{1,0},{2,3},{3,2},{4,5},{5,4},{6,7},{7,6},{8,9},{9,8},{10,11... | collective-permute-start | bytes 2359304 | tf_op jit(solution)/shard_map/ppermute | solution.py:189
  14.8 21.5 %collective-permute-start.11 = (bf16[512,768]{1,0:T(8,128)(2,1)}, bf16[512,768]{1,0:T(8,128)(2,1)S(1)}, u32[]{:S(2)}, u32[]{:S(2)}) collective-permute-start(bf16[512,768]{1,0:T(8,128)(2,1)} %refs_6_), channel_id=1, source_target_pairs={{0,1},{1,0},{2,3},{3,2},{4,5},{5,4},{6,7},{7,6},{8,9},{9,8},{10,11... | collective-permute-start | bytes 2359304 | tf_op jit(solution)/shard_map/ppermute | solution.py:189
  14.8 6.3 %collective-permute-start.1 = (bf16[4,12288]{1,0:T(4,128)(2,1)S(1)}, bf16[4,12288]{1,0:T(4,128)(2,1)S(1)}, u32[]{:S(2)}, u32[]{:S(2)}) collective-permute-start(bf16[4,12288]{1,0:T(4,128)(2,1)S(1)} %collective-permute-done.refs_2_), channel_id=1, source_target_pairs={{0,2},{1,3},{2,0},{3,1},{4,6},{5,7},{6,4},{7,5},{8,10},{9,11},{10,... | collective-permute-start | bytes 294920 | tf_op jit(solution)/shard_map/ppermute | solution.py:186
  16.5 5.6 %collective-permute-start.3 = (bf16[4,12288]{1,0:T(4,128)(2,1)S(1)}, bf16[4,12288]{1,0:T(4,128)(2,1)S(1)}, u32[]{:S(2)}, u32[]{:S(2)}) collective-permute-start(bf16[4,12288]{1,0:T(4,128)(2,1)S(1)} %collective-permute-done.2.refs_3_), channel_id=1, source_target_pairs={{0,2},{1,3},{2,0},{3,1},{4,6},{5,7},{6,4},{7,5},{8,10},{9,11},{10,... | collective-permute-start | bytes 294920 | tf_op jit(solution)/shard_map/ppermute | solution.py:186
  20.2 11.6 %copy-start.1 = (f32[128]{0:T(128)S(1)}, f32[128]{0:T(128)}, u32[]{:S(2)}) copy-start(f32[128]{0:T(128)} %param.19) | copy-start | bytes 1540
  22.9 4.3 %collective-permute-start.9 = (f32[32,512]{1,0:T(8,128)S(1)}, f32[32,512]{1,0:T(8,128)S(1)}, u32[]{:S(2)}, u32[]{:S(2)}) collective-permute-start(f32[32,512]{1,0:T(8,128)S(1)} %get-tuple-element.71), channel_id=1, source_target_pairs={{0,2},{1,3},{2,0},{3,1},{4,6},{5,7},{6,4},{7,5},{8,10},{9,11},{10,... | collective-permute-start | bytes 196616 | tf_op jit(solution)/shard_map/ppermute | solution.py:186
  27.2 7.0 %collective-permute-start.13 = (f32[32,512]{1,0:T(8,128)S(1)}, f32[32,512]{1,0:T(8,128)S(1)}, u32[]{:S(2)}, u32[]{:S(2)}) collective-permute-start(f32[32,512]{1,0:T(8,128)S(1)} %get-tuple-element.82), channel_id=1, source_target_pairs={{0,12},{1,13},{2,14},{3,15},{4,8},{5,9},{6,10},{7,11},{8,4},{9,5},... | collective-permute-start | bytes 196616 | tf_op jit(solution)/shard_map/ppermute | solution.py:183
  31.1 5.2 %collective-permute-start.14 = (f32[32,512]{1,0:T(8,128)S(1)}, f32[32,512]{1,0:T(8,128)S(1)}, u32[]{:S(2)}, u32[]{:S(2)}) collective-permute-start(f32[32,512]{1,0:T(8,128)S(1)} %get-tuple-element.83), channel_id=1, source_target_pairs={{0,8},{1,9},{2,10},{3,11},{4,12},{5,13},{6,14},{7,15},{8,0},{9,1},... | collective-permute-start | bytes 196616 | tf_op jit(solution)/shard_map/ppermute | solution.py:183
  31.1 5.2 %collective-permute-start.15 = (f32[32,512]{1,0:T(8,128)S(1)}, f32[32,512]{1,0:T(8,128)S(1)}, u32[]{:S(2)}, u32[]{:S(2)}) collective-permute-start(f32[32,512]{1,0:T(8,128)S(1)} %get-tuple-element.84), channel_id=1, source_target_pairs={{0,4},{1,5},{2,6},{3,7},{4,0},{5,1},{6,2},{7,3},{8,12},{9,13},{10,... | collective-permute-start | bytes 196616 | tf_op jit(solution)/shard_map/ppermute | solution.py:183
  33.0 3.3 %copy-start = (f32[512]{0:T(512)S(1)}, f32[512]{0:T(512)}, u32[]{:S(2)}) copy-start(f32[512]{0:T(512)} %param.22) | copy-start | bytes 6148
  36.7 5.8 %collective-permute-start.21 = (bf16[4,12288]{1,0:T(4,128)(2,1)S(1)}, bf16[4,12288]{1,0:T(4,128)(2,1)S(1)}, u32[]{:S(2)}, u32[]{:S(2)}) collective-permute-start(bf16[4,12288]{1,0:T(4,128)(2,1)S(1)} %get-tuple-element.92), channel_id=1, source_target_pairs={{0,2},{1,3},{2,0},{3,1},{4,6},{5,7},{6,4},{7,5},{8,10},{9,11},{10,... | collective-permute-start | bytes 294920 | tf_op jit(solution)/shard_map/ppermute | solution.py:186
  38.3 6.1 %collective-permute-start.19 = (bf16[4,12288]{1,0:T(4,128)(2,1)S(1)}, bf16[4,12288]{1,0:T(4,128)(2,1)S(1)}, u32[]{:S(2)}, u32[]{:S(2)}) collective-permute-start(bf16[4,12288]{1,0:T(4,128)(2,1)S(1)} %get-tuple-element.90), channel_id=1, source_target_pairs={{0,2},{1,3},{2,0},{3,1},{4,6},{5,7},{6,4},{7,5},{8,10},{9,11},{10,... | collective-permute-start | bytes 294920 | tf_op jit(solution)/shard_map/ppermute | solution.py:186
  38.8 6.4 %collective-permute-start.17 = (bf16[4,12288]{1,0:T(4,128)(2,1)S(1)}, bf16[4,12288]{1,0:T(4,128)(2,1)S(1)}, u32[]{:S(2)}, u32[]{:S(2)}) collective-permute-start(bf16[4,12288]{1,0:T(4,128)(2,1)S(1)} %get-tuple-element.88), channel_id=1, source_target_pairs={{0,2},{1,3},{2,0},{3,1},{4,6},{5,7},{6,4},{7,5},{8,10},{9,11},{10,... | collective-permute-start | bytes 294920 | tf_op jit(solution)/shard_map/ppermute | solution.py:186
  40.4 7.0 %collective-permute-start.16 = (bf16[4,12288]{1,0:T(4,128)(2,1)S(1)}, bf16[4,12288]{1,0:T(4,128)(2,1)S(1)}, u32[]{:S(2)}, u32[]{:S(2)}) collective-permute-start(bf16[4,12288]{1,0:T(4,128)(2,1)S(1)} %get-tuple-element.86), channel_id=1, source_target_pairs={{0,2},{1,3},{2,0},{3,1},{4,6},{5,7},{6,4},{7,5},{8,10},{9,11},{10,... | collective-permute-start | bytes 294920 | tf_op jit(solution)/shard_map/ppermute | solution.py:186
  42.6 6.5 %collective-permute-start.22 = (bf16[4,12288]{1,0:T(4,128)(2,1)S(1)}, bf16[4,12288]{1,0:T(4,128)(2,1)S(1)}, u32[]{:S(2)}, u32[]{:S(2)}) collective-permute-start(bf16[4,12288]{1,0:T(4,128)(2,1)S(1)} %add_convert_fusion), channel_id=1, source_target_pairs={{0,12},{1,13},{2,14},{3,15},{4,8},{5,9},{6,10},{7,11},{8,4},{9,5},... | collective-permute-start | bytes 294920 | tf_op jit(solution)/shard_map/ppermute | solution.py:183
  44.5 6.7 %collective-permute-start.20 = (bf16[4,12288]{1,0:T(4,128)(2,1)S(1)}, bf16[4,12288]{1,0:T(4,128)(2,1)S(1)}, u32[]{:S(2)}, u32[]{:S(2)}) collective-permute-start(bf16[4,12288]{1,0:T(4,128)(2,1)S(1)} %add_convert_fusion.1), channel_id=1, source_target_pairs={{0,8},{1,9},{2,10},{3,11},{4,12},{5,13},{6,14},{7,15},{8,0},{9,1},... | collective-permute-start | bytes 294920 | tf_op jit(solution)/shard_map/ppermute | solution.py:183
  45.3 5.9 %collective-permute-start.18 = (bf16[4,12288]{1,0:T(4,128)(2,1)S(1)}, bf16[4,12288]{1,0:T(4,128)(2,1)S(1)}, u32[]{:S(2)}, u32[]{:S(2)}) collective-permute-start(bf16[4,12288]{1,0:T(4,128)(2,1)S(1)} %add_convert_fusion.2), channel_id=1, source_target_pairs={{0,4},{1,5},{2,6},{3,7},{4,0},{5,1},{6,2},{7,3},{8,12},{9,13},{10,... | collective-permute-start | bytes 294920 | tf_op jit(solution)/shard_map/ppermute | solution.py:183

commit v25 on v24

--- a/solution.py
+++ b/solution.py
@@ -195,7 +195,6 @@
     span = 2 * share
 
     held = [hidden] + [across(hidden, k) for k in range(1, groups)]
-    w_in_mate = core(w_in)
     held[1], lists, counts, block_slot = lax.optimization_barrier((held[1], lists, counts, block_slot))
 
     table = activity(lists, counts, block_slot)
@@ -220,11 +219,12 @@
         [pltpu.SemaphoreType.DMA((len(near),))],
         8 * MIB,
     )(*[pltpu.with_memory_space_constraint(x, pltpu.HBM) for x in near])
+    w_in_first = w_in
     hidden_near, gain, shift, low_in, w_in, w_out_near, low_out_near = near
-    *_, w_in_mate, w_out_sent, low_out_sent = lax.optimization_barrier(
-        (*held, *beyond[: groups // 2], w_in_mate, w_out, low_out)
+    *_, w_in_sent, w_out_sent = lax.optimization_barrier(
+        (*held, *beyond[: groups // 2], w_in_first, w_out)
     )
-    w_out_mate, low_out_mate = core(w_out_sent), core(low_out_sent)
+    w_in_mate, w_out_mate = core(w_in_sent), core(w_out_sent)
     held[0] = hidden_near
 
     soon = groups // 2
@@ -244,7 +244,8 @@
         (),
         4 * MIB,
     )(place, *beyond[soon:], normed, first, gain, shift, low_in, low_in_mate)
-    got = beside(message)
+    message, low_out_sent = lax.optimization_barrier((message, low_out))
+    got, low_out_mate = beside(message), core(low_out_sent)
     step = piece(width, 2048)
     act = call(
         functools.partial(act_body, step),

time: 52.1 us -> 57.4 us (1.10)
  waiting for transfers between devices: 14.9 us -> 21.5 us
  starting transfers between devices: 25.2 us -> 23.9 us
    ppermute x5, waiting for transfers between devices: 1.1 us -> 4.75 us  [core(): return lax.ppermute(x, 'blk', [(i, i ^ 1) for i in range(devices)])]
    ppermute x9, waiting for transfers between devices: 6.18 us -> 8.85 us  [beside(): return lax.ppermute(x, 'blk', [(i, i ^ 2) for i in range(devices)])]
    ppermute x9, starting transfers between devices: 9.96 us -> 8.62 us  [beside(): return lax.ppermute(x, 'blk', [(i, i ^ 2) for i in range(devices)])]
  transfers between devices with their start and end apart: 23 -> 23, of which waited for: 10 -> 13; matrix products, arithmetic and copies ran while one was open for 6% -> 5% of each run, Pallas kernels for 14% -> 13%
where the time goes in v25:
time: 57.4 us; the launch traced here: 57.2 us
  starting transfers between devices  23.9 us (42%)
  waiting for transfers between devices  21.5 us (37%)
  Pallas kernels  8.53 us (15%)
  other arithmetic  2.25 us (4%)
  local copies, waits for them, and re-layouts  0.88 us (2%)
    ppermute x9, starting transfers between devices, across(): return lax.ppermute(x, 'blk', [(i, i ^ 4 * k) for i in range(devices)])  14.5 us
    ppermute x9, waiting for transfers between devices, beside(): return lax.ppermute(x, 'blk', [(i, i ^ 2) for i in range(devices)])  8.85 us
    ppermute x9, starting transfers between devices, beside(): return lax.ppermute(x, 'blk', [(i, i ^ 2) for i in range(devices)])  8.62 us
    ppermute x9, waiting for transfers between devices, across(): return lax.ppermute(x, 'blk', [(i, i ^ 4 * k) for i in range(devices)])  7.9 us
    ppermute x5, waiting for transfers between devices, core(): return lax.ppermute(x, 'blk', [(i, i ^ 1) for i in range(devices)])  4.75 us
    pallas_call x1, Pallas kernels, shards(): call(functools.partial(load_body, len(near)), [shape(*x.shape, dtype=x.dt...  3.39 us
    pallas_call x1, Pallas kernels, shards(): call(functools.partial(act_body, step), [shape(rows, 2 * block)], [VMEM]...  1.19 us
    pallas_call x1, Pallas kernels, shards(): call(functools.partial(part_body, step), [shape(rows, width, dtype=f32)],...  1.19 us
  transfers between devices with their start and end apart: 23, of which 13 were waited for; matrix products, arithmetic and copies ran while one was open for 5% of the time, Pallas kernels for 13%

profile of v25, /device:TPU:0, one launch (start us, length us, event | category | flops | bytes accessed | tf_op | source)
XLA Modules:
  0.0 57.2 jit_solution(9009768587615730967)
XLA Ops:
  0.0 3.0 %collective-permute-start.4 = (bf16[4,12288]{1,0:T(4,128)(2,1)}, bf16[4,12288]{1,0:T(4,128)(2,1)S(1)}, u32[]{:S(2)}, u32[]{:S(2)}) collective-permute-start(bf16[4,12288]{1,0:T(4,128)(2,1)} %refs_0_), channel_id=1, source_target_pairs={{0,4},{1,5},{2,6},{3,7},{4,0},{5,1},{6,2},{7,3},{8,12},{9,13},{10,... | collective-permute-start | bytes 294920 | tf_op jit(solution)/shard_map/ppermute | solution.py:183
  3.0 2.6 %collective-permute-start = (bf16[4,12288]{1,0:T(4,128)(2,1)}, bf16[4,12288]{1,0:T(4,128)(2,1)S(1)}, u32[]{:S(2)}, u32[]{:S(2)}) collective-permute-start(bf16[4,12288]{1,0:T(4,128)(2,1)} %refs_0_), channel_id=1, source_target_pairs={{0,8},{1,9},{2,10},{3,11},{4,12},{5,13},{6,14},{7,15},{8,0},{9,1},... | collective-permute-start | bytes 294920 | tf_op jit(solution)/shard_map/ppermute | solution.py:183
  5.8 1.1 %collective-permute-done.5.b_mate = f32[1,128]{1,0:T(1,128)S(1)} collective-permute-done((f32[1,128]{1,0:T(1,128)}, f32[1,128]{1,0:T(1,128)S(1)}, u32[]{:S(2)}, u32[]{:S(2)}) %collective-permute-start.5) | collective-permute-done | bytes 544 | tf_op jit(solution)/shard_map/ppermute | solution.py:189
  6.9 1.7 %collective-permute-start.6 = (bf16[4,12288]{1,0:T(4,128)(2,1)}, bf16[4,12288]{1,0:T(4,128)(2,1)S(1)}, u32[]{:S(2)}, u32[]{:S(2)}) collective-permute-start(bf16[4,12288]{1,0:T(4,128)(2,1)} %refs_0_), channel_id=1, source_target_pairs={{0,2},{1,3},{2,0},{3,1},{4,6},{5,7},{6,4},{7,5},{8,10},{9,11},{10,... | collective-permute-start | bytes 294920 | tf_op jit(solution)/shard_map/ppermute | solution.py:186
  8.6 0.8 %copy.13 = s32[4,6]{0,1:T(8,128)S(1)} copy(s32[4,6]{1,0:T(4,128)} %param.15) | data formatting | bytes 192 | tf_op jit(solution)/shard_map/optimization_barrier | solution.py:198
  9.4 0.7 %fusion.1 = s32[4,6]{0,1:T(8,128)S(1)} fusion(s32[4]{0:T(128)} %param.16), kind=kLoop, calls=%fused_computation.12 | loop fusion | flops 48 | bytes 112 | tf_op jit(solution)/shard_map/convert_element_type | solution.py:150
  10.0 0.7 %fusion = s32[16,16]{1,0:T(8,128)S(1)} fusion(s32[16]{0:T(128)} %param.17), kind=kLoop, calls=%fused_computation.10 | loop fusion | flops 512 | bytes 1088 | tf_op jit(solution)/shard_map/convert_element_type | solution.py:153
  12.0 1.7 %collective-permute-done.refs_2_ = bf16[4,12288]{1,0:T(4,128)(2,1)S(1)} collective-permute-done((bf16[4,12288]{1,0:T(4,128)(2,1)}, bf16[4,12288]{1,0:T(4,128)(2,1)S(1)}, u32[]{:S(2)}, u32[]{:S(2)}) %collective-permute-start) | collective-permute-done | bytes 98336 | tf_op jit(solution)/shard_map/ppermute | solution.py:183
  13.7 1.7 %collective-permute-done.7.refs_5_ = bf16[4,12288]{1,0:T(4,128)(2,1)S(1)} collective-permute-done((bf16[4,12288]{1,0:T(4,128)(2,1)S(1)}, bf16[4,12288]{1,0:T(4,128)(2,1)S(1)}, u32[]{:S(2)}, u32[]{:S(2)}) %collective-permute-start.7) | collective-permute-done | bytes 98336 | tf_op jit(solution)/shard_map/ppermute | solution.py:186
  15.4 0.5 collective-permute-start.12
  16.4 1.6 %collective-permute-start.3 = (bf16[4,12288]{1,0:T(4,128)(2,1)S(1)}, bf16[4,12288]{1,0:T(4,128)(2,1)S(1)}, u32[]{:S(2)}, u32[]{:S(2)}) collective-permute-start(bf16[4,12288]{1,0:T(4,128)(2,1)S(1)} %collective-permute-done.2.refs_3_), channel_id=1, source_target_pairs={{0,2},{1,3},{2,0},{3,1},{4,6},{5,7},{6,4},{7,5},{8,10},{9,11},{10,... | collective-permute-start | bytes 294920 | tf_op jit(solution)/shard_map/ppermute | solution.py:186
  17.9 3.4 %shard_map.118 = (bf16[4,12288]{1,0:T(4,128)(2,1)S(1)}, f32[1,12288]{1,0:T(1,128)S(1)}, f32[1,12288]{1,0:T(1,128)S(1)}, bf16[768,512]{1,0:T(8,128)(2,1)S(1)}, bf...) custom-call(bf16[4,12288]{1,0:T(4,128)(2,1)} %refs_0_, ...), custom_call_target="tpu_custom_call" | custom-call | bytes 8388608 | tf_op jit(solution)/shard_map/pallas_call | solution.py:214
  21.4 0.8 %shard_map.119 = (bf16[16,12288]{1,0:T(8,128)(2,1)S(1)}, bf16[8,12288]{1,0:T(8,128)(2,1)S(1)}) custom-call(bf16[4,12288]{1,0:T(4,128)(2,1)S(1)} %get-tuple-element.62.refs_0_, bf16[4,12288]{1,0:T(4,128)(2,1)S(1)} %collective-permute-done.4.refs_1_, bf16[4,12288]{1,0:T(4,128)(2,1)S(1)} %collective-permute-done.refs_2_, ...), custom_call_target="tpu_custom_call" | custom-call | bytes 4194304 | tf_op jit(solution)/shard_map/pallas_call | solution.py:231
  22.2 1.1 %collective-permute-done.3.refs_1_ = bf16[4,12288]{1,0:T(4,128)(2,1)S(1)} collective-permute-done((bf16[4,12288]{1,0:T(4,128)(2,1)S(1)}, bf16[4,12288]{1,0:T(4,128)(2,1)S(1)}, u32[]{:S(2)}, u32[]{:S(2)}) %collective-permute-start.3) | collective-permute-done | bytes 98336 | tf_op jit(solution)/shard_map/ppermute | solution.py:186
  23.2 3.7 %collective-permute-done.8.refs_7_ = bf16[768,512]{1,0:T(8,128)(2,1)S(1)} collective-permute-done((bf16[768,512]{1,0:T(8,128)(2,1)}, bf16[768,512]{1,0:T(8,128)(2,1)S(1)}, u32[]{:S(2)}, u32[]{:S(2)}) %collective-permute-start.8) | collective-permute-done | bytes 786464 | tf_op jit(solution)/shard_map/ppermute | solution.py:189
  26.9 0.8 %shard_map.120 = (bf16[16,12288]{1,0:T(8,128)(2,1)S(1)}, f32[32,512]{1,0:T(8,128)S(1)}, f32[32,512]{1,0:T(8,128)S(1)}) custom-call(s32[1]{0:T(128)} %bitcast.place, bf16[4,12288]{1,0:T(4,128)(2,1)S(1)} %collective-permute-done.1.refs_0_, bf16[4,12288]{1,0:T(4,128)(2,1)S(1)} %collective-permute-done.3.refs_1_, ...), custom_call_target="tpu_custom_call" | custom-call | bytes 4194304 | tf_op jit(solution)/shard_map/pallas_call | solution.py:239
  28.4 3.9 %collective-permute-done.9.got = f32[32,512]{1,0:T(8,128)S(1)} collective-permute-done((f32[32,512]{1,0:T(8,128)S(1)}, f32[32,512]{1,0:T(8,128)S(1)}, u32[]{:S(2)}, u32[]{:S(2)}) %collective-permute-start.9) | collective-permute-done | bytes 65568 | tf_op jit(solution)/shard_map/ppermute | solution.py:186
  32.3 3.7 %collective-permute-start.13 = (f32[32,512]{1,0:T(8,128)S(1)}, f32[32,512]{1,0:T(8,128)S(1)}, u32[]{:S(2)}, u32[]{:S(2)}) collective-permute-start(f32[32,512]{1,0:T(8,128)S(1)} %get-tuple-element.84), channel_id=1, source_target_pairs={{0,12},{1,13},{2,14},{3,15},{4,8},{5,9},{6,10},{7,11},{8,4},{9,5},... | collective-permute-start | bytes 196616 | tf_op jit(solution)/shard_map/ppermute | solution.py:183
  36.0 0.8 %collective-permute-start.15 = (f32[32,512]{1,0:T(8,128)S(1)}, f32[32,512]{1,0:T(8,128)S(1)}, u32[]{:S(2)}, u32[]{:S(2)}) collective-permute-start(f32[32,512]{1,0:T(8,128)S(1)} %get-tuple-element.86), channel_id=1, source_target_pairs={{0,4},{1,5},{2,6},{3,7},{4,0},{5,1},{6,2},{7,3},{8,12},{9,13},{10,... | collective-permute-start | bytes 196616 | tf_op jit(solution)/shard_map/ppermute | solution.py:183
  36.8 1.2 %shard_map.122.act = bf16[32,256]{1,0:T(8,128)(2,1)S(1)} custom-call(bf16[16,12288]{1,0:T(8,128)(2,1)S(1)} %get-tuple-element.67.refs_2_.near, bf16[16,12288]{1,0:T(8,128)(2,1)S(1)} %get-tuple-element.77.far, bf16[12288,128]{1,0:T(8,128)(2,1)S(1)} %get-tuple-element.78.w_own, bf16[12288,128]{1,0:T(8,128)(2,1)S(1)} %collective-permute-done.11.w_mate, ...), custom_call_target="tpu_custom_call" | custom-call | bytes 4194304 | tf_op jit(solution)/shard_map/pallas_call | solution.py:250
  38.0 1.2 %shard_map.123.part = f32[32,12288]{1,0:T(8,128)S(1)} custom-call(bf16[32,256]{1,0:T(8,128)(2,1)S(1)} %shard_map.122.act, bf16[128,12288]{1,0:T(8,128)(2,1)S(1)} %get-tuple-element.82.w_own, bf16[128,12288]{1,0:T(8,128)(2,1)S(1)} %collective-permute-done.12.w_mate), custom_call_target="tpu_custom_call" | custom-call | bytes 6291456 | tf_op jit(solution)/shard_map/pallas_call | solution.py:265
  39.2 2.0 %collective-permute-done.14.refs_1_ = f32[32,512]{1,0:T(8,128)S(1)} collective-permute-done((f32[32,512]{1,0:T(8,128)S(1)}, f32[32,512]{1,0:T(8,128)S(1)}, u32[]{:S(2)}, u32[]{:S(2)}) %collective-permute-start.14) | collective-permute-done | bytes 65568 | tf_op jit(solution)/shard_map/ppermute | solution.py:183
  42.0 0.6 %collective-permute-start.21 = (bf16[4,12288]{1,0:T(4,128)(2,1)S(1)}, bf16[4,12288]{1,0:T(4,128)(2,1)S(1)}, u32[]{:S(2)}, u32[]{:S(2)}) collective-permute-start(bf16[4,12288]{1,0:T(4,128)(2,1)S(1)} %get-tuple-element.94), channel_id=1, source_target_pairs={{0,2},{1,3},{2,0},{3,1},{4,6},{5,7},{6,4},{7,5},{8,10},{9,11},{10,... | collective-permute-start | bytes 294920 | tf_op jit(solution)/shard_map/ppermute | solution.py:186
  42.6 1.5 %collective-permute-start.19 = (bf16[4,12288]{1,0:T(4,128)(2,1)S(1)}, bf16[4,12288]{1,0:T(4,128)(2,1)S(1)}, u32[]{:S(2)}, u32[]{:S(2)}) collective-permute-start(bf16[4,12288]{1,0:T(4,128)(2,1)S(1)} %get-tuple-element.92), channel_id=1, source_target_pairs={{0,2},{1,3},{2,0},{3,1},{4,6},{5,7},{6,4},{7,5},{8,10},{9,11},{10,... | collective-permute-start | bytes 294920 | tf_op jit(solution)/shard_map/ppermute | solution.py:186
  44.6 1.5 %collective-permute-start.16 = (bf16[4,12288]{1,0:T(4,128)(2,1)S(1)}, bf16[4,12288]{1,0:T(4,128)(2,1)S(1)}, u32[]{:S(2)}, u32[]{:S(2)}) collective-permute-start(bf16[4,12288]{1,0:T(4,128)(2,1)S(1)} %get-tuple-element.88), channel_id=1, source_target_pairs={{0,2},{1,3},{2,0},{3,1},{4,6},{5,7},{6,4},{7,5},{8,10},{9,11},{10,... | collective-permute-start | bytes 294920 | tf_op jit(solution)/shard_map/ppermute | solution.py:186
  46.1 1.7 %collective-permute-done.21 = bf16[4,12288]{1,0:T(4,128)(2,1)S(1)} collective-permute-done((bf16[4,12288]{1,0:T(4,128)(2,1)S(1)}, bf16[4,12288]{1,0:T(4,128)(2,1)S(1)}, u32[]{:S(2)}, u32[]{:S(2)}) %collective-permute-start.21) | collective-permute-done | bytes 98336 | tf_op jit(solution)/shard_map/ppermute | solution.py:186
  47.9 1.9 %collective-permute-start.22 = (bf16[4,12288]{1,0:T(4,128)(2,1)S(1)}, bf16[4,12288]{1,0:T(4,128)(2,1)S(1)}, u32[]{:S(2)}, u32[]{:S(2)}) collective-permute-start(bf16[4,12288]{1,0:T(4,128)(2,1)S(1)} %add_convert_fusion), channel_id=1, source_target_pairs={{0,12},{1,13},{2,14},{3,15},{4,8},{5,9},{6,10},{7,11},{8,4},{9,5},... | collective-permute-start | bytes 294920 | tf_op jit(solution)/shard_map/ppermute | solution.py:183
  49.9 0.7 %collective-permute-start.20 = (bf16[4,12288]{1,0:T(4,128)(2,1)S(1)}, bf16[4,12288]{1,0:T(4,128)(2,1)S(1)}, u32[]{:S(2)}, u32[]{:S(2)}) collective-permute-start(bf16[4,12288]{1,0:T(4,128)(2,1)S(1)} %add_convert_fusion.1), channel_id=1, source_target_pairs={{0,8},{1,9},{2,10},{3,11},{4,12},{5,13},{6,14},{7,15},{8,0},{9,1},... | collective-permute-start | bytes 294920 | tf_op jit(solution)/shard_map/ppermute | solution.py:183
  50.7 1.8 %collective-permute-start.18 = (bf16[4,12288]{1,0:T(4,128)(2,1)S(1)}, bf16[4,12288]{1,0:T(4,128)(2,1)S(1)}, u32[]{:S(2)}, u32[]{:S(2)}) collective-permute-start(bf16[4,12288]{1,0:T(4,128)(2,1)S(1)} %add_convert_fusion.2), channel_id=1, source_target_pairs={{0,4},{1,5},{2,6},{3,7},{4,0},{5,1},{6,2},{7,3},{8,12},{9,13},{10,... | collective-permute-start | bytes 294920 | tf_op jit(solution)/shard_map/ppermute | solution.py:183
  52.6 1.7 %collective-permute-done.22.refs_3_ = bf16[4,12288]{1,0:T(4,128)(2,1)S(1)} collective-permute-done((bf16[4,12288]{1,0:T(4,128)(2,1)S(1)}, bf16[4,12288]{1,0:T(4,128)(2,1)S(1)}, u32[]{:S(2)}, u32[]{:S(2)}) %collective-permute-start.22) | collective-permute-done | bytes 98336 | tf_op jit(solution)/shard_map/ppermute | solution.py:183
  54.4 2.1 %collective-permute-done.20.refs_2_ = bf16[4,12288]{1,0:T(4,128)(2,1)S(1)} collective-permute-done((bf16[4,12288]{1,0:T(4,128)(2,1)S(1)}, bf16[4,12288]{1,0:T(4,128)(2,1)S(1)}, u32[]{:S(2)}, u32[]{:S(2)}) %collective-permute-start.20) | collective-permute-done | bytes 98336 | tf_op jit(solution)/shard_map/ppermute | solution.py:183
  56.5 0.7 %shard_map.125 = bf16[4,12288]{1,0:T(4,128)(2,1)} custom-call(f32[4,12288]{1,0:T(4,128)S(1)} %convert_add_fusion.refs_0_, bf16[4,12288]{1,0:T(4,128)(2,1)S(1)} %collective-permute-done.18.refs_1_, bf16[4,12288]{1,0:T(4,128)(2,1)S(1)} %collective-permute-done.20.refs_2_, bf16[4,12288]{1,0:T(4,128)(2,1)S(1)} %collective-permute-done.22.refs_3_), custom_call_target="tpu_custom_call" | custom-call | bytes 2097152 | tf_op jit(solution)/shard_map/pallas_call | solution.py:286
  (45 shorter events, 4.2 us)
Async XLA Ops:
  0.0 8.6 %collective-permute-start.4 = (bf16[4,12288]{1,0:T(4,128)(2,1)}, bf16[4,12288]{1,0:T(4,128)(2,1)S(1)}, u32[]{:S(2)}, u32[]{:S(2)}) collective-permute-start(bf16[4,12288]{1,0:T(4,128)(2,1)} %refs_0_), channel_id=1, source_target_pairs={{0,4},{1,5},{2,6},{3,7},{4,0},{5,1},{6,2},{7,3},{8,12},{9,13},{10,... | collective-permute-start | bytes 294920 | tf_op jit(solution)/shard_map/ppermute | solution.py:183
  3.0 10.6 %collective-permute-start = (bf16[4,12288]{1,0:T(4,128)(2,1)}, bf16[4,12288]{1,0:T(4,128)(2,1)S(1)}, u32[]{:S(2)}, u32[]{:S(2)}) collective-permute-start(bf16[4,12288]{1,0:T(4,128)(2,1)} %refs_0_), channel_id=1, source_target_pairs={{0,8},{1,9},{2,10},{3,11},{4,12},{5,13},{6,14},{7,15},{8,0},{9,1},... | collective-permute-start | bytes 294920 | tf_op jit(solution)/shard_map/ppermute | solution.py:183
  5.6 8.1 %collective-permute-start.2 = (bf16[4,12288]{1,0:T(4,128)(2,1)}, bf16[4,12288]{1,0:T(4,128)(2,1)S(1)}, u32[]{:S(2)}, u32[]{:S(2)}) collective-permute-start(bf16[4,12288]{1,0:T(4,128)(2,1)} %refs_0_), channel_id=1, source_target_pairs={{0,12},{1,13},{2,14},{3,15},{4,8},{5,9},{6,10},{7,11},{8,4},{9,5},... | collective-permute-start | bytes 294920 | tf_op jit(solution)/shard_map/ppermute | solution.py:183
  5.6 1.3 %collective-permute-start.5 = (f32[1,128]{1,0:T(1,128)}, f32[1,128]{1,0:T(1,128)S(1)}, u32[]{:S(2)}, u32[]{:S(2)}) collective-permute-start(f32[1,128]{1,0:T(1,128)} %bitcast.12), channel_id=1, source_target_pairs={{0,1},{1,0},{2,3},{3,2},{4,5},{5,4},{6,7},{7,6},{8,9},{9,8},{10,11... | collective-permute-start | bytes 1544 | tf_op jit(solution)/shard_map/ppermute | solution.py:189
  6.9 5.1 %collective-permute-start.6 = (bf16[4,12288]{1,0:T(4,128)(2,1)}, bf16[4,12288]{1,0:T(4,128)(2,1)S(1)}, u32[]{:S(2)}, u32[]{:S(2)}) collective-permute-start(bf16[4,12288]{1,0:T(4,128)(2,1)} %refs_0_), channel_id=1, source_target_pairs={{0,2},{1,3},{2,0},{3,1},{4,6},{5,7},{6,4},{7,5},{8,10},{9,11},{10,... | collective-permute-start | bytes 294920 | tf_op jit(solution)/shard_map/ppermute | solution.py:186
  10.8 4.6 %collective-permute-start.7 = (bf16[4,12288]{1,0:T(4,128)(2,1)S(1)}, bf16[4,12288]{1,0:T(4,128)(2,1)S(1)}, u32[]{:S(2)}, u32[]{:S(2)}) collective-permute-start(bf16[4,12288]{1,0:T(4,128)(2,1)S(1)} %collective-permute-done.4.refs_1_), channel_id=1, source_target_pairs={{0,2},{1,3},{2,0},{3,1},{4,6},{5,7},{6,4},{7,5},{8,10},{9,11},{10,... | collective-permute-start | bytes 294920 | tf_op jit(solution)/shard_map/ppermute | solution.py:186
  15.4 20.6 %collective-permute-start.11 = (bf16[12288,128]{1,0:T(8,128)(2,1)}, bf16[12288,128]{1,0:T(8,128)(2,1)S(1)}, u32[]{:S(2)}, u32[]{:S(2)}) collective-permute-start(bf16[12288,128]{1,0:T(8,128)(2,1)} %refs_4_), channel_id=1, source_target_pairs={{0,1},{1,0},{2,3},{3,2},{4,5},{5,4},{6,7},{7,6},{8,9},{9,8},{10,11... | collective-permute-start | bytes 9437192 | tf_op jit(solution)/shard_map/ppermute | solution.py:189
  15.4 22.6 %collective-permute-start.12 = (bf16[128,12288]{1,0:T(8,128)(2,1)}, bf16[128,12288]{1,0:T(8,128)(2,1)S(1)}, u32[]{:S(2)}, u32[]{:S(2)}) collective-permute-start(bf16[128,12288]{1,0:T(8,128)(2,1)} %refs_5_), channel_id=1, source_target_pairs={{0,1},{1,0},{2,3},{3,2},{4,5},{5,4},{6,7},{7,6},{8,9},{9,8},{10,11... | collective-permute-start | bytes 9437192 | tf_op jit(solution)/shard_map/ppermute | solution.py:189
  15.9 11.0 %collective-permute-start.8 = (bf16[768,512]{1,0:T(8,128)(2,1)}, bf16[768,512]{1,0:T(8,128)(2,1)S(1)}, u32[]{:S(2)}, u32[]{:S(2)}) collective-permute-start(bf16[768,512]{1,0:T(8,128)(2,1)} %refs_3_), channel_id=1, source_target_pairs={{0,1},{1,0},{2,3},{3,2},{4,5},{5,4},{6,7},{7,6},{8,9},{9,8},{10,11... | collective-permute-start | bytes 2359304 | tf_op jit(solution)/shard_map/ppermute | solution.py:189
  15.9 6.2 %collective-permute-start.1 = (bf16[4,12288]{1,0:T(4,128)(2,1)S(1)}, bf16[4,12288]{1,0:T(4,128)(2,1)S(1)}, u32[]{:S(2)}, u32[]{:S(2)}) collective-permute-start(bf16[4,12288]{1,0:T(4,128)(2,1)S(1)} %collective-permute-done.refs_2_), channel_id=1, source_target_pairs={{0,2},{1,3},{2,0},{3,1},{4,6},{5,7},{6,4},{7,5},{8,10},{9,11},{10,... | collective-permute-start | bytes 294920 | tf_op jit(solution)/shard_map/ppermute | solution.py:186
  16.4 6.9 %collective-permute-start.3 = (bf16[4,12288]{1,0:T(4,128)(2,1)S(1)}, bf16[4,12288]{1,0:T(4,128)(2,1)S(1)}, u32[]{:S(2)}, u32[]{:S(2)}) collective-permute-start(bf16[4,12288]{1,0:T(4,128)(2,1)S(1)} %collective-permute-done.2.refs_3_), channel_id=1, source_target_pairs={{0,2},{1,3},{2,0},{3,1},{4,6},{5,7},{6,4},{7,5},{8,10},{9,11},{10,... | collective-permute-start | bytes 294920 | tf_op jit(solution)/shard_map/ppermute | solution.py:186
  21.3 6.4 %copy-start.2 = (bf16[512,768]{1,0:T(8,128)(2,1)S(1)}, bf16[512,768]{1,0:T(8,128)(2,1)}, u32[]{:S(2)}) copy-start(bf16[512,768]{1,0:T(8,128)(2,1)} %refs_6_) | copy-start | bytes 2359300
  21.3 15.4 %copy-start.1 = (f32[128]{0:T(128)S(1)}, f32[128]{0:T(128)}, u32[]{:S(2)}) copy-start(f32[128]{0:T(128)} %param.19) | copy-start | bytes 1540
  27.7 13.9 %collective-permute-start.10 = (bf16[512,768]{1,0:T(8,128)(2,1)S(1)}, bf16[512,768]{1,0:T(8,128)(2,1)S(1)}, u32[]{:S(2)}, u32[]{:S(2)}) collective-permute-start(bf16[512,768]{1,0:T(8,128)(2,1)S(1)} %copy-done.2), channel_id=1, source_target_pairs={{0,1},{1,0},{2,3},{3,2},{4,5},{5,4},{6,7},{7,6},{8,9},{9,8},{10,11... | collective-permute-start | bytes 2359304 | tf_op jit(solution)/shard_map/ppermute | solution.py:189
  27.9 4.4 %collective-permute-start.9 = (f32[32,512]{1,0:T(8,128)S(1)}, f32[32,512]{1,0:T(8,128)S(1)}, u32[]{:S(2)}, u32[]{:S(2)}) collective-permute-start(f32[32,512]{1,0:T(8,128)S(1)} %get-tuple-element.73), channel_id=1, source_target_pairs={{0,2},{1,3},{2,0},{3,1},{4,6},{5,7},{6,4},{7,5},{8,10},{9,11},{10,... | collective-permute-start | bytes 196616 | tf_op jit(solution)/shard_map/ppermute | solution.py:186
  32.3 6.9 %collective-permute-start.13 = (f32[32,512]{1,0:T(8,128)S(1)}, f32[32,512]{1,0:T(8,128)S(1)}, u32[]{:S(2)}, u32[]{:S(2)}) collective-permute-start(f32[32,512]{1,0:T(8,128)S(1)} %get-tuple-element.84), channel_id=1, source_target_pairs={{0,12},{1,13},{2,14},{3,15},{4,8},{5,9},{6,10},{7,11},{8,4},{9,5},... | collective-permute-start | bytes 196616 | tf_op jit(solution)/shard_map/ppermute | solution.py:183
  36.0 5.2 %collective-permute-start.14 = (f32[32,512]{1,0:T(8,128)S(1)}, f32[32,512]{1,0:T(8,128)S(1)}, u32[]{:S(2)}, u32[]{:S(2)}) collective-permute-start(f32[32,512]{1,0:T(8,128)S(1)} %get-tuple-element.85), channel_id=1, source_target_pairs={{0,8},{1,9},{2,10},{3,11},{4,12},{5,13},{6,14},{7,15},{8,0},{9,1},... | collective-permute-start | bytes 196616 | tf_op jit(solution)/shard_map/ppermute | solution.py:183
  36.0 5.6 %collective-permute-start.15 = (f32[32,512]{1,0:T(8,128)S(1)}, f32[32,512]{1,0:T(8,128)S(1)}, u32[]{:S(2)}, u32[]{:S(2)}) collective-permute-start(f32[32,512]{1,0:T(8,128)S(1)} %get-tuple-element.86), channel_id=1, source_target_pairs={{0,4},{1,5},{2,6},{3,7},{4,0},{5,1},{6,2},{7,3},{8,12},{9,13},{10,... | collective-permute-start | bytes 196616 | tf_op jit(solution)/shard_map/ppermute | solution.py:183
  38.0 3.6 %copy-start = (f32[512]{0:T(512)S(1)}, f32[512]{0:T(512)}, u32[]{:S(2)}) copy-start(f32[512]{0:T(512)} %param.22) | copy-start | bytes 6148
  42.0 5.8 %collective-permute-start.21 = (bf16[4,12288]{1,0:T(4,128)(2,1)S(1)}, bf16[4,12288]{1,0:T(4,128)(2,1)S(1)}, u32[]{:S(2)}, u32[]{:S(2)}) collective-permute-start(bf16[4,12288]{1,0:T(4,128)(2,1)S(1)} %get-tuple-element.94), channel_id=1, source_target_pairs={{0,2},{1,3},{2,0},{3,1},{4,6},{5,7},{6,4},{7,5},{8,10},{9,11},{10,... | collective-permute-start | bytes 294920 | tf_op jit(solution)/shard_map/ppermute | solution.py:186
  42.6 7.2 %collective-permute-start.19 = (bf16[4,12288]{1,0:T(4,128)(2,1)S(1)}, bf16[4,12288]{1,0:T(4,128)(2,1)S(1)}, u32[]{:S(2)}, u32[]{:S(2)}) collective-permute-start(bf16[4,12288]{1,0:T(4,128)(2,1)S(1)} %get-tuple-element.92), channel_id=1, source_target_pairs={{0,2},{1,3},{2,0},{3,1},{4,6},{5,7},{6,4},{7,5},{8,10},{9,11},{10,... | collective-permute-start | bytes 294920 | tf_op jit(solution)/shard_map/ppermute | solution.py:186
  44.1 6.6 %collective-permute-start.17 = (bf16[4,12288]{1,0:T(4,128)(2,1)S(1)}, bf16[4,12288]{1,0:T(4,128)(2,1)S(1)}, u32[]{:S(2)}, u32[]{:S(2)}) collective-permute-start(bf16[4,12288]{1,0:T(4,128)(2,1)S(1)} %get-tuple-element.90), channel_id=1, source_target_pairs={{0,2},{1,3},{2,0},{3,1},{4,6},{5,7},{6,4},{7,5},{8,10},{9,11},{10,... | collective-permute-start | bytes 294920 | tf_op jit(solution)/shard_map/ppermute | solution.py:186
  44.6 8.0 %collective-permute-start.16 = (bf16[4,12288]{1,0:T(4,128)(2,1)S(1)}, bf16[4,12288]{1,0:T(4,128)(2,1)S(1)}, u32[]{:S(2)}, u32[]{:S(2)}) collective-permute-start(bf16[4,12288]{1,0:T(4,128)(2,1)S(1)} %get-tuple-element.88), channel_id=1, source_target_pairs={{0,2},{1,3},{2,0},{3,1},{4,6},{5,7},{6,4},{7,5},{8,10},{9,11},{10,... | collective-permute-start | bytes 294920 | tf_op jit(solution)/shard_map/ppermute | solution.py:186
  47.9 6.5 %collective-permute-start.22 = (bf16[4,12288]{1,0:T(4,128)(2,1)S(1)}, bf16[4,12288]{1,0:T(4,128)(2,1)S(1)}, u32[]{:S(2)}, u32[]{:S(2)}) collective-permute-start(bf16[4,12288]{1,0:T(4,128)(2,1)S(1)} %add_convert_fusion), channel_id=1, source_target_pairs={{0,12},{1,13},{2,14},{3,15},{4,8},{5,9},{6,10},{7,11},{8,4},{9,5},... | collective-permute-start | bytes 294920 | tf_op jit(solution)/shard_map/ppermute | solution.py:183
  49.9 6.6 %collective-permute-start.20 = (bf16[4,12288]{1,0:T(4,128)(2,1)S(1)}, bf16[4,12288]{1,0:T(4,128)(2,1)S(1)}, u32[]{:S(2)}, u32[]{:S(2)}) collective-permute-start(bf16[4,12288]{1,0:T(4,128)(2,1)S(1)} %add_convert_fusion.1), channel_id=1, source_target_pairs={{0,8},{1,9},{2,10},{3,11},{4,12},{5,13},{6,14},{7,15},{8,0},{9,1},... | collective-permute-start | bytes 294920 | tf_op jit(solution)/shard_map/ppermute | solution.py:183
  50.7 5.7 %collective-permute-start.18 = (bf16[4,12288]{1,0:T(4,128)(2,1)S(1)}, bf16[4,12288]{1,0:T(4,128)(2,1)S(1)}, u32[]{:S(2)}, u32[]{:S(2)}) collective-permute-start(bf16[4,12288]{1,0:T(4,128)(2,1)S(1)} %add_convert_fusion.2), channel_id=1, source_target_pairs={{0,4},{1,5},{2,6},{3,7},{4,0},{5,1},{6,2},{7,3},{8,12},{9,13},{10,... | collective-permute-start | bytes 294920 | tf_op jit(solution)/shard_map/ppermute | solution.py:183

commit v26 on v21

--- a/solution.py
+++ b/solution.py
@@ -278,10 +278,18 @@
         6 * MIB,
     )(place, total, low_bias.reshape(1, rank), low_out_near, low_out_mate, part, *got)
 
-    sums = []
+    sums, here, mark = [], None, None
     for k in range(groups - 1, -1, -1):
-        here = parts[k] + beside(parts[groups + k]).astype(f32)
-        sums.append(across(here.astype(bf16), k) if k else here)
+        mine = parts[groups + k]
+        if k == 0:
+            mine, _ = lax.optimization_barrier((mine, mark))
+        come = beside(mine)
+        if here is not None:
+            come, _ = lax.optimization_barrier((come, here))
+        here = parts[k] + come.astype(f32)
+        here = here.astype(bf16) if k else here
+        mark = here if k == groups // 2 else mark
+        sums.append(across(here, k) if k else here)
     return call(functools.partial(last_body, groups), [shape(row_dev, width)], [VMEM] * groups, 16)(*sums[::-1])[0]
 
 

time: 51.1 us -> 51.5 us (level)
  starting transfers between devices: 25.2 us -> 26.2 us
  waiting for transfers between devices: 13.9 us -> 13.3 us
    ppermute x9, waiting for transfers between devices: 7.24 us -> 4.99 us  [across(): return lax.ppermute(x, 'blk', [(i, i ^ 4 * k) for i in range(devices)])]
    ppermute x9, waiting for transfers between devices: 5.61 us -> 7.22 us  [beside(): return lax.ppermute(x, 'blk', [(i, i ^ 2) for i in range(devices)])]
    ppermute x9, starting transfers between devices: 9.93 us -> 10.5 us  [beside(): return lax.ppermute(x, 'blk', [(i, i ^ 2) for i in range(devices)])]
  transfers between devices with their start and end apart: 23 -> 23, of which waited for: 10 -> 10; matrix products, arithmetic and copies ran while one was open for 6% -> 6% of each run, Pallas kernels for 15% -> 14%
where the time goes in v26:
time: 51.5 us; the launch traced here: 51.3 us
  starting transfers between devices  26.2 us (51%)
  waiting for transfers between devices  13.3 us (26%)
  Pallas kernels  8.58 us (17%)
  other arithmetic  2.23 us (4%)
  local copies, waits for them, and re-layouts  0.86 us (2%)
    ppermute x9, starting transfers between devices, across(): return lax.ppermute(x, 'blk', [(i, i ^ 4 * k) for i in range(devices)])  14.7 us
    ppermute x9, starting transfers between devices, beside(): return lax.ppermute(x, 'blk', [(i, i ^ 2) for i in range(devices)])  10.5 us
    ppermute x9, waiting for transfers between devices, beside(): return lax.ppermute(x, 'blk', [(i, i ^ 2) for i in range(devices)])  7.22 us
    ppermute x9, waiting for transfers between devices, across(): return lax.ppermute(x, 'blk', [(i, i ^ 4 * k) for i in range(devices)])  4.99 us
    pallas_call x1, Pallas kernels, shards(): call(functools.partial(load_body, len(near)), [shape(*x.shape, dtype=x.dt...  3.39 us
    pallas_call x1, Pallas kernels, shards(): call(functools.partial(act_body, step), [shape(rows, 2 * block)], [VMEM]...  1.21 us
    pallas_call x1, Pallas kernels, shards(): call(functools.partial(part_body, step), [shape(rows, width, dtype=f32)],...  1.19 us
    ppermute x5, waiting for transfers between devices, core(): return lax.ppermute(x, 'blk', [(i, i ^ 1) for i in range(devices)])  1.1 us
  transfers between devices with their start and end apart: 23, of which 10 were waited for; matrix products, arithmetic and copies ran while one was open for 6% of the time, Pallas kernels for 14%

profile of v26, /device:TPU:0, one launch (start us, length us, event | category | flops | bytes accessed | tf_op | source)
XLA Modules:
  0.0 51.3 jit_solution(6164112005644678718)
XLA Ops:
  0.5 2.6 %collective-permute-start.4 = (bf16[4,12288]{1,0:T(4,128)(2,1)}, bf16[4,12288]{1,0:T(4,128)(2,1)S(1)}, u32[]{:S(2)}, u32[]{:S(2)}) collective-permute-start(bf16[4,12288]{1,0:T(4,128)(2,1)} %refs_0_), channel_id=1, source_target_pairs={{0,4},{1,5},{2,6},{3,7},{4,0},{5,1},{6,2},{7,3},{8,12},{9,13},{10,... | collective-permute-start | bytes 294920 | tf_op jit(solution)/shard_map/ppermute | solution.py:183
  3.0 2.6 %collective-permute-start = (bf16[4,12288]{1,0:T(4,128)(2,1)}, bf16[4,12288]{1,0:T(4,128)(2,1)S(1)}, u32[]{:S(2)}, u32[]{:S(2)}) collective-permute-start(bf16[4,12288]{1,0:T(4,128)(2,1)} %refs_0_), channel_id=1, source_target_pairs={{0,8},{1,9},{2,10},{3,11},{4,12},{5,13},{6,14},{7,15},{8,0},{9,1},... | collective-permute-start | bytes 294920 | tf_op jit(solution)/shard_map/ppermute | solution.py:183
  5.8 1.1 %collective-permute-done.5.b_mate = f32[1,128]{1,0:T(1,128)S(1)} collective-permute-done((f32[1,128]{1,0:T(1,128)}, f32[1,128]{1,0:T(1,128)S(1)}, u32[]{:S(2)}, u32[]{:S(2)}) %collective-permute-start.5) | collective-permute-done | bytes 544 | tf_op jit(solution)/shard_map/ppermute | solution.py:189
  6.9 2.0 %collective-permute-start.6 = (bf16[4,12288]{1,0:T(4,128)(2,1)}, bf16[4,12288]{1,0:T(4,128)(2,1)S(1)}, u32[]{:S(2)}, u32[]{:S(2)}) collective-permute-start(bf16[4,12288]{1,0:T(4,128)(2,1)} %refs_0_), channel_id=1, source_target_pairs={{0,2},{1,3},{2,0},{3,1},{4,6},{5,7},{6,4},{7,5},{8,10},{9,11},{10,... | collective-permute-start | bytes 294920 | tf_op jit(solution)/shard_map/ppermute | solution.py:186
  8.8 0.8 %copy.13 = s32[4,6]{0,1:T(8,128)S(1)} copy(s32[4,6]{1,0:T(4,128)} %param.15) | data formatting | bytes 192 | tf_op jit(solution)/shard_map/optimization_barrier | solution.py:199
  9.7 0.7 %fusion.1 = s32[4,6]{0,1:T(8,128)S(1)} fusion(s32[4]{0:T(128)} %param.16), kind=kLoop, calls=%fused_computation.12 | loop fusion | flops 48 | bytes 112 | tf_op jit(solution)/shard_map/convert_element_type | solution.py:150
  10.4 0.7 %fusion = s32[16,16]{1,0:T(8,128)S(1)} fusion(s32[16]{0:T(128)} %param.17), kind=kLoop, calls=%fused_computation.10 | loop fusion | flops 512 | bytes 1088 | tf_op jit(solution)/shard_map/convert_element_type | solution.py:153
  11.6 0.7 %collective-permute-done.6.refs_4_ = bf16[4,12288]{1,0:T(4,128)(2,1)S(1)} collective-permute-done((bf16[4,12288]{1,0:T(4,128)(2,1)}, bf16[4,12288]{1,0:T(4,128)(2,1)S(1)}, u32[]{:S(2)}, u32[]{:S(2)}) %collective-permute-start.6) | collective-permute-done | bytes 98336 | tf_op jit(solution)/shard_map/ppermute | solution.py:186
  12.3 1.7 %collective-permute-done.refs_2_ = bf16[4,12288]{1,0:T(4,128)(2,1)S(1)} collective-permute-done((bf16[4,12288]{1,0:T(4,128)(2,1)}, bf16[4,12288]{1,0:T(4,128)(2,1)S(1)}, u32[]{:S(2)}, u32[]{:S(2)}) %collective-permute-start) | collective-permute-done | bytes 98336 | tf_op jit(solution)/shard_map/ppermute | solution.py:183
  14.8 1.7 %collective-permute-start.1 = (bf16[4,12288]{1,0:T(4,128)(2,1)S(1)}, bf16[4,12288]{1,0:T(4,128)(2,1)S(1)}, u32[]{:S(2)}, u32[]{:S(2)}) collective-permute-start(bf16[4,12288]{1,0:T(4,128)(2,1)S(1)} %collective-permute-done.refs_2_), channel_id=1, source_target_pairs={{0,2},{1,3},{2,0},{3,1},{4,6},{5,7},{6,4},{7,5},{8,10},{9,11},{10,... | collective-permute-start | bytes 294920 | tf_op jit(solution)/shard_map/ppermute | solution.py:186
  16.8 3.4 %shard_map.118 = (bf16[4,12288]{1,0:T(4,128)(2,1)S(1)}, f32[1,12288]{1,0:T(1,128)S(1)}, f32[1,12288]{1,0:T(1,128)S(1)}, bf16[768,512]{1,0:T(8,128)(2,1)S(1)}, bf...) custom-call(bf16[4,12288]{1,0:T(4,128)(2,1)} %refs_0_, ...), custom_call_target="tpu_custom_call" | custom-call | bytes 8388608 | tf_op jit(solution)/shard_map/pallas_call | solution.py:215
  20.2 0.8 %shard_map.119 = (bf16[16,12288]{1,0:T(8,128)(2,1)S(1)}, bf16[8,12288]{1,0:T(8,128)(2,1)S(1)}) custom-call(bf16[4,12288]{1,0:T(4,128)(2,1)S(1)} %get-tuple-element.65.refs_0_, bf16[4,12288]{1,0:T(4,128)(2,1)S(1)} %collective-permute-done.4.refs_1_, bf16[4,12288]{1,0:T(4,128)(2,1)S(1)} %collective-permute-done.refs_2_, ...), custom_call_target="tpu_custom_call" | custom-call | bytes 4194304 | tf_op jit(solution)/shard_map/pallas_call | solution.py:231
  21.0 1.0 %collective-permute-done.3.refs_1_ = bf16[4,12288]{1,0:T(4,128)(2,1)S(1)} collective-permute-done((bf16[4,12288]{1,0:T(4,128)(2,1)S(1)}, bf16[4,12288]{1,0:T(4,128)(2,1)S(1)}, u32[]{:S(2)}, u32[]{:S(2)}) %collective-permute-start.3) | collective-permute-done | bytes 98336 | tf_op jit(solution)/shard_map/ppermute | solution.py:186
  22.1 0.8 %shard_map.120 = (bf16[16,12288]{1,0:T(8,128)(2,1)S(1)}, f32[32,512]{1,0:T(8,128)S(1)}, bf16[32,512]{1,0:T(8,128)(2,1)S(1)}) custom-call(s32[1]{0:T(128)} %bitcast.place, bf16[4,12288]{1,0:T(4,128)(2,1)S(1)} %collective-permute-done.1.refs_0_, bf16[4,12288]{1,0:T(4,128)(2,1)S(1)} %collective-permute-done.3.refs_1_, ...), custom_call_target="tpu_custom_call" | custom-call | bytes 4194304 | tf_op jit(solution)/shard_map/pallas_call | solution.py:239
  22.9 1.8 %collective-permute-start.9 = (bf16[32,512]{1,0:T(8,128)(2,1)S(1)}, bf16[32,512]{1,0:T(8,128)(2,1)S(1)}, u32[]{:S(2)}, u32[]{:S(2)}) collective-permute-start(bf16[32,512]{1,0:T(8,128)(2,1)S(1)} %get-tuple-element.75), channel_id=1, source_target_pairs={{0,2},{1,3},{2,0},{3,1},{4,6},{5,7},{6,4},{7,5},{8,10},{9,11},{10,... | collective-permute-start | bytes 98312 | tf_op jit(solution)/shard_map/ppermute | solution.py:186
  24.6 2.2 %collective-permute-done.9.got = bf16[32,512]{1,0:T(8,128)(2,1)S(1)} collective-permute-done((bf16[32,512]{1,0:T(8,128)(2,1)S(1)}, bf16[32,512]{1,0:T(8,128)(2,1)S(1)}, u32[]{:S(2)}, u32[]{:S(2)}) %collective-permute-start.9) | collective-permute-done | bytes 32800 | tf_op jit(solution)/shard_map/ppermute | solution.py:186
  26.8 3.9 %collective-permute-start.13 = (bf16[32,512]{1,0:T(8,128)(2,1)S(1)}, bf16[32,512]{1,0:T(8,128)(2,1)S(1)}, u32[]{:S(2)}, u32[]{:S(2)}) collective-permute-start(bf16[32,512]{1,0:T(8,128)(2,1)S(1)} %get-tuple-element.86), channel_id=1, source_target_pairs={{0,12},{1,13},{2,14},{3,15},{4,8},{5,9},{6,10},{7,11},{8,4},{9,5},... | collective-permute-start | bytes 98312 | tf_op jit(solution)/shard_map/ppermute | solution.py:183
  30.7 0.6 %collective-permute-start.15 = (bf16[32,512]{1,0:T(8,128)(2,1)S(1)}, bf16[32,512]{1,0:T(8,128)(2,1)S(1)}, u32[]{:S(2)}, u32[]{:S(2)}) collective-permute-start(bf16[32,512]{1,0:T(8,128)(2,1)S(1)} %get-tuple-element.88), channel_id=1, source_target_pairs={{0,4},{1,5},{2,6},{3,7},{4,0},{5,1},{6,2},{7,3},{8,12},{9,13},{10,... | collective-permute-start | bytes 98312 | tf_op jit(solution)/shard_map/ppermute | solution.py:183
  31.4 1.2 %shard_map.122.act = bf16[32,256]{1,0:T(8,128)(2,1)S(1)} custom-call(bf16[16,12288]{1,0:T(8,128)(2,1)S(1)} %get-tuple-element.70.refs_2_.near, bf16[16,12288]{1,0:T(8,128)(2,1)S(1)} %get-tuple-element.79.far, bf16[12288,128]{1,0:T(8,128)(2,1)S(1)} %get-tuple-element.80.w_own, bf16[12288,128]{1,0:T(8,128)(2,1)S(1)} %collective-permute-done.10.w_mate, ...), custom_call_target="tpu_custom_call" | custom-call | bytes 4194304 | tf_op jit(solution)/shard_map/pallas_call | solution.py:249
  32.6 1.2 %shard_map.123.part = f32[32,12288]{1,0:T(8,128)S(1)} custom-call(bf16[32,256]{1,0:T(8,128)(2,1)S(1)} %shard_map.122.act, bf16[128,12288]{1,0:T(8,128)(2,1)S(1)} %get-tuple-element.84.w_own, bf16[128,12288]{1,0:T(8,128)(2,1)S(1)} %collective-permute-done.12.w_mate), custom_call_target="tpu_custom_call" | custom-call | bytes 6291456 | tf_op jit(solution)/shard_map/pallas_call | solution.py:264
  33.8 1.7 %collective-permute-done.14.refs_1_ = bf16[32,512]{1,0:T(8,128)(2,1)S(1)} collective-permute-done((bf16[32,512]{1,0:T(8,128)(2,1)S(1)}, bf16[32,512]{1,0:T(8,128)(2,1)S(1)}, u32[]{:S(2)}, u32[]{:S(2)}) %collective-permute-start.14) | collective-permute-done | bytes 32800 | tf_op jit(solution)/shard_map/ppermute | solution.py:183
  36.0 1.6 %collective-permute-start.17 = (bf16[4,12288]{1,0:T(4,128)(2,1)S(1)}, bf16[4,12288]{1,0:T(4,128)(2,1)S(1)}, u32[]{:S(2)}, u32[]{:S(2)}) collective-permute-start(bf16[4,12288]{1,0:T(4,128)(2,1)S(1)} %get-tuple-element.94), channel_id=1, source_target_pairs={{0,2},{1,3},{2,0},{3,1},{4,6},{5,7},{6,4},{7,5},{8,10},{9,11},{10,... | collective-permute-start | bytes 294920 | tf_op jit(solution)/shard_map/ppermute | solution.py:186
  37.6 0.5 collective-permute-start.16
  38.1 1.5 %collective-permute-start.19 = (bf16[4,12288]{1,0:T(4,128)(2,1)S(1)}, bf16[4,12288]{1,0:T(4,128)(2,1)S(1)}, u32[]{:S(2)}, u32[]{:S(2)}) collective-permute-start(bf16[4,12288]{1,0:T(4,128)(2,1)S(1)} %get-tuple-element.98), channel_id=1, source_target_pairs={{0,2},{1,3},{2,0},{3,1},{4,6},{5,7},{6,4},{7,5},{8,10},{9,11},{10,... | collective-permute-start | bytes 294920 | tf_op jit(solution)/shard_map/ppermute | solution.py:186
  39.6 1.1 %collective-permute-done.17 = bf16[4,12288]{1,0:T(4,128)(2,1)S(1)} collective-permute-done((bf16[4,12288]{1,0:T(4,128)(2,1)S(1)}, bf16[4,12288]{1,0:T(4,128)(2,1)S(1)}, u32[]{:S(2)}, u32[]{:S(2)}) %collective-permute-start.17) | collective-permute-done | bytes 98336 | tf_op jit(solution)/shard_map/ppermute | solution.py:186
  40.7 2.2 %collective-permute-start.22 = (bf16[4,12288]{1,0:T(4,128)(2,1)S(1)}, bf16[4,12288]{1,0:T(4,128)(2,1)S(1)}, u32[]{:S(2)}, u32[]{:S(2)}) collective-permute-start(bf16[4,12288]{1,0:T(4,128)(2,1)S(1)} %add_convert_fusion.2), channel_id=1, source_target_pairs={{0,12},{1,13},{2,14},{3,15},{4,8},{5,9},{6,10},{7,11},{8,4},{9,5},... | collective-permute-start | bytes 294920 | tf_op jit(solution)/shard_map/ppermute | solution.py:183
  43.0 1.3 %collective-permute-start.21 = (bf16[4,12288]{1,0:T(4,128)(2,1)S(1)}, bf16[4,12288]{1,0:T(4,128)(2,1)S(1)}, u32[]{:S(2)}, u32[]{:S(2)}) collective-permute-start(bf16[4,12288]{1,0:T(4,128)(2,1)S(1)} %add_convert_fusion.1), channel_id=1, source_target_pairs={{0,8},{1,9},{2,10},{3,11},{4,12},{5,13},{6,14},{7,15},{8,0},{9,1},... | collective-permute-start | bytes 294920 | tf_op jit(solution)/shard_map/ppermute | solution.py:183
  44.3 1.1 %collective-permute-start.18 = (bf16[4,12288]{1,0:T(4,128)(2,1)S(1)}, bf16[4,12288]{1,0:T(4,128)(2,1)S(1)}, u32[]{:S(2)}, u32[]{:S(2)}) collective-permute-start(bf16[4,12288]{1,0:T(4,128)(2,1)S(1)} %get-tuple-element.96), channel_id=1, source_target_pairs={{0,2},{1,3},{2,0},{3,1},{4,6},{5,7},{6,4},{7,5},{8,10},{9,11},{10,... | collective-permute-start | bytes 294920 | tf_op jit(solution)/shard_map/ppermute | solution.py:186
  45.5 1.5 %collective-permute-start.20 = (bf16[4,12288]{1,0:T(4,128)(2,1)S(1)}, bf16[4,12288]{1,0:T(4,128)(2,1)S(1)}, u32[]{:S(2)}, u32[]{:S(2)}) collective-permute-start(bf16[4,12288]{1,0:T(4,128)(2,1)S(1)} %add_convert_fusion), channel_id=1, source_target_pairs={{0,4},{1,5},{2,6},{3,7},{4,0},{5,1},{6,2},{7,3},{8,12},{9,13},{10,... | collective-permute-start | bytes 294920 | tf_op jit(solution)/shard_map/ppermute | solution.py:183
  47.0 2.0 %collective-permute-done.18 = bf16[4,12288]{1,0:T(4,128)(2,1)S(1)} collective-permute-done((bf16[4,12288]{1,0:T(4,128)(2,1)S(1)}, bf16[4,12288]{1,0:T(4,128)(2,1)S(1)}, u32[]{:S(2)}, u32[]{:S(2)}) %collective-permute-start.18) | collective-permute-done | bytes 98336 | tf_op jit(solution)/shard_map/ppermute | solution.py:186
  49.0 1.6 %collective-permute-done.20.refs_1_ = bf16[4,12288]{1,0:T(4,128)(2,1)S(1)} collective-permute-done((bf16[4,12288]{1,0:T(4,128)(2,1)S(1)}, bf16[4,12288]{1,0:T(4,128)(2,1)S(1)}, u32[]{:S(2)}, u32[]{:S(2)}) %collective-permute-start.20) | collective-permute-done | bytes 98336 | tf_op jit(solution)/shard_map/ppermute | solution.py:183
  50.6 0.7 %shard_map.125 = bf16[4,12288]{1,0:T(4,128)(2,1)} custom-call(f32[4,12288]{1,0:T(4,128)S(1)} %convert_add_fusion.refs_0_, bf16[4,12288]{1,0:T(4,128)(2,1)S(1)} %collective-permute-done.20.refs_1_, bf16[4,12288]{1,0:T(4,128)(2,1)S(1)} %collective-permute-done.21.refs_2_, bf16[4,12288]{1,0:T(4,128)(2,1)S(1)} %collective-permute-done.22.refs_3_), custom_call_target="tpu_custom_call" | custom-call | bytes 2097152 | tf_op jit(solution)/shard_map/pallas_call | solution.py:293
  (43 shorter events, 3.0 us)
Async XLA Ops:
  0.0 14.3 %collective-permute-start.10 = (bf16[12288,128]{1,0:T(8,128)(2,1)}, bf16[12288,128]{1,0:T(8,128)(2,1)S(1)}, u32[]{:S(2)}, u32[]{:S(2)}) collective-permute-start(bf16[12288,128]{1,0:T(8,128)(2,1)} %refs_4_), channel_id=1, source_target_pairs={{0,1},{1,0},{2,3},{3,2},{4,5},{5,4},{6,7},{7,6},{8,9},{9,8},{10,11... | collective-permute-start | bytes 9437192 | tf_op jit(solution)/shard_map/ppermute | solution.py:189
  0.5 8.4 %collective-permute-start.4 = (bf16[4,12288]{1,0:T(4,128)(2,1)}, bf16[4,12288]{1,0:T(4,128)(2,1)S(1)}, u32[]{:S(2)}, u32[]{:S(2)}) collective-permute-start(bf16[4,12288]{1,0:T(4,128)(2,1)} %refs_0_), channel_id=1, source_target_pairs={{0,4},{1,5},{2,6},{3,7},{4,0},{5,1},{6,2},{7,3},{8,12},{9,13},{10,... | collective-permute-start | bytes 294920 | tf_op jit(solution)/shard_map/ppermute | solution.py:183
  3.0 11.0 %collective-permute-start = (bf16[4,12288]{1,0:T(4,128)(2,1)}, bf16[4,12288]{1,0:T(4,128)(2,1)S(1)}, u32[]{:S(2)}, u32[]{:S(2)}) collective-permute-start(bf16[4,12288]{1,0:T(4,128)(2,1)} %refs_0_), channel_id=1, source_target_pairs={{0,8},{1,9},{2,10},{3,11},{4,12},{5,13},{6,14},{7,15},{8,0},{9,1},... | collective-permute-start | bytes 294920 | tf_op jit(solution)/shard_map/ppermute | solution.py:183
  5.6 8.4 %collective-permute-start.2 = (bf16[4,12288]{1,0:T(4,128)(2,1)}, bf16[4,12288]{1,0:T(4,128)(2,1)S(1)}, u32[]{:S(2)}, u32[]{:S(2)}) collective-permute-start(bf16[4,12288]{1,0:T(4,128)(2,1)} %refs_0_), channel_id=1, source_target_pairs={{0,12},{1,13},{2,14},{3,15},{4,8},{5,9},{6,10},{7,11},{8,4},{9,5},... | collective-permute-start | bytes 294920 | tf_op jit(solution)/shard_map/ppermute | solution.py:183
  5.6 1.3 %collective-permute-start.5 = (f32[1,128]{1,0:T(1,128)}, f32[1,128]{1,0:T(1,128)S(1)}, u32[]{:S(2)}, u32[]{:S(2)}) collective-permute-start(f32[1,128]{1,0:T(1,128)} %bitcast.12), channel_id=1, source_target_pairs={{0,1},{1,0},{2,3},{3,2},{4,5},{5,4},{6,7},{7,6},{8,9},{9,8},{10,11... | collective-permute-start | bytes 1544 | tf_op jit(solution)/shard_map/ppermute | solution.py:189
  6.9 5.4 %collective-permute-start.6 = (bf16[4,12288]{1,0:T(4,128)(2,1)}, bf16[4,12288]{1,0:T(4,128)(2,1)S(1)}, u32[]{:S(2)}, u32[]{:S(2)}) collective-permute-start(bf16[4,12288]{1,0:T(4,128)(2,1)} %refs_0_), channel_id=1, source_target_pairs={{0,2},{1,3},{2,0},{3,1},{4,6},{5,7},{6,4},{7,5},{8,10},{9,11},{10,... | collective-permute-start | bytes 294920 | tf_op jit(solution)/shard_map/ppermute | solution.py:186
  9.6 4.6 %collective-permute-start.7 = (bf16[4,12288]{1,0:T(4,128)(2,1)S(1)}, bf16[4,12288]{1,0:T(4,128)(2,1)S(1)}, u32[]{:S(2)}, u32[]{:S(2)}) collective-permute-start(bf16[4,12288]{1,0:T(4,128)(2,1)S(1)} %collective-permute-done.4.refs_1_), channel_id=1, source_target_pairs={{0,2},{1,3},{2,0},{3,1},{4,6},{5,7},{6,4},{7,5},{8,10},{9,11},{10,... | collective-permute-start | bytes 294920 | tf_op jit(solution)/shard_map/ppermute | solution.py:186
  14.3 18.3 %collective-permute-start.12 = (bf16[128,12288]{1,0:T(8,128)(2,1)}, bf16[128,12288]{1,0:T(8,128)(2,1)S(1)}, u32[]{:S(2)}, u32[]{:S(2)}) collective-permute-start(bf16[128,12288]{1,0:T(8,128)(2,1)} %refs_5_), channel_id=1, source_target_pairs={{0,1},{1,0},{2,3},{3,2},{4,5},{5,4},{6,7},{7,6},{8,9},{9,8},{10,11... | collective-permute-start | bytes 9437192 | tf_op jit(solution)/shard_map/ppermute | solution.py:189
  14.3 7.8 %collective-permute-start.8 = (bf16[768,512]{1,0:T(8,128)(2,1)}, bf16[768,512]{1,0:T(8,128)(2,1)S(1)}, u32[]{:S(2)}, u32[]{:S(2)}) collective-permute-start(bf16[768,512]{1,0:T(8,128)(2,1)} %refs_3_), channel_id=1, source_target_pairs={{0,1},{1,0},{2,3},{3,2},{4,5},{5,4},{6,7},{7,6},{8,9},{9,8},{10,11... | collective-permute-start | bytes 2359304 | tf_op jit(solution)/shard_map/ppermute | solution.py:189
  14.8 20.8 %collective-permute-start.11 = (bf16[512,768]{1,0:T(8,128)(2,1)}, bf16[512,768]{1,0:T(8,128)(2,1)S(1)}, u32[]{:S(2)}, u32[]{:S(2)}) collective-permute-start(bf16[512,768]{1,0:T(8,128)(2,1)} %refs_6_), channel_id=1, source_target_pairs={{0,1},{1,0},{2,3},{3,2},{4,5},{5,4},{6,7},{7,6},{8,9},{9,8},{10,11... | collective-permute-start | bytes 2359304 | tf_op jit(solution)/shard_map/ppermute | solution.py:189
  14.8 6.3 %collective-permute-start.1 = (bf16[4,12288]{1,0:T(4,128)(2,1)S(1)}, bf16[4,12288]{1,0:T(4,128)(2,1)S(1)}, u32[]{:S(2)}, u32[]{:S(2)}) collective-permute-start(bf16[4,12288]{1,0:T(4,128)(2,1)S(1)} %collective-permute-done.refs_2_), channel_id=1, source_target_pairs={{0,2},{1,3},{2,0},{3,1},{4,6},{5,7},{6,4},{7,5},{8,10},{9,11},{10,... | collective-permute-start | bytes 294920 | tf_op jit(solution)/shard_map/ppermute | solution.py:186
  16.5 5.6 %collective-permute-start.3 = (bf16[4,12288]{1,0:T(4,128)(2,1)S(1)}, bf16[4,12288]{1,0:T(4,128)(2,1)S(1)}, u32[]{:S(2)}, u32[]{:S(2)}) collective-permute-start(bf16[4,12288]{1,0:T(4,128)(2,1)S(1)} %collective-permute-done.2.refs_3_), channel_id=1, source_target_pairs={{0,2},{1,3},{2,0},{3,1},{4,6},{5,7},{6,4},{7,5},{8,10},{9,11},{10,... | collective-permute-start | bytes 294920 | tf_op jit(solution)/shard_map/ppermute | solution.py:186
  20.2 11.2 %copy-start.1 = (f32[128]{0:T(128)S(1)}, f32[128]{0:T(128)}, u32[]{:S(2)}) copy-start(f32[128]{0:T(128)} %param.19) | copy-start | bytes 1540
  22.9 3.9 %collective-permute-start.9 = (bf16[32,512]{1,0:T(8,128)(2,1)S(1)}, bf16[32,512]{1,0:T(8,128)(2,1)S(1)}, u32[]{:S(2)}, u32[]{:S(2)}) collective-permute-start(bf16[32,512]{1,0:T(8,128)(2,1)S(1)} %get-tuple-element.75), channel_id=1, source_target_pairs={{0,2},{1,3},{2,0},{3,1},{4,6},{5,7},{6,4},{7,5},{8,10},{9,11},{10,... | collective-permute-start | bytes 98312 | tf_op jit(solution)/shard_map/ppermute | solution.py:186
  26.8 7.0 %collective-permute-start.13 = (bf16[32,512]{1,0:T(8,128)(2,1)S(1)}, bf16[32,512]{1,0:T(8,128)(2,1)S(1)}, u32[]{:S(2)}, u32[]{:S(2)}) collective-permute-start(bf16[32,512]{1,0:T(8,128)(2,1)S(1)} %get-tuple-element.86), channel_id=1, source_target_pairs={{0,12},{1,13},{2,14},{3,15},{4,8},{5,9},{6,10},{7,11},{8,4},{9,5},... | collective-permute-start | bytes 98312 | tf_op jit(solution)/shard_map/ppermute | solution.py:183
  30.7 4.8 %collective-permute-start.14 = (bf16[32,512]{1,0:T(8,128)(2,1)S(1)}, bf16[32,512]{1,0:T(8,128)(2,1)S(1)}, u32[]{:S(2)}, u32[]{:S(2)}) collective-permute-start(bf16[32,512]{1,0:T(8,128)(2,1)S(1)} %get-tuple-element.87), channel_id=1, source_target_pairs={{0,8},{1,9},{2,10},{3,11},{4,12},{5,13},{6,14},{7,15},{8,0},{9,1},... | collective-permute-start | bytes 98312 | tf_op jit(solution)/shard_map/ppermute | solution.py:183
  30.7 4.8 %collective-permute-start.15 = (bf16[32,512]{1,0:T(8,128)(2,1)S(1)}, bf16[32,512]{1,0:T(8,128)(2,1)S(1)}, u32[]{:S(2)}, u32[]{:S(2)}) collective-permute-start(bf16[32,512]{1,0:T(8,128)(2,1)S(1)} %get-tuple-element.88), channel_id=1, source_target_pairs={{0,4},{1,5},{2,6},{3,7},{4,0},{5,1},{6,2},{7,3},{8,12},{9,13},{10,... | collective-permute-start | bytes 98312 | tf_op jit(solution)/shard_map/ppermute | solution.py:183
  32.6 2.9 %copy-start = (f32[512]{0:T(512)S(1)}, f32[512]{0:T(512)}, u32[]{:S(2)}) copy-start(f32[512]{0:T(512)} %param.22) | copy-start | bytes 6148
  36.0 4.7 %collective-permute-start.17 = (bf16[4,12288]{1,0:T(4,128)(2,1)S(1)}, bf16[4,12288]{1,0:T(4,128)(2,1)S(1)}, u32[]{:S(2)}, u32[]{:S(2)}) collective-permute-start(bf16[4,12288]{1,0:T(4,128)(2,1)S(1)} %get-tuple-element.94), channel_id=1, source_target_pairs={{0,2},{1,3},{2,0},{3,1},{4,6},{5,7},{6,4},{7,5},{8,10},{9,11},{10,... | collective-permute-start | bytes 294920 | tf_op jit(solution)/shard_map/ppermute | solution.py:186
  37.6 5.4 %collective-permute-start.16 = (bf16[4,12288]{1,0:T(4,128)(2,1)S(1)}, bf16[4,12288]{1,0:T(4,128)(2,1)S(1)}, u32[]{:S(2)}, u32[]{:S(2)}) collective-permute-start(bf16[4,12288]{1,0:T(4,128)(2,1)S(1)} %get-tuple-element.92), channel_id=1, source_target_pairs={{0,2},{1,3},{2,0},{3,1},{4,6},{5,7},{6,4},{7,5},{8,10},{9,11},{10,... | collective-permute-start | bytes 294920 | tf_op jit(solution)/shard_map/ppermute | solution.py:186
  38.1 6.2 %collective-permute-start.19 = (bf16[4,12288]{1,0:T(4,128)(2,1)S(1)}, bf16[4,12288]{1,0:T(4,128)(2,1)S(1)}, u32[]{:S(2)}, u32[]{:S(2)}) collective-permute-start(bf16[4,12288]{1,0:T(4,128)(2,1)S(1)} %get-tuple-element.98), channel_id=1, source_target_pairs={{0,2},{1,3},{2,0},{3,1},{4,6},{5,7},{6,4},{7,5},{8,10},{9,11},{10,... | collective-permute-start | bytes 294920 | tf_op jit(solution)/shard_map/ppermute | solution.py:186
  40.7 9.9 %collective-permute-start.22 = (bf16[4,12288]{1,0:T(4,128)(2,1)S(1)}, bf16[4,12288]{1,0:T(4,128)(2,1)S(1)}, u32[]{:S(2)}, u32[]{:S(2)}) collective-permute-start(bf16[4,12288]{1,0:T(4,128)(2,1)S(1)} %add_convert_fusion.2), channel_id=1, source_target_pairs={{0,12},{1,13},{2,14},{3,15},{4,8},{5,9},{6,10},{7,11},{8,4},{9,5},... | collective-permute-start | bytes 294920 | tf_op jit(solution)/shard_map/ppermute | solution.py:183
  43.0 7.6 %collective-permute-start.21 = (bf16[4,12288]{1,0:T(4,128)(2,1)S(1)}, bf16[4,12288]{1,0:T(4,128)(2,1)S(1)}, u32[]{:S(2)}, u32[]{:S(2)}) collective-permute-start(bf16[4,12288]{1,0:T(4,128)(2,1)S(1)} %add_convert_fusion.1), channel_id=1, source_target_pairs={{0,8},{1,9},{2,10},{3,11},{4,12},{5,13},{6,14},{7,15},{8,0},{9,1},... | collective-permute-start | bytes 294920 | tf_op jit(solution)/shard_map/ppermute | solution.py:183
  44.3 4.6 %collective-permute-start.18 = (bf16[4,12288]{1,0:T(4,128)(2,1)S(1)}, bf16[4,12288]{1,0:T(4,128)(2,1)S(1)}, u32[]{:S(2)}, u32[]{:S(2)}) collective-permute-start(bf16[4,12288]{1,0:T(4,128)(2,1)S(1)} %get-tuple-element.96), channel_id=1, source_target_pairs={{0,2},{1,3},{2,0},{3,1},{4,6},{5,7},{6,4},{7,5},{8,10},{9,11},{10,... | collective-permute-start | bytes 294920 | tf_op jit(solution)/shard_map/ppermute | solution.py:186
  45.5 5.1 %collective-permute-start.20 = (bf16[4,12288]{1,0:T(4,128)(2,1)S(1)}, bf16[4,12288]{1,0:T(4,128)(2,1)S(1)}, u32[]{:S(2)}, u32[]{:S(2)}) collective-permute-start(bf16[4,12288]{1,0:T(4,128)(2,1)S(1)} %add_convert_fusion), channel_id=1, source_target_pairs={{0,4},{1,5},{2,6},{3,7},{4,0},{5,1},{6,2},{7,3},{8,12},{9,13},{10,... | collective-permute-start | bytes 294920 | tf_op jit(solution)/shard_map/ppermute | solution.py:183

commit v27 on v21

--- a/solution.py
+++ b/solution.py
@@ -196,7 +196,9 @@
 
     held = [hidden] + [across(hidden, k) for k in range(1, groups)]
     w_in_mate = core(w_in)
-    held[1], lists, counts, block_slot = lax.optimization_barrier((held[1], lists, counts, block_slot))
+    early, bias_mate = lax.optimization_barrier((hidden, core(bias)))
+    beyond = [beside(h) for h in [early] + held[1:]]
+    beyond[0], lists, counts, block_slot = lax.optimization_barrier((beyond[0], lists, counts, block_slot))
 
     table = activity(lists, counts, block_slot)
     by = plane ^ jnp.arange(groups)
@@ -208,8 +210,6 @@
 
     low_in_sent, mask = lax.optimization_barrier((low_in, mask))
     low_in_mate = core(low_in_sent)
-    early, bias_mate = lax.optimization_barrier((hidden, core(bias)))
-    beyond = [beside(h) for h in [early] + held[1:]]
     near = (hidden, gain, shift, low_in, w_in, w_out, low_out)
     *near, mask, beyond[0] = lax.optimization_barrier((*near, mask, beyond[0]))
     near = call(

time: 51.1 us -> 52.7 us (1.031)
  Pallas kernels: 8.57 us -> 9.44 us
    ppermute x9, waiting for transfers between devices: 5.61 us -> 7.65 us  [beside(): return lax.ppermute(x, 'blk', [(i, i ^ 2) for i in range(devices)])]
    ppermute x9, waiting for transfers between devices: 7.24 us -> 5.57 us  [across(): return lax.ppermute(x, 'blk', [(i, i ^ 4 * k) for i in range(devices)])]
    pallas_call x1, Pallas kernels: 0.83 us -> 1.69 us  [shards(): call(functools.partial(early_body, groups, soon), [shape(some, width), sh...]
  transfers between devices with their start and end apart: 23 -> 23, of which waited for: 10 -> 8; matrix products, arithmetic and copies ran while one was open for 6% -> 6% of each run, Pallas kernels for 15% -> 16%
where the time goes in v27:
time: 52.7 us; the launch traced here: 52.5 us
  starting transfers between devices  25.4 us (48%)
  waiting for transfers between devices  14.4 us (27%)
  Pallas kernels  9.44 us (18%)
  other arithmetic  2.23 us (4%)
  local copies, waits for them, and re-layouts  0.86 us (2%)
    ppermute x9, starting transfers between devices, across(): return lax.ppermute(x, 'blk', [(i, i ^ 4 * k) for i in range(devices)])  14.3 us
    ppermute x9, starting transfers between devices, beside(): return lax.ppermute(x, 'blk', [(i, i ^ 2) for i in range(devices)])  9.98 us
    ppermute x9, waiting for transfers between devices, beside(): return lax.ppermute(x, 'blk', [(i, i ^ 2) for i in range(devices)])  7.65 us
    ppermute x9, waiting for transfers between devices, across(): return lax.ppermute(x, 'blk', [(i, i ^ 4 * k) for i in range(devices)])  5.57 us
    pallas_call x1, Pallas kernels, shards(): call(functools.partial(load_body, len(near)), [shape(*x.shape, dtype=x.dt...  3.39 us
    pallas_call x1, Pallas kernels, shards(): call(functools.partial(early_body, groups, soon), [shape(some, width), sh...  1.69 us
    pallas_call x1, Pallas kernels, shards(): call(functools.partial(act_body, step), [shape(rows, 2 * block)], [VMEM]...  1.21 us
    pallas_call x1, Pallas kernels, shards(): call(functools.partial(part_body, step), [shape(rows, width, dtype=f32)],...  1.19 us
  transfers between devices with their start and end apart: 23, of which 8 were waited for; matrix products, arithmetic and copies ran while one was open for 6% of the time, Pallas kernels for 16%

profile of v27, /device:TPU:0, one launch (start us, length us, event | category | flops | bytes accessed | tf_op | source)
XLA Modules:
  0.0 52.5 jit_solution(10714115742738937349)
XLA Ops:
  0.0 0.5 collective-permute-start.10
  0.5 2.6 %collective-permute-start.6 = (bf16[4,12288]{1,0:T(4,128)(2,1)}, bf16[4,12288]{1,0:T(4,128)(2,1)S(1)}, u32[]{:S(2)}, u32[]{:S(2)}) collective-permute-start(bf16[4,12288]{1,0:T(4,128)(2,1)} %refs_0_), channel_id=1, source_target_pairs={{0,4},{1,5},{2,6},{3,7},{4,0},{5,1},{6,2},{7,3},{8,12},{9,13},{10,... | collective-permute-start | bytes 294920 | tf_op jit(solution)/shard_map/ppermute | solution.py:183
  3.0 2.6 %collective-permute-start = (bf16[4,12288]{1,0:T(4,128)(2,1)}, bf16[4,12288]{1,0:T(4,128)(2,1)S(1)}, u32[]{:S(2)}, u32[]{:S(2)}) collective-permute-start(bf16[4,12288]{1,0:T(4,128)(2,1)} %refs_0_), channel_id=1, source_target_pairs={{0,8},{1,9},{2,10},{3,11},{4,12},{5,13},{6,14},{7,15},{8,0},{9,1},... | collective-permute-start | bytes 294920 | tf_op jit(solution)/shard_map/ppermute | solution.py:183
  5.7 1.2 %collective-permute-done.4.b_mate = f32[1,128]{1,0:T(1,128)S(1)} collective-permute-done((f32[1,128]{1,0:T(1,128)}, f32[1,128]{1,0:T(1,128)S(1)}, u32[]{:S(2)}, u32[]{:S(2)}) %collective-permute-start.4) | collective-permute-done | bytes 544 | tf_op jit(solution)/shard_map/ppermute | solution.py:189
  6.9 2.0 %collective-permute-start.5 = (bf16[4,12288]{1,0:T(4,128)(2,1)}, bf16[4,12288]{1,0:T(4,128)(2,1)S(1)}, u32[]{:S(2)}, u32[]{:S(2)}) collective-permute-start(bf16[4,12288]{1,0:T(4,128)(2,1)} %refs_0_), channel_id=1, source_target_pairs={{0,2},{1,3},{2,0},{3,1},{4,6},{5,7},{6,4},{7,5},{8,10},{9,11},{10,... | collective-permute-start | bytes 294920 | tf_op jit(solution)/shard_map/ppermute | solution.py:186
  9.0 3.7 %collective-permute-done.5.refs_4_ = bf16[4,12288]{1,0:T(4,128)(2,1)S(1)} collective-permute-done((bf16[4,12288]{1,0:T(4,128)(2,1)}, bf16[4,12288]{1,0:T(4,128)(2,1)S(1)}, u32[]{:S(2)}, u32[]{:S(2)}) %collective-permute-start.5) | collective-permute-done | bytes 98336 | tf_op jit(solution)/shard_map/ppermute | solution.py:186
  12.7 0.8 %copy.13 = s32[4,6]{0,1:T(8,128)S(1)} copy(s32[4,6]{1,0:T(4,128)} %param.15) | data formatting | bytes 192 | tf_op jit(solution)/shard_map/optimization_barrier | solution.py:201
  13.5 0.7 %fusion.1 = s32[4,6]{0,1:T(8,128)S(1)} fusion(s32[4]{0:T(128)} %param.16), kind=kLoop, calls=%fused_computation.12 | loop fusion | flops 48 | bytes 112 | tf_op jit(solution)/shard_map/convert_element_type | solution.py:150
  14.2 0.7 %fusion = s32[16,16]{1,0:T(8,128)S(1)} fusion(s32[16]{0:T(128)} %param.17), kind=kLoop, calls=%fused_computation.10 | loop fusion | flops 512 | bytes 1088 | tf_op jit(solution)/shard_map/convert_element_type | solution.py:153
  15.6 0.5 collective-permute-start.8
  16.1 2.0 %collective-permute-start.1 = (bf16[4,12288]{1,0:T(4,128)(2,1)S(1)}, bf16[4,12288]{1,0:T(4,128)(2,1)S(1)}, u32[]{:S(2)}, u32[]{:S(2)}) collective-permute-start(bf16[4,12288]{1,0:T(4,128)(2,1)S(1)} %collective-permute-done.refs_2_), channel_id=1, source_target_pairs={{0,2},{1,3},{2,0},{3,1},{4,6},{5,7},{6,4},{7,5},{8,10},{9,11},{10,... | collective-permute-start | bytes 294920 | tf_op jit(solution)/shard_map/ppermute | solution.py:186
  18.2 3.4 %shard_map.118 = (bf16[4,12288]{1,0:T(4,128)(2,1)S(1)}, f32[1,12288]{1,0:T(1,128)S(1)}, f32[1,12288]{1,0:T(1,128)S(1)}, bf16[768,512]{1,0:T(8,128)(2,1)S(1)}, bf...) custom-call(bf16[4,12288]{1,0:T(4,128)(2,1)} %refs_0_, ...), custom_call_target="tpu_custom_call" | custom-call | bytes 8388608 | tf_op jit(solution)/shard_map/pallas_call | solution.py:215
  21.6 1.7 %shard_map.119 = (bf16[16,12288]{1,0:T(8,128)(2,1)S(1)}, bf16[8,12288]{1,0:T(8,128)(2,1)S(1)}) custom-call(bf16[4,12288]{1,0:T(4,128)(2,1)S(1)} %get-tuple-element.62.refs_0_, bf16[4,12288]{1,0:T(4,128)(2,1)S(1)} %collective-permute-done.6.refs_1_, bf16[4,12288]{1,0:T(4,128)(2,1)S(1)} %collective-permute-done.refs_2_, ...), custom_call_target="tpu_custom_call" | custom-call | bytes 4194304 | tf_op jit(solution)/shard_map/pallas_call | solution.py:231
  23.6 0.8 %shard_map.120 = (bf16[16,12288]{1,0:T(8,128)(2,1)S(1)}, f32[32,512]{1,0:T(8,128)S(1)}, bf16[32,512]{1,0:T(8,128)(2,1)S(1)}) custom-call(s32[1]{0:T(128)} %bitcast.place, bf16[4,12288]{1,0:T(4,128)(2,1)S(1)} %collective-permute-done.1.refs_0_, bf16[4,12288]{1,0:T(4,128)(2,1)S(1)} %collective-permute-done.3.refs_1_, ...), custom_call_target="tpu_custom_call" | custom-call | bytes 4194304 | tf_op jit(solution)/shard_map/pallas_call | solution.py:239
  24.4 1.8 %collective-permute-start.9 = (bf16[32,512]{1,0:T(8,128)(2,1)S(1)}, bf16[32,512]{1,0:T(8,128)(2,1)S(1)}, u32[]{:S(2)}, u32[]{:S(2)}) collective-permute-start(bf16[32,512]{1,0:T(8,128)(2,1)S(1)} %get-tuple-element.71), channel_id=1, source_target_pairs={{0,2},{1,3},{2,0},{3,1},{4,6},{5,7},{6,4},{7,5},{8,10},{9,11},{10,... | collective-permute-start | bytes 98312 | tf_op jit(solution)/shard_map/ppermute | solution.py:186
  26.2 2.2 %collective-permute-done.9.got = bf16[32,512]{1,0:T(8,128)(2,1)S(1)} collective-permute-done((bf16[32,512]{1,0:T(8,128)(2,1)S(1)}, bf16[32,512]{1,0:T(8,128)(2,1)S(1)}, u32[]{:S(2)}, u32[]{:S(2)}) %collective-permute-start.9) | collective-permute-done | bytes 32800 | tf_op jit(solution)/shard_map/ppermute | solution.py:186
  28.4 3.9 %collective-permute-start.13 = (bf16[32,512]{1,0:T(8,128)(2,1)S(1)}, bf16[32,512]{1,0:T(8,128)(2,1)S(1)}, u32[]{:S(2)}, u32[]{:S(2)}) collective-permute-start(bf16[32,512]{1,0:T(8,128)(2,1)S(1)} %get-tuple-element.82), channel_id=1, source_target_pairs={{0,12},{1,13},{2,14},{3,15},{4,8},{5,9},{6,10},{7,11},{8,4},{9,5},... | collective-permute-start | bytes 98312 | tf_op jit(solution)/shard_map/ppermute | solution.py:183
  32.3 0.6 %collective-permute-start.15 = (bf16[32,512]{1,0:T(8,128)(2,1)S(1)}, bf16[32,512]{1,0:T(8,128)(2,1)S(1)}, u32[]{:S(2)}, u32[]{:S(2)}) collective-permute-start(bf16[32,512]{1,0:T(8,128)(2,1)S(1)} %get-tuple-element.84), channel_id=1, source_target_pairs={{0,4},{1,5},{2,6},{3,7},{4,0},{5,1},{6,2},{7,3},{8,12},{9,13},{10,... | collective-permute-start | bytes 98312 | tf_op jit(solution)/shard_map/ppermute | solution.py:183
  32.9 1.2 %shard_map.122.act = bf16[32,256]{1,0:T(8,128)(2,1)S(1)} custom-call(bf16[16,12288]{1,0:T(8,128)(2,1)S(1)} %get-tuple-element.66.refs_2_.near, bf16[16,12288]{1,0:T(8,128)(2,1)S(1)} %get-tuple-element.75.far, bf16[12288,128]{1,0:T(8,128)(2,1)S(1)} %get-tuple-element.76.w_own, bf16[12288,128]{1,0:T(8,128)(2,1)S(1)} %collective-permute-done.10.w_mate, ...), custom_call_target="tpu_custom_call" | custom-call | bytes 4194304 | tf_op jit(solution)/shard_map/pallas_call | solution.py:249
  34.2 1.2 %shard_map.123.part = f32[32,12288]{1,0:T(8,128)S(1)} custom-call(bf16[32,256]{1,0:T(8,128)(2,1)S(1)} %shard_map.122.act, bf16[128,12288]{1,0:T(8,128)(2,1)S(1)} %get-tuple-element.80.w_own, bf16[128,12288]{1,0:T(8,128)(2,1)S(1)} %collective-permute-done.12.w_mate), custom_call_target="tpu_custom_call" | custom-call | bytes 6291456 | tf_op jit(solution)/shard_map/pallas_call | solution.py:264
  35.4 1.7 %collective-permute-done.14.refs_1_ = bf16[32,512]{1,0:T(8,128)(2,1)S(1)} collective-permute-done((bf16[32,512]{1,0:T(8,128)(2,1)S(1)}, bf16[32,512]{1,0:T(8,128)(2,1)S(1)}, u32[]{:S(2)}, u32[]{:S(2)}) %collective-permute-start.14) | collective-permute-done | bytes 32800 | tf_op jit(solution)/shard_map/ppermute | solution.py:183
  37.1 0.4 shard_map.124
  37.6 1.6 %collective-permute-start.21 = (bf16[4,12288]{1,0:T(4,128)(2,1)S(1)}, bf16[4,12288]{1,0:T(4,128)(2,1)S(1)}, u32[]{:S(2)}, u32[]{:S(2)}) collective-permute-start(bf16[4,12288]{1,0:T(4,128)(2,1)S(1)} %get-tuple-element.92), channel_id=1, source_target_pairs={{0,2},{1,3},{2,0},{3,1},{4,6},{5,7},{6,4},{7,5},{8,10},{9,11},{10,... | collective-permute-start | bytes 294920 | tf_op jit(solution)/shard_map/ppermute | solution.py:186
  39.1 0.5 collective-permute-start.19
  39.6 1.5 %collective-permute-start.17 = (bf16[4,12288]{1,0:T(4,128)(2,1)S(1)}, bf16[4,12288]{1,0:T(4,128)(2,1)S(1)}, u32[]{:S(2)}, u32[]{:S(2)}) collective-permute-start(bf16[4,12288]{1,0:T(4,128)(2,1)S(1)} %get-tuple-element.88), channel_id=1, source_target_pairs={{0,2},{1,3},{2,0},{3,1},{4,6},{5,7},{6,4},{7,5},{8,10},{9,11},{10,... | collective-permute-start | bytes 294920 | tf_op jit(solution)/shard_map/ppermute | solution.py:186
  41.2 0.5 collective-permute-start.16
  41.7 1.5 %collective-permute-done.21 = bf16[4,12288]{1,0:T(4,128)(2,1)S(1)} collective-permute-done((bf16[4,12288]{1,0:T(4,128)(2,1)S(1)}, bf16[4,12288]{1,0:T(4,128)(2,1)S(1)}, u32[]{:S(2)}, u32[]{:S(2)}) %collective-permute-start.21) | collective-permute-done | bytes 98336 | tf_op jit(solution)/shard_map/ppermute | solution.py:186
  43.2 2.3 %collective-permute-start.22 = (bf16[4,12288]{1,0:T(4,128)(2,1)S(1)}, bf16[4,12288]{1,0:T(4,128)(2,1)S(1)}, u32[]{:S(2)}, u32[]{:S(2)}) collective-permute-start(bf16[4,12288]{1,0:T(4,128)(2,1)S(1)} %add_convert_fusion), channel_id=1, source_target_pairs={{0,12},{1,13},{2,14},{3,15},{4,8},{5,9},{6,10},{7,11},{8,4},{9,5},... | collective-permute-start | bytes 294920 | tf_op jit(solution)/shard_map/ppermute | solution.py:183
  45.9 1.9 %collective-permute-start.18 = (bf16[4,12288]{1,0:T(4,128)(2,1)S(1)}, bf16[4,12288]{1,0:T(4,128)(2,1)S(1)}, u32[]{:S(2)}, u32[]{:S(2)}) collective-permute-start(bf16[4,12288]{1,0:T(4,128)(2,1)S(1)} %add_convert_fusion.2), channel_id=1, source_target_pairs={{0,4},{1,5},{2,6},{3,7},{4,0},{5,1},{6,2},{7,3},{8,12},{9,13},{10,... | collective-permute-start | bytes 294920 | tf_op jit(solution)/shard_map/ppermute | solution.py:183
  47.9 1.7 %collective-permute-done.22.refs_3_ = bf16[4,12288]{1,0:T(4,128)(2,1)S(1)} collective-permute-done((bf16[4,12288]{1,0:T(4,128)(2,1)S(1)}, bf16[4,12288]{1,0:T(4,128)(2,1)S(1)}, u32[]{:S(2)}, u32[]{:S(2)}) %collective-permute-start.22) | collective-permute-done | bytes 98336 | tf_op jit(solution)/shard_map/ppermute | solution.py:183
  49.7 2.1 %collective-permute-done.20.refs_2_ = bf16[4,12288]{1,0:T(4,128)(2,1)S(1)} collective-permute-done((bf16[4,12288]{1,0:T(4,128)(2,1)S(1)}, bf16[4,12288]{1,0:T(4,128)(2,1)S(1)}, u32[]{:S(2)}, u32[]{:S(2)}) %collective-permute-start.20) | collective-permute-done | bytes 98336 | tf_op jit(solution)/shard_map/ppermute | solution.py:183
  51.8 0.7 %shard_map.125 = bf16[4,12288]{1,0:T(4,128)(2,1)} custom-call(f32[4,12288]{1,0:T(4,128)S(1)} %convert_add_fusion.refs_0_, bf16[4,12288]{1,0:T(4,128)(2,1)S(1)} %collective-permute-done.18.refs_1_, bf16[4,12288]{1,0:T(4,128)(2,1)S(1)} %collective-permute-done.20.refs_2_, bf16[4,12288]{1,0:T(4,128)(2,1)S(1)} %collective-permute-done.22.refs_3_), custom_call_target="tpu_custom_call" | custom-call | bytes 2097152 | tf_op jit(solution)/shard_map/pallas_call | solution.py:285
  (43 shorter events, 1.9 us)
Async XLA Ops:
  0.0 15.5 %collective-permute-start.10 = (bf16[12288,128]{1,0:T(8,128)(2,1)}, bf16[12288,128]{1,0:T(8,128)(2,1)S(1)}, u32[]{:S(2)}, u32[]{:S(2)}) collective-permute-start(bf16[12288,128]{1,0:T(8,128)(2,1)} %refs_4_), channel_id=1, source_target_pairs={{0,1},{1,0},{2,3},{3,2},{4,5},{5,4},{6,7},{7,6},{8,9},{9,8},{10,11... | collective-permute-start | bytes 9437192 | tf_op jit(solution)/shard_map/ppermute | solution.py:189
  0.5 8.5 %collective-permute-start.6 = (bf16[4,12288]{1,0:T(4,128)(2,1)}, bf16[4,12288]{1,0:T(4,128)(2,1)S(1)}, u32[]{:S(2)}, u32[]{:S(2)}) collective-permute-start(bf16[4,12288]{1,0:T(4,128)(2,1)} %refs_0_), channel_id=1, source_target_pairs={{0,4},{1,5},{2,6},{3,7},{4,0},{5,1},{6,2},{7,3},{8,12},{9,13},{10,... | collective-permute-start | bytes 294920 | tf_op jit(solution)/shard_map/ppermute | solution.py:183
  3.0 12.4 %collective-permute-start = (bf16[4,12288]{1,0:T(4,128)(2,1)}, bf16[4,12288]{1,0:T(4,128)(2,1)S(1)}, u32[]{:S(2)}, u32[]{:S(2)}) collective-permute-start(bf16[4,12288]{1,0:T(4,128)(2,1)} %refs_0_), channel_id=1, source_target_pairs={{0,8},{1,9},{2,10},{3,11},{4,12},{5,13},{6,14},{7,15},{8,0},{9,1},... | collective-permute-start | bytes 294920 | tf_op jit(solution)/shard_map/ppermute | solution.py:183
  5.6 9.8 %collective-permute-start.2 = (bf16[4,12288]{1,0:T(4,128)(2,1)}, bf16[4,12288]{1,0:T(4,128)(2,1)S(1)}, u32[]{:S(2)}, u32[]{:S(2)}) collective-permute-start(bf16[4,12288]{1,0:T(4,128)(2,1)} %refs_0_), channel_id=1, source_target_pairs={{0,12},{1,13},{2,14},{3,15},{4,8},{5,9},{6,10},{7,11},{8,4},{9,5},... | collective-permute-start | bytes 294920 | tf_op jit(solution)/shard_map/ppermute | solution.py:183
  5.6 1.3 %collective-permute-start.4 = (f32[1,128]{1,0:T(1,128)}, f32[1,128]{1,0:T(1,128)S(1)}, u32[]{:S(2)}, u32[]{:S(2)}) collective-permute-start(f32[1,128]{1,0:T(1,128)} %bitcast.12), channel_id=1, source_target_pairs={{0,1},{1,0},{2,3},{3,2},{4,5},{5,4},{6,7},{7,6},{8,9},{9,8},{10,11... | collective-permute-start | bytes 1544 | tf_op jit(solution)/shard_map/ppermute | solution.py:189
  6.9 5.8 %collective-permute-start.5 = (bf16[4,12288]{1,0:T(4,128)(2,1)}, bf16[4,12288]{1,0:T(4,128)(2,1)S(1)}, u32[]{:S(2)}, u32[]{:S(2)}) collective-permute-start(bf16[4,12288]{1,0:T(4,128)(2,1)} %refs_0_), channel_id=1, source_target_pairs={{0,2},{1,3},{2,0},{3,1},{4,6},{5,7},{6,4},{7,5},{8,10},{9,11},{10,... | collective-permute-start | bytes 294920 | tf_op jit(solution)/shard_map/ppermute | solution.py:186
  8.9 6.5 %collective-permute-start.7 = (bf16[4,12288]{1,0:T(4,128)(2,1)S(1)}, bf16[4,12288]{1,0:T(4,128)(2,1)}, u32[]{:S(2)}, u32[]{:S(2)}) collective-permute-start(bf16[4,12288]{1,0:T(4,128)(2,1)S(1)} %collective-permute-done.6.refs_1_), channel_id=1, source_target_pairs={{0,2},{1,3},{2,0},{3,1},{4,6},{5,7},{6,4},{7,5},{8,10},{9,11},{10,... | collective-permute-start | bytes 294920 | tf_op jit(solution)/shard_map/ppermute | solution.py:186
  15.5 18.7 %collective-permute-start.12 = (bf16[128,12288]{1,0:T(8,128)(2,1)}, bf16[128,12288]{1,0:T(8,128)(2,1)S(1)}, u32[]{:S(2)}, u32[]{:S(2)}) collective-permute-start(bf16[128,12288]{1,0:T(8,128)(2,1)} %refs_5_), channel_id=1, source_target_pairs={{0,1},{1,0},{2,3},{3,2},{4,5},{5,4},{6,7},{7,6},{8,9},{9,8},{10,11... | collective-permute-start | bytes 9437192 | tf_op jit(solution)/shard_map/ppermute | solution.py:189
  15.6 8.1 %collective-permute-start.8 = (bf16[768,512]{1,0:T(8,128)(2,1)}, bf16[768,512]{1,0:T(8,128)(2,1)S(1)}, u32[]{:S(2)}, u32[]{:S(2)}) collective-permute-start(bf16[768,512]{1,0:T(8,128)(2,1)} %refs_3_), channel_id=1, source_target_pairs={{0,1},{1,0},{2,3},{3,2},{4,5},{5,4},{6,7},{7,6},{8,9},{9,8},{10,11... | collective-permute-start | bytes 2359304 | tf_op jit(solution)/shard_map/ppermute | solution.py:189
  16.1 21.0 %collective-permute-start.11 = (bf16[512,768]{1,0:T(8,128)(2,1)}, bf16[512,768]{1,0:T(8,128)(2,1)S(1)}, u32[]{:S(2)}, u32[]{:S(2)}) collective-permute-start(bf16[512,768]{1,0:T(8,128)(2,1)} %refs_6_), channel_id=1, source_target_pairs={{0,1},{1,0},{2,3},{3,2},{4,5},{5,4},{6,7},{7,6},{8,9},{9,8},{10,11... | collective-permute-start | bytes 2359304 | tf_op jit(solution)/shard_map/ppermute | solution.py:189
  16.1 7.2 %collective-permute-start.1 = (bf16[4,12288]{1,0:T(4,128)(2,1)S(1)}, bf16[4,12288]{1,0:T(4,128)(2,1)S(1)}, u32[]{:S(2)}, u32[]{:S(2)}) collective-permute-start(bf16[4,12288]{1,0:T(4,128)(2,1)S(1)} %collective-permute-done.refs_2_), channel_id=1, source_target_pairs={{0,2},{1,3},{2,0},{3,1},{4,6},{5,7},{6,4},{7,5},{8,10},{9,11},{10,... | collective-permute-start | bytes 294920 | tf_op jit(solution)/shard_map/ppermute | solution.py:186
  18.1 5.5 %collective-permute-start.3 = (bf16[4,12288]{1,0:T(4,128)(2,1)S(1)}, bf16[4,12288]{1,0:T(4,128)(2,1)S(1)}, u32[]{:S(2)}, u32[]{:S(2)}) collective-permute-start(bf16[4,12288]{1,0:T(4,128)(2,1)S(1)} %collective-permute-done.2.refs_3_), channel_id=1, source_target_pairs={{0,2},{1,3},{2,0},{3,1},{4,6},{5,7},{6,4},{7,5},{8,10},{9,11},{10,... | collective-permute-start | bytes 294920 | tf_op jit(solution)/shard_map/ppermute | solution.py:186
  21.6 11.3 %copy-start.1 = (f32[128]{0:T(128)S(1)}, f32[128]{0:T(128)}, u32[]{:S(2)}) copy-start(f32[128]{0:T(128)} %param.19) | copy-start | bytes 1540
  24.4 3.9 %collective-permute-start.9 = (bf16[32,512]{1,0:T(8,128)(2,1)S(1)}, bf16[32,512]{1,0:T(8,128)(2,1)S(1)}, u32[]{:S(2)}, u32[]{:S(2)}) collective-permute-start(bf16[32,512]{1,0:T(8,128)(2,1)S(1)} %get-tuple-element.71), channel_id=1, source_target_pairs={{0,2},{1,3},{2,0},{3,1},{4,6},{5,7},{6,4},{7,5},{8,10},{9,11},{10,... | collective-permute-start | bytes 98312 | tf_op jit(solution)/shard_map/ppermute | solution.py:186
  28.4 7.0 %collective-permute-start.13 = (bf16[32,512]{1,0:T(8,128)(2,1)S(1)}, bf16[32,512]{1,0:T(8,128)(2,1)S(1)}, u32[]{:S(2)}, u32[]{:S(2)}) collective-permute-start(bf16[32,512]{1,0:T(8,128)(2,1)S(1)} %get-tuple-element.82), channel_id=1, source_target_pairs={{0,12},{1,13},{2,14},{3,15},{4,8},{5,9},{6,10},{7,11},{8,4},{9,5},... | collective-permute-start | bytes 98312 | tf_op jit(solution)/shard_map/ppermute | solution.py:183
  32.3 4.8 %collective-permute-start.14 = (bf16[32,512]{1,0:T(8,128)(2,1)S(1)}, bf16[32,512]{1,0:T(8,128)(2,1)S(1)}, u32[]{:S(2)}, u32[]{:S(2)}) collective-permute-start(bf16[32,512]{1,0:T(8,128)(2,1)S(1)} %get-tuple-element.83), channel_id=1, source_target_pairs={{0,8},{1,9},{2,10},{3,11},{4,12},{5,13},{6,14},{7,15},{8,0},{9,1},... | collective-permute-start | bytes 98312 | tf_op jit(solution)/shard_map/ppermute | solution.py:183
  32.3 4.8 %collective-permute-start.15 = (bf16[32,512]{1,0:T(8,128)(2,1)S(1)}, bf16[32,512]{1,0:T(8,128)(2,1)S(1)}, u32[]{:S(2)}, u32[]{:S(2)}) collective-permute-start(bf16[32,512]{1,0:T(8,128)(2,1)S(1)} %get-tuple-element.84), channel_id=1, source_target_pairs={{0,4},{1,5},{2,6},{3,7},{4,0},{5,1},{6,2},{7,3},{8,12},{9,13},{10,... | collective-permute-start | bytes 98312 | tf_op jit(solution)/shard_map/ppermute | solution.py:183
  34.1 2.9 %copy-start = (f32[512]{0:T(512)S(1)}, f32[512]{0:T(512)}, u32[]{:S(2)}) copy-start(f32[512]{0:T(512)} %param.22) | copy-start | bytes 6148
  37.6 5.6 %collective-permute-start.21 = (bf16[4,12288]{1,0:T(4,128)(2,1)S(1)}, bf16[4,12288]{1,0:T(4,128)(2,1)S(1)}, u32[]{:S(2)}, u32[]{:S(2)}) collective-permute-start(bf16[4,12288]{1,0:T(4,128)(2,1)S(1)} %get-tuple-element.92), channel_id=1, source_target_pairs={{0,2},{1,3},{2,0},{3,1},{4,6},{5,7},{6,4},{7,5},{8,10},{9,11},{10,... | collective-permute-start | bytes 294920 | tf_op jit(solution)/shard_map/ppermute | solution.py:186
  39.1 6.4 %collective-permute-start.19 = (bf16[4,12288]{1,0:T(4,128)(2,1)S(1)}, bf16[4,12288]{1,0:T(4,128)(2,1)S(1)}, u32[]{:S(2)}, u32[]{:S(2)}) collective-permute-start(bf16[4,12288]{1,0:T(4,128)(2,1)S(1)} %get-tuple-element.90), channel_id=1, source_target_pairs={{0,2},{1,3},{2,0},{3,1},{4,6},{5,7},{6,4},{7,5},{8,10},{9,11},{10,... | collective-permute-start | bytes 294920 | tf_op jit(solution)/shard_map/ppermute | solution.py:186
  39.6 6.2 %collective-permute-start.17 = (bf16[4,12288]{1,0:T(4,128)(2,1)S(1)}, bf16[4,12288]{1,0:T(4,128)(2,1)S(1)}, u32[]{:S(2)}, u32[]{:S(2)}) collective-permute-start(bf16[4,12288]{1,0:T(4,128)(2,1)S(1)} %get-tuple-element.88), channel_id=1, source_target_pairs={{0,2},{1,3},{2,0},{3,1},{4,6},{5,7},{6,4},{7,5},{8,10},{9,11},{10,... | collective-permute-start | bytes 294920 | tf_op jit(solution)/shard_map/ppermute | solution.py:186
  41.2 6.7 %collective-permute-start.16 = (bf16[4,12288]{1,0:T(4,128)(2,1)S(1)}, bf16[4,12288]{1,0:T(4,128)(2,1)S(1)}, u32[]{:S(2)}, u32[]{:S(2)}) collective-permute-start(bf16[4,12288]{1,0:T(4,128)(2,1)S(1)} %get-tuple-element.86), channel_id=1, source_target_pairs={{0,2},{1,3},{2,0},{3,1},{4,6},{5,7},{6,4},{7,5},{8,10},{9,11},{10,... | collective-permute-start | bytes 294920 | tf_op jit(solution)/shard_map/ppermute | solution.py:186
  43.2 6.5 %collective-permute-start.22 = (bf16[4,12288]{1,0:T(4,128)(2,1)S(1)}, bf16[4,12288]{1,0:T(4,128)(2,1)S(1)}, u32[]{:S(2)}, u32[]{:S(2)}) collective-permute-start(bf16[4,12288]{1,0:T(4,128)(2,1)S(1)} %add_convert_fusion), channel_id=1, source_target_pairs={{0,12},{1,13},{2,14},{3,15},{4,8},{5,9},{6,10},{7,11},{8,4},{9,5},... | collective-permute-start | bytes 294920 | tf_op jit(solution)/shard_map/ppermute | solution.py:183
  45.6 6.2 %collective-permute-start.20 = (bf16[4,12288]{1,0:T(4,128)(2,1)S(1)}, bf16[4,12288]{1,0:T(4,128)(2,1)S(1)}, u32[]{:S(2)}, u32[]{:S(2)}) collective-permute-start(bf16[4,12288]{1,0:T(4,128)(2,1)S(1)} %add_convert_fusion.1), channel_id=1, source_target_pairs={{0,8},{1,9},{2,10},{3,11},{4,12},{5,13},{6,14},{7,15},{8,0},{9,1},... | collective-permute-start | bytes 294920 | tf_op jit(solution)/shard_map/ppermute | solution.py:183
  45.9 5.8 %collective-permute-start.18 = (bf16[4,12288]{1,0:T(4,128)(2,1)S(1)}, bf16[4,12288]{1,0:T(4,128)(2,1)S(1)}, u32[]{:S(2)}, u32[]{:S(2)}) collective-permute-start(bf16[4,12288]{1,0:T(4,128)(2,1)S(1)} %add_convert_fusion.2), channel_id=1, source_target_pairs={{0,4},{1,5},{2,6},{3,7},{4,0},{5,1},{6,2},{7,3},{8,12},{9,13},{10,... | collective-permute-start | bytes 294920 | tf_op jit(solution)/shard_map/ppermute | solution.py:183
